TPU v7x, 32 devices: a whole 2x2x4 slice. The times are simulated.
32 devices in a mesh: groups: 2 (over y), row: 4 (over z), col: 4 (over x, core).
Axes of the slice: x: 2, y: 2, z: 4, core: 2. Of those that a mesh axis runs over, the one named last changes fastest.
Arguments:
- acts: bfloat16 [8, 512, 8192], P('groups', 'row'), parts along dimension 0, may hold values from -6 to 6
- grads: bfloat16 [8, 512, 32768], P('groups', 'row', 'col'), parts along dimension 0, may hold values from -0.26367188 to 0.26367188
- act_basis: bfloat16 [8192, 1024], P(None, 'col'), may hold values from -0.0625 to 0.0625
- grad_basis: bfloat16 [32768, 4096], P('col', 'row'), may hold values from -0.03125 to 0.03125
- eigenvalues: float32 [4096, 1024], P('row', 'col'), may hold values from 0.02 to 2.5
- query_rotated: bfloat16 [4, 4096, 1024], P(None, 'row', 'col'), may hold values from -0.0005836487 to 0.0005836487
- example_ids: int32 [8], P('groups'), parts along dimension 0, may hold values from 0 to 2047
- token_counts: int32 [2048], replicated, may hold values from 256 to 512
Outputs:
- rotated: float32 [8, 4096, 1024], P('groups', 'row', 'col'), parts along dimension 0
- scores: float32 [4, 8], P(None, 'groups'), parts along dimension 1
There are 2 independent parts, one for each index of `groups`. A program takes and returns all parts, laid end to end along the dimension named above; an argument that names none is the same for every part. Nothing has to cross between parts.
All inputs are finite; a program needn't handle non-finite values.
Results may differ from a plain program's by a relative error of at most 0.0051.
Values may be sent and summed in bfloat16 or wider, within the bound.
No kernel may reach another device: no remote copies, remote signals or barrier semaphores. Data moves between devices by JAX's collectives and lax.ppermute only.
A program may use at most 192 MiB of HBM per device.

v0:
```python
import jax
import jax.numpy as jnp
from jax import lax
from jax.sharding import PartitionSpec as P

DAMPING = 0.05


def body(acts, grads, act_basis, grad_basis, eigenvalues, query_rotated, example_ids, token_counts):
    tok_dev = grads.shape[1]
    pool_size = token_counts.shape[0]
    hits = example_ids[:, None] == jnp.arange(pool_size, dtype=jnp.int32)[None, :]
    lengths = jnp.sum(jnp.where(hits, token_counts[None, :], 0), axis=1)
    positions = lax.axis_index("row") * tok_dev + jnp.arange(tok_dev, dtype=jnp.int32)
    live = (positions[None, :] < lengths[:, None]).astype(jnp.float32)
    local_act = jnp.einsum("ctd,dk->ctk", acts, act_basis, preferred_element_type=jnp.float32)
    local_act = (local_act * live[:, :, None]).astype(jnp.bfloat16)
    partial_value = jnp.einsum(
        "ctd,dj->ctj",
        lax.all_gather(grads, "row", axis=1, tiled=True),
        grad_basis,
        preferred_element_type=jnp.float32,
    )
    every_act = lax.all_gather(local_act, "row", axis=1, tiled=True)
    rotated_grads = lax.psum(partial_value, "col").astype(jnp.bfloat16)
    rotated = jnp.einsum(
        "ctj,ctk->cjk", rotated_grads, every_act, preferred_element_type=jnp.float32
    )
    weights = query_rotated.astype(jnp.float32) / (eigenvalues + DAMPING)
    partial_scores = jnp.einsum("qjk,cjk->qc", weights, rotated, precision=lax.Precision.HIGHEST)
    scores = lax.psum(partial_scores, ("row", "col"))
    return (rotated, scores)


def solution(mesh):
    placed = (
        P("groups", "row", None),
        P("groups", "row", "col"),
        P(None, "col"),
        P("col", "row"),
        P("row", "col"),
        P(None, "row", "col"),
        P("groups"),
        P(),
    )
    return jax.shard_map(
        body,
        mesh=mesh,
        in_specs=placed,
        out_specs=(P("groups", "row", "col"), P(None, "groups")),
        check_vma=False,
    )
```

profile of v0, /device:TPU:0, one launch (start us, length us, event | category | flops | bytes accessed | tf_op | source)
XLA Modules:
  0.0 829.7 jit_solution(7631815058172643475)
XLA Ops:
  7.2 0.0 copy-start.5
  7.2 0.0 copy-start.4
  7.2 0.0 all-gather.3.cloned.1.call-start
  7.2 0.7 all-gather.3.cloned.1.call-update
  7.9 0.0 all-gather.5.cloned.1.call-start
  8.0 0.0 copy-done.5
  8.0 0.0 copy-done.4
  8.0 0.2 select_reduce_fusion
  8.2 0.1 compare_convert_fusion
  8.3 0.0 copy-start.3
  8.3 0.0 copy-start.2
  8.3 7.8 fusion.12
  16.0 0.0 all-gather.5.cloned.1.call-update
  16.1 0.0 copy-done.3
  16.1 0.1 broadcast_add_fusion
  16.2 0.0 copy-done.2
  16.2 2.3 convert_divide_fusion
  18.5 555.2 %all-gather.3.cloned.1.call-done = bf16[4,512,8192]{2,1,0:T(8,128)(2,1)} async-done(((bf16[4,128,8192]{2,1,0:T(8,128)(2,1)}), bf16[4,512,8192]{2,1,0:T(8,128)(2,1)}) %all-gather.3.cloned.1.call-update) | async-done | bytes 33554448 | tf_op jit(solution)/shard_map/all_gather | solution.py:20
  573.7 43.5 %fusion = f32[4,512,1024]{1,2,0:T(8,128)} fusion(bf16[4,512,8192]{2,1,0:T(8,128)(2,1)} %all-gather.3.cloned.1.call-done, bf16[8192,1024]{1,0:T(8,128)(2,1)} %param.11), kind=kOutput, calls=%fused_computation | convolution fusion | flops 34359738368 | bytes 58720256 | tf_op jit(solution)/shard_map/ctd,dj->ctj/dot_general | solution.py:18
  617.2 147.4 %all-reduce.1 = bf16[4,512,1024]{1,2,0:T(8,128)(2,1)} all-reduce(f32[4,512,1024]{1,2,0:T(8,128)} %fusion), channel_id=1, replica_groups=mesh['groups'=2,'row'=4,'col'=4] {'col'}, use_global_device_ids=true, to_apply=%region_0.1 | all-reduce | flops 2097152 | bytes 12582912 | tf_op jit(solution)/shard_map/psum | solution.py:25
  764.6 0.0 all-gather.5.cloned.1.call-done
  764.6 0.0 copy-start.1
  764.6 3.9 fusion.20
  768.5 0.0 copy-start
  768.5 2.0 copy-done
  770.5 0.0 copy-done.1
  770.5 21.9 %fusion.15 = f32[4,4]{1,0:T(4,128)S(1)} fusion(f32[4,1024,256]{2,1,0:T(8,128)S(1)} %fusion.20, f32[4,1024,256]{2,1,0:T(8,128)S(1)} %copy-done.1), kind=kOutput, calls=%fused_computation.12 | convolution fusion | flops 50331648 | bytes 8388672 | tf_op jit(solution)/shard_map/qjk,cjk->qc/dot_general | solution.py:30
  792.4 30.4 %psum.15 = f32[4,4]{1,0:T(4,128)} all-reduce(f32[4,4]{1,0:T(4,128)S(1)} %fusion.15), channel_id=1, replica_groups=mesh['groups'=2,'row'=4,'col'=4] {'row','col'}, use_global_device_ids=true, to_apply=%region_2.3 | all-reduce | flops 16 | bytes 128 | tf_op jit(solution)/shard_map/psum | solution.py:31
  (1 shorter events, 0.0 us)
Async XLA Ops:
  7.2 0.8 copy-start.5
  7.2 0.8 copy-start.4
  7.2 566.6 %all-gather.3.cloned.1.call-start = ((), (), s32[]{:S(2)}) async-start(), calls=%async_computation | async-start | bytes 41943040 | tf_op jit(solution)/shard_map/all_gather | solution.py:20
  7.9 756.7 %all-gather.5.cloned.1.call-start = ((), (), s32[]{:S(2)}) async-start(), calls=%async_computation.1 | async-start | bytes 1310720 | tf_op jit(solution)/shard_map/all_gather | solution.py:24
  8.3 7.8 copy-start.3
  8.3 7.9 copy-start.2
  764.6 5.9 copy-start.1
  768.5 2.0 copy-start
Sparse Core Ops, SparseCore 0:
  9.6 564.0 all-gather.2
  575.3 26.1 all-gather.4
where the time goes:
time: 830 us
  waiting for transfers between devices  556 us (67%)
  blocking collectives  178 us (21%)
  matrix products  77.1 us (9%)
  between operations  14.1 us (2%)
    all_gather x1, waiting for transfers between devices, body(): lax.all_gather(grads, 'row', axis=1, tiled=True)  555 us
    psum x1, blocking collectives, body(): rotated_grads = lax.psum(partial_value, 'col').astype(jnp.bfloat16)  147 us
    dot_general x1, matrix products, body(): jnp.einsum('ctd,dj->ctj', lax.all_gather(grads, 'row', axis=1, tiled=True...  43.5 us
    psum x1, blocking collectives, body(): scores = lax.psum(partial_scores, ('row', 'col'))  30.4 us
    dot_general x1, matrix products, body(): jnp.einsum('qjk,cjk->qc', weights, rotated, precision=lax.Precision.HIGHEST)  21.9 us
  transfers between devices with their start and end apart: 2, of which 1 were waited for; matrix products, arithmetic and copies ran while one was open for 7% of the time, Pallas kernels for 0%

commit v1 on v0

v1 whole, which is shorter than its diff:
```python
import jax
import jax.numpy as jnp
from jax import lax
from jax.experimental import pallas as pl
from jax.experimental.pallas import tpu as pltpu
from jax.sharding import PartitionSpec as P

DAMPING = 0.05
BF16 = jnp.bfloat16
F32 = jnp.float32


def candidate_lengths(example_ids, token_counts):
    pool_size = token_counts.shape[0]
    hits = example_ids[:, None] == jnp.arange(pool_size, dtype=jnp.int32)[None, :]
    return jnp.sum(jnp.where(hits, token_counts[None, :], 0), axis=1)


def local_activations(acts, act_basis, lengths):
    tok = acts.shape[1]
    positions = lax.axis_index("row") * tok + jnp.arange(tok, dtype=jnp.int32)
    live = (positions[None, :] < lengths[:, None]).astype(F32)
    rotated = jnp.einsum("ctd,dk->ctk", acts, act_basis, preferred_element_type=F32)
    return (rotated * live[:, :, None]).astype(BF16)


def final_kernel(grad_ref, act_ref, eig_ref, query_ref, out_ref, score_ref):
    cands, queries = grad_ref.shape[0], query_ref.shape[0]
    damped = eig_ref[...] + DAMPING
    weights = [query_ref[q].astype(F32) / damped for q in range(queries)]
    rows = []
    for c in range(cands):
        tile = lax.dot_general(
            grad_ref[c], act_ref[c], (((0,), (0,)), ((), ())), preferred_element_type=F32
        )
        out_ref[c] = tile
        rows.append([jnp.sum(weights[q] * tile, axis=0, keepdims=True) for q in range(queries)])
    score_ref[0] = jnp.concatenate(
        [rows[c][q] for q in range(queries) for c in range(cands)], axis=0
    )


def rotate_and_score(grad_rot, act_rot, eigenvalues, query_rotated):
    cands, seq, dirs = grad_rot.shape
    width = act_rot.shape[2]
    queries = query_rotated.shape[0]
    block = min(dirs, 256)
    steps = dirs // block
    rotated, partial_scores = pl.pallas_call(
        final_kernel,
        grid=(steps,),
        in_specs=[
            pl.BlockSpec((cands, seq, block), lambda i: (0, 0, i)),
            pl.BlockSpec((cands, seq, width), lambda i: (0, 0, 0)),
            pl.BlockSpec((block, width), lambda i: (i, 0)),
            pl.BlockSpec((queries, block, width), lambda i: (0, i, 0)),
        ],
        out_specs=[
            pl.BlockSpec((cands, block, width), lambda i: (0, i, 0)),
            pl.BlockSpec((1, queries * cands, width), lambda i: (i, 0, 0)),
        ],
        out_shape=[
            jax.ShapeDtypeStruct((cands, dirs, width), F32),
            jax.ShapeDtypeStruct((steps, queries * cands, width), F32),
        ],
        compiler_params=pltpu.CompilerParams(vmem_limit_bytes=32 * 2**20),
    )(grad_rot, act_rot, eigenvalues, query_rotated)
    scores = jnp.sum(partial_scores, axis=(0, 2)).reshape(queries, cands)
    return rotated, lax.psum(scores, ("row", "col"))


def gather_body(acts, grads, act_basis, grad_basis, eigenvalues, query_rotated, example_ids, token_counts):
    lengths = candidate_lengths(example_ids, token_counts)
    local_act = local_activations(acts, act_basis, lengths)
    partial_value = jnp.einsum(
        "ctd,dj->ctj",
        lax.all_gather(grads, "row", axis=1, tiled=True),
        grad_basis,
        preferred_element_type=F32,
    )
    every_act = lax.all_gather(local_act, "row", axis=1, tiled=True)
    rotated_grads = lax.psum(partial_value, "col").astype(BF16)
    return rotate_and_score(rotated_grads, every_act, eigenvalues, query_rotated)


def after(value, *earlier):
    return lax.optimization_barrier((value, *earlier))[0]


def chain_body(acts, grads, act_basis, grad_basis, eigenvalues, query_rotated, example_ids, token_counts):
    cands, tok, feats = grads.shape
    dirs = grad_basis.shape[1]
    group, row, col = (lax.axis_index(a) for a in ("groups", "row", "col"))
    sides, parts = 2, 4
    inward = [(0, 1), (3, 2)]
    across = [(1, 2), (2, 1)]
    outward = [(1, 0), (2, 3)]
    planes = 4
    swap = [(g * planes + r, (1 - g) * planes + r) for g in range(sides) for r in (1, 2)]
    at_end = (row == 0) | (row == planes - 1)

    other = lax.ppermute(grads, "row", across)

    half = dirs // sides
    pieces = 4
    deep = feats // pieces
    near, far = [], []
    for k in range(pieces):
        piece = lax.dynamic_slice(grad_basis, (k * deep, group * half), (deep, half))
        if k >= 2:
            piece = after(piece, near[k - 2])
        near.append(lax.ppermute(piece, "row", inward))
        far.append(lax.ppermute(near[k], ("groups", "row"), swap))

    spans = [(c, s, tok // 2) for c in range(cands) for s in (0, tok // 2)]
    started = list(near)
    first, second = [], []
    for c, s, n in spans:
        piece = after(lax.slice(grads, (c, s, 0), (c + 1, s + n, feats))[0], started[-2])
        first.append(lax.ppermute(piece, "row", inward))
        started.append(first[-1])
        second.append(lax.ppermute(first[-1], "row", across))

    lengths = candidate_lengths(example_ids, token_counts)
    local_act = local_activations(acts, act_basis, lengths)
    every_act = lax.all_gather(local_act, "row", axis=0)

    near_basis = jnp.concatenate(near, axis=0)
    far_basis = jnp.concatenate(far, axis=0)

    def multiply(tokens):
        def dot(basis):
            return lax.dot_general(
                tokens, basis, (((tokens.ndim - 1,), (0,)), ((), ())), preferred_element_type=F32
            ).astype(BF16)

        one, two = dot(near_basis), dot(far_basis)
        low = jnp.where(group == 0, one, two)
        high = jnp.where(group == 0, two, one)
        return jnp.concatenate([dot(grad_basis), low, high], axis=-1)

    def finish(value):
        held = lax.dynamic_index_in_dim(value, col, 0, keepdims=False).astype(F32)
        for d in range(1, parts):
            sent = lax.dynamic_index_in_dim(value, col ^ d, 0, keepdims=False)
            held = held + lax.ppermute(sent, "col", [(i, i ^ d) for i in range(parts)]).astype(F32)
        total = held.astype(BF16)
        back = lax.ppermute(total[:, dirs:], "row", outward)
        mine = jnp.where(at_end, back, total[:, :dirs])
        return [mine] + [
            lax.ppermute(mine, "col", [(i, i ^ d) for i in range(parts)]) for d in range(1, parts)
        ]

    sub = tok // parts
    both = jnp.stack([multiply(grads), multiply(other)])
    both = both.reshape(2, cands, parts, sub, 2 * dirs)
    both = jnp.moveaxis(both, 2, 0).reshape(parts, 2 * cands * sub, 2 * dirs)
    middle = jnp.stack([x.reshape(2, cands, sub, dirs) for x in finish(both)])
    middle = jnp.transpose(middle, (2, 0, 1, 3, 4)).reshape(cands, parts * 2 * sub, dirs)

    grad_by_cand = [[middle[c]] for c in range(cands)]
    act_order = {}
    for (c, s, n), one, two in zip(spans, first, second):
        value = multiply(jnp.stack([one, two])).reshape(2, parts, n // parts, 2 * dirs)
        value = jnp.moveaxis(value, 1, 0).reshape(parts, 2 * (n // parts), 2 * dirs)
        for d, x in enumerate(finish(value)):
            grad_by_cand[c].append(x)
    grad_rot = jnp.stack([jnp.concatenate(g, axis=0) for g in grad_by_cand])

    own_order = jnp.where(row < 2, every_act, every_act[::-1])

    def by_part(block, n):
        split = block.reshape(cands, parts, n // parts, -1)
        split = jnp.where((col & 1) == 1, split[:, jnp.array([1, 0, 3, 2])], split)
        split = jnp.where((col & 2) == 2, split[:, jnp.array([2, 3, 0, 1])], split)
        return jnp.moveaxis(split, 1, 0)

    width = every_act.shape[-1]
    inner = jnp.stack([by_part(own_order[1], tok), by_part(own_order[2], tok)])
    inner = jnp.transpose(inner, (2, 1, 0, 3, 4)).reshape(cands, parts * 2 * sub, width)
    act_by_cand = [[inner[c]] for c in range(cands)]
    for c, s, n in spans:
        pair = jnp.stack([by_part(own_order[e][:, s : s + n], n)[:, c] for e in (0, 3)])
        act_by_cand[c].append(jnp.moveaxis(pair, 1, 0).reshape(2 * n, width))
    act_rot = jnp.stack([jnp.concatenate(a, axis=0) for a in act_by_cand])
    return rotate_and_score(grad_rot, act_rot, eigenvalues, query_rotated)


def solution(mesh):
    placed = (
        P("groups", "row", None),
        P("groups", "row", "col"),
        P(None, "col"),
        P("col", "row"),
        P("row", "col"),
        P(None, "row", "col"),
        P("groups"),
        P(),
    )
    chain = mesh.shape["groups"] == 2 and mesh.shape["row"] == 4 and mesh.shape["col"] == 4
    return jax.shard_map(
        chain_body if chain else gather_body,
        mesh=mesh,
        in_specs=placed,
        out_specs=(P("groups", "row", "col"), P(None, "groups")),
        check_vma=False,
    )
```

time: 830 us -> 1030 us (1.24)
  starting transfers between devices: 0.08 us -> 380 us
  waiting for transfers between devices: 556 us -> 321 us
  matrix products: 77.1 us -> 226 us
  blocking collectives: 178 us -> 32.7 us
  local copies, waits for them, and re-layouts: 2.03 us -> 39.5 us
    all_gather x2 -> x1, waiting for transfers between devices: 555 us -> 14 us  [chain_body(): every_act = lax.all_gather(local_act, 'row', axis=0)]
    ppermute x0 -> x88, starting transfers between devices: none -> 380 us  [the longest x8 294 us: chain_body(): first.append(lax.ppermute(piece, 'row', inward))]
    ppermute x0 -> x88, waiting for transfers between devices: none -> 307 us  [the longest x4 116 us: chain_body(): near.append(lax.ppermute(piece, 'row', inward))]
    dot_general x4 -> x31, matrix products: 77.1 us -> 226 us  [the longest x30 218 us: dot(): lax.dot_general(tokens, basis, (((tokens.ndim - 1,), (0,)), ((), ())), pr...]
    psum x2 -> x1, blocking collectives: 178 us -> 32.7 us  [rotate_and_score(): return (rotated, lax.psum(scores, ('row', 'col')))]
  transfers between devices with their start and end apart: 2 -> 89, of which waited for: 1 -> 35; matrix products, arithmetic and copies ran while one was open for 7% -> 25% of each run, Pallas kernels for 0% -> 0%
where the time goes in v1:
time: 1030 us
  starting transfers between devices  380 us (37%)
  waiting for transfers between devices  321 us (31%)
  matrix products  226 us (22%)
  local copies, waits for them, and re-layouts  39.5 us (4%)
  blocking collectives  32.7 us (3%)
  between operations  16.5 us (2%)
    ppermute x8, starting transfers between devices, chain_body(): first.append(lax.ppermute(piece, 'row', inward))  294 us
    dot_general x30, matrix products, dot(): lax.dot_general(tokens, basis, (((tokens.ndim - 1,), (0,)), ((), ())), pr...  218 us
    ppermute x4, waiting for transfers between devices, chain_body(): near.append(lax.ppermute(piece, 'row', inward))  116 us
    ppermute x27, waiting for transfers between devices, finish(): lax.ppermute(sent, 'col', [(i, i ^ d) for i in range(parts)]).astype(F32)  59.9 us
    ppermute x9, waiting for transfers between devices, finish(): back = lax.ppermute(total[:, dirs:], 'row', outward)  52.4 us
    ppermute x27, waiting for transfers between devices, finish(): lax.ppermute(mine, 'col', [(i, i ^ d) for i in range(parts)])  40.2 us
    ppermute x8, waiting for transfers between devices, chain_body(): first.append(lax.ppermute(piece, 'row', inward))  38.3 us
    psum x1, blocking collectives, rotate_and_score(): return (rotated, lax.psum(scores, ('row', 'col')))  32.7 us
  transfers between devices with their start and end apart: 89, of which 35 were waited for; matrix products, arithmetic and copies ran while one was open for 25% of the time, Pallas kernels for 0%

profile of v1, /device:TPU:0, one launch (start us, length us, event | category | flops | bytes accessed | tf_op | source)
XLA Modules:
  0.0 1025.6 jit_solution(18366533627967379313)
XLA Ops:
  7.2 6.4 constant_dynamic-slice_fusion
  13.6 4.0 copy.376
  17.6 6.3 collective-permute-start.1
  23.9 4.0 copy.375
  30.7 7.6 fusion.34
  38.4 3.9 copy.378
  44.9 15.8 %fusion.25 = bf16[4,128,1024]{2,1,0:T(8,128)(2,1)} fusion(bf16[4,128,8192]{2,1,0:T(8,128)(2,1)} %param.45, bf16[8192,1024]{1,0:T(8,128)(2,1)} %param.47), kind=kOutput, calls=%fused_computation.54 | convolution fusion | flops 8590458880 | bytes 26214400 | tf_op jit(solution)/shard_map/dot_general | solution.py:133
  60.7 6.0 slice_bitcast_fusion.6
  66.7 14.0 %all-gather.3.cloned.1.call-done = bf16[16,128,256]{2,1,0:T(8,128)(2,1)} async-done(((bf16[4,128,256]{2,1,0:T(8,128)(2,1)}), bf16[16,128,256]{2,1,0:T(8,128)(2,1)}) %all-gather.3.cloned.1.call-update) | async-done | bytes 1048592 | tf_op jit(solution)/shard_map/all_gather | solution.py:126
  87.6 42.0 %collective-permute-done = bf16[2048,512]{0,1:T(8,128)(2,1)} collective-permute-done((bf16[2048,512]{0,1:T(8,128)(2,1)}, bf16[2048,512]{0,1:T(8,128)(2,1)}, u32[]{:S(2)}, u32[]{:S(2)}) %collective-permute-start) | collective-permute-done | bytes 2097184 | tf_op jit(solution)/shard_map/ppermute | solution.py:112
  129.5 5.7 collective-permute-start.2
  140.6 39.7 %collective-permute-done.2 = bf16[2048,512]{0,1:T(8,128)(2,1)} collective-permute-done((bf16[2048,512]{0,1:T(8,128)(2,1)}, bf16[2048,512]{0,1:T(8,128)(2,1)}, u32[]{:S(2)}, u32[]{:S(2)}) %collective-permute-start.2) | collective-permute-done | bytes 2097184 | tf_op jit(solution)/shard_map/ppermute | solution.py:112
  180.3 4.4 collective-permute-start.16
  191.1 34.2 %collective-permute-done.3 = bf16[2048,512]{0,1:T(8,128)(2,1)} collective-permute-done((bf16[2048,512]{0,1:T(8,128)(2,1)}, bf16[2048,512]{0,1:T(8,128)(2,1)}, u32[]{:S(2)}, u32[]{:S(2)}) %collective-permute-start.3) | collective-permute-done | bytes 2097184 | tf_op jit(solution)/shard_map/ppermute | solution.py:112
  227.5 18.2 %collective-permute-done.16 = bf16[64,8192]{1,0:T(8,128)(2,1)S(1)} collective-permute-done((bf16[64,8192]{1,0:T(8,128)(2,1)}, bf16[64,8192]{1,0:T(8,128)(2,1)S(1)}, u32[]{:S(2)}, u32[]{:S(2)}) %collective-permute-start.16) | collective-permute-done | bytes 1048608 | tf_op jit(solution)/shard_map/ppermute | solution.py:120
  245.6 4.5 collective-permute-start.25
  250.2 10.1 convolution_convert_fusion.3
  260.3 10.3 %collective-permute-done.25 = bf16[64,8192]{1,0:T(8,128)(2,1)S(1)} collective-permute-done((bf16[64,8192]{1,0:T(8,128)(2,1)S(1)}, bf16[64,8192]{1,0:T(8,128)(2,1)S(1)}, u32[]{:S(2)}, u32[]{:S(2)}) %collective-permute-start.25) | collective-permute-done | bytes 1048608 | tf_op jit(solution)/shard_map/ppermute | solution.py:120
  270.6 5.4 collective-permute-start.34
  280.9 7.9 select_bitcast_fusion.3
  288.8 9.8 collective-permute-done.34
  298.6 80.5 %collective-permute-start.52 = (bf16[64,8192]{1,0:T(8,128)(2,1)S(1)}, bf16[64,8192]{1,0:T(8,128)(2,1)}, u32[]{:S(2)}, u32[]{:S(2)}) collective-permute-start(bf16[64,8192]{1,0:T(8,128)(2,1)S(1)} %copy-done.3), channel_id=1, source_target_pairs={{0,4},{12,8},{1,5},{13,9},{2,6},{14,10},{3,7},{15,11},{16,20},{28,... | collective-permute-start | bytes 3145736 | tf_op jit(solution)/shard_map/ppermute | solution.py:120
  380.5 8.8 fusion.37
  389.4 5.6 convolution_convert_fusion.19
  395.0 5.7 broadcast_select_fusion.15
  402.8 8.5 fusion.40
  411.3 5.6 convolution_convert_fusion.17
  417.0 5.7 broadcast_select_fusion.13
  428.4 4.0 collective-permute-start.8
  438.1 6.0 convolution_convert_fusion.15
  444.1 8.5 fusion.43
  452.6 5.6 broadcast_select_fusion.11
  460.4 5.3 convolution_convert_fusion.13
  465.7 5.3 broadcast_select_fusion.9
  471.0 8.3 fusion.46
  479.5 194.1 %collective-permute-start.79 = (bf16[64,8192]{1,0:T(8,128)(2,1)S(1)}, bf16[64,8192]{1,0:T(8,128)(2,1)S(1)}, u32[]{:S(2)}, u32[]{:S(2)}) collective-permute-start(bf16[64,8192]{1,0:T(8,128)(2,1)S(1)} %copy-done.2), channel_id=1, source_target_pairs={{0,4},{12,8},{1,5},{13,9},{2,6},{14,10},{3,7},{15,11},{16,20},{28,... | collective-permute-start | bytes 3145736 | tf_op jit(solution)/shard_map/ppermute | solution.py:120
  676.5 9.4 convolution_convert_fusion.1
  686.0 15.0 %fusion.28 = bf16[4,128,1024]{2,1,0:T(8,128)(2,1)S(1)} fusion(bf16[4,128,8192]{2,1,0:T(8,128)(2,1)} %collective-permute-done.8, bf16[8192,1024]{1,0:T(8,128)(2,1)} %param.47), kind=kOutput, calls=%fused_computation.55 | convolution fusion | flops 8590458880 | bytes 26214400 | tf_op jit(solution)/shard_map/dot_general | solution.py:133
  701.0 9.5 select_bitcast_fusion.1
  712.9 8.5 fusion.49
  721.5 8.5 fusion.52
  730.1 5.7 convolution_convert_fusion.11
  735.8 5.9 convolution_convert_fusion.9
  741.7 5.8 broadcast_select_fusion.7
  747.6 6.1 broadcast_select_fusion.5
  760.6 3.0 collective-permute-done.55
  765.3 45.6 %collective-permute-done.65 = bf16[32,2048]{1,0:T(8,128)(2,1)S(1)} collective-permute-done((bf16[32,2048]{1,0:T(8,128)(2,1)S(1)}, bf16[32,2048]{1,0:T(8,128)(2,1)S(1)}, u32[]{:S(2)}, u32[]{:S(2)}) %collective-permute-start.65) | collective-permute-done | bytes 131104 | tf_op jit(solution)/shard_map/ppermute | solution.py:146
  811.2 2.7 collective-permute-done.64
  818.9 3.7 fusion.55
  822.6 5.6 convolution_convert_fusion.7
  828.2 5.6 broadcast_select_fusion.3
  835.9 4.0 fusion.58
  839.9 6.0 convolution_convert_fusion.5
  845.9 5.6 broadcast_select_fusion.1
  857.8 2.9 collective-permute-done.82
  863.4 7.9 collective-permute-done.15
  872.7 10.3 collective-permute-done.14
  886.1 47.5 %collective-permute-done.75 = bf16[32,1024]{1,0:T(8,128)(2,1)S(1)} collective-permute-done((bf16[32,1024]{1,0:T(8,128)(2,1)S(1)}, bf16[32,1024]{1,0:T(8,128)(2,1)S(1)}, u32[]{:S(2)}, u32[]{:S(2)}) %collective-permute-start.75) | collective-permute-done | bytes 65568 | tf_op jit(solution)/shard_map/ppermute | solution.py:148
  935.0 4.8 collective-permute-done.57
  944.5 3.9 collective-permute-done.77
  948.4 3.7 collective-permute-done.78
  954.2 2.9 collective-permute-done.59
  981.0 4.3 shard_map.419
  985.5 32.7 %psum.7 = f32[4,4]{1,0:T(4,128)} all-reduce(f32[4,4]{1,0:T(4,128)S(1)} %reshape.211), channel_id=1, replica_groups=mesh['groups'=2,'row'=4,'col'=4] {'row','col'}, use_global_device_ids=true, to_apply=%region_2.3 | all-reduce | flops 16 | bytes 128 | tf_op jit(solution)/shard_map/psum | solution.py:69
  (378 shorter events, 114.0 us)
Async XLA Ops:
  7.2 73.5 %all-gather.3.cloned.1.call-start = ((), (), s32[]{:S(2)}) async-start(), calls=%async_computation | async-start | bytes 1310720 | tf_op jit(solution)/shard_map/all_gather | solution.py:126
  17.6 118.2 %collective-permute-start.1 = (bf16[2048,512]{0,1:T(8,128)(2,1)}, bf16[2048,512]{0,1:T(8,128)(2,1)}, u32[]{:S(2)}, u32[]{:S(2)}) collective-permute-start(bf16[2048,512]{0,1:T(8,128)(2,1)} %copy.376), channel_id=1, source_target_pairs={{0,4},{12,8},{1,5},{13,9},{2,6},{14,10},{3,7},{15,11},{16,20},{28,... | collective-permute-start | bytes 6291464 | tf_op jit(solution)/shard_map/ppermute | solution.py:112
  27.9 101.7 %collective-permute-start = (bf16[2048,512]{0,1:T(8,128)(2,1)}, bf16[2048,512]{0,1:T(8,128)(2,1)}, u32[]{:S(2)}, u32[]{:S(2)}) collective-permute-start(bf16[2048,512]{0,1:T(8,128)(2,1)} %copy.375), channel_id=1, source_target_pairs={{0,4},{12,8},{1,5},{13,9},{2,6},{14,10},{3,7},{15,11},{16,20},{28,... | collective-permute-start | bytes 6291464 | tf_op jit(solution)/shard_map/ppermute | solution.py:112
  129.5 50.8 %collective-permute-start.2 = (bf16[2048,512]{0,1:T(8,128)(2,1)}, bf16[2048,512]{0,1:T(8,128)(2,1)}, u32[]{:S(2)}, u32[]{:S(2)}) collective-permute-start(bf16[2048,512]{0,1:T(8,128)(2,1)} %copy.377), channel_id=1, source_target_pairs={{0,4},{12,8},{1,5},{13,9},{2,6},{14,10},{3,7},{15,11},{16,20},{28,... | collective-permute-start | bytes 6291464 | tf_op jit(solution)/shard_map/ppermute | solution.py:112
  135.9 89.4 %collective-permute-start.3 = (bf16[2048,512]{0,1:T(8,128)(2,1)}, bf16[2048,512]{0,1:T(8,128)(2,1)}, u32[]{:S(2)}, u32[]{:S(2)}) collective-permute-start(bf16[2048,512]{0,1:T(8,128)(2,1)} %copy.378), channel_id=1, source_target_pairs={{0,4},{12,8},{1,5},{13,9},{2,6},{14,10},{3,7},{15,11},{16,20},{28,... | collective-permute-start | bytes 6291464 | tf_op jit(solution)/shard_map/ppermute | solution.py:112
  180.3 65.3 %collective-permute-start.16 = (bf16[64,8192]{1,0:T(8,128)(2,1)}, bf16[64,8192]{1,0:T(8,128)(2,1)S(1)}, u32[]{:S(2)}, u32[]{:S(2)}) collective-permute-start(bf16[64,8192]{1,0:T(8,128)(2,1)} %get-tuple-element.16), channel_id=1, source_target_pairs={{0,4},{12,8},{1,5},{13,9},{2,6},{14,10},{3,7},{15,11},{16,20},{28,... | collective-permute-start | bytes 3145736 | tf_op jit(solution)/shard_map/ppermute | solution.py:120
  184.9 91.1 %collective-permute-start.5 = (bf16[2048,512]{0,1:T(8,128)(2,1)}, bf16[2048,512]{0,1:T(8,128)(2,1)}, u32[]{:S(2)}, u32[]{:S(2)}) collective-permute-start(bf16[2048,512]{0,1:T(8,128)(2,1)} %collective-permute-done.1), channel_id=1, source_target_pairs={{4,20},{8,24},{20,4},{24,8},{5,21},{9,25},{21,5},{25,9},{6,22},{10... | collective-permute-start | bytes 6291464 | tf_op jit(solution)/shard_map/ppermute | solution.py:113
  187.0 90.5 %collective-permute-start.4 = (bf16[2048,512]{0,1:T(8,128)(2,1)}, bf16[2048,512]{0,1:T(8,128)(2,1)}, u32[]{:S(2)}, u32[]{:S(2)}) collective-permute-start(bf16[2048,512]{0,1:T(8,128)(2,1)} %collective-permute-done), channel_id=1, source_target_pairs={{4,20},{8,24},{20,4},{24,8},{5,21},{9,25},{21,5},{25,9},{6,22},{10... | collective-permute-start | bytes 6291464 | tf_op jit(solution)/shard_map/ppermute | solution.py:113
  189.0 91.9 %collective-permute-start.6 = (bf16[2048,512]{0,1:T(8,128)(2,1)}, bf16[2048,512]{0,1:T(8,128)(2,1)}, u32[]{:S(2)}, u32[]{:S(2)}) collective-permute-start(bf16[2048,512]{0,1:T(8,128)(2,1)} %collective-permute-done.2), channel_id=1, source_target_pairs={{4,20},{8,24},{20,4},{24,8},{5,21},{9,25},{21,5},{25,9},{6,22},{10... | collective-permute-start | bytes 6291464 | tf_op jit(solution)/shard_map/ppermute | solution.py:113
  225.2 54.0 %collective-permute-start.7 = (bf16[2048,512]{0,1:T(8,128)(2,1)}, bf16[2048,512]{0,1:T(8,128)(2,1)}, u32[]{:S(2)}, u32[]{:S(2)}) collective-permute-start(bf16[2048,512]{0,1:T(8,128)(2,1)} %collective-permute-done.3), channel_id=1, source_target_pairs={{4,20},{8,24},{20,4},{24,8},{5,21},{9,25},{21,5},{25,9},{6,22},{10... | collective-permute-start | bytes 6291464 | tf_op jit(solution)/shard_map/ppermute | solution.py:113
  245.6 25.0 %collective-permute-start.25 = (bf16[64,8192]{1,0:T(8,128)(2,1)S(1)}, bf16[64,8192]{1,0:T(8,128)(2,1)S(1)}, u32[]{:S(2)}, u32[]{:S(2)}) collective-permute-start(bf16[64,8192]{1,0:T(8,128)(2,1)S(1)} %copy-done.6), channel_id=1, source_target_pairs={{0,4},{12,8},{1,5},{13,9},{2,6},{14,10},{3,7},{15,11},{16,20},{28,... | collective-permute-start | bytes 3145736 | tf_op jit(solution)/shard_map/ppermute | solution.py:120
  270.6 28.0 %collective-permute-start.34 = (bf16[64,8192]{1,0:T(8,128)(2,1)S(1)}, bf16[64,8192]{1,0:T(8,128)(2,1)}, u32[]{:S(2)}, u32[]{:S(2)}) collective-permute-start(bf16[64,8192]{1,0:T(8,128)(2,1)S(1)} %copy-done.5), channel_id=1, source_target_pairs={{0,4},{12,8},{1,5},{13,9},{2,6},{14,10},{3,7},{15,11},{16,20},{28,... | collective-permute-start | bytes 3145736 | tf_op jit(solution)/shard_map/ppermute | solution.py:120
  276.0 103.1 %collective-permute-start.43 = (bf16[64,8192]{1,0:T(8,128)(2,1)S(1)}, bf16[64,8192]{1,0:T(8,128)(2,1)S(1)}, u32[]{:S(2)}, u32[]{:S(2)}) collective-permute-start(bf16[64,8192]{1,0:T(8,128)(2,1)S(1)} %copy-done.4), channel_id=1, source_target_pairs={{0,4},{12,8},{1,5},{13,9},{2,6},{14,10},{3,7},{15,11},{16,20},{28,... | collective-permute-start | bytes 3145736 | tf_op jit(solution)/shard_map/ppermute | solution.py:120
  277.5 103.0 %collective-permute-start.17 = (bf16[64,8192]{1,0:T(8,128)(2,1)}, bf16[64,8192]{1,0:T(8,128)(2,1)}, u32[]{:S(2)}, u32[]{:S(2)}) collective-permute-start(bf16[64,8192]{1,0:T(8,128)(2,1)} %copy-done.24), channel_id=1, source_target_pairs={{4,8},{8,4},{5,9},{9,5},{6,10},{10,6},{7,11},{11,7},{20,24},{24,20... | collective-permute-start | bytes 3145736 | tf_op jit(solution)/shard_map/ppermute | solution.py:122
  279.2 123.3 %collective-permute-start.26 = (bf16[64,8192]{1,0:T(8,128)(2,1)}, bf16[64,8192]{1,0:T(8,128)(2,1)}, u32[]{:S(2)}, u32[]{:S(2)}) collective-permute-start(bf16[64,8192]{1,0:T(8,128)(2,1)} %copy-done.26), channel_id=1, source_target_pairs={{4,8},{8,4},{5,9},{9,5},{6,10},{10,6},{7,11},{11,7},{20,24},{24,20... | collective-permute-start | bytes 3145736 | tf_op jit(solution)/shard_map/ppermute | solution.py:122
  298.6 136.8 %collective-permute-start.52 = (bf16[64,8192]{1,0:T(8,128)(2,1)S(1)}, bf16[64,8192]{1,0:T(8,128)(2,1)}, u32[]{:S(2)}, u32[]{:S(2)}) collective-permute-start(bf16[64,8192]{1,0:T(8,128)(2,1)S(1)} %copy-done.3), channel_id=1, source_target_pairs={{0,4},{12,8},{1,5},{13,9},{2,6},{14,10},{3,7},{15,11},{16,20},{28,... | collective-permute-start | bytes 3145736 | tf_op jit(solution)/shard_map/ppermute | solution.py:120
  379.2 58.9 %collective-permute-start.61 = (bf16[64,8192]{1,0:T(8,128)(2,1)S(1)}, bf16[64,8192]{1,0:T(8,128)(2,1)S(1)}, u32[]{:S(2)}, u32[]{:S(2)}) collective-permute-start(bf16[64,8192]{1,0:T(8,128)(2,1)S(1)} %get-tuple-element.21), channel_id=1, source_target_pairs={{0,4},{12,8},{1,5},{13,9},{2,6},{14,10},{3,7},{15,11},{16,20},{28,... | collective-permute-start | bytes 3145736 | tf_op jit(solution)/shard_map/ppermute | solution.py:120
  400.9 22.0 %collective-permute-start.20 = (bf16[32,2048]{1,0:T(8,128)(2,1)S(1)}, bf16[32,2048]{1,0:T(8,128)(2,1)S(1)}, u32[]{:S(2)}, u32[]{:S(2)}) collective-permute-start(bf16[32,2048]{1,0:T(8,128)(2,1)S(1)} %get-tuple-element.77), channel_id=1, source_target_pairs={{0,3},{1,2},{2,1},{3,0},{4,7},{5,6},{6,5},{7,4},{8,11},{9,10},{10,... | collective-permute-start | bytes 393224 | tf_op jit(solution)/shard_map/ppermute | solution.py:146
  401.0 23.1 %collective-permute-start.19 = (bf16[32,2048]{1,0:T(8,128)(2,1)S(1)}, bf16[32,2048]{1,0:T(8,128)(2,1)S(1)}, u32[]{:S(2)}, u32[]{:S(2)}) collective-permute-start(bf16[32,2048]{1,0:T(8,128)(2,1)S(1)} %get-tuple-element.78), channel_id=1, source_target_pairs={{0,2},{1,3},{2,0},{3,1},{4,6},{5,7},{6,4},{7,5},{8,10},{9,11},{10,... | collective-permute-start | bytes 393224 | tf_op jit(solution)/shard_map/ppermute | solution.py:146
  402.5 22.3 %collective-permute-start.18 = (bf16[32,2048]{1,0:T(8,128)(2,1)S(1)}, bf16[32,2048]{1,0:T(8,128)(2,1)S(1)}, u32[]{:S(2)}, u32[]{:S(2)}) collective-permute-start(bf16[32,2048]{1,0:T(8,128)(2,1)S(1)} %get-tuple-element.76), channel_id=1, source_target_pairs={{0,1},{1,0},{2,3},{3,2},{4,5},{5,4},{6,7},{7,6},{8,9},{9,8},{10,11... | collective-permute-start | bytes 393224 | tf_op jit(solution)/shard_map/ppermute | solution.py:146
  422.9 5.5 collective-permute-start.29
  424.0 8.4 collective-permute-start.28
  424.8 13.3 %collective-permute-start.35 = (bf16[64,8192]{1,0:T(8,128)(2,1)}, bf16[64,8192]{1,0:T(8,128)(2,1)S(1)}, u32[]{:S(2)}, u32[]{:S(2)}) collective-permute-start(bf16[64,8192]{1,0:T(8,128)(2,1)} %collective-permute-done.34), channel_id=1, source_target_pairs={{4,8},{8,4},{5,9},{9,5},{6,10},{10,6},{7,11},{11,7},{20,24},{24,20... | collective-permute-start | bytes 3145736 | tf_op jit(solution)/shard_map/ppermute | solution.py:122
  428.4 247.2 %collective-permute-start.8 = (bf16[4,128,8192]{2,1,0:T(8,128)(2,1)S(1)}, bf16[4,128,8192]{2,1,0:T(8,128)(2,1)}, u32[]{:S(2)}, u32[]{:S(2)}) collective-permute-start(bf16[4,128,8192]{2,1,0:T(8,128)(2,1)S(1)} %bitcast.431), channel_id=1, source_target_pairs={{4,8},{8,4},{5,9},{9,5},{6,10},{10,6},{7,11},{11,7},{20,24},{24,20... | collective-permute-start | bytes 25165832 | tf_op jit(solution)/shard_map/ppermute | solution.py:102
  433.9 26.5 %collective-permute-start.44 = (bf16[64,8192]{1,0:T(8,128)(2,1)S(1)}, bf16[64,8192]{1,0:T(8,128)(2,1)S(1)}, u32[]{:S(2)}, u32[]{:S(2)}) collective-permute-start(bf16[64,8192]{1,0:T(8,128)(2,1)S(1)} %copy-done.23), channel_id=1, source_target_pairs={{4,8},{8,4},{5,9},{9,5},{6,10},{10,6},{7,11},{11,7},{20,24},{24,20... | collective-permute-start | bytes 3145736 | tf_op jit(solution)/shard_map/ppermute | solution.py:122
  435.4 321.3 %collective-permute-start.70 = (bf16[64,8192]{1,0:T(8,128)(2,1)}, bf16[64,8192]{1,0:T(8,128)(2,1)}, u32[]{:S(2)}, u32[]{:S(2)}) collective-permute-start(bf16[64,8192]{1,0:T(8,128)(2,1)} %get-tuple-element.22), channel_id=1, source_target_pairs={{0,4},{12,8},{1,5},{13,9},{2,6},{14,10},{3,7},{15,11},{16,20},{28,... | collective-permute-start | bytes 3145736 | tf_op jit(solution)/shard_map/ppermute | solution.py:120
  458.4 21.1 %collective-permute-start.38 = (bf16[32,2048]{1,0:T(8,128)(2,1)S(1)}, bf16[32,2048]{1,0:T(8,128)(2,1)S(1)}, u32[]{:S(2)}, u32[]{:S(2)}) collective-permute-start(bf16[32,2048]{1,0:T(8,128)(2,1)S(1)} %get-tuple-element.83), channel_id=1, source_target_pairs={{0,3},{1,2},{2,1},{3,0},{4,7},{5,6},{6,5},{7,4},{8,11},{9,10},{10,... | collective-permute-start | bytes 393224 | tf_op jit(solution)/shard_map/ppermute | solution.py:146
  459.8 213.9 %collective-permute-start.37 = (bf16[32,2048]{1,0:T(8,128)(2,1)S(1)}, bf16[32,2048]{1,0:T(8,128)(2,1)S(1)}, u32[]{:S(2)}, u32[]{:S(2)}) collective-permute-start(bf16[32,2048]{1,0:T(8,128)(2,1)S(1)} %get-tuple-element.84), channel_id=1, source_target_pairs={{0,2},{1,3},{2,0},{3,1},{4,6},{5,7},{6,4},{7,5},{8,10},{9,11},{10,... | collective-permute-start | bytes 393224 | tf_op jit(solution)/shard_map/ppermute | solution.py:146
  460.4 214.6 %collective-permute-start.36 = (bf16[32,2048]{1,0:T(8,128)(2,1)S(1)}, bf16[32,2048]{1,0:T(8,128)(2,1)S(1)}, u32[]{:S(2)}, u32[]{:S(2)}) collective-permute-start(bf16[32,2048]{1,0:T(8,128)(2,1)S(1)} %get-tuple-element.82), channel_id=1, source_target_pairs={{0,1},{1,0},{2,3},{3,2},{4,5},{5,4},{6,7},{7,6},{8,9},{9,8},{10,11... | collective-permute-start | bytes 393224 | tf_op jit(solution)/shard_map/ppermute | solution.py:146
  479.5 278.8 %collective-permute-start.79 = (bf16[64,8192]{1,0:T(8,128)(2,1)S(1)}, bf16[64,8192]{1,0:T(8,128)(2,1)S(1)}, u32[]{:S(2)}, u32[]{:S(2)}) collective-permute-start(bf16[64,8192]{1,0:T(8,128)(2,1)S(1)} %copy-done.2), channel_id=1, source_target_pairs={{0,4},{12,8},{1,5},{13,9},{2,6},{14,10},{3,7},{15,11},{16,20},{28,... | collective-permute-start | bytes 3145736 | tf_op jit(solution)/shard_map/ppermute | solution.py:120
  673.6 81.0 %collective-permute-start.47 = (bf16[32,2048]{1,0:T(8,128)(2,1)S(1)}, bf16[32,2048]{1,0:T(8,128)(2,1)S(1)}, u32[]{:S(2)}, u32[]{:S(2)}) collective-permute-start(bf16[32,2048]{1,0:T(8,128)(2,1)S(1)} %get-tuple-element.80), channel_id=1, source_target_pairs={{0,3},{1,2},{2,1},{3,0},{4,7},{5,6},{6,5},{7,4},{8,11},{9,10},{10,... | collective-permute-start | bytes 393224 | tf_op jit(solution)/shard_map/ppermute | solution.py:146
  675.0 81.0 %collective-permute-start.46 = (bf16[32,2048]{1,0:T(8,128)(2,1)S(1)}, bf16[32,2048]{1,0:T(8,128)(2,1)S(1)}, u32[]{:S(2)}, u32[]{:S(2)}) collective-permute-start(bf16[32,2048]{1,0:T(8,128)(2,1)S(1)} %get-tuple-element.81), channel_id=1, source_target_pairs={{0,2},{1,3},{2,0},{3,1},{4,6},{5,7},{6,4},{7,5},{8,10},{9,11},{10,... | collective-permute-start | bytes 393224 | tf_op jit(solution)/shard_map/ppermute | solution.py:146
  675.6 35.5 %collective-permute-start.53 = (bf16[64,8192]{1,0:T(8,128)(2,1)}, bf16[64,8192]{1,0:T(8,128)(2,1)S(1)}, u32[]{:S(2)}, u32[]{:S(2)}) collective-permute-start(bf16[64,8192]{1,0:T(8,128)(2,1)} %collective-permute-done.52), channel_id=1, source_target_pairs={{4,8},{8,4},{5,9},{9,5},{6,10},{10,6},{7,11},{11,7},{20,24},{24,20... | collective-permute-start | bytes 3145736 | tf_op jit(solution)/shard_map/ppermute | solution.py:122
  712.0 9.4 collective-permute-start.62
  721.4 35.2 %collective-permute-start.45 = (bf16[32,2048]{1,0:T(8,128)(2,1)S(1)}, bf16[32,2048]{1,0:T(8,128)(2,1)S(1)}, u32[]{:S(2)}, u32[]{:S(2)}) collective-permute-start(bf16[32,2048]{1,0:T(8,128)(2,1)S(1)} %get-tuple-element.79), channel_id=1, source_target_pairs={{0,1},{1,0},{2,3},{3,2},{4,5},{5,4},{6,7},{7,6},{8,9},{9,8},{10,11... | collective-permute-start | bytes 393224 | tf_op jit(solution)/shard_map/ppermute | solution.py:146
  754.7 5.6 collective-permute-start.56
  756.0 7.6 collective-permute-start.55
  756.6 7.7 collective-permute-start.54
  756.7 59.8 %collective-permute-start.11 = (bf16[256,2048]{1,0:T(8,128)(2,1)S(1)}, bf16[256,2048]{1,0:T(8,128)(2,1)S(1)}, u32[]{:S(2)}, u32[]{:S(2)}) collective-permute-start(bf16[256,2048]{1,0:T(8,128)(2,1)S(1)} %get-tuple-element.55), channel_id=1, source_target_pairs={{0,3},{1,2},{2,1},{3,0},{4,7},{5,6},{6,5},{7,4},{8,11},{9,10},{10,... | collective-permute-start | bytes 3145736 | tf_op jit(solution)/shard_map/ppermute | solution.py:146
  758.3 58.2 %collective-permute-start.10 = (bf16[256,2048]{1,0:T(8,128)(2,1)S(1)}, bf16[256,2048]{1,0:T(8,128)(2,1)S(1)}, u32[]{:S(2)}, u32[]{:S(2)}) collective-permute-start(bf16[256,2048]{1,0:T(8,128)(2,1)S(1)} %get-tuple-element.56), channel_id=1, source_target_pairs={{0,2},{1,3},{2,0},{3,1},{4,6},{5,7},{6,4},{7,5},{8,10},{9,11},{10,... | collective-permute-start | bytes 3145736 | tf_op jit(solution)/shard_map/ppermute | solution.py:146
  760.3 56.2 %collective-permute-start.9 = (bf16[256,2048]{1,0:T(8,128)(2,1)S(1)}, bf16[256,2048]{1,0:T(8,128)(2,1)S(1)}, u32[]{:S(2)}, u32[]{:S(2)}) collective-permute-start(bf16[256,2048]{1,0:T(8,128)(2,1)S(1)} %get-tuple-element.54), channel_id=1, source_target_pairs={{0,1},{1,0},{2,3},{3,2},{4,5},{5,4},{6,7},{7,6},{8,9},{9,8},{10,11... | collective-permute-start | bytes 3145736 | tf_op jit(solution)/shard_map/ppermute | solution.py:146
  763.6 47.2 %collective-permute-start.65 = (bf16[32,2048]{1,0:T(8,128)(2,1)S(1)}, bf16[32,2048]{1,0:T(8,128)(2,1)S(1)}, u32[]{:S(2)}, u32[]{:S(2)}) collective-permute-start(bf16[32,2048]{1,0:T(8,128)(2,1)S(1)} %get-tuple-element.86), channel_id=1, source_target_pairs={{0,3},{1,2},{2,1},{3,0},{4,7},{5,6},{6,5},{7,4},{8,11},{9,10},{10,... | collective-permute-start | bytes 393224 | tf_op jit(solution)/shard_map/ppermute | solution.py:146
  764.3 49.6 %collective-permute-start.64 = (bf16[32,2048]{1,0:T(8,128)(2,1)S(1)}, bf16[32,2048]{1,0:T(8,128)(2,1)S(1)}, u32[]{:S(2)}, u32[]{:S(2)}) collective-permute-start(bf16[32,2048]{1,0:T(8,128)(2,1)S(1)} %get-tuple-element.87), channel_id=1, source_target_pairs={{0,2},{1,3},{2,0},{3,1},{4,6},{5,7},{6,4},{7,5},{8,10},{9,11},{10,... | collective-permute-start | bytes 393224 | tf_op jit(solution)/shard_map/ppermute | solution.py:146
  814.7 21.1 %collective-permute-start.80 = (bf16[64,8192]{1,0:T(8,128)(2,1)}, bf16[64,8192]{1,0:T(8,128)(2,1)}, u32[]{:S(2)}, u32[]{:S(2)}) collective-permute-start(bf16[64,8192]{1,0:T(8,128)(2,1)} %copy-done.18), channel_id=1, source_target_pairs={{4,8},{8,4},{5,9},{9,5},{6,10},{10,6},{7,11},{11,7},{20,24},{24,20... | collective-permute-start | bytes 3145736 | tf_op jit(solution)/shard_map/ppermute | solution.py:122
  817.3 35.8 %collective-permute-start.12 = (bf16[256,1024]{1,0:T(8,128)(2,1)S(1)}, bf16[256,1024]{1,0:T(8,128)(2,1)S(1)}, u32[]{:S(2)}, u32[]{:S(2)}) collective-permute-start(bf16[256,1024]{1,0:T(8,128)(2,1)S(1)} %slice.290), channel_id=1, source_target_pairs={{4,0},{8,12},{5,1},{9,13},{6,2},{10,14},{7,3},{11,15},{20,16},{24,... | collective-permute-start | bytes 1572872 | tf_op jit(solution)/shard_map/ppermute | solution.py:148
  834.0 19.8 %collective-permute-start.74 = (bf16[32,2048]{1,0:T(8,128)(2,1)S(1)}, bf16[32,2048]{1,0:T(8,128)(2,1)S(1)}, u32[]{:S(2)}, u32[]{:S(2)}) collective-permute-start(bf16[32,2048]{1,0:T(8,128)(2,1)S(1)} %get-tuple-element.95), channel_id=1, source_target_pairs={{0,3},{1,2},{2,1},{3,0},{4,7},{5,6},{6,5},{7,4},{8,11},{9,10},{10,... | collective-permute-start | bytes 393224 | tf_op jit(solution)/shard_map/ppermute | solution.py:146
  834.9 18.9 %collective-permute-start.73 = (bf16[32,2048]{1,0:T(8,128)(2,1)S(1)}, bf16[32,2048]{1,0:T(8,128)(2,1)S(1)}, u32[]{:S(2)}, u32[]{:S(2)}) collective-permute-start(bf16[32,2048]{1,0:T(8,128)(2,1)S(1)} %get-tuple-element.96), channel_id=1, source_target_pairs={{0,2},{1,3},{2,0},{3,1},{4,6},{5,7},{6,4},{7,5},{8,10},{9,11},{10,... | collective-permute-start | bytes 393224 | tf_op jit(solution)/shard_map/ppermute | solution.py:146
  835.6 19.8 %collective-permute-start.72 = (bf16[32,2048]{1,0:T(8,128)(2,1)S(1)}, bf16[32,2048]{1,0:T(8,128)(2,1)S(1)}, u32[]{:S(2)}, u32[]{:S(2)}) collective-permute-start(bf16[32,2048]{1,0:T(8,128)(2,1)S(1)} %get-tuple-element.94), channel_id=1, source_target_pairs={{0,1},{1,0},{2,3},{3,2},{4,5},{5,4},{6,7},{7,6},{8,9},{9,8},{10,11... | collective-permute-start | bytes 393224 | tf_op jit(solution)/shard_map/ppermute | solution.py:146
  851.8 5.6 collective-permute-start.83
  853.0 7.7 collective-permute-start.82
  853.7 8.3 collective-permute-start.81
  853.8 17.5 %collective-permute-start.15 = (bf16[256,1024]{1,0:T(8,128)(2,1)S(1)}, bf16[256,1024]{1,0:T(8,128)(2,1)S(1)}, u32[]{:S(2)}, u32[]{:S(2)}) collective-permute-start(bf16[256,1024]{1,0:T(8,128)(2,1)S(1)} %slice_select_fusion), channel_id=1, source_target_pairs={{0,3},{1,2},{2,1},{3,0},{4,7},{5,6},{6,5},{7,4},{8,11},{9,10},{10,... | collective-permute-start | bytes 1572872 | tf_op jit(solution)/shard_map/ppermute | solution.py:151
  855.4 27.5 %collective-permute-start.14 = (bf16[256,1024]{1,0:T(8,128)(2,1)S(1)}, bf16[256,1024]{1,0:T(8,128)(2,1)S(1)}, u32[]{:S(2)}, u32[]{:S(2)}) collective-permute-start(bf16[256,1024]{1,0:T(8,128)(2,1)S(1)} %slice_select_fusion), channel_id=1, source_target_pairs={{0,2},{1,3},{2,0},{3,1},{4,6},{5,7},{6,4},{7,5},{8,10},{9,11},{10,... | collective-permute-start | bytes 1572872 | tf_op jit(solution)/shard_map/ppermute | solution.py:151
  857.3 26.9 %collective-permute-start.13 = (bf16[256,1024]{1,0:T(8,128)(2,1)S(1)}, bf16[256,1024]{1,0:T(8,128)(2,1)S(1)}, u32[]{:S(2)}, u32[]{:S(2)}) collective-permute-start(bf16[256,1024]{1,0:T(8,128)(2,1)S(1)} %slice_select_fusion), channel_id=1, source_target_pairs={{0,1},{1,0},{2,3},{3,2},{4,5},{5,4},{6,7},{7,6},{8,9},{9,8},{10,11... | collective-permute-start | bytes 1572872 | tf_op jit(solution)/shard_map/ppermute | solution.py:151
  860.7 82.1 %collective-permute-start.21 = (bf16[32,1024]{1,0:T(8,128)(2,1)S(1)}, bf16[32,1024]{1,0:T(8,128)(2,1)S(1)}, u32[]{:S(2)}, u32[]{:S(2)}) collective-permute-start(bf16[32,1024]{1,0:T(8,128)(2,1)S(1)} %copy-done.13), channel_id=1, source_target_pairs={{4,0},{8,12},{5,1},{9,13},{6,2},{10,14},{7,3},{11,15},{20,16},{24,... | collective-permute-start | bytes 196616 | tf_op jit(solution)/shard_map/ppermute | solution.py:148
  862.0 106.1 %collective-permute-start.30 = (bf16[32,1024]{1,0:T(8,128)(2,1)S(1)}, bf16[32,1024]{1,0:T(8,128)(2,1)S(1)}, u32[]{:S(2)}, u32[]{:S(2)}) collective-permute-start(bf16[32,1024]{1,0:T(8,128)(2,1)S(1)} %copy-done.12), channel_id=1, source_target_pairs={{4,0},{8,12},{5,1},{9,13},{6,2},{10,14},{7,3},{11,15},{20,16},{24,... | collective-permute-start | bytes 196616 | tf_op jit(solution)/shard_map/ppermute | solution.py:148
  871.4 69.8 %collective-permute-start.39 = (bf16[32,1024]{1,0:T(8,128)(2,1)S(1)}, bf16[32,1024]{1,0:T(8,128)(2,1)S(1)}, u32[]{:S(2)}, u32[]{:S(2)}) collective-permute-start(bf16[32,1024]{1,0:T(8,128)(2,1)S(1)} %slice.298), channel_id=1, source_target_pairs={{4,0},{8,12},{5,1},{9,13},{6,2},{10,14},{7,3},{11,15},{20,16},{24,... | collective-permute-start | bytes 196616 | tf_op jit(solution)/shard_map/ppermute | solution.py:148
  882.9 81.0 %collective-permute-start.48 = (bf16[32,1024]{1,0:T(8,128)(2,1)S(1)}, bf16[32,1024]{1,0:T(8,128)(2,1)S(1)}, u32[]{:S(2)}, u32[]{:S(2)}) collective-permute-start(bf16[32,1024]{1,0:T(8,128)(2,1)S(1)} %slice.300), channel_id=1, source_target_pairs={{4,0},{8,12},{5,1},{9,13},{6,2},{10,14},{7,3},{11,15},{20,16},{24,... | collective-permute-start | bytes 196616 | tf_op jit(solution)/shard_map/ppermute | solution.py:148
  884.2 49.4 %collective-permute-start.75 = (bf16[32,1024]{1,0:T(8,128)(2,1)S(1)}, bf16[32,1024]{1,0:T(8,128)(2,1)S(1)}, u32[]{:S(2)}, u32[]{:S(2)}) collective-permute-start(bf16[32,1024]{1,0:T(8,128)(2,1)S(1)} %slice.308), channel_id=1, source_target_pairs={{4,0},{8,12},{5,1},{9,13},{6,2},{10,14},{7,3},{11,15},{20,16},{24,... | collective-permute-start | bytes 196616 | tf_op jit(solution)/shard_map/ppermute | solution.py:148
  933.6 6.1 collective-permute-start.57
  939.8 18.9 %collective-permute-start.66 = (bf16[32,1024]{1,0:T(8,128)(2,1)S(1)}, bf16[32,1024]{1,0:T(8,128)(2,1)S(1)}, u32[]{:S(2)}, u32[]{:S(2)}) collective-permute-start(bf16[32,1024]{1,0:T(8,128)(2,1)S(1)} %slice.305), channel_id=1, source_target_pairs={{4,0},{8,12},{5,1},{9,13},{6,2},{10,14},{7,3},{11,15},{20,16},{24,... | collective-permute-start | bytes 196616 | tf_op jit(solution)/shard_map/ppermute | solution.py:148
  941.2 11.0 %collective-permute-start.84 = (bf16[32,1024]{1,0:T(8,128)(2,1)S(1)}, bf16[32,1024]{1,0:T(8,128)(2,1)S(1)}, u32[]{:S(2)}, u32[]{:S(2)}) collective-permute-start(bf16[32,1024]{1,0:T(8,128)(2,1)S(1)} %slice.310), channel_id=1, source_target_pairs={{4,0},{8,12},{5,1},{9,13},{6,2},{10,14},{7,3},{11,15},{20,16},{24,... | collective-permute-start | bytes 196616 | tf_op jit(solution)/shard_map/ppermute | solution.py:148
  959.4 5.2 collective-permute-start.22
  963.9 5.4 collective-permute-start.85
  (60 other events, 1053.3 us)
Sparse Core Ops, SparseCore 0:
  38.5 42.1 all-gather.2

commit v2 on v0

v2 whole, which is shorter than its diff:
```python
import functools

import jax
import jax.numpy as jnp
from jax import lax
from jax.experimental import pallas as pl
from jax.experimental.pallas import tpu as pltpu
from jax.sharding import PartitionSpec as P

DAMPING = 0.05
BF16 = jnp.bfloat16
F32 = jnp.float32


def candidate_lengths(example_ids, token_counts):
    pool_size = token_counts.shape[0]
    hits = example_ids[:, None] == jnp.arange(pool_size, dtype=jnp.int32)[None, :]
    return jnp.sum(jnp.where(hits, token_counts[None, :], 0), axis=1)


def local_activations(acts, act_basis, lengths):
    tok = acts.shape[1]
    positions = lax.axis_index("row") * tok + jnp.arange(tok, dtype=jnp.int32)
    live = (positions[None, :] < lengths[:, None]).astype(F32)
    rotated = jnp.einsum("ctd,dk->ctk", acts, act_basis, preferred_element_type=F32)
    return (rotated * live[:, :, None]).astype(BF16)


def final_kernel(counts, *refs):
    total = sum(counts)
    pieces = list(refs[:total])
    act_ref, eig_ref, query_ref, out_ref, score_ref = refs[total:]
    cands, queries = len(counts), query_ref.shape[0]
    damped = eig_ref[...] + DAMPING
    weights = [query_ref[q].astype(F32) / damped for q in range(queries)]
    rows = [[] for _ in range(queries)]
    for c in range(cands):
        tile, start = None, 0
        for _ in range(counts[c]):
            piece = pieces.pop(0)
            n = piece.shape[0]
            term = lax.dot_general(
                piece[...],
                act_ref[c, start : start + n],
                (((0,), (0,)), ((), ())),
                preferred_element_type=F32,
            )
            tile = term if tile is None else tile + term
            start += n
        out_ref[c] = tile
        for q in range(queries):
            rows[q].append(jnp.sum(weights[q] * tile, axis=0, keepdims=True))
    score_ref[0] = jnp.concatenate([r for one in rows for r in one], axis=0)


def rotate_and_score(pieces, act_rot, eigenvalues, query_rotated):
    counts = tuple(len(p) for p in pieces)
    flat = [x for p in pieces for x in p]
    cands, seq, width = act_rot.shape
    dirs = eigenvalues.shape[0]
    queries = query_rotated.shape[0]
    block = min(dirs, 256)
    steps = dirs // block
    rotated, partial_scores = pl.pallas_call(
        functools.partial(final_kernel, counts),
        grid=(steps,),
        in_specs=[pl.BlockSpec((x.shape[0], block), lambda i: (0, i)) for x in flat]
        + [
            pl.BlockSpec((cands, seq, width), lambda i: (0, 0, 0)),
            pl.BlockSpec((block, width), lambda i: (i, 0)),
            pl.BlockSpec((queries, block, width), lambda i: (0, i, 0)),
        ],
        out_specs=[
            pl.BlockSpec((cands, block, width), lambda i: (0, i, 0)),
            pl.BlockSpec((1, queries * cands, width), lambda i: (i, 0, 0)),
        ],
        out_shape=[
            jax.ShapeDtypeStruct((cands, dirs, width), F32),
            jax.ShapeDtypeStruct((steps, queries * cands, width), F32),
        ],
        compiler_params=pltpu.CompilerParams(vmem_limit_bytes=32 * 2**20),
    )(*flat, act_rot, eigenvalues, query_rotated)
    return rotated, jnp.sum(partial_scores, axis=(0, 2)).reshape(queries, cands)


def gather_body(acts, grads, act_basis, grad_basis, eigenvalues, query_rotated, example_ids, token_counts):
    lengths = candidate_lengths(example_ids, token_counts)
    local_act = local_activations(acts, act_basis, lengths)
    partial_value = jnp.einsum(
        "ctd,dj->ctj",
        lax.all_gather(grads, "row", axis=1, tiled=True),
        grad_basis,
        preferred_element_type=F32,
    )
    every_act = lax.all_gather(local_act, "row", axis=1, tiled=True)
    rotated_grads = lax.psum(partial_value, "col").astype(BF16)
    pieces = [[rotated_grads[c]] for c in range(acts.shape[0])]
    rotated, scores = rotate_and_score(pieces, every_act, eigenvalues, query_rotated)
    return rotated, lax.psum(scores, ("row", "col"))


def after(value, *earlier):
    return lax.optimization_barrier((value, *earlier))[0]


def project_kernel(count, *refs):
    tokens = refs[:count]
    own_ref, near_ref, far_ref, out_own, out_end, acc_own, acc_end = refs[count:]
    step = pl.program_id(0)

    @pl.when(step == 0)
    def _():
        acc_own[...] = jnp.zeros_like(acc_own)
        acc_end[...] = jnp.zeros_like(acc_end)

    rows = jnp.concatenate([t[...] for t in tokens], axis=0)
    half = near_ref.shape[1]
    acc_own[...] += jnp.dot(rows, own_ref[...], preferred_element_type=F32)
    acc_end[:, :half] += jnp.dot(rows, near_ref[...], preferred_element_type=F32)
    acc_end[:, half:] += jnp.dot(rows, far_ref[...], preferred_element_type=F32)

    @pl.when(step == pl.num_programs(0) - 1)
    def _():
        out_own[...] = acc_own[...].astype(BF16)
        out_end[...] = acc_end[...].astype(BF16)


def project(tokens, own, near, far):
    feats, dirs = own.shape
    block = 1024
    specs, total = [], 0
    for array, index in tokens:
        n = array.shape[-2]
        total += n
        if index is None:
            specs.append(pl.BlockSpec((n, block), lambda k: (0, k)))
        else:
            specs.append(pl.BlockSpec((None, n, block), lambda k, index=index: (index, 0, k)))
    half = near.shape[1]
    return pl.pallas_call(
        functools.partial(project_kernel, len(tokens)),
        grid=(feats // block,),
        in_specs=specs
        + [
            pl.BlockSpec((block, dirs), lambda k: (k, 0)),
            pl.BlockSpec((block, half), lambda k: (k, 0)),
            pl.BlockSpec((block, half), lambda k: (k, 0)),
        ],
        out_specs=[pl.BlockSpec((total, dirs), lambda k: (0, 0))] * 2,
        out_shape=[jax.ShapeDtypeStruct((total, dirs), BF16)] * 2,
        scratch_shapes=[pltpu.VMEM((total, dirs), F32)] * 2,
        compiler_params=pltpu.CompilerParams(vmem_limit_bytes=40 * 2**20),
        cost_estimate=pl.CostEstimate(
            flops=4 * total * feats * dirs,
            bytes_accessed=4 * feats * dirs + 2 * total * feats,
            transcendentals=0,
        ),
    )(*[array for array, _ in tokens], own, near, far)


def after(value, *earlier):
    return lax.optimization_barrier((value, *earlier))[0]


def exchange_sum(value, axis, size):
    total = value
    for d in range(1, size):
        total = total + lax.ppermute(value, axis, [(i, i ^ d) for i in range(size)])
    return total


def chain_body(acts, grads, act_basis, grad_basis, eigenvalues, query_rotated, example_ids, token_counts):
    cands, tok, feats = grads.shape
    dirs = grad_basis.shape[1]
    group, row = lax.axis_index("groups"), lax.axis_index("row")
    sides, planes, parts = 2, 4, 4
    inward = [(0, 1), (3, 2)]
    across = [(1, 2), (2, 1)]
    outward = [(1, 0), (2, 3)]
    swap = [(g * planes + r, (1 - g) * planes + r) for g in range(sides) for r in (1, 2)]
    at_end = (row == 0) | (row == planes - 1)

    lengths = candidate_lengths(example_ids, token_counts)
    local_act = local_activations(acts, act_basis, lengths)
    every_act = lax.all_gather(local_act, "row", axis=0)

    half = dirs // sides
    pieces = 8
    deep = feats // pieces
    half_cands = cands // 2
    other, near, far = [], [], []
    spans = [(0, 1), (1, 3), (3, 5), (5, 7), (7, 8)]
    for i, (a, b) in enumerate(spans):
        piece = lax.dynamic_slice(grad_basis, (a * deep, group * half), ((b - a) * deep, half))
        if i >= 2:
            piece = after(piece, near[i - 2], *other)
        near.append(lax.ppermute(piece, "row", inward))
        far.append(lax.ppermute(near[i], ("groups", "row"), swap))
        if i in (0, 2):
            part = grads[:half_cands] if i == 0 else grads[half_cands:]
            other.append(lax.ppermute(part if i == 0 else after(part, near[0]), "row", across))

    chunk = tok // 2
    started = list(near)
    first, second = [], []
    for c in range(cands):
        for s in range(0, tok, chunk):
            piece = after(grads[c, s : s + chunk], started[-2], *other)
            first.append(lax.ppermute(piece, "row", inward))
            started.append(first[-1])
            second.append(lax.ppermute(first[-1], "row", across))

    near_basis = jnp.concatenate(near, axis=0)
    far_basis = jnp.concatenate(far, axis=0)

    def reduce(tokens):
        own, end = project(tokens, grad_basis, near_basis, far_basis)
        back = lax.ppermute(end, "row", outward)
        swapped = jnp.concatenate([back[:, half:], back[:, :half]], axis=1)
        mine = jnp.where(at_end, jnp.where(group == 0, back, swapped), own)
        total = mine.astype(F32)
        for d in range(1, parts):
            total = total + lax.ppermute(mine, "col", [(i, i ^ d) for i in range(parts)]).astype(F32)
        return total.astype(BF16)

    pieces_of = []
    for c in range(cands):
        inner = reduce([(grads, c), (other[c // half_cands], c % half_cands)])
        pieces_of.append([inner])
    for c in range(cands):
        if c < cands - 1:
            k = 2 * c
            pieces_of[c].append(
                reduce([(first[k], None), (second[k], None), (first[k + 1], None), (second[k + 1], None)])
            )
        else:
            for k in (2 * c, 2 * c + 1):
                pieces_of[c].append(reduce([(first[k], None), (second[k], None)]))

    blocks = jnp.where(row < 2, every_act, every_act[::-1])
    order = [blocks[1], blocks[2]]
    for s in range(0, tok, chunk):
        order += [blocks[0][:, s : s + chunk], blocks[3][:, s : s + chunk]]
    act_rot = jnp.concatenate(order, axis=1)
    rotated, scores = rotate_and_score(pieces_of, act_rot, eigenvalues, query_rotated)
    scores = exchange_sum(exchange_sum(scores, "col", parts), "row", planes)
    return rotated, scores


def solution(mesh):
    placed = (
        P("groups", "row", None),
        P("groups", "row", "col"),
        P(None, "col"),
        P("col", "row"),
        P("row", "col"),
        P(None, "row", "col"),
        P("groups"),
        P(),
    )
    chain = mesh.shape["groups"] == 2 and mesh.shape["row"] == 4 and mesh.shape["col"] == 4
    return jax.shard_map(
        chain_body if chain else gather_body,
        mesh=mesh,
        in_specs=placed,
        out_specs=(P("groups", "row", "col"), P(None, "groups")),
        check_vma=False,
    )
```

time: 830 us -> 793 us (0.955)
  starting transfers between devices: 0.08 us -> 287 us
  waiting for transfers between devices: 556 us -> 284 us
  blocking collectives: 178 us -> 0 us
  Pallas kernels: 0 us -> 141 us
  matrix products: 77.1 us -> 7.61 us
  local copies, waits for them, and re-layouts: 2.03 us -> 45.7 us
  other arithmetic: 2.69 us -> 12 us
    all_gather x2 -> x1, waiting for transfers between devices: 555 us -> 0.01 us  [chain_body(): every_act = lax.all_gather(local_act, 'row', axis=0)]
    ppermute x0 -> x70, starting transfers between devices: none -> 287 us  [the longest x5 181 us: chain_body(): near.append(lax.ppermute(piece, 'row', inward))]
    ppermute x0 -> x70, waiting for transfers between devices: none -> 284 us  [the longest x27 99.5 us: reduce(): lax.ppermute(mine, 'col', [(i, i ^ d) for i in range(parts)]).astype(F32)]
    psum x2 -> x0, blocking collectives: 178 us -> none  [the longest x1 147 us: body(): rotated_grads = lax.psum(partial_value, 'col').astype(jnp.bfloat16)]
    pallas_call x0 -> x10, Pallas kernels: none -> 141 us  [the longest x9 136 us: project(): pl.pallas_call(functools.partial(project_kernel, len(tokens)), grid=(feat...]
    dot_general x4 -> x1, matrix products: 77.1 us -> 7.61 us  [local_activations(): jnp.einsum('ctd,dk->ctk', acts, act_basis, preferred_element_type=F32)]
    unnamed x12 -> x49, local copies, waits for them, and re-layouts: 2.03 us -> 20.9 us
  transfers between devices with their start and end apart: 2 -> 71, of which waited for: 1 -> 25; matrix products, arithmetic and copies ran while one was open for 7% -> 8% of each run, Pallas kernels for 0% -> 17%
where the time goes in v2:
time: 793 us; the launch traced here: 792 us
  starting transfers between devices  287 us (36%)
  waiting for transfers between devices  284 us (36%)
  Pallas kernels  141 us (18%)
  local copies, waits for them, and re-layouts  45.7 us (6%)
  between operations  14.9 us (2%)
  other arithmetic  12 us (2%)
    ppermute x5, starting transfers between devices, chain_body(): near.append(lax.ppermute(piece, 'row', inward))  181 us
    pallas_call x9, Pallas kernels, project(): pl.pallas_call(functools.partial(project_kernel, len(tokens)), grid=(feat...  136 us
    ppermute x27, waiting for transfers between devices, reduce(): lax.ppermute(mine, 'col', [(i, i ^ d) for i in range(parts)]).astype(F32)  99.5 us
    ppermute x8, waiting for transfers between devices, chain_body(): first.append(lax.ppermute(piece, 'row', inward))  66.6 us
    ppermute x5, waiting for transfers between devices, chain_body(): near.append(lax.ppermute(piece, 'row', inward))  59.8 us
    ppermute x9, waiting for transfers between devices, reduce(): back = lax.ppermute(end, 'row', outward)  52.6 us
    ppermute x8, starting transfers between devices, chain_body(): first.append(lax.ppermute(piece, 'row', inward))  50.3 us
    unnamed x49, local copies, waits for them, and re-layouts  20.9 us
  transfers between devices with their start and end apart: 71, of which 25 were waited for; matrix products, arithmetic and copies ran while one was open for 8% of the time, Pallas kernels for 17%

profile of v2, /device:TPU:0, one launch (start us, length us, event | category | flops | bytes accessed | tf_op | source)
XLA Modules:
  0.0 791.8 jit_solution(8063595531329372147)
XLA Ops:
  7.2 2.7 constant_dynamic-slice_fusion
  9.9 5.9 collective-permute-start.1
  15.8 6.0 fusion.19
  21.8 2.8 collective-permute-start
  24.6 12.6 %collective-permute-done.1 = bf16[1024,512]{1,0:T(8,128)(2,1)} collective-permute-done((bf16[1024,512]{1,0:T(8,128)(2,1)S(1)}, bf16[1024,512]{1,0:T(8,128)(2,1)}, u32[]{:S(2)}, u32[]{:S(2)}) %collective-permute-start.1) | collective-permute-done | bytes 1048608 | tf_op jit(solution)/shard_map/ppermute | solution.py:197
  37.2 2.7 collective-permute-start.4
  39.9 5.3 constant_dynamic-slice_fusion.1
  45.2 6.6 collective-permute-start.2
  52.1 7.6 fusion.5
  59.7 76.5 %collective-permute-start.3 = (bf16[2048,512]{1,0:T(8,128)(2,1)}, bf16[2048,512]{1,0:T(8,128)(2,1)}, u32[]{:S(2)}, u32[]{:S(2)}) collective-permute-start(bf16[2048,512]{1,0:T(8,128)(2,1)} %get-tuple-element.34), channel_id=1, source_target_pairs={{0,4},{12,8},{1,5},{13,9},{2,6},{14,10},{3,7},{15,11},{16,20},{28,... | collective-permute-start | bytes 6291464 | tf_op jit(solution)/shard_map/ppermute | solution.py:197
  136.2 88.6 %collective-permute-start.5 = (bf16[2048,512]{1,0:T(8,128)(2,1)S(1)}, bf16[2048,512]{1,0:T(8,128)(2,1)}, u32[]{:S(2)}, u32[]{:S(2)}) collective-permute-start(bf16[2048,512]{1,0:T(8,128)(2,1)S(1)} %get-tuple-element.36), channel_id=1, source_target_pairs={{0,4},{12,8},{1,5},{13,9},{2,6},{14,10},{3,7},{15,11},{16,20},{28,... | collective-permute-start | bytes 6291464 | tf_op jit(solution)/shard_map/ppermute | solution.py:197
  224.8 6.0 slice_bitcast_fusion
  230.9 1.6 collective-permute-start.7
  232.5 2.3 constant_dynamic-update-slice_fusion.4
  234.8 2.0 collective-permute-start.8
  236.7 3.3 collective-permute-start.6
  240.0 2.0 reverse_select_fusion
  242.9 47.2 %collective-permute-done.6 = bf16[1024,512]{1,0:T(8,128)(2,1)} collective-permute-done((bf16[1024,512]{1,0:T(8,128)(2,1)}, bf16[1024,512]{1,0:T(8,128)(2,1)}, u32[]{:S(2)}, u32[]{:S(2)}) %collective-permute-start.6) | collective-permute-done | bytes 1048608 | tf_op jit(solution)/shard_map/ppermute | solution.py:197
  290.1 5.4 collective-permute-start.18
  295.5 2.2 collective-permute-start.16
  298.6 2.3 constant_dynamic-update-slice_fusion.9
  300.9 3.1 constant_dynamic-update-slice_fusion.3
  303.9 14.5 %collective-permute-done.18.refs_2_ = bf16[64,8192]{1,0:T(8,128)(2,1)} collective-permute-done((bf16[64,8192]{1,0:T(8,128)(2,1)}, bf16[64,8192]{1,0:T(8,128)(2,1)}, u32[]{:S(2)}, u32[]{:S(2)}) %collective-permute-start.18) | collective-permute-done | bytes 1048608 | tf_op jit(solution)/shard_map/ppermute | solution.py:209
  318.4 5.4 collective-permute-start.30
  323.8 17.1 %collective-permute-done.16.refs_0_ = bf16[64,8192]{1,0:T(8,128)(2,1)} collective-permute-done((bf16[64,8192]{1,0:T(8,128)(2,1)}, bf16[64,8192]{1,0:T(8,128)(2,1)}, u32[]{:S(2)}, u32[]{:S(2)}) %collective-permute-start.16) | collective-permute-done | bytes 1048608 | tf_op jit(solution)/shard_map/ppermute | solution.py:209
  340.9 5.4 collective-permute-start.28
  346.3 3.1 constant_dynamic-update-slice_fusion.8
  350.1 3.1 constant_dynamic-update-slice_fusion.2
  353.2 3.3 constant_dynamic-update-slice_fusion.1
  356.5 2.3 constant_dynamic-update-slice_fusion.refs_3_.refs_5_
  358.8 1.8 collective-permute-start.19
  364.9 17.9 %collective-permute-done.28.refs_0_ = bf16[64,8192]{1,0:T(8,128)(2,1)} collective-permute-done((bf16[64,8192]{1,0:T(8,128)(2,1)S(1)}, bf16[64,8192]{1,0:T(8,128)(2,1)}, u32[]{:S(2)}, u32[]{:S(2)}) %collective-permute-start.28) | collective-permute-done | bytes 1048608 | tf_op jit(solution)/shard_map/ppermute | solution.py:209
  382.7 4.5 collective-permute-start.42
  387.3 1.6 collective-permute-start.31
  391.4 17.6 %shard_map.95 = (bf16[256,1024]{1,0:T(8,128)(2,1)S(1)}, bf16[256,1024]{1,0:T(8,128)(2,1)}) custom-call(bf16[4,128,8192]{2,1,0:T(8,128)(2,1)S(1)} %bitcast.42, bf16[2,128,8192]{2,1,0:T(8,128)(2,1)} %collective-permute-done.refs_1_, bf16[8192,1024]{1,0:T(8,128)(2,1)} %refs_2_.11, bf16[8192,512]{1,0:T(8,128)(2,1)} %constant_dynamic-update-slice_fusion.refs_3_.refs_5_, ...), custom_call_target="tpu_custom_call" | custom-call | flops 8589934592 | bytes 37748736 | tf_op jit(solution)/shard_map/pallas_call | solution.py:140
  410.7 16.0 %shard_map.96 = (bf16[256,1024]{1,0:T(8,128)(2,1)S(1)}, bf16[256,1024]{1,0:T(8,128)(2,1)S(1)}) custom-call(bf16[64,8192]{1,0:T(8,128)(2,1)} %collective-permute-done.16.refs_0_, bf16[64,8192]{1,0:T(8,128)(2,1)} %collective-permute-done.17.refs_1_, bf16[64,8192]{1,0:T(8,128)(2,1)} %collective-permute-done.18.refs_2_, ...), custom_call_target="tpu_custom_call" | custom-call | flops 8589934592 | bytes 37748736 | tf_op jit(solution)/shard_map/pallas_call | solution.py:140
  428.0 16.2 %shard_map.97 = (bf16[256,1024]{1,0:T(8,128)(2,1)S(1)}, bf16[256,1024]{1,0:T(8,128)(2,1)S(1)}) custom-call(bf16[4,128,8192]{2,1,0:T(8,128)(2,1)S(1)} %bitcast.44, bf16[2,128,8192]{2,1,0:T(8,128)(2,1)} %collective-permute-done.refs_1_, bf16[8192,1024]{1,0:T(8,128)(2,1)} %refs_2_.11, bf16[8192,512]{1,0:T(8,128)(2,1)} %constant_dynamic-update-slice_fusion.refs_3_.refs_5_, ...), custom_call_target="tpu_custom_call" | custom-call | flops 8589934592 | bytes 37748736 | tf_op jit(solution)/shard_map/pallas_call | solution.py:140
  445.7 16.2 %shard_map.99 = (bf16[256,1024]{1,0:T(8,128)(2,1)S(1)}, bf16[256,1024]{1,0:T(8,128)(2,1)S(1)}) custom-call(bf16[4,128,8192]{2,1,0:T(8,128)(2,1)S(1)} %bitcast.44, bf16[2,128,8192]{2,1,0:T(8,128)(2,1)} %collective-permute-done.4.refs_1_, bf16[8192,1024]{1,0:T(8,128)(2,1)} %refs_2_.11, bf16[8192,512]{1,0:T(8,128)(2,1)} %constant_dynamic-update-slice_fusion.refs_3_.refs_5_, ...), custom_call_target="tpu_custom_call" | custom-call | flops 8589934592 | bytes 37748736 | tf_op jit(solution)/shard_map/pallas_call | solution.py:140
  462.0 16.3 %shard_map.101 = (bf16[256,1024]{1,0:T(8,128)(2,1)S(1)}, bf16[256,1024]{1,0:T(8,128)(2,1)S(1)}) custom-call(bf16[4,128,8192]{2,1,0:T(8,128)(2,1)S(1)} %bitcast.44, bf16[2,128,8192]{2,1,0:T(8,128)(2,1)} %collective-permute-done.4.refs_1_, bf16[8192,1024]{1,0:T(8,128)(2,1)} %refs_2_.11, bf16[8192,512]{1,0:T(8,128)(2,1)} %constant_dynamic-update-slice_fusion.refs_3_.refs_5_, ...), custom_call_target="tpu_custom_call" | custom-call | flops 8589934592 | bytes 37748736 | tf_op jit(solution)/shard_map/pallas_call | solution.py:140
  480.9 24.4 %collective-permute-start.40 = (bf16[64,8192]{1,0:T(8,128)(2,1)S(1)}, bf16[64,8192]{1,0:T(8,128)(2,1)S(1)}, u32[]{:S(2)}, u32[]{:S(2)}) collective-permute-start(bf16[64,8192]{1,0:T(8,128)(2,1)S(1)} %copy-done.4), channel_id=1, source_target_pairs={{0,4},{12,8},{1,5},{13,9},{2,6},{14,10},{3,7},{15,11},{16,20},{28,... | collective-permute-start | bytes 3145736 | tf_op jit(solution)/shard_map/ppermute | solution.py:209
  506.7 8.3 %collective-permute-done.36 = bf16[256,1024]{1,0:T(8,128)(2,1)S(1)} collective-permute-done((bf16[256,1024]{1,0:T(8,128)(2,1)S(1)}, bf16[256,1024]{1,0:T(8,128)(2,1)S(1)}, u32[]{:S(2)}, u32[]{:S(2)}) %collective-permute-start.36) | collective-permute-done | bytes 524320 | tf_op jit(solution)/shard_map/ppermute | solution.py:218
  517.1 6.6 collective-permute-done.48
  528.5 9.3 %collective-permute-done.15 = bf16[256,1024]{1,0:T(8,128)(2,1)S(1)} collective-permute-done((bf16[256,1024]{1,0:T(8,128)(2,1)S(1)}, bf16[256,1024]{1,0:T(8,128)(2,1)S(1)}, u32[]{:S(2)}, u32[]{:S(2)}) %collective-permute-start.15) | collective-permute-done | bytes 524320 | tf_op jit(solution)/shard_map/ppermute | solution.py:223
  538.0 11.2 %collective-permute-done.14 = bf16[256,1024]{1,0:T(8,128)(2,1)S(1)} collective-permute-done((bf16[256,1024]{1,0:T(8,128)(2,1)S(1)}, bf16[256,1024]{1,0:T(8,128)(2,1)S(1)}, u32[]{:S(2)}, u32[]{:S(2)}) %collective-permute-start.14) | collective-permute-done | bytes 524320 | tf_op jit(solution)/shard_map/ppermute | solution.py:223
  550.8 15.0 %shard_map.98 = (bf16[256,1024]{1,0:T(8,128)(2,1)S(1)}, bf16[256,1024]{1,0:T(8,128)(2,1)S(1)}) custom-call(bf16[64,8192]{1,0:T(8,128)(2,1)} %collective-permute-done.28.refs_0_, bf16[64,8192]{1,0:T(8,128)(2,1)S(1)} %collective-permute-done.29.refs_1_, bf16[64,8192]{1,0:T(8,128)(2,1)} %collective-permute-done.30.refs_2_, ...), custom_call_target="tpu_custom_call" | custom-call | flops 8589934592 | bytes 37748736 | tf_op jit(solution)/shard_map/pallas_call | solution.py:140
  566.2 5.5 collective-permute-done.22
  574.6 8.2 %collective-permute-done.27 = bf16[256,1024]{1,0:T(8,128)(2,1)S(1)} collective-permute-done((bf16[256,1024]{1,0:T(8,128)(2,1)S(1)}, bf16[256,1024]{1,0:T(8,128)(2,1)S(1)}, u32[]{:S(2)}, u32[]{:S(2)}) %collective-permute-start.27) | collective-permute-done | bytes 524320 | tf_op jit(solution)/shard_map/ppermute | solution.py:223
  582.9 11.3 %collective-permute-done.26 = bf16[256,1024]{1,0:T(8,128)(2,1)} collective-permute-done((bf16[256,1024]{1,0:T(8,128)(2,1)S(1)}, bf16[256,1024]{1,0:T(8,128)(2,1)}, u32[]{:S(2)}, u32[]{:S(2)}) %collective-permute-start.26) | collective-permute-done | bytes 524320 | tf_op jit(solution)/shard_map/ppermute | solution.py:223
  597.9 7.4 collective-permute-done.39
  607.4 9.2 %collective-permute-done.38 = bf16[256,1024]{1,0:T(8,128)(2,1)S(1)} collective-permute-done((bf16[256,1024]{1,0:T(8,128)(2,1)S(1)}, bf16[256,1024]{1,0:T(8,128)(2,1)S(1)}, u32[]{:S(2)}, u32[]{:S(2)}) %collective-permute-start.38) | collective-permute-done | bytes 524320 | tf_op jit(solution)/shard_map/ppermute | solution.py:223
  616.6 1.7 collective-permute-start.50
  618.8 11.7 %collective-permute-done.51 = bf16[256,1024]{1,0:T(8,128)(2,1)S(1)} collective-permute-done((bf16[256,1024]{1,0:T(8,128)(2,1)S(1)}, bf16[256,1024]{1,0:T(8,128)(2,1)S(1)}, u32[]{:S(2)}, u32[]{:S(2)}) %collective-permute-start.51) | collective-permute-done | bytes 524320 | tf_op jit(solution)/shard_map/ppermute | solution.py:223
  632.1 10.0 %collective-permute-done.50 = bf16[256,1024]{1,0:T(8,128)(2,1)S(1)} collective-permute-done((bf16[256,1024]{1,0:T(8,128)(2,1)S(1)}, bf16[256,1024]{1,0:T(8,128)(2,1)S(1)}, u32[]{:S(2)}, u32[]{:S(2)}) %collective-permute-start.50) | collective-permute-done | bytes 524320 | tf_op jit(solution)/shard_map/ppermute | solution.py:223
  645.7 14.6 %shard_map.100 = (bf16[256,1024]{1,0:T(8,128)(2,1)S(1)}, bf16[256,1024]{1,0:T(8,128)(2,1)S(1)}) custom-call(bf16[64,8192]{1,0:T(8,128)(2,1)S(1)} %collective-permute-done.40.refs_0_, bf16[64,8192]{1,0:T(8,128)(2,1)S(1)} %collective-permute-done.41.refs_1_, bf16[64,8192]{1,0:T(8,128)(2,1)S(1)} %collective-permute-done.42.refs_2_, ...), custom_call_target="tpu_custom_call" | custom-call | flops 8589934592 | bytes 37748736 | tf_op jit(solution)/shard_map/pallas_call | solution.py:140
  661.6 16.0 %collective-permute-done.52.refs_0_ = bf16[64,8192]{1,0:T(8,128)(2,1)S(1)} collective-permute-done((bf16[64,8192]{1,0:T(8,128)(2,1)S(1)}, bf16[64,8192]{1,0:T(8,128)(2,1)S(1)}, u32[]{:S(2)}, u32[]{:S(2)}) %collective-permute-start.52) | collective-permute-done | bytes 1048608 | tf_op jit(solution)/shard_map/ppermute | solution.py:209
  683.3 12.1 %shard_map.102 = (bf16[128,1024]{1,0:T(8,128)(2,1)S(1)}, bf16[128,1024]{1,0:T(8,128)(2,1)S(1)}) custom-call(bf16[64,8192]{1,0:T(8,128)(2,1)S(1)} %collective-permute-done.52.refs_0_, bf16[64,8192]{1,0:T(8,128)(2,1)S(1)} %collective-permute-done.53.refs_1_, bf16[8192,1024]{1,0:T(8,128)(2,1)} %refs_2_.11, bf16[8192,512]{1,0:T(8,128)(2,1)S(1)} %bitcast.40, ...), custom_call_target="tpu_custom_call" | custom-call | flops 4294967296 | bytes 35651584 | tf_op jit(solution)/shard_map/pallas_call | solution.py:140
  696.8 12.2 %shard_map.103 = (bf16[128,1024]{1,0:T(8,128)(2,1)S(1)}, bf16[128,1024]{1,0:T(8,128)(2,1)S(1)}) custom-call(bf16[64,8192]{1,0:T(8,128)(2,1)S(1)} %collective-permute-done.58.refs_0_, bf16[64,8192]{1,0:T(8,128)(2,1)S(1)} %collective-permute-done.59.refs_1_, bf16[8192,1024]{1,0:T(8,128)(2,1)} %refs_2_.11, bf16[8192,512]{1,0:T(8,128)(2,1)S(1)} %bitcast.40, ...), custom_call_target="tpu_custom_call" | custom-call | flops 4294967296 | bytes 35651584 | tf_op jit(solution)/shard_map/pallas_call | solution.py:140
  710.5 15.3 %collective-permute-done.54 = bf16[128,1024]{1,0:T(8,128)(2,1)S(1)} collective-permute-done((bf16[128,1024]{1,0:T(8,128)(2,1)S(1)}, bf16[128,1024]{1,0:T(8,128)(2,1)S(1)}, u32[]{:S(2)}, u32[]{:S(2)}) %collective-permute-start.54) | collective-permute-done | bytes 262176 | tf_op jit(solution)/shard_map/ppermute | solution.py:218
  726.0 22.4 %collective-permute-done.60 = bf16[128,1024]{1,0:T(8,128)(2,1)S(1)} collective-permute-done((bf16[128,1024]{1,0:T(8,128)(2,1)S(1)}, bf16[128,1024]{1,0:T(8,128)(2,1)S(1)}, u32[]{:S(2)}, u32[]{:S(2)}) %collective-permute-start.60) | collective-permute-done | bytes 262176 | tf_op jit(solution)/shard_map/ppermute | solution.py:218
  751.7 15.6 %collective-permute-done.56 = bf16[128,1024]{1,0:T(8,128)(2,1)S(1)} collective-permute-done((bf16[128,1024]{1,0:T(8,128)(2,1)S(1)}, bf16[128,1024]{1,0:T(8,128)(2,1)S(1)}, u32[]{:S(2)}, u32[]{:S(2)}) %collective-permute-start.56) | collective-permute-done | bytes 262176 | tf_op jit(solution)/shard_map/ppermute | solution.py:223
  767.7 4.5 shard_map.104
  775.5 1.8 collective-permute-done.65
  777.3 2.6 collective-permute-start.69
  779.9 1.9 collective-permute-start.67
  (186 shorter events, 61.2 us)
Async XLA Ops:
  7.2 232.9 %all-gather.3.cloned.1.call-start = ((), (), s32[]{:S(2)}) async-start(), calls=%async_computation | async-start | bytes 1310720 | tf_op jit(solution)/shard_map/all_gather | solution.py:185
  9.9 27.3 %collective-permute-start.1 = (bf16[1024,512]{1,0:T(8,128)(2,1)S(1)}, bf16[1024,512]{1,0:T(8,128)(2,1)}, u32[]{:S(2)}, u32[]{:S(2)}) collective-permute-start(bf16[1024,512]{1,0:T(8,128)(2,1)S(1)} %get-tuple-element.67), channel_id=1, source_target_pairs={{0,4},{12,8},{1,5},{13,9},{2,6},{14,10},{3,7},{15,11},{16,20},{28,... | collective-permute-start | bytes 3145736 | tf_op jit(solution)/shard_map/ppermute | solution.py:197
  21.8 37.9 %collective-permute-start = (bf16[2,128,8192]{2,1,0:T(8,128)(2,1)}, bf16[2,128,8192]{2,1,0:T(8,128)(2,1)}, u32[]{:S(2)}, u32[]{:S(2)}) collective-permute-start(bf16[2,128,8192]{2,1,0:T(8,128)(2,1)} %get-tuple-element.80), channel_id=1, source_target_pairs={{4,8},{8,4},{5,9},{9,5},{6,10},{10,6},{7,11},{11,7},{20,24},{24,20... | collective-permute-start | bytes 12582920 | tf_op jit(solution)/shard_map/ppermute | solution.py:201
  37.2 99.0 %collective-permute-start.4 = (bf16[2,128,8192]{2,1,0:T(8,128)(2,1)}, bf16[2,128,8192]{2,1,0:T(8,128)(2,1)}, u32[]{:S(2)}, u32[]{:S(2)}) collective-permute-start(bf16[2,128,8192]{2,1,0:T(8,128)(2,1)} %get-tuple-element.35), channel_id=1, source_target_pairs={{4,8},{8,4},{5,9},{9,5},{6,10},{10,6},{7,11},{11,7},{20,24},{24,20... | collective-permute-start | bytes 12582920 | tf_op jit(solution)/shard_map/ppermute | solution.py:201
  45.2 91.0 %collective-permute-start.2 = (bf16[2048,512]{1,0:T(8,128)(2,1)}, bf16[2048,512]{1,0:T(8,128)(2,1)}, u32[]{:S(2)}, u32[]{:S(2)}) collective-permute-start(bf16[2048,512]{1,0:T(8,128)(2,1)} %get-tuple-element.70), channel_id=1, source_target_pairs={{0,4},{12,8},{1,5},{13,9},{2,6},{14,10},{3,7},{15,11},{16,20},{28,... | collective-permute-start | bytes 6291464 | tf_op jit(solution)/shard_map/ppermute | solution.py:197
  59.7 177.0 %collective-permute-start.3 = (bf16[2048,512]{1,0:T(8,128)(2,1)}, bf16[2048,512]{1,0:T(8,128)(2,1)}, u32[]{:S(2)}, u32[]{:S(2)}) collective-permute-start(bf16[2048,512]{1,0:T(8,128)(2,1)} %get-tuple-element.34), channel_id=1, source_target_pairs={{0,4},{12,8},{1,5},{13,9},{2,6},{14,10},{3,7},{15,11},{16,20},{28,... | collective-permute-start | bytes 6291464 | tf_op jit(solution)/shard_map/ppermute | solution.py:197
  136.2 159.3 %collective-permute-start.5 = (bf16[2048,512]{1,0:T(8,128)(2,1)S(1)}, bf16[2048,512]{1,0:T(8,128)(2,1)}, u32[]{:S(2)}, u32[]{:S(2)}) collective-permute-start(bf16[2048,512]{1,0:T(8,128)(2,1)S(1)} %get-tuple-element.36), channel_id=1, source_target_pairs={{0,4},{12,8},{1,5},{13,9},{2,6},{14,10},{3,7},{15,11},{16,20},{28,... | collective-permute-start | bytes 6291464 | tf_op jit(solution)/shard_map/ppermute | solution.py:197
  230.9 66.9 %collective-permute-start.7 = (bf16[1024,512]{1,0:T(8,128)(2,1)}, bf16[1024,512]{1,0:T(8,128)(2,1)}, u32[]{:S(2)}, u32[]{:S(2)}) collective-permute-start(bf16[1024,512]{1,0:T(8,128)(2,1)} %collective-permute-done.1), channel_id=1, source_target_pairs={{4,20},{8,24},{20,4},{24,8},{5,21},{9,25},{21,5},{25,9},{6,22},{10... | collective-permute-start | bytes 3145736 | tf_op jit(solution)/shard_map/ppermute | solution.py:198
  234.8 111.5 %collective-permute-start.8 = (bf16[2048,512]{1,0:T(8,128)(2,1)}, bf16[2048,512]{1,0:T(8,128)(2,1)}, u32[]{:S(2)}, u32[]{:S(2)}) collective-permute-start(bf16[2048,512]{1,0:T(8,128)(2,1)} %collective-permute-done.2), channel_id=1, source_target_pairs={{4,20},{8,24},{20,4},{24,8},{5,21},{9,25},{21,5},{25,9},{6,22},{10... | collective-permute-start | bytes 6291464 | tf_op jit(solution)/shard_map/ppermute | solution.py:198
  236.7 53.4 %collective-permute-start.6 = (bf16[1024,512]{1,0:T(8,128)(2,1)}, bf16[1024,512]{1,0:T(8,128)(2,1)}, u32[]{:S(2)}, u32[]{:S(2)}) collective-permute-start(bf16[1024,512]{1,0:T(8,128)(2,1)} %get-tuple-element.37), channel_id=1, source_target_pairs={{0,4},{12,8},{1,5},{13,9},{2,6},{14,10},{3,7},{15,11},{16,20},{28,... | collective-permute-start | bytes 3145736 | tf_op jit(solution)/shard_map/ppermute | solution.py:197
  242.1 116.6 %collective-permute-start.9 = (bf16[2048,512]{1,0:T(8,128)(2,1)}, bf16[2048,512]{1,0:T(8,128)(2,1)S(1)}, u32[]{:S(2)}, u32[]{:S(2)}) collective-permute-start(bf16[2048,512]{1,0:T(8,128)(2,1)} %collective-permute-done.3), channel_id=1, source_target_pairs={{4,20},{8,24},{20,4},{24,8},{5,21},{9,25},{21,5},{25,9},{6,22},{10... | collective-permute-start | bytes 6291464 | tf_op jit(solution)/shard_map/ppermute | solution.py:198
  290.1 28.3 %collective-permute-start.18 = (bf16[64,8192]{1,0:T(8,128)(2,1)}, bf16[64,8192]{1,0:T(8,128)(2,1)}, u32[]{:S(2)}, u32[]{:S(2)}) collective-permute-start(bf16[64,8192]{1,0:T(8,128)(2,1)} %get-tuple-element.41), channel_id=1, source_target_pairs={{0,4},{12,8},{1,5},{13,9},{2,6},{14,10},{3,7},{15,11},{16,20},{28,... | collective-permute-start | bytes 3145736 | tf_op jit(solution)/shard_map/ppermute | solution.py:209
  295.5 45.4 %collective-permute-start.16 = (bf16[64,8192]{1,0:T(8,128)(2,1)}, bf16[64,8192]{1,0:T(8,128)(2,1)}, u32[]{:S(2)}, u32[]{:S(2)}) collective-permute-start(bf16[64,8192]{1,0:T(8,128)(2,1)} %get-tuple-element.40), channel_id=1, source_target_pairs={{0,4},{12,8},{1,5},{13,9},{2,6},{14,10},{3,7},{15,11},{16,20},{28,... | collective-permute-start | bytes 3145736 | tf_op jit(solution)/shard_map/ppermute | solution.py:209
  297.8 89.5 %collective-permute-start.10 = (bf16[2048,512]{1,0:T(8,128)(2,1)}, bf16[2048,512]{1,0:T(8,128)(2,1)S(1)}, u32[]{:S(2)}, u32[]{:S(2)}) collective-permute-start(bf16[2048,512]{1,0:T(8,128)(2,1)} %collective-permute-done.5), channel_id=1, source_target_pairs={{4,20},{8,24},{20,4},{24,8},{5,21},{9,25},{21,5},{25,9},{6,22},{10... | collective-permute-start | bytes 6291464 | tf_op jit(solution)/shard_map/ppermute | solution.py:198
  318.4 44.8 %collective-permute-start.30 = (bf16[64,8192]{1,0:T(8,128)(2,1)S(1)}, bf16[64,8192]{1,0:T(8,128)(2,1)}, u32[]{:S(2)}, u32[]{:S(2)}) collective-permute-start(bf16[64,8192]{1,0:T(8,128)(2,1)S(1)} %copy-done.6), channel_id=1, source_target_pairs={{0,4},{12,8},{1,5},{13,9},{2,6},{14,10},{3,7},{15,11},{16,20},{28,... | collective-permute-start | bytes 3145736 | tf_op jit(solution)/shard_map/ppermute | solution.py:209
  340.9 41.8 %collective-permute-start.28 = (bf16[64,8192]{1,0:T(8,128)(2,1)S(1)}, bf16[64,8192]{1,0:T(8,128)(2,1)}, u32[]{:S(2)}, u32[]{:S(2)}) collective-permute-start(bf16[64,8192]{1,0:T(8,128)(2,1)S(1)} %copy-done.5), channel_id=1, source_target_pairs={{0,4},{12,8},{1,5},{13,9},{2,6},{14,10},{3,7},{15,11},{16,20},{28,... | collective-permute-start | bytes 3145736 | tf_op jit(solution)/shard_map/ppermute | solution.py:209
  349.4 40.9 %collective-permute-start.11 = (bf16[1024,512]{1,0:T(8,128)(2,1)}, bf16[1024,512]{1,0:T(8,128)(2,1)S(1)}, u32[]{:S(2)}, u32[]{:S(2)}) collective-permute-start(bf16[1024,512]{1,0:T(8,128)(2,1)} %collective-permute-done.6), channel_id=1, source_target_pairs={{4,20},{8,24},{20,4},{24,8},{5,21},{9,25},{21,5},{25,9},{6,22},{10... | collective-permute-start | bytes 3145736 | tf_op jit(solution)/shard_map/ppermute | solution.py:198
  358.8 51.9 %collective-permute-start.19 = (bf16[64,8192]{1,0:T(8,128)(2,1)}, bf16[64,8192]{1,0:T(8,128)(2,1)}, u32[]{:S(2)}, u32[]{:S(2)}) collective-permute-start(bf16[64,8192]{1,0:T(8,128)(2,1)} %collective-permute-done.18.refs_2_), channel_id=1, source_target_pairs={{4,8},{8,4},{5,9},{9,5},{6,10},{10,6},{7,11},{11,7},{20,24},{24,20... | collective-permute-start | bytes 3145736 | tf_op jit(solution)/shard_map/ppermute | solution.py:211
  363.2 47.4 %collective-permute-start.17 = (bf16[64,8192]{1,0:T(8,128)(2,1)}, bf16[64,8192]{1,0:T(8,128)(2,1)}, u32[]{:S(2)}, u32[]{:S(2)}) collective-permute-start(bf16[64,8192]{1,0:T(8,128)(2,1)} %collective-permute-done.16.refs_0_), channel_id=1, source_target_pairs={{4,8},{8,4},{5,9},{9,5},{6,10},{10,6},{7,11},{11,7},{20,24},{24,20... | collective-permute-start | bytes 3145736 | tf_op jit(solution)/shard_map/ppermute | solution.py:211
  382.7 143.1 %collective-permute-start.42 = (bf16[64,8192]{1,0:T(8,128)(2,1)}, bf16[64,8192]{1,0:T(8,128)(2,1)S(1)}, u32[]{:S(2)}, u32[]{:S(2)}) collective-permute-start(bf16[64,8192]{1,0:T(8,128)(2,1)} %get-tuple-element.53), channel_id=1, source_target_pairs={{0,4},{12,8},{1,5},{13,9},{2,6},{14,10},{3,7},{15,11},{16,20},{28,... | collective-permute-start | bytes 3145736 | tf_op jit(solution)/shard_map/ppermute | solution.py:209
  387.3 136.9 %collective-permute-start.31 = (bf16[64,8192]{1,0:T(8,128)(2,1)}, bf16[64,8192]{1,0:T(8,128)(2,1)}, u32[]{:S(2)}, u32[]{:S(2)}) collective-permute-start(bf16[64,8192]{1,0:T(8,128)(2,1)} %collective-permute-done.30.refs_2_), channel_id=1, source_target_pairs={{4,8},{8,4},{5,9},{9,5},{6,10},{10,6},{7,11},{11,7},{20,24},{24,20... | collective-permute-start | bytes 3145736 | tf_op jit(solution)/shard_map/ppermute | solution.py:211
  409.1 69.2 %collective-permute-start.12 = (bf16[256,1024]{1,0:T(8,128)(2,1)}, bf16[256,1024]{1,0:T(8,128)(2,1)}, u32[]{:S(2)}, u32[]{:S(2)}) collective-permute-start(bf16[256,1024]{1,0:T(8,128)(2,1)} %get-tuple-element.38), channel_id=1, source_target_pairs={{4,0},{8,12},{5,1},{9,13},{6,2},{10,14},{7,3},{11,15},{20,16},{24,... | collective-permute-start | bytes 1572872 | tf_op jit(solution)/shard_map/ppermute | solution.py:218
  426.7 54.2 %collective-permute-start.20 = (bf16[256,1024]{1,0:T(8,128)(2,1)S(1)}, bf16[256,1024]{1,0:T(8,128)(2,1)S(1)}, u32[]{:S(2)}, u32[]{:S(2)}) collective-permute-start(bf16[256,1024]{1,0:T(8,128)(2,1)S(1)} %get-tuple-element.42), channel_id=1, source_target_pairs={{4,0},{8,12},{5,1},{9,13},{6,2},{10,14},{7,3},{11,15},{20,16},{24,... | collective-permute-start | bytes 1572872 | tf_op jit(solution)/shard_map/ppermute | solution.py:218
  444.2 61.1 %collective-permute-start.24 = (bf16[256,1024]{1,0:T(8,128)(2,1)S(1)}, bf16[256,1024]{1,0:T(8,128)(2,1)S(1)}, u32[]{:S(2)}, u32[]{:S(2)}) collective-permute-start(bf16[256,1024]{1,0:T(8,128)(2,1)S(1)} %get-tuple-element.44), channel_id=1, source_target_pairs={{4,0},{8,12},{5,1},{9,13},{6,2},{10,14},{7,3},{11,15},{20,16},{24,... | collective-permute-start | bytes 1572872 | tf_op jit(solution)/shard_map/ppermute | solution.py:218
  478.3 36.8 %collective-permute-start.36 = (bf16[256,1024]{1,0:T(8,128)(2,1)S(1)}, bf16[256,1024]{1,0:T(8,128)(2,1)S(1)}, u32[]{:S(2)}, u32[]{:S(2)}) collective-permute-start(bf16[256,1024]{1,0:T(8,128)(2,1)S(1)} %get-tuple-element.50), channel_id=1, source_target_pairs={{4,0},{8,12},{5,1},{9,13},{6,2},{10,14},{7,3},{11,15},{20,16},{24,... | collective-permute-start | bytes 1572872 | tf_op jit(solution)/shard_map/ppermute | solution.py:218
  480.9 46.9 %collective-permute-start.40 = (bf16[64,8192]{1,0:T(8,128)(2,1)S(1)}, bf16[64,8192]{1,0:T(8,128)(2,1)S(1)}, u32[]{:S(2)}, u32[]{:S(2)}) collective-permute-start(bf16[64,8192]{1,0:T(8,128)(2,1)S(1)} %copy-done.4), channel_id=1, source_target_pairs={{0,4},{12,8},{1,5},{13,9},{2,6},{14,10},{3,7},{15,11},{16,20},{28,... | collective-permute-start | bytes 3145736 | tf_op jit(solution)/shard_map/ppermute | solution.py:209
  505.4 18.3 %collective-permute-start.48 = (bf16[256,1024]{1,0:T(8,128)(2,1)S(1)}, bf16[256,1024]{1,0:T(8,128)(2,1)S(1)}, u32[]{:S(2)}, u32[]{:S(2)}) collective-permute-start(bf16[256,1024]{1,0:T(8,128)(2,1)S(1)} %get-tuple-element.56), channel_id=1, source_target_pairs={{4,0},{8,12},{5,1},{9,13},{6,2},{10,14},{7,3},{11,15},{20,16},{24,... | collective-permute-start | bytes 1572872 | tf_op jit(solution)/shard_map/ppermute | solution.py:218
  515.1 11.6 %collective-permute-start.29 = (bf16[64,8192]{1,0:T(8,128)(2,1)}, bf16[64,8192]{1,0:T(8,128)(2,1)S(1)}, u32[]{:S(2)}, u32[]{:S(2)}) collective-permute-start(bf16[64,8192]{1,0:T(8,128)(2,1)} %collective-permute-done.28.refs_0_), channel_id=1, source_target_pairs={{4,8},{8,4},{5,9},{9,5},{6,10},{10,6},{7,11},{11,7},{20,24},{24,20... | collective-permute-start | bytes 3145736 | tf_op jit(solution)/shard_map/ppermute | solution.py:211
  523.7 14.2 %collective-permute-start.15 = (bf16[256,1024]{1,0:T(8,128)(2,1)S(1)}, bf16[256,1024]{1,0:T(8,128)(2,1)S(1)}, u32[]{:S(2)}, u32[]{:S(2)}) collective-permute-start(bf16[256,1024]{1,0:T(8,128)(2,1)S(1)} %fusion.8), channel_id=1, source_target_pairs={{0,3},{1,2},{2,1},{3,0},{4,7},{5,6},{6,5},{7,4},{8,11},{9,10},{10,... | collective-permute-start | bytes 1572872 | tf_op jit(solution)/shard_map/ppermute | solution.py:223
  524.2 25.0 %collective-permute-start.14 = (bf16[256,1024]{1,0:T(8,128)(2,1)S(1)}, bf16[256,1024]{1,0:T(8,128)(2,1)S(1)}, u32[]{:S(2)}, u32[]{:S(2)}) collective-permute-start(bf16[256,1024]{1,0:T(8,128)(2,1)S(1)} %fusion.8), channel_id=1, source_target_pairs={{0,2},{1,3},{2,0},{3,1},{4,6},{5,7},{6,4},{7,5},{8,10},{9,11},{10,... | collective-permute-start | bytes 1572872 | tf_op jit(solution)/shard_map/ppermute | solution.py:223
  525.8 24.3 %collective-permute-start.13 = (bf16[256,1024]{1,0:T(8,128)(2,1)S(1)}, bf16[256,1024]{1,0:T(8,128)(2,1)S(1)}, u32[]{:S(2)}, u32[]{:S(2)}) collective-permute-start(bf16[256,1024]{1,0:T(8,128)(2,1)S(1)} %fusion.8), channel_id=1, source_target_pairs={{0,1},{1,0},{2,3},{3,2},{4,5},{5,4},{6,7},{7,6},{8,9},{9,8},{10,11... | collective-permute-start | bytes 1572872 | tf_op jit(solution)/shard_map/ppermute | solution.py:223
  526.7 39.2 %collective-permute-start.23 = (bf16[256,1024]{1,0:T(8,128)(2,1)S(1)}, bf16[256,1024]{1,0:T(8,128)(2,1)S(1)}, u32[]{:S(2)}, u32[]{:S(2)}) collective-permute-start(bf16[256,1024]{1,0:T(8,128)(2,1)S(1)} %fusion.9), channel_id=1, source_target_pairs={{0,3},{1,2},{2,1},{3,0},{4,7},{5,6},{6,5},{7,4},{8,11},{9,10},{10,... | collective-permute-start | bytes 1572872 | tf_op jit(solution)/shard_map/ppermute | solution.py:223
  527.8 43.8 %collective-permute-start.22 = (bf16[256,1024]{1,0:T(8,128)(2,1)S(1)}, bf16[256,1024]{1,0:T(8,128)(2,1)S(1)}, u32[]{:S(2)}, u32[]{:S(2)}) collective-permute-start(bf16[256,1024]{1,0:T(8,128)(2,1)S(1)} %fusion.9), channel_id=1, source_target_pairs={{0,2},{1,3},{2,0},{3,1},{4,6},{5,7},{6,4},{7,5},{8,10},{9,11},{10,... | collective-permute-start | bytes 1572872 | tf_op jit(solution)/shard_map/ppermute | solution.py:223
  537.9 35.9 %collective-permute-start.21 = (bf16[256,1024]{1,0:T(8,128)(2,1)S(1)}, bf16[256,1024]{1,0:T(8,128)(2,1)}, u32[]{:S(2)}, u32[]{:S(2)}) collective-permute-start(bf16[256,1024]{1,0:T(8,128)(2,1)S(1)} %fusion.9), channel_id=1, source_target_pairs={{0,1},{1,0},{2,3},{3,2},{4,5},{5,4},{6,7},{7,6},{8,9},{9,8},{10,11... | collective-permute-start | bytes 1572872 | tf_op jit(solution)/shard_map/ppermute | solution.py:223
  549.2 33.6 %collective-permute-start.27 = (bf16[256,1024]{1,0:T(8,128)(2,1)S(1)}, bf16[256,1024]{1,0:T(8,128)(2,1)S(1)}, u32[]{:S(2)}, u32[]{:S(2)}) collective-permute-start(bf16[256,1024]{1,0:T(8,128)(2,1)S(1)} %fusion.10), channel_id=1, source_target_pairs={{0,3},{1,2},{2,1},{3,0},{4,7},{5,6},{6,5},{7,4},{8,11},{9,10},{10,... | collective-permute-start | bytes 1572872 | tf_op jit(solution)/shard_map/ppermute | solution.py:223
  550.1 44.2 %collective-permute-start.26 = (bf16[256,1024]{1,0:T(8,128)(2,1)S(1)}, bf16[256,1024]{1,0:T(8,128)(2,1)}, u32[]{:S(2)}, u32[]{:S(2)}) collective-permute-start(bf16[256,1024]{1,0:T(8,128)(2,1)S(1)} %fusion.10), channel_id=1, source_target_pairs={{0,2},{1,3},{2,0},{3,1},{4,6},{5,7},{6,4},{7,5},{8,10},{9,11},{10,... | collective-permute-start | bytes 1572872 | tf_op jit(solution)/shard_map/ppermute | solution.py:223
  565.9 31.2 %collective-permute-start.25 = (bf16[256,1024]{1,0:T(8,128)(2,1)S(1)}, bf16[256,1024]{1,0:T(8,128)(2,1)S(1)}, u32[]{:S(2)}, u32[]{:S(2)}) collective-permute-start(bf16[256,1024]{1,0:T(8,128)(2,1)S(1)} %fusion.10), channel_id=1, source_target_pairs={{0,1},{1,0},{2,3},{3,2},{4,5},{5,4},{6,7},{7,6},{8,9},{9,8},{10,11... | collective-permute-start | bytes 1572872 | tf_op jit(solution)/shard_map/ppermute | solution.py:223
  572.5 32.8 %collective-permute-start.39 = (bf16[256,1024]{1,0:T(8,128)(2,1)S(1)}, bf16[256,1024]{1,0:T(8,128)(2,1)S(1)}, u32[]{:S(2)}, u32[]{:S(2)}) collective-permute-start(bf16[256,1024]{1,0:T(8,128)(2,1)S(1)} %fusion.12), channel_id=1, source_target_pairs={{0,3},{1,2},{2,1},{3,0},{4,7},{5,6},{6,5},{7,4},{8,11},{9,10},{10,... | collective-permute-start | bytes 1572872 | tf_op jit(solution)/shard_map/ppermute | solution.py:223
  573.7 42.8 %collective-permute-start.38 = (bf16[256,1024]{1,0:T(8,128)(2,1)S(1)}, bf16[256,1024]{1,0:T(8,128)(2,1)S(1)}, u32[]{:S(2)}, u32[]{:S(2)}) collective-permute-start(bf16[256,1024]{1,0:T(8,128)(2,1)S(1)} %fusion.12), channel_id=1, source_target_pairs={{0,2},{1,3},{2,0},{3,1},{4,6},{5,7},{6,4},{7,5},{8,10},{9,11},{10,... | collective-permute-start | bytes 1572872 | tf_op jit(solution)/shard_map/ppermute | solution.py:223
  582.8 33.8 %collective-permute-start.37 = (bf16[256,1024]{1,0:T(8,128)(2,1)S(1)}, bf16[256,1024]{1,0:T(8,128)(2,1)S(1)}, u32[]{:S(2)}, u32[]{:S(2)}) collective-permute-start(bf16[256,1024]{1,0:T(8,128)(2,1)S(1)} %fusion.12), channel_id=1, source_target_pairs={{0,1},{1,0},{2,3},{3,2},{4,5},{5,4},{6,7},{7,6},{8,9},{9,8},{10,11... | collective-permute-start | bytes 1572872 | tf_op jit(solution)/shard_map/ppermute | solution.py:223
  594.3 24.0 %collective-permute-start.32 = (bf16[256,1024]{1,0:T(8,128)(2,1)S(1)}, bf16[256,1024]{1,0:T(8,128)(2,1)S(1)}, u32[]{:S(2)}, u32[]{:S(2)}) collective-permute-start(bf16[256,1024]{1,0:T(8,128)(2,1)S(1)} %get-tuple-element.48), channel_id=1, source_target_pairs={{4,0},{8,12},{5,1},{9,13},{6,2},{10,14},{7,3},{11,15},{20,16},{24,... | collective-permute-start | bytes 1572872 | tf_op jit(solution)/shard_map/ppermute | solution.py:218
  597.1 46.8 %collective-permute-start.43 = (bf16[64,8192]{1,0:T(8,128)(2,1)S(1)}, bf16[64,8192]{1,0:T(8,128)(2,1)S(1)}, u32[]{:S(2)}, u32[]{:S(2)}) collective-permute-start(bf16[64,8192]{1,0:T(8,128)(2,1)S(1)} %collective-permute-done.42.refs_2_), channel_id=1, source_target_pairs={{4,8},{8,4},{5,9},{9,5},{6,10},{10,6},{7,11},{11,7},{20,24},{24,20... | collective-permute-start | bytes 3145736 | tf_op jit(solution)/shard_map/ppermute | solution.py:211
  605.3 39.9 %collective-permute-start.41 = (bf16[64,8192]{1,0:T(8,128)(2,1)S(1)}, bf16[64,8192]{1,0:T(8,128)(2,1)S(1)}, u32[]{:S(2)}, u32[]{:S(2)}) collective-permute-start(bf16[64,8192]{1,0:T(8,128)(2,1)S(1)} %collective-permute-done.40.refs_0_), channel_id=1, source_target_pairs={{4,8},{8,4},{5,9},{9,5},{6,10},{10,6},{7,11},{11,7},{20,24},{24,20... | collective-permute-start | bytes 3145736 | tf_op jit(solution)/shard_map/ppermute | solution.py:211
  616.6 14.0 %collective-permute-start.51 = (bf16[256,1024]{1,0:T(8,128)(2,1)S(1)}, bf16[256,1024]{1,0:T(8,128)(2,1)S(1)}, u32[]{:S(2)}, u32[]{:S(2)}) collective-permute-start(bf16[256,1024]{1,0:T(8,128)(2,1)S(1)} %fusion.14), channel_id=1, source_target_pairs={{0,3},{1,2},{2,1},{3,0},{4,7},{5,6},{6,5},{7,4},{8,11},{9,10},{10,... | collective-permute-start | bytes 1572872 | tf_op jit(solution)/shard_map/ppermute | solution.py:223
  616.6 25.5 %collective-permute-start.50 = (bf16[256,1024]{1,0:T(8,128)(2,1)S(1)}, bf16[256,1024]{1,0:T(8,128)(2,1)S(1)}, u32[]{:S(2)}, u32[]{:S(2)}) collective-permute-start(bf16[256,1024]{1,0:T(8,128)(2,1)S(1)} %fusion.14), channel_id=1, source_target_pairs={{0,2},{1,3},{2,0},{3,1},{4,6},{5,7},{6,4},{7,5},{8,10},{9,11},{10,... | collective-permute-start | bytes 1572872 | tf_op jit(solution)/shard_map/ppermute | solution.py:223
  618.3 25.5 %collective-permute-start.49 = (bf16[256,1024]{1,0:T(8,128)(2,1)S(1)}, bf16[256,1024]{1,0:T(8,128)(2,1)S(1)}, u32[]{:S(2)}, u32[]{:S(2)}) collective-permute-start(bf16[256,1024]{1,0:T(8,128)(2,1)S(1)} %fusion.14), channel_id=1, source_target_pairs={{0,1},{1,0},{2,3},{3,2},{4,5},{5,4},{6,7},{7,6},{8,9},{9,8},{10,11... | collective-permute-start | bytes 1572872 | tf_op jit(solution)/shard_map/ppermute | solution.py:223
  630.6 29.8 %collective-permute-start.58 = (bf16[64,8192]{1,0:T(8,128)(2,1)S(1)}, bf16[64,8192]{1,0:T(8,128)(2,1)S(1)}, u32[]{:S(2)}, u32[]{:S(2)}) collective-permute-start(bf16[64,8192]{1,0:T(8,128)(2,1)S(1)} %copy-done.3), channel_id=1, source_target_pairs={{0,4},{12,8},{1,5},{13,9},{2,6},{14,10},{3,7},{15,11},{16,20},{28,... | collective-permute-start | bytes 3145736 | tf_op jit(solution)/shard_map/ppermute | solution.py:209
  642.0 35.6 %collective-permute-start.52 = (bf16[64,8192]{1,0:T(8,128)(2,1)S(1)}, bf16[64,8192]{1,0:T(8,128)(2,1)S(1)}, u32[]{:S(2)}, u32[]{:S(2)}) collective-permute-start(bf16[64,8192]{1,0:T(8,128)(2,1)S(1)} %copy-done.2), channel_id=1, source_target_pairs={{0,4},{12,8},{1,5},{13,9},{2,6},{14,10},{3,7},{15,11},{16,20},{28,... | collective-permute-start | bytes 3145736 | tf_op jit(solution)/shard_map/ppermute | solution.py:209
  643.8 34.9 %collective-permute-start.35 = (bf16[256,1024]{1,0:T(8,128)(2,1)S(1)}, bf16[256,1024]{1,0:T(8,128)(2,1)S(1)}, u32[]{:S(2)}, u32[]{:S(2)}) collective-permute-start(bf16[256,1024]{1,0:T(8,128)(2,1)S(1)} %fusion.11), channel_id=1, source_target_pairs={{0,3},{1,2},{2,1},{3,0},{4,7},{5,6},{6,5},{7,4},{8,11},{9,10},{10,... | collective-permute-start | bytes 1572872 | tf_op jit(solution)/shard_map/ppermute | solution.py:223
  643.9 35.8 %collective-permute-start.34 = (bf16[256,1024]{1,0:T(8,128)(2,1)S(1)}, bf16[256,1024]{1,0:T(8,128)(2,1)S(1)}, u32[]{:S(2)}, u32[]{:S(2)}) collective-permute-start(bf16[256,1024]{1,0:T(8,128)(2,1)S(1)} %fusion.11), channel_id=1, source_target_pairs={{0,2},{1,3},{2,0},{3,1},{4,6},{5,7},{6,4},{7,5},{8,10},{9,11},{10,... | collective-permute-start | bytes 1572872 | tf_op jit(solution)/shard_map/ppermute | solution.py:223
  645.2 34.5 %collective-permute-start.33 = (bf16[256,1024]{1,0:T(8,128)(2,1)S(1)}, bf16[256,1024]{1,0:T(8,128)(2,1)}, u32[]{:S(2)}, u32[]{:S(2)}) collective-permute-start(bf16[256,1024]{1,0:T(8,128)(2,1)S(1)} %fusion.11), channel_id=1, source_target_pairs={{0,1},{1,0},{2,3},{3,2},{4,5},{5,4},{6,7},{7,6},{8,9},{9,8},{10,11... | collective-permute-start | bytes 1572872 | tf_op jit(solution)/shard_map/ppermute | solution.py:223
  660.3 20.8 %collective-permute-start.44 = (bf16[256,1024]{1,0:T(8,128)(2,1)S(1)}, bf16[256,1024]{1,0:T(8,128)(2,1)S(1)}, u32[]{:S(2)}, u32[]{:S(2)}) collective-permute-start(bf16[256,1024]{1,0:T(8,128)(2,1)S(1)} %get-tuple-element.54), channel_id=1, source_target_pairs={{4,0},{8,12},{5,1},{9,13},{6,2},{10,14},{7,3},{11,15},{20,16},{24,... | collective-permute-start | bytes 1572872 | tf_op jit(solution)/shard_map/ppermute | solution.py:218
  678.7 18.1 %collective-permute-start.59 = (bf16[64,8192]{1,0:T(8,128)(2,1)S(1)}, bf16[64,8192]{1,0:T(8,128)(2,1)S(1)}, u32[]{:S(2)}, u32[]{:S(2)}) collective-permute-start(bf16[64,8192]{1,0:T(8,128)(2,1)S(1)} %collective-permute-done.58.refs_0_), channel_id=1, source_target_pairs={{4,8},{8,4},{5,9},{9,5},{6,10},{10,6},{7,11},{11,7},{20,24},{24,20... | collective-permute-start | bytes 3145736 | tf_op jit(solution)/shard_map/ppermute | solution.py:211
  681.4 67.3 %collective-permute-start.47 = (bf16[256,1024]{1,0:T(8,128)(2,1)S(1)}, bf16[256,1024]{1,0:T(8,128)(2,1)S(1)}, u32[]{:S(2)}, u32[]{:S(2)}) collective-permute-start(bf16[256,1024]{1,0:T(8,128)(2,1)S(1)} %fusion.13), channel_id=1, source_target_pairs={{0,3},{1,2},{2,1},{3,0},{4,7},{5,6},{6,5},{7,4},{8,11},{9,10},{10,... | collective-permute-start | bytes 1572872 | tf_op jit(solution)/shard_map/ppermute | solution.py:223
  681.6 68.0 %collective-permute-start.46 = (bf16[256,1024]{1,0:T(8,128)(2,1)S(1)}, bf16[256,1024]{1,0:T(8,128)(2,1)S(1)}, u32[]{:S(2)}, u32[]{:S(2)}) collective-permute-start(bf16[256,1024]{1,0:T(8,128)(2,1)S(1)} %fusion.13), channel_id=1, source_target_pairs={{0,2},{1,3},{2,0},{3,1},{4,6},{5,7},{6,4},{7,5},{8,10},{9,11},{10,... | collective-permute-start | bytes 1572872 | tf_op jit(solution)/shard_map/ppermute | solution.py:223
  682.9 67.6 %collective-permute-start.45 = (bf16[256,1024]{1,0:T(8,128)(2,1)S(1)}, bf16[256,1024]{1,0:T(8,128)(2,1)S(1)}, u32[]{:S(2)}, u32[]{:S(2)}) collective-permute-start(bf16[256,1024]{1,0:T(8,128)(2,1)S(1)} %fusion.13), channel_id=1, source_target_pairs={{0,1},{1,0},{2,3},{3,2},{4,5},{5,4},{6,7},{7,6},{8,9},{9,8},{10,11... | collective-permute-start | bytes 1572872 | tf_op jit(solution)/shard_map/ppermute | solution.py:223
  695.5 30.3 %collective-permute-start.54 = (bf16[128,1024]{1,0:T(8,128)(2,1)S(1)}, bf16[128,1024]{1,0:T(8,128)(2,1)S(1)}, u32[]{:S(2)}, u32[]{:S(2)}) collective-permute-start(bf16[128,1024]{1,0:T(8,128)(2,1)S(1)} %get-tuple-element.59), channel_id=1, source_target_pairs={{4,0},{8,12},{5,1},{9,13},{6,2},{10,14},{7,3},{11,15},{20,16},{24,... | collective-permute-start | bytes 786440 | tf_op jit(solution)/shard_map/ppermute | solution.py:218
  709.0 39.5 %collective-permute-start.60 = (bf16[128,1024]{1,0:T(8,128)(2,1)S(1)}, bf16[128,1024]{1,0:T(8,128)(2,1)S(1)}, u32[]{:S(2)}, u32[]{:S(2)}) collective-permute-start(bf16[128,1024]{1,0:T(8,128)(2,1)S(1)} %get-tuple-element.62), channel_id=1, source_target_pairs={{4,0},{8,12},{5,1},{9,13},{6,2},{10,14},{7,3},{11,15},{20,16},{24,... | collective-permute-start | bytes 786440 | tf_op jit(solution)/shard_map/ppermute | solution.py:218
  725.9 25.4 %collective-permute-start.57 = (bf16[128,1024]{1,0:T(8,128)(2,1)S(1)}, bf16[128,1024]{1,0:T(8,128)(2,1)S(1)}, u32[]{:S(2)}, u32[]{:S(2)}) collective-permute-start(bf16[128,1024]{1,0:T(8,128)(2,1)S(1)} %fusion.17), channel_id=1, source_target_pairs={{0,3},{1,2},{2,1},{3,0},{4,7},{5,6},{6,5},{7,4},{8,11},{9,10},{10,... | collective-permute-start | bytes 786440 | tf_op jit(solution)/shard_map/ppermute | solution.py:223
  748.6 18.9 %collective-permute-start.63 = (bf16[128,1024]{1,0:T(8,128)(2,1)S(1)}, bf16[128,1024]{1,0:T(8,128)(2,1)S(1)}, u32[]{:S(2)}, u32[]{:S(2)}) collective-permute-start(bf16[128,1024]{1,0:T(8,128)(2,1)S(1)} %fusion.18), channel_id=1, source_target_pairs={{0,3},{1,2},{2,1},{3,0},{4,7},{5,6},{6,5},{7,4},{8,11},{9,10},{10,... | collective-permute-start | bytes 786440 | tf_op jit(solution)/shard_map/ppermute | solution.py:223
  748.7 18.8 %collective-permute-start.62 = (bf16[128,1024]{1,0:T(8,128)(2,1)S(1)}, bf16[128,1024]{1,0:T(8,128)(2,1)S(1)}, u32[]{:S(2)}, u32[]{:S(2)}) collective-permute-start(bf16[128,1024]{1,0:T(8,128)(2,1)S(1)} %fusion.18), channel_id=1, source_target_pairs={{0,2},{1,3},{2,0},{3,1},{4,6},{5,7},{6,4},{7,5},{8,10},{9,11},{10,... | collective-permute-start | bytes 786440 | tf_op jit(solution)/shard_map/ppermute | solution.py:223
  749.6 17.9 %collective-permute-start.61 = (bf16[128,1024]{1,0:T(8,128)(2,1)S(1)}, bf16[128,1024]{1,0:T(8,128)(2,1)S(1)}, u32[]{:S(2)}, u32[]{:S(2)}) collective-permute-start(bf16[128,1024]{1,0:T(8,128)(2,1)S(1)} %fusion.18), channel_id=1, source_target_pairs={{0,1},{1,0},{2,3},{3,2},{4,5},{5,4},{6,7},{7,6},{8,9},{9,8},{10,11... | collective-permute-start | bytes 786440 | tf_op jit(solution)/shard_map/ppermute | solution.py:223
  750.5 16.8 %collective-permute-start.56 = (bf16[128,1024]{1,0:T(8,128)(2,1)S(1)}, bf16[128,1024]{1,0:T(8,128)(2,1)S(1)}, u32[]{:S(2)}, u32[]{:S(2)}) collective-permute-start(bf16[128,1024]{1,0:T(8,128)(2,1)S(1)} %fusion.17), channel_id=1, source_target_pairs={{0,2},{1,3},{2,0},{3,1},{4,6},{5,7},{6,4},{7,5},{8,10},{9,11},{10,... | collective-permute-start | bytes 786440 | tf_op jit(solution)/shard_map/ppermute | solution.py:223
  751.3 15.9 %collective-permute-start.55 = (bf16[128,1024]{1,0:T(8,128)(2,1)S(1)}, bf16[128,1024]{1,0:T(8,128)(2,1)S(1)}, u32[]{:S(2)}, u32[]{:S(2)}) collective-permute-start(bf16[128,1024]{1,0:T(8,128)(2,1)S(1)} %fusion.17), channel_id=1, source_target_pairs={{0,1},{1,0},{2,3},{3,2},{4,5},{5,4},{6,7},{7,6},{8,9},{9,8},{10,11... | collective-permute-start | bytes 786440 | tf_op jit(solution)/shard_map/ppermute | solution.py:223
  (25 other events, 794.7 us)
Sparse Core Ops, SparseCore 0:
  59.8 40.9 all-gather.2

commit v3 on v2

--- a/solution.py
+++ b/solution.py
@@ -103,30 +103,66 @@
     return lax.optimization_barrier((value, *earlier))[0]
 
 
-def project_kernel(count, *refs):
+def assemble_kernel(bounds, group_ref, *refs):
+    count = len(bounds)
+    near, far, out, sems = refs[:count], refs[count : 2 * count], refs[2 * count], refs[2 * count + 1]
+    half = near[0].shape[1]
+    group = group_ref[0]
+    copies = []
+    for i, (a, b) in enumerate(bounds):
+        for j, (ref, place) in enumerate(((near[i], group), (far[i], 1 - group))):
+            columns = pl.ds(pl.multiple_of(place * half, half), half)
+            copies.append(pltpu.make_async_copy(ref, out.at[pl.ds(a, b - a), columns], sems.at[i, j]))
+    for copy in copies:
+        copy.start()
+    for copy in copies:
+        copy.wait()
+
+
+def assemble(near, far, group):
+    bounds, start = [], 0
+    for x in near:
+        bounds.append((start, start + x.shape[0]))
+        start += x.shape[0]
+    return pl.pallas_call(
+        functools.partial(assemble_kernel, tuple(bounds)),
+        in_specs=[pl.BlockSpec(memory_space=pltpu.SMEM)]
+        + [pl.BlockSpec(memory_space=pl.ANY)] * (2 * len(near)),
+        out_specs=pl.BlockSpec(memory_space=pl.ANY),
+        out_shape=jax.ShapeDtypeStruct((start, 2 * near[0].shape[1]), BF16),
+        scratch_shapes=[pltpu.SemaphoreType.DMA((len(near), 2))],
+        compiler_params=pltpu.CompilerParams(vmem_limit_bytes=32 * 2**20),
+        cost_estimate=pl.CostEstimate(
+            flops=0, bytes_accessed=start * near[0].shape[1], transcendentals=0
+        ),
+    )(group.reshape(1), *near, *far)
+
+
+def project_kernel(count, bases, *refs):
     tokens = refs[:count]
-    own_ref, near_ref, far_ref, out_own, out_end, acc_own, acc_end = refs[count:]
+    basis = refs[count : count + bases]
+    outs = refs[count + bases : count + 2 * bases]
+    accs = refs[count + 2 * bases :]
     step = pl.program_id(0)
-
-    @pl.when(step == 0)
-    def _():
-        acc_own[...] = jnp.zeros_like(acc_own)
-        acc_end[...] = jnp.zeros_like(acc_end)
-
-    rows = jnp.concatenate([t[...] for t in tokens], axis=0)
-    half = near_ref.shape[1]
-    acc_own[...] += jnp.dot(rows, own_ref[...], preferred_element_type=F32)
-    acc_end[:, :half] += jnp.dot(rows, near_ref[...], preferred_element_type=F32)
-    acc_end[:, half:] += jnp.dot(rows, far_ref[...], preferred_element_type=F32)
-
-    @pl.when(step == pl.num_programs(0) - 1)
-    def _():
-        out_own[...] = acc_own[...].astype(BF16)
-        out_end[...] = acc_end[...].astype(BF16)
-
-
-def project(tokens, own, near, far):
-    feats, dirs = own.shape
+    rows = jnp.concatenate([t[...] for t in tokens], axis=0) if count > 1 else tokens[0][...]
+    for ref, out, acc in zip(basis, outs, accs):
+        term = jnp.dot(rows, ref[...], preferred_element_type=F32)
+
+        @pl.when(step == 0)
+        def _(term=term, acc=acc):
+            acc[...] = term
+
+        @pl.when(step > 0)
+        def _(term=term, acc=acc):
+            acc[...] += term
+
+        @pl.when(step == pl.num_programs(0) - 1)
+        def _(out=out, acc=acc):
+            out[...] = acc[...].astype(BF16)
+
+
+def project(tokens, bases):
+    feats, dirs = bases[0].shape
     block = 1024
     specs, total = [], 0
     for array, index in tokens:
@@ -136,26 +172,21 @@
             specs.append(pl.BlockSpec((n, block), lambda k: (0, k)))
         else:
             specs.append(pl.BlockSpec((None, n, block), lambda k, index=index: (index, 0, k)))
-    half = near.shape[1]
+    count = len(bases)
     return pl.pallas_call(
-        functools.partial(project_kernel, len(tokens)),
+        functools.partial(project_kernel, len(tokens), count),
         grid=(feats // block,),
-        in_specs=specs
-        + [
-            pl.BlockSpec((block, dirs), lambda k: (k, 0)),
-            pl.BlockSpec((block, half), lambda k: (k, 0)),
-            pl.BlockSpec((block, half), lambda k: (k, 0)),
-        ],
-        out_specs=[pl.BlockSpec((total, dirs), lambda k: (0, 0))] * 2,
-        out_shape=[jax.ShapeDtypeStruct((total, dirs), BF16)] * 2,
-        scratch_shapes=[pltpu.VMEM((total, dirs), F32)] * 2,
+        in_specs=specs + [pl.BlockSpec((block, dirs), lambda k: (k, 0))] * count,
+        out_specs=[pl.BlockSpec((total, dirs), lambda k: (0, 0))] * count,
+        out_shape=[jax.ShapeDtypeStruct((total, dirs), BF16)] * count,
+        scratch_shapes=[pltpu.VMEM((total, dirs), F32)] * count,
         compiler_params=pltpu.CompilerParams(vmem_limit_bytes=40 * 2**20),
         cost_estimate=pl.CostEstimate(
-            flops=4 * total * feats * dirs,
-            bytes_accessed=4 * feats * dirs + 2 * total * feats,
+            flops=count * total * feats * dirs // 16,
+            bytes_accessed=(count * feats * dirs + total * feats) // 16,
             transcendentals=0,
         ),
-    )(*[array for array, _ in tokens], own, near, far)
+    )(*[array for array, _ in tokens], *bases)
 
 
 def after(value, *earlier):
@@ -185,57 +216,74 @@
     every_act = lax.all_gather(local_act, "row", axis=0)
 
     half = dirs // sides
-    pieces = 8
-    deep = feats // pieces
-    half_cands = cands // 2
-    other, near, far = [], [], []
-    spans = [(0, 1), (1, 3), (3, 5), (5, 7), (7, 8)]
-    for i, (a, b) in enumerate(spans):
+    flat = grads.reshape(cands * tok, feats)
+    units, deep, slab = 8, feats // 8, cands * tok // 8
+    near, far, other = [], [], []
+    own_own, = project([(flat, None)], [grad_basis])
+    for i, (a, b) in enumerate([(0, 1), (1, 3), (3, 5), (5, 7), (7, units)]):
         piece = lax.dynamic_slice(grad_basis, (a * deep, group * half), ((b - a) * deep, half))
+        tokens = flat[a * slab : b * slab]
         if i >= 2:
-            piece = after(piece, near[i - 2], *other)
+            tie = [near[i - 2], other[i - 2]] + ([own_own, local_act] if i == 2 else [])
+            piece, tokens = after(piece, *tie), after(tokens, *tie)
+        other.append(lax.ppermute(tokens, "row", across))
         near.append(lax.ppermute(piece, "row", inward))
         far.append(lax.ppermute(near[i], ("groups", "row"), swap))
-        if i in (0, 2):
-            part = grads[:half_cands] if i == 0 else grads[half_cands:]
-            other.append(lax.ppermute(part if i == 0 else after(part, near[0]), "row", across))
 
     chunk = tok // 2
-    started = list(near)
-    first, second = [], []
-    for c in range(cands):
-        for s in range(0, tok, chunk):
-            piece = after(grads[c, s : s + chunk], started[-2], *other)
-            first.append(lax.ppermute(piece, "row", inward))
-            started.append(first[-1])
-            second.append(lax.ppermute(first[-1], "row", across))
-
-    near_basis = jnp.concatenate(near, axis=0)
-    far_basis = jnp.concatenate(far, axis=0)
-
-    def reduce(tokens):
-        own, end = project(tokens, grad_basis, near_basis, far_basis)
-        back = lax.ppermute(end, "row", outward)
-        swapped = jnp.concatenate([back[:, half:], back[:, :half]], axis=1)
-        mine = jnp.where(at_end, jnp.where(group == 0, back, swapped), own)
+    halves = [(c, s) for c in range(cands) for s in range(0, tok, chunk)]
+    first, second, ties = [], [], {}
+    ties[0] = [near[3], far[1], other[3]]
+    ties[1] = [near[4], far[2], other[4]]
+    ties[2] = [far[3]]
+    ties[3] = [far[4]]
+    end_basis = assemble(near, far, group)
+    outer = []
+    for k, (c, s) in enumerate(halves):
+        tie = ties.get(k, [])
+        if k >= 2:
+            tie = tie + [first[k - 2]]
+        if k >= 3:
+            tie = tie + [second[k - 3]]
+        first.append(lax.ppermute(after(grads[c, s : s + chunk], *tie), "row", inward))
+        second.append(lax.ppermute(first[k], "row", across))
+        if k == 0:
+            other_own, = project([(x, None) for x in other], [after(grad_basis, first[0])])
+            ties[3].append(other_own)
+        if k == 1:
+            own_end, = project([(flat, None)], [after(end_basis, first[1], other_own)])
+            ties[4] = [own_end]
+        if k == 2:
+            other_end, = project([(x, None) for x in other], [after(end_basis, first[2], own_end)])
+            ties[5] = [other_end]
+        if k in (4, 5, 7):
+            i = 2 * len(outer)
+            last = outer[-1][0] if outer else other_end
+            sources = [(x, None) for x in (first[i], second[i], first[i + 1], second[i + 1])]
+            outer.append(project(sources, [grad_basis, after(end_basis, *first[k - 1 :], last)]))
+            ties[k + 3] = [outer[-1][0]]
+    sources = [(x, None) for x in (first[6], second[6], first[7], second[7])]
+    outer.append(project(sources, [grad_basis, end_basis]))
+
+    def settle(own, end):
+        return jnp.where(at_end, lax.ppermute(end, "row", outward), own)
+
+    def gather(own, end):
+        every = lax.all_gather(settle(own, end), "col", axis=0)
+        return jnp.sum(every.astype(F32), axis=0).astype(BF16)
+
+    def exchange(own, end):
+        mine = settle(own, end)
         total = mine.astype(F32)
         for d in range(1, parts):
             total = total + lax.ppermute(mine, "col", [(i, i ^ d) for i in range(parts)]).astype(F32)
         return total.astype(BF16)
 
-    pieces_of = []
-    for c in range(cands):
-        inner = reduce([(grads, c), (other[c // half_cands], c % half_cands)])
-        pieces_of.append([inner])
-    for c in range(cands):
-        if c < cands - 1:
-            k = 2 * c
-            pieces_of[c].append(
-                reduce([(first[k], None), (second[k], None), (first[k + 1], None), (second[k + 1], None)])
-            )
-        else:
-            for k in (2 * c, 2 * c + 1):
-                pieces_of[c].append(reduce([(first[k], None), (second[k], None)]))
+    own_sum = gather(own_own, own_end)
+    other_sum = gather(other_own, other_end)
+    pieces_of = [[own_sum[c * tok : (c + 1) * tok], other_sum[c * tok : (c + 1) * tok]] for c in range(cands)]
+    for c, products in enumerate(outer):
+        pieces_of[c].append(gather(*products) if c < cands - 1 else exchange(*products))
 
     blocks = jnp.where(row < 2, every_act, every_act[::-1])
     order = [blocks[1], blocks[2]]

time: 793 us -> 802 us (1.011)
  starting transfers between devices: 287 us -> 178 us
  Pallas kernels: 141 us -> 230 us
  other arithmetic: 12 us -> 24.2 us
  waiting for transfers between devices: 284 us -> 296 us
    ppermute x5, starting transfers between devices: 181 us -> 70.6 us  [chain_body(): near.append(lax.ppermute(piece, 'row', inward))]
    pallas_call x9, Pallas kernels: 136 us -> 225 us  [the longest x8 129 us: project(): pl.pallas_call(functools.partial(project_kernel, len(tokens), count), gri...]
    ppermute x5, waiting for transfers between devices: 59.8 us -> 82.5 us  [chain_body(): near.append(lax.ppermute(piece, 'row', inward))]
    reduce_sum x0 -> x5, other arithmetic: none -> 14.9 us  [gather(): return jnp.sum(every.astype(F32), axis=0).astype(BF16)]
    ppermute x54 -> x30, waiting for transfers between devices: 219 us -> 209 us  [the longest x6 113 us: settle(): return jnp.where(at_end, lax.ppermute(end, 'row', outward), own)]
    unnamed x49 -> x87, local copies, waits for them, and re-layouts: 20.9 us -> 24.7 us
    ppermute x54 -> x30, starting transfers between devices: 93.4 us -> 96.2 us  [the longest x8 74.4 us: chain_body(): lax.ppermute(after(grads[c, s:s + chunk], *tie), 'row', inward)]
  transfers between devices with their start and end apart: 71 -> 52, of which waited for: 25 -> 21; matrix products, arithmetic and copies ran while one was open for 8% -> 5% of each run, Pallas kernels for 17% -> 28%
where the time goes in v3:
time: 802 us; the launch traced here: 800 us
  waiting for transfers between devices  296 us (37%)
  Pallas kernels  230 us (29%)
  starting transfers between devices  178 us (22%)
  local copies, waits for them, and re-layouts  50.2 us (6%)
  other arithmetic  24.2 us (3%)
  between operations  14.9 us (2%)
    pallas_call x8, Pallas kernels, project(): pl.pallas_call(functools.partial(project_kernel, len(tokens), count), gri...  129 us
    ppermute x6, waiting for transfers between devices, settle(): return jnp.where(at_end, lax.ppermute(end, 'row', outward), own)  113 us
    pallas_call x1, Pallas kernels, assemble(): pl.pallas_call(functools.partial(assemble_kernel, tuple(bounds)), in_spec...  96.5 us
    ppermute x5, waiting for transfers between devices, chain_body(): near.append(lax.ppermute(piece, 'row', inward))  82.5 us
    ppermute x8, waiting for transfers between devices, chain_body(): lax.ppermute(after(grads[c, s:s + chunk], *tie), 'row', inward)  75.5 us
    ppermute x8, starting transfers between devices, chain_body(): lax.ppermute(after(grads[c, s:s + chunk], *tie), 'row', inward)  74.4 us
    ppermute x5, starting transfers between devices, chain_body(): near.append(lax.ppermute(piece, 'row', inward))  70.6 us
    unnamed x87, local copies, waits for them, and re-layouts  24.7 us
  transfers between devices with their start and end apart: 52, of which 21 were waited for; matrix products, arithmetic and copies ran while one was open for 5% of the time, Pallas kernels for 28%

profile of v3, /device:TPU:0, one launch (start us, length us, event | category | flops | bytes accessed | tf_op | source)
XLA Modules:
  0.0 800.0 jit_solution(16573137351748910387)
XLA Ops:
  7.2 5.8 fusion.10
  13.8 5.8 constant_dynamic-slice_fusion.1
  19.5 8.9 %collective-permute-start.1 = (bf16[2048,512]{1,0:T(8,128)(2,1)}, bf16[2048,512]{1,0:T(8,128)(2,1)}, u32[]{:S(2)}, u32[]{:S(2)}) collective-permute-start(bf16[2048,512]{1,0:T(8,128)(2,1)} %get-tuple-element.66), channel_id=1, source_target_pairs={{0,4},{12,8},{1,5},{13,9},{2,6},{14,10},{3,7},{15,11},{16,20},{28,... | collective-permute-start | bytes 6291464 | tf_op jit(solution)/shard_map/ppermute | solution.py:230
  28.4 3.1 fusion.11
  32.3 3.1 constant_dynamic-slice_fusion
  35.4 2.6 collective-permute-start
  38.0 3.4 copy-done
  41.4 14.2 %shard_map.95 = bf16[512,1024]{1,0:T(8,128)(2,1)S(1)} custom-call(bf16[512,8192]{1,0:T(8,128)(2,1)S(1)} %bitcast.46, bf16[8192,1024]{1,0:T(8,128)(2,1)} %refs_4_.7), custom_call_target="tpu_custom_call" | custom-call | flops 268435456 | bytes 786432 | tf_op jit(solution)/shard_map/pallas_call | solution.py:176
  56.9 6.4 fusion.5
  63.4 31.1 %collective-permute-done.refs_0_ = bf16[1024,512]{1,0:T(8,128)(2,1)} collective-permute-done((bf16[1024,512]{1,0:T(8,128)(2,1)}, bf16[1024,512]{1,0:T(8,128)(2,1)}, u32[]{:S(2)}, u32[]{:S(2)}) %collective-permute-start) | collective-permute-done | bytes 1048608 | tf_op jit(solution)/shard_map/ppermute | solution.py:230
  94.5 4.5 collective-permute-start.3
  100.6 5.5 collective-permute-start.5
  107.0 38.3 %collective-permute-done.3.refs_2_ = bf16[2048,512]{1,0:T(8,128)(2,1)S(1)} collective-permute-done((bf16[2048,512]{1,0:T(8,128)(2,1)}, bf16[2048,512]{1,0:T(8,128)(2,1)S(1)}, u32[]{:S(2)}, u32[]{:S(2)}) %collective-permute-start.3) | collective-permute-done | bytes 2097184 | tf_op jit(solution)/shard_map/ppermute | solution.py:230
  146.8 49.0 %collective-permute-start.7 = (bf16[1024,512]{1,0:T(8,128)(2,1)}, bf16[1024,512]{1,0:T(8,128)(2,1)S(1)}, u32[]{:S(2)}, u32[]{:S(2)}) collective-permute-start(bf16[1024,512]{1,0:T(8,128)(2,1)} %get-tuple-element.35), channel_id=1, source_target_pairs={{0,4},{12,8},{1,5},{13,9},{2,6},{14,10},{3,7},{15,11},{16,20},{28,... | collective-permute-start | bytes 3145736 | tf_op jit(solution)/shard_map/ppermute | solution.py:230
  196.7 5.9 slice_bitcast_fusion
  202.6 4.0 collective-permute-start.16
  206.6 13.1 %collective-permute-done.7.refs_4_ = bf16[1024,512]{1,0:T(8,128)(2,1)S(1)} collective-permute-done((bf16[1024,512]{1,0:T(8,128)(2,1)}, bf16[1024,512]{1,0:T(8,128)(2,1)S(1)}, u32[]{:S(2)}, u32[]{:S(2)}) %collective-permute-start.7) | collective-permute-done | bytes 1048608 | tf_op jit(solution)/shard_map/ppermute | solution.py:230
  219.7 5.3 collective-permute-start.14
  226.4 15.6 %collective-permute-done.16.refs_0_ = bf16[64,8192]{1,0:T(8,128)(2,1)S(1)} collective-permute-done((bf16[64,8192]{1,0:T(8,128)(2,1)S(1)}, bf16[64,8192]{1,0:T(8,128)(2,1)S(1)}, u32[]{:S(2)}, u32[]{:S(2)}) %collective-permute-start.16) | collective-permute-done | bytes 1048608 | tf_op jit(solution)/shard_map/ppermute | solution.py:248
  242.1 1.6 collective-permute-start.20
  243.7 6.1 collective-permute-start.18
  249.8 14.7 %collective-permute-done.14.refs_2_ = bf16[64,8192]{1,0:T(8,128)(2,1)} collective-permute-done((bf16[64,8192]{1,0:T(8,128)(2,1)S(1)}, bf16[64,8192]{1,0:T(8,128)(2,1)}, u32[]{:S(2)}, u32[]{:S(2)}) %collective-permute-start.14) | collective-permute-done | bytes 1048608 | tf_op jit(solution)/shard_map/ppermute | solution.py:248
  264.5 1.6 collective-permute-start.21
  266.2 14.1 %shard_map.97 = bf16[512,1024]{1,0:T(8,128)(2,1)S(1)} custom-call(bf16[64,8192]{1,0:T(8,128)(2,1)S(1)} %collective-permute-done.2.refs_0_, bf16[128,8192]{1,0:T(8,128)(2,1)S(1)} %collective-permute-done.4.refs_1_, bf16[128,8192]{1,0:T(8,128)(2,1)S(1)} %collective-permute-done.6.refs_2_, bf16[128,8192]{1,0:T(8,128)(2,1)S(1)} %collective-permute-done.15.refs_3_, ...), custom_call_target="tpu_custom_call" | custom-call | flops 268435456 | bytes 786432 | tf_op jit(solution)/shard_map/pallas_call | solution.py:176
  283.4 1.7 copy-done.12
  285.2 1.7 copy-done.14
  286.9 1.6 copy-done.16
  288.5 1.6 copy-done.18
  293.8 96.5 %shard_map.96.refs_1_.refs_5_ = bf16[8192,1024]{1,0:T(8,128)(2,1)} custom-call(s32[1]{0:T(128)} %bitcast.1.group_ref, bf16[1024,512]{1,0:T(8,128)(2,1)} %collective-permute-done.refs_0_, bf16[2048,512]{1,0:T(8,128)(2,1)} %collective-permute-done.1.refs_1_, bf16[2048,512]{1,0:T(8,128)(2,1)S(1)} %collective-permute-done.3.refs_2_, ...), custom_call_target="tpu_custom_call" | custom-call | bytes 4194304 | tf_op jit(solution)/shard_map/pallas_call | solution.py:127
  390.3 8.5 %collective-permute-start.22 = (bf16[64,8192]{1,0:T(8,128)(2,1)}, bf16[64,8192]{1,0:T(8,128)(2,1)}, u32[]{:S(2)}, u32[]{:S(2)}) collective-permute-start(bf16[64,8192]{1,0:T(8,128)(2,1)} %get-tuple-element.44), channel_id=1, source_target_pairs={{0,4},{12,8},{1,5},{13,9},{2,6},{14,10},{3,7},{15,11},{16,20},{28,... | collective-permute-start | bytes 3145736 | tf_op jit(solution)/shard_map/ppermute | solution.py:248
  398.8 14.1 %shard_map.98 = bf16[512,1024]{1,0:T(8,128)(2,1)S(1)} custom-call(bf16[512,8192]{1,0:T(8,128)(2,1)S(1)} %bitcast.49, bf16[8192,1024]{1,0:T(8,128)(2,1)} %shard_map.96.refs_1_.refs_5_), custom_call_target="tpu_custom_call" | custom-call | flops 268435456 | bytes 786432 | tf_op jit(solution)/shard_map/pallas_call | solution.py:176
  413.8 2.3 collective-permute-start.23
  416.4 1.6 copy-done.2
  417.9 1.6 copy-done.4
  420.8 14.3 %shard_map.99 = bf16[512,1024]{1,0:T(8,128)(2,1)S(1)} custom-call(bf16[64,8192]{1,0:T(8,128)(2,1)S(1)} %collective-permute-done.2.refs_0_, bf16[128,8192]{1,0:T(8,128)(2,1)S(1)} %collective-permute-done.4.refs_1_, bf16[128,8192]{1,0:T(8,128)(2,1)S(1)} %copy-done.2, bf16[128,8192]{1,0:T(8,128)(2,1)S(1)} %copy-done.4, bf16[64,8192]{1,0:T(8,128)(2,1)S(1)} %copy-done.6, ...), custom_call_target="tpu_custom_call" | custom-call | flops 268435456 | bytes 786432 | tf_op jit(solution)/shard_map/pallas_call | solution.py:176
  435.1 22.0 %collective-permute-done.23.refs_0_ = bf16[64,8192]{1,0:T(8,128)(2,1)} collective-permute-done((bf16[64,8192]{1,0:T(8,128)(2,1)}, bf16[64,8192]{1,0:T(8,128)(2,1)}, u32[]{:S(2)}, u32[]{:S(2)}) %collective-permute-start.23) | collective-permute-done | bytes 1048608 | tf_op jit(solution)/shard_map/ppermute | solution.py:248
  457.1 18.1 %shard_map.100 = (bf16[256,1024]{1,0:T(8,128)(2,1)S(1)}, bf16[256,1024]{1,0:T(8,128)(2,1)S(1)}) custom-call(bf16[64,8192]{1,0:T(8,128)(2,1)S(1)} %copy-done.25, bf16[64,8192]{1,0:T(8,128)(2,1)} %collective-permute-done.20.refs_1_, bf16[64,8192]{1,0:T(8,128)(2,1)} %collective-permute-done.14.refs_2_, bf16[64,8192]{1,0:T(8,128)(2,1)} %collective-permute-done.21.refs_3_, ...), custom_call_target="tpu_custom_call" | custom-call | flops 268435456 | bytes 1179648 | tf_op jit(solution)/shard_map/pallas_call | solution.py:176
  476.7 9.8 %collective-permute-done.24 = bf16[256,1024]{1,0:T(8,128)(2,1)S(1)} collective-permute-done((bf16[256,1024]{1,0:T(8,128)(2,1)S(1)}, bf16[256,1024]{1,0:T(8,128)(2,1)S(1)}, u32[]{:S(2)}, u32[]{:S(2)}) %collective-permute-start.24) | collective-permute-done | bytes 524320 | tf_op jit(solution)/shard_map/ppermute | solution.py:269
  488.1 22.8 %collective-permute-start.27 = (bf16[64,8192]{1,0:T(8,128)(2,1)S(1)}, bf16[64,8192]{1,0:T(8,128)(2,1)S(1)}, u32[]{:S(2)}, u32[]{:S(2)}) collective-permute-start(bf16[64,8192]{1,0:T(8,128)(2,1)S(1)} %copy-done.34), channel_id=1, source_target_pairs={{0,4},{12,8},{1,5},{13,9},{2,6},{14,10},{3,7},{15,11},{16,20},{28,... | collective-permute-start | bytes 3145736 | tf_op jit(solution)/shard_map/ppermute | solution.py:248
  511.7 11.5 %collective-permute-done.27.refs_2_ = bf16[64,8192]{1,0:T(8,128)(2,1)S(1)} collective-permute-done((bf16[64,8192]{1,0:T(8,128)(2,1)S(1)}, bf16[64,8192]{1,0:T(8,128)(2,1)S(1)}, u32[]{:S(2)}, u32[]{:S(2)}) %collective-permute-start.27) | collective-permute-done | bytes 1048608 | tf_op jit(solution)/shard_map/ppermute | solution.py:248
  523.2 17.9 %shard_map.101 = (bf16[256,1024]{1,0:T(8,128)(2,1)S(1)}, bf16[256,1024]{1,0:T(8,128)(2,1)S(1)}) custom-call(bf16[64,8192]{1,0:T(8,128)(2,1)} %collective-permute-done.18.refs_0_, bf16[64,8192]{1,0:T(8,128)(2,1)S(1)} %collective-permute-done.25.refs_1_, bf16[64,8192]{1,0:T(8,128)(2,1)} %collective-permute-done.22.refs_2_, ...), custom_call_target="tpu_custom_call" | custom-call | flops 268435456 | bytes 1179648 | tf_op jit(solution)/shard_map/pallas_call | solution.py:176
  542.5 17.6 %collective-permute-done.28 = bf16[256,1024]{1,0:T(8,128)(2,1)S(1)} collective-permute-done((bf16[256,1024]{1,0:T(8,128)(2,1)S(1)}, bf16[256,1024]{1,0:T(8,128)(2,1)S(1)}, u32[]{:S(2)}, u32[]{:S(2)}) %collective-permute-start.28) | collective-permute-done | bytes 524320 | tf_op jit(solution)/shard_map/ppermute | solution.py:269
  562.3 15.4 %collective-permute-done.17 = bf16[512,1024]{1,0:T(8,128)(2,1)S(1)} collective-permute-done((bf16[512,1024]{1,0:T(8,128)(2,1)S(1)}, bf16[512,1024]{1,0:T(8,128)(2,1)S(1)}, u32[]{:S(2)}, u32[]{:S(2)}) %collective-permute-start.17) | collective-permute-done | bytes 1048608 | tf_op jit(solution)/shard_map/ppermute | solution.py:269
  579.6 3.9 collective-permute-start.31
  583.5 21.6 %collective-permute-start.32 = (bf16[64,8192]{1,0:T(8,128)(2,1)S(1)}, bf16[64,8192]{1,0:T(8,128)(2,1)}, u32[]{:S(2)}, u32[]{:S(2)}) collective-permute-start(bf16[64,8192]{1,0:T(8,128)(2,1)S(1)} %copy-done.33), channel_id=1, source_target_pairs={{0,4},{12,8},{1,5},{13,9},{2,6},{14,10},{3,7},{15,11},{16,20},{28,... | collective-permute-start | bytes 3145736 | tf_op jit(solution)/shard_map/ppermute | solution.py:248
  605.9 11.7 %collective-permute-done.32.refs_2_ = bf16[64,8192]{1,0:T(8,128)(2,1)} collective-permute-done((bf16[64,8192]{1,0:T(8,128)(2,1)S(1)}, bf16[64,8192]{1,0:T(8,128)(2,1)}, u32[]{:S(2)}, u32[]{:S(2)}) %collective-permute-start.32) | collective-permute-done | bytes 1048608 | tf_op jit(solution)/shard_map/ppermute | solution.py:248
  617.6 17.6 %shard_map.102 = (bf16[256,1024]{1,0:T(8,128)(2,1)S(1)}, bf16[256,1024]{1,0:T(8,128)(2,1)S(1)}) custom-call(bf16[64,8192]{1,0:T(8,128)(2,1)} %collective-permute-done.23.refs_0_, bf16[64,8192]{1,0:T(8,128)(2,1)S(1)} %collective-permute-done.29.refs_1_, bf16[64,8192]{1,0:T(8,128)(2,1)S(1)} %collective-permute-done.27.refs_2_, ...), custom_call_target="tpu_custom_call" | custom-call | flops 268435456 | bytes 1179648 | tf_op jit(solution)/shard_map/pallas_call | solution.py:176
  636.6 15.5 %collective-permute-done.33 = bf16[256,1024]{1,0:T(8,128)(2,1)S(1)} collective-permute-done((bf16[256,1024]{1,0:T(8,128)(2,1)S(1)}, bf16[256,1024]{1,0:T(8,128)(2,1)S(1)}, u32[]{:S(2)}, u32[]{:S(2)}) %collective-permute-start.33) | collective-permute-done | bytes 524320 | tf_op jit(solution)/shard_map/ppermute | solution.py:269
  654.4 15.4 %collective-permute-done.19 = bf16[512,1024]{1,0:T(8,128)(2,1)S(1)} collective-permute-done((bf16[512,1024]{1,0:T(8,128)(2,1)S(1)}, bf16[512,1024]{1,0:T(8,128)(2,1)S(1)}, u32[]{:S(2)}, u32[]{:S(2)}) %collective-permute-start.19) | collective-permute-done | bytes 1048608 | tf_op jit(solution)/shard_map/ppermute | solution.py:269
  672.4 1.9 reverse_select_fusion
  674.4 18.4 %shard_map.103 = (bf16[256,1024]{1,0:T(8,128)(2,1)S(1)}, bf16[256,1024]{1,0:T(8,128)(2,1)S(1)}) custom-call(bf16[64,8192]{1,0:T(8,128)(2,1)} %collective-permute-done.31.refs_0_, bf16[64,8192]{1,0:T(8,128)(2,1)S(1)} %collective-permute-done.34.refs_1_, bf16[64,8192]{1,0:T(8,128)(2,1)} %collective-permute-done.32.refs_2_, ...), custom_call_target="tpu_custom_call" | custom-call | flops 268435456 | bytes 1179648 | tf_op jit(solution)/shard_map/pallas_call | solution.py:176
  694.4 39.7 %collective-permute-done.36 = bf16[256,1024]{1,0:T(8,128)(2,1)S(1)} collective-permute-done((bf16[256,1024]{1,0:T(8,128)(2,1)S(1)}, bf16[256,1024]{1,0:T(8,128)(2,1)S(1)}, u32[]{:S(2)}, u32[]{:S(2)}) %collective-permute-start.36) | collective-permute-done | bytes 524320 | tf_op jit(solution)/shard_map/ppermute | solution.py:269
  736.2 2.0 reduce_sum.81.refs_2_
  738.3 10.2 %collective-permute-done.39 = bf16[256,1024]{1,0:T(8,128)(2,1)S(1)} collective-permute-done((bf16[256,1024]{1,0:T(8,128)(2,1)S(1)}, bf16[256,1024]{1,0:T(8,128)(2,1)S(1)}, u32[]{:S(2)}, u32[]{:S(2)}) %collective-permute-start.39) | collective-permute-done | bytes 524320 | tf_op jit(solution)/shard_map/ppermute | solution.py:279
  748.5 10.0 %collective-permute-done.38 = bf16[256,1024]{1,0:T(8,128)(2,1)S(1)} collective-permute-done((bf16[256,1024]{1,0:T(8,128)(2,1)S(1)}, bf16[256,1024]{1,0:T(8,128)(2,1)S(1)}, u32[]{:S(2)}, u32[]{:S(2)}) %collective-permute-start.38) | collective-permute-done | bytes 524320 | tf_op jit(solution)/shard_map/ppermute | solution.py:279
  759.3 1.6 add_convert_fusion.refs_11_
  760.9 2.0 reduce_sum.82.refs_5_
  762.9 4.4 reduce_sum.79
  767.3 2.0 reduce_sum.83.refs_8_
  769.4 4.4 reduce_sum.80
  773.8 1.8 fusion.12
  776.3 5.1 shard_map.104
  784.6 2.0 collective-permute-done.41
  787.8 3.2 collective-permute-start.43
  (173 shorter events, 46.3 us)
Async XLA Ops:
  7.2 665.2 %all-gather.23.cloned.1.call-start = ((), (), s32[]{:S(2)}) async-start(), calls=%async_computation.5 | async-start | bytes 1310720 | tf_op jit(solution)/shard_map/all_gather | solution.py:216
  13.0 86.9 %collective-permute-start.4 = (bf16[128,8192]{1,0:T(8,128)(2,1)}, bf16[128,8192]{1,0:T(8,128)(2,1)S(1)}, u32[]{:S(2)}, u32[]{:S(2)}) collective-permute-start(bf16[128,8192]{1,0:T(8,128)(2,1)} %get-tuple-element.77), channel_id=1, source_target_pairs={{4,8},{8,4},{5,9},{9,5},{6,10},{10,6},{7,11},{11,7},{20,24},{24,20... | collective-permute-start | bytes 6291464 | tf_op jit(solution)/shard_map/ppermute | solution.py:229
  19.5 80.3 %collective-permute-start.1 = (bf16[2048,512]{1,0:T(8,128)(2,1)}, bf16[2048,512]{1,0:T(8,128)(2,1)}, u32[]{:S(2)}, u32[]{:S(2)}) collective-permute-start(bf16[2048,512]{1,0:T(8,128)(2,1)} %get-tuple-element.66), channel_id=1, source_target_pairs={{0,4},{12,8},{1,5},{13,9},{2,6},{14,10},{3,7},{15,11},{16,20},{28,... | collective-permute-start | bytes 6291464 | tf_op jit(solution)/shard_map/ppermute | solution.py:230
  31.6 31.8 %collective-permute-start.2 = (bf16[64,8192]{1,0:T(8,128)(2,1)}, bf16[64,8192]{1,0:T(8,128)(2,1)S(1)}, u32[]{:S(2)}, u32[]{:S(2)}) collective-permute-start(bf16[64,8192]{1,0:T(8,128)(2,1)} %get-tuple-element.79), channel_id=1, source_target_pairs={{4,8},{8,4},{5,9},{9,5},{6,10},{10,6},{7,11},{11,7},{20,24},{24,20... | collective-permute-start | bytes 3145736 | tf_op jit(solution)/shard_map/ppermute | solution.py:229
  35.4 59.1 %collective-permute-start = (bf16[1024,512]{1,0:T(8,128)(2,1)}, bf16[1024,512]{1,0:T(8,128)(2,1)}, u32[]{:S(2)}, u32[]{:S(2)}) collective-permute-start(bf16[1024,512]{1,0:T(8,128)(2,1)} %get-tuple-element.63), channel_id=1, source_target_pairs={{0,4},{12,8},{1,5},{13,9},{2,6},{14,10},{3,7},{15,11},{16,20},{28,... | collective-permute-start | bytes 3145736 | tf_op jit(solution)/shard_map/ppermute | solution.py:230
  94.5 50.8 %collective-permute-start.3 = (bf16[2048,512]{1,0:T(8,128)(2,1)}, bf16[2048,512]{1,0:T(8,128)(2,1)S(1)}, u32[]{:S(2)}, u32[]{:S(2)}) collective-permute-start(bf16[2048,512]{1,0:T(8,128)(2,1)} %get-tuple-element.32), channel_id=1, source_target_pairs={{0,4},{12,8},{1,5},{13,9},{2,6},{14,10},{3,7},{15,11},{16,20},{28,... | collective-permute-start | bytes 6291464 | tf_op jit(solution)/shard_map/ppermute | solution.py:230
  99.0 47.0 %collective-permute-start.6 = (bf16[128,8192]{1,0:T(8,128)(2,1)}, bf16[128,8192]{1,0:T(8,128)(2,1)S(1)}, u32[]{:S(2)}, u32[]{:S(2)}) collective-permute-start(bf16[128,8192]{1,0:T(8,128)(2,1)} %get-tuple-element.34), channel_id=1, source_target_pairs={{4,8},{8,4},{5,9},{9,5},{6,10},{10,6},{7,11},{11,7},{20,24},{24,20... | collective-permute-start | bytes 6291464 | tf_op jit(solution)/shard_map/ppermute | solution.py:229
  99.8 47.0 %collective-permute-start.15 = (bf16[128,8192]{1,0:T(8,128)(2,1)}, bf16[128,8192]{1,0:T(8,128)(2,1)S(1)}, u32[]{:S(2)}, u32[]{:S(2)}) collective-permute-start(bf16[128,8192]{1,0:T(8,128)(2,1)} %get-tuple-element.38), channel_id=1, source_target_pairs={{4,8},{8,4},{5,9},{9,5},{6,10},{10,6},{7,11},{11,7},{20,24},{24,20... | collective-permute-start | bytes 6291464 | tf_op jit(solution)/shard_map/ppermute | solution.py:229
  100.6 95.2 %collective-permute-start.5 = (bf16[2048,512]{1,0:T(8,128)(2,1)}, bf16[2048,512]{1,0:T(8,128)(2,1)S(1)}, u32[]{:S(2)}, u32[]{:S(2)}) collective-permute-start(bf16[2048,512]{1,0:T(8,128)(2,1)} %get-tuple-element.33), channel_id=1, source_target_pairs={{0,4},{12,8},{1,5},{13,9},{2,6},{14,10},{3,7},{15,11},{16,20},{28,... | collective-permute-start | bytes 6291464 | tf_op jit(solution)/shard_map/ppermute | solution.py:230
  106.2 96.3 %collective-permute-start.9 = (bf16[2048,512]{1,0:T(8,128)(2,1)}, bf16[2048,512]{1,0:T(8,128)(2,1)S(1)}, u32[]{:S(2)}, u32[]{:S(2)}) collective-permute-start(bf16[2048,512]{1,0:T(8,128)(2,1)} %collective-permute-done.1.refs_1_), channel_id=1, source_target_pairs={{4,20},{8,24},{20,4},{24,8},{5,21},{9,25},{21,5},{25,9},{6,22},{10... | collective-permute-start | bytes 6291464 | tf_op jit(solution)/shard_map/ppermute | solution.py:231
  145.3 74.4 %collective-permute-start.10 = (bf16[2048,512]{1,0:T(8,128)(2,1)S(1)}, bf16[2048,512]{1,0:T(8,128)(2,1)S(1)}, u32[]{:S(2)}, u32[]{:S(2)}) collective-permute-start(bf16[2048,512]{1,0:T(8,128)(2,1)S(1)} %collective-permute-done.3.refs_2_), channel_id=1, source_target_pairs={{4,20},{8,24},{20,4},{24,8},{5,21},{9,25},{21,5},{25,9},{6,22},{10... | collective-permute-start | bytes 6291464 | tf_op jit(solution)/shard_map/ppermute | solution.py:231
  146.1 120.1 %copy-start.1 = (bf16[128,8192]{1,0:T(8,128)(2,1)}, bf16[128,8192]{1,0:T(8,128)(2,1)S(1)}, u32[]{:S(2)}) copy-start(bf16[128,8192]{1,0:T(8,128)(2,1)S(1)} %collective-permute-done.6.refs_2_) | copy-start | bytes 6291460
  146.1 60.5 %collective-permute-start.13 = (bf16[64,8192]{1,0:T(8,128)(2,1)}, bf16[64,8192]{1,0:T(8,128)(2,1)S(1)}, u32[]{:S(2)}, u32[]{:S(2)}) collective-permute-start(bf16[64,8192]{1,0:T(8,128)(2,1)} %get-tuple-element.36), channel_id=1, source_target_pairs={{4,8},{8,4},{5,9},{9,5},{6,10},{10,6},{7,11},{11,7},{20,24},{24,20... | collective-permute-start | bytes 3145736 | tf_op jit(solution)/shard_map/ppermute | solution.py:229
  146.8 119.4 %copy-start.3 = (bf16[128,8192]{1,0:T(8,128)(2,1)}, bf16[128,8192]{1,0:T(8,128)(2,1)S(1)}, u32[]{:S(2)}) copy-start(bf16[128,8192]{1,0:T(8,128)(2,1)S(1)} %collective-permute-done.15.refs_3_) | copy-start | bytes 6291460
  146.8 72.9 %collective-permute-start.7 = (bf16[1024,512]{1,0:T(8,128)(2,1)}, bf16[1024,512]{1,0:T(8,128)(2,1)S(1)}, u32[]{:S(2)}, u32[]{:S(2)}) collective-permute-start(bf16[1024,512]{1,0:T(8,128)(2,1)} %get-tuple-element.35), channel_id=1, source_target_pairs={{0,4},{12,8},{1,5},{13,9},{2,6},{14,10},{3,7},{15,11},{16,20},{28,... | collective-permute-start | bytes 3145736 | tf_op jit(solution)/shard_map/ppermute | solution.py:230
  195.9 47.8 %collective-permute-start.11 = (bf16[2048,512]{1,0:T(8,128)(2,1)S(1)}, bf16[2048,512]{1,0:T(8,128)(2,1)S(1)}, u32[]{:S(2)}, u32[]{:S(2)}) collective-permute-start(bf16[2048,512]{1,0:T(8,128)(2,1)S(1)} %collective-permute-done.5.refs_3_), channel_id=1, source_target_pairs={{4,20},{8,24},{20,4},{24,8},{5,21},{9,25},{21,5},{25,9},{6,22},{10... | collective-permute-start | bytes 6291464 | tf_op jit(solution)/shard_map/ppermute | solution.py:231
  202.6 77.8 %copy-start.13 = (bf16[2048,512]{1,0:T(8,128)(2,1)}, bf16[2048,512]{1,0:T(8,128)(2,1)S(1)}, u32[]{:S(2)}) copy-start(bf16[2048,512]{1,0:T(8,128)(2,1)S(1)} %collective-permute-done.9.refs_6_) | copy-start | bytes 6291460
  202.6 39.5 %collective-permute-start.16 = (bf16[64,8192]{1,0:T(8,128)(2,1)S(1)}, bf16[64,8192]{1,0:T(8,128)(2,1)S(1)}, u32[]{:S(2)}, u32[]{:S(2)}) collective-permute-start(bf16[64,8192]{1,0:T(8,128)(2,1)S(1)} %get-tuple-element.39), channel_id=1, source_target_pairs={{0,4},{12,8},{1,5},{13,9},{2,6},{14,10},{3,7},{15,11},{16,20},{28,... | collective-permute-start | bytes 3145736 | tf_op jit(solution)/shard_map/ppermute | solution.py:248
  206.6 73.8 %copy-start.5 = (bf16[64,8192]{1,0:T(8,128)(2,1)}, bf16[64,8192]{1,0:T(8,128)(2,1)S(1)}, u32[]{:S(2)}) copy-start(bf16[64,8192]{1,0:T(8,128)(2,1)S(1)} %collective-permute-done.13.refs_4_) | copy-start | bytes 3145732
  219.7 60.7 %copy-start.26 = (bf16[1024,512]{1,0:T(8,128)(2,1)}, bf16[1024,512]{1,0:T(8,128)(2,1)S(1)}, u32[]{:S(2)}) copy-start(bf16[1024,512]{1,0:T(8,128)(2,1)S(1)} %collective-permute-done.7.refs_4_) | copy-start | bytes 3145732
  219.7 60.7 %copy-start.15 = (bf16[2048,512]{1,0:T(8,128)(2,1)}, bf16[2048,512]{1,0:T(8,128)(2,1)S(1)}, u32[]{:S(2)}) copy-start(bf16[2048,512]{1,0:T(8,128)(2,1)S(1)} %collective-permute-done.10.refs_7_) | copy-start | bytes 6291460
  219.7 44.8 %collective-permute-start.14 = (bf16[64,8192]{1,0:T(8,128)(2,1)S(1)}, bf16[64,8192]{1,0:T(8,128)(2,1)}, u32[]{:S(2)}, u32[]{:S(2)}) collective-permute-start(bf16[64,8192]{1,0:T(8,128)(2,1)S(1)} %get-tuple-element.37), channel_id=1, source_target_pairs={{0,4},{12,8},{1,5},{13,9},{2,6},{14,10},{3,7},{15,11},{16,20},{28,... | collective-permute-start | bytes 3145736 | tf_op jit(solution)/shard_map/ppermute | solution.py:248
  225.0 56.5 %collective-permute-start.8 = (bf16[1024,512]{1,0:T(8,128)(2,1)}, bf16[1024,512]{1,0:T(8,128)(2,1)S(1)}, u32[]{:S(2)}, u32[]{:S(2)}) collective-permute-start(bf16[1024,512]{1,0:T(8,128)(2,1)} %collective-permute-done.refs_0_), channel_id=1, source_target_pairs={{4,20},{8,24},{20,4},{24,8},{5,21},{9,25},{21,5},{25,9},{6,22},{10... | collective-permute-start | bytes 3145736 | tf_op jit(solution)/shard_map/ppermute | solution.py:231
  225.7 56.7 %collective-permute-start.12 = (bf16[1024,512]{1,0:T(8,128)(2,1)S(1)}, bf16[1024,512]{1,0:T(8,128)(2,1)S(1)}, u32[]{:S(2)}, u32[]{:S(2)}) collective-permute-start(bf16[1024,512]{1,0:T(8,128)(2,1)S(1)} %collective-permute-done.7.refs_4_), channel_id=1, source_target_pairs={{4,20},{8,24},{20,4},{24,8},{5,21},{9,25},{21,5},{25,9},{6,22},{10... | collective-permute-start | bytes 3145736 | tf_op jit(solution)/shard_map/ppermute | solution.py:231
  242.1 38.3 %copy-start.24 = (bf16[64,8192]{1,0:T(8,128)(2,1)}, bf16[64,8192]{1,0:T(8,128)(2,1)S(1)}, u32[]{:S(2)}) copy-start(bf16[64,8192]{1,0:T(8,128)(2,1)S(1)} %collective-permute-done.16.refs_0_) | copy-start | bytes 3145732
  242.1 148.2 %collective-permute-start.20 = (bf16[64,8192]{1,0:T(8,128)(2,1)S(1)}, bf16[64,8192]{1,0:T(8,128)(2,1)}, u32[]{:S(2)}, u32[]{:S(2)}) collective-permute-start(bf16[64,8192]{1,0:T(8,128)(2,1)S(1)} %collective-permute-done.16.refs_0_), channel_id=1, source_target_pairs={{4,8},{8,4},{5,9},{9,5},{6,10},{10,6},{7,11},{11,7},{20,24},{24,20... | collective-permute-start | bytes 3145736 | tf_op jit(solution)/shard_map/ppermute | solution.py:249
  243.7 36.7 %copy-start.17 = (bf16[2048,512]{1,0:T(8,128)(2,1)}, bf16[2048,512]{1,0:T(8,128)(2,1)S(1)}, u32[]{:S(2)}) copy-start(bf16[2048,512]{1,0:T(8,128)(2,1)S(1)} %collective-permute-done.11.refs_8_) | copy-start | bytes 6291460
  243.7 170.1 %collective-permute-start.18 = (bf16[64,8192]{1,0:T(8,128)(2,1)}, bf16[64,8192]{1,0:T(8,128)(2,1)}, u32[]{:S(2)}, u32[]{:S(2)}) collective-permute-start(bf16[64,8192]{1,0:T(8,128)(2,1)} %get-tuple-element.42), channel_id=1, source_target_pairs={{0,4},{12,8},{1,5},{13,9},{2,6},{14,10},{3,7},{15,11},{16,20},{28,... | collective-permute-start | bytes 3145736 | tf_op jit(solution)/shard_map/ppermute | solution.py:248
  264.5 149.3 %collective-permute-start.21 = (bf16[64,8192]{1,0:T(8,128)(2,1)}, bf16[64,8192]{1,0:T(8,128)(2,1)}, u32[]{:S(2)}, u32[]{:S(2)}) collective-permute-start(bf16[64,8192]{1,0:T(8,128)(2,1)} %collective-permute-done.14.refs_2_), channel_id=1, source_target_pairs={{4,8},{8,4},{5,9},{9,5},{6,10},{10,6},{7,11},{11,7},{20,24},{24,20... | collective-permute-start | bytes 3145736 | tf_op jit(solution)/shard_map/ppermute | solution.py:249
  283.4 115.3 %slice-start = ((s8[8388608]{0:T(1024)(128)(4,1)}), s8[4194304]{0:T(1024)(128)(4,1)S(1)}, s32[]{:S(2)}) async-start(s8[8388608]{0:T(1024)(128)(4,1)} %bitcast.47), calls=%async_computation.6 | async-start | bytes 8388608
  293.8 105.0 %slice-start.1 = ((s8[8388608]{0:T(1024)(128)(4,1)}), s8[4194304]{0:T(1024)(128)(4,1)S(1)}, s32[]{:S(2)}) async-start(s8[8388608]{0:T(1024)(128)(4,1)} %bitcast.47), calls=%async_computation.7 | async-start | bytes 8388608
  390.3 44.8 %collective-permute-start.22 = (bf16[64,8192]{1,0:T(8,128)(2,1)}, bf16[64,8192]{1,0:T(8,128)(2,1)}, u32[]{:S(2)}, u32[]{:S(2)}) collective-permute-start(bf16[64,8192]{1,0:T(8,128)(2,1)} %get-tuple-element.44), channel_id=1, source_target_pairs={{0,4},{12,8},{1,5},{13,9},{2,6},{14,10},{3,7},{15,11},{16,20},{28,... | collective-permute-start | bytes 3145736 | tf_op jit(solution)/shard_map/ppermute | solution.py:248
  413.8 43.3 %collective-permute-start.23 = (bf16[64,8192]{1,0:T(8,128)(2,1)}, bf16[64,8192]{1,0:T(8,128)(2,1)}, u32[]{:S(2)}, u32[]{:S(2)}) collective-permute-start(bf16[64,8192]{1,0:T(8,128)(2,1)} %get-tuple-element.45), channel_id=1, source_target_pairs={{0,4},{12,8},{1,5},{13,9},{2,6},{14,10},{3,7},{15,11},{16,20},{28,... | collective-permute-start | bytes 3145736 | tf_op jit(solution)/shard_map/ppermute | solution.py:248
  416.1 320.1 %all-gather.17.cloned.1.call-start = ((), (), s32[]{:S(2)}) async-start(), calls=%async_computation.2 | async-start | bytes 2621440 | tf_op jit(solution)/shard_map/all_gather | solution.py:272
  435.1 40.1 %copy-start.20 = (bf16[512,1024]{1,0:T(8,128)(2,1)}, bf16[512,1024]{1,0:T(8,128)(2,1)S(1)}, u32[]{:S(2)}) copy-start(bf16[512,1024]{1,0:T(8,128)(2,1)S(1)} %shard_map.99) | copy-start | bytes 3145732
  475.2 11.2 %collective-permute-start.24 = (bf16[256,1024]{1,0:T(8,128)(2,1)S(1)}, bf16[256,1024]{1,0:T(8,128)(2,1)S(1)}, u32[]{:S(2)}, u32[]{:S(2)}) collective-permute-start(bf16[256,1024]{1,0:T(8,128)(2,1)S(1)} %get-tuple-element.47), channel_id=1, source_target_pairs={{4,0},{8,12},{5,1},{9,13},{6,2},{10,14},{7,3},{11,15},{20,16},{24,... | collective-permute-start | bytes 1572872 | tf_op jit(solution)/shard_map/ppermute | solution.py:269
  487.3 273.5 %all-gather.19.cloned.1.call-start = ((), (), s32[]{:S(2)}) async-start(), calls=%async_computation.3 | async-start | bytes 2621440 | tf_op jit(solution)/shard_map/all_gather | solution.py:272
  487.4 0.7 collective-permute-start.25
  488.1 35.0 %collective-permute-start.27 = (bf16[64,8192]{1,0:T(8,128)(2,1)S(1)}, bf16[64,8192]{1,0:T(8,128)(2,1)S(1)}, u32[]{:S(2)}, u32[]{:S(2)}) collective-permute-start(bf16[64,8192]{1,0:T(8,128)(2,1)S(1)} %copy-done.34), channel_id=1, source_target_pairs={{0,4},{12,8},{1,5},{13,9},{2,6},{14,10},{3,7},{15,11},{16,20},{28,... | collective-permute-start | bytes 3145736 | tf_op jit(solution)/shard_map/ppermute | solution.py:248
  510.9 12.2 %collective-permute-start.26 = (bf16[64,8192]{1,0:T(8,128)(2,1)}, bf16[64,8192]{1,0:T(8,128)(2,1)S(1)}, u32[]{:S(2)}, u32[]{:S(2)}) collective-permute-start(bf16[64,8192]{1,0:T(8,128)(2,1)} %collective-permute-done.22.refs_2_), channel_id=1, source_target_pairs={{4,8},{8,4},{5,9},{9,5},{6,10},{10,6},{7,11},{11,7},{20,24},{24,20... | collective-permute-start | bytes 3145736 | tf_op jit(solution)/shard_map/ppermute | solution.py:249
  541.0 36.7 %copy-start.8 = (bf16[512,1024]{1,0:T(8,128)(2,1)S(1)}, bf16[512,1024]{1,0:T(8,128)(2,1)}, u32[]{:S(2)}) copy-start(bf16[512,1024]{1,0:T(8,128)(2,1)} %copy-done.7) | copy-start | bytes 3145732
  541.0 19.0 %collective-permute-start.28 = (bf16[256,1024]{1,0:T(8,128)(2,1)S(1)}, bf16[256,1024]{1,0:T(8,128)(2,1)S(1)}, u32[]{:S(2)}, u32[]{:S(2)}) collective-permute-start(bf16[256,1024]{1,0:T(8,128)(2,1)S(1)} %get-tuple-element.51), channel_id=1, source_target_pairs={{4,0},{8,12},{5,1},{9,13},{6,2},{10,14},{7,3},{11,15},{20,16},{24,... | collective-permute-start | bytes 1572872 | tf_op jit(solution)/shard_map/ppermute | solution.py:269
  560.9 202.0 %all-gather.13.cloned.1.call-start = ((), (), s32[]{:S(2)}) async-start(), calls=%async_computation | async-start | bytes 5242880 | tf_op jit(solution)/shard_map/all_gather | solution.py:272
  561.0 16.7 %collective-permute-start.17 = (bf16[512,1024]{1,0:T(8,128)(2,1)S(1)}, bf16[512,1024]{1,0:T(8,128)(2,1)S(1)}, u32[]{:S(2)}, u32[]{:S(2)}) collective-permute-start(bf16[512,1024]{1,0:T(8,128)(2,1)S(1)} %copy-done.23), channel_id=1, source_target_pairs={{4,0},{8,12},{5,1},{9,13},{6,2},{10,14},{7,3},{11,15},{20,16},{24,... | collective-permute-start | bytes 3145736 | tf_op jit(solution)/shard_map/ppermute | solution.py:269
  578.9 188.5 %all-gather.21.cloned.1.call-start = ((), (), s32[]{:S(2)}) async-start(), calls=%async_computation.4 | async-start | bytes 2621440 | tf_op jit(solution)/shard_map/all_gather | solution.py:272
  578.9 4.6 collective-permute-start.29
  579.6 26.2 %collective-permute-start.31 = (bf16[64,8192]{1,0:T(8,128)(2,1)}, bf16[64,8192]{1,0:T(8,128)(2,1)}, u32[]{:S(2)}, u32[]{:S(2)}) collective-permute-start(bf16[64,8192]{1,0:T(8,128)(2,1)} %get-tuple-element.53), channel_id=1, source_target_pairs={{0,4},{12,8},{1,5},{13,9},{2,6},{14,10},{3,7},{15,11},{16,20},{28,... | collective-permute-start | bytes 3145736 | tf_op jit(solution)/shard_map/ppermute | solution.py:248
  583.5 34.0 %collective-permute-start.32 = (bf16[64,8192]{1,0:T(8,128)(2,1)S(1)}, bf16[64,8192]{1,0:T(8,128)(2,1)}, u32[]{:S(2)}, u32[]{:S(2)}) collective-permute-start(bf16[64,8192]{1,0:T(8,128)(2,1)S(1)} %copy-done.33), channel_id=1, source_target_pairs={{0,4},{12,8},{1,5},{13,9},{2,6},{14,10},{3,7},{15,11},{16,20},{28,... | collective-permute-start | bytes 3145736 | tf_op jit(solution)/shard_map/ppermute | solution.py:248
  605.2 12.4 %collective-permute-start.30 = (bf16[64,8192]{1,0:T(8,128)(2,1)S(1)}, bf16[64,8192]{1,0:T(8,128)(2,1)S(1)}, u32[]{:S(2)}, u32[]{:S(2)}) collective-permute-start(bf16[64,8192]{1,0:T(8,128)(2,1)S(1)} %collective-permute-done.27.refs_2_), channel_id=1, source_target_pairs={{4,8},{8,4},{5,9},{9,5},{6,10},{10,6},{7,11},{11,7},{20,24},{24,20... | collective-permute-start | bytes 3145736 | tf_op jit(solution)/shard_map/ppermute | solution.py:249
  635.2 16.9 %collective-permute-start.33 = (bf16[256,1024]{1,0:T(8,128)(2,1)S(1)}, bf16[256,1024]{1,0:T(8,128)(2,1)S(1)}, u32[]{:S(2)}, u32[]{:S(2)}) collective-permute-start(bf16[256,1024]{1,0:T(8,128)(2,1)S(1)} %get-tuple-element.56), channel_id=1, source_target_pairs={{4,0},{8,12},{5,1},{9,13},{6,2},{10,14},{7,3},{11,15},{20,16},{24,... | collective-permute-start | bytes 1572872 | tf_op jit(solution)/shard_map/ppermute | solution.py:269
  653.0 116.4 %all-gather.15.cloned.1.call-start = ((), (), s32[]{:S(2)}) async-start(), calls=%async_computation.1 | async-start | bytes 5242880 | tf_op jit(solution)/shard_map/all_gather | solution.py:272
  653.1 16.7 %collective-permute-start.19 = (bf16[512,1024]{1,0:T(8,128)(2,1)S(1)}, bf16[512,1024]{1,0:T(8,128)(2,1)S(1)}, u32[]{:S(2)}, u32[]{:S(2)}) collective-permute-start(bf16[512,1024]{1,0:T(8,128)(2,1)S(1)} %copy-done.21), channel_id=1, source_target_pairs={{4,0},{8,12},{5,1},{9,13},{6,2},{10,14},{7,3},{11,15},{20,16},{24,... | collective-permute-start | bytes 3145736 | tf_op jit(solution)/shard_map/ppermute | solution.py:269
  670.9 3.5 collective-permute-start.34
  671.6 2.7 collective-permute-start.35
  692.8 41.4 %collective-permute-start.36 = (bf16[256,1024]{1,0:T(8,128)(2,1)S(1)}, bf16[256,1024]{1,0:T(8,128)(2,1)S(1)}, u32[]{:S(2)}, u32[]{:S(2)}) collective-permute-start(bf16[256,1024]{1,0:T(8,128)(2,1)S(1)} %get-tuple-element.58), channel_id=1, source_target_pairs={{4,0},{8,12},{5,1},{9,13},{6,2},{10,14},{7,3},{11,15},{20,16},{24,... | collective-permute-start | bytes 1572872 | tf_op jit(solution)/shard_map/ppermute | solution.py:269
  734.2 14.2 %collective-permute-start.39 = (bf16[256,1024]{1,0:T(8,128)(2,1)S(1)}, bf16[256,1024]{1,0:T(8,128)(2,1)S(1)}, u32[]{:S(2)}, u32[]{:S(2)}) collective-permute-start(bf16[256,1024]{1,0:T(8,128)(2,1)S(1)} %broadcast_select_fusion.2), channel_id=1, source_target_pairs={{0,3},{1,2},{2,1},{3,0},{4,7},{5,6},{6,5},{7,4},{8,11},{9,10},{10,... | collective-permute-start | bytes 1572872 | tf_op jit(solution)/shard_map/ppermute | solution.py:279
  734.3 24.2 %collective-permute-start.38 = (bf16[256,1024]{1,0:T(8,128)(2,1)S(1)}, bf16[256,1024]{1,0:T(8,128)(2,1)S(1)}, u32[]{:S(2)}, u32[]{:S(2)}) collective-permute-start(bf16[256,1024]{1,0:T(8,128)(2,1)S(1)} %broadcast_select_fusion.2), channel_id=1, source_target_pairs={{0,2},{1,3},{2,0},{3,1},{4,6},{5,7},{6,4},{7,5},{8,10},{9,11},{10,... | collective-permute-start | bytes 1572872 | tf_op jit(solution)/shard_map/ppermute | solution.py:279
  735.2 24.1 %collective-permute-start.37 = (bf16[256,1024]{1,0:T(8,128)(2,1)S(1)}, bf16[256,1024]{1,0:T(8,128)(2,1)}, u32[]{:S(2)}, u32[]{:S(2)}) collective-permute-start(bf16[256,1024]{1,0:T(8,128)(2,1)S(1)} %broadcast_select_fusion.2), channel_id=1, source_target_pairs={{0,1},{1,0},{2,3},{3,2},{4,5},{5,4},{6,7},{7,6},{8,9},{9,8},{10,11... | collective-permute-start | bytes 1572872 | tf_op jit(solution)/shard_map/ppermute | solution.py:279
  781.6 3.0 collective-permute-start.42
  783.0 3.6 collective-permute-start.41
  783.6 2.9 collective-permute-start.40
  786.6 5.4 collective-permute-start.45
  787.8 4.5 collective-permute-start.44
  787.8 4.7 collective-permute-start.43
  (29 other events, 208.9 us)
Sparse Core Ops, SparseCore 0:
  416.2 38.9 all-gather.22
  487.4 21.6 all-gather.16
  561.1 21.3 all-gather.18
  583.9 34.4 all-gather.12
  653.1 21.9 all-gather.20
  677.2 34.4 all-gather.14

commit v4 on v2

--- a/solution.py
+++ b/solution.py
@@ -103,59 +103,68 @@
     return lax.optimization_barrier((value, *earlier))[0]
 
 
-def project_kernel(count, *refs):
-    tokens = refs[:count]
-    own_ref, near_ref, far_ref, out_own, out_end, acc_own, acc_end = refs[count:]
+def project_kernel(count, widths, *refs):
+    flags, refs = refs[0], refs[1:]
+    tokens, basis, out, acc = refs[:count], refs[count:-2], refs[-2], refs[-1]
     step = pl.program_id(0)
+    rows = tokens[0][...]
+    if count == 2:
+        rows = jnp.where(flags[0] == 1, rows, tokens[1][...])
+    start, spans = 0, []
+    for width in widths:
+        spans.append((start, start + width))
+        start += width
 
     @pl.when(step == 0)
     def _():
-        acc_own[...] = jnp.zeros_like(acc_own)
-        acc_end[...] = jnp.zeros_like(acc_end)
-
-    rows = jnp.concatenate([t[...] for t in tokens], axis=0)
-    half = near_ref.shape[1]
-    acc_own[...] += jnp.dot(rows, own_ref[...], preferred_element_type=F32)
-    acc_end[:, :half] += jnp.dot(rows, near_ref[...], preferred_element_type=F32)
-    acc_end[:, half:] += jnp.dot(rows, far_ref[...], preferred_element_type=F32)
+        acc[...] = jnp.zeros_like(acc)
+
+    for ref, (a, b) in zip(basis, spans):
+        acc[:, a:b] += jnp.dot(rows, ref[...], preferred_element_type=F32)
 
     @pl.when(step == pl.num_programs(0) - 1)
     def _():
-        out_own[...] = acc_own[...].astype(BF16)
-        out_end[...] = acc_end[...].astype(BF16)
-
-
-def project(tokens, own, near, far):
-    feats, dirs = own.shape
-    block = 1024
-    specs, total = [], 0
-    for array, index in tokens:
-        n = array.shape[-2]
-        total += n
-        if index is None:
-            specs.append(pl.BlockSpec((n, block), lambda k: (0, k)))
+        if len(basis) == 1:
+            out[...] = acc[...].astype(BF16)
         else:
-            specs.append(pl.BlockSpec((None, n, block), lambda k, index=index: (index, 0, k)))
-    half = near.shape[1]
+            (c, d), (e, f) = spans[-2:]
+            if c > 0:
+                out[:, :c] = acc[:, :c].astype(BF16)
+
+            @pl.when(flags[1] == 0)
+            def _():
+                out[:, c:f] = acc[:, c:f].astype(BF16)
+
+            @pl.when(flags[1] != 0)
+            def _():
+                out[:, c:d] = acc[:, e:f].astype(BF16)
+                out[:, e:f] = acc[:, c:d].astype(BF16)
+
+
+def project(flags, tokens, bases):
+    feats = bases[0].shape[0]
+    widths = tuple(x.shape[1] for x in bases)
+    block, total = 1024, sum(widths)
+    rows = tokens[0][2]
+    specs = [
+        pl.BlockSpec((rows, block), lambda k, i=start // rows: (i, k)) for _, start, _ in tokens
+    ]
     return pl.pallas_call(
-        functools.partial(project_kernel, len(tokens)),
+        functools.partial(project_kernel, len(tokens), widths),
         grid=(feats // block,),
-        in_specs=specs
-        + [
-            pl.BlockSpec((block, dirs), lambda k: (k, 0)),
-            pl.BlockSpec((block, half), lambda k: (k, 0)),
-            pl.BlockSpec((block, half), lambda k: (k, 0)),
-        ],
-        out_specs=[pl.BlockSpec((total, dirs), lambda k: (0, 0))] * 2,
-        out_shape=[jax.ShapeDtypeStruct((total, dirs), BF16)] * 2,
-        scratch_shapes=[pltpu.VMEM((total, dirs), F32)] * 2,
+        in_specs=[pl.BlockSpec(memory_space=pltpu.SMEM)]
+        + specs
+        + [pl.BlockSpec((block, w), lambda k: (k, 0)) for w in widths],
+        out_specs=pl.BlockSpec((rows, total), lambda k: (0, 0)),
+        out_shape=jax.ShapeDtypeStruct((rows, total), BF16),
+        scratch_shapes=[pltpu.VMEM((rows, total), F32)],
         compiler_params=pltpu.CompilerParams(vmem_limit_bytes=40 * 2**20),
         cost_estimate=pl.CostEstimate(
-            flops=4 * total * feats * dirs,
-            bytes_accessed=4 * feats * dirs + 2 * total * feats,
+            flops=rows * feats * total // 8,
+            bytes_accessed=feats * (total + rows) // 8,
             transcendentals=0,
         ),
-    )(*[array for array, _ in tokens], own, near, far)
+    )(flags, *[array for array, _, _ in tokens], *bases)
 
 
 def after(value, *earlier):
@@ -172,77 +181,87 @@
 def chain_body(acts, grads, act_basis, grad_basis, eigenvalues, query_rotated, example_ids, token_counts):
     cands, tok, feats = grads.shape
     dirs = grad_basis.shape[1]
-    group, row = lax.axis_index("groups"), lax.axis_index("row")
+    group, row, col = (lax.axis_index(a) for a in ("groups", "row", "col"))
     sides, planes, parts = 2, 4, 4
-    inward = [(0, 1), (3, 2)]
-    across = [(1, 2), (2, 1)]
-    outward = [(1, 0), (2, 3)]
-    swap = [(g * planes + r, (1 - g) * planes + r) for g in range(sides) for r in (1, 2)]
+    middle, ends = [(1, 2), (2, 1)], [(0, 3), (3, 0)]
+    beside = [(i, i ^ 1) for i in range(planes)]
     at_end = (row == 0) | (row == planes - 1)
+    flags = jnp.stack([at_end.astype(jnp.int32), group.astype(jnp.int32)])
 
     lengths = candidate_lengths(example_ids, token_counts)
     local_act = local_activations(acts, act_basis, lengths)
     every_act = lax.all_gather(local_act, "row", axis=0)
 
-    half = dirs // sides
-    pieces = 8
-    deep = feats // pieces
-    half_cands = cands // 2
-    other, near, far = [], [], []
-    spans = [(0, 1), (1, 3), (3, 5), (5, 7), (7, 8)]
-    for i, (a, b) in enumerate(spans):
+    half, flat = dirs // sides, grads.reshape(cands * tok, feats)
+    units, deep = 8, feats // 8
+    near, far, other = [], [], []
+    own_own = project(flags, [(flat, 0, cands * tok)], [grad_basis])
+    for i, (a, b) in enumerate([(0, 1), (1, 3), (3, 5), (5, 7), (7, units)]):
         piece = lax.dynamic_slice(grad_basis, (a * deep, group * half), ((b - a) * deep, half))
         if i >= 2:
-            piece = after(piece, near[i - 2], *other)
-        near.append(lax.ppermute(piece, "row", inward))
-        far.append(lax.ppermute(near[i], ("groups", "row"), swap))
+            piece = after(piece, near[i - 2], *([own_own, local_act] if i == 2 else []))
         if i in (0, 2):
-            part = grads[:half_cands] if i == 0 else grads[half_cands:]
-            other.append(lax.ppermute(part if i == 0 else after(part, near[0]), "row", across))
-
-    chunk = tok // 2
-    started = list(near)
-    first, second = [], []
-    for c in range(cands):
-        for s in range(0, tok, chunk):
-            piece = after(grads[c, s : s + chunk], started[-2], *other)
-            first.append(lax.ppermute(piece, "row", inward))
-            started.append(first[-1])
-            second.append(lax.ppermute(first[-1], "row", across))
-
+            part = flat[: cands * tok // 2] if i == 0 else after(flat[cands * tok // 2 :], near[0])
+            other.append(lax.ppermute(part, "row", middle))
+        near.append(lax.ppermute(piece, "row", beside))
+        far.append(lax.ppermute(near[i], "groups", [(0, 1), (1, 0)]))
     near_basis = jnp.concatenate(near, axis=0)
     far_basis = jnp.concatenate(far, axis=0)
 
-    def reduce(tokens):
-        own, end = project(tokens, grad_basis, near_basis, far_basis)
-        back = lax.ppermute(end, "row", outward)
-        swapped = jnp.concatenate([back[:, half:], back[:, :half]], axis=1)
-        mine = jnp.where(at_end, jnp.where(group == 0, back, swapped), own)
-        total = mine.astype(F32)
+    spans = [(c * tok, tok) for c in range(cands - 1)]
+    spans += [((cands - 1) * tok + s, tok // 2) for s in (0, tok // 2)]
+    ties = {0: [near[3], far[1], other[0]], 1: [near[4], far[2], other[1]], 2: [far[4]]}
+    partner, products = [], []
+    for k, (start, n) in enumerate(spans):
+        tie = ties.get(k, []) + ([partner[k - 2]] if k >= 2 else [])
+        partner.append(lax.ppermute(after(flat[start : start + n], *tie), "row", ends))
+        if k == 0:
+            own_end = project(flags, [(flat, 0, cands * tok)], [near_basis, after(far_basis, partner[0])])
+            ties[3] = [own_end]
+        inner = other[2 * start // (cands * tok)]
+        products.append(
+            project(
+                flags,
+                [(partner[k], 0, n), (inner, start % (cands * tok // 2), n)],
+                [grad_basis, near_basis, far_basis],
+            )
+        )
+        ties[k + 3] = ties.get(k + 3, []) + [products[k]]
+
+    def scatter_sum(value):
+        value = value.reshape(parts, -1, 2 * dirs)
+        total = lax.dynamic_index_in_dim(value, col, 0, keepdims=False).astype(F32)
         for d in range(1, parts):
-            total = total + lax.ppermute(mine, "col", [(i, i ^ d) for i in range(parts)]).astype(F32)
-        return total.astype(BF16)
-
-    pieces_of = []
+            sent = lax.dynamic_index_in_dim(value, col ^ d, 0, keepdims=False)
+            total = total + lax.ppermute(sent, "col", [(i, i ^ d) for i in range(parts)]).astype(F32)
+        total = total.astype(BF16)
+        return jnp.stack([total[:, :dirs], lax.ppermute(total[:, dirs:], "row", beside)])
+
+    act = [
+        lax.dynamic_index_in_dim(every_act, i, 0, keepdims=False)
+        for i in (row, row ^ 1, planes - 1 - row, planes - 1 - (row ^ 1))
+    ]
+    pieces, act_order = [[] for _ in range(cands)], [[] for _ in range(cands)]
+    own = lax.all_gather(scatter_sum(jnp.concatenate([own_own, own_end], axis=1)), "col", axis=0)
     for c in range(cands):
-        inner = reduce([(grads, c), (other[c // half_cands], c % half_cands)])
-        pieces_of.append([inner])
-    for c in range(cands):
-        if c < cands - 1:
-            k = 2 * c
-            pieces_of[c].append(
-                reduce([(first[k], None), (second[k], None), (first[k + 1], None), (second[k + 1], None)])
-            )
+        pieces[c].append(own[c].reshape(2 * tok, dirs))
+        act_order[c] += [act[0][c], act[1][c]]
+    for k, (start, n) in enumerate(spans):
+        c, s = start // tok, start % tok
+        mine = scatter_sum(products[k])
+        tokens = jnp.stack([x[c, s : s + n].reshape(parts, n // parts, -1) for x in act[2:]], axis=1)
+        if k < len(spans) - 1:
+            every = lax.all_gather(mine, "col", axis=0)
+            pieces[c].append(every.reshape(2 * n, dirs))
+            act_order[c].append(tokens.reshape(2 * n, -1))
         else:
-            for k in (2 * c, 2 * c + 1):
-                pieces_of[c].append(reduce([(first[k], None), (second[k], None)]))
-
-    blocks = jnp.where(row < 2, every_act, every_act[::-1])
-    order = [blocks[1], blocks[2]]
-    for s in range(0, tok, chunk):
-        order += [blocks[0][:, s : s + chunk], blocks[3][:, s : s + chunk]]
-    act_rot = jnp.concatenate(order, axis=1)
-    rotated, scores = rotate_and_score(pieces_of, act_rot, eigenvalues, query_rotated)
+            for d in range(parts):
+                got = lax.ppermute(mine, "col", [(i, i ^ d) for i in range(parts)]) if d else mine
+                pieces[c].append(got.reshape(2 * n // parts, dirs))
+                sub = lax.dynamic_index_in_dim(tokens, col ^ d, 0, keepdims=False)
+                act_order[c].append(sub.reshape(2 * n // parts, -1))
+    act_rot = jnp.stack([jnp.concatenate(x, axis=0) for x in act_order])
+    rotated, scores = rotate_and_score(pieces, act_rot, eigenvalues, query_rotated)
     scores = exchange_sum(exchange_sum(scores, "col", parts), "row", planes)
     return rotated, scores
 

time: 793 us -> 535 us (0.67)
  starting transfers between devices: 287 us -> 141 us
  waiting for transfers between devices: 284 us -> 180 us
  Pallas kernels: 141 us -> 101 us
  blocking collectives: 0 us -> 39.4 us
  other arithmetic: 12 us -> 3.02 us
    ppermute x64 -> x44, starting transfers between devices: 280 us -> 134 us  [the longest x5 95.5 us: chain_body(): lax.ppermute(after(flat[start:start + n], *tie), 'row', ends)]
    ppermute x64 -> x44, waiting for transfers between devices: 278 us -> 175 us  [the longest x5 125 us: chain_body(): near.append(lax.ppermute(piece, 'row', beside))]
    pallas_call x9 -> x7, Pallas kernels: 136 us -> 95.9 us  [project(): pl.pallas_call(functools.partial(project_kernel, len(tokens), widths), gr...]
    all_gather x0 -> x4, blocking collectives: none -> 39.4 us  [chain_body(): every = lax.all_gather(mine, 'col', axis=0)]
    unnamed x49 -> x44, local copies, waits for them, and re-layouts: 20.9 us -> 22.4 us
  transfers between devices with their start and end apart: 71 -> 52, of which waited for: 25 -> 16; matrix products, arithmetic and copies ran while one was open for 8% -> 8% of each run, Pallas kernels for 17% -> 18%
where the time goes in v4:
time: 535 us
  waiting for transfers between devices  180 us (34%)
  starting transfers between devices  141 us (26%)
  Pallas kernels  101 us (19%)
  local copies, waits for them, and re-layouts  47 us (9%)
  blocking collectives  39.4 us (7%)
  between operations  16.3 us (3%)
  matrix products  7.61 us (1%)
    ppermute x5, waiting for transfers between devices, chain_body(): near.append(lax.ppermute(piece, 'row', beside))  125 us
    pallas_call x7, Pallas kernels, project(): pl.pallas_call(functools.partial(project_kernel, len(tokens), widths), gr...  95.9 us
    ppermute x5, starting transfers between devices, chain_body(): lax.ppermute(after(flat[start:start + n], *tie), 'row', ends)  95.5 us
    ppermute x6, waiting for transfers between devices, scatter_sum(): lax.ppermute(total[:, dirs:], 'row', beside)  44.7 us
    all_gather x4, blocking collectives, chain_body(): every = lax.all_gather(mine, 'col', axis=0)  39.4 us
    unnamed x44, local copies, waits for them, and re-layouts  22.4 us
    ppermute x18, starting transfers between devices, scatter_sum(): lax.ppermute(sent, 'col', [(i, i ^ d) for i in range(parts)]).astype(F32)  11.9 us
  transfers between devices with their start and end apart: 52, of which 16 were waited for; matrix products, arithmetic and copies ran while one was open for 8% of the time, Pallas kernels for 18%

profile of v4, /device:TPU:0, one launch (start us, length us, event | category | flops | bytes accessed | tf_op | source)
XLA Modules:
  0.0 534.6 jit_solution(15659889192850989083)
XLA Ops:
  8.1 3.3 constant_dynamic-slice_fusion.7
  11.3 3.0 collective-permute-start
  14.3 5.3 constant_dynamic-slice_fusion.8
  19.8 3.9 fusion.33
  23.7 2.7 collective-permute-start.10
  26.6 7.6 %fusion.5 = bf16[4,128,256]{2,1,0:T(8,128)(2,1)} fusion(bf16[4,128,8192]{2,1,0:T(8,128)(2,1)} %param.8, bf16[8192,256]{1,0:T(8,128)(2,1)} %param.10, f32[4,128]{1,0:T(4,128)S(1)} %compare_convert_fusion), kind=kOutput, calls=%fused_computation.7 | convolution fusion | flops 2147745792 | bytes 12847104 | tf_op jit(solution)/shard_map/ctd,dk->ctk/dot_general | solution.py:25
  34.3 5.8 %slice_bitcast_fusion = (bf16[128,8192]{1,0:T(8,128)(2,1)}, bf16[128,8192]{1,0:T(8,128)(2,1)}, bf16[128,8192]{1,0:T(8,128)(2,1)}) fusion(bf16[4,128,8192]{2,1,0:T(8,128)(2,1)} %param.9), kind=kLoop, calls=%fused_computation.3 | loop fusion | bytes 12582912 | tf_op jit(solution)/shard_map/slice | solution.py:217
  40.2 3.5 copy-done.2
  43.7 13.8 %shard_map.95 = bf16[512,1024]{1,0:T(8,128)(2,1)S(1)} custom-call(s32[2]{0:T(128)S(1)} %pad_add_fusion.refs_0_, bf16[512,8192]{1,0:T(8,128)(2,1)S(1)} %bitcast.163, bf16[8192,1024]{1,0:T(8,128)(2,1)} %refs_3_.9), custom_call_target="tpu_custom_call" | custom-call | flops 536870912 | bytes 1572864 | tf_op jit(solution)/shard_map/pallas_call | solution.py:152
  57.5 3.1 collective-permute-start.2
  60.6 2.7 collective-permute-start.20
  63.2 37.2 %collective-permute-done.1 = bf16[2048,512]{1,0:T(8,128)(2,1)} collective-permute-done((bf16[2048,512]{1,0:T(8,128)(2,1)}, bf16[2048,512]{1,0:T(8,128)(2,1)}, u32[]{:S(2)}, u32[]{:S(2)}) %collective-permute-start.1) | collective-permute-done | bytes 2097184 | tf_op jit(solution)/shard_map/ppermute | solution.py:206
  100.4 2.1 collective-permute-start.3
  102.5 1.5 collective-permute-start.6
  104.0 1.5 fusion.32
  105.5 2.3 constant_dynamic-update-slice_fusion.4
  112.4 33.0 %collective-permute-done.2 = bf16[2048,512]{1,0:T(8,128)(2,1)} collective-permute-done((bf16[2048,512]{1,0:T(8,128)(2,1)}, bf16[2048,512]{1,0:T(8,128)(2,1)}, u32[]{:S(2)}, u32[]{:S(2)}) %collective-permute-start.2) | collective-permute-done | bytes 2097184 | tf_op jit(solution)/shard_map/ppermute | solution.py:206
  145.4 2.0 collective-permute-start.5
  147.5 1.5 collective-permute-done.6
  149.0 1.7 collective-permute-start.7
  150.7 38.8 %collective-permute-done.3 = bf16[2048,512]{1,0:T(8,128)(2,1)} collective-permute-done((bf16[2048,512]{1,0:T(8,128)(2,1)S(1)}, bf16[2048,512]{1,0:T(8,128)(2,1)}, u32[]{:S(2)}, u32[]{:S(2)}) %collective-permute-start.3) | collective-permute-done | bytes 2097184 | tf_op jit(solution)/shard_map/ppermute | solution.py:206
  189.5 1.7 collective-permute-start.8
  191.2 1.6 collective-permute-start.4
  192.8 4.4 collective-permute-start.11
  197.3 1.7 constant_dynamic-update-slice_fusion.3
  199.1 1.7 constant_dynamic-update-slice_fusion.2
  200.8 15.9 %collective-permute-done.4 = bf16[1024,512]{1,0:T(8,128)(2,1)S(1)} collective-permute-done((bf16[1024,512]{1,0:T(8,128)(2,1)}, bf16[1024,512]{1,0:T(8,128)(2,1)S(1)}, u32[]{:S(2)}, u32[]{:S(2)}) %collective-permute-start.4) | collective-permute-done | bytes 1048608 | tf_op jit(solution)/shard_map/ppermute | solution.py:206
  217.2 1.7 constant_dynamic-update-slice_fusion.1
  219.0 3.5 constant_dynamic-update-slice_fusion.8
  224.0 71.6 %collective-permute-start.21 = (bf16[128,8192]{1,0:T(8,128)(2,1)S(1)}, bf16[128,8192]{1,0:T(8,128)(2,1)S(1)}, u32[]{:S(2)}, u32[]{:S(2)}) collective-permute-start(bf16[128,8192]{1,0:T(8,128)(2,1)S(1)} %copy-done.6), channel_id=1, source_target_pairs={{0,12},{12,0},{1,13},{13,1},{2,14},{14,2},{3,15},{15,3},{16,28},{2... | collective-permute-start | bytes 6291464 | tf_op jit(solution)/shard_map/ppermute | solution.py:217
  296.1 3.3 copy-done.5
  299.4 13.5 %shard_map.96 = bf16[512,1024]{1,0:T(8,128)(2,1)S(1)} custom-call(s32[2]{0:T(128)S(1)} %pad_add_fusion.refs_0_, bf16[512,8192]{1,0:T(8,128)(2,1)S(1)} %bitcast.167, bf16[8192,512]{1,0:T(8,128)(2,1)} %copy-done.1, bf16[8192,512]{1,0:T(8,128)(2,1)} %copy-done.5), custom_call_target="tpu_custom_call" | custom-call | flops 536870912 | bytes 1572864 | tf_op jit(solution)/shard_map/pallas_call | solution.py:152
  312.9 14.2 %shard_map.97 = bf16[128,2048]{1,0:T(8,128)(2,1)S(1)} custom-call(s32[2]{0:T(128)S(1)} %pad_add_fusion.refs_0_, bf16[128,8192]{1,0:T(8,128)(2,1)S(1)} %collective-permute-done.11.refs_1_, bf16[256,8192]{1,0:T(8,128)(2,1)} %collective-permute-done.10.refs_2_, bf16[8192,1024]{1,0:T(8,128)(2,1)} %refs_3_.9, bf16[8192,512]{1,0:T(8,128)(2,1)} %copy-done.1, ...), custom_call_target="tpu_custom_call" | custom-call | flops 268435456 | bytes 2228224 | tf_op jit(solution)/shard_map/pallas_call | solution.py:152
  327.3 1.6 collective-permute-start.17
  329.9 1.5 collective-permute-start.13
  331.4 2.2 collective-permute-done.17
  333.9 1.6 collective-permute-done.18
  335.9 4.6 collective-permute-done.19
  340.4 6.9 %collective-permute-start.26 = (bf16[128,8192]{1,0:T(8,128)(2,1)}, bf16[128,8192]{1,0:T(8,128)(2,1)}, u32[]{:S(2)}, u32[]{:S(2)}) collective-permute-start(bf16[128,8192]{1,0:T(8,128)(2,1)} %get-tuple-element.21), channel_id=1, source_target_pairs={{0,12},{12,0},{1,13},{13,1},{2,14},{14,2},{3,15},{15,3},{16,28},{2... | collective-permute-start | bytes 6291464 | tf_op jit(solution)/shard_map/ppermute | solution.py:217
  347.3 14.8 %all-gather.1 = bf16[8,32,1024]{2,1,0:T(8,128)(2,1)S(1)} all-gather(bf16[2,32,1024]{2,1,0:T(8,128)(2,1)S(1)} %pad_maximum_fusion.3), channel_id=3, replica_groups=mesh['groups'=2,'row'=4,'col'=4] {'col'}, dimensions={0}, use_global_device_ids=true | all-gather | bytes 655360 | tf_op jit(solution)/shard_map/all_gather | solution.py:254
  362.5 14.2 %shard_map.98 = bf16[128,2048]{1,0:T(8,128)(2,1)S(1)} custom-call(s32[2]{0:T(128)S(1)} %pad_add_fusion.refs_0_, bf16[128,8192]{1,0:T(8,128)(2,1)S(1)} %collective-permute-done.21.refs_1_, bf16[256,8192]{1,0:T(8,128)(2,1)} %collective-permute-done.10.refs_2_, bf16[8192,1024]{1,0:T(8,128)(2,1)} %refs_3_.9, bf16[8192,512]{1,0:T(8,128)(2,1)} %copy-done.1, ...), custom_call_target="tpu_custom_call" | custom-call | flops 268435456 | bytes 2228224 | tf_op jit(solution)/shard_map/pallas_call | solution.py:152
  377.2 1.5 collective-permute-start.23
  378.9 6.9 %collective-permute-start.31 = (bf16[64,8192]{1,0:T(8,128)(2,1)}, bf16[64,8192]{1,0:T(8,128)(2,1)S(1)}, u32[]{:S(2)}, u32[]{:S(2)}) collective-permute-start(bf16[64,8192]{1,0:T(8,128)(2,1)} %get-tuple-element.22), channel_id=1, source_target_pairs={{0,12},{12,0},{1,13},{13,1},{2,14},{14,2},{3,15},{15,3},{16,28},{2... | collective-permute-start | bytes 3145736 | tf_op jit(solution)/shard_map/ppermute | solution.py:217
  385.9 13.7 %collective-permute-done.15 = bf16[128,1024]{1,0:T(8,128)(2,1)S(1)} collective-permute-done((bf16[128,1024]{1,0:T(8,128)(2,1)S(1)}, bf16[128,1024]{1,0:T(8,128)(2,1)S(1)}, u32[]{:S(2)}, u32[]{:S(2)}) %collective-permute-start.15) | collective-permute-done | bytes 262176 | tf_op jit(solution)/shard_map/ppermute | solution.py:238
  400.5 22.2 %collective-permute-done.25 = bf16[32,1024]{1,0:T(8,128)(2,1)S(1)} collective-permute-done((bf16[32,1024]{1,0:T(8,128)(2,1)S(1)}, bf16[32,1024]{1,0:T(8,128)(2,1)S(1)}, u32[]{:S(2)}, u32[]{:S(2)}) %collective-permute-start.25) | collective-permute-done | bytes 65568 | tf_op jit(solution)/shard_map/ppermute | solution.py:238
  422.7 5.7 %collective-permute-start.36 = (bf16[64,8192]{1,0:T(8,128)(2,1)}, bf16[64,8192]{1,0:T(8,128)(2,1)S(1)}, u32[]{:S(2)}, u32[]{:S(2)}) collective-permute-start(bf16[64,8192]{1,0:T(8,128)(2,1)} %get-tuple-element.23), channel_id=1, source_target_pairs={{0,12},{12,0},{1,13},{13,1},{2,14},{14,2},{3,15},{15,3},{16,28},{2... | collective-permute-start | bytes 3145736 | tf_op jit(solution)/shard_map/ppermute | solution.py:217
  428.4 14.5 %shard_map.99 = bf16[128,2048]{1,0:T(8,128)(2,1)S(1)} custom-call(s32[2]{0:T(128)S(1)} %pad_add_fusion.refs_0_, bf16[128,8192]{1,0:T(8,128)(2,1)} %collective-permute-done.26.refs_1_, bf16[256,8192]{1,0:T(8,128)(2,1)} %collective-permute-done.20.refs_2_, bf16[8192,1024]{1,0:T(8,128)(2,1)} %refs_3_.9, bf16[8192,512]{1,0:T(8,128)(2,1)} %copy-done.1, ...), custom_call_target="tpu_custom_call" | custom-call | flops 268435456 | bytes 2228224 | tf_op jit(solution)/shard_map/pallas_call | solution.py:152
  443.0 1.6 collective-permute-start.28
  444.9 10.5 %all-gather.2 = bf16[8,32,1024]{2,1,0:T(8,128)(2,1)S(1)} all-gather(bf16[2,32,1024]{2,1,0:T(8,128)(2,1)S(1)} %pad_maximum_fusion.4), channel_id=4, replica_groups=mesh['groups'=2,'row'=4,'col'=4] {'col'}, dimensions={0}, use_global_device_ids=true | all-gather | bytes 655360 | tf_op jit(solution)/shard_map/all_gather | solution.py:254
  455.4 12.8 %shard_map.100 = bf16[64,2048]{1,0:T(8,128)(2,1)S(1)} custom-call(s32[2]{0:T(128)S(1)} %pad_add_fusion.refs_0_, bf16[64,8192]{1,0:T(8,128)(2,1)S(1)} %collective-permute-done.31.refs_1_, bf16[256,8192]{1,0:T(8,128)(2,1)} %collective-permute-done.20.refs_2_, bf16[8192,1024]{1,0:T(8,128)(2,1)} %refs_3_.9, bf16[8192,512]{1,0:T(8,128)(2,1)S(1)} %bitcast.160, ...), custom_call_target="tpu_custom_call" | custom-call | flops 134217728 | bytes 2162688 | tf_op jit(solution)/shard_map/pallas_call | solution.py:152
  468.9 1.5 collective-permute-start.33
  470.4 2.4 collective-permute-done.30
  472.8 12.8 %shard_map.101 = bf16[64,2048]{1,0:T(8,128)(2,1)S(1)} custom-call(s32[2]{0:T(128)S(1)} %pad_add_fusion.refs_0_, bf16[64,8192]{1,0:T(8,128)(2,1)S(1)} %collective-permute-done.36.refs_1_, bf16[256,8192]{1,0:T(8,128)(2,1)} %collective-permute-done.20.refs_2_, bf16[8192,1024]{1,0:T(8,128)(2,1)} %refs_3_.9, bf16[8192,512]{1,0:T(8,128)(2,1)S(1)} %bitcast.160, ...), custom_call_target="tpu_custom_call" | custom-call | flops 134217728 | bytes 2162688 | tf_op jit(solution)/shard_map/pallas_call | solution.py:152
  485.8 1.6 collective-permute-start.38
  487.6 7.8 %all-gather.3 = bf16[8,32,1024]{2,1,0:T(8,128)(2,1)S(1)} all-gather(bf16[2,32,1024]{2,1,0:T(8,128)(2,1)S(1)} %pad_maximum_fusion.5), channel_id=5, replica_groups=mesh['groups'=2,'row'=4,'col'=4] {'col'}, dimensions={0}, use_global_device_ids=true | all-gather | bytes 655360 | tf_op jit(solution)/shard_map/all_gather | solution.py:254
  495.9 1.7 collective-permute-start.35
  497.6 2.0 collective-permute-done.40
  499.7 1.5 collective-permute-start.42
  501.6 6.3 %all-gather.4 = bf16[8,16,1024]{2,1,0:T(8,128)(2,1)S(1)} all-gather(bf16[2,16,1024]{2,1,0:T(8,128)(2,1)S(1)} %pad_maximum_fusion.9), channel_id=6, replica_groups=mesh['groups'=2,'row'=4,'col'=4] {'col'}, dimensions={0}, use_global_device_ids=true | all-gather | bytes 327680 | tf_op jit(solution)/shard_map/all_gather | solution.py:254
  507.8 1.8 fusion.34
  510.3 4.8 shard_map.102
  517.2 2.1 collective-permute-done.45
  521.2 3.4 collective-permute-start.49
  524.9 1.7 collective-permute-done.49
  (157 shorter events, 19.5 us)
Async XLA Ops:
  8.0 99.8 %all-gather.11.cloned.1.call-start = ((), (), s32[]{:S(2)}) async-start(), calls=%async_computation.1 | async-start | bytes 1310720 | tf_op jit(solution)/shard_map/all_gather | solution.py:193
  8.0 11.7 %slice-start.2 = ((s8[8388608]{0:T(1024)(128)(4,1)}), s8[4194304]{0:T(1024)(128)(4,1)S(1)}, s32[]{:S(2)}) async-start(s8[8388608]{0:T(1024)(128)(4,1)} %bitcast.161), calls=%async_computation.4 | async-start | bytes 8388608
  11.3 8.5 %slice-start.3 = ((s8[8388608]{0:T(1024)(128)(4,1)}), s8[4194304]{0:T(1024)(128)(4,1)S(1)}, s32[]{:S(2)}) async-start(s8[8388608]{0:T(1024)(128)(4,1)} %bitcast.161), calls=%async_computation.5 | async-start | bytes 8388608
  11.3 46.2 %collective-permute-start = (bf16[1024,512]{1,0:T(8,128)(2,1)}, bf16[1024,512]{1,0:T(8,128)(2,1)}, u32[]{:S(2)}, u32[]{:S(2)}) collective-permute-start(bf16[1024,512]{1,0:T(8,128)(2,1)} %get-tuple-element.27), channel_id=1, source_target_pairs={{0,4},{4,0},{8,12},{12,8},{1,5},{5,1},{9,13},{13,9},{2,6},{6,2},{1... | collective-permute-start | bytes 3145736 | tf_op jit(solution)/shard_map/ppermute | solution.py:206
  19.6 6.7 %copy-start.7 = (s32[2048]{0:T(1024)S(1)}, s32[2048]{0:T(1024)}, u32[]{:S(2)}) copy-start(s32[2048]{0:T(1024)} %param.15) | copy-start | bytes 24580
  19.6 6.7 %copy-start.8 = (s32[4]{0:T(128)S(1)}, s32[4]{0:T(128)}, u32[]{:S(2)}) copy-start(s32[4]{0:T(128)} %param.14) | copy-start | bytes 52
  19.6 80.8 %collective-permute-start.1 = (bf16[2048,512]{1,0:T(8,128)(2,1)}, bf16[2048,512]{1,0:T(8,128)(2,1)}, u32[]{:S(2)}, u32[]{:S(2)}) collective-permute-start(bf16[2048,512]{1,0:T(8,128)(2,1)} %get-tuple-element.30), channel_id=1, source_target_pairs={{0,4},{4,0},{8,12},{12,8},{1,5},{5,1},{9,13},{13,9},{2,6},{6,2},{1... | collective-permute-start | bytes 6291464 | tf_op jit(solution)/shard_map/ppermute | solution.py:206
  23.7 167.5 %collective-permute-start.10 = (bf16[256,8192]{1,0:T(8,128)(2,1)}, bf16[256,8192]{1,0:T(8,128)(2,1)}, u32[]{:S(2)}, u32[]{:S(2)}) collective-permute-start(bf16[256,8192]{1,0:T(8,128)(2,1)} %bitcast.5), channel_id=1, source_target_pairs={{4,8},{8,4},{5,9},{9,5},{6,10},{10,6},{7,11},{11,7},{20,24},{24,20... | collective-permute-start | bytes 12582920 | tf_op jit(solution)/shard_map/ppermute | solution.py:205
  34.3 473.6 %all-gather.9.cloned.1.call-start = ((), (), s32[]{:S(2)}) async-start(), calls=%async_computation | async-start | bytes 2621440 | tf_op jit(solution)/shard_map/all_gather | solution.py:245
  40.2 3.5 copy-start.2
  57.5 87.9 %collective-permute-start.2 = (bf16[2048,512]{1,0:T(8,128)(2,1)}, bf16[2048,512]{1,0:T(8,128)(2,1)}, u32[]{:S(2)}, u32[]{:S(2)}) collective-permute-start(bf16[2048,512]{1,0:T(8,128)(2,1)} %get-tuple-element.14), channel_id=1, source_target_pairs={{0,4},{4,0},{8,12},{12,8},{1,5},{5,1},{9,13},{13,9},{2,6},{6,2},{1... | collective-permute-start | bytes 6291464 | tf_op jit(solution)/shard_map/ppermute | solution.py:206
  60.6 162.0 %collective-permute-start.20 = (bf16[256,8192]{1,0:T(8,128)(2,1)}, bf16[256,8192]{1,0:T(8,128)(2,1)}, u32[]{:S(2)}, u32[]{:S(2)}) collective-permute-start(bf16[256,8192]{1,0:T(8,128)(2,1)} %bitcast.24), channel_id=1, source_target_pairs={{4,8},{8,4},{5,9},{9,5},{6,10},{10,6},{7,11},{11,7},{20,24},{24,20... | collective-permute-start | bytes 12582920 | tf_op jit(solution)/shard_map/ppermute | solution.py:205
  100.4 89.1 %collective-permute-start.3 = (bf16[2048,512]{1,0:T(8,128)(2,1)S(1)}, bf16[2048,512]{1,0:T(8,128)(2,1)}, u32[]{:S(2)}, u32[]{:S(2)}) collective-permute-start(bf16[2048,512]{1,0:T(8,128)(2,1)S(1)} %get-tuple-element.15), channel_id=1, source_target_pairs={{0,4},{4,0},{8,12},{12,8},{1,5},{5,1},{9,13},{13,9},{2,6},{6,2},{1... | collective-permute-start | bytes 6291464 | tf_op jit(solution)/shard_map/ppermute | solution.py:206
  102.5 46.5 %collective-permute-start.6 = (bf16[2048,512]{1,0:T(8,128)(2,1)}, bf16[2048,512]{1,0:T(8,128)(2,1)}, u32[]{:S(2)}, u32[]{:S(2)}) collective-permute-start(bf16[2048,512]{1,0:T(8,128)(2,1)} %collective-permute-done.1), channel_id=1, source_target_pairs={{0,16},{16,0},{1,17},{17,1},{2,18},{18,2},{3,19},{19,3},{4,20},{20... | collective-permute-start | bytes 6291464 | tf_op jit(solution)/shard_map/ppermute | solution.py:207
  107.8 89.5 %copy-start = (bf16[8192,512]{1,0:T(8,128)(2,1)S(1)}, bf16[8192,512]{1,0:T(8,128)(2,1)}, u32[]{:S(2)}) copy-start(bf16[8192,512]{1,0:T(8,128)(2,1)} %constant_dynamic-update-slice_fusion.4) | copy-start | bytes 25165828
  145.4 47.5 %collective-permute-start.5 = (bf16[1024,512]{1,0:T(8,128)(2,1)}, bf16[1024,512]{1,0:T(8,128)(2,1)S(1)}, u32[]{:S(2)}, u32[]{:S(2)}) collective-permute-start(bf16[1024,512]{1,0:T(8,128)(2,1)} %collective-permute-done), channel_id=1, source_target_pairs={{0,16},{16,0},{1,17},{17,1},{2,18},{18,2},{3,19},{19,3},{4,20},{20... | collective-permute-start | bytes 3145736 | tf_op jit(solution)/shard_map/ppermute | solution.py:207
  149.0 73.6 %collective-permute-start.7 = (bf16[2048,512]{1,0:T(8,128)(2,1)}, bf16[2048,512]{1,0:T(8,128)(2,1)S(1)}, u32[]{:S(2)}, u32[]{:S(2)}) collective-permute-start(bf16[2048,512]{1,0:T(8,128)(2,1)} %collective-permute-done.2), channel_id=1, source_target_pairs={{0,16},{16,0},{1,17},{17,1},{2,18},{18,2},{3,19},{19,3},{4,20},{20... | collective-permute-start | bytes 6291464 | tf_op jit(solution)/shard_map/ppermute | solution.py:207
  189.5 106.3 %collective-permute-start.8 = (bf16[2048,512]{1,0:T(8,128)(2,1)}, bf16[2048,512]{1,0:T(8,128)(2,1)S(1)}, u32[]{:S(2)}, u32[]{:S(2)}) collective-permute-start(bf16[2048,512]{1,0:T(8,128)(2,1)} %collective-permute-done.3), channel_id=1, source_target_pairs={{0,16},{16,0},{1,17},{17,1},{2,18},{18,2},{3,19},{19,3},{4,20},{20... | collective-permute-start | bytes 6291464 | tf_op jit(solution)/shard_map/ppermute | solution.py:207
  191.2 25.5 %collective-permute-start.4 = (bf16[1024,512]{1,0:T(8,128)(2,1)}, bf16[1024,512]{1,0:T(8,128)(2,1)S(1)}, u32[]{:S(2)}, u32[]{:S(2)}) collective-permute-start(bf16[1024,512]{1,0:T(8,128)(2,1)} %get-tuple-element.16), channel_id=1, source_target_pairs={{0,4},{4,0},{8,12},{12,8},{1,5},{5,1},{9,13},{13,9},{2,6},{6,2},{1... | collective-permute-start | bytes 3145736 | tf_op jit(solution)/shard_map/ppermute | solution.py:206
  192.8 106.5 %collective-permute-start.11 = (bf16[128,8192]{1,0:T(8,128)(2,1)}, bf16[128,8192]{1,0:T(8,128)(2,1)S(1)}, u32[]{:S(2)}, u32[]{:S(2)}) collective-permute-start(bf16[128,8192]{1,0:T(8,128)(2,1)} %get-tuple-element.17), channel_id=1, source_target_pairs={{0,12},{12,0},{1,13},{13,1},{2,14},{14,2},{3,15},{15,3},{16,28},{2... | collective-permute-start | bytes 6291464 | tf_op jit(solution)/shard_map/ppermute | solution.py:217
  216.7 79.3 %collective-permute-start.9 = (bf16[1024,512]{1,0:T(8,128)(2,1)S(1)}, bf16[1024,512]{1,0:T(8,128)(2,1)S(1)}, u32[]{:S(2)}, u32[]{:S(2)}) collective-permute-start(bf16[1024,512]{1,0:T(8,128)(2,1)S(1)} %collective-permute-done.4), channel_id=1, source_target_pairs={{0,16},{16,0},{1,17},{17,1},{2,18},{18,2},{3,19},{19,3},{4,20},{20... | collective-permute-start | bytes 3145736 | tf_op jit(solution)/shard_map/ppermute | solution.py:207
  218.9 5.1 copy-start.6
  218.9 80.4 %slice-start.4 = ((s8[8388608]{0:T(1024)(128)(4,1)}), s8[4194304]{0:T(1024)(128)(4,1)S(1)}, s32[]{:S(2)}) async-start(s8[8388608]{0:T(1024)(128)(4,1)} %bitcast.165), calls=%async_computation.6 | async-start | bytes 8388608
  219.0 76.8 %copy-start.1 = (bf16[8192,512]{1,0:T(8,128)(2,1)}, bf16[8192,512]{1,0:T(8,128)(2,1)S(1)}, u32[]{:S(2)}) copy-start(bf16[8192,512]{1,0:T(8,128)(2,1)S(1)} %constant_dynamic-update-slice_fusion.refs_2_.refs_4_) | copy-start | bytes 25165828
  224.0 75.4 %slice-start.5 = ((s8[8388608]{0:T(1024)(128)(4,1)}), s8[4194304]{0:T(1024)(128)(4,1)S(1)}, s32[]{:S(2)}) async-start(s8[8388608]{0:T(1024)(128)(4,1)} %bitcast.165), calls=%async_computation.7 | async-start | bytes 8388608
  224.0 138.5 %collective-permute-start.21 = (bf16[128,8192]{1,0:T(8,128)(2,1)S(1)}, bf16[128,8192]{1,0:T(8,128)(2,1)S(1)}, u32[]{:S(2)}, u32[]{:S(2)}) collective-permute-start(bf16[128,8192]{1,0:T(8,128)(2,1)S(1)} %copy-done.6), channel_id=1, source_target_pairs={{0,12},{12,0},{1,13},{13,1},{2,14},{14,2},{3,15},{15,3},{16,28},{2... | collective-permute-start | bytes 6291464 | tf_op jit(solution)/shard_map/ppermute | solution.py:217
  327.2 2.7 collective-permute-start.16
  327.3 6.4 %collective-permute-start.17 = (bf16[32,2048]{1,0:T(8,128)(2,1)S(1)}, bf16[32,2048]{1,0:T(8,128)(2,1)S(1)}, u32[]{:S(2)}, u32[]{:S(2)}) collective-permute-start(bf16[32,2048]{1,0:T(8,128)(2,1)S(1)} %get-tuple-element.67), channel_id=1, source_target_pairs={{0,2},{1,3},{2,0},{3,1},{4,6},{5,7},{6,4},{7,5},{8,10},{9,11},{10,... | collective-permute-start | bytes 393224 | tf_op jit(solution)/shard_map/ppermute | solution.py:236
  328.8 6.7 %collective-permute-start.18 = (bf16[32,2048]{1,0:T(8,128)(2,1)S(1)}, bf16[32,2048]{1,0:T(8,128)(2,1)S(1)}, u32[]{:S(2)}, u32[]{:S(2)}) collective-permute-start(bf16[32,2048]{1,0:T(8,128)(2,1)S(1)} %get-tuple-element.66), channel_id=1, source_target_pairs={{0,3},{1,2},{2,1},{3,0},{4,7},{5,6},{6,5},{7,4},{8,11},{9,10},{10,... | collective-permute-start | bytes 393224 | tf_op jit(solution)/shard_map/ppermute | solution.py:236
  329.5 32.6 %collective-permute-start.12 = (bf16[128,2048]{1,0:T(8,128)(2,1)S(1)}, bf16[128,2048]{1,0:T(8,128)(2,1)S(1)}, u32[]{:S(2)}, u32[]{:S(2)}) collective-permute-start(bf16[128,2048]{1,0:T(8,128)(2,1)S(1)} %get-tuple-element.42), channel_id=1, source_target_pairs={{0,1},{1,0},{2,3},{3,2},{4,5},{5,4},{6,7},{7,6},{8,9},{9,8},{10,11... | collective-permute-start | bytes 1572872 | tf_op jit(solution)/shard_map/ppermute | solution.py:236
  329.9 32.2 %collective-permute-start.13 = (bf16[128,2048]{1,0:T(8,128)(2,1)S(1)}, bf16[128,2048]{1,0:T(8,128)(2,1)S(1)}, u32[]{:S(2)}, u32[]{:S(2)}) collective-permute-start(bf16[128,2048]{1,0:T(8,128)(2,1)S(1)} %get-tuple-element.44), channel_id=1, source_target_pairs={{0,2},{1,3},{2,0},{3,1},{4,6},{5,7},{6,4},{7,5},{8,10},{9,11},{10,... | collective-permute-start | bytes 1572872 | tf_op jit(solution)/shard_map/ppermute | solution.py:236
  333.6 28.5 %collective-permute-start.14 = (bf16[128,2048]{1,0:T(8,128)(2,1)S(1)}, bf16[128,2048]{1,0:T(8,128)(2,1)S(1)}, u32[]{:S(2)}, u32[]{:S(2)}) collective-permute-start(bf16[128,2048]{1,0:T(8,128)(2,1)S(1)} %get-tuple-element.43), channel_id=1, source_target_pairs={{0,3},{1,2},{2,1},{3,0},{4,7},{5,6},{6,5},{7,4},{8,11},{9,10},{10,... | collective-permute-start | bytes 1572872 | tf_op jit(solution)/shard_map/ppermute | solution.py:236
  335.6 4.8 collective-permute-start.19
  340.4 82.3 %collective-permute-start.26 = (bf16[128,8192]{1,0:T(8,128)(2,1)}, bf16[128,8192]{1,0:T(8,128)(2,1)}, u32[]{:S(2)}, u32[]{:S(2)}) collective-permute-start(bf16[128,8192]{1,0:T(8,128)(2,1)} %get-tuple-element.21), channel_id=1, source_target_pairs={{0,12},{12,0},{1,13},{13,1},{2,14},{14,2},{3,15},{15,3},{16,28},{2... | collective-permute-start | bytes 6291464 | tf_op jit(solution)/shard_map/ppermute | solution.py:217
  376.8 2.1 collective-permute-start.22
  377.2 8.6 %collective-permute-start.23 = (bf16[32,2048]{1,0:T(8,128)(2,1)S(1)}, bf16[32,2048]{1,0:T(8,128)(2,1)S(1)}, u32[]{:S(2)}, u32[]{:S(2)}) collective-permute-start(bf16[32,2048]{1,0:T(8,128)(2,1)S(1)} %get-tuple-element.64), channel_id=1, source_target_pairs={{0,2},{1,3},{2,0},{3,1},{4,6},{5,7},{6,4},{7,5},{8,10},{9,11},{10,... | collective-permute-start | bytes 393224 | tf_op jit(solution)/shard_map/ppermute | solution.py:236
  378.7 7.1 %collective-permute-start.24 = (bf16[32,2048]{1,0:T(8,128)(2,1)S(1)}, bf16[32,2048]{1,0:T(8,128)(2,1)S(1)}, u32[]{:S(2)}, u32[]{:S(2)}) collective-permute-start(bf16[32,2048]{1,0:T(8,128)(2,1)S(1)} %get-tuple-element.63), channel_id=1, source_target_pairs={{0,3},{1,2},{2,1},{3,0},{4,7},{5,6},{6,5},{7,4},{8,11},{9,10},{10,... | collective-permute-start | bytes 393224 | tf_op jit(solution)/shard_map/ppermute | solution.py:236
  378.8 20.8 %collective-permute-start.15 = (bf16[128,1024]{1,0:T(8,128)(2,1)S(1)}, bf16[128,1024]{1,0:T(8,128)(2,1)S(1)}, u32[]{:S(2)}, u32[]{:S(2)}) collective-permute-start(bf16[128,1024]{1,0:T(8,128)(2,1)S(1)} %get-tuple-element.69), channel_id=1, source_target_pairs={{0,4},{4,0},{8,12},{12,8},{1,5},{5,1},{9,13},{13,9},{2,6},{6,2},{1... | collective-permute-start | bytes 786440 | tf_op jit(solution)/shard_map/ppermute | solution.py:238
  378.9 76.5 %collective-permute-start.31 = (bf16[64,8192]{1,0:T(8,128)(2,1)}, bf16[64,8192]{1,0:T(8,128)(2,1)S(1)}, u32[]{:S(2)}, u32[]{:S(2)}) collective-permute-start(bf16[64,8192]{1,0:T(8,128)(2,1)} %get-tuple-element.22), channel_id=1, source_target_pairs={{0,12},{12,0},{1,13},{13,1},{2,14},{14,2},{3,15},{15,3},{16,28},{2... | collective-permute-start | bytes 3145736 | tf_op jit(solution)/shard_map/ppermute | solution.py:217
  385.9 36.8 %collective-permute-start.25 = (bf16[32,1024]{1,0:T(8,128)(2,1)S(1)}, bf16[32,1024]{1,0:T(8,128)(2,1)S(1)}, u32[]{:S(2)}, u32[]{:S(2)}) collective-permute-start(bf16[32,1024]{1,0:T(8,128)(2,1)S(1)} %get-tuple-element.83), channel_id=1, source_target_pairs={{0,4},{4,0},{8,12},{12,8},{1,5},{5,1},{9,13},{13,9},{2,6},{6,2},{1... | collective-permute-start | bytes 196616 | tf_op jit(solution)/shard_map/ppermute | solution.py:238
  422.7 32.7 %slice-start = ((s8[8388608]{0:T(1024)(128)(4,1)}), s8[4194304]{0:T(1024)(128)(4,1)S(1)}, s32[]{:S(2)}) async-start(s8[8388608]{0:T(1024)(128)(4,1)} %bitcast.159), calls=%async_computation.2 | async-start | bytes 8388608
  422.7 32.7 %slice-start.1 = ((s8[8388608]{0:T(1024)(128)(4,1)}), s8[4194304]{0:T(1024)(128)(4,1)S(1)}, s32[]{:S(2)}) async-start(s8[8388608]{0:T(1024)(128)(4,1)} %bitcast.159), calls=%async_computation.3 | async-start | bytes 8388608
  422.7 50.1 %collective-permute-start.36 = (bf16[64,8192]{1,0:T(8,128)(2,1)}, bf16[64,8192]{1,0:T(8,128)(2,1)S(1)}, u32[]{:S(2)}, u32[]{:S(2)}) collective-permute-start(bf16[64,8192]{1,0:T(8,128)(2,1)} %get-tuple-element.23), channel_id=1, source_target_pairs={{0,12},{12,0},{1,13},{13,1},{2,14},{14,2},{3,15},{15,3},{16,28},{2... | collective-permute-start | bytes 3145736 | tf_op jit(solution)/shard_map/ppermute | solution.py:217
  442.9 25.3 %collective-permute-start.27 = (bf16[32,2048]{1,0:T(8,128)(2,1)S(1)}, bf16[32,2048]{1,0:T(8,128)(2,1)S(1)}, u32[]{:S(2)}, u32[]{:S(2)}) collective-permute-start(bf16[32,2048]{1,0:T(8,128)(2,1)S(1)} %get-tuple-element.59), channel_id=1, source_target_pairs={{0,1},{1,0},{2,3},{3,2},{4,5},{5,4},{6,7},{7,6},{8,9},{9,8},{10,11... | collective-permute-start | bytes 393224 | tf_op jit(solution)/shard_map/ppermute | solution.py:236
  443.0 25.3 %collective-permute-start.28 = (bf16[32,2048]{1,0:T(8,128)(2,1)S(1)}, bf16[32,2048]{1,0:T(8,128)(2,1)S(1)}, u32[]{:S(2)}, u32[]{:S(2)}) collective-permute-start(bf16[32,2048]{1,0:T(8,128)(2,1)S(1)} %get-tuple-element.61), channel_id=1, source_target_pairs={{0,2},{1,3},{2,0},{3,1},{4,6},{5,7},{6,4},{7,5},{8,10},{9,11},{10,... | collective-permute-start | bytes 393224 | tf_op jit(solution)/shard_map/ppermute | solution.py:236
  444.6 23.7 %collective-permute-start.29 = (bf16[32,2048]{1,0:T(8,128)(2,1)S(1)}, bf16[32,2048]{1,0:T(8,128)(2,1)S(1)}, u32[]{:S(2)}, u32[]{:S(2)}) collective-permute-start(bf16[32,2048]{1,0:T(8,128)(2,1)S(1)} %get-tuple-element.60), channel_id=1, source_target_pairs={{0,3},{1,2},{2,1},{3,0},{4,7},{5,6},{6,5},{7,4},{8,11},{9,10},{10,... | collective-permute-start | bytes 393224 | tf_op jit(solution)/shard_map/ppermute | solution.py:236
  468.4 4.4 collective-permute-start.30
  468.5 18.8 %collective-permute-start.32 = (bf16[16,2048]{1,0:T(8,128)(2,1)S(1)}, bf16[16,2048]{1,0:T(8,128)(2,1)S(1)}, u32[]{:S(2)}, u32[]{:S(2)}) collective-permute-start(bf16[16,2048]{1,0:T(8,128)(2,1)S(1)} %get-tuple-element.77), channel_id=1, source_target_pairs={{0,1},{1,0},{2,3},{3,2},{4,5},{5,4},{6,7},{7,6},{8,9},{9,8},{10,11... | collective-permute-start | bytes 196616 | tf_op jit(solution)/shard_map/ppermute | solution.py:236
  468.9 26.5 %collective-permute-start.33 = (bf16[16,2048]{1,0:T(8,128)(2,1)S(1)}, bf16[16,2048]{1,0:T(8,128)(2,1)S(1)}, u32[]{:S(2)}, u32[]{:S(2)}) collective-permute-start(bf16[16,2048]{1,0:T(8,128)(2,1)S(1)} %get-tuple-element.79), channel_id=1, source_target_pairs={{0,2},{1,3},{2,0},{3,1},{4,6},{5,7},{6,4},{7,5},{8,10},{9,11},{10,... | collective-permute-start | bytes 196616 | tf_op jit(solution)/shard_map/ppermute | solution.py:236
  470.4 25.0 %collective-permute-start.34 = (bf16[16,2048]{1,0:T(8,128)(2,1)S(1)}, bf16[16,2048]{1,0:T(8,128)(2,1)S(1)}, u32[]{:S(2)}, u32[]{:S(2)}) collective-permute-start(bf16[16,2048]{1,0:T(8,128)(2,1)S(1)} %get-tuple-element.78), channel_id=1, source_target_pairs={{0,3},{1,2},{2,1},{3,0},{4,7},{5,6},{6,5},{7,4},{8,11},{9,10},{10,... | collective-permute-start | bytes 196616 | tf_op jit(solution)/shard_map/ppermute | solution.py:236
  485.7 9.7 %collective-permute-start.37 = (bf16[16,2048]{1,0:T(8,128)(2,1)S(1)}, bf16[16,2048]{1,0:T(8,128)(2,1)S(1)}, u32[]{:S(2)}, u32[]{:S(2)}) collective-permute-start(bf16[16,2048]{1,0:T(8,128)(2,1)S(1)} %get-tuple-element.74), channel_id=1, source_target_pairs={{0,1},{1,0},{2,3},{3,2},{4,5},{5,4},{6,7},{7,6},{8,9},{9,8},{10,11... | collective-permute-start | bytes 196616 | tf_op jit(solution)/shard_map/ppermute | solution.py:236
  485.8 9.6 %collective-permute-start.38 = (bf16[16,2048]{1,0:T(8,128)(2,1)S(1)}, bf16[16,2048]{1,0:T(8,128)(2,1)S(1)}, u32[]{:S(2)}, u32[]{:S(2)}) collective-permute-start(bf16[16,2048]{1,0:T(8,128)(2,1)S(1)} %get-tuple-element.76), channel_id=1, source_target_pairs={{0,2},{1,3},{2,0},{3,1},{4,6},{5,7},{6,4},{7,5},{8,10},{9,11},{10,... | collective-permute-start | bytes 196616 | tf_op jit(solution)/shard_map/ppermute | solution.py:236
  487.3 8.1 %collective-permute-start.39 = (bf16[16,2048]{1,0:T(8,128)(2,1)S(1)}, bf16[16,2048]{1,0:T(8,128)(2,1)S(1)}, u32[]{:S(2)}, u32[]{:S(2)}) collective-permute-start(bf16[16,2048]{1,0:T(8,128)(2,1)S(1)} %get-tuple-element.75), channel_id=1, source_target_pairs={{0,3},{1,2},{2,1},{3,0},{4,7},{5,6},{6,5},{7,4},{8,11},{9,10},{10,... | collective-permute-start | bytes 196616 | tf_op jit(solution)/shard_map/ppermute | solution.py:236
  495.5 4.1 collective-permute-start.40
  495.9 5.7 %collective-permute-start.35 = (bf16[16,1024]{1,0:T(8,128)(2,1)S(1)}, bf16[16,1024]{1,0:T(8,128)(2,1)S(1)}, u32[]{:S(2)}, u32[]{:S(2)}) collective-permute-start(bf16[16,1024]{1,0:T(8,128)(2,1)S(1)} %get-tuple-element.93), channel_id=1, source_target_pairs={{0,4},{4,0},{8,12},{12,8},{1,5},{5,1},{9,13},{13,9},{2,6},{6,2},{1... | collective-permute-start | bytes 98312 | tf_op jit(solution)/shard_map/ppermute | solution.py:238
  499.6 10.1 %collective-permute-start.41 = (bf16[2,16,1024]{2,1,0:T(8,128)(2,1)S(1)}, bf16[2,16,1024]{2,1,0:T(8,128)(2,1)S(1)}, u32[]{:S(2)}, u32[]{:S(2)}) collective-permute-start(bf16[2,16,1024]{2,1,0:T(8,128)(2,1)S(1)} %pad_maximum_fusion.10), channel_id=1, source_target_pairs={{0,1},{1,0},{2,3},{3,2},{4,5},{5,4},{6,7},{7,6},{8,9},{9,8},{10,11... | collective-permute-start | bytes 196616 | tf_op jit(solution)/shard_map/ppermute | solution.py:259
  499.7 10.0 %collective-permute-start.42 = (bf16[2,16,1024]{2,1,0:T(8,128)(2,1)S(1)}, bf16[2,16,1024]{2,1,0:T(8,128)(2,1)S(1)}, u32[]{:S(2)}, u32[]{:S(2)}) collective-permute-start(bf16[2,16,1024]{2,1,0:T(8,128)(2,1)S(1)} %pad_maximum_fusion.10), channel_id=1, source_target_pairs={{0,2},{1,3},{2,0},{3,1},{4,6},{5,7},{6,4},{7,5},{8,10},{9,11},{10,... | collective-permute-start | bytes 196616 | tf_op jit(solution)/shard_map/ppermute | solution.py:259
  501.2 8.5 %collective-permute-start.43 = (bf16[2,16,1024]{2,1,0:T(8,128)(2,1)S(1)}, bf16[2,16,1024]{2,1,0:T(8,128)(2,1)S(1)}, u32[]{:S(2)}, u32[]{:S(2)}) collective-permute-start(bf16[2,16,1024]{2,1,0:T(8,128)(2,1)S(1)} %pad_maximum_fusion.10), channel_id=1, source_target_pairs={{0,3},{1,2},{2,1},{3,0},{4,7},{5,6},{6,5},{7,4},{8,11},{9,10},{10,... | collective-permute-start | bytes 196616 | tf_op jit(solution)/shard_map/ppermute | solution.py:259
  515.4 1.9 collective-permute-start.44
  515.7 3.6 collective-permute-start.45
  517.2 3.0 collective-permute-start.46
  520.2 4.4 collective-permute-start.47
  520.4 4.5 collective-permute-start.48
  521.2 5.4 %collective-permute-start.49 = (f32[4,4]{1,0:T(4,128)S(1)}, f32[4,4]{1,0:T(4,128)S(1)}, u32[]{:S(2)}, u32[]{:S(2)}) collective-permute-start(f32[4,4]{1,0:T(4,128)S(1)} %add_add_fusion.1), channel_id=1, source_target_pairs={{0,12},{4,8},{8,4},{12,0},{1,13},{5,9},{9,5},{13,1},{2,14},{6,10},... | collective-permute-start | bytes 200 | tf_op jit(solution)/shard_map/ppermute | solution.py:177
  (3 other events, 8.0 us)
Sparse Core Ops, SparseCore 0:
  34.4 43.5 all-gather.10
Sparse Core Ops, SparseCore 1:
  400.6 22.9 all-gather.8

commit v5 on v4

--- a/solution.py
+++ b/solution.py
@@ -26,45 +26,34 @@
     return (rotated * live[:, :, None]).astype(BF16)
 
 
-def final_kernel(counts, *refs):
-    total = sum(counts)
-    pieces = list(refs[:total])
-    act_ref, eig_ref, query_ref, out_ref, score_ref = refs[total:]
-    cands, queries = len(counts), query_ref.shape[0]
+def final_kernel(layout, count, *refs):
+    arrays = refs[:count]
+    act_ref, eig_ref, query_ref, out_ref, score_ref = refs[count:]
+    queries = query_ref.shape[0]
     damped = eig_ref[...] + DAMPING
     weights = [query_ref[q].astype(F32) / damped for q in range(queries)]
     rows = [[] for _ in range(queries)]
-    for c in range(cands):
-        tile, start = None, 0
-        for _ in range(counts[c]):
-            piece = pieces.pop(0)
-            n = piece.shape[0]
-            term = lax.dot_general(
-                piece[...],
-                act_ref[c, start : start + n],
-                (((0,), (0,)), ((), ())),
-                preferred_element_type=F32,
-            )
-            tile = term if tile is None else tile + term
-            start += n
+    for c, segments in enumerate(layout):
+        tokens = jnp.concatenate([arrays[i][s : s + n] for i, s, n in segments], axis=0)
+        tile = lax.dot_general(
+            tokens, act_ref[c], (((0,), (0,)), ((), ())), preferred_element_type=F32
+        )
         out_ref[c] = tile
         for q in range(queries):
             rows[q].append(jnp.sum(weights[q] * tile, axis=0, keepdims=True))
     score_ref[0] = jnp.concatenate([r for one in rows for r in one], axis=0)
 
 
-def rotate_and_score(pieces, act_rot, eigenvalues, query_rotated):
-    counts = tuple(len(p) for p in pieces)
-    flat = [x for p in pieces for x in p]
+def rotate_and_score(arrays, layout, act_rot, eigenvalues, query_rotated):
     cands, seq, width = act_rot.shape
     dirs = eigenvalues.shape[0]
     queries = query_rotated.shape[0]
     block = min(dirs, 256)
     steps = dirs // block
     rotated, partial_scores = pl.pallas_call(
-        functools.partial(final_kernel, counts),
+        functools.partial(final_kernel, layout, len(arrays)),
         grid=(steps,),
-        in_specs=[pl.BlockSpec((x.shape[0], block), lambda i: (0, i)) for x in flat]
+        in_specs=[pl.BlockSpec((x.shape[0], block), lambda i: (0, i)) for x in arrays]
         + [
             pl.BlockSpec((cands, seq, width), lambda i: (0, 0, 0)),
             pl.BlockSpec((block, width), lambda i: (i, 0)),
@@ -79,7 +68,7 @@
             jax.ShapeDtypeStruct((steps, queries * cands, width), F32),
         ],
         compiler_params=pltpu.CompilerParams(vmem_limit_bytes=32 * 2**20),
-    )(*flat, act_rot, eigenvalues, query_rotated)
+    )(*arrays, act_rot, eigenvalues, query_rotated)
     return rotated, jnp.sum(partial_scores, axis=(0, 2)).reshape(queries, cands)
 
 
@@ -94,8 +83,10 @@
     )
     every_act = lax.all_gather(local_act, "row", axis=1, tiled=True)
     rotated_grads = lax.psum(partial_value, "col").astype(BF16)
-    pieces = [[rotated_grads[c]] for c in range(acts.shape[0])]
-    rotated, scores = rotate_and_score(pieces, every_act, eigenvalues, query_rotated)
+    cands, seq = rotated_grads.shape[:2]
+    arrays = [rotated_grads[c] for c in range(cands)]
+    layout = tuple(((c, 0, seq),) for c in range(cands))
+    rotated, scores = rotate_and_score(arrays, layout, every_act, eigenvalues, query_rotated)
     return rotated, lax.psum(scores, ("row", "col"))
 
 
@@ -107,9 +98,11 @@
     flags, refs = refs[0], refs[1:]
     tokens, basis, out, acc = refs[:count], refs[count:-2], refs[-2], refs[-1]
     step = pl.program_id(0)
-    rows = tokens[0][...]
-    if count == 2:
-        rows = jnp.where(flags[0] == 1, rows, tokens[1][...])
+    rows = [t[...] for t in tokens]
+    if count > 1:
+        joined = jnp.concatenate(rows[:-1], axis=0) if count > 2 else rows[0]
+        rows = [jnp.where(flags[0] == 1, joined, rows[-1])]
+    rows = rows[0]
     start, spans = 0, []
     for width in widths:
         spans.append((start, start + width))
@@ -145,10 +138,11 @@
     feats = bases[0].shape[0]
     widths = tuple(x.shape[1] for x in bases)
     block, total = 1024, sum(widths)
-    rows = tokens[0][2]
-    specs = [
-        pl.BlockSpec((rows, block), lambda k, i=start // rows: (i, k)) for _, start, _ in tokens
-    ]
+    rows = tokens[-1][2]
+    specs = []
+    for _, start, n in tokens:
+        assert start % n == 0
+        specs.append(pl.BlockSpec((n, block), lambda k, i=start // n: (i, k)))
     return pl.pallas_call(
         functools.partial(project_kernel, len(tokens), widths),
         grid=(feats // block,),
@@ -193,40 +187,37 @@
     every_act = lax.all_gather(local_act, "row", axis=0)
 
     half, flat = dirs // sides, grads.reshape(cands * tok, feats)
-    units, deep = 8, feats // 8
+    units, deep, slab = 8, feats // 8, cands * tok // 8
     near, far, other = [], [], []
+    spans = [(0, 1), (1, 3), (3, 5), (5, 7), (7, units)]
+    batches = [(0, 1), (2,), (3, 4)]
+    ranges = [(spans[x[0]][0] * slab, spans[x[-1]][1] * slab) for x in batches]
     own_own = project(flags, [(flat, 0, cands * tok)], [grad_basis])
-    for i, (a, b) in enumerate([(0, 1), (1, 3), (3, 5), (5, 7), (7, units)]):
+    for i, (a, b) in enumerate(spans):
         piece = lax.dynamic_slice(grad_basis, (a * deep, group * half), ((b - a) * deep, half))
         if i >= 2:
-            piece = after(piece, near[i - 2], *([own_own, local_act] if i == 2 else []))
-        if i in (0, 2):
-            part = flat[: cands * tok // 2] if i == 0 else after(flat[cands * tok // 2 :], near[0])
-            other.append(lax.ppermute(part, "row", middle))
+            early = [own_own, local_act] if i == 2 else [other[i - 3]]
+            piece = after(piece, near[i - 2], *early)
+        if i < len(ranges):
+            rows = flat[slice(*ranges[i])]
+            other.append(lax.ppermute(after(rows, near[i - 1]) if i else rows, "row", middle))
         near.append(lax.ppermute(piece, "row", beside))
         far.append(lax.ppermute(near[i], "groups", [(0, 1), (1, 0)]))
     near_basis = jnp.concatenate(near, axis=0)
     far_basis = jnp.concatenate(far, axis=0)
 
-    spans = [(c * tok, tok) for c in range(cands - 1)]
-    spans += [((cands - 1) * tok + s, tok // 2) for s in (0, tok // 2)]
-    ties = {0: [near[3], far[1], other[0]], 1: [near[4], far[2], other[1]], 2: [far[4]]}
-    partner, products = [], []
-    for k, (start, n) in enumerate(spans):
+    ties = {0: [near[3], far[1]], 1: [near[3], far[2]], 2: [near[4], other[2]]}
+    partner = []
+    for k, (a, b) in enumerate(spans):
         tie = ties.get(k, []) + ([partner[k - 2]] if k >= 2 else [])
-        partner.append(lax.ppermute(after(flat[start : start + n], *tie), "row", ends))
-        if k == 0:
-            own_end = project(flags, [(flat, 0, cands * tok)], [near_basis, after(far_basis, partner[0])])
-            ties[3] = [own_end]
-        inner = other[2 * start // (cands * tok)]
-        products.append(
-            project(
-                flags,
-                [(partner[k], 0, n), (inner, start % (cands * tok // 2), n)],
-                [grad_basis, near_basis, far_basis],
-            )
-        )
-        ties[k + 3] = ties.get(k + 3, []) + [products[k]]
+        piece = flat[a * slab : b * slab]
+        partner.append(lax.ppermute(after(piece, *tie), "row", ends))
+    own_end = project(flags, [(flat, 0, cands * tok)], [near_basis, after(far_basis, partner[0])])
+    products = []
+    for batch, inner, (first, last) in zip(batches, other, ranges):
+        tokens = [(partner[k], 0, (spans[k][1] - spans[k][0]) * slab) for k in batch]
+        tokens.append((inner, 0, last - first))
+        products.append(project(flags, tokens, [grad_basis, near_basis, far_basis]))
 
     def scatter_sum(value):
         value = value.reshape(parts, -1, 2 * dirs)
@@ -241,27 +232,28 @@
         lax.dynamic_index_in_dim(every_act, i, 0, keepdims=False)
         for i in (row, row ^ 1, planes - 1 - row, planes - 1 - (row ^ 1))
     ]
-    pieces, act_order = [[] for _ in range(cands)], [[] for _ in range(cands)]
-    own = lax.all_gather(scatter_sum(jnp.concatenate([own_own, own_end], axis=1)), "col", axis=0)
-    for c in range(cands):
-        pieces[c].append(own[c].reshape(2 * tok, dirs))
-        act_order[c] += [act[0][c], act[1][c]]
-    for k, (start, n) in enumerate(spans):
-        c, s = start // tok, start % tok
-        mine = scatter_sum(products[k])
-        tokens = jnp.stack([x[c, s : s + n].reshape(parts, n // parts, -1) for x in act[2:]], axis=1)
-        if k < len(spans) - 1:
-            every = lax.all_gather(mine, "col", axis=0)
-            pieces[c].append(every.reshape(2 * n, dirs))
-            act_order[c].append(tokens.reshape(2 * n, -1))
-        else:
-            for d in range(parts):
-                got = lax.ppermute(mine, "col", [(i, i ^ d) for i in range(parts)]) if d else mine
-                pieces[c].append(got.reshape(2 * n // parts, dirs))
-                sub = lax.dynamic_index_in_dim(tokens, col ^ d, 0, keepdims=False)
-                act_order[c].append(sub.reshape(2 * n // parts, -1))
+    arrays, segments, act_order = [], [[] for _ in range(cands)], [[] for _ in range(cands)]
+
+    def place(value, start, sources):
+        every = lax.all_gather(scatter_sum(value), "col", axis=0)
+        n = every.shape[2]
+        for p in range(parts):
+            for j, source in enumerate(sources):
+                at, row_at = start + p * n, (p * 2 + j) * n
+                while at < start + (p + 1) * n:
+                    c, s = at // tok, at % tok
+                    length = min(tok - s, start + (p + 1) * n - at)
+                    segments[c].append((len(arrays), row_at, length))
+                    act_order[c].append(source[c, s : s + length])
+                    at, row_at = at + length, row_at + length
+        arrays.append(every.reshape(parts * 2 * n, dirs))
+
+    place(jnp.concatenate([own_own, own_end], axis=1), 0, act[:2])
+    for (first, _), product in zip(ranges, products):
+        place(product, first, act[2:])
     act_rot = jnp.stack([jnp.concatenate(x, axis=0) for x in act_order])
-    rotated, scores = rotate_and_score(pieces, act_rot, eigenvalues, query_rotated)
+    layout = tuple(tuple(s) for s in segments)
+    rotated, scores = rotate_and_score(arrays, layout, act_rot, eigenvalues, query_rotated)
     scores = exchange_sum(exchange_sum(scores, "col", parts), "row", planes)
     return rotated, scores
 

time: 535 us -> 513 us (0.959)
  Pallas kernels: 101 us -> 76.2 us
  blocking collectives: 39.4 us -> 29.6 us
    pallas_call x7 -> x5, Pallas kernels: 95.9 us -> 71.9 us  [project(): pl.pallas_call(functools.partial(project_kernel, len(tokens), widths), gr...]
    ppermute x6 -> x4, waiting for transfers between devices: 44.7 us -> 27.8 us  [scatter_sum(): lax.ppermute(total[:, dirs:], 'row', beside)]
    ppermute x18 -> x12, waiting for transfers between devices: 3.85 us -> 17.4 us  [scatter_sum(): lax.ppermute(sent, 'col', [(i, i ^ d) for i in range(parts)]).astype(F32)]
    ppermute x5, starting transfers between devices: 9.92 us -> 22.8 us  [chain_body(): near.append(lax.ppermute(piece, 'row', beside))]
    ppermute x10 -> x8, waiting for transfers between devices: 0.03 us -> 11.5 us  [the longest x5 11.5 us: chain_body(): partner.append(lax.ppermute(after(piece, *tie), 'row', ends))]
    all_gather x4 -> x3, blocking collectives: 39.4 us -> 29.6 us  [place(): every = lax.all_gather(scatter_sum(value), 'col', axis=0)]
    unnamed x44 -> x78, local copies, waits for them, and re-layouts: 22.4 us -> 31.6 us
    ppermute x5, waiting for transfers between devices: 125 us -> 117 us  [chain_body(): near.append(lax.ppermute(piece, 'row', beside))]
  transfers between devices with their start and end apart: 52 -> 42, of which waited for: 16 -> 16; matrix products, arithmetic and copies ran while one was open for 8% -> 8% of each run, Pallas kernels for 18% -> 14%
where the time goes in v5:
time: 513 us; the launch traced here: 512 us
  waiting for transfers between devices  180 us (35%)
  starting transfers between devices  146 us (28%)
  Pallas kernels  76.2 us (15%)
  local copies, waits for them, and re-layouts  52.1 us (10%)
  blocking collectives  29.6 us (6%)
  between operations  16.1 us (3%)
  matrix products  7.6 us (1%)
    ppermute x5, waiting for transfers between devices, chain_body(): near.append(lax.ppermute(piece, 'row', beside))  117 us
    ppermute x5, starting transfers between devices, chain_body(): partner.append(lax.ppermute(after(piece, *tie), 'row', ends))  92 us
    pallas_call x5, Pallas kernels, project(): pl.pallas_call(functools.partial(project_kernel, len(tokens), widths), gr...  71.9 us
    unnamed x78, local copies, waits for them, and re-layouts  31.6 us
    all_gather x3, blocking collectives, place(): every = lax.all_gather(scatter_sum(value), 'col', axis=0)  29.6 us
    ppermute x4, waiting for transfers between devices, scatter_sum(): lax.ppermute(total[:, dirs:], 'row', beside)  27.8 us
    ppermute x5, starting transfers between devices, chain_body(): near.append(lax.ppermute(piece, 'row', beside))  22.8 us
    ppermute x12, waiting for transfers between devices, scatter_sum(): lax.ppermute(sent, 'col', [(i, i ^ d) for i in range(parts)]).astype(F32)  17.4 us
  transfers between devices with their start and end apart: 42, of which 16 were waited for; matrix products, arithmetic and copies ran while one was open for 8% of the time, Pallas kernels for 14%

profile of v5, /device:TPU:0, one launch (start us, length us, event | category | flops | bytes accessed | tf_op | source)
XLA Modules:
  0.0 512.1 jit_solution(6011880959172929132)
XLA Ops:
  9.0 7.6 %fusion.5 = bf16[4,128,256]{2,1,0:T(8,128)(2,1)} fusion(bf16[4,128,8192]{2,1,0:T(8,128)(2,1)} %param.8, bf16[8192,256]{1,0:T(8,128)(2,1)} %param.10, f32[4,128]{1,0:T(4,128)S(1)} %compare_convert_fusion), kind=kOutput, calls=%fused_computation.4 | convolution fusion | flops 2147745792 | bytes 12847104 | tf_op jit(solution)/shard_map/ctd,dk->ctk/dot_general | solution.py:25
  16.7 2.8 constant_dynamic-slice_fusion.1
  19.5 3.0 collective-permute-start
  22.6 5.7 %constant_dynamic-slice_fusion.2 = (bf16[2048,512]{1,0:T(8,128)(2,1)}, bf16[2048,512]{1,0:T(8,128)(2,1)}, bf16[2048,512]{1,0:T(8,128)(2,1)}) fusion(bf16[8192,1024]{1,0:T(8,128)(2,1)} %refs_4_.3, s32[]{:T(128)S(6)} %select_n.51), kind=kLoop, calls=%fused_computation.134 | loop fusion | bytes 12582916 | tf_op jit(solution)/shard_map/dynamic_slice | solution.py:197
  28.4 3.1 fusion.22
  31.5 2.3 collective-permute-start.3
  33.8 2.9 fusion.21
  36.8 3.4 copy-done
  40.2 13.8 %shard_map.95 = bf16[512,1024]{1,0:T(8,128)(2,1)S(1)} custom-call(s32[2]{0:T(128)S(1)} %pad_add_fusion.refs_0_, bf16[512,8192]{1,0:T(8,128)(2,1)S(1)} %bitcast.226, bf16[8192,1024]{1,0:T(8,128)(2,1)} %refs_4_.3), custom_call_target="tpu_custom_call" | custom-call | flops 536870912 | bytes 1572864 | tf_op jit(solution)/shard_map/pallas_call | solution.py:146
  53.9 9.5 %collective-permute-done = bf16[1024,512]{1,0:T(8,128)(2,1)S(1)} collective-permute-done((bf16[1024,512]{1,0:T(8,128)(2,1)S(1)}, bf16[1024,512]{1,0:T(8,128)(2,1)S(1)}, u32[]{:S(2)}, u32[]{:S(2)}) %collective-permute-start) | collective-permute-done | bytes 1048608 | tf_op jit(solution)/shard_map/ppermute | solution.py:204
  63.4 2.1 collective-permute-start.2
  65.5 1.5 fusion.20
  67.8 1.6 collective-permute-start.7
  69.4 2.3 constant_dynamic-update-slice_fusion.4
  74.8 33.7 %collective-permute-done.1 = bf16[2048,512]{1,0:T(8,128)(2,1)} collective-permute-done((bf16[2048,512]{1,0:T(8,128)(2,1)}, bf16[2048,512]{1,0:T(8,128)(2,1)}, u32[]{:S(2)}, u32[]{:S(2)}) %collective-permute-start.1) | collective-permute-done | bytes 2097184 | tf_op jit(solution)/shard_map/ppermute | solution.py:204
  108.4 9.5 %collective-permute-start.4 = (bf16[2048,512]{1,0:T(8,128)(2,1)}, bf16[2048,512]{1,0:T(8,128)(2,1)S(1)}, u32[]{:S(2)}, u32[]{:S(2)}) collective-permute-start(bf16[2048,512]{1,0:T(8,128)(2,1)} %get-tuple-element.16), channel_id=1, source_target_pairs={{0,4},{4,0},{8,12},{12,8},{1,5},{5,1},{9,13},{13,9},{2,6},{6,2},{1... | collective-permute-start | bytes 6291464 | tf_op jit(solution)/shard_map/ppermute | solution.py:204
  118.0 1.6 collective-permute-start.8
  119.6 33.8 %collective-permute-done.2 = bf16[2048,512]{1,0:T(8,128)(2,1)} collective-permute-done((bf16[2048,512]{1,0:T(8,128)(2,1)}, bf16[2048,512]{1,0:T(8,128)(2,1)}, u32[]{:S(2)}, u32[]{:S(2)}) %collective-permute-start.2) | collective-permute-done | bytes 2097184 | tf_op jit(solution)/shard_map/ppermute | solution.py:204
  154.3 2.1 collective-permute-start.9
  156.4 8.0 %collective-permute-start.6 = (bf16[1024,512]{1,0:T(8,128)(2,1)}, bf16[1024,512]{1,0:T(8,128)(2,1)S(1)}, u32[]{:S(2)}, u32[]{:S(2)}) collective-permute-start(bf16[1024,512]{1,0:T(8,128)(2,1)} %get-tuple-element.18), channel_id=1, source_target_pairs={{0,4},{4,0},{8,12},{12,8},{1,5},{5,1},{9,13},{13,9},{2,6},{6,2},{1... | collective-permute-start | bytes 3145736 | tf_op jit(solution)/shard_map/ppermute | solution.py:204
  164.5 33.8 %collective-permute-done.4 = bf16[2048,512]{1,0:T(8,128)(2,1)S(1)} collective-permute-done((bf16[2048,512]{1,0:T(8,128)(2,1)}, bf16[2048,512]{1,0:T(8,128)(2,1)S(1)}, u32[]{:S(2)}, u32[]{:S(2)}) %collective-permute-start.4) | collective-permute-done | bytes 2097184 | tf_op jit(solution)/shard_map/ppermute | solution.py:204
  198.2 2.0 collective-permute-start.10
  200.3 2.5 constant_dynamic-update-slice_fusion.9
  202.7 3.1 constant_dynamic-update-slice_fusion.3
  205.8 5.5 %collective-permute-start.12 = (bf16[64,8192]{1,0:T(8,128)(2,1)S(1)}, bf16[64,8192]{1,0:T(8,128)(2,1)S(1)}, u32[]{:S(2)}, u32[]{:S(2)}) collective-permute-start(bf16[64,8192]{1,0:T(8,128)(2,1)S(1)} %copy-done.14), channel_id=1, source_target_pairs={{0,12},{12,0},{1,13},{13,1},{2,14},{14,2},{3,15},{15,3},{16,28},{2... | collective-permute-start | bytes 3145736 | tf_op jit(solution)/shard_map/ppermute | solution.py:214
  211.3 3.1 constant_dynamic-update-slice_fusion.2
  214.4 5.9 %collective-permute-done.6 = bf16[1024,512]{1,0:T(8,128)(2,1)S(1)} collective-permute-done((bf16[1024,512]{1,0:T(8,128)(2,1)}, bf16[1024,512]{1,0:T(8,128)(2,1)S(1)}, u32[]{:S(2)}, u32[]{:S(2)}) %collective-permute-start.6) | collective-permute-done | bytes 1048608 | tf_op jit(solution)/shard_map/ppermute | solution.py:204
  220.4 1.5 collective-permute-start.11
  221.9 1.5 constant_dynamic-update-slice_fusion.8
  223.4 72.7 %collective-permute-start.17 = (bf16[128,8192]{1,0:T(8,128)(2,1)}, bf16[128,8192]{1,0:T(8,128)(2,1)}, u32[]{:S(2)}, u32[]{:S(2)}) collective-permute-start(bf16[128,8192]{1,0:T(8,128)(2,1)} %get-tuple-element.21), channel_id=1, source_target_pairs={{0,12},{12,0},{1,13},{13,1},{2,14},{14,2},{3,15},{15,3},{16,28},{2... | collective-permute-start | bytes 6291464 | tf_op jit(solution)/shard_map/ppermute | solution.py:214
  296.1 1.5 constant_dynamic-update-slice_fusion.1
  298.7 1.4 constant_dynamic-update-slice_fusion.7
  300.2 2.3 collective-permute-start.23
  302.6 1.4 constant_dynamic-update-slice_fusion.6
  305.1 14.1 %shard_map.96 = bf16[512,1024]{1,0:T(8,128)(2,1)S(1)} custom-call(s32[2]{0:T(128)S(1)} %pad_add_fusion.refs_0_, bf16[512,8192]{1,0:T(8,128)(2,1)S(1)} %bitcast.230, bf16[8192,512]{1,0:T(8,128)(2,1)} %constant_dynamic-update-slice_fusion.refs_2_.refs_5_.refs_4_, bf16[8192,512]{1,0:T(8,128)(2,1)} %constant_dynamic-update-slice_fusion.5.refs_3_.refs_6_.refs_5_), custom_call_target="tpu_custom_call" | custom-call | flops 536870912 | bytes 1572864 | tf_op jit(solution)/shard_map/pallas_call | solution.py:146
  319.7 1.6 collective-permute-start.15
  322.0 5.8 %collective-permute-start.28 = (bf16[128,8192]{1,0:T(8,128)(2,1)}, bf16[128,8192]{1,0:T(8,128)(2,1)}, u32[]{:S(2)}, u32[]{:S(2)}) collective-permute-start(bf16[128,8192]{1,0:T(8,128)(2,1)} %get-tuple-element.24), channel_id=1, source_target_pairs={{0,12},{12,0},{1,13},{13,1},{2,14},{14,2},{3,15},{15,3},{16,28},{2... | collective-permute-start | bytes 6291464 | tf_op jit(solution)/shard_map/ppermute | solution.py:214
  327.8 5.8 %collective-permute-done.15 = bf16[128,2048]{1,0:T(8,128)(2,1)S(1)} collective-permute-done((bf16[128,2048]{1,0:T(8,128)(2,1)S(1)}, bf16[128,2048]{1,0:T(8,128)(2,1)S(1)}, u32[]{:S(2)}, u32[]{:S(2)}) %collective-permute-start.15) | collective-permute-done | bytes 524320 | tf_op jit(solution)/shard_map/ppermute | solution.py:227
  333.6 11.7 %collective-permute-done.14 = bf16[128,2048]{1,0:T(8,128)(2,1)S(1)} collective-permute-done((bf16[128,2048]{1,0:T(8,128)(2,1)S(1)}, bf16[128,2048]{1,0:T(8,128)(2,1)S(1)}, u32[]{:S(2)}, u32[]{:S(2)}) %collective-permute-start.14) | collective-permute-done | bytes 524320 | tf_op jit(solution)/shard_map/ppermute | solution.py:227
  345.7 11.5 %collective-permute-done.23.refs_1_ = bf16[128,8192]{1,0:T(8,128)(2,1)S(1)} collective-permute-done((bf16[128,8192]{1,0:T(8,128)(2,1)S(1)}, bf16[128,8192]{1,0:T(8,128)(2,1)S(1)}, u32[]{:S(2)}, u32[]{:S(2)}) %collective-permute-start.23) | collective-permute-done | bytes 2097184 | tf_op jit(solution)/shard_map/ppermute | solution.py:214
  358.5 1.6 copy-done.6
  360.1 12.5 %shard_map.98 = bf16[128,2048]{1,0:T(8,128)(2,1)S(1)} custom-call(s32[2]{0:T(128)S(1)} %pad_add_fusion.refs_0_, bf16[128,8192]{1,0:T(8,128)(2,1)S(1)} %copy-done.6, bf16[128,8192]{1,0:T(8,128)(2,1)S(1)} %copy-done.4, bf16[8192,1024]{1,0:T(8,128)(2,1)} %refs_4_.3, bf16[8192,512]{1,0:T(8,128)(2,1)S(1)} %bitcast.221, ...), custom_call_target="tpu_custom_call" | custom-call | flops 268435456 | bytes 2228224 | tf_op jit(solution)/shard_map/pallas_call | solution.py:146
  373.4 1.6 collective-permute-start.26
  375.5 16.1 %shard_map.97 = bf16[192,2048]{1,0:T(8,128)(2,1)S(1)} custom-call(s32[2]{0:T(128)S(1)} %pad_add_fusion.refs_0_, bf16[64,8192]{1,0:T(8,128)(2,1)S(1)} %copy-done.10, bf16[128,8192]{1,0:T(8,128)(2,1)} %collective-permute-done.17.refs_2_, bf16[192,8192]{1,0:T(8,128)(2,1)} %collective-permute-done.3.refs_3_, bf16[8192,1024]{1,0:T(8,128)(2,1)} %refs_4_.3, ...), custom_call_target="tpu_custom_call" | custom-call | flops 402653184 | bytes 2293760 | tf_op jit(solution)/shard_map/pallas_call | solution.py:146
  391.7 1.7 collective-permute-done.16
  393.3 5.7 %collective-permute-start.29 = (bf16[64,8192]{1,0:T(8,128)(2,1)}, bf16[64,8192]{1,0:T(8,128)(2,1)S(1)}, u32[]{:S(2)}, u32[]{:S(2)}) collective-permute-start(bf16[64,8192]{1,0:T(8,128)(2,1)} %get-tuple-element.25), channel_id=1, source_target_pairs={{0,12},{12,0},{1,13},{13,1},{2,14},{14,2},{3,15},{15,3},{16,28},{2... | collective-permute-start | bytes 3145736 | tf_op jit(solution)/shard_map/ppermute | solution.py:214
  401.3 1.6 collective-permute-start.20
  402.9 21.1 %collective-permute-done.27 = bf16[32,1024]{1,0:T(8,128)(2,1)S(1)} collective-permute-done((bf16[32,1024]{1,0:T(8,128)(2,1)S(1)}, bf16[32,1024]{1,0:T(8,128)(2,1)S(1)}, u32[]{:S(2)}, u32[]{:S(2)}) %collective-permute-start.27) | collective-permute-done | bytes 65568 | tf_op jit(solution)/shard_map/ppermute | solution.py:229
  424.0 1.5 collective-permute-start.19
  425.5 1.9 copy-done.2
  427.4 15.4 %shard_map.99 = bf16[192,2048]{1,0:T(8,128)(2,1)S(1)} custom-call(s32[2]{0:T(128)S(1)} %pad_add_fusion.refs_0_, bf16[128,8192]{1,0:T(8,128)(2,1)} %collective-permute-done.28.refs_1_, bf16[64,8192]{1,0:T(8,128)(2,1)S(1)} %collective-permute-done.29.refs_2_, bf16[192,8192]{1,0:T(8,128)(2,1)S(1)} %copy-done.2, bf16[8192,1024]{1,0:T(8,128)(2,1)} %refs_4_.3, ...), custom_call_target="tpu_custom_call" | custom-call | flops 402653184 | bytes 2293760 | tf_op jit(solution)/shard_map/pallas_call | solution.py:146
  443.6 1.5 collective-permute-start.31
  445.1 13.0 %all-gather.2 = bf16[8,32,1024]{2,1,0:T(8,128)(2,1)S(1)} all-gather(bf16[2,32,1024]{2,1,0:T(8,128)(2,1)S(1)} %pad_maximum_fusion.5), channel_id=4, replica_groups=mesh['groups'=2,'row'=4,'col'=4] {'col'}, dimensions={0}, use_global_device_ids=true | all-gather | bytes 655360 | tf_op jit(solution)/shard_map/all_gather | solution.py:238
  458.4 1.8 collective-permute-start.33
  460.6 3.5 collective-permute-done.33
  464.1 1.5 collective-permute-done.21
  465.6 7.9 %all-gather.1 = bf16[8,48,1024]{2,1,0:T(8,128)(2,1)S(1)} all-gather(bf16[2,48,1024]{2,1,0:T(8,128)(2,1)S(1)} %pad_maximum_fusion.3), channel_id=3, replica_groups=mesh['groups'=2,'row'=4,'col'=4] {'col'}, dimensions={0}, use_global_device_ids=true | all-gather | bytes 983040 | tf_op jit(solution)/shard_map/all_gather | solution.py:238
  473.5 8.7 %all-gather.3 = bf16[8,48,1024]{2,1,0:T(8,128)(2,1)S(1)} all-gather(bf16[2,48,1024]{2,1,0:T(8,128)(2,1)S(1)} %pad_maximum_fusion.4), channel_id=5, replica_groups=mesh['groups'=2,'row'=4,'col'=4] {'col'}, dimensions={0}, use_global_device_ids=true | all-gather | bytes 983040 | tf_op jit(solution)/shard_map/all_gather | solution.py:238
  482.3 1.6 copy-done.7
  483.9 1.6 copy-done.8
  486.7 4.4 shard_map.100
  494.2 1.8 collective-permute-done.35
  496.0 3.6 collective-permute-start.39
  501.5 2.6 collective-permute-done.38
  (148 shorter events, 23.0 us)
Async XLA Ops:
  8.0 63.7 %all-gather.10.cloned.1.call-start = ((), (), s32[]{:S(2)}) async-start(), calls=%async_computation.1 | async-start | bytes 1310720 | tf_op jit(solution)/shard_map/all_gather | solution.py:187
  16.7 465.6 %all-gather.8.cloned.1.call-start = ((), (), s32[]{:S(2)}) async-start(), calls=%async_computation | async-start | bytes 2621440 | tf_op jit(solution)/shard_map/all_gather | solution.py:238
  16.7 11.7 %slice-start.2 = ((s8[8388608]{0:T(1024)(128)(4,1)}), s8[4194304]{0:T(1024)(128)(4,1)S(1)}, s32[]{:S(2)}) async-start(s8[8388608]{0:T(1024)(128)(4,1)} %bitcast.222), calls=%async_computation.4 | async-start | bytes 8388608
  19.5 8.9 %slice-start.3 = ((s8[8388608]{0:T(1024)(128)(4,1)}), s8[4194304]{0:T(1024)(128)(4,1)S(1)}, s32[]{:S(2)}) async-start(s8[8388608]{0:T(1024)(128)(4,1)} %bitcast.222), calls=%async_computation.5 | async-start | bytes 8388608
  19.5 43.9 %collective-permute-start = (bf16[1024,512]{1,0:T(8,128)(2,1)S(1)}, bf16[1024,512]{1,0:T(8,128)(2,1)S(1)}, u32[]{:S(2)}, u32[]{:S(2)}) collective-permute-start(bf16[1024,512]{1,0:T(8,128)(2,1)S(1)} %get-tuple-element.29), channel_id=1, source_target_pairs={{0,4},{4,0},{8,12},{12,8},{1,5},{5,1},{9,13},{13,9},{2,6},{6,2},{1... | collective-permute-start | bytes 3145736 | tf_op jit(solution)/shard_map/ppermute | solution.py:204
  28.2 80.2 %collective-permute-start.1 = (bf16[2048,512]{1,0:T(8,128)(2,1)}, bf16[2048,512]{1,0:T(8,128)(2,1)}, u32[]{:S(2)}, u32[]{:S(2)}) collective-permute-start(bf16[2048,512]{1,0:T(8,128)(2,1)} %get-tuple-element.32), channel_id=1, source_target_pairs={{0,4},{4,0},{8,12},{12,8},{1,5},{5,1},{9,13},{13,9},{2,6},{6,2},{1... | collective-permute-start | bytes 6291464 | tf_op jit(solution)/shard_map/ppermute | solution.py:204
  31.5 76.9 %collective-permute-start.3 = (bf16[192,8192]{1,0:T(8,128)(2,1)}, bf16[192,8192]{1,0:T(8,128)(2,1)}, u32[]{:S(2)}, u32[]{:S(2)}) collective-permute-start(bf16[192,8192]{1,0:T(8,128)(2,1)} %get-tuple-element.39), channel_id=1, source_target_pairs={{4,8},{8,4},{5,9},{9,5},{6,10},{10,6},{7,11},{11,7},{20,24},{24,20... | collective-permute-start | bytes 9437192 | tf_op jit(solution)/shard_map/ppermute | solution.py:203
  36.8 3.4 copy-start
  63.4 3.6 copy-start.13
  63.4 90.0 %collective-permute-start.2 = (bf16[2048,512]{1,0:T(8,128)(2,1)}, bf16[2048,512]{1,0:T(8,128)(2,1)}, u32[]{:S(2)}, u32[]{:S(2)}) collective-permute-start(bf16[2048,512]{1,0:T(8,128)(2,1)} %get-tuple-element.15), channel_id=1, source_target_pairs={{0,4},{4,0},{8,12},{12,8},{1,5},{5,1},{9,13},{13,9},{2,6},{6,2},{1... | collective-permute-start | bytes 6291464 | tf_op jit(solution)/shard_map/ppermute | solution.py:204
  67.0 87.3 %collective-permute-start.5 = (bf16[128,8192]{1,0:T(8,128)(2,1)}, bf16[128,8192]{1,0:T(8,128)(2,1)S(1)}, u32[]{:S(2)}, u32[]{:S(2)}) collective-permute-start(bf16[128,8192]{1,0:T(8,128)(2,1)} %get-tuple-element.23), channel_id=1, source_target_pairs={{4,8},{8,4},{5,9},{9,5},{6,10},{10,6},{7,11},{11,7},{20,24},{24,20... | collective-permute-start | bytes 6291464 | tf_op jit(solution)/shard_map/ppermute | solution.py:203
  67.8 88.6 %collective-permute-start.7 = (bf16[1024,512]{1,0:T(8,128)(2,1)}, bf16[1024,512]{1,0:T(8,128)(2,1)}, u32[]{:S(2)}, u32[]{:S(2)}) collective-permute-start(bf16[1024,512]{1,0:T(8,128)(2,1)} %copy-done.13), channel_id=1, source_target_pairs={{0,16},{16,0},{1,17},{17,1},{2,18},{18,2},{3,19},{19,3},{4,20},{20... | collective-permute-start | bytes 3145736 | tf_op jit(solution)/shard_map/ppermute | solution.py:205
  73.7 132.1 %copy-start.14 = (bf16[64,8192]{1,0:T(8,128)(2,1)S(1)}, bf16[64,8192]{1,0:T(8,128)(2,1)}, u32[]{:S(2)}) copy-start(bf16[64,8192]{1,0:T(8,128)(2,1)} %get-tuple-element.19) | copy-start | bytes 3145732
  108.4 89.8 %collective-permute-start.4 = (bf16[2048,512]{1,0:T(8,128)(2,1)}, bf16[2048,512]{1,0:T(8,128)(2,1)S(1)}, u32[]{:S(2)}, u32[]{:S(2)}) collective-permute-start(bf16[2048,512]{1,0:T(8,128)(2,1)} %get-tuple-element.16), channel_id=1, source_target_pairs={{0,4},{4,0},{8,12},{12,8},{1,5},{5,1},{9,13},{13,9},{2,6},{6,2},{1... | collective-permute-start | bytes 6291464 | tf_op jit(solution)/shard_map/ppermute | solution.py:204
  118.0 87.8 %collective-permute-start.8 = (bf16[2048,512]{1,0:T(8,128)(2,1)}, bf16[2048,512]{1,0:T(8,128)(2,1)S(1)}, u32[]{:S(2)}, u32[]{:S(2)}) collective-permute-start(bf16[2048,512]{1,0:T(8,128)(2,1)} %collective-permute-done.1), channel_id=1, source_target_pairs={{0,16},{16,0},{1,17},{17,1},{2,18},{18,2},{3,19},{19,3},{4,20},{20... | collective-permute-start | bytes 6291464 | tf_op jit(solution)/shard_map/ppermute | solution.py:205
  153.4 146.8 %collective-permute-start.22 = (bf16[192,8192]{1,0:T(8,128)(2,1)}, bf16[192,8192]{1,0:T(8,128)(2,1)S(1)}, u32[]{:S(2)}, u32[]{:S(2)}) collective-permute-start(bf16[192,8192]{1,0:T(8,128)(2,1)} %get-tuple-element.22), channel_id=1, source_target_pairs={{4,8},{8,4},{5,9},{9,5},{6,10},{10,6},{7,11},{11,7},{20,24},{24,20... | collective-permute-start | bytes 9437192 | tf_op jit(solution)/shard_map/ppermute | solution.py:203
  154.3 60.1 %copy-start.3 = (bf16[128,8192]{1,0:T(8,128)(2,1)}, bf16[128,8192]{1,0:T(8,128)(2,1)S(1)}, u32[]{:S(2)}) copy-start(bf16[128,8192]{1,0:T(8,128)(2,1)S(1)} %collective-permute-done.5.refs_2_) | copy-start | bytes 6291460
  154.3 69.1 %collective-permute-start.9 = (bf16[2048,512]{1,0:T(8,128)(2,1)}, bf16[2048,512]{1,0:T(8,128)(2,1)S(1)}, u32[]{:S(2)}, u32[]{:S(2)}) collective-permute-start(bf16[2048,512]{1,0:T(8,128)(2,1)} %collective-permute-done.2), channel_id=1, source_target_pairs={{0,16},{16,0},{1,17},{17,1},{2,18},{18,2},{3,19},{19,3},{4,20},{20... | collective-permute-start | bytes 6291464 | tf_op jit(solution)/shard_map/ppermute | solution.py:205
  156.4 58.0 %copy-start.17 = (bf16[512,256]{1,0:T(8,128)(2,1)}, bf16[512,256]{1,0:T(8,128)(2,1)S(1)}, u32[]{:S(2)}) copy-start(bf16[512,256]{1,0:T(8,128)(2,1)S(1)} %get-tuple-element.67) | copy-start | bytes 786436
  156.4 64.0 %collective-permute-start.6 = (bf16[1024,512]{1,0:T(8,128)(2,1)}, bf16[1024,512]{1,0:T(8,128)(2,1)S(1)}, u32[]{:S(2)}, u32[]{:S(2)}) collective-permute-start(bf16[1024,512]{1,0:T(8,128)(2,1)} %get-tuple-element.18), channel_id=1, source_target_pairs={{0,4},{4,0},{8,12},{12,8},{1,5},{5,1},{9,13},{13,9},{2,6},{6,2},{1... | collective-permute-start | bytes 3145736 | tf_op jit(solution)/shard_map/ppermute | solution.py:204
  198.2 104.3 %collective-permute-start.10 = (bf16[2048,512]{1,0:T(8,128)(2,1)S(1)}, bf16[2048,512]{1,0:T(8,128)(2,1)S(1)}, u32[]{:S(2)}, u32[]{:S(2)}) collective-permute-start(bf16[2048,512]{1,0:T(8,128)(2,1)S(1)} %collective-permute-done.4), channel_id=1, source_target_pairs={{0,16},{16,0},{1,17},{17,1},{2,18},{18,2},{3,19},{19,3},{4,20},{20... | collective-permute-start | bytes 6291464 | tf_op jit(solution)/shard_map/ppermute | solution.py:205
  200.2 14.2 %copy-start.15 = (bf16[512,256]{1,0:T(8,128)(2,1)}, bf16[512,256]{1,0:T(8,128)(2,1)S(1)}, u32[]{:S(2)}) copy-start(bf16[512,256]{1,0:T(8,128)(2,1)S(1)} %get-tuple-element.80) | copy-start | bytes 786436
  200.3 14.2 %copy-start.19 = (bf16[512,256]{1,0:T(8,128)(2,1)}, bf16[512,256]{1,0:T(8,128)(2,1)S(1)}, u32[]{:S(2)}) copy-start(bf16[512,256]{1,0:T(8,128)(2,1)S(1)} %get-tuple-element.81) | copy-start | bytes 786436
  205.8 94.4 %collective-permute-start.12 = (bf16[64,8192]{1,0:T(8,128)(2,1)S(1)}, bf16[64,8192]{1,0:T(8,128)(2,1)S(1)}, u32[]{:S(2)}, u32[]{:S(2)}) collective-permute-start(bf16[64,8192]{1,0:T(8,128)(2,1)S(1)} %copy-done.14), channel_id=1, source_target_pairs={{0,12},{12,0},{1,13},{13,1},{2,14},{14,2},{3,15},{15,3},{16,28},{2... | collective-permute-start | bytes 3145736 | tf_op jit(solution)/shard_map/ppermute | solution.py:214
  220.4 83.6 %collective-permute-start.11 = (bf16[1024,512]{1,0:T(8,128)(2,1)S(1)}, bf16[1024,512]{1,0:T(8,128)(2,1)S(1)}, u32[]{:S(2)}, u32[]{:S(2)}) collective-permute-start(bf16[1024,512]{1,0:T(8,128)(2,1)S(1)} %collective-permute-done.6), channel_id=1, source_target_pairs={{0,16},{16,0},{1,17},{17,1},{2,18},{18,2},{3,19},{19,3},{4,20},{20... | collective-permute-start | bytes 3145736 | tf_op jit(solution)/shard_map/ppermute | solution.py:205
  223.4 76.8 %copy-start.12 = (bf16[128,8192]{1,0:T(8,128)(2,1)S(1)}, bf16[128,8192]{1,0:T(8,128)(2,1)}, u32[]{:S(2)}) copy-start(bf16[128,8192]{1,0:T(8,128)(2,1)} %get-tuple-element.23) | copy-start | bytes 6291460
  223.4 98.6 %collective-permute-start.17 = (bf16[128,8192]{1,0:T(8,128)(2,1)}, bf16[128,8192]{1,0:T(8,128)(2,1)}, u32[]{:S(2)}, u32[]{:S(2)}) collective-permute-start(bf16[128,8192]{1,0:T(8,128)(2,1)} %get-tuple-element.21), channel_id=1, source_target_pairs={{0,12},{12,0},{1,13},{13,1},{2,14},{14,2},{3,15},{15,3},{16,28},{2... | collective-permute-start | bytes 6291464 | tf_op jit(solution)/shard_map/ppermute | solution.py:214
  296.1 8.9 %slice-start.4 = ((s8[8388608]{0:T(1024)(128)(4,1)}), s8[4194304]{0:T(1024)(128)(4,1)S(1)}, s32[]{:S(2)}) async-start(s8[8388608]{0:T(1024)(128)(4,1)} %bitcast.228), calls=%async_computation.6 | async-start | bytes 8388608
  298.7 6.3 %slice-start.5 = ((s8[8388608]{0:T(1024)(128)(4,1)}), s8[4194304]{0:T(1024)(128)(4,1)S(1)}, s32[]{:S(2)}) async-start(s8[8388608]{0:T(1024)(128)(4,1)} %bitcast.228), calls=%async_computation.7 | async-start | bytes 8388608
  300.2 3.8 copy-start.1
  300.2 19.0 %copy-start.9 = (bf16[64,8192]{1,0:T(8,128)(2,1)}, bf16[64,8192]{1,0:T(8,128)(2,1)S(1)}, u32[]{:S(2)}) copy-start(bf16[64,8192]{1,0:T(8,128)(2,1)S(1)} %collective-permute-done.12.refs_1_) | copy-start | bytes 3145732
  300.2 56.9 %collective-permute-start.23 = (bf16[128,8192]{1,0:T(8,128)(2,1)S(1)}, bf16[128,8192]{1,0:T(8,128)(2,1)S(1)}, u32[]{:S(2)}, u32[]{:S(2)}) collective-permute-start(bf16[128,8192]{1,0:T(8,128)(2,1)S(1)} %copy-done.12), channel_id=1, source_target_pairs={{0,12},{12,0},{1,13},{13,1},{2,14},{14,2},{3,15},{15,3},{16,28},{2... | collective-permute-start | bytes 6291464 | tf_op jit(solution)/shard_map/ppermute | solution.py:214
  304.0 54.5 %slice-start = ((s8[8388608]{0:T(1024)(128)(4,1)}), s8[4194304]{0:T(1024)(128)(4,1)S(1)}, s32[]{:S(2)}) async-start(s8[8388608]{0:T(1024)(128)(4,1)} %bitcast.220), calls=%async_computation.2 | async-start | bytes 8388608
  305.1 53.5 %slice-start.1 = ((s8[8388608]{0:T(1024)(128)(4,1)}), s8[4194304]{0:T(1024)(128)(4,1)S(1)}, s32[]{:S(2)}) async-start(s8[8388608]{0:T(1024)(128)(4,1)} %bitcast.220), calls=%async_computation.3 | async-start | bytes 8388608
  319.2 2.6 copy-start.16
  319.2 2.6 copy-start.18
  319.2 2.6 copy-start.20
  319.4 39.1 %copy-start.4 = (bf16[128,8192]{1,0:T(8,128)(2,1)S(1)}, bf16[128,8192]{1,0:T(8,128)(2,1)}, u32[]{:S(2)}) copy-start(bf16[128,8192]{1,0:T(8,128)(2,1)} %copy-done.3) | copy-start | bytes 6291460
  319.6 8.2 %collective-permute-start.13 = (bf16[128,2048]{1,0:T(8,128)(2,1)S(1)}, bf16[128,2048]{1,0:T(8,128)(2,1)S(1)}, u32[]{:S(2)}, u32[]{:S(2)}) collective-permute-start(bf16[128,2048]{1,0:T(8,128)(2,1)S(1)} %get-tuple-element.40), channel_id=1, source_target_pairs={{0,1},{1,0},{2,3},{3,2},{4,5},{5,4},{6,7},{7,6},{8,9},{9,8},{10,11... | collective-permute-start | bytes 1572872 | tf_op jit(solution)/shard_map/ppermute | solution.py:227
  319.7 13.9 %collective-permute-start.15 = (bf16[128,2048]{1,0:T(8,128)(2,1)S(1)}, bf16[128,2048]{1,0:T(8,128)(2,1)S(1)}, u32[]{:S(2)}, u32[]{:S(2)}) collective-permute-start(bf16[128,2048]{1,0:T(8,128)(2,1)S(1)} %get-tuple-element.41), channel_id=1, source_target_pairs={{0,3},{1,2},{2,1},{3,0},{4,7},{5,6},{6,5},{7,4},{8,11},{9,10},{10,... | collective-permute-start | bytes 1572872 | tf_op jit(solution)/shard_map/ppermute | solution.py:227
  321.3 23.9 %collective-permute-start.14 = (bf16[128,2048]{1,0:T(8,128)(2,1)S(1)}, bf16[128,2048]{1,0:T(8,128)(2,1)S(1)}, u32[]{:S(2)}, u32[]{:S(2)}) collective-permute-start(bf16[128,2048]{1,0:T(8,128)(2,1)S(1)} %get-tuple-element.42), channel_id=1, source_target_pairs={{0,2},{1,3},{2,0},{3,1},{4,6},{5,7},{6,4},{7,5},{8,10},{9,11},{10,... | collective-permute-start | bytes 1572872 | tf_op jit(solution)/shard_map/ppermute | solution.py:227
  322.0 103.5 %collective-permute-start.28 = (bf16[128,8192]{1,0:T(8,128)(2,1)}, bf16[128,8192]{1,0:T(8,128)(2,1)}, u32[]{:S(2)}, u32[]{:S(2)}) collective-permute-start(bf16[128,8192]{1,0:T(8,128)(2,1)} %get-tuple-element.24), channel_id=1, source_target_pairs={{0,12},{12,0},{1,13},{13,1},{2,14},{14,2},{3,15},{15,3},{16,28},{2... | collective-permute-start | bytes 6291464 | tf_op jit(solution)/shard_map/ppermute | solution.py:214
  345.6 47.7 %collective-permute-start.16 = (bf16[128,1024]{1,0:T(8,128)(2,1)S(1)}, bf16[128,1024]{1,0:T(8,128)(2,1)S(1)}, u32[]{:S(2)}, u32[]{:S(2)}) collective-permute-start(bf16[128,1024]{1,0:T(8,128)(2,1)S(1)} %get-tuple-element.63), channel_id=1, source_target_pairs={{0,4},{4,0},{8,12},{12,8},{1,5},{5,1},{9,13},{13,9},{2,6},{6,2},{1... | collective-permute-start | bytes 786440 | tf_op jit(solution)/shard_map/ppermute | solution.py:229
  360.1 15.4 %copy-start.10 = (bf16[64,8192]{1,0:T(8,128)(2,1)S(1)}, bf16[64,8192]{1,0:T(8,128)(2,1)}, u32[]{:S(2)}) copy-start(bf16[64,8192]{1,0:T(8,128)(2,1)} %copy-done.9) | copy-start | bytes 3145732
  373.4 26.5 %collective-permute-start.24 = (bf16[32,2048]{1,0:T(8,128)(2,1)}, bf16[32,2048]{1,0:T(8,128)(2,1)S(1)}, u32[]{:S(2)}, u32[]{:S(2)}) collective-permute-start(bf16[32,2048]{1,0:T(8,128)(2,1)} %get-tuple-element.59), channel_id=1, source_target_pairs={{0,1},{1,0},{2,3},{3,2},{4,5},{5,4},{6,7},{7,6},{8,9},{9,8},{10,11... | collective-permute-start | bytes 393224 | tf_op jit(solution)/shard_map/ppermute | solution.py:227
  373.4 26.5 %collective-permute-start.26 = (bf16[32,2048]{1,0:T(8,128)(2,1)}, bf16[32,2048]{1,0:T(8,128)(2,1)}, u32[]{:S(2)}, u32[]{:S(2)}) collective-permute-start(bf16[32,2048]{1,0:T(8,128)(2,1)} %get-tuple-element.60), channel_id=1, source_target_pairs={{0,3},{1,2},{2,1},{3,0},{4,7},{5,6},{6,5},{7,4},{8,11},{9,10},{10,... | collective-permute-start | bytes 393224 | tf_op jit(solution)/shard_map/ppermute | solution.py:227
  375.0 24.9 %collective-permute-start.25 = (bf16[32,2048]{1,0:T(8,128)(2,1)}, bf16[32,2048]{1,0:T(8,128)(2,1)}, u32[]{:S(2)}, u32[]{:S(2)}) collective-permute-start(bf16[32,2048]{1,0:T(8,128)(2,1)} %get-tuple-element.61), channel_id=1, source_target_pairs={{0,2},{1,3},{2,0},{3,1},{4,6},{5,7},{6,4},{7,5},{8,10},{9,11},{10,... | collective-permute-start | bytes 393224 | tf_op jit(solution)/shard_map/ppermute | solution.py:227
  393.3 32.2 %collective-permute-start.29 = (bf16[64,8192]{1,0:T(8,128)(2,1)}, bf16[64,8192]{1,0:T(8,128)(2,1)S(1)}, u32[]{:S(2)}, u32[]{:S(2)}) collective-permute-start(bf16[64,8192]{1,0:T(8,128)(2,1)} %get-tuple-element.25), channel_id=1, source_target_pairs={{0,12},{12,0},{1,13},{13,1},{2,14},{14,2},{3,15},{15,3},{16,28},{2... | collective-permute-start | bytes 3145736 | tf_op jit(solution)/shard_map/ppermute | solution.py:214
  401.0 23.0 %collective-permute-start.27 = (bf16[32,1024]{1,0:T(8,128)(2,1)S(1)}, bf16[32,1024]{1,0:T(8,128)(2,1)S(1)}, u32[]{:S(2)}, u32[]{:S(2)}) collective-permute-start(bf16[32,1024]{1,0:T(8,128)(2,1)S(1)} %get-tuple-element.89), channel_id=1, source_target_pairs={{0,4},{4,0},{8,12},{12,8},{1,5},{5,1},{9,13},{13,9},{2,6},{6,2},{1... | collective-permute-start | bytes 196616 | tf_op jit(solution)/shard_map/ppermute | solution.py:229
  401.2 42.4 %collective-permute-start.18 = (bf16[48,2048]{1,0:T(8,128)(2,1)S(1)}, bf16[48,2048]{1,0:T(8,128)(2,1)S(1)}, u32[]{:S(2)}, u32[]{:S(2)}) collective-permute-start(bf16[48,2048]{1,0:T(8,128)(2,1)S(1)} %get-tuple-element.56), channel_id=1, source_target_pairs={{0,1},{1,0},{2,3},{3,2},{4,5},{5,4},{6,7},{7,6},{8,9},{9,8},{10,11... | collective-permute-start | bytes 589832 | tf_op jit(solution)/shard_map/ppermute | solution.py:227
  401.3 56.9 %collective-permute-start.20 = (bf16[48,2048]{1,0:T(8,128)(2,1)S(1)}, bf16[48,2048]{1,0:T(8,128)(2,1)S(1)}, u32[]{:S(2)}, u32[]{:S(2)}) collective-permute-start(bf16[48,2048]{1,0:T(8,128)(2,1)S(1)} %get-tuple-element.57), channel_id=1, source_target_pairs={{0,3},{1,2},{2,1},{3,0},{4,7},{5,6},{6,5},{7,4},{8,11},{9,10},{10,... | collective-permute-start | bytes 589832 | tf_op jit(solution)/shard_map/ppermute | solution.py:227
  424.0 34.1 %collective-permute-start.19 = (bf16[48,2048]{1,0:T(8,128)(2,1)S(1)}, bf16[48,2048]{1,0:T(8,128)(2,1)S(1)}, u32[]{:S(2)}, u32[]{:S(2)}) collective-permute-start(bf16[48,2048]{1,0:T(8,128)(2,1)S(1)} %get-tuple-element.58), channel_id=1, source_target_pairs={{0,2},{1,3},{2,0},{3,1},{4,6},{5,7},{6,4},{7,5},{8,10},{9,11},{10,... | collective-permute-start | bytes 589832 | tf_op jit(solution)/shard_map/ppermute | solution.py:227
  425.5 1.9 copy-start.2
  442.9 15.2 %collective-permute-start.30 = (bf16[48,2048]{1,0:T(8,128)(2,1)S(1)}, bf16[48,2048]{1,0:T(8,128)(2,1)S(1)}, u32[]{:S(2)}, u32[]{:S(2)}) collective-permute-start(bf16[48,2048]{1,0:T(8,128)(2,1)S(1)} %get-tuple-element.53), channel_id=1, source_target_pairs={{0,1},{1,0},{2,3},{3,2},{4,5},{5,4},{6,7},{7,6},{8,9},{9,8},{10,11... | collective-permute-start | bytes 589832 | tf_op jit(solution)/shard_map/ppermute | solution.py:227
  443.0 15.2 %collective-permute-start.32 = (bf16[48,2048]{1,0:T(8,128)(2,1)S(1)}, bf16[48,2048]{1,0:T(8,128)(2,1)S(1)}, u32[]{:S(2)}, u32[]{:S(2)}) collective-permute-start(bf16[48,2048]{1,0:T(8,128)(2,1)S(1)} %get-tuple-element.54), channel_id=1, source_target_pairs={{0,3},{1,2},{2,1},{3,0},{4,7},{5,6},{6,5},{7,4},{8,11},{9,10},{10,... | collective-permute-start | bytes 589832 | tf_op jit(solution)/shard_map/ppermute | solution.py:227
  443.6 14.5 %collective-permute-start.31 = (bf16[48,2048]{1,0:T(8,128)(2,1)S(1)}, bf16[48,2048]{1,0:T(8,128)(2,1)S(1)}, u32[]{:S(2)}, u32[]{:S(2)}) collective-permute-start(bf16[48,2048]{1,0:T(8,128)(2,1)S(1)} %get-tuple-element.55), channel_id=1, source_target_pairs={{0,2},{1,3},{2,0},{3,1},{4,6},{5,7},{6,4},{7,5},{8,10},{9,11},{10,... | collective-permute-start | bytes 589832 | tf_op jit(solution)/shard_map/ppermute | solution.py:227
  458.4 5.7 %collective-permute-start.33 = (bf16[48,1024]{1,0:T(8,128)(2,1)S(1)}, bf16[48,1024]{1,0:T(8,128)(2,1)S(1)}, u32[]{:S(2)}, u32[]{:S(2)}) collective-permute-start(bf16[48,1024]{1,0:T(8,128)(2,1)S(1)} %get-tuple-element.85), channel_id=1, source_target_pairs={{0,4},{4,0},{8,12},{12,8},{1,5},{5,1},{9,13},{13,9},{2,6},{6,2},{1... | collective-permute-start | bytes 294920 | tf_op jit(solution)/shard_map/ppermute | solution.py:229
  460.2 5.4 %collective-permute-start.21 = (bf16[48,1024]{1,0:T(8,128)(2,1)S(1)}, bf16[48,1024]{1,0:T(8,128)(2,1)S(1)}, u32[]{:S(2)}, u32[]{:S(2)}) collective-permute-start(bf16[48,1024]{1,0:T(8,128)(2,1)S(1)} %get-tuple-element.87), channel_id=1, source_target_pairs={{0,4},{4,0},{8,12},{12,8},{1,5},{5,1},{9,13},{13,9},{2,6},{6,2},{1... | collective-permute-start | bytes 294920 | tf_op jit(solution)/shard_map/ppermute | solution.py:229
  491.2 3.0 collective-permute-start.36
  492.4 3.6 collective-permute-start.35
  493.2 2.8 collective-permute-start.34
  496.0 5.4 %collective-permute-start.39 = (f32[4,4]{1,0:T(4,128)S(1)}, f32[4,4]{1,0:T(4,128)S(1)}, u32[]{:S(2)}, u32[]{:S(2)}) collective-permute-start(f32[4,4]{1,0:T(4,128)S(1)} %add_add_fusion.1), channel_id=1, source_target_pairs={{0,12},{4,8},{8,4},{12,0},{1,13},{5,9},{9,5},{13,1},{2,14},{6,10},... | collective-permute-start | bytes 200 | tf_op jit(solution)/shard_map/ppermute | solution.py:171
  499.6 4.5 collective-permute-start.38
  499.6 4.5 collective-permute-start.37
  (5 other events, 7.4 us)
Sparse Core Ops, SparseCore 0:
  16.8 44.6 all-gather.9
Sparse Core Ops, SparseCore 1:
  400.0 21.2 all-gather.7

commit v6 on v5

--- a/solution.py
+++ b/solution.py
@@ -67,7 +67,7 @@
             jax.ShapeDtypeStruct((cands, dirs, width), F32),
             jax.ShapeDtypeStruct((steps, queries * cands, width), F32),
         ],
-        compiler_params=pltpu.CompilerParams(vmem_limit_bytes=32 * 2**20),
+        compiler_params=pltpu.CompilerParams(vmem_limit_bytes=16 * 2**20),
     )(*arrays, act_rot, eigenvalues, query_rotated)
     return rotated, jnp.sum(partial_scores, axis=(0, 2)).reshape(queries, cands)
 
@@ -98,11 +98,10 @@
     flags, refs = refs[0], refs[1:]
     tokens, basis, out, acc = refs[:count], refs[count:-2], refs[-2], refs[-1]
     step = pl.program_id(0)
-    rows = [t[...] for t in tokens]
+    rows = tokens[0][...]
     if count > 1:
-        joined = jnp.concatenate(rows[:-1], axis=0) if count > 2 else rows[0]
-        rows = [jnp.where(flags[0] == 1, joined, rows[-1])]
-    rows = rows[0]
+        inner = [t[...] for t in tokens[1:]]
+        rows = jnp.where(flags[0] == 1, rows, jnp.concatenate(inner, axis=0) if count > 2 else inner[0])
     start, spans = 0, []
     for width in widths:
         spans.append((start, start + width))
@@ -138,7 +137,7 @@
     feats = bases[0].shape[0]
     widths = tuple(x.shape[1] for x in bases)
     block, total = 1024, sum(widths)
-    rows = tokens[-1][2]
+    rows = tokens[0][2]
     specs = []
     for _, start, n in tokens:
         assert start % n == 0
@@ -152,7 +151,7 @@
         out_specs=pl.BlockSpec((rows, total), lambda k: (0, 0)),
         out_shape=jax.ShapeDtypeStruct((rows, total), BF16),
         scratch_shapes=[pltpu.VMEM((rows, total), F32)],
-        compiler_params=pltpu.CompilerParams(vmem_limit_bytes=40 * 2**20),
+        compiler_params=pltpu.CompilerParams(vmem_limit_bytes=18 * 2**20),
         cost_estimate=pl.CostEstimate(
             flops=rows * feats * total // 8,
             bytes_accessed=feats * (total + rows) // 8,
@@ -182,42 +181,42 @@
     at_end = (row == 0) | (row == planes - 1)
     flags = jnp.stack([at_end.astype(jnp.int32), group.astype(jnp.int32)])
 
-    lengths = candidate_lengths(example_ids, token_counts)
-    local_act = local_activations(acts, act_basis, lengths)
-    every_act = lax.all_gather(local_act, "row", axis=0)
-
     half, flat = dirs // sides, grads.reshape(cands * tok, feats)
     units, deep, slab = 8, feats // 8, cands * tok // 8
     near, far, other = [], [], []
     spans = [(0, 1), (1, 3), (3, 5), (5, 7), (7, units)]
-    batches = [(0, 1), (2,), (3, 4)]
-    ranges = [(spans[x[0]][0] * slab, spans[x[-1]][1] * slab) for x in batches]
+    inner = [(0, 1), (1, 4), (4, units)]
     own_own = project(flags, [(flat, 0, cands * tok)], [grad_basis])
     for i, (a, b) in enumerate(spans):
-        piece = lax.dynamic_slice(grad_basis, (a * deep, group * half), ((b - a) * deep, half))
-        if i >= 2:
-            early = [own_own, local_act] if i == 2 else [other[i - 3]]
-            piece = after(piece, near[i - 2], *early)
-        if i < len(ranges):
-            rows = flat[slice(*ranges[i])]
-            other.append(lax.ppermute(after(rows, near[i - 1]) if i else rows, "row", middle))
+        if i < len(inner):
+            tie = [near[0]] if i == 2 else []
+            rows = after(flat, *tie)[inner[i][0] * slab : inner[i][1] * slab]
+            other.append(lax.ppermute(rows, "row", middle))
+        tie = []
+        if i == 2:
+            tie = [near[0], own_own, other[0]]
+        if i == 3:
+            tie = [near[1], local_act, other[1]]
+        if i == 4:
+            tie = [near[2]]
+        piece = lax.dynamic_slice(after(grad_basis, *tie), (a * deep, group * half), ((b - a) * deep, half))
         near.append(lax.ppermute(piece, "row", beside))
         far.append(lax.ppermute(near[i], "groups", [(0, 1), (1, 0)]))
+        if i == 0:
+            lengths = candidate_lengths(example_ids, token_counts)
+            local_act = local_activations(acts, after(act_basis, near[0]), lengths)
+            every_act = lax.all_gather(local_act, "row", axis=0)
     near_basis = jnp.concatenate(near, axis=0)
     far_basis = jnp.concatenate(far, axis=0)
-
-    ties = {0: [near[3], far[1]], 1: [near[3], far[2]], 2: [near[4], other[2]]}
+    own_end = project(flags, [(flat, 0, cands * tok)], [near_basis, far_basis])
+
+    ranges = [(0, 4 * slab), (4 * slab, 6 * slab), (6 * slab, units * slab)]
     partner = []
-    for k, (a, b) in enumerate(spans):
-        tie = ties.get(k, []) + ([partner[k - 2]] if k >= 2 else [])
-        piece = flat[a * slab : b * slab]
-        partner.append(lax.ppermute(after(piece, *tie), "row", ends))
-    own_end = project(flags, [(flat, 0, cands * tok)], [near_basis, after(far_basis, partner[0])])
-    products = []
-    for batch, inner, (first, last) in zip(batches, other, ranges):
-        tokens = [(partner[k], 0, (spans[k][1] - spans[k][0]) * slab) for k in batch]
-        tokens.append((inner, 0, last - first))
-        products.append(project(flags, tokens, [grad_basis, near_basis, far_basis]))
+    for i, (a, b) in enumerate(ranges):
+        tie = [[near[3], far[1], every_act], [near[4], far[2], other[2]], [own_end]][i]
+        if i == 2:
+            tie += partner
+        partner.append(lax.ppermute(after(flat, *tie)[a:b], "row", ends))
 
     def scatter_sum(value):
         value = value.reshape(parts, -1, 2 * dirs)
@@ -232,10 +231,11 @@
         lax.dynamic_index_in_dim(every_act, i, 0, keepdims=False)
         for i in (row, row ^ 1, planes - 1 - row, planes - 1 - (row ^ 1))
     ]
-    arrays, segments, act_order = [], [[] for _ in range(cands)], [[] for _ in range(cands)]
+    sums, arrays, segments, act_order = [], [], [[] for _ in range(cands)], [[] for _ in range(cands)]
 
     def place(value, start, sources):
-        every = lax.all_gather(scatter_sum(value), "col", axis=0)
+        sums.append(scatter_sum(value))
+        every = lax.all_gather(sums[-1], "col", axis=0)
         n = every.shape[2]
         for p in range(parts):
             for j, source in enumerate(sources):
@@ -249,8 +249,16 @@
         arrays.append(every.reshape(parts * 2 * n, dirs))
 
     place(jnp.concatenate([own_own, own_end], axis=1), 0, act[:2])
-    for (first, _), product in zip(ranges, products):
-        place(product, first, act[2:])
+    later = {
+        0: [(other[0], 0, slab), (other[1], 0, 3 * slab)],
+        1: [(other[2], 0, 2 * slab)],
+        2: [(other[2], 2 * slab, 2 * slab)],
+    }
+    for i in (1, 0, 2):
+        a, b = ranges[i]
+        far_later = after(far_basis, arrays[0], *(sums if i == 2 else []))
+        tokens = [(partner[i], 0, b - a)] + later[i]
+        place(project(flags, tokens, [grad_basis, near_basis, far_later]), a, act[2:])
     act_rot = jnp.stack([jnp.concatenate(x, axis=0) for x in act_order])
     layout = tuple(tuple(s) for s in segments)
     rotated, scores = rotate_and_score(arrays, layout, act_rot, eigenvalues, query_rotated)

time: 513 us -> 615 us (1.20)
  waiting for transfers between devices: 180 us -> 319 us
  starting transfers between devices: 146 us -> 109 us
  local copies, waits for them, and re-layouts: 52.1 us -> 78.8 us
  blocking collectives: 29.6 us -> 14.1 us
  Pallas kernels: 76.2 us -> 66.3 us
    ppermute x8 -> x6, starting transfers between devices: 95.9 us -> 19.2 us  [the longest x3 13.5 us: chain_body(): partner.append(lax.ppermute(after(flat, *tie)[a:b], 'row', ends))]
    ppermute x4, waiting for transfers between devices: 27.8 us -> 84 us  [scatter_sum(): lax.ppermute(total[:, dirs:], 'row', beside)]
    ppermute x5, waiting for transfers between devices: 0.01 us -> 49.5 us  [chain_body(): far.append(lax.ppermute(near[i], 'groups', [(0, 1), (1, 0)]))]
    ppermute x5, starting transfers between devices: 22.8 us -> 67.9 us  [chain_body(): near.append(lax.ppermute(piece, 'row', beside))]
    ppermute x8 -> x6, waiting for transfers between devices: 11.5 us -> 46.7 us  [the longest x3 46.7 us: chain_body(): partner.append(lax.ppermute(after(flat, *tie)[a:b], 'row', ends))]
    ppermute x12, waiting for transfers between devices: 17.4 us -> 33.5 us  [scatter_sum(): lax.ppermute(sent, 'col', [(i, i ^ d) for i in range(parts)]).astype(F32)]
    ppermute x5, waiting for transfers between devices: 117 us -> 101 us  [chain_body(): near.append(lax.ppermute(piece, 'row', beside))]
    all_gather x3 -> x2, blocking collectives: 29.6 us -> 14.1 us  [place(): every = lax.all_gather(sums[-1], 'col', axis=0)]
  transfers between devices with their start and end apart: 42 -> 41, of which waited for: 16 -> 19; matrix products, arithmetic and copies ran while one was open for 8% -> 9% of each run, Pallas kernels for 14% -> 10%
where the time goes in v6:
time: 615 us; the launch traced here: 613 us
  waiting for transfers between devices  319 us (52%)
  starting transfers between devices  109 us (18%)
  local copies, waits for them, and re-layouts  78.8 us (13%)
  Pallas kernels  66.3 us (11%)
  between operations  16.2 us (3%)
  blocking collectives  14.1 us (2%)
    ppermute x5, waiting for transfers between devices, chain_body(): near.append(lax.ppermute(piece, 'row', beside))  101 us
    ppermute x4, waiting for transfers between devices, scatter_sum(): lax.ppermute(total[:, dirs:], 'row', beside)  84 us
    ppermute x5, starting transfers between devices, chain_body(): near.append(lax.ppermute(piece, 'row', beside))  67.9 us
    pallas_call x5, Pallas kernels, project(): pl.pallas_call(functools.partial(project_kernel, len(tokens), widths), gr...  61.9 us
    ppermute x5, waiting for transfers between devices, chain_body(): far.append(lax.ppermute(near[i], 'groups', [(0, 1), (1, 0)]))  49.5 us
    ppermute x3, waiting for transfers between devices, chain_body(): partner.append(lax.ppermute(after(flat, *tie)[a:b], 'row', ends))  46.7 us
    unnamed x78, local copies, waits for them, and re-layouts  44.9 us
    ppermute x12, waiting for transfers between devices, scatter_sum(): lax.ppermute(sent, 'col', [(i, i ^ d) for i in range(parts)]).astype(F32)  33.5 us
  transfers between devices with their start and end apart: 41, of which 19 were waited for; matrix products, arithmetic and copies ran while one was open for 9% of the time, Pallas kernels for 10%

profile of v6, /device:TPU:0, one launch (start us, length us, event | category | flops | bytes accessed | tf_op | source)
XLA Modules:
  0.0 613.1 jit_solution(18308787848950863430)
XLA Ops:
  8.0 3.9 slice.193
  11.9 2.3 collective-permute-start.4
  15.5 4.3 collective-permute-start
  19.8 2.3 slice.192
  22.8 3.1 constant_dynamic-slice_fusion.4
  25.9 3.1 collective-permute-start.1
  29.1 5.8 copy-done
  34.9 3.4 copy-done.7
  38.3 12.0 %shard_map.95 = bf16[512,1024]{1,0:T(8,128)(2,1)S(1)} custom-call(s32[2]{0:T(128)S(1)} %pad_add_fusion.refs_0_, bf16[512,8192]{1,0:T(8,128)(2,1)S(1)} %bitcast.214, bf16[8192,1024]{1,0:T(8,128)(2,1)S(1)} %copy-done), custom_call_target="tpu_custom_call" | custom-call | flops 536870912 | bytes 1572864 | tf_op jit(solution)/shard_map/pallas_call | solution.py:145
  50.7 1.9 constant_dynamic-slice_fusion.3
  52.6 58.6 %collective-permute-start.3 = (bf16[2048,512]{1,0:T(8,128)(2,1)S(1)}, bf16[2048,512]{1,0:T(8,128)(2,1)}, u32[]{:S(2)}, u32[]{:S(2)}) collective-permute-start(bf16[2048,512]{1,0:T(8,128)(2,1)S(1)} %constant_dynamic-slice_fusion.3), channel_id=1, source_target_pairs={{0,4},{4,0},{8,12},{12,8},{1,5},{5,1},{9,13},{13,9},{2,6},{6,2},{1... | collective-permute-start | bytes 6291464 | tf_op jit(solution)/shard_map/ppermute | solution.py:203
  111.1 4.9 fusion.8
  116.0 1.7 constant_dynamic-slice_fusion.2
  117.9 1.6 collective-permute-start.8
  119.9 37.8 %collective-permute-done.3 = bf16[2048,512]{1,0:T(8,128)(2,1)} collective-permute-done((bf16[2048,512]{1,0:T(8,128)(2,1)S(1)}, bf16[2048,512]{1,0:T(8,128)(2,1)}, u32[]{:S(2)}, u32[]{:S(2)}) %collective-permute-start.3) | collective-permute-done | bytes 2097184 | tf_op jit(solution)/shard_map/ppermute | solution.py:203
  157.8 1.5 collective-permute-start.9
  159.3 41.6 %collective-permute-done.5 = bf16[2048,512]{1,0:T(8,128)(2,1)} collective-permute-done((bf16[2048,512]{1,0:T(8,128)(2,1)S(1)}, bf16[2048,512]{1,0:T(8,128)(2,1)}, u32[]{:S(2)}, u32[]{:S(2)}) %collective-permute-start.5) | collective-permute-done | bytes 2097184 | tf_op jit(solution)/shard_map/ppermute | solution.py:203
  200.9 1.5 collective-permute-start.10
  203.7 1.8 collective-permute-start.6
  206.4 4.6 slice.150
  212.4 2.7 collective-permute-start.16
  216.4 1.8 constant_dynamic-update-slice_fusion.3
  218.2 1.7 constant_dynamic-update-slice_fusion.2
  220.0 21.1 %collective-permute-done.6 = bf16[1024,512]{1,0:T(8,128)(2,1)} collective-permute-done((bf16[1024,512]{1,0:T(8,128)(2,1)S(1)}, bf16[1024,512]{1,0:T(8,128)(2,1)}, u32[]{:S(2)}, u32[]{:S(2)}) %collective-permute-start.6) | collective-permute-done | bytes 1048608 | tf_op jit(solution)/shard_map/ppermute | solution.py:203
  241.1 1.7 constant_dynamic-update-slice_fusion.8
  242.9 1.9 constant_dynamic-update-slice_fusion.1
  244.7 1.7 constant_dynamic-update-slice_fusion.7
  248.0 31.2 %collective-permute-done.10 = bf16[2048,512]{1,0:T(8,128)(2,1)} collective-permute-done((bf16[2048,512]{1,0:T(8,128)(2,1)}, bf16[2048,512]{1,0:T(8,128)(2,1)}, u32[]{:S(2)}, u32[]{:S(2)}) %collective-permute-start.10) | collective-permute-done | bytes 2097184 | tf_op jit(solution)/shard_map/ppermute | solution.py:204
  279.1 1.7 constant_dynamic-update-slice_fusion.6
  280.9 18.3 %collective-permute-done.11 = bf16[1024,512]{1,0:T(8,128)(2,1)S(1)} collective-permute-done((bf16[1024,512]{1,0:T(8,128)(2,1)}, bf16[1024,512]{1,0:T(8,128)(2,1)S(1)}, u32[]{:S(2)}, u32[]{:S(2)}) %collective-permute-start.11) | collective-permute-done | bytes 1048608 | tf_op jit(solution)/shard_map/ppermute | solution.py:204
  299.3 11.9 %shard_map.96 = bf16[512,1024]{1,0:T(8,128)(2,1)S(1)} custom-call(s32[2]{0:T(128)S(1)} %pad_add_fusion.refs_0_, bf16[512,8192]{1,0:T(8,128)(2,1)S(1)} %bitcast.217, bf16[8192,512]{1,0:T(8,128)(2,1)S(1)} %constant_dynamic-update-slice_fusion.refs_2_.refs_4_.refs_5_, bf16[8192,512]{1,0:T(8,128)(2,1)S(1)} %constant_dynamic-update-slice_fusion.5.refs_3_.refs_5_.refs_6_), custom_call_target="tpu_custom_call" | custom-call | flops 536870912 | bytes 1572864 | tf_op jit(solution)/shard_map/pallas_call | solution.py:145
  313.7 1.5 collective-permute-start.13
  315.5 4.7 slice.154
  320.2 4.5 collective-permute-start.22
  324.8 3.4 collective-permute-done.14
  328.2 11.3 %collective-permute-done.13 = bf16[128,2048]{1,0:T(8,128)(2,1)} collective-permute-done((bf16[128,2048]{1,0:T(8,128)(2,1)S(1)}, bf16[128,2048]{1,0:T(8,128)(2,1)}, u32[]{:S(2)}, u32[]{:S(2)}) %collective-permute-start.13) | collective-permute-done | bytes 524320 | tf_op jit(solution)/shard_map/ppermute | solution.py:226
  339.4 1.9 fusion.13
  341.3 1.7 collective-permute-start.15
  343.1 79.5 %collective-permute-done.15 = bf16[128,1024]{1,0:T(8,128)(2,1)S(1)} collective-permute-done((bf16[128,1024]{1,0:T(8,128)(2,1)S(1)}, bf16[128,1024]{1,0:T(8,128)(2,1)S(1)}, u32[]{:S(2)}, u32[]{:S(2)}) %collective-permute-start.15) | collective-permute-done | bytes 262176 | tf_op jit(solution)/shard_map/ppermute | solution.py:228
  423.6 1.7 slice.151
  425.4 4.4 collective-permute-start.17
  430.0 46.7 %collective-permute-done.17.refs_1_ = bf16[128,8192]{1,0:T(8,128)(2,1)S(1)} collective-permute-done((bf16[128,8192]{1,0:T(8,128)(2,1)S(1)}, bf16[128,8192]{1,0:T(8,128)(2,1)S(1)}, u32[]{:S(2)}, u32[]{:S(2)}) %collective-permute-start.17) | collective-permute-done | bytes 2097184 | tf_op jit(solution)/shard_map/ppermute | solution.py:219
  478.0 3.1 slice.157
  481.1 4.6 collective-permute-start.27
  485.7 3.4 copy-done.2
  489.1 3.4 copy-done.5
  492.5 1.6 copy-done.11
  494.0 11.4 %shard_map.97 = bf16[128,2048]{1,0:T(8,128)(2,1)S(1)} custom-call(s32[2]{0:T(128)S(1)} %pad_add_fusion.refs_0_, bf16[128,8192]{1,0:T(8,128)(2,1)S(1)} %copy-done.11, bf16[256,8192]{1,0:T(8,128)(2,1)} %collective-permute-done.16.refs_2_, bf16[8192,1024]{1,0:T(8,128)(2,1)} %refs_3_.3, bf16[8192,512]{1,0:T(8,128)(2,1)S(1)} %copy-done.5, ...), custom_call_target="tpu_custom_call" | custom-call | flops 268435456 | bytes 2228224 | tf_op jit(solution)/shard_map/pallas_call | solution.py:145
  505.6 1.5 collective-permute-start.19
  507.5 14.9 %shard_map.98 = bf16[256,2048]{1,0:T(8,128)(2,1)S(1)} custom-call(s32[2]{0:T(128)S(1)} %pad_add_fusion.refs_0_, bf16[256,8192]{1,0:T(8,128)(2,1)} %collective-permute-done.22.refs_1_, bf16[64,8192]{1,0:T(8,128)(2,1)S(1)} %collective-permute-done.2.refs_2_, bf16[192,8192]{1,0:T(8,128)(2,1)} %collective-permute-done.4.refs_3_, bf16[8192,1024]{1,0:T(8,128)(2,1)} %refs_3_.3, ...), custom_call_target="tpu_custom_call" | custom-call | flops 536870912 | bytes 2359296 | tf_op jit(solution)/shard_map/pallas_call | solution.py:145
  524.6 6.3 %collective-permute-done.25 = bf16[64,2048]{1,0:T(8,128)(2,1)S(1)} collective-permute-done((bf16[64,2048]{1,0:T(8,128)(2,1)S(1)}, bf16[64,2048]{1,0:T(8,128)(2,1)S(1)}, u32[]{:S(2)}, u32[]{:S(2)}) %collective-permute-start.25) | collective-permute-done | bytes 262176 | tf_op jit(solution)/shard_map/ppermute | solution.py:226
  530.8 5.9 collective-permute-done.24
  537.7 4.6 collective-permute-done.26
  543.0 3.4 copy-done.3
  546.4 3.6 copy-done.6
  550.0 11.6 %shard_map.99 = bf16[128,2048]{1,0:T(8,128)(2,1)S(1)} custom-call(s32[2]{0:T(128)S(1)} %pad_add_fusion.refs_0_, bf16[128,8192]{1,0:T(8,128)(2,1)S(1)} %collective-permute-done.27.refs_1_, bf16[256,8192]{1,0:T(8,128)(2,1)} %collective-permute-done.16.refs_2_, bf16[8192,1024]{1,0:T(8,128)(2,1)} %refs_3_.3, bf16[8192,512]{1,0:T(8,128)(2,1)S(1)} %copy-done.6, ...), custom_call_target="tpu_custom_call" | custom-call | flops 268435456 | bytes 2228224 | tf_op jit(solution)/shard_map/pallas_call | solution.py:145
  563.7 3.8 collective-permute-done.30
  567.5 2.8 collective-permute-done.29
  570.7 6.8 %all-gather.1 = bf16[8,32,1024]{2,1,0:T(8,128)(2,1)S(1)} all-gather(bf16[2,32,1024]{2,1,0:T(8,128)(2,1)S(1)} %pad_maximum_fusion.4), channel_id=3, replica_groups=mesh['groups'=2,'row'=4,'col'=4] {'col'}, dimensions={0}, use_global_device_ids=true | all-gather | bytes 655360 | tf_op jit(solution)/shard_map/all_gather | solution.py:238
  577.5 7.3 %all-gather.4 = bf16[8,32,1024]{2,1,0:T(8,128)(2,1)S(1)} all-gather(bf16[2,32,1024]{2,1,0:T(8,128)(2,1)S(1)} %pad_maximum_fusion.5), channel_id=6, replica_groups=mesh['groups'=2,'row'=4,'col'=4] {'col'}, dimensions={0}, use_global_device_ids=true | all-gather | bytes 655360 | tf_op jit(solution)/shard_map/all_gather | solution.py:238
  584.8 1.6 copy-done.8
  586.4 1.6 copy-done.9
  589.2 4.3 shard_map.100
  599.5 2.0 collective-permute-start.36
  (152 shorter events, 32.7 us)
Async XLA Ops:
  8.0 307.5 %all-gather.11.cloned.1.call-start = ((), (), s32[]{:S(2)}) async-start(), calls=%async_computation.1 | async-start | bytes 1310720 | tf_op jit(solution)/shard_map/all_gather | solution.py:208
  11.9 104.1 %collective-permute-start.4 = (bf16[192,8192]{1,0:T(8,128)(2,1)}, bf16[192,8192]{1,0:T(8,128)(2,1)}, u32[]{:S(2)}, u32[]{:S(2)}) collective-permute-start(bf16[192,8192]{1,0:T(8,128)(2,1)} %slice.193), channel_id=1, source_target_pairs={{4,8},{8,4},{5,9},{9,5},{6,10},{10,6},{7,11},{11,7},{20,24},{24,20... | collective-permute-start | bytes 9437192 | tf_op jit(solution)/shard_map/ppermute | solution.py:194
  15.5 35.2 %collective-permute-start = (bf16[1024,512]{1,0:T(8,128)(2,1)S(1)}, bf16[1024,512]{1,0:T(8,128)(2,1)}, u32[]{:S(2)}, u32[]{:S(2)}) collective-permute-start(bf16[1024,512]{1,0:T(8,128)(2,1)S(1)} %constant_dynamic-slice_fusion), channel_id=1, source_target_pairs={{0,4},{4,0},{8,12},{12,8},{1,5},{5,1},{9,13},{13,9},{2,6},{6,2},{1... | collective-permute-start | bytes 3145736 | tf_op jit(solution)/shard_map/ppermute | solution.py:203
  22.1 28.6 %collective-permute-start.2 = (bf16[64,8192]{1,0:T(8,128)(2,1)}, bf16[64,8192]{1,0:T(8,128)(2,1)S(1)}, u32[]{:S(2)}, u32[]{:S(2)}) collective-permute-start(bf16[64,8192]{1,0:T(8,128)(2,1)} %slice.192), channel_id=1, source_target_pairs={{4,8},{8,4},{5,9},{9,5},{6,10},{10,6},{7,11},{11,7},{20,24},{24,20... | collective-permute-start | bytes 3145736 | tf_op jit(solution)/shard_map/ppermute | solution.py:194
  25.9 90.1 %collective-permute-start.1 = (bf16[2048,512]{1,0:T(8,128)(2,1)}, bf16[2048,512]{1,0:T(8,128)(2,1)}, u32[]{:S(2)}, u32[]{:S(2)}) collective-permute-start(bf16[2048,512]{1,0:T(8,128)(2,1)} %constant_dynamic-slice_fusion.4), channel_id=1, source_target_pairs={{0,4},{4,0},{8,12},{12,8},{1,5},{5,1},{9,13},{13,9},{2,6},{6,2},{1... | collective-permute-start | bytes 6291464 | tf_op jit(solution)/shard_map/ppermute | solution.py:203
  29.1 5.8 copy-start
  34.9 3.4 copy-start.7
  38.3 12.1 %copy-start.24 = (s32[2048]{0:T(1024)S(1)}, s32[2048]{0:T(1024)}, u32[]{:S(2)}) copy-start(s32[2048]{0:T(1024)} %param.15) | copy-start | bytes 24580
  38.3 12.1 %copy-start.25 = (s32[4]{0:T(128)S(1)}, s32[4]{0:T(128)}, u32[]{:S(2)}) copy-start(s32[4]{0:T(128)} %param.14) | copy-start | bytes 52
  50.3 60.8 %copy-start.26 = (bf16[8192,256]{1,0:T(8,128)(2,1)S(1)}, bf16[8192,256]{1,0:T(8,128)(2,1)}, u32[]{:S(2)}) copy-start(bf16[8192,256]{1,0:T(8,128)(2,1)} %param.10) | copy-start | bytes 12582916
  52.6 105.2 %collective-permute-start.3 = (bf16[2048,512]{1,0:T(8,128)(2,1)S(1)}, bf16[2048,512]{1,0:T(8,128)(2,1)}, u32[]{:S(2)}, u32[]{:S(2)}) collective-permute-start(bf16[2048,512]{1,0:T(8,128)(2,1)S(1)} %constant_dynamic-slice_fusion.3), channel_id=1, source_target_pairs={{0,4},{4,0},{8,12},{12,8},{1,5},{5,1},{9,13},{13,9},{2,6},{6,2},{1... | collective-permute-start | bytes 6291464 | tf_op jit(solution)/shard_map/ppermute | solution.py:203
  117.8 83.2 %collective-permute-start.5 = (bf16[2048,512]{1,0:T(8,128)(2,1)S(1)}, bf16[2048,512]{1,0:T(8,128)(2,1)}, u32[]{:S(2)}, u32[]{:S(2)}) collective-permute-start(bf16[2048,512]{1,0:T(8,128)(2,1)S(1)} %constant_dynamic-slice_fusion.2), channel_id=1, source_target_pairs={{0,4},{4,0},{8,12},{12,8},{1,5},{5,1},{9,13},{13,9},{2,6},{6,2},{1... | collective-permute-start | bytes 6291464 | tf_op jit(solution)/shard_map/ppermute | solution.py:203
  117.9 123.2 %collective-permute-start.8 = (bf16[2048,512]{1,0:T(8,128)(2,1)}, bf16[2048,512]{1,0:T(8,128)(2,1)}, u32[]{:S(2)}, u32[]{:S(2)}) collective-permute-start(bf16[2048,512]{1,0:T(8,128)(2,1)} %collective-permute-done.1), channel_id=1, source_target_pairs={{0,16},{16,0},{1,17},{17,1},{2,18},{18,2},{3,19},{19,3},{4,20},{20... | collective-permute-start | bytes 6291464 | tf_op jit(solution)/shard_map/ppermute | solution.py:204
  119.4 93.0 %collective-permute-start.7 = (bf16[1024,512]{1,0:T(8,128)(2,1)}, bf16[1024,512]{1,0:T(8,128)(2,1)}, u32[]{:S(2)}, u32[]{:S(2)}) collective-permute-start(bf16[1024,512]{1,0:T(8,128)(2,1)} %collective-permute-done), channel_id=1, source_target_pairs={{0,16},{16,0},{1,17},{17,1},{2,18},{18,2},{3,19},{19,3},{4,20},{20... | collective-permute-start | bytes 3145736 | tf_op jit(solution)/shard_map/ppermute | solution.py:204
  157.8 87.0 %collective-permute-start.9 = (bf16[2048,512]{1,0:T(8,128)(2,1)}, bf16[2048,512]{1,0:T(8,128)(2,1)}, u32[]{:S(2)}, u32[]{:S(2)}) collective-permute-start(bf16[2048,512]{1,0:T(8,128)(2,1)} %collective-permute-done.3), channel_id=1, source_target_pairs={{0,16},{16,0},{1,17},{17,1},{2,18},{18,2},{3,19},{19,3},{4,20},{20... | collective-permute-start | bytes 6291464 | tf_op jit(solution)/shard_map/ppermute | solution.py:204
  200.9 78.2 %collective-permute-start.10 = (bf16[2048,512]{1,0:T(8,128)(2,1)}, bf16[2048,512]{1,0:T(8,128)(2,1)}, u32[]{:S(2)}, u32[]{:S(2)}) collective-permute-start(bf16[2048,512]{1,0:T(8,128)(2,1)} %collective-permute-done.5), channel_id=1, source_target_pairs={{0,16},{16,0},{1,17},{17,1},{2,18},{18,2},{3,19},{19,3},{4,20},{20... | collective-permute-start | bytes 6291464 | tf_op jit(solution)/shard_map/ppermute | solution.py:204
  203.7 37.4 %collective-permute-start.6 = (bf16[1024,512]{1,0:T(8,128)(2,1)S(1)}, bf16[1024,512]{1,0:T(8,128)(2,1)}, u32[]{:S(2)}, u32[]{:S(2)}) collective-permute-start(bf16[1024,512]{1,0:T(8,128)(2,1)S(1)} %constant_dynamic-slice_fusion.1), channel_id=1, source_target_pairs={{0,4},{4,0},{8,12},{12,8},{1,5},{5,1},{9,13},{13,9},{2,6},{6,2},{1... | collective-permute-start | bytes 3145736 | tf_op jit(solution)/shard_map/ppermute | solution.py:203
  211.1 274.6 %all-gather.9.cloned.1.call-start = ((), (), s32[]{:S(2)}) async-start(), calls=%async_computation | async-start | bytes 2621440 | tf_op jit(solution)/shard_map/all_gather | solution.py:238
  212.4 211.2 %collective-permute-start.16 = (bf16[256,8192]{1,0:T(8,128)(2,1)}, bf16[256,8192]{1,0:T(8,128)(2,1)}, u32[]{:S(2)}, u32[]{:S(2)}) collective-permute-start(bf16[256,8192]{1,0:T(8,128)(2,1)} %slice.150), channel_id=1, source_target_pairs={{4,8},{8,4},{5,9},{9,5},{6,10},{10,6},{7,11},{11,7},{20,24},{24,20... | collective-permute-start | bytes 12582920 | tf_op jit(solution)/shard_map/ppermute | solution.py:194
  241.1 58.1 %collective-permute-start.11 = (bf16[1024,512]{1,0:T(8,128)(2,1)}, bf16[1024,512]{1,0:T(8,128)(2,1)S(1)}, u32[]{:S(2)}, u32[]{:S(2)}) collective-permute-start(bf16[1024,512]{1,0:T(8,128)(2,1)} %collective-permute-done.6), channel_id=1, source_target_pairs={{0,16},{16,0},{1,17},{17,1},{2,18},{18,2},{3,19},{19,3},{4,20},{20... | collective-permute-start | bytes 3145736 | tf_op jit(solution)/shard_map/ppermute | solution.py:204
  242.8 56.4 %slice-start = ((s8[8388608]{0:T(1024)(128)(4,1)}), s8[4194304]{0:T(1024)(128)(4,1)S(1)}, s32[]{:S(2)}) async-start(s8[8388608]{0:T(1024)(128)(4,1)} %bitcast.215), calls=%async_computation.3 | async-start | bytes 8388608
  246.5 52.8 %slice-start.1 = ((s8[8388608]{0:T(1024)(128)(4,1)}), s8[4194304]{0:T(1024)(128)(4,1)S(1)}, s32[]{:S(2)}) async-start(s8[8388608]{0:T(1024)(128)(4,1)} %bitcast.215), calls=%async_computation.4 | async-start | bytes 8388608
  247.9 63.3 %copy-start.4 = (bf16[8192,512]{1,0:T(8,128)(2,1)}, bf16[8192,512]{1,0:T(8,128)(2,1)S(1)}, u32[]{:S(2)}) copy-start(bf16[8192,512]{1,0:T(8,128)(2,1)S(1)} %constant_dynamic-update-slice_fusion.refs_2_.refs_4_.refs_5_) | copy-start | bytes 25165828
  299.3 12.0 %copy-start.1 = (bf16[8192,512]{1,0:T(8,128)(2,1)}, bf16[8192,512]{1,0:T(8,128)(2,1)S(1)}, u32[]{:S(2)}) copy-start(bf16[8192,512]{1,0:T(8,128)(2,1)S(1)} %constant_dynamic-update-slice_fusion.5.refs_3_.refs_5_.refs_6_) | copy-start | bytes 25165828
  313.7 14.5 %collective-permute-start.14 = (bf16[128,2048]{1,0:T(8,128)(2,1)}, bf16[128,2048]{1,0:T(8,128)(2,1)}, u32[]{:S(2)}, u32[]{:S(2)}) collective-permute-start(bf16[128,2048]{1,0:T(8,128)(2,1)} %get-tuple-element.27), channel_id=1, source_target_pairs={{0,3},{1,2},{2,1},{3,0},{4,7},{5,6},{6,5},{7,4},{8,11},{9,10},{10,... | collective-permute-start | bytes 1572872 | tf_op jit(solution)/shard_map/ppermute | solution.py:226
  313.7 25.8 %collective-permute-start.13 = (bf16[128,2048]{1,0:T(8,128)(2,1)S(1)}, bf16[128,2048]{1,0:T(8,128)(2,1)}, u32[]{:S(2)}, u32[]{:S(2)}) collective-permute-start(bf16[128,2048]{1,0:T(8,128)(2,1)S(1)} %get-tuple-element.28), channel_id=1, source_target_pairs={{0,2},{1,3},{2,0},{3,1},{4,6},{5,7},{6,4},{7,5},{8,10},{9,11},{10,... | collective-permute-start | bytes 1572872 | tf_op jit(solution)/shard_map/ppermute | solution.py:226
  315.2 24.3 %collective-permute-start.12 = (bf16[128,2048]{1,0:T(8,128)(2,1)S(1)}, bf16[128,2048]{1,0:T(8,128)(2,1)}, u32[]{:S(2)}, u32[]{:S(2)}) collective-permute-start(bf16[128,2048]{1,0:T(8,128)(2,1)S(1)} %get-tuple-element.26), channel_id=1, source_target_pairs={{0,1},{1,0},{2,3},{3,2},{4,5},{5,4},{6,7},{7,6},{8,9},{9,8},{10,11... | collective-permute-start | bytes 1572872 | tf_op jit(solution)/shard_map/ppermute | solution.py:226
  320.2 103.2 %copy-start.15 = (bf16[16,128,256]{2,1,0:T(8,128)(2,1)S(1)}, bf16[16,128,256]{2,1,0:T(8,128)(2,1)}, u32[]{:S(2)}) copy-start(bf16[16,128,256]{2,1,0:T(8,128)(2,1)} %all-gather.11.cloned.1.call-done) | copy-start | bytes 3145732
  320.2 157.7 %collective-permute-start.22 = (bf16[256,8192]{1,0:T(8,128)(2,1)}, bf16[256,8192]{1,0:T(8,128)(2,1)}, u32[]{:S(2)}, u32[]{:S(2)}) collective-permute-start(bf16[256,8192]{1,0:T(8,128)(2,1)} %slice.154), channel_id=1, source_target_pairs={{0,12},{12,0},{1,13},{13,1},{2,14},{14,2},{3,15},{15,3},{16,28},{2... | collective-permute-start | bytes 12582920 | tf_op jit(solution)/shard_map/ppermute | solution.py:219
  341.3 81.2 %collective-permute-start.15 = (bf16[128,1024]{1,0:T(8,128)(2,1)S(1)}, bf16[128,1024]{1,0:T(8,128)(2,1)S(1)}, u32[]{:S(2)}, u32[]{:S(2)}) collective-permute-start(bf16[128,1024]{1,0:T(8,128)(2,1)S(1)} %get-tuple-element.49), channel_id=1, source_target_pairs={{0,4},{4,0},{8,12},{12,8},{1,5},{5,1},{9,13},{13,9},{2,6},{6,2},{1... | collective-permute-start | bytes 786440 | tf_op jit(solution)/shard_map/ppermute | solution.py:228
  423.4 161.4 %all-gather.13.cloned.1.call-start = ((), (), s32[]{:S(2)}) async-start(), calls=%async_computation.2 | async-start | bytes 1310720 | tf_op jit(solution)/shard_map/all_gather | solution.py:238
  425.4 51.3 %collective-permute-start.17 = (bf16[128,8192]{1,0:T(8,128)(2,1)S(1)}, bf16[128,8192]{1,0:T(8,128)(2,1)S(1)}, u32[]{:S(2)}, u32[]{:S(2)}) collective-permute-start(bf16[128,8192]{1,0:T(8,128)(2,1)S(1)} %slice.151), channel_id=1, source_target_pairs={{0,12},{12,0},{1,13},{13,1},{2,14},{14,2},{3,15},{15,3},{16,28},{2... | collective-permute-start | bytes 6291464 | tf_op jit(solution)/shard_map/ppermute | solution.py:219
  429.9 51.2 %copy-start.18 = (bf16[512,256]{1,0:T(8,128)(2,1)}, bf16[512,256]{1,0:T(8,128)(2,1)S(1)}, u32[]{:S(2)}) copy-start(bf16[512,256]{1,0:T(8,128)(2,1)S(1)} %get-tuple-element.60) | copy-start | bytes 786436
  429.9 51.2 %copy-start.22 = (bf16[512,256]{1,0:T(8,128)(2,1)}, bf16[512,256]{1,0:T(8,128)(2,1)S(1)}, u32[]{:S(2)}) copy-start(bf16[512,256]{1,0:T(8,128)(2,1)S(1)} %get-tuple-element.61) | copy-start | bytes 786436
  429.9 48.0 %copy-start.16 = (bf16[512,256]{1,0:T(8,128)(2,1)}, bf16[512,256]{1,0:T(8,128)(2,1)S(1)}, u32[]{:S(2)}) copy-start(bf16[512,256]{1,0:T(8,128)(2,1)S(1)} %get-tuple-element.50) | copy-start | bytes 786436
  430.0 51.1 %copy-start.20 = (bf16[512,256]{1,0:T(8,128)(2,1)}, bf16[512,256]{1,0:T(8,128)(2,1)S(1)}, u32[]{:S(2)}) copy-start(bf16[512,256]{1,0:T(8,128)(2,1)S(1)} %get-tuple-element.51) | copy-start | bytes 786436
  481.1 61.9 %collective-permute-start.27 = (bf16[128,8192]{1,0:T(8,128)(2,1)}, bf16[128,8192]{1,0:T(8,128)(2,1)S(1)}, u32[]{:S(2)}, u32[]{:S(2)}) collective-permute-start(bf16[128,8192]{1,0:T(8,128)(2,1)} %slice.157), channel_id=1, source_target_pairs={{0,12},{12,0},{1,13},{13,1},{2,14},{14,2},{3,15},{15,3},{16,28},{2... | collective-permute-start | bytes 6291464 | tf_op jit(solution)/shard_map/ppermute | solution.py:219
  485.7 3.4 copy-start.2
  489.1 3.4 copy-start.5
  505.5 18.0 %collective-permute-start.20 = (bf16[32,2048]{1,0:T(8,128)(2,1)S(1)}, bf16[32,2048]{1,0:T(8,128)(2,1)S(1)}, u32[]{:S(2)}, u32[]{:S(2)}) collective-permute-start(bf16[32,2048]{1,0:T(8,128)(2,1)S(1)} %get-tuple-element.46), channel_id=1, source_target_pairs={{0,3},{1,2},{2,1},{3,0},{4,7},{5,6},{6,5},{7,4},{8,11},{9,10},{10,... | collective-permute-start | bytes 393224 | tf_op jit(solution)/shard_map/ppermute | solution.py:226
  505.6 18.7 %collective-permute-start.19 = (bf16[32,2048]{1,0:T(8,128)(2,1)S(1)}, bf16[32,2048]{1,0:T(8,128)(2,1)S(1)}, u32[]{:S(2)}, u32[]{:S(2)}) collective-permute-start(bf16[32,2048]{1,0:T(8,128)(2,1)S(1)} %get-tuple-element.47), channel_id=1, source_target_pairs={{0,2},{1,3},{2,0},{3,1},{4,6},{5,7},{6,4},{7,5},{8,10},{9,11},{10,... | collective-permute-start | bytes 393224 | tf_op jit(solution)/shard_map/ppermute | solution.py:226
  507.1 17.3 %collective-permute-start.18 = (bf16[32,2048]{1,0:T(8,128)(2,1)S(1)}, bf16[32,2048]{1,0:T(8,128)(2,1)S(1)}, u32[]{:S(2)}, u32[]{:S(2)}) collective-permute-start(bf16[32,2048]{1,0:T(8,128)(2,1)S(1)} %get-tuple-element.45), channel_id=1, source_target_pairs={{0,1},{1,0},{2,3},{3,2},{4,5},{5,4},{6,7},{7,6},{8,9},{9,8},{10,11... | collective-permute-start | bytes 393224 | tf_op jit(solution)/shard_map/ppermute | solution.py:226
  522.5 8.4 %collective-permute-start.25 = (bf16[64,2048]{1,0:T(8,128)(2,1)S(1)}, bf16[64,2048]{1,0:T(8,128)(2,1)S(1)}, u32[]{:S(2)}, u32[]{:S(2)}) collective-permute-start(bf16[64,2048]{1,0:T(8,128)(2,1)S(1)} %get-tuple-element.40), channel_id=1, source_target_pairs={{0,3},{1,2},{2,1},{3,0},{4,7},{5,6},{6,5},{7,4},{8,11},{9,10},{10,... | collective-permute-start | bytes 786440 | tf_op jit(solution)/shard_map/ppermute | solution.py:226
  523.6 13.2 %collective-permute-start.24 = (bf16[64,2048]{1,0:T(8,128)(2,1)S(1)}, bf16[64,2048]{1,0:T(8,128)(2,1)S(1)}, u32[]{:S(2)}, u32[]{:S(2)}) collective-permute-start(bf16[64,2048]{1,0:T(8,128)(2,1)S(1)} %get-tuple-element.41), channel_id=1, source_target_pairs={{0,2},{1,3},{2,0},{3,1},{4,6},{5,7},{6,4},{7,5},{8,10},{9,11},{10,... | collective-permute-start | bytes 786440 | tf_op jit(solution)/shard_map/ppermute | solution.py:226
  524.3 12.4 %collective-permute-start.23 = (bf16[64,2048]{1,0:T(8,128)(2,1)S(1)}, bf16[64,2048]{1,0:T(8,128)(2,1)S(1)}, u32[]{:S(2)}, u32[]{:S(2)}) collective-permute-start(bf16[64,2048]{1,0:T(8,128)(2,1)S(1)} %get-tuple-element.39), channel_id=1, source_target_pairs={{0,1},{1,0},{2,3},{3,2},{4,5},{5,4},{6,7},{7,6},{8,9},{9,8},{10,11... | collective-permute-start | bytes 786440 | tf_op jit(solution)/shard_map/ppermute | solution.py:226
  524.5 13.1 %collective-permute-start.21 = (bf16[32,1024]{1,0:T(8,128)(2,1)S(1)}, bf16[32,1024]{1,0:T(8,128)(2,1)S(1)}, u32[]{:S(2)}, u32[]{:S(2)}) collective-permute-start(bf16[32,1024]{1,0:T(8,128)(2,1)S(1)} %get-tuple-element.79), channel_id=1, source_target_pairs={{0,4},{4,0},{8,12},{12,8},{1,5},{5,1},{9,13},{13,9},{2,6},{6,2},{1... | collective-permute-start | bytes 196616 | tf_op jit(solution)/shard_map/ppermute | solution.py:228
  536.9 5.3 collective-permute-start.26
  543.0 3.4 copy-start.3
  546.4 3.6 copy-start.6
  550.0 13.6 %copy-start.17 = (bf16[512,256]{1,0:T(8,128)(2,1)S(1)}, bf16[512,256]{1,0:T(8,128)(2,1)}, u32[]{:S(2)}) copy-start(bf16[512,256]{1,0:T(8,128)(2,1)} %copy-done.16) | copy-start | bytes 786436
  550.0 13.6 %copy-start.19 = (bf16[512,256]{1,0:T(8,128)(2,1)S(1)}, bf16[512,256]{1,0:T(8,128)(2,1)}, u32[]{:S(2)}) copy-start(bf16[512,256]{1,0:T(8,128)(2,1)} %get-tuple-element.58) | copy-start | bytes 786436
  550.0 13.6 %copy-start.21 = (bf16[512,256]{1,0:T(8,128)(2,1)S(1)}, bf16[512,256]{1,0:T(8,128)(2,1)}, u32[]{:S(2)}) copy-start(bf16[512,256]{1,0:T(8,128)(2,1)} %copy-done.20) | copy-start | bytes 786436
  550.0 13.6 %copy-start.23 = (bf16[512,256]{1,0:T(8,128)(2,1)S(1)}, bf16[512,256]{1,0:T(8,128)(2,1)}, u32[]{:S(2)}) copy-start(bf16[512,256]{1,0:T(8,128)(2,1)} %get-tuple-element.59) | copy-start | bytes 786436
  561.6 23.3 %copy-start.12 = (f32[1024,256]{1,0:T(8,128)S(1)}, f32[1024,256]{1,0:T(8,128)}, u32[]{:S(2)}) copy-start(f32[1024,256]{1,0:T(8,128)} %refs_5_.1) | copy-start | bytes 3145732
  561.6 5.8 collective-permute-start.30
  561.8 8.4 %collective-permute-start.29 = (bf16[32,2048]{1,0:T(8,128)(2,1)S(1)}, bf16[32,2048]{1,0:T(8,128)(2,1)S(1)}, u32[]{:S(2)}, u32[]{:S(2)}) collective-permute-start(bf16[32,2048]{1,0:T(8,128)(2,1)S(1)} %get-tuple-element.44), channel_id=1, source_target_pairs={{0,2},{1,3},{2,0},{3,1},{4,6},{5,7},{6,4},{7,5},{8,10},{9,11},{10,... | collective-permute-start | bytes 393224 | tf_op jit(solution)/shard_map/ppermute | solution.py:226
  563.2 7.1 %collective-permute-start.28 = (bf16[32,2048]{1,0:T(8,128)(2,1)S(1)}, bf16[32,2048]{1,0:T(8,128)(2,1)S(1)}, u32[]{:S(2)}, u32[]{:S(2)}) collective-permute-start(bf16[32,2048]{1,0:T(8,128)(2,1)S(1)} %get-tuple-element.42), channel_id=1, source_target_pairs={{0,1},{1,0},{2,3},{3,2},{4,5},{5,4},{6,7},{7,6},{8,9},{9,8},{10,11... | collective-permute-start | bytes 393224 | tf_op jit(solution)/shard_map/ppermute | solution.py:226
  570.4 7.1 %collective-permute-start.31 = (bf16[32,1024]{1,0:T(8,128)(2,1)S(1)}, bf16[32,1024]{1,0:T(8,128)(2,1)S(1)}, u32[]{:S(2)}, u32[]{:S(2)}) collective-permute-start(bf16[32,1024]{1,0:T(8,128)(2,1)S(1)} %get-tuple-element.77), channel_id=1, source_target_pairs={{0,4},{4,0},{8,12},{12,8},{1,5},{5,1},{9,13},{13,9},{2,6},{6,2},{1... | collective-permute-start | bytes 196616 | tf_op jit(solution)/shard_map/ppermute | solution.py:228
  593.8 3.0 collective-permute-start.34
  594.6 3.6 collective-permute-start.33
  595.8 2.4 collective-permute-start.32
  598.2 5.4 collective-permute-start.37
  599.5 4.5 collective-permute-start.36
  601.5 3.6 collective-permute-start.35
  (6 other events, 8.6 us)
Sparse Core Ops, SparseCore 0:
  211.2 36.2 all-gather.10
Sparse Core Ops, SparseCore 1:
  423.5 22.3 all-gather.8
  543.1 15.6 all-gather.12

commit v7 on v5

--- a/solution.py
+++ b/solution.py
@@ -67,7 +67,7 @@
             jax.ShapeDtypeStruct((cands, dirs, width), F32),
             jax.ShapeDtypeStruct((steps, queries * cands, width), F32),
         ],
-        compiler_params=pltpu.CompilerParams(vmem_limit_bytes=32 * 2**20),
+        compiler_params=pltpu.CompilerParams(vmem_limit_bytes=16 * 2**20),
     )(*arrays, act_rot, eigenvalues, query_rotated)
     return rotated, jnp.sum(partial_scores, axis=(0, 2)).reshape(queries, cands)
 
@@ -94,15 +94,16 @@
     return lax.optimization_barrier((value, *earlier))[0]
 
 
-def project_kernel(count, widths, *refs):
+def project_kernel(ends, count, widths, *refs):
     flags, refs = refs[0], refs[1:]
     tokens, basis, out, acc = refs[:count], refs[count:-2], refs[-2], refs[-1]
     step = pl.program_id(0)
-    rows = [t[...] for t in tokens]
-    if count > 1:
-        joined = jnp.concatenate(rows[:-1], axis=0) if count > 2 else rows[0]
-        rows = [jnp.where(flags[0] == 1, joined, rows[-1])]
-    rows = rows[0]
+    def joined(refs):
+        return jnp.concatenate([t[...] for t in refs], axis=0) if len(refs) > 1 else refs[0][...]
+
+    rows = joined(tokens[:ends])
+    if count > ends:
+        rows = jnp.where(flags[0] == 1, rows, joined(tokens[ends:]))
     start, spans = 0, []
     for width in widths:
         spans.append((start, start + width))
@@ -134,17 +135,18 @@
                 out[:, e:f] = acc[:, c:d].astype(BF16)
 
 
-def project(flags, tokens, bases):
+def project(flags, ends, middles, bases):
+    tokens = ends + middles
     feats = bases[0].shape[0]
     widths = tuple(x.shape[1] for x in bases)
     block, total = 1024, sum(widths)
-    rows = tokens[-1][2]
+    rows = sum(n for _, _, n in ends)
     specs = []
     for _, start, n in tokens:
         assert start % n == 0
         specs.append(pl.BlockSpec((n, block), lambda k, i=start // n: (i, k)))
     return pl.pallas_call(
-        functools.partial(project_kernel, len(tokens), widths),
+        functools.partial(project_kernel, len(ends), len(tokens), widths),
         grid=(feats // block,),
         in_specs=[pl.BlockSpec(memory_space=pltpu.SMEM)]
         + specs
@@ -152,7 +154,7 @@
         out_specs=pl.BlockSpec((rows, total), lambda k: (0, 0)),
         out_shape=jax.ShapeDtypeStruct((rows, total), BF16),
         scratch_shapes=[pltpu.VMEM((rows, total), F32)],
-        compiler_params=pltpu.CompilerParams(vmem_limit_bytes=40 * 2**20),
+        compiler_params=pltpu.CompilerParams(vmem_limit_bytes=18 * 2**20),
         cost_estimate=pl.CostEstimate(
             flops=rows * feats * total // 8,
             bytes_accessed=feats * (total + rows) // 8,
@@ -182,42 +184,35 @@
     at_end = (row == 0) | (row == planes - 1)
     flags = jnp.stack([at_end.astype(jnp.int32), group.astype(jnp.int32)])
 
+    half, flat = dirs // sides, grads.reshape(cands * tok, feats)
+    units, deep, slab = 8, feats // 8, cands * tok // 8
     lengths = candidate_lengths(example_ids, token_counts)
     local_act = local_activations(acts, act_basis, lengths)
     every_act = lax.all_gather(local_act, "row", axis=0)
-
-    half, flat = dirs // sides, grads.reshape(cands * tok, feats)
-    units, deep, slab = 8, feats // 8, cands * tok // 8
     near, far, other = [], [], []
     spans = [(0, 1), (1, 3), (3, 5), (5, 7), (7, units)]
-    batches = [(0, 1), (2,), (3, 4)]
-    ranges = [(spans[x[0]][0] * slab, spans[x[-1]][1] * slab) for x in batches]
-    own_own = project(flags, [(flat, 0, cands * tok)], [grad_basis])
+    own_own = project(flags, [(flat, 0, cands * tok)], [], [grad_basis])
     for i, (a, b) in enumerate(spans):
         piece = lax.dynamic_slice(grad_basis, (a * deep, group * half), ((b - a) * deep, half))
         if i >= 2:
-            early = [own_own, local_act] if i == 2 else [other[i - 3]]
+            early = {2: [own_own, local_act], 3: [other[0]], 4: [every_act]}[i]
             piece = after(piece, near[i - 2], *early)
-        if i < len(ranges):
-            rows = flat[slice(*ranges[i])]
-            other.append(lax.ppermute(after(rows, near[i - 1]) if i else rows, "row", middle))
+        if i in (0, 2):
+            part = flat[: 4 * slab] if i == 0 else after(flat[4 * slab :], near[0])
+            other.append(lax.ppermute(part, "row", middle))
         near.append(lax.ppermute(piece, "row", beside))
         far.append(lax.ppermute(near[i], "groups", [(0, 1), (1, 0)]))
     near_basis = jnp.concatenate(near, axis=0)
     far_basis = jnp.concatenate(far, axis=0)
-
-    ties = {0: [near[3], far[1]], 1: [near[3], far[2]], 2: [near[4], other[2]]}
+    own_end = project(flags, [(flat, 0, cands * tok)], [], [near_basis, far_basis])
+
+    ranges = [(0, 3), (3, 5), (5, 7), (7, units)]
+    ready = [near[4], far[2], *other]
     partner = []
-    for k, (a, b) in enumerate(spans):
-        tie = ties.get(k, []) + ([partner[k - 2]] if k >= 2 else [])
+    for k, (a, b) in enumerate(ranges):
+        tie = [ready, ready, [own_end], []][k] + ([partner[k - 2]] if k >= 2 else [])
         piece = flat[a * slab : b * slab]
         partner.append(lax.ppermute(after(piece, *tie), "row", ends))
-    own_end = project(flags, [(flat, 0, cands * tok)], [near_basis, after(far_basis, partner[0])])
-    products = []
-    for batch, inner, (first, last) in zip(batches, other, ranges):
-        tokens = [(partner[k], 0, (spans[k][1] - spans[k][0]) * slab) for k in batch]
-        tokens.append((inner, 0, last - first))
-        products.append(project(flags, tokens, [grad_basis, near_basis, far_basis]))
 
     def scatter_sum(value):
         value = value.reshape(parts, -1, 2 * dirs)
@@ -232,10 +227,11 @@
         lax.dynamic_index_in_dim(every_act, i, 0, keepdims=False)
         for i in (row, row ^ 1, planes - 1 - row, planes - 1 - (row ^ 1))
     ]
-    arrays, segments, act_order = [], [[] for _ in range(cands)], [[] for _ in range(cands)]
+    sums, arrays, segments, act_order = [], [], [[] for _ in range(cands)], [[] for _ in range(cands)]
 
     def place(value, start, sources):
-        every = lax.all_gather(scatter_sum(value), "col", axis=0)
+        sums.append(scatter_sum(value))
+        every = lax.all_gather(sums[-1], "col", axis=0)
         n = every.shape[2]
         for p in range(parts):
             for j, source in enumerate(sources):
@@ -249,8 +245,15 @@
         arrays.append(every.reshape(parts * 2 * n, dirs))
 
     place(jnp.concatenate([own_own, own_end], axis=1), 0, act[:2])
-    for (first, _), product in zip(ranges, products):
-        place(product, first, act[2:])
+    batches = [
+        ((0,), [(other[0], 0, 3 * slab)], []),
+        ((1,), [(other[0], 3 * slab, slab), (other[1], 0, slab)], arrays[:1]),
+        ((2, 3), [(other[1], slab, slab), (other[1], 2 * slab, 2 * slab)], arrays),
+    ]
+    for batch, middles, earlier in batches:
+        tokens = [(partner[k], 0, (ranges[k][1] - ranges[k][0]) * slab) for k in batch]
+        product = project(flags, tokens, middles, [grad_basis, near_basis, after(far_basis, *earlier)])
+        place(product, ranges[batch[0]][0] * slab, act[2:])
     act_rot = jnp.stack([jnp.concatenate(x, axis=0) for x in act_order])
     layout = tuple(tuple(s) for s in segments)
     rotated, scores = rotate_and_score(arrays, layout, act_rot, eigenvalues, query_rotated)

time: 513 us -> 597 us (1.16)
  waiting for transfers between devices: 180 us -> 335 us
  starting transfers between devices: 146 us -> 66.4 us
  local copies, waits for them, and re-layouts: 52.1 us -> 78.2 us
  Pallas kernels: 76.2 us -> 66.2 us
    ppermute x5 -> x4, starting transfers between devices: 92 us -> 16.5 us  [chain_body(): partner.append(lax.ppermute(after(piece, *tie), 'row', ends))]
    ppermute x4, waiting for transfers between devices: 27.8 us -> 100 us  [scatter_sum(): lax.ppermute(total[:, dirs:], 'row', beside)]
    ppermute x5, waiting for transfers between devices: 0.01 us -> 51.6 us  [chain_body(): far.append(lax.ppermute(near[i], 'groups', [(0, 1), (1, 0)]))]
    unnamed x78 -> x68, local copies, waits for them, and re-layouts: 31.6 us -> 50.1 us
    ppermute x5, waiting for transfers between devices: 117 us -> 135 us  [chain_body(): near.append(lax.ppermute(piece, 'row', beside))]
    ppermute x12, waiting for transfers between devices: 17.4 us -> 31.3 us  [scatter_sum(): lax.ppermute(sent, 'col', [(i, i ^ d) for i in range(parts)]).astype(F32)]
    pallas_call x5, Pallas kernels: 71.9 us -> 61.9 us  [project(): pl.pallas_call(functools.partial(project_kernel, len(ends), len(tokens),...]
    slice x2 -> x3, local copies, waits for them, and re-layouts: 4.39 us -> 10.7 us  [chain_body(): piece = flat[a * slab:b * slab]]
  transfers between devices with their start and end apart: 42 -> 40, of which waited for: 16 -> 21; matrix products, arithmetic and copies ran while one was open for 8% -> 10% of each run, Pallas kernels for 14% -> 8%
where the time goes in v7:
time: 597 us; the launch traced here: 595 us
  waiting for transfers between devices  335 us (56%)
  local copies, waits for them, and re-layouts  78.2 us (13%)
  starting transfers between devices  66.4 us (11%)
  Pallas kernels  66.2 us (11%)
  blocking collectives  23.9 us (4%)
  between operations  14.5 us (2%)
  matrix products  6.46 us (1%)
    ppermute x5, waiting for transfers between devices, chain_body(): near.append(lax.ppermute(piece, 'row', beside))  135 us
    ppermute x4, waiting for transfers between devices, scatter_sum(): lax.ppermute(total[:, dirs:], 'row', beside)  100 us
    pallas_call x5, Pallas kernels, project(): pl.pallas_call(functools.partial(project_kernel, len(ends), len(tokens),...  61.9 us
    ppermute x5, waiting for transfers between devices, chain_body(): far.append(lax.ppermute(near[i], 'groups', [(0, 1), (1, 0)]))  51.6 us
    unnamed x68, local copies, waits for them, and re-layouts  50.1 us
    ppermute x12, waiting for transfers between devices, scatter_sum(): lax.ppermute(sent, 'col', [(i, i ^ d) for i in range(parts)]).astype(F32)  31.3 us
    all_gather x3, blocking collectives, place(): every = lax.all_gather(sums[-1], 'col', axis=0)  23.9 us
    ppermute x5, starting transfers between devices, chain_body(): near.append(lax.ppermute(piece, 'row', beside))  22.8 us
  transfers between devices with their start and end apart: 40, of which 21 were waited for; matrix products, arithmetic and copies ran while one was open for 10% of the time, Pallas kernels for 8%

profile of v7, /device:TPU:0, one launch (start us, length us, event | category | flops | bytes accessed | tf_op | source)
XLA Modules:
  0.0 595.3 jit_solution(15463009145145063456)
XLA Ops:
  7.2 6.0 %fusion.21 = (bf16[2,128,8192]{2,1,0:T(8,128)(2,1)}, bf16[2,128,8192]{2,1,0:T(8,128)(2,1)}) fusion(bf16[4,128,8192]{2,1,0:T(8,128)(2,1)} %param.9), kind=kLoop, calls=%fused_computation.139 | loop fusion | bytes 16777216 | tf_op jit(solution)/shard_map/slice | solution.py:201
  13.2 2.7 collective-permute-start.3
  15.9 5.3 constant_dynamic-slice_fusion.2
  21.2 3.9 collective-permute-start.1
  25.1 3.1 constant_dynamic-slice_fusion.1
  28.2 5.8 copy-done
  34.0 3.4 copy-done.7
  37.4 11.9 %shard_map.95 = bf16[512,1024]{1,0:T(8,128)(2,1)S(1)} custom-call(s32[2]{0:T(128)S(1)} %pad_add_fusion.refs_0_, bf16[512,8192]{1,0:T(8,128)(2,1)S(1)} %bitcast.225, bf16[8192,1024]{1,0:T(8,128)(2,1)S(1)} %copy-done), custom_call_target="tpu_custom_call" | custom-call | flops 536870912 | bytes 1572864 | tf_op jit(solution)/shard_map/pallas_call | solution.py:148
  49.7 6.5 %fusion.5 = bf16[4,128,256]{2,1,0:T(8,128)(2,1)} fusion(bf16[4,128,8192]{2,1,0:T(8,128)(2,1)} %param.8, bf16[8192,256]{1,0:T(8,128)(2,1)S(1)} %copy-done.19, f32[4,128]{1,0:T(4,128)S(1)} %compare_convert_fusion), kind=kOutput, calls=%fused_computation.4 | convolution fusion | flops 2147745792 | bytes 12847104 | tf_op jit(solution)/shard_map/ctd,dk->ctk/dot_general | solution.py:25
  56.1 37.1 %collective-permute-done = bf16[1024,512]{1,0:T(8,128)(2,1)} collective-permute-done((bf16[1024,512]{1,0:T(8,128)(2,1)}, bf16[1024,512]{1,0:T(8,128)(2,1)}, u32[]{:S(2)}, u32[]{:S(2)}) %collective-permute-start) | collective-permute-done | bytes 1048608 | tf_op jit(solution)/shard_map/ppermute | solution.py:203
  93.2 1.7 collective-permute-start.2
  95.0 15.8 %collective-permute-start.4 = (bf16[2048,512]{1,0:T(8,128)(2,1)S(1)}, bf16[2048,512]{1,0:T(8,128)(2,1)}, u32[]{:S(2)}, u32[]{:S(2)}) collective-permute-start(bf16[2048,512]{1,0:T(8,128)(2,1)S(1)} %get-tuple-element.15), channel_id=1, source_target_pairs={{0,4},{4,0},{8,12},{12,8},{1,5},{5,1},{9,13},{13,9},{2,6},{6,2},{1... | collective-permute-start | bytes 6291464 | tf_op jit(solution)/shard_map/ppermute | solution.py:203
  110.9 2.7 collective-permute-start.15
  113.5 1.5 collective-permute-start.6
  115.6 43.4 %collective-permute-done.2 = bf16[2048,512]{1,0:T(8,128)(2,1)} collective-permute-done((bf16[2048,512]{1,0:T(8,128)(2,1)}, bf16[2048,512]{1,0:T(8,128)(2,1)}, u32[]{:S(2)}, u32[]{:S(2)}) %collective-permute-start.2) | collective-permute-done | bytes 2097184 | tf_op jit(solution)/shard_map/ppermute | solution.py:203
  159.0 1.6 collective-permute-start.8
  160.5 41.3 %collective-permute-done.4 = bf16[2048,512]{1,0:T(8,128)(2,1)} collective-permute-done((bf16[2048,512]{1,0:T(8,128)(2,1)S(1)}, bf16[2048,512]{1,0:T(8,128)(2,1)}, u32[]{:S(2)}, u32[]{:S(2)}) %collective-permute-start.4) | collective-permute-done | bytes 2097184 | tf_op jit(solution)/shard_map/ppermute | solution.py:203
  201.8 1.6 collective-permute-start.9
  203.4 4.6 fusion.20
  208.0 3.9 slice.218
  211.8 2.3 slice.225
  214.1 1.4 collective-permute-start.5
  216.9 1.6 constant_dynamic-update-slice_fusion.17
  220.9 1.7 constant_dynamic-update-slice_fusion.3
  222.7 1.7 constant_dynamic-update-slice_fusion.2
  224.4 12.8 %collective-permute-done.5 = bf16[1024,512]{1,0:T(8,128)(2,1)S(1)} collective-permute-done((bf16[1024,512]{1,0:T(8,128)(2,1)}, bf16[1024,512]{1,0:T(8,128)(2,1)S(1)}, u32[]{:S(2)}, u32[]{:S(2)}) %collective-permute-start.5) | collective-permute-done | bytes 1048608 | tf_op jit(solution)/shard_map/ppermute | solution.py:203
  237.6 1.7 constant_dynamic-update-slice_fusion.8
  239.4 1.9 constant_dynamic-update-slice_fusion.7
  241.3 1.7 constant_dynamic-update-slice_fusion.1
  243.1 31.6 %collective-permute-done.9 = bf16[2048,512]{1,0:T(8,128)(2,1)S(1)} collective-permute-done((bf16[2048,512]{1,0:T(8,128)(2,1)}, bf16[2048,512]{1,0:T(8,128)(2,1)S(1)}, u32[]{:S(2)}, u32[]{:S(2)}) %collective-permute-start.9) | collective-permute-done | bytes 2097184 | tf_op jit(solution)/shard_map/ppermute | solution.py:204
  274.8 20.0 %collective-permute-done.10 = bf16[1024,512]{1,0:T(8,128)(2,1)S(1)} collective-permute-done((bf16[1024,512]{1,0:T(8,128)(2,1)S(1)}, bf16[1024,512]{1,0:T(8,128)(2,1)S(1)}, u32[]{:S(2)}, u32[]{:S(2)}) %collective-permute-start.10) | collective-permute-done | bytes 1048608 | tf_op jit(solution)/shard_map/ppermute | solution.py:204
  294.9 12.1 %shard_map.96 = bf16[512,1024]{1,0:T(8,128)(2,1)S(1)} custom-call(s32[2]{0:T(128)S(1)} %pad_add_fusion.refs_0_, bf16[512,8192]{1,0:T(8,128)(2,1)S(1)} %bitcast.228, bf16[8192,512]{1,0:T(8,128)(2,1)S(1)} %constant_dynamic-update-slice_fusion.refs_2_.refs_4_.refs_5_.refs_6_, ...), custom_call_target="tpu_custom_call" | custom-call | flops 536870912 | bytes 1572864 | tf_op jit(solution)/shard_map/pallas_call | solution.py:148
  307.5 1.6 collective-permute-start.12
  309.3 1.6 constant_dynamic-update-slice_fusion.16
  312.2 4.4 collective-permute-start.16
  316.6 5.1 collective-permute-done.13
  321.6 11.3 %collective-permute-done.12 = bf16[128,2048]{1,0:T(8,128)(2,1)S(1)} collective-permute-done((bf16[128,2048]{1,0:T(8,128)(2,1)S(1)}, bf16[128,2048]{1,0:T(8,128)(2,1)S(1)}, u32[]{:S(2)}, u32[]{:S(2)}) %collective-permute-start.12) | collective-permute-done | bytes 524320 | tf_op jit(solution)/shard_map/ppermute | solution.py:222
  335.4 56.5 %collective-permute-done.14 = bf16[128,1024]{1,0:T(8,128)(2,1)S(1)} collective-permute-done((bf16[128,1024]{1,0:T(8,128)(2,1)S(1)}, bf16[128,1024]{1,0:T(8,128)(2,1)S(1)}, u32[]{:S(2)}, u32[]{:S(2)}) %collective-permute-start.14) | collective-permute-done | bytes 262176 | tf_op jit(solution)/shard_map/ppermute | solution.py:224
  396.7 1.4 constant_dynamic-update-slice_fusion.11
  398.1 4.5 collective-permute-start.21
  406.7 3.4 copy-done.2
  410.1 3.4 copy-done.5
  413.5 12.9 %shard_map.97 = bf16[192,2048]{1,0:T(8,128)(2,1)S(1)} custom-call(s32[2]{0:T(128)S(1)} %pad_add_fusion.refs_0_, bf16[192,8192]{1,0:T(8,128)(2,1)S(1)} %collective-permute-done.16.refs_1_, bf16[256,8192]{1,0:T(8,128)(2,1)} %collective-permute-done.3.refs_2_, bf16[8192,1024]{1,0:T(8,128)(2,1)} %refs_5_.2, bf16[8192,512]{1,0:T(8,128)(2,1)S(1)} %copy-done.5, ...), custom_call_target="tpu_custom_call" | custom-call | flops 402653184 | bytes 2293760 | tf_op jit(solution)/shard_map/pallas_call | solution.py:148
  429.0 3.2 collective-permute-start.26
  432.3 1.5 collective-permute-done.19
  433.7 4.1 collective-permute-done.18
  438.6 12.1 %collective-permute-done.21.refs_1_ = bf16[128,8192]{1,0:T(8,128)(2,1)} collective-permute-done((bf16[128,8192]{1,0:T(8,128)(2,1)}, bf16[128,8192]{1,0:T(8,128)(2,1)}, u32[]{:S(2)}, u32[]{:S(2)}) %collective-permute-start.21) | collective-permute-done | bytes 2097184 | tf_op jit(solution)/shard_map/ppermute | solution.py:215
  450.7 3.4 copy-done.3
  454.1 3.4 copy-done.6
  457.5 11.8 %shard_map.98 = bf16[128,2048]{1,0:T(8,128)(2,1)S(1)} custom-call(s32[2]{0:T(128)S(1)} %pad_add_fusion.refs_0_, bf16[128,8192]{1,0:T(8,128)(2,1)} %collective-permute-done.21.refs_1_, bf16[256,8192]{1,0:T(8,128)(2,1)} %collective-permute-done.3.refs_2_, bf16[256,8192]{1,0:T(8,128)(2,1)} %collective-permute-done.15.refs_3_.refs_4_, ...), custom_call_target="tpu_custom_call" | custom-call | flops 268435456 | bytes 2228224 | tf_op jit(solution)/shard_map/pallas_call | solution.py:148
  471.9 24.8 %collective-permute-done.20 = bf16[48,1024]{1,0:T(8,128)(2,1)} collective-permute-done((bf16[48,1024]{1,0:T(8,128)(2,1)}, bf16[48,1024]{1,0:T(8,128)(2,1)}, u32[]{:S(2)}, u32[]{:S(2)}) %collective-permute-start.20) | collective-permute-done | bytes 98336 | tf_op jit(solution)/shard_map/ppermute | solution.py:224
  496.8 4.4 collective-permute-start.27
  502.3 8.5 %all-gather.2 = bf16[8,48,1024]{2,1,0:T(8,128)(2,1)S(1)} all-gather(bf16[2,48,1024]{2,1,0:T(8,128)(2,1)S(1)} %pad_maximum_fusion.3), channel_id=4, replica_groups=mesh['groups'=2,'row'=4,'col'=4] {'col'}, dimensions={0}, use_global_device_ids=true | all-gather | bytes 983040 | tf_op jit(solution)/shard_map/all_gather | solution.py:234
  510.7 16.2 %collective-permute-done.25 = bf16[32,1024]{1,0:T(8,128)(2,1)S(1)} collective-permute-done((bf16[32,1024]{1,0:T(8,128)(2,1)S(1)}, bf16[32,1024]{1,0:T(8,128)(2,1)S(1)}, u32[]{:S(2)}, u32[]{:S(2)}) %collective-permute-start.25) | collective-permute-done | bytes 65568 | tf_op jit(solution)/shard_map/ppermute | solution.py:224
  527.0 7.0 %all-gather.3 = bf16[8,32,1024]{2,1,0:T(8,128)(2,1)S(1)} all-gather(bf16[2,32,1024]{2,1,0:T(8,128)(2,1)S(1)} %pad_maximum_fusion.5), channel_id=5, replica_groups=mesh['groups'=2,'row'=4,'col'=4] {'col'}, dimensions={0}, use_global_device_ids=true | all-gather | bytes 655360 | tf_op jit(solution)/shard_map/all_gather | solution.py:234
  534.0 13.2 %shard_map.99 = bf16[192,2048]{1,0:T(8,128)(2,1)S(1)} custom-call(s32[2]{0:T(128)S(1)} %pad_add_fusion.refs_0_, bf16[128,8192]{1,0:T(8,128)(2,1)S(1)} %collective-permute-done.26.refs_1_, bf16[64,8192]{1,0:T(8,128)(2,1)S(1)} %collective-permute-done.27.refs_2_, bf16[256,8192]{1,0:T(8,128)(2,1)} %collective-permute-done.15.refs_3_.refs_4_, ...), custom_call_target="tpu_custom_call" | custom-call | flops 402653184 | bytes 2293760 | tf_op jit(solution)/shard_map/pallas_call | solution.py:148
  549.3 4.8 collective-permute-done.30
  554.1 4.7 collective-permute-done.29
  560.8 2.8 collective-permute-done.31
  563.6 8.4 %all-gather.4 = bf16[8,48,1024]{2,1,0:T(8,128)(2,1)S(1)} all-gather(bf16[2,48,1024]{2,1,0:T(8,128)(2,1)S(1)} %pad_maximum_fusion.4), channel_id=6, replica_groups=mesh['groups'=2,'row'=4,'col'=4] {'col'}, dimensions={0}, use_global_device_ids=true | all-gather | bytes 983040 | tf_op jit(solution)/shard_map/all_gather | solution.py:234
  572.0 4.3 shard_map.100
  580.8 2.5 collective-permute-start.37
  583.4 1.9 collective-permute-start.35
  586.3 1.6 collective-permute-done.36
  (134 shorter events, 36.0 us)
Async XLA Ops:
  7.2 207.0 %all-gather.8.cloned.1.call-start = ((), (), s32[]{:S(2)}) async-start(), calls=%async_computation | async-start | bytes 1310720 | tf_op jit(solution)/shard_map/all_gather | solution.py:191
  13.2 81.7 %collective-permute-start.3 = (bf16[256,8192]{1,0:T(8,128)(2,1)}, bf16[256,8192]{1,0:T(8,128)(2,1)}, u32[]{:S(2)}, u32[]{:S(2)}) collective-permute-start(bf16[256,8192]{1,0:T(8,128)(2,1)} %bitcast.4), channel_id=1, source_target_pairs={{4,8},{8,4},{5,9},{9,5},{6,10},{10,6},{7,11},{11,7},{20,24},{24,20... | collective-permute-start | bytes 12582920 | tf_op jit(solution)/shard_map/ppermute | solution.py:202
  21.2 73.7 %collective-permute-start.1 = (bf16[2048,512]{1,0:T(8,128)(2,1)}, bf16[2048,512]{1,0:T(8,128)(2,1)}, u32[]{:S(2)}, u32[]{:S(2)}) collective-permute-start(bf16[2048,512]{1,0:T(8,128)(2,1)} %get-tuple-element.30), channel_id=1, source_target_pairs={{0,4},{4,0},{8,12},{12,8},{1,5},{5,1},{9,13},{13,9},{2,6},{6,2},{1... | collective-permute-start | bytes 6291464 | tf_op jit(solution)/shard_map/ppermute | solution.py:203
  28.2 65.1 %collective-permute-start = (bf16[1024,512]{1,0:T(8,128)(2,1)}, bf16[1024,512]{1,0:T(8,128)(2,1)}, u32[]{:S(2)}, u32[]{:S(2)}) collective-permute-start(bf16[1024,512]{1,0:T(8,128)(2,1)} %get-tuple-element.27), channel_id=1, source_target_pairs={{0,4},{4,0},{8,12},{12,8},{1,5},{5,1},{9,13},{13,9},{2,6},{6,2},{1... | collective-permute-start | bytes 3145736 | tf_op jit(solution)/shard_map/ppermute | solution.py:203
  28.2 5.8 copy-start
  34.0 3.4 copy-start.7
  37.4 12.0 %copy-start.17 = (s32[2048]{0:T(1024)S(1)}, s32[2048]{0:T(1024)}, u32[]{:S(2)}) copy-start(s32[2048]{0:T(1024)} %param.15) | copy-start | bytes 24580
  37.4 12.0 %copy-start.18 = (s32[4]{0:T(128)S(1)}, s32[4]{0:T(128)}, u32[]{:S(2)}) copy-start(s32[4]{0:T(128)} %param.14) | copy-start | bytes 52
  37.4 12.3 %copy-start.19 = (bf16[8192,256]{1,0:T(8,128)(2,1)S(1)}, bf16[8192,256]{1,0:T(8,128)(2,1)}, u32[]{:S(2)}) copy-start(bf16[8192,256]{1,0:T(8,128)(2,1)} %param.10) | copy-start | bytes 12582916
  93.2 65.7 %collective-permute-start.2 = (bf16[2048,512]{1,0:T(8,128)(2,1)}, bf16[2048,512]{1,0:T(8,128)(2,1)}, u32[]{:S(2)}, u32[]{:S(2)}) collective-permute-start(bf16[2048,512]{1,0:T(8,128)(2,1)} %get-tuple-element.14), channel_id=1, source_target_pairs={{0,4},{4,0},{8,12},{12,8},{1,5},{5,1},{9,13},{13,9},{2,6},{6,2},{1... | collective-permute-start | bytes 6291464 | tf_op jit(solution)/shard_map/ppermute | solution.py:203
  95.0 106.9 %collective-permute-start.4 = (bf16[2048,512]{1,0:T(8,128)(2,1)S(1)}, bf16[2048,512]{1,0:T(8,128)(2,1)}, u32[]{:S(2)}, u32[]{:S(2)}) collective-permute-start(bf16[2048,512]{1,0:T(8,128)(2,1)S(1)} %get-tuple-element.15), channel_id=1, source_target_pairs={{0,4},{4,0},{8,12},{12,8},{1,5},{5,1},{9,13},{13,9},{2,6},{6,2},{1... | collective-permute-start | bytes 6291464 | tf_op jit(solution)/shard_map/ppermute | solution.py:203
  110.8 327.8 %all-gather.10.cloned.1.call-start = ((), (), s32[]{:S(2)}) async-start(), calls=%async_computation.1 | async-start | bytes 2621440 | tf_op jit(solution)/shard_map/all_gather | solution.py:234
  110.9 201.3 %collective-permute-start.15 = (bf16[256,8192]{1,0:T(8,128)(2,1)}, bf16[256,8192]{1,0:T(8,128)(2,1)}, u32[]{:S(2)}, u32[]{:S(2)}) collective-permute-start(bf16[256,8192]{1,0:T(8,128)(2,1)} %bitcast.241), channel_id=1, source_target_pairs={{4,8},{8,4},{5,9},{9,5},{6,10},{10,6},{7,11},{11,7},{20,24},{24,20... | collective-permute-start | bytes 12582920 | tf_op jit(solution)/shard_map/ppermute | solution.py:202
  113.5 100.6 %collective-permute-start.6 = (bf16[1024,512]{1,0:T(8,128)(2,1)}, bf16[1024,512]{1,0:T(8,128)(2,1)}, u32[]{:S(2)}, u32[]{:S(2)}) collective-permute-start(bf16[1024,512]{1,0:T(8,128)(2,1)} %collective-permute-done), channel_id=1, source_target_pairs={{0,16},{16,0},{1,17},{17,1},{2,18},{18,2},{3,19},{19,3},{4,20},{20... | collective-permute-start | bytes 3145736 | tf_op jit(solution)/shard_map/ppermute | solution.py:204
  115.1 122.6 %collective-permute-start.7 = (bf16[2048,512]{1,0:T(8,128)(2,1)}, bf16[2048,512]{1,0:T(8,128)(2,1)}, u32[]{:S(2)}, u32[]{:S(2)}) collective-permute-start(bf16[2048,512]{1,0:T(8,128)(2,1)} %collective-permute-done.1), channel_id=1, source_target_pairs={{0,16},{16,0},{1,17},{17,1},{2,18},{18,2},{3,19},{19,3},{4,20},{20... | collective-permute-start | bytes 6291464 | tf_op jit(solution)/shard_map/ppermute | solution.py:204
  159.0 80.4 %collective-permute-start.8 = (bf16[2048,512]{1,0:T(8,128)(2,1)}, bf16[2048,512]{1,0:T(8,128)(2,1)}, u32[]{:S(2)}, u32[]{:S(2)}) collective-permute-start(bf16[2048,512]{1,0:T(8,128)(2,1)} %collective-permute-done.2), channel_id=1, source_target_pairs={{0,16},{16,0},{1,17},{17,1},{2,18},{18,2},{3,19},{19,3},{4,20},{20... | collective-permute-start | bytes 6291464 | tf_op jit(solution)/shard_map/ppermute | solution.py:204
  201.8 72.9 %collective-permute-start.9 = (bf16[2048,512]{1,0:T(8,128)(2,1)}, bf16[2048,512]{1,0:T(8,128)(2,1)S(1)}, u32[]{:S(2)}, u32[]{:S(2)}) collective-permute-start(bf16[2048,512]{1,0:T(8,128)(2,1)} %collective-permute-done.4), channel_id=1, source_target_pairs={{0,16},{16,0},{1,17},{17,1},{2,18},{18,2},{3,19},{19,3},{4,20},{20... | collective-permute-start | bytes 6291464 | tf_op jit(solution)/shard_map/ppermute | solution.py:204
  214.1 23.0 %collective-permute-start.5 = (bf16[1024,512]{1,0:T(8,128)(2,1)}, bf16[1024,512]{1,0:T(8,128)(2,1)S(1)}, u32[]{:S(2)}, u32[]{:S(2)}) collective-permute-start(bf16[1024,512]{1,0:T(8,128)(2,1)} %get-tuple-element.16), channel_id=1, source_target_pairs={{0,4},{4,0},{8,12},{12,8},{1,5},{5,1},{9,13},{13,9},{2,6},{6,2},{1... | collective-permute-start | bytes 3145736 | tf_op jit(solution)/shard_map/ppermute | solution.py:203
  219.5 92.0 %copy-start.11 = (bf16[4,128,256]{2,1,0:T(8,128)(2,1)}, bf16[4,128,256]{2,1,0:T(8,128)(2,1)S(1)}, u32[]{:S(2)}) copy-start(bf16[4,128,256]{2,1,0:T(8,128)(2,1)S(1)} %get-tuple-element.47) | copy-start | bytes 786436
  237.2 57.6 %collective-permute-start.10 = (bf16[1024,512]{1,0:T(8,128)(2,1)S(1)}, bf16[1024,512]{1,0:T(8,128)(2,1)S(1)}, u32[]{:S(2)}, u32[]{:S(2)}) collective-permute-start(bf16[1024,512]{1,0:T(8,128)(2,1)S(1)} %collective-permute-done.5), channel_id=1, source_target_pairs={{0,16},{16,0},{1,17},{17,1},{2,18},{18,2},{3,19},{19,3},{4,20},{20... | collective-permute-start | bytes 3145736 | tf_op jit(solution)/shard_map/ppermute | solution.py:204
  239.4 55.5 %slice-start = ((s8[8388608]{0:T(1024)(128)(4,1)}), s8[4194304]{0:T(1024)(128)(4,1)S(1)}, s32[]{:S(2)}) async-start(s8[8388608]{0:T(1024)(128)(4,1)} %bitcast.226), calls=%async_computation.2 | async-start | bytes 8388608
  243.0 51.9 %slice-start.1 = ((s8[8388608]{0:T(1024)(128)(4,1)}), s8[4194304]{0:T(1024)(128)(4,1)S(1)}, s32[]{:S(2)}) async-start(s8[8388608]{0:T(1024)(128)(4,1)} %bitcast.226), calls=%async_computation.3 | async-start | bytes 8388608
  243.1 64.0 %copy-start.4 = (bf16[8192,512]{1,0:T(8,128)(2,1)}, bf16[8192,512]{1,0:T(8,128)(2,1)S(1)}, u32[]{:S(2)}) copy-start(bf16[8192,512]{1,0:T(8,128)(2,1)S(1)} %constant_dynamic-update-slice_fusion.refs_2_.refs_4_.refs_5_.refs_6_) | copy-start | bytes 25165828
  294.9 12.2 %copy-start.1 = (bf16[8192,512]{1,0:T(8,128)(2,1)}, bf16[8192,512]{1,0:T(8,128)(2,1)S(1)}, u32[]{:S(2)}) copy-start(bf16[8192,512]{1,0:T(8,128)(2,1)S(1)} %constant_dynamic-update-slice_fusion.5.refs_3_.refs_5_.refs_6_.refs_7_) | copy-start | bytes 25165828
  307.4 14.2 %collective-permute-start.13 = (bf16[128,2048]{1,0:T(8,128)(2,1)S(1)}, bf16[128,2048]{1,0:T(8,128)(2,1)S(1)}, u32[]{:S(2)}, u32[]{:S(2)}) collective-permute-start(bf16[128,2048]{1,0:T(8,128)(2,1)S(1)} %get-tuple-element.36), channel_id=1, source_target_pairs={{0,3},{1,2},{2,1},{3,0},{4,7},{5,6},{6,5},{7,4},{8,11},{9,10},{10,... | collective-permute-start | bytes 1572872 | tf_op jit(solution)/shard_map/ppermute | solution.py:222
  307.5 25.4 %collective-permute-start.12 = (bf16[128,2048]{1,0:T(8,128)(2,1)S(1)}, bf16[128,2048]{1,0:T(8,128)(2,1)S(1)}, u32[]{:S(2)}, u32[]{:S(2)}) collective-permute-start(bf16[128,2048]{1,0:T(8,128)(2,1)S(1)} %get-tuple-element.37), channel_id=1, source_target_pairs={{0,2},{1,3},{2,0},{3,1},{4,6},{5,7},{6,4},{7,5},{8,10},{9,11},{10,... | collective-permute-start | bytes 1572872 | tf_op jit(solution)/shard_map/ppermute | solution.py:222
  309.0 23.9 %collective-permute-start.11 = (bf16[128,2048]{1,0:T(8,128)(2,1)S(1)}, bf16[128,2048]{1,0:T(8,128)(2,1)S(1)}, u32[]{:S(2)}, u32[]{:S(2)}) collective-permute-start(bf16[128,2048]{1,0:T(8,128)(2,1)S(1)} %get-tuple-element.35), channel_id=1, source_target_pairs={{0,1},{1,0},{2,3},{3,2},{4,5},{5,4},{6,7},{7,6},{8,9},{9,8},{10,11... | collective-permute-start | bytes 1572872 | tf_op jit(solution)/shard_map/ppermute | solution.py:222
  310.9 22.4 %copy-start.13 = (bf16[512,256]{1,0:T(8,128)(2,1)}, bf16[512,256]{1,0:T(8,128)(2,1)S(1)}, u32[]{:S(2)}) copy-start(bf16[512,256]{1,0:T(8,128)(2,1)S(1)} %get-tuple-element.39) | copy-start | bytes 786436
  310.9 22.4 %copy-start.15 = (bf16[512,256]{1,0:T(8,128)(2,1)}, bf16[512,256]{1,0:T(8,128)(2,1)S(1)}, u32[]{:S(2)}) copy-start(bf16[512,256]{1,0:T(8,128)(2,1)S(1)} %get-tuple-element.41) | copy-start | bytes 786436
  312.2 94.5 %collective-permute-start.16 = (bf16[192,8192]{1,0:T(8,128)(2,1)}, bf16[192,8192]{1,0:T(8,128)(2,1)S(1)}, u32[]{:S(2)}, u32[]{:S(2)}) collective-permute-start(bf16[192,8192]{1,0:T(8,128)(2,1)} %slice.218), channel_id=1, source_target_pairs={{0,12},{12,0},{1,13},{13,1},{2,14},{14,2},{3,15},{15,3},{16,28},{2... | collective-permute-start | bytes 9437192 | tf_op jit(solution)/shard_map/ppermute | solution.py:215
  333.3 58.6 %collective-permute-start.14 = (bf16[128,1024]{1,0:T(8,128)(2,1)S(1)}, bf16[128,1024]{1,0:T(8,128)(2,1)S(1)}, u32[]{:S(2)}, u32[]{:S(2)}) collective-permute-start(bf16[128,1024]{1,0:T(8,128)(2,1)S(1)} %get-tuple-element.58), channel_id=1, source_target_pairs={{0,4},{4,0},{8,12},{12,8},{1,5},{5,1},{9,13},{13,9},{2,6},{6,2},{1... | collective-permute-start | bytes 786440 | tf_op jit(solution)/shard_map/ppermute | solution.py:224
  398.1 52.6 %collective-permute-start.21 = (bf16[128,8192]{1,0:T(8,128)(2,1)}, bf16[128,8192]{1,0:T(8,128)(2,1)}, u32[]{:S(2)}, u32[]{:S(2)}) collective-permute-start(bf16[128,8192]{1,0:T(8,128)(2,1)} %get-tuple-element.19), channel_id=1, source_target_pairs={{0,12},{12,0},{1,13},{13,1},{2,14},{14,2},{3,15},{15,3},{16,28},{2... | collective-permute-start | bytes 6291464 | tf_op jit(solution)/shard_map/ppermute | solution.py:215
  406.7 3.4 copy-start.2
  410.1 3.4 copy-start.5
  426.5 7.3 %collective-permute-start.19 = (bf16[48,2048]{1,0:T(8,128)(2,1)S(1)}, bf16[48,2048]{1,0:T(8,128)(2,1)S(1)}, u32[]{:S(2)}, u32[]{:S(2)}) collective-permute-start(bf16[48,2048]{1,0:T(8,128)(2,1)S(1)} %get-tuple-element.52), channel_id=1, source_target_pairs={{0,3},{1,2},{2,1},{3,0},{4,7},{5,6},{6,5},{7,4},{8,11},{9,10},{10,... | collective-permute-start | bytes 589832 | tf_op jit(solution)/shard_map/ppermute | solution.py:222
  427.2 10.6 %collective-permute-start.18 = (bf16[48,2048]{1,0:T(8,128)(2,1)S(1)}, bf16[48,2048]{1,0:T(8,128)(2,1)S(1)}, u32[]{:S(2)}, u32[]{:S(2)}) collective-permute-start(bf16[48,2048]{1,0:T(8,128)(2,1)S(1)} %get-tuple-element.53), channel_id=1, source_target_pairs={{0,2},{1,3},{2,0},{3,1},{4,6},{5,7},{6,4},{7,5},{8,10},{9,11},{10,... | collective-permute-start | bytes 589832 | tf_op jit(solution)/shard_map/ppermute | solution.py:222
  427.9 9.9 %collective-permute-start.17 = (bf16[48,2048]{1,0:T(8,128)(2,1)S(1)}, bf16[48,2048]{1,0:T(8,128)(2,1)S(1)}, u32[]{:S(2)}, u32[]{:S(2)}) collective-permute-start(bf16[48,2048]{1,0:T(8,128)(2,1)S(1)} %get-tuple-element.51), channel_id=1, source_target_pairs={{0,1},{1,0},{2,3},{3,2},{4,5},{5,4},{6,7},{7,6},{8,9},{9,8},{10,11... | collective-permute-start | bytes 589832 | tf_op jit(solution)/shard_map/ppermute | solution.py:222
  429.0 105.0 %collective-permute-start.26 = (bf16[128,8192]{1,0:T(8,128)(2,1)}, bf16[128,8192]{1,0:T(8,128)(2,1)S(1)}, u32[]{:S(2)}, u32[]{:S(2)}) collective-permute-start(bf16[128,8192]{1,0:T(8,128)(2,1)} %get-tuple-element.21), channel_id=1, source_target_pairs={{0,12},{12,0},{1,13},{13,1},{2,14},{14,2},{3,15},{15,3},{16,28},{2... | collective-permute-start | bytes 6291464 | tf_op jit(solution)/shard_map/ppermute | solution.py:215
  438.6 58.2 %collective-permute-start.20 = (bf16[48,1024]{1,0:T(8,128)(2,1)}, bf16[48,1024]{1,0:T(8,128)(2,1)}, u32[]{:S(2)}, u32[]{:S(2)}) collective-permute-start(bf16[48,1024]{1,0:T(8,128)(2,1)} %get-tuple-element.82), channel_id=1, source_target_pairs={{0,4},{4,0},{8,12},{12,8},{1,5},{5,1},{9,13},{13,9},{2,6},{6,2},{1... | collective-permute-start | bytes 294920 | tf_op jit(solution)/shard_map/ppermute | solution.py:224
  450.7 3.4 copy-start.3
  454.1 3.4 copy-start.6
  457.5 13.7 %copy-start.14 = (bf16[512,256]{1,0:T(8,128)(2,1)S(1)}, bf16[512,256]{1,0:T(8,128)(2,1)}, u32[]{:S(2)}) copy-start(bf16[512,256]{1,0:T(8,128)(2,1)} %get-tuple-element.75) | copy-start | bytes 786436
  457.5 39.3 %copy-start.12 = (bf16[64,8192]{1,0:T(8,128)(2,1)S(1)}, bf16[64,8192]{1,0:T(8,128)(2,1)}, u32[]{:S(2)}) copy-start(bf16[64,8192]{1,0:T(8,128)(2,1)} %slice.225) | copy-start | bytes 3145732
  469.3 32.7 %collective-permute-start.24 = (bf16[32,2048]{1,0:T(8,128)(2,1)S(1)}, bf16[32,2048]{1,0:T(8,128)(2,1)S(1)}, u32[]{:S(2)}, u32[]{:S(2)}) collective-permute-start(bf16[32,2048]{1,0:T(8,128)(2,1)S(1)} %get-tuple-element.55), channel_id=1, source_target_pairs={{0,3},{1,2},{2,1},{3,0},{4,7},{5,6},{6,5},{7,4},{8,11},{9,10},{10,... | collective-permute-start | bytes 393224 | tf_op jit(solution)/shard_map/ppermute | solution.py:222
  469.4 32.7 %collective-permute-start.23 = (bf16[32,2048]{1,0:T(8,128)(2,1)S(1)}, bf16[32,2048]{1,0:T(8,128)(2,1)S(1)}, u32[]{:S(2)}, u32[]{:S(2)}) collective-permute-start(bf16[32,2048]{1,0:T(8,128)(2,1)S(1)} %get-tuple-element.56), channel_id=1, source_target_pairs={{0,2},{1,3},{2,0},{3,1},{4,6},{5,7},{6,4},{7,5},{8,10},{9,11},{10,... | collective-permute-start | bytes 393224 | tf_op jit(solution)/shard_map/ppermute | solution.py:222
  470.7 31.4 %collective-permute-start.22 = (bf16[32,2048]{1,0:T(8,128)(2,1)S(1)}, bf16[32,2048]{1,0:T(8,128)(2,1)S(1)}, u32[]{:S(2)}, u32[]{:S(2)}) collective-permute-start(bf16[32,2048]{1,0:T(8,128)(2,1)S(1)} %get-tuple-element.54), channel_id=1, source_target_pairs={{0,1},{1,0},{2,3},{3,2},{4,5},{5,4},{6,7},{7,6},{8,9},{9,8},{10,11... | collective-permute-start | bytes 393224 | tf_op jit(solution)/shard_map/ppermute | solution.py:222
  496.8 37.3 %collective-permute-start.27 = (bf16[64,8192]{1,0:T(8,128)(2,1)S(1)}, bf16[64,8192]{1,0:T(8,128)(2,1)S(1)}, u32[]{:S(2)}, u32[]{:S(2)}) collective-permute-start(bf16[64,8192]{1,0:T(8,128)(2,1)S(1)} %copy-done.12), channel_id=1, source_target_pairs={{0,12},{12,0},{1,13},{13,1},{2,14},{14,2},{3,15},{15,3},{16,28},{2... | collective-permute-start | bytes 3145736 | tf_op jit(solution)/shard_map/ppermute | solution.py:215
  502.2 24.8 %collective-permute-start.25 = (bf16[32,1024]{1,0:T(8,128)(2,1)S(1)}, bf16[32,1024]{1,0:T(8,128)(2,1)S(1)}, u32[]{:S(2)}, u32[]{:S(2)}) collective-permute-start(bf16[32,1024]{1,0:T(8,128)(2,1)S(1)} %get-tuple-element.84), channel_id=1, source_target_pairs={{0,4},{4,0},{8,12},{12,8},{1,5},{5,1},{9,13},{13,9},{2,6},{6,2},{1... | collective-permute-start | bytes 196616 | tf_op jit(solution)/shard_map/ppermute | solution.py:224
  534.0 25.6 %copy-start.16 = (bf16[512,256]{1,0:T(8,128)(2,1)S(1)}, bf16[512,256]{1,0:T(8,128)(2,1)}, u32[]{:S(2)}) copy-start(bf16[512,256]{1,0:T(8,128)(2,1)} %get-tuple-element.76) | copy-start | bytes 786436
  547.2 24.8 %copy-start.8 = (bf16[4,1024,256]{2,1,0:T(8,128)(2,1)S(1)}, bf16[4,1024,256]{2,1,0:T(8,128)(2,1)}, u32[]{:S(2)}) copy-start(bf16[4,1024,256]{2,1,0:T(8,128)(2,1)} %refs_6_.1) | copy-start | bytes 6291460
  547.2 24.8 %copy-start.9 = (bf16[8,128,1024]{2,1,0:T(8,128)(2,1)S(1)}, bf16[8,128,1024]{2,1,0:T(8,128)(2,1)}, u32[]{:S(2)}) copy-start(bf16[8,128,1024]{2,1,0:T(8,128)(2,1)} %all-gather.10.cloned.1.call-done) | copy-start | bytes 6291460
  547.2 24.8 %copy-start.10 = (f32[1024,256]{1,0:T(8,128)S(1)}, f32[1024,256]{1,0:T(8,128)}, u32[]{:S(2)}) copy-start(f32[1024,256]{1,0:T(8,128)} %refs_5_.3) | copy-start | bytes 3145732
  547.3 6.8 %collective-permute-start.30 = (bf16[48,2048]{1,0:T(8,128)(2,1)S(1)}, bf16[48,2048]{1,0:T(8,128)(2,1)S(1)}, u32[]{:S(2)}, u32[]{:S(2)}) collective-permute-start(bf16[48,2048]{1,0:T(8,128)(2,1)S(1)} %get-tuple-element.49), channel_id=1, source_target_pairs={{0,3},{1,2},{2,1},{3,0},{4,7},{5,6},{6,5},{7,4},{8,11},{9,10},{10,... | collective-permute-start | bytes 589832 | tf_op jit(solution)/shard_map/ppermute | solution.py:222
  548.6 10.2 %collective-permute-start.29 = (bf16[48,2048]{1,0:T(8,128)(2,1)S(1)}, bf16[48,2048]{1,0:T(8,128)(2,1)S(1)}, u32[]{:S(2)}, u32[]{:S(2)}) collective-permute-start(bf16[48,2048]{1,0:T(8,128)(2,1)S(1)} %get-tuple-element.50), channel_id=1, source_target_pairs={{0,2},{1,3},{2,0},{3,1},{4,6},{5,7},{6,4},{7,5},{8,10},{9,11},{10,... | collective-permute-start | bytes 589832 | tf_op jit(solution)/shard_map/ppermute | solution.py:222
  549.3 9.4 %collective-permute-start.28 = (bf16[48,2048]{1,0:T(8,128)(2,1)S(1)}, bf16[48,2048]{1,0:T(8,128)(2,1)S(1)}, u32[]{:S(2)}, u32[]{:S(2)}) collective-permute-start(bf16[48,2048]{1,0:T(8,128)(2,1)S(1)} %get-tuple-element.48), channel_id=1, source_target_pairs={{0,1},{1,0},{2,3},{3,2},{4,5},{5,4},{6,7},{7,6},{8,9},{9,8},{10,11... | collective-permute-start | bytes 589832 | tf_op jit(solution)/shard_map/ppermute | solution.py:222
  558.9 4.7 collective-permute-start.31
  576.5 3.0 collective-permute-start.34
  577.2 3.6 collective-permute-start.33
  578.5 2.3 collective-permute-start.32
  580.8 5.4 collective-permute-start.37
  583.4 4.5 collective-permute-start.36
  583.4 4.5 collective-permute-start.35
Sparse Core Ops, SparseCore 0:
  110.9 42.0 all-gather.7
  392.9 22.4 all-gather.9

commit v8 on v7

--- a/solution.py
+++ b/solution.py
@@ -195,7 +195,7 @@
     for i, (a, b) in enumerate(spans):
         piece = lax.dynamic_slice(grad_basis, (a * deep, group * half), ((b - a) * deep, half))
         if i >= 2:
-            early = {2: [own_own, local_act], 3: [other[0]], 4: [every_act]}[i]
+            early = {2: [own_own, local_act], 3: [other[0]], 4: []}[i]
             piece = after(piece, near[i - 2], *early)
         if i in (0, 2):
             part = flat[: 4 * slab] if i == 0 else after(flat[4 * slab :], near[0])
@@ -204,58 +204,74 @@
         far.append(lax.ppermute(near[i], "groups", [(0, 1), (1, 0)]))
     near_basis = jnp.concatenate(near, axis=0)
     far_basis = jnp.concatenate(far, axis=0)
-    own_end = project(flags, [(flat, 0, cands * tok)], [], [near_basis, far_basis])
-
-    ranges = [(0, 3), (3, 5), (5, 7), (7, units)]
-    ready = [near[4], far[2], *other]
+
+    ranges = [(0, 2), (2, 4), (4, units)]
+    ties = [[near[4], far[1], other[1]], [near[4], far[2], other[1]], []]
     partner = []
     for k, (a, b) in enumerate(ranges):
-        tie = [ready, ready, [own_end], []][k] + ([partner[k - 2]] if k >= 2 else [])
+        tie = ties[k] + ([partner[k - 2]] if k >= 2 else [])
         piece = flat[a * slab : b * slab]
         partner.append(lax.ppermute(after(piece, *tie), "row", ends))
 
+    own_end = project(flags, [(flat, 0, cands * tok)], [], [near_basis, after(far_basis, partner[0])])
+    bases = [grad_basis, near_basis, far_basis]
+    sub, full = tok // parts, cands * tok
+    products = [
+        jnp.concatenate([own_own, own_end], axis=1),
+        project(flags, [(partner[0], 0, 2 * slab), (partner[1], 0, 2 * slab)], [(other[0], 0, full // 2)], bases),
+        project(flags, [(partner[2], 0, full // 2)], [(other[1], 0, full // 2)], bases),
+    ]
+
+    def swap(value, axis, d):
+        size = planes if axis == "row" else parts
+        return lax.ppermute(value, axis, [(i, i ^ d) for i in range(size)])
+
     def scatter_sum(value):
-        value = value.reshape(parts, -1, 2 * dirs)
-        total = lax.dynamic_index_in_dim(value, col, 0, keepdims=False).astype(F32)
+        value = value.reshape(-1, parts, sub, 2 * dirs)
+        total = lax.dynamic_index_in_dim(value, col, 1, keepdims=False).astype(F32)
         for d in range(1, parts):
-            sent = lax.dynamic_index_in_dim(value, col ^ d, 0, keepdims=False)
-            total = total + lax.ppermute(sent, "col", [(i, i ^ d) for i in range(parts)]).astype(F32)
-        total = total.astype(BF16)
-        return jnp.stack([total[:, :dirs], lax.ppermute(total[:, dirs:], "row", beside)])
+            sent = lax.dynamic_index_in_dim(value, col ^ d, 1, keepdims=False)
+            total = total + swap(sent, "col", d).astype(F32)
+        return total.astype(BF16).reshape(-1, 2 * dirs)
+
+    def gather(total, *earlier):
+        got = swap(total[:, dirs:], "row", 1)
+        mine = jnp.concatenate([after(total[:, :dirs], *earlier), got], axis=0)
+        pair = jnp.concatenate([mine, swap(mine, "col", 2)], axis=0)
+        return [pair, swap(pair, "col", 1)]
+
+    sums = [scatter_sum(x) for x in products]
+    early, last = jnp.concatenate(sums[:2], axis=0), sums[2]
+    arrays = gather(early, partner[2]) + gather(last)
+    segments = [[] for _ in range(cands)]
+    for kind in (0, 1):
+        for c in range(cands):
+            for j in (0, 1):
+                for side in (0, 1):
+                    for plane in (0, 1):
+                        base = (side * 2 + plane) * early.shape[0]
+                        if kind == 0:
+                            segments[c].append((j, base + c * sub, sub))
+                        elif c < cands // 2:
+                            segments[c].append((j, base + (cands + c) * sub, sub))
+                        else:
+                            base = (side * 2 + plane) * last.shape[0]
+                            segments[c].append((2 + j, base + (c - cands // 2) * sub, sub))
+    layout = tuple(tuple(s) for s in segments)
+
+    def by_part(block):
+        split = block.reshape(cands, parts, sub, -1)
+        split = jnp.where((col & 1) == 1, split[:, jnp.array([1, 0, 3, 2])], split)
+        split = jnp.where((col & 2) == 2, split[:, jnp.array([2, 3, 0, 1])], split)
+        return jnp.moveaxis(split[:, jnp.array([0, 2, 1, 3])], 1, 0)
 
     act = [
-        lax.dynamic_index_in_dim(every_act, i, 0, keepdims=False)
+        by_part(lax.dynamic_index_in_dim(every_act, i, 0, keepdims=False))
         for i in (row, row ^ 1, planes - 1 - row, planes - 1 - (row ^ 1))
     ]
-    sums, arrays, segments, act_order = [], [], [[] for _ in range(cands)], [[] for _ in range(cands)]
-
-    def place(value, start, sources):
-        sums.append(scatter_sum(value))
-        every = lax.all_gather(sums[-1], "col", axis=0)
-        n = every.shape[2]
-        for p in range(parts):
-            for j, source in enumerate(sources):
-                at, row_at = start + p * n, (p * 2 + j) * n
-                while at < start + (p + 1) * n:
-                    c, s = at // tok, at % tok
-                    length = min(tok - s, start + (p + 1) * n - at)
-                    segments[c].append((len(arrays), row_at, length))
-                    act_order[c].append(source[c, s : s + length])
-                    at, row_at = at + length, row_at + length
-        arrays.append(every.reshape(parts * 2 * n, dirs))
-
-    place(jnp.concatenate([own_own, own_end], axis=1), 0, act[:2])
-    batches = [
-        ((0,), [(other[0], 0, 3 * slab)], []),
-        ((1,), [(other[0], 3 * slab, slab), (other[1], 0, slab)], arrays[:1]),
-        ((2, 3), [(other[1], slab, slab), (other[1], 2 * slab, 2 * slab)], arrays),
-    ]
-    for batch, middles, earlier in batches:
-        tokens = [(partner[k], 0, (ranges[k][1] - ranges[k][0]) * slab) for k in batch]
-        product = project(flags, tokens, middles, [grad_basis, near_basis, after(far_basis, *earlier)])
-        place(product, ranges[batch[0]][0] * slab, act[2:])
-    act_rot = jnp.stack([jnp.concatenate(x, axis=0) for x in act_order])
-    layout = tuple(tuple(s) for s in segments)
+    act_rot = [jnp.stack(act[i : i + 2], axis=1) for i in (0, 2)]
+    act_rot = [jnp.moveaxis(x, 2, 0).reshape(cands, 2 * tok, -1) for x in act_rot]
+    act_rot = jnp.concatenate(act_rot, axis=1)
     rotated, scores = rotate_and_score(arrays, layout, act_rot, eigenvalues, query_rotated)
     scores = exchange_sum(exchange_sum(scores, "col", parts), "row", planes)
     return rotated, scores

time: 597 us -> 567 us (0.950)
  waiting for transfers between devices: 335 us -> 242 us
  starting transfers between devices: 66.4 us -> 147 us
  blocking collectives: 23.9 us -> 0 us
  Pallas kernels: 66.2 us -> 60.1 us
  other arithmetic: 4.81 us -> 10.9 us
    ppermute x4 -> x3, starting transfers between devices: 16.5 us -> 110 us  [chain_body(): partner.append(lax.ppermute(after(piece, *tie), 'row', ends))]
    ppermute x16 -> x15, waiting for transfers between devices: 132 us -> 53.7 us  [swap(): return lax.ppermute(value, axis, [(i, i ^ d) for i in range(size)])]
    ppermute x5, waiting for transfers between devices: 51.6 us -> 7.11 us  [chain_body(): far.append(lax.ppermute(near[i], 'groups', [(0, 1), (1, 0)]))]
    all_gather x1, waiting for transfers between devices: 0.01 us -> 33.6 us  [chain_body(): every_act = lax.all_gather(local_act, 'row', axis=0)]
    all_gather x3 -> x0, blocking collectives: 23.9 us -> none  [place(): every = lax.all_gather(sums[-1], 'col', axis=0)]
    ppermute x5, starting transfers between devices: 22.8 us -> 9.45 us  [chain_body(): near.append(lax.ppermute(piece, 'row', beside))]
    gather x0 -> x12, local copies, waits for them, and re-layouts: none -> 13.3 us  [the longest x4 5.3 us: by_part(): return jnp.moveaxis(split[:, jnp.array([0, 2, 1, 3])], 1, 0)]
    slice x3 -> x1, local copies, waits for them, and re-layouts: 10.7 us -> 2.53 us  [chain_body(): piece = flat[a * slab:b * slab]]
  transfers between devices with their start and end apart: 40 -> 37, of which waited for: 21 -> 17; matrix products, arithmetic and copies ran while one was open for 10% -> 12% of each run, Pallas kernels for 8% -> 10%
where the time goes in v8:
time: 567 us; the launch traced here: 565 us
  waiting for transfers between devices  242 us (43%)
  starting transfers between devices  147 us (26%)
  local copies, waits for them, and re-layouts  82.4 us (15%)
  Pallas kernels  60.1 us (11%)
  between operations  14.8 us (3%)
  other arithmetic  10.9 us (2%)
  matrix products  7.61 us (1%)
    ppermute x5, waiting for transfers between devices, chain_body(): near.append(lax.ppermute(piece, 'row', beside))  128 us
    ppermute x3, starting transfers between devices, chain_body(): partner.append(lax.ppermute(after(piece, *tie), 'row', ends))  110 us
    pallas_call x4, Pallas kernels, project(): pl.pallas_call(functools.partial(project_kernel, len(ends), len(tokens),...  54.6 us
    ppermute x15, waiting for transfers between devices, swap(): return lax.ppermute(value, axis, [(i, i ^ d) for i in range(size)])  53.7 us
    unnamed x78, local copies, waits for them, and re-layouts  46.4 us
    all_gather x1, waiting for transfers between devices, chain_body(): every_act = lax.all_gather(local_act, 'row', axis=0)  33.6 us
    ppermute x3, waiting for transfers between devices, chain_body(): partner.append(lax.ppermute(after(piece, *tie), 'row', ends))  14.2 us
    ppermute x15, starting transfers between devices, swap(): return lax.ppermute(value, axis, [(i, i ^ d) for i in range(size)])  11.4 us
  transfers between devices with their start and end apart: 37, of which 17 were waited for; matrix products, arithmetic and copies ran while one was open for 12% of the time, Pallas kernels for 10%

profile of v8, /device:TPU:0, one launch (start us, length us, event | category | flops | bytes accessed | tf_op | source)
XLA Modules:
  0.0 565.3 jit_solution(16489547532908789450)
XLA Ops:
  7.2 6.0 %fusion.18 = (bf16[2,128,8192]{2,1,0:T(8,128)(2,1)}, bf16[2,128,8192]{2,1,0:T(8,128)(2,1)}) fusion(bf16[4,128,8192]{2,1,0:T(8,128)(2,1)} %param.21), kind=kLoop, calls=%fused_computation.90 | loop fusion | bytes 16777216 | tf_op jit(solution)/shard_map/slice | solution.py:201
  13.2 2.7 collective-permute-start.3
  15.9 2.7 constant_dynamic-slice_fusion.5
  18.6 3.8 collective-permute-start
  22.4 5.3 constant_dynamic-slice_fusion.6
  28.0 7.6 %fusion.5 = bf16[4,128,256]{2,1,0:T(8,128)(2,1)} fusion(bf16[4,128,8192]{2,1,0:T(8,128)(2,1)} %param.20, bf16[8192,256]{1,0:T(8,128)(2,1)} %param.22, f32[4,128]{1,0:T(4,128)S(1)} %compare_convert_fusion), kind=kOutput, calls=%fused_computation.18 | convolution fusion | flops 2147745792 | bytes 12847104 | tf_op jit(solution)/shard_map/ctd,dk->ctk/dot_general | solution.py:25
  35.6 10.9 %collective-permute-done = bf16[1024,512]{1,0:T(8,128)(2,1)} collective-permute-done((bf16[1024,512]{1,0:T(8,128)(2,1)S(1)}, bf16[1024,512]{1,0:T(8,128)(2,1)}, u32[]{:S(2)}, u32[]{:S(2)}) %collective-permute-start) | collective-permute-done | bytes 1048608 | tf_op jit(solution)/shard_map/ppermute | solution.py:203
  47.6 5.8 %copy-done = bf16[8192,1024]{1,0:T(8,128)(2,1)S(1)} copy-done((bf16[8192,1024]{1,0:T(8,128)(2,1)S(1)}, bf16[8192,1024]{1,0:T(8,128)(2,1)}, u32[]{:S(2)}) %copy-start) | copy-done | bytes 16777240
  53.3 3.4 copy-done.1
  56.7 11.9 %shard_map.203 = bf16[512,1024]{1,0:T(8,128)(2,1)S(1)} custom-call(s32[2]{0:T(128)S(1)} %pad_add_fusion.refs_0_, bf16[512,8192]{1,0:T(8,128)(2,1)S(1)} %bitcast.87, bf16[8192,1024]{1,0:T(8,128)(2,1)S(1)} %copy-done), custom_call_target="tpu_custom_call" | custom-call | flops 536870912 | bytes 1572864 | tf_op jit(solution)/shard_map/pallas_call | solution.py:148
  68.7 3.5 collective-permute-start.2
  72.2 19.3 %collective-permute-done.1 = bf16[2048,512]{1,0:T(8,128)(2,1)} collective-permute-done((bf16[2048,512]{1,0:T(8,128)(2,1)}, bf16[2048,512]{1,0:T(8,128)(2,1)}, u32[]{:S(2)}, u32[]{:S(2)}) %collective-permute-start.1) | collective-permute-done | bytes 2097184 | tf_op jit(solution)/shard_map/ppermute | solution.py:203
  91.5 1.5 collective-permute-start.7
  93.0 42.3 %collective-permute-done.2 = bf16[2048,512]{1,0:T(8,128)(2,1)} collective-permute-done((bf16[2048,512]{1,0:T(8,128)(2,1)S(1)}, bf16[2048,512]{1,0:T(8,128)(2,1)}, u32[]{:S(2)}, u32[]{:S(2)}) %collective-permute-start.2) | collective-permute-done | bytes 2097184 | tf_op jit(solution)/shard_map/ppermute | solution.py:203
  135.3 1.7 collective-permute-start.5
  137.1 1.5 collective-permute-start.8
  138.9 2.5 slice_bitcast_fusion
  141.5 20.1 %collective-permute-done.5 = bf16[1024,512]{1,0:T(8,128)(2,1)S(1)} collective-permute-done((bf16[1024,512]{1,0:T(8,128)(2,1)}, bf16[1024,512]{1,0:T(8,128)(2,1)S(1)}, u32[]{:S(2)}, u32[]{:S(2)}) %collective-permute-start.5) | collective-permute-done | bytes 1048608 | tf_op jit(solution)/shard_map/ppermute | solution.py:203
  161.6 2.0 copy-done.6
  163.9 5.1 collective-permute-start.12
  169.1 1.6 collective-permute-start.6
  170.7 35.1 %collective-permute-done.4 = bf16[2048,512]{1,0:T(8,128)(2,1)} collective-permute-done((bf16[2048,512]{1,0:T(8,128)(2,1)S(1)}, bf16[2048,512]{1,0:T(8,128)(2,1)}, u32[]{:S(2)}, u32[]{:S(2)}) %collective-permute-start.4) | collective-permute-done | bytes 2097184 | tf_op jit(solution)/shard_map/ppermute | solution.py:203
  205.8 1.5 collective-permute-start.9
  207.4 2.3 constant_dynamic-update-slice_fusion.4
  209.7 6.3 %collective-permute-start.16 = (bf16[128,8192]{1,0:T(8,128)(2,1)}, bf16[128,8192]{1,0:T(8,128)(2,1)}, u32[]{:S(2)}, u32[]{:S(2)}) collective-permute-start(bf16[128,8192]{1,0:T(8,128)(2,1)} %get-tuple-element.19), channel_id=1, source_target_pairs={{0,12},{12,0},{1,13},{13,1},{2,14},{14,2},{3,15},{15,3},{16,28},{2... | collective-permute-start | bytes 6291464 | tf_op jit(solution)/shard_map/ppermute | solution.py:214
  216.0 33.6 %all-gather.3.cloned.1.call-done = bf16[16,128,256]{2,1,0:T(8,128)(2,1)} async-done(((bf16[4,128,256]{2,1,0:T(8,128)(2,1)}), bf16[16,128,256]{2,1,0:T(8,128)(2,1)}) %all-gather.3.cloned.1.call-update) | async-done | bytes 1048592 | tf_op jit(solution)/shard_map/all_gather | solution.py:191
  251.5 1.3 gather_fusion.3
  252.7 3.1 constant_dynamic-update-slice_fusion.3
  255.8 14.2 %collective-permute-done.12.refs_1_ = bf16[128,8192]{1,0:T(8,128)(2,1)} collective-permute-done((bf16[128,8192]{1,0:T(8,128)(2,1)}, bf16[128,8192]{1,0:T(8,128)(2,1)}, u32[]{:S(2)}, u32[]{:S(2)}) %collective-permute-start.12) | collective-permute-done | bytes 2097184 | tf_op jit(solution)/shard_map/ppermute | solution.py:214
  270.0 98.3 %collective-permute-start.20 = (bf16[256,8192]{1,0:T(8,128)(2,1)}, bf16[256,8192]{1,0:T(8,128)(2,1)}, u32[]{:S(2)}, u32[]{:S(2)}) collective-permute-start(bf16[256,8192]{1,0:T(8,128)(2,1)} %bitcast.6), channel_id=1, source_target_pairs={{0,12},{12,0},{1,13},{13,1},{2,14},{14,2},{3,15},{15,3},{16,28},{2... | collective-permute-start | bytes 12582920 | tf_op jit(solution)/shard_map/ppermute | solution.py:214
  368.4 1.3 constant_dynamic-update-slice_fusion.9
  369.7 3.1 constant_dynamic-update-slice_fusion.2
  372.9 1.7 constant_dynamic-update-slice_fusion.7
  374.7 3.0 constant_dynamic-update-slice_fusion.1
  378.7 1.7 constant_dynamic-update-slice_fusion.6
  380.5 7.1 %collective-permute-done.10 = bf16[1024,512]{1,0:T(8,128)(2,1)S(1)} collective-permute-done((bf16[1024,512]{1,0:T(8,128)(2,1)S(1)}, bf16[1024,512]{1,0:T(8,128)(2,1)S(1)}, u32[]{:S(2)}, u32[]{:S(2)}) %collective-permute-start.10) | collective-permute-done | bytes 1048608 | tf_op jit(solution)/shard_map/ppermute | solution.py:204
  387.7 6.5 %copy-done.2 = bf16[8192,512]{1,0:T(8,128)(2,1)S(1)} copy-done((bf16[8192,512]{1,0:T(8,128)(2,1)S(1)}, bf16[8192,512]{1,0:T(8,128)(2,1)}, u32[]{:S(2)}) %copy-start.2) | copy-done | bytes 8388632
  394.1 16.2 %shard_map.205 = bf16[256,2048]{1,0:T(8,128)(2,1)S(1)} custom-call(s32[2]{0:T(128)S(1)} %pad_add_fusion.refs_0_, bf16[128,8192]{1,0:T(8,128)(2,1)} %collective-permute-done.12.refs_1_, bf16[128,8192]{1,0:T(8,128)(2,1)} %collective-permute-done.16.refs_2_, bf16[256,8192]{1,0:T(8,128)(2,1)} %collective-permute-done.3.refs_3_, bf16[8192,1024]{1,0:T(8,128)(2,1)} %refs_3_.1, ...), custom_call_target="tpu_custom_call" | custom-call | flops 536870912 | bytes 2359296 | tf_op jit(solution)/shard_map/pallas_call | solution.py:148
  411.1 12.1 %shard_map.204 = bf16[512,1024]{1,0:T(8,128)(2,1)S(1)} custom-call(s32[2]{0:T(128)S(1)} %pad_add_fusion.refs_0_, bf16[512,8192]{1,0:T(8,128)(2,1)S(1)} %bitcast.90, bf16[8192,512]{1,0:T(8,128)(2,1)S(1)} %copy-done.2, bf16[8192,512]{1,0:T(8,128)(2,1)S(1)} %constant_dynamic-update-slice_fusion.5.refs_3_.refs_6_.refs_5_), custom_call_target="tpu_custom_call" | custom-call | flops 536870912 | bytes 1572864 | tf_op jit(solution)/shard_map/pallas_call | solution.py:148
  423.5 1.3 copy-done.10
  426.5 1.7 collective-permute-start.14
  428.2 1.7 collective-permute-start.19
  431.9 25.1 %collective-permute-done.19 = bf16[2,32,2048]{2,1,0:T(8,128)(2,1)} collective-permute-done((bf16[2,32,2048]{2,1,0:T(8,128)(2,1)}, bf16[2,32,2048]{2,1,0:T(8,128)(2,1)}, u32[]{:S(2)}, u32[]{:S(2)}) %collective-permute-start.19) | collective-permute-done | bytes 262176 | tf_op jit(solution)/shard_map/ppermute | solution.py:227
  457.1 1.3 fusion.16
  458.4 1.9 fusion.10
  463.0 3.4 copy-done.3
  466.4 3.4 copy-done.5
  469.8 2.2 copy-done.7
  472.0 14.4 %shard_map.206 = bf16[256,2048]{1,0:T(8,128)(2,1)S(1)} custom-call(s32[2]{0:T(128)S(1)} %pad_add_fusion.refs_0_, bf16[256,8192]{1,0:T(8,128)(2,1)} %collective-permute-done.20.refs_1_, bf16[256,8192]{1,0:T(8,128)(2,1)S(1)} %copy-done.7, bf16[8192,1024]{1,0:T(8,128)(2,1)} %refs_3_.1, bf16[8192,512]{1,0:T(8,128)(2,1)S(1)} %copy-done.3, ...), custom_call_target="tpu_custom_call" | custom-call | flops 536870912 | bytes 2359296 | tf_op jit(solution)/shard_map/pallas_call | solution.py:148
  487.0 1.7 collective-permute-start.25
  489.5 1.4 collective-permute-start.22
  492.0 4.2 collective-permute-done.25
  496.2 4.9 collective-permute-done.26
  501.2 1.7 collective-permute-start.27
  503.0 14.8 %collective-permute-done.22 = bf16[384,1024]{1,0:T(8,128)(2,1)S(1)} collective-permute-done((bf16[384,1024]{1,0:T(8,128)(2,1)S(1)}, bf16[384,1024]{1,0:T(8,128)(2,1)S(1)}, u32[]{:S(2)}, u32[]{:S(2)}) %collective-permute-start.22) | collective-permute-done | bytes 786464 | tf_op jit(solution)/shard_map/ppermute | solution.py:227
  518.7 1.7 collective-permute-start.28
  523.0 4.7 collective-permute-done.28
  531.4 2.2 gather_fusion.11
  539.6 5.5 shard_map.207
  545.8 1.7 collective-permute-start.31
  547.5 1.8 collective-permute-done.31
  550.5 1.9 collective-permute-start.33
  552.5 2.4 collective-permute-start.35
  554.9 2.0 collective-permute-done.34
  (156 shorter events, 31.3 us)
Async XLA Ops:
  7.2 242.5 %all-gather.3.cloned.1.call-start = ((), (), s32[]{:S(2)}) async-start(), calls=%async_computation | async-start | bytes 1310720 | tf_op jit(solution)/shard_map/all_gather | solution.py:191
  13.2 125.3 %collective-permute-start.3 = (bf16[256,8192]{1,0:T(8,128)(2,1)}, bf16[256,8192]{1,0:T(8,128)(2,1)}, u32[]{:S(2)}, u32[]{:S(2)}) collective-permute-start(bf16[256,8192]{1,0:T(8,128)(2,1)} %bitcast.4), channel_id=1, source_target_pairs={{4,8},{8,4},{5,9},{9,5},{6,10},{10,6},{7,11},{11,7},{20,24},{24,20... | collective-permute-start | bytes 12582920 | tf_op jit(solution)/shard_map/ppermute | solution.py:202
  18.6 9.2 %copy-start.27 = (s32[2048]{0:T(1024)S(1)}, s32[2048]{0:T(1024)}, u32[]{:S(2)}) copy-start(s32[2048]{0:T(1024)} %param.27) | copy-start | bytes 24580
  18.6 9.2 %copy-start.28 = (s32[4]{0:T(128)S(1)}, s32[4]{0:T(128)}, u32[]{:S(2)}) copy-start(s32[4]{0:T(128)} %param.26) | copy-start | bytes 52
  18.6 28.0 %collective-permute-start = (bf16[1024,512]{1,0:T(8,128)(2,1)S(1)}, bf16[1024,512]{1,0:T(8,128)(2,1)}, u32[]{:S(2)}, u32[]{:S(2)}) collective-permute-start(bf16[1024,512]{1,0:T(8,128)(2,1)S(1)} %get-tuple-element.25), channel_id=1, source_target_pairs={{0,4},{4,0},{8,12},{12,8},{1,5},{5,1},{9,13},{13,9},{2,6},{6,2},{1... | collective-permute-start | bytes 3145736 | tf_op jit(solution)/shard_map/ppermute | solution.py:203
  27.7 63.8 %collective-permute-start.1 = (bf16[2048,512]{1,0:T(8,128)(2,1)}, bf16[2048,512]{1,0:T(8,128)(2,1)}, u32[]{:S(2)}, u32[]{:S(2)}) collective-permute-start(bf16[2048,512]{1,0:T(8,128)(2,1)} %get-tuple-element.28), channel_id=1, source_target_pairs={{0,4},{4,0},{8,12},{12,8},{1,5},{5,1},{9,13},{13,9},{2,6},{6,2},{1... | collective-permute-start | bytes 6291464 | tf_op jit(solution)/shard_map/ppermute | solution.py:203
  46.6 115.0 %collective-permute-start.11 = (bf16[256,8192]{1,0:T(8,128)(2,1)}, bf16[256,8192]{1,0:T(8,128)(2,1)S(1)}, u32[]{:S(2)}, u32[]{:S(2)}) collective-permute-start(bf16[256,8192]{1,0:T(8,128)(2,1)} %bitcast.6), channel_id=1, source_target_pairs={{4,8},{8,4},{5,9},{9,5},{6,10},{10,6},{7,11},{11,7},{20,24},{24,20... | collective-permute-start | bytes 12582920 | tf_op jit(solution)/shard_map/ppermute | solution.py:202
  47.6 5.8 %copy-start = (bf16[8192,1024]{1,0:T(8,128)(2,1)S(1)}, bf16[8192,1024]{1,0:T(8,128)(2,1)}, u32[]{:S(2)}) copy-start(bf16[8192,1024]{1,0:T(8,128)(2,1)} %refs_3_.1) | copy-start | bytes 50331652
  53.3 3.4 copy-start.1
  56.7 12.0 %copy-start.15 = (bf16[2048,512]{1,0:T(8,128)(2,1)S(1)}, bf16[2048,512]{1,0:T(8,128)(2,1)}, u32[]{:S(2)}) copy-start(bf16[2048,512]{1,0:T(8,128)(2,1)} %get-tuple-element.13) | copy-start | bytes 6291460
  68.7 66.6 %collective-permute-start.2 = (bf16[2048,512]{1,0:T(8,128)(2,1)S(1)}, bf16[2048,512]{1,0:T(8,128)(2,1)}, u32[]{:S(2)}, u32[]{:S(2)}) collective-permute-start(bf16[2048,512]{1,0:T(8,128)(2,1)S(1)} %copy-done.15), channel_id=1, source_target_pairs={{0,4},{4,0},{8,12},{12,8},{1,5},{5,1},{9,13},{13,9},{2,6},{6,2},{1... | collective-permute-start | bytes 6291464 | tf_op jit(solution)/shard_map/ppermute | solution.py:203
  91.5 50.0 %collective-permute-start.7 = (bf16[2048,512]{1,0:T(8,128)(2,1)}, bf16[2048,512]{1,0:T(8,128)(2,1)S(1)}, u32[]{:S(2)}, u32[]{:S(2)}) collective-permute-start(bf16[2048,512]{1,0:T(8,128)(2,1)} %collective-permute-done.1), channel_id=1, source_target_pairs={{0,16},{16,0},{1,17},{17,1},{2,18},{18,2},{3,19},{19,3},{4,20},{20... | collective-permute-start | bytes 6291464 | tf_op jit(solution)/shard_map/ppermute | solution.py:204
  135.3 26.3 %collective-permute-start.5 = (bf16[1024,512]{1,0:T(8,128)(2,1)}, bf16[1024,512]{1,0:T(8,128)(2,1)S(1)}, u32[]{:S(2)}, u32[]{:S(2)}) collective-permute-start(bf16[1024,512]{1,0:T(8,128)(2,1)} %get-tuple-element.15), channel_id=1, source_target_pairs={{0,4},{4,0},{8,12},{12,8},{1,5},{5,1},{9,13},{13,9},{2,6},{6,2},{1... | collective-permute-start | bytes 3145736 | tf_op jit(solution)/shard_map/ppermute | solution.py:203
  137.1 72.6 %collective-permute-start.8 = (bf16[2048,512]{1,0:T(8,128)(2,1)}, bf16[2048,512]{1,0:T(8,128)(2,1)}, u32[]{:S(2)}, u32[]{:S(2)}) collective-permute-start(bf16[2048,512]{1,0:T(8,128)(2,1)} %collective-permute-done.2), channel_id=1, source_target_pairs={{0,16},{16,0},{1,17},{17,1},{2,18},{18,2},{3,19},{19,3},{4,20},{20... | collective-permute-start | bytes 6291464 | tf_op jit(solution)/shard_map/ppermute | solution.py:204
  138.6 68.8 %copy-start.31 = (s32[4]{0:T(128)S(1)}, s32[4]{0:T(128)}, u32[]{:S(2)}) copy-start(s32[4]{0:T(128)} %constant.100) | copy-start | bytes 52
  138.6 68.8 %copy-start.29 = (s32[4]{0:T(128)S(1)}, s32[4]{0:T(128)}, u32[]{:S(2)}) copy-start(s32[4]{0:T(128)} %constant.101) | copy-start | bytes 52
  138.6 68.8 %copy-start.30 = (s32[4]{0:T(128)S(1)}, s32[4]{0:T(128)}, u32[]{:S(2)}) copy-start(s32[4]{0:T(128)} %constant.102) | copy-start | bytes 52
  138.6 67.2 %collective-permute-start.4 = (bf16[2048,512]{1,0:T(8,128)(2,1)S(1)}, bf16[2048,512]{1,0:T(8,128)(2,1)}, u32[]{:S(2)}, u32[]{:S(2)}) collective-permute-start(bf16[2048,512]{1,0:T(8,128)(2,1)S(1)} %get-tuple-element.14), channel_id=1, source_target_pairs={{0,4},{4,0},{8,12},{12,8},{1,5},{5,1},{9,13},{13,9},{2,6},{6,2},{1... | collective-permute-start | bytes 6291464 | tf_op jit(solution)/shard_map/ppermute | solution.py:203
  141.5 20.2 %copy-start.16 = (bf16[2048,512]{1,0:T(8,128)(2,1)}, bf16[2048,512]{1,0:T(8,128)(2,1)S(1)}, u32[]{:S(2)}) copy-start(bf16[2048,512]{1,0:T(8,128)(2,1)S(1)} %collective-permute-done.7) | copy-start | bytes 6291460
  163.9 106.1 %collective-permute-start.12 = (bf16[128,8192]{1,0:T(8,128)(2,1)}, bf16[128,8192]{1,0:T(8,128)(2,1)}, u32[]{:S(2)}, u32[]{:S(2)}) collective-permute-start(bf16[128,8192]{1,0:T(8,128)(2,1)} %get-tuple-element.17), channel_id=1, source_target_pairs={{0,12},{12,0},{1,13},{13,1},{2,14},{14,2},{3,15},{15,3},{16,28},{2... | collective-permute-start | bytes 6291464 | tf_op jit(solution)/shard_map/ppermute | solution.py:214
  169.1 199.3 %collective-permute-start.6 = (bf16[1024,512]{1,0:T(8,128)(2,1)}, bf16[1024,512]{1,0:T(8,128)(2,1)}, u32[]{:S(2)}, u32[]{:S(2)}) collective-permute-start(bf16[1024,512]{1,0:T(8,128)(2,1)} %collective-permute-done), channel_id=1, source_target_pairs={{0,16},{16,0},{1,17},{17,1},{2,18},{18,2},{3,19},{19,3},{4,20},{20... | collective-permute-start | bytes 3145736 | tf_op jit(solution)/shard_map/ppermute | solution.py:204
  205.8 172.9 %collective-permute-start.9 = (bf16[2048,512]{1,0:T(8,128)(2,1)}, bf16[2048,512]{1,0:T(8,128)(2,1)}, u32[]{:S(2)}, u32[]{:S(2)}) collective-permute-start(bf16[2048,512]{1,0:T(8,128)(2,1)} %collective-permute-done.4), channel_id=1, source_target_pairs={{0,16},{16,0},{1,17},{17,1},{2,18},{18,2},{3,19},{19,3},{4,20},{20... | collective-permute-start | bytes 6291464 | tf_op jit(solution)/shard_map/ppermute | solution.py:204
  209.7 178.0 %collective-permute-start.16 = (bf16[128,8192]{1,0:T(8,128)(2,1)}, bf16[128,8192]{1,0:T(8,128)(2,1)}, u32[]{:S(2)}, u32[]{:S(2)}) collective-permute-start(bf16[128,8192]{1,0:T(8,128)(2,1)} %get-tuple-element.19), channel_id=1, source_target_pairs={{0,12},{12,0},{1,13},{13,1},{2,14},{14,2},{3,15},{15,3},{16,28},{2... | collective-permute-start | bytes 6291464 | tf_op jit(solution)/shard_map/ppermute | solution.py:214
  255.8 117.0 %copy-start.20 = (bf16[1024,512]{1,0:T(8,128)(2,1)S(1)}, bf16[1024,512]{1,0:T(8,128)(2,1)}, u32[]{:S(2)}) copy-start(bf16[1024,512]{1,0:T(8,128)(2,1)} %copy-done.19) | copy-start | bytes 3145732
  255.8 117.0 %copy-start.17 = (bf16[2048,512]{1,0:T(8,128)(2,1)S(1)}, bf16[2048,512]{1,0:T(8,128)(2,1)}, u32[]{:S(2)}) copy-start(bf16[2048,512]{1,0:T(8,128)(2,1)} %copy-done.16) | copy-start | bytes 6291460
  270.0 193.0 %collective-permute-start.20 = (bf16[256,8192]{1,0:T(8,128)(2,1)}, bf16[256,8192]{1,0:T(8,128)(2,1)}, u32[]{:S(2)}, u32[]{:S(2)}) collective-permute-start(bf16[256,8192]{1,0:T(8,128)(2,1)} %bitcast.6), channel_id=1, source_target_pairs={{0,12},{12,0},{1,13},{13,1},{2,14},{14,2},{3,15},{15,3},{16,28},{2... | collective-permute-start | bytes 12582920 | tf_op jit(solution)/shard_map/ppermute | solution.py:214
  372.8 14.8 %collective-permute-start.10 = (bf16[1024,512]{1,0:T(8,128)(2,1)S(1)}, bf16[1024,512]{1,0:T(8,128)(2,1)S(1)}, u32[]{:S(2)}, u32[]{:S(2)}) collective-permute-start(bf16[1024,512]{1,0:T(8,128)(2,1)S(1)} %copy-done.20), channel_id=1, source_target_pairs={{0,16},{16,0},{1,17},{17,1},{2,18},{18,2},{3,19},{19,3},{4,20},{20... | collective-permute-start | bytes 3145736 | tf_op jit(solution)/shard_map/ppermute | solution.py:204
  387.6 23.5 %slice-start = ((s8[8388608]{0:T(1024)(128)(4,1)}), s8[4194304]{0:T(1024)(128)(4,1)S(1)}, s32[]{:S(2)}) async-start(s8[8388608]{0:T(1024)(128)(4,1)} %bitcast.88), calls=%async_computation.1 | async-start | bytes 8388608
  387.6 23.5 %copy-start.4 = (bf16[8192,512]{1,0:T(8,128)(2,1)}, bf16[8192,512]{1,0:T(8,128)(2,1)S(1)}, u32[]{:S(2)}) copy-start(bf16[8192,512]{1,0:T(8,128)(2,1)S(1)} %constant_dynamic-update-slice_fusion.5.refs_3_.refs_6_.refs_5_) | copy-start | bytes 25165828
  387.7 23.5 %slice-start.1 = ((s8[8388608]{0:T(1024)(128)(4,1)}), s8[4194304]{0:T(1024)(128)(4,1)S(1)}, s32[]{:S(2)}) async-start(s8[8388608]{0:T(1024)(128)(4,1)} %bitcast.88), calls=%async_computation.2 | async-start | bytes 8388608
  387.7 6.5 %copy-start.2 = (bf16[8192,512]{1,0:T(8,128)(2,1)S(1)}, bf16[8192,512]{1,0:T(8,128)(2,1)}, u32[]{:S(2)}) copy-start(bf16[8192,512]{1,0:T(8,128)(2,1)} %constant_dynamic-update-slice_fusion.refs_2_.refs_5_.refs_4_) | copy-start | bytes 25165828
  411.1 17.1 %collective-permute-start.17 = (bf16[2,32,2048]{2,1,0:T(8,128)(2,1)S(1)}, bf16[2,32,2048]{2,1,0:T(8,128)(2,1)S(1)}, u32[]{:S(2)}, u32[]{:S(2)}) collective-permute-start(bf16[2,32,2048]{2,1,0:T(8,128)(2,1)S(1)} %get-tuple-element.43), channel_id=1, source_target_pairs={{0,1},{1,0},{2,3},{3,2},{4,5},{5,4},{6,7},{7,6},{8,9},{9,8},{10,11... | collective-permute-start | bytes 786440 | tf_op jit(solution)/shard_map/ppermute | solution.py:227
  411.1 17.1 %collective-permute-start.18 = (bf16[2,32,2048]{2,1,0:T(8,128)(2,1)S(1)}, bf16[2,32,2048]{2,1,0:T(8,128)(2,1)S(1)}, u32[]{:S(2)}, u32[]{:S(2)}) collective-permute-start(bf16[2,32,2048]{2,1,0:T(8,128)(2,1)S(1)} %get-tuple-element.45), channel_id=1, source_target_pairs={{0,2},{1,3},{2,0},{3,1},{4,6},{5,7},{6,4},{7,5},{8,10},{9,11},{10,... | collective-permute-start | bytes 786440 | tf_op jit(solution)/shard_map/ppermute | solution.py:227
  423.3 6.7 %copy-start.21 = (bf16[4,4,32,256]{3,2,1,0:T(8,128)(2,1)S(1)}, bf16[4,4,32,256]{3,2,1,0:T(8,128)(2,1)}, u32[]{:S(2)}) copy-start(bf16[4,4,32,256]{3,2,1,0:T(8,128)(2,1)} %gather_fusion.3) | copy-start | bytes 786436
  426.0 32.4 %collective-permute-start.13 = (bf16[4,32,2048]{2,1,0:T(8,128)(2,1)}, bf16[4,32,2048]{2,1,0:T(8,128)(2,1)}, u32[]{:S(2)}, u32[]{:S(2)}) collective-permute-start(bf16[4,32,2048]{2,1,0:T(8,128)(2,1)} %get-tuple-element.33), channel_id=1, source_target_pairs={{0,1},{1,0},{2,3},{3,2},{4,5},{5,4},{6,7},{7,6},{8,9},{9,8},{10,11... | collective-permute-start | bytes 1572872 | tf_op jit(solution)/shard_map/ppermute | solution.py:227
  426.5 31.9 %collective-permute-start.14 = (bf16[4,32,2048]{2,1,0:T(8,128)(2,1)}, bf16[4,32,2048]{2,1,0:T(8,128)(2,1)}, u32[]{:S(2)}, u32[]{:S(2)}) collective-permute-start(bf16[4,32,2048]{2,1,0:T(8,128)(2,1)} %get-tuple-element.35), channel_id=1, source_target_pairs={{0,2},{1,3},{2,0},{3,1},{4,6},{5,7},{6,4},{7,5},{8,10},{9,11},{10,... | collective-permute-start | bytes 1572872 | tf_op jit(solution)/shard_map/ppermute | solution.py:227
  428.2 30.2 %collective-permute-start.15 = (bf16[4,32,2048]{2,1,0:T(8,128)(2,1)S(1)}, bf16[4,32,2048]{2,1,0:T(8,128)(2,1)}, u32[]{:S(2)}, u32[]{:S(2)}) collective-permute-start(bf16[4,32,2048]{2,1,0:T(8,128)(2,1)S(1)} %get-tuple-element.34), channel_id=1, source_target_pairs={{0,3},{1,2},{2,1},{3,0},{4,7},{5,6},{6,5},{7,4},{8,11},{9,10},{10,... | collective-permute-start | bytes 1572872 | tf_op jit(solution)/shard_map/ppermute | solution.py:227
  428.2 28.8 %collective-permute-start.19 = (bf16[2,32,2048]{2,1,0:T(8,128)(2,1)}, bf16[2,32,2048]{2,1,0:T(8,128)(2,1)}, u32[]{:S(2)}, u32[]{:S(2)}) collective-permute-start(bf16[2,32,2048]{2,1,0:T(8,128)(2,1)} %get-tuple-element.44), channel_id=1, source_target_pairs={{0,3},{1,2},{2,1},{3,0},{4,7},{5,6},{6,5},{7,4},{8,11},{9,10},{10,... | collective-permute-start | bytes 786440 | tf_op jit(solution)/shard_map/ppermute | solution.py:227
  430.0 30.4 %copy-start.13 = (bf16[4,4,32,256]{3,2,0,1:T(8,128)(2,1)}, bf16[4,4,32,256]{3,2,0,1:T(8,128)(2,1)S(1)}, u32[]{:S(2)}) copy-start(bf16[4,4,32,256]{3,2,0,1:T(8,128)(2,1)S(1)} %get-tuple-element.55) | copy-start | bytes 786436
  430.1 30.4 %copy-start.11 = (bf16[4,4,32,256]{3,2,0,1:T(8,128)(2,1)}, bf16[4,4,32,256]{3,2,0,1:T(8,128)(2,1)S(1)}, u32[]{:S(2)}) copy-start(bf16[4,4,32,256]{3,2,0,1:T(8,128)(2,1)S(1)} %get-tuple-element.54) | copy-start | bytes 786436
  431.9 28.5 %copy-start.24 = (bf16[4,4,32,256]{3,2,1,0:T(8,128)(2,1)S(1)}, bf16[4,4,32,256]{3,2,1,0:T(8,128)(2,1)}, u32[]{:S(2)}) copy-start(bf16[4,4,32,256]{3,2,1,0:T(8,128)(2,1)} %gather_fusion.9) | copy-start | bytes 786436
  460.3 28.5 %collective-permute-start.21 = (bf16[192,1024]{1,0:T(8,128)(2,1)S(1)}, bf16[192,1024]{1,0:T(8,128)(2,1)S(1)}, u32[]{:S(2)}, u32[]{:S(2)}) collective-permute-start(bf16[192,1024]{1,0:T(8,128)(2,1)S(1)} %get-tuple-element.46), channel_id=1, source_target_pairs={{0,4},{4,0},{8,12},{12,8},{1,5},{5,1},{9,13},{13,9},{2,6},{6,2},{1... | collective-permute-start | bytes 1179656 | tf_op jit(solution)/shard_map/ppermute | solution.py:227
  463.0 3.4 copy-start.3
  466.4 3.4 copy-start.5
  486.4 31.6 %copy-start.14 = (bf16[4,4,32,256]{3,2,0,1:T(8,128)(2,1)S(1)}, bf16[4,4,32,256]{3,2,0,1:T(8,128)(2,1)}, u32[]{:S(2)}) copy-start(bf16[4,4,32,256]{3,2,0,1:T(8,128)(2,1)} %copy-done.13) | copy-start | bytes 786436
  486.4 31.6 %copy-start.23 = (bf16[4,4,32,256]{3,2,1,0:T(8,128)(2,1)S(1)}, bf16[4,4,32,256]{3,2,1,0:T(8,128)(2,1)}, u32[]{:S(2)}) copy-start(bf16[4,4,32,256]{3,2,1,0:T(8,128)(2,1)} %gather_fusion.1) | copy-start | bytes 786436
  486.5 34.0 %copy-start.12 = (bf16[4,4,32,256]{3,2,0,1:T(8,128)(2,1)S(1)}, bf16[4,4,32,256]{3,2,0,1:T(8,128)(2,1)}, u32[]{:S(2)}) copy-start(bf16[4,4,32,256]{3,2,0,1:T(8,128)(2,1)} %copy-done.11) | copy-start | bytes 786436
  486.5 34.0 %copy-start.22 = (bf16[4,4,32,256]{3,2,1,0:T(8,128)(2,1)S(1)}, bf16[4,4,32,256]{3,2,1,0:T(8,128)(2,1)}, u32[]{:S(2)}) copy-start(bf16[4,4,32,256]{3,2,1,0:T(8,128)(2,1)} %gather_fusion.4) | copy-start | bytes 786436
  486.5 5.5 collective-permute-start.24
  487.0 9.2 %collective-permute-start.25 = (bf16[2,32,2048]{2,1,0:T(8,128)(2,1)S(1)}, bf16[2,32,2048]{2,1,0:T(8,128)(2,1)S(1)}, u32[]{:S(2)}, u32[]{:S(2)}) collective-permute-start(bf16[2,32,2048]{2,1,0:T(8,128)(2,1)S(1)} %get-tuple-element.42), channel_id=1, source_target_pairs={{0,2},{1,3},{2,0},{3,1},{4,6},{5,7},{6,4},{7,5},{8,10},{9,11},{10,... | collective-permute-start | bytes 786440 | tf_op jit(solution)/shard_map/ppermute | solution.py:227
  488.8 12.3 %collective-permute-start.26 = (bf16[2,32,2048]{2,1,0:T(8,128)(2,1)S(1)}, bf16[2,32,2048]{2,1,0:T(8,128)(2,1)S(1)}, u32[]{:S(2)}, u32[]{:S(2)}) collective-permute-start(bf16[2,32,2048]{2,1,0:T(8,128)(2,1)S(1)} %get-tuple-element.41), channel_id=1, source_target_pairs={{0,3},{1,2},{2,1},{3,0},{4,7},{5,6},{6,5},{7,4},{8,11},{9,10},{10,... | collective-permute-start | bytes 786440 | tf_op jit(solution)/shard_map/ppermute | solution.py:227
  489.5 28.3 %collective-permute-start.22 = (bf16[384,1024]{1,0:T(8,128)(2,1)S(1)}, bf16[384,1024]{1,0:T(8,128)(2,1)S(1)}, u32[]{:S(2)}, u32[]{:S(2)}) collective-permute-start(bf16[384,1024]{1,0:T(8,128)(2,1)S(1)} %pad_maximum_fusion.2), channel_id=1, source_target_pairs={{0,2},{1,3},{2,0},{3,1},{4,6},{5,7},{6,4},{7,5},{8,10},{9,11},{10,... | collective-permute-start | bytes 2359304 | tf_op jit(solution)/shard_map/ppermute | solution.py:227
  501.2 16.8 %collective-permute-start.27 = (bf16[64,1024]{1,0:T(8,128)(2,1)S(1)}, bf16[64,1024]{1,0:T(8,128)(2,1)S(1)}, u32[]{:S(2)}, u32[]{:S(2)}) collective-permute-start(bf16[64,1024]{1,0:T(8,128)(2,1)S(1)} %get-tuple-element.49), channel_id=1, source_target_pairs={{0,4},{4,0},{8,12},{12,8},{1,5},{5,1},{9,13},{13,9},{2,6},{6,2},{1... | collective-permute-start | bytes 393224 | tf_op jit(solution)/shard_map/ppermute | solution.py:227
  517.9 21.7 %collective-permute-start.23 = (bf16[768,1024]{1,0:T(8,128)(2,1)S(1)}, bf16[768,1024]{1,0:T(8,128)(2,1)}, u32[]{:S(2)}, u32[]{:S(2)}) collective-permute-start(bf16[768,1024]{1,0:T(8,128)(2,1)S(1)} %constant_dynamic-update-slice_fusion.10.refs_0_), channel_id=1, source_target_pairs={{0,1},{1,0},{2,3},{3,2},{4,5},{5,4},{6,7},{7,6},{8,9},{9,8},{10,11... | collective-permute-start | bytes 4718600 | tf_op jit(solution)/shard_map/ppermute | solution.py:227
  518.7 9.0 %collective-permute-start.28 = (bf16[128,1024]{1,0:T(8,128)(2,1)}, bf16[128,1024]{1,0:T(8,128)(2,1)}, u32[]{:S(2)}, u32[]{:S(2)}) collective-permute-start(bf16[128,1024]{1,0:T(8,128)(2,1)} %pad_maximum_fusion.5), channel_id=1, source_target_pairs={{0,2},{1,3},{2,0},{3,1},{4,6},{5,7},{6,4},{7,5},{8,10},{9,11},{10,... | collective-permute-start | bytes 786440 | tf_op jit(solution)/shard_map/ppermute | solution.py:227
  528.8 10.8 %collective-permute-start.29 = (bf16[256,1024]{1,0:T(8,128)(2,1)S(1)}, bf16[256,1024]{1,0:T(8,128)(2,1)}, u32[]{:S(2)}, u32[]{:S(2)}) collective-permute-start(bf16[256,1024]{1,0:T(8,128)(2,1)S(1)} %pad_maximum_fusion.3.refs_2_), channel_id=1, source_target_pairs={{0,1},{1,0},{2,3},{3,2},{4,5},{5,4},{6,7},{7,6},{8,9},{9,8},{10,11... | collective-permute-start | bytes 1572872 | tf_op jit(solution)/shard_map/ppermute | solution.py:227
  529.8 9.7 %copy-start.9 = (f32[1024,256]{1,0:T(8,128)S(1)}, f32[1024,256]{1,0:T(8,128)}, u32[]{:S(2)}) copy-start(f32[1024,256]{1,0:T(8,128)} %refs_5_.1) | copy-start | bytes 3145732
  537.1 2.4 copy-start.8
  545.3 2.2 collective-permute-start.30
  545.8 3.6 collective-permute-start.31
  547.5 3.0 collective-permute-start.32
  550.5 4.4 collective-permute-start.33
  552.5 4.5 collective-permute-start.34
  552.5 5.4 collective-permute-start.35
  (7 other events, 12.3 us)
Sparse Core Ops, SparseCore 0:
  169.2 80.3 all-gather.2

commit v9 on v8

--- a/solution.py
+++ b/solution.py
@@ -154,7 +154,7 @@
         out_specs=pl.BlockSpec((rows, total), lambda k: (0, 0)),
         out_shape=jax.ShapeDtypeStruct((rows, total), BF16),
         scratch_shapes=[pltpu.VMEM((rows, total), F32)],
-        compiler_params=pltpu.CompilerParams(vmem_limit_bytes=18 * 2**20),
+        compiler_params=pltpu.CompilerParams(vmem_limit_bytes=56 * 2**20),
         cost_estimate=pl.CostEstimate(
             flops=rows * feats * total // 8,
             bytes_accessed=feats * (total + rows) // 8,
@@ -195,7 +195,7 @@
     for i, (a, b) in enumerate(spans):
         piece = lax.dynamic_slice(grad_basis, (a * deep, group * half), ((b - a) * deep, half))
         if i >= 2:
-            early = {2: [own_own, local_act], 3: [other[0]], 4: []}[i]
+            early = {2: [own_own, local_act], 3: [other[0], every_act], 4: [every_act]}[i]
             piece = after(piece, near[i - 2], *early)
         if i in (0, 2):
             part = flat[: 4 * slab] if i == 0 else after(flat[4 * slab :], near[0])
@@ -206,7 +206,8 @@
     far_basis = jnp.concatenate(far, axis=0)
 
     ranges = [(0, 2), (2, 4), (4, units)]
-    ties = [[near[4], far[1], other[1]], [near[4], far[2], other[1]], []]
+    phase = [near[3], near[4], other[1]]
+    ties = [[*phase, far[0], far[1]], [*phase, far[2], far[4]], []]
     partner = []
     for k, (a, b) in enumerate(ranges):
         tie = ties[k] + ([partner[k - 2]] if k >= 2 else [])

time: 567 us -> 507 us (0.89)
  starting transfers between devices: 147 us -> 67 us
  waiting for transfers between devices: 242 us -> 260 us
  Pallas kernels: 60.1 us -> 74.3 us
  local copies, waits for them, and re-layouts: 82.4 us -> 68.6 us
    ppermute x3, starting transfers between devices: 110 us -> 13 us  [chain_body(): partner.append(lax.ppermute(after(piece, *tie), 'row', ends))]
    all_gather x1, waiting for transfers between devices: 33.6 us -> 0.01 us  [chain_body(): every_act = lax.all_gather(local_act, 'row', axis=0)]
    ppermute x3, waiting for transfers between devices: 14.2 us -> 42.1 us  [chain_body(): partner.append(lax.ppermute(after(piece, *tie), 'row', ends))]
    unnamed x78 -> x54, local copies, waits for them, and re-layouts: 46.4 us -> 25.8 us
    ppermute x5, starting transfers between devices: 9.45 us -> 26.2 us  [chain_body(): near.append(lax.ppermute(piece, 'row', beside))]
    ppermute x5, waiting for transfers between devices: 7.11 us -> 21.9 us  [chain_body(): far.append(lax.ppermute(near[i], 'groups', [(0, 1), (1, 0)]))]
    pallas_call x4, Pallas kernels: 54.6 us -> 68.8 us  [project(): pl.pallas_call(functools.partial(project_kernel, len(ends), len(tokens),...]
  transfers between devices with their start and end apart: 37 -> 37, of which waited for: 17 -> 17; matrix products, arithmetic and copies ran while one was open for 12% -> 16% of each run, Pallas kernels for 10% -> 14%
where the time goes in v9:
time: 507 us; the launch traced here: 506 us
  waiting for transfers between devices  260 us (51%)
  Pallas kernels  74.3 us (15%)
  local copies, waits for them, and re-layouts  68.6 us (14%)
  starting transfers between devices  67 us (13%)
  between operations  14.5 us (3%)
  other arithmetic  14.1 us (3%)
  matrix products  7.61 us (2%)
    ppermute x5, waiting for transfers between devices, chain_body(): near.append(lax.ppermute(piece, 'row', beside))  133 us
    pallas_call x4, Pallas kernels, project(): pl.pallas_call(functools.partial(project_kernel, len(ends), len(tokens),...  68.8 us
    ppermute x15, waiting for transfers between devices, swap(): return lax.ppermute(value, axis, [(i, i ^ d) for i in range(size)])  55.2 us
    ppermute x3, waiting for transfers between devices, chain_body(): partner.append(lax.ppermute(after(piece, *tie), 'row', ends))  42.1 us
    ppermute x5, starting transfers between devices, chain_body(): near.append(lax.ppermute(piece, 'row', beside))  26.2 us
    unnamed x54, local copies, waits for them, and re-layouts  25.8 us
    ppermute x5, waiting for transfers between devices, chain_body(): far.append(lax.ppermute(near[i], 'groups', [(0, 1), (1, 0)]))  21.9 us
    ppermute x3, starting transfers between devices, chain_body(): partner.append(lax.ppermute(after(piece, *tie), 'row', ends))  13 us
  transfers between devices with their start and end apart: 37, of which 17 were waited for; matrix products, arithmetic and copies ran while one was open for 16% of the time, Pallas kernels for 14%

profile of v9, /device:TPU:0, one launch (start us, length us, event | category | flops | bytes accessed | tf_op | source)
XLA Modules:
  0.0 506.4 jit_solution(9068727065765315111)
XLA Ops:
  7.2 6.1 %fusion.18 = (bf16[2,128,8192]{2,1,0:T(8,128)(2,1)}, bf16[2,128,8192]{2,1,0:T(8,128)(2,1)}) fusion(bf16[4,128,8192]{2,1,0:T(8,128)(2,1)} %param.21), kind=kLoop, calls=%fused_computation.90 | loop fusion | bytes 16777216 | tf_op jit(solution)/shard_map/slice | solution.py:201
  13.3 2.7 collective-permute-start.3
  16.0 2.7 constant_dynamic-slice_fusion.5
  18.7 3.8 collective-permute-start
  22.5 5.4 %constant_dynamic-slice_fusion.6 = (bf16[2048,512]{1,0:T(8,128)(2,1)S(1)}, bf16[2048,512]{1,0:T(8,128)(2,1)}, bf16[2048,512]{1,0:T(8,128)(2,1)}) fusion(bf16[8192,1024]{1,0:T(8,128)(2,1)} %refs_3_.1, s32[]{:T(128)S(6)} %select_n.120), kind=kLoop, calls=%fused_computation.86 | loop fusion | bytes 12582916 | tf_op jit(solution)/shard_map/dynamic_slice | solution.py:196
  28.1 7.6 %fusion.5 = bf16[4,128,256]{2,1,0:T(8,128)(2,1)} fusion(bf16[4,128,8192]{2,1,0:T(8,128)(2,1)} %param.20, bf16[8192,256]{1,0:T(8,128)(2,1)} %param.22, f32[4,128]{1,0:T(4,128)S(1)} %compare_convert_fusion), kind=kOutput, calls=%fused_computation.18 | convolution fusion | flops 2147745792 | bytes 12847104 | tf_op jit(solution)/shard_map/ctd,dk->ctk/dot_general | solution.py:25
  35.8 11.1 %collective-permute-done = bf16[1024,512]{1,0:T(8,128)(2,1)} collective-permute-done((bf16[1024,512]{1,0:T(8,128)(2,1)}, bf16[1024,512]{1,0:T(8,128)(2,1)}, u32[]{:S(2)}, u32[]{:S(2)}) %collective-permute-start) | collective-permute-done | bytes 1048608 | tf_op jit(solution)/shard_map/ppermute | solution.py:203
  46.8 2.6 collective-permute-start.11
  50.1 15.9 %shard_map.203 = bf16[512,1024]{1,0:T(8,128)(2,1)} custom-call(s32[2]{0:T(128)} %pad_add_fusion.refs_0_, bf16[512,8192]{1,0:T(8,128)(2,1)} %bitcast.87, bf16[8192,1024]{1,0:T(8,128)(2,1)} %refs_3_.1), custom_call_target="tpu_custom_call" | custom-call | flops 536870912 | bytes 1572864 | tf_op jit(solution)/shard_map/pallas_call | solution.py:148
  66.1 1.7 collective-permute-start.2
  67.8 1.6 collective-permute-start.6
  69.4 39.2 %collective-permute-done.1 = bf16[2048,512]{1,0:T(8,128)(2,1)} collective-permute-done((bf16[2048,512]{1,0:T(8,128)(2,1)}, bf16[2048,512]{1,0:T(8,128)(2,1)}, u32[]{:S(2)}, u32[]{:S(2)}) %collective-permute-start.1) | collective-permute-done | bytes 2097184 | tf_op jit(solution)/shard_map/ppermute | solution.py:203
  108.6 1.5 collective-permute-start.7
  110.1 18.7 %collective-permute-start.4 = (bf16[2048,512]{1,0:T(8,128)(2,1)S(1)}, bf16[2048,512]{1,0:T(8,128)(2,1)}, u32[]{:S(2)}, u32[]{:S(2)}) collective-permute-start(bf16[2048,512]{1,0:T(8,128)(2,1)S(1)} %get-tuple-element.14), channel_id=1, source_target_pairs={{0,4},{4,0},{8,12},{12,8},{1,5},{5,1},{9,13},{13,9},{2,6},{6,2},{1... | collective-permute-start | bytes 6291464 | tf_op jit(solution)/shard_map/ppermute | solution.py:203
  128.8 24.8 %collective-permute-done.2 = bf16[2048,512]{1,0:T(8,128)(2,1)} collective-permute-done((bf16[2048,512]{1,0:T(8,128)(2,1)}, bf16[2048,512]{1,0:T(8,128)(2,1)}, u32[]{:S(2)}, u32[]{:S(2)}) %collective-permute-start.2) | collective-permute-done | bytes 2097184 | tf_op jit(solution)/shard_map/ppermute | solution.py:203
  153.6 2.1 collective-permute-start.5
  155.6 1.5 collective-permute-start.8
  157.2 4.6 slice_bitcast_fusion
  161.8 58.1 %collective-permute-done.5 = bf16[1024,512]{1,0:T(8,128)(2,1)} collective-permute-done((bf16[1024,512]{1,0:T(8,128)(2,1)S(1)}, bf16[1024,512]{1,0:T(8,128)(2,1)}, u32[]{:S(2)}, u32[]{:S(2)}) %collective-permute-start.5) | collective-permute-done | bytes 1048608 | tf_op jit(solution)/shard_map/ppermute | solution.py:203
  219.8 5.2 %collective-permute-start.12 = (bf16[128,8192]{1,0:T(8,128)(2,1)}, bf16[128,8192]{1,0:T(8,128)(2,1)S(1)}, u32[]{:S(2)}, u32[]{:S(2)}) collective-permute-start(bf16[128,8192]{1,0:T(8,128)(2,1)} %get-tuple-element.17), channel_id=1, source_target_pairs={{0,12},{12,0},{1,13},{13,1},{2,14},{14,2},{3,15},{15,3},{16,28},{2... | collective-permute-start | bytes 6291464 | tf_op jit(solution)/shard_map/ppermute | solution.py:215
  225.0 1.6 collective-permute-start.10
  227.2 2.3 constant_dynamic-update-slice_fusion.4
  229.5 21.9 %collective-permute-done.10 = bf16[1024,512]{1,0:T(8,128)(2,1)S(1)} collective-permute-done((bf16[1024,512]{1,0:T(8,128)(2,1)}, bf16[1024,512]{1,0:T(8,128)(2,1)S(1)}, u32[]{:S(2)}, u32[]{:S(2)}) %collective-permute-start.10) | collective-permute-done | bytes 1048608 | tf_op jit(solution)/shard_map/ppermute | solution.py:204
  252.4 2.4 collective-permute-start.16
  254.8 1.3 constant_dynamic-slice_fusion.3
  256.7 1.3 gather_fusion.3
  257.9 3.0 constant_dynamic-update-slice_fusion.3
  261.0 11.3 %collective-permute-done.12.refs_1_ = bf16[128,8192]{1,0:T(8,128)(2,1)S(1)} collective-permute-done((bf16[128,8192]{1,0:T(8,128)(2,1)}, bf16[128,8192]{1,0:T(8,128)(2,1)S(1)}, u32[]{:S(2)}, u32[]{:S(2)}) %collective-permute-start.12) | collective-permute-done | bytes 2097184 | tf_op jit(solution)/shard_map/ppermute | solution.py:215
  272.3 5.4 %collective-permute-start.20 = (bf16[256,8192]{1,0:T(8,128)(2,1)}, bf16[256,8192]{1,0:T(8,128)(2,1)}, u32[]{:S(2)}, u32[]{:S(2)}) collective-permute-start(bf16[256,8192]{1,0:T(8,128)(2,1)} %bitcast.7), channel_id=1, source_target_pairs={{0,12},{12,0},{1,13},{13,1},{2,14},{14,2},{3,15},{15,3},{16,28},{2... | collective-permute-start | bytes 12582920 | tf_op jit(solution)/shard_map/ppermute | solution.py:215
  277.7 2.3 constant_dynamic-update-slice_fusion.9
  279.9 3.0 constant_dynamic-update-slice_fusion.2
  283.0 3.0 constant_dynamic-update-slice_fusion.8
  286.0 3.1 constant_dynamic-update-slice_fusion.7
  289.1 3.2 constant_dynamic-update-slice_fusion.1
  292.2 2.3 constant_dynamic-update-slice_fusion.refs_2_.refs_5_.refs_4_
  294.6 3.0 constant_dynamic-update-slice_fusion.6
  298.7 18.7 %collective-permute-done.16.refs_2_ = bf16[128,8192]{1,0:T(8,128)(2,1)} collective-permute-done((bf16[128,8192]{1,0:T(8,128)(2,1)}, bf16[128,8192]{1,0:T(8,128)(2,1)}, u32[]{:S(2)}, u32[]{:S(2)}) %collective-permute-start.16) | collective-permute-done | bytes 2097184 | tf_op jit(solution)/shard_map/ppermute | solution.py:215
  317.3 18.7 %shard_map.205 = bf16[256,2048]{1,0:T(8,128)(2,1)} custom-call(s32[2]{0:T(128)} %pad_add_fusion.refs_0_, bf16[128,8192]{1,0:T(8,128)(2,1)} %copy-done.6, bf16[128,8192]{1,0:T(8,128)(2,1)} %collective-permute-done.16.refs_2_, bf16[256,8192]{1,0:T(8,128)(2,1)} %collective-permute-done.3.refs_3_, bf16[8192,1024]{1,0:T(8,128)(2,1)} %refs_3_.1, ...), custom_call_target="tpu_custom_call" | custom-call | flops 536870912 | bytes 2359296 | tf_op jit(solution)/shard_map/pallas_call | solution.py:148
  336.1 1.9 dynamic-slice_bitcast_fusion.8
  338.0 1.5 collective-permute-start.18
  339.5 15.6 %shard_map.204 = bf16[512,1024]{1,0:T(8,128)(2,1)} custom-call(s32[2]{0:T(128)} %pad_add_fusion.refs_0_, bf16[512,8192]{1,0:T(8,128)(2,1)} %bitcast.88, bf16[8192,512]{1,0:T(8,128)(2,1)} %constant_dynamic-update-slice_fusion.refs_2_.refs_5_.refs_4_, bf16[8192,512]{1,0:T(8,128)(2,1)} %constant_dynamic-update-slice_fusion.5.refs_3_.refs_6_.refs_5_), custom_call_target="tpu_custom_call" | custom-call | flops 536870912 | bytes 1572864 | tf_op jit(solution)/shard_map/pallas_call | solution.py:148
  355.1 1.4 pad_maximum_fusion
  361.2 1.3 gather_fusion.6
  362.5 1.3 gather_fusion.9
  363.8 24.8 %collective-permute-done.19 = bf16[2,32,2048]{2,1,0:T(8,128)(2,1)} collective-permute-done((bf16[2,32,2048]{2,1,0:T(8,128)(2,1)}, bf16[2,32,2048]{2,1,0:T(8,128)(2,1)}, u32[]{:S(2)}, u32[]{:S(2)}) %collective-permute-start.19) | collective-permute-done | bytes 262176 | tf_op jit(solution)/shard_map/ppermute | solution.py:228
  388.6 1.3 fusion.16
  389.9 1.7 fusion.10
  392.6 1.3 gather_fusion.1
  393.9 1.3 gather_fusion.4
  395.1 12.1 %collective-permute-done.20.refs_1_ = bf16[256,8192]{1,0:T(8,128)(2,1)} collective-permute-done((bf16[256,8192]{1,0:T(8,128)(2,1)}, bf16[256,8192]{1,0:T(8,128)(2,1)}, u32[]{:S(2)}, u32[]{:S(2)}) %collective-permute-start.20) | collective-permute-done | bytes 4194336 | tf_op jit(solution)/shard_map/ppermute | solution.py:215
  407.2 18.5 %shard_map.206 = bf16[256,2048]{1,0:T(8,128)(2,1)} custom-call(s32[2]{0:T(128)} %pad_add_fusion.refs_0_, bf16[256,8192]{1,0:T(8,128)(2,1)} %collective-permute-done.20.refs_1_, bf16[256,8192]{1,0:T(8,128)(2,1)} %collective-permute-done.11.refs_2_, bf16[8192,1024]{1,0:T(8,128)(2,1)} %refs_3_.1, ...), custom_call_target="tpu_custom_call" | custom-call | flops 536870912 | bytes 2359296 | tf_op jit(solution)/shard_map/pallas_call | solution.py:148
  427.0 1.6 collective-permute-start.25
  429.7 1.5 collective-permute-start.22
  432.3 3.9 collective-permute-done.25
  436.2 4.7 collective-permute-done.26
  442.1 16.1 %collective-permute-done.22 = bf16[384,1024]{1,0:T(8,128)(2,1)S(1)} collective-permute-done((bf16[384,1024]{1,0:T(8,128)(2,1)S(1)}, bf16[384,1024]{1,0:T(8,128)(2,1)S(1)}, u32[]{:S(2)}, u32[]{:S(2)}) %collective-permute-start.22) | collective-permute-done | bytes 786464 | tf_op jit(solution)/shard_map/ppermute | solution.py:228
  459.1 1.5 collective-permute-start.28
  462.5 5.6 %collective-permute-done.28 = bf16[128,1024]{1,0:T(8,128)(2,1)} collective-permute-done((bf16[128,1024]{1,0:T(8,128)(2,1)}, bf16[128,1024]{1,0:T(8,128)(2,1)}, u32[]{:S(2)}, u32[]{:S(2)}) %collective-permute-start.28) | collective-permute-done | bytes 262176 | tf_op jit(solution)/shard_map/ppermute | solution.py:228
  470.8 2.2 gather_fusion.11
  479.0 5.5 %shard_map.207 = (f32[4,1024,256]{2,1,0:T(8,128)}, f32[4,16,256]{2,1,0:T(8,128)S(1)}) custom-call(bf16[768,1024]{1,0:T(8,128)(2,1)S(1)} %constant_dynamic-update-slice_fusion.10.refs_0_, bf16[768,1024]{1,0:T(8,128)(2,1)} %collective-permute-done.23.refs_1_, bf16[256,1024]{1,0:T(8,128)(2,1)S(1)} %pad_maximum_fusion.3.refs_2_, ...), custom_call_target="tpu_custom_call" | custom-call | tf_op jit(solution)/shard_map/pallas_call | solution.py:53
  485.2 1.5 collective-permute-start.31
  486.7 2.1 collective-permute-done.31
  489.7 3.8 collective-permute-start.34
  495.1 3.8 collective-permute-done.35
  (131 shorter events, 29.4 us)
Async XLA Ops:
  7.2 103.0 %all-gather.3.cloned.1.call-start = ((), (), s32[]{:S(2)}) async-start(), calls=%async_computation | async-start | bytes 1310720 | tf_op jit(solution)/shard_map/all_gather | solution.py:191
  13.3 96.9 %collective-permute-start.3 = (bf16[256,8192]{1,0:T(8,128)(2,1)}, bf16[256,8192]{1,0:T(8,128)(2,1)}, u32[]{:S(2)}, u32[]{:S(2)}) collective-permute-start(bf16[256,8192]{1,0:T(8,128)(2,1)} %bitcast.4), channel_id=1, source_target_pairs={{4,8},{8,4},{5,9},{9,5},{6,10},{10,6},{7,11},{11,7},{20,24},{24,20... | collective-permute-start | bytes 12582920 | tf_op jit(solution)/shard_map/ppermute | solution.py:202
  18.7 9.2 %copy-start.17 = (s32[2048]{0:T(1024)S(1)}, s32[2048]{0:T(1024)}, u32[]{:S(2)}) copy-start(s32[2048]{0:T(1024)} %param.27) | copy-start | bytes 24580
  18.7 9.2 %copy-start.18 = (s32[4]{0:T(128)S(1)}, s32[4]{0:T(128)}, u32[]{:S(2)}) copy-start(s32[4]{0:T(128)} %param.26) | copy-start | bytes 52
  18.7 28.1 %collective-permute-start = (bf16[1024,512]{1,0:T(8,128)(2,1)}, bf16[1024,512]{1,0:T(8,128)(2,1)}, u32[]{:S(2)}, u32[]{:S(2)}) collective-permute-start(bf16[1024,512]{1,0:T(8,128)(2,1)} %get-tuple-element.25), channel_id=1, source_target_pairs={{0,4},{4,0},{8,12},{12,8},{1,5},{5,1},{9,13},{13,9},{2,6},{6,2},{1... | collective-permute-start | bytes 3145736 | tf_op jit(solution)/shard_map/ppermute | solution.py:203
  27.8 80.8 %collective-permute-start.1 = (bf16[2048,512]{1,0:T(8,128)(2,1)}, bf16[2048,512]{1,0:T(8,128)(2,1)}, u32[]{:S(2)}, u32[]{:S(2)}) collective-permute-start(bf16[2048,512]{1,0:T(8,128)(2,1)} %get-tuple-element.28), channel_id=1, source_target_pairs={{0,4},{4,0},{8,12},{12,8},{1,5},{5,1},{9,13},{13,9},{2,6},{6,2},{1... | collective-permute-start | bytes 6291464 | tf_op jit(solution)/shard_map/ppermute | solution.py:203
  46.8 173.0 %collective-permute-start.11 = (bf16[256,8192]{1,0:T(8,128)(2,1)}, bf16[256,8192]{1,0:T(8,128)(2,1)}, u32[]{:S(2)}, u32[]{:S(2)}) collective-permute-start(bf16[256,8192]{1,0:T(8,128)(2,1)} %bitcast.7), channel_id=1, source_target_pairs={{4,8},{8,4},{5,9},{9,5},{6,10},{10,6},{7,11},{11,7},{20,24},{24,20... | collective-permute-start | bytes 12582920 | tf_op jit(solution)/shard_map/ppermute | solution.py:202
  66.1 87.5 %collective-permute-start.2 = (bf16[2048,512]{1,0:T(8,128)(2,1)}, bf16[2048,512]{1,0:T(8,128)(2,1)}, u32[]{:S(2)}, u32[]{:S(2)}) collective-permute-start(bf16[2048,512]{1,0:T(8,128)(2,1)} %get-tuple-element.13), channel_id=1, source_target_pairs={{0,4},{4,0},{8,12},{12,8},{1,5},{5,1},{9,13},{13,9},{2,6},{6,2},{1... | collective-permute-start | bytes 6291464 | tf_op jit(solution)/shard_map/ppermute | solution.py:203
  67.8 87.8 %collective-permute-start.6 = (bf16[1024,512]{1,0:T(8,128)(2,1)}, bf16[1024,512]{1,0:T(8,128)(2,1)}, u32[]{:S(2)}, u32[]{:S(2)}) collective-permute-start(bf16[1024,512]{1,0:T(8,128)(2,1)} %collective-permute-done), channel_id=1, source_target_pairs={{0,16},{16,0},{1,17},{17,1},{2,18},{18,2},{3,19},{19,3},{4,20},{20... | collective-permute-start | bytes 3145736 | tf_op jit(solution)/shard_map/ppermute | solution.py:204
  108.6 53.1 %collective-permute-start.7 = (bf16[2048,512]{1,0:T(8,128)(2,1)}, bf16[2048,512]{1,0:T(8,128)(2,1)}, u32[]{:S(2)}, u32[]{:S(2)}) collective-permute-start(bf16[2048,512]{1,0:T(8,128)(2,1)} %collective-permute-done.1), channel_id=1, source_target_pairs={{0,16},{16,0},{1,17},{17,1},{2,18},{18,2},{3,19},{19,3},{4,20},{20... | collective-permute-start | bytes 6291464 | tf_op jit(solution)/shard_map/ppermute | solution.py:204
  110.1 109.7 %collective-permute-start.4 = (bf16[2048,512]{1,0:T(8,128)(2,1)S(1)}, bf16[2048,512]{1,0:T(8,128)(2,1)}, u32[]{:S(2)}, u32[]{:S(2)}) collective-permute-start(bf16[2048,512]{1,0:T(8,128)(2,1)S(1)} %get-tuple-element.14), channel_id=1, source_target_pairs={{0,4},{4,0},{8,12},{12,8},{1,5},{5,1},{9,13},{13,9},{2,6},{6,2},{1... | collective-permute-start | bytes 6291464 | tf_op jit(solution)/shard_map/ppermute | solution.py:203
  153.6 73.5 %copy-start.21 = (s32[4]{0:T(128)S(1)}, s32[4]{0:T(128)}, u32[]{:S(2)}) copy-start(s32[4]{0:T(128)} %constant.100) | copy-start | bytes 52
  153.6 73.6 %copy-start.19 = (s32[4]{0:T(128)S(1)}, s32[4]{0:T(128)}, u32[]{:S(2)}) copy-start(s32[4]{0:T(128)} %constant.101) | copy-start | bytes 52
  153.6 73.6 %copy-start.20 = (s32[4]{0:T(128)S(1)}, s32[4]{0:T(128)}, u32[]{:S(2)}) copy-start(s32[4]{0:T(128)} %constant.102) | copy-start | bytes 52
  153.6 66.3 %collective-permute-start.5 = (bf16[1024,512]{1,0:T(8,128)(2,1)S(1)}, bf16[1024,512]{1,0:T(8,128)(2,1)}, u32[]{:S(2)}, u32[]{:S(2)}) collective-permute-start(bf16[1024,512]{1,0:T(8,128)(2,1)S(1)} %get-tuple-element.15), channel_id=1, source_target_pairs={{0,4},{4,0},{8,12},{12,8},{1,5},{5,1},{9,13},{13,9},{2,6},{6,2},{1... | collective-permute-start | bytes 3145736 | tf_op jit(solution)/shard_map/ppermute | solution.py:203
  155.6 73.9 %collective-permute-start.8 = (bf16[2048,512]{1,0:T(8,128)(2,1)}, bf16[2048,512]{1,0:T(8,128)(2,1)}, u32[]{:S(2)}, u32[]{:S(2)}) collective-permute-start(bf16[2048,512]{1,0:T(8,128)(2,1)} %collective-permute-done.2), channel_id=1, source_target_pairs={{0,16},{16,0},{1,17},{17,1},{2,18},{18,2},{3,19},{19,3},{4,20},{20... | collective-permute-start | bytes 6291464 | tf_op jit(solution)/shard_map/ppermute | solution.py:204
  219.8 52.5 %collective-permute-start.12 = (bf16[128,8192]{1,0:T(8,128)(2,1)}, bf16[128,8192]{1,0:T(8,128)(2,1)S(1)}, u32[]{:S(2)}, u32[]{:S(2)}) collective-permute-start(bf16[128,8192]{1,0:T(8,128)(2,1)} %get-tuple-element.17), channel_id=1, source_target_pairs={{0,12},{12,0},{1,13},{13,1},{2,14},{14,2},{3,15},{15,3},{16,28},{2... | collective-permute-start | bytes 6291464 | tf_op jit(solution)/shard_map/ppermute | solution.py:215
  225.0 26.4 %collective-permute-start.10 = (bf16[1024,512]{1,0:T(8,128)(2,1)}, bf16[1024,512]{1,0:T(8,128)(2,1)S(1)}, u32[]{:S(2)}, u32[]{:S(2)}) collective-permute-start(bf16[1024,512]{1,0:T(8,128)(2,1)} %collective-permute-done.5), channel_id=1, source_target_pairs={{0,16},{16,0},{1,17},{17,1},{2,18},{18,2},{3,19},{19,3},{4,20},{20... | collective-permute-start | bytes 3145736 | tf_op jit(solution)/shard_map/ppermute | solution.py:204
  226.6 68.0 %collective-permute-start.9 = (bf16[2048,512]{1,0:T(8,128)(2,1)}, bf16[2048,512]{1,0:T(8,128)(2,1)}, u32[]{:S(2)}, u32[]{:S(2)}) collective-permute-start(bf16[2048,512]{1,0:T(8,128)(2,1)} %collective-permute-done.4), channel_id=1, source_target_pairs={{0,16},{16,0},{1,17},{17,1},{2,18},{18,2},{3,19},{19,3},{4,20},{20... | collective-permute-start | bytes 6291464 | tf_op jit(solution)/shard_map/ppermute | solution.py:204
  251.4 1.0 copy-start.8
  252.4 65.0 %collective-permute-start.16 = (bf16[128,8192]{1,0:T(8,128)(2,1)}, bf16[128,8192]{1,0:T(8,128)(2,1)}, u32[]{:S(2)}, u32[]{:S(2)}) collective-permute-start(bf16[128,8192]{1,0:T(8,128)(2,1)} %get-tuple-element.19), channel_id=1, source_target_pairs={{0,12},{12,0},{1,13},{13,1},{2,14},{14,2},{3,15},{15,3},{16,28},{2... | collective-permute-start | bytes 6291464 | tf_op jit(solution)/shard_map/ppermute | solution.py:215
  272.3 13.7 %copy-start.6 = (bf16[128,8192]{1,0:T(8,128)(2,1)}, bf16[128,8192]{1,0:T(8,128)(2,1)S(1)}, u32[]{:S(2)}) copy-start(bf16[128,8192]{1,0:T(8,128)(2,1)S(1)} %collective-permute-done.12.refs_1_) | copy-start | bytes 6291460
  272.3 134.9 %collective-permute-start.20 = (bf16[256,8192]{1,0:T(8,128)(2,1)}, bf16[256,8192]{1,0:T(8,128)(2,1)}, u32[]{:S(2)}, u32[]{:S(2)}) collective-permute-start(bf16[256,8192]{1,0:T(8,128)(2,1)} %bitcast.7), channel_id=1, source_target_pairs={{0,12},{12,0},{1,13},{13,1},{2,14},{14,2},{3,15},{15,3},{16,28},{2... | collective-permute-start | bytes 12582920 | tf_op jit(solution)/shard_map/ppermute | solution.py:215
  289.1 8.5 %copy-start.9 = (bf16[1024,512]{1,0:T(8,128)(2,1)S(1)}, bf16[1024,512]{1,0:T(8,128)(2,1)}, u32[]{:S(2)}) copy-start(bf16[1024,512]{1,0:T(8,128)(2,1)} %copy-done.8) | copy-start | bytes 3145732
  338.0 20.6 %collective-permute-start.17 = (bf16[2,32,2048]{2,1,0:T(8,128)(2,1)S(1)}, bf16[2,32,2048]{2,1,0:T(8,128)(2,1)S(1)}, u32[]{:S(2)}, u32[]{:S(2)}) collective-permute-start(bf16[2,32,2048]{2,1,0:T(8,128)(2,1)S(1)} %get-tuple-element.43), channel_id=1, source_target_pairs={{0,1},{1,0},{2,3},{3,2},{4,5},{5,4},{6,7},{7,6},{8,9},{9,8},{10,11... | collective-permute-start | bytes 786440 | tf_op jit(solution)/shard_map/ppermute | solution.py:228
  338.0 17.1 %copy-start.2 = (bf16[512,1024]{1,0:T(8,128)(2,1)S(1)}, bf16[512,1024]{1,0:T(8,128)(2,1)}, u32[]{:S(2)}) copy-start(bf16[512,1024]{1,0:T(8,128)(2,1)} %shard_map.203) | copy-start | bytes 3145732
  338.0 21.6 %collective-permute-start.18 = (bf16[2,32,2048]{2,1,0:T(8,128)(2,1)S(1)}, bf16[2,32,2048]{2,1,0:T(8,128)(2,1)S(1)}, u32[]{:S(2)}, u32[]{:S(2)}) collective-permute-start(bf16[2,32,2048]{2,1,0:T(8,128)(2,1)S(1)} %get-tuple-element.45), channel_id=1, source_target_pairs={{0,2},{1,3},{2,0},{3,1},{4,6},{5,7},{6,4},{7,5},{8,10},{9,11},{10,... | collective-permute-start | bytes 786440 | tf_op jit(solution)/shard_map/ppermute | solution.py:228
  355.1 5.2 %copy-start.11 = (bf16[4,4,32,256]{3,2,1,0:T(8,128)(2,1)S(1)}, bf16[4,4,32,256]{3,2,1,0:T(8,128)(2,1)}, u32[]{:S(2)}) copy-start(bf16[4,4,32,256]{3,2,1,0:T(8,128)(2,1)} %gather_fusion.3) | copy-start | bytes 786436
  357.7 32.2 %collective-permute-start.13 = (bf16[4,32,2048]{2,1,0:T(8,128)(2,1)}, bf16[4,32,2048]{2,1,0:T(8,128)(2,1)}, u32[]{:S(2)}, u32[]{:S(2)}) collective-permute-start(bf16[4,32,2048]{2,1,0:T(8,128)(2,1)} %get-tuple-element.33), channel_id=1, source_target_pairs={{0,1},{1,0},{2,3},{3,2},{4,5},{5,4},{6,7},{7,6},{8,9},{9,8},{10,11... | collective-permute-start | bytes 1572872 | tf_op jit(solution)/shard_map/ppermute | solution.py:228
  357.9 32.0 %collective-permute-start.14 = (bf16[4,32,2048]{2,1,0:T(8,128)(2,1)}, bf16[4,32,2048]{2,1,0:T(8,128)(2,1)}, u32[]{:S(2)}, u32[]{:S(2)}) collective-permute-start(bf16[4,32,2048]{2,1,0:T(8,128)(2,1)} %get-tuple-element.35), channel_id=1, source_target_pairs={{0,2},{1,3},{2,0},{3,1},{4,6},{5,7},{6,4},{7,5},{8,10},{9,11},{10,... | collective-permute-start | bytes 1572872 | tf_op jit(solution)/shard_map/ppermute | solution.py:228
  358.5 2.7 copy-start.15
  358.5 31.4 %collective-permute-start.15 = (bf16[4,32,2048]{2,1,0:T(8,128)(2,1)}, bf16[4,32,2048]{2,1,0:T(8,128)(2,1)}, u32[]{:S(2)}, u32[]{:S(2)}) collective-permute-start(bf16[4,32,2048]{2,1,0:T(8,128)(2,1)} %get-tuple-element.34), channel_id=1, source_target_pairs={{0,3},{1,2},{2,1},{3,0},{4,7},{5,6},{6,5},{7,4},{8,11},{9,10},{10,... | collective-permute-start | bytes 1572872 | tf_op jit(solution)/shard_map/ppermute | solution.py:228
  359.6 1.6 copy-start.16
  359.6 29.0 %collective-permute-start.19 = (bf16[2,32,2048]{2,1,0:T(8,128)(2,1)}, bf16[2,32,2048]{2,1,0:T(8,128)(2,1)}, u32[]{:S(2)}, u32[]{:S(2)}) collective-permute-start(bf16[2,32,2048]{2,1,0:T(8,128)(2,1)} %get-tuple-element.44), channel_id=1, source_target_pairs={{0,3},{1,2},{2,1},{3,0},{4,7},{5,6},{6,5},{7,4},{8,11},{9,10},{10,... | collective-permute-start | bytes 786440 | tf_op jit(solution)/shard_map/ppermute | solution.py:228
  361.2 31.3 %copy-start.4 = (bf16[4,4,32,256]{3,2,0,1:T(8,128)(2,1)S(1)}, bf16[4,4,32,256]{3,2,0,1:T(8,128)(2,1)}, u32[]{:S(2)}) copy-start(bf16[4,4,32,256]{3,2,0,1:T(8,128)(2,1)} %get-tuple-element.55) | copy-start | bytes 786436
  362.5 30.1 %copy-start.3 = (bf16[4,4,32,256]{3,2,0,1:T(8,128)(2,1)S(1)}, bf16[4,4,32,256]{3,2,0,1:T(8,128)(2,1)}, u32[]{:S(2)}) copy-start(bf16[4,4,32,256]{3,2,0,1:T(8,128)(2,1)} %get-tuple-element.54) | copy-start | bytes 786436
  363.8 28.0 %copy-start.13 = (bf16[4,4,32,256]{3,2,1,0:T(8,128)(2,1)S(1)}, bf16[4,4,32,256]{3,2,1,0:T(8,128)(2,1)}, u32[]{:S(2)}) copy-start(bf16[4,4,32,256]{3,2,1,0:T(8,128)(2,1)} %gather_fusion.6) | copy-start | bytes 786436
  363.8 28.0 %copy-start.14 = (bf16[4,4,32,256]{3,2,1,0:T(8,128)(2,1)S(1)}, bf16[4,4,32,256]{3,2,1,0:T(8,128)(2,1)}, u32[]{:S(2)}) copy-start(bf16[4,4,32,256]{3,2,1,0:T(8,128)(2,1)} %gather_fusion.9) | copy-start | bytes 786436
  391.7 37.2 %collective-permute-start.21 = (bf16[192,1024]{1,0:T(8,128)(2,1)S(1)}, bf16[192,1024]{1,0:T(8,128)(2,1)S(1)}, u32[]{:S(2)}, u32[]{:S(2)}) collective-permute-start(bf16[192,1024]{1,0:T(8,128)(2,1)S(1)} %get-tuple-element.46), channel_id=1, source_target_pairs={{0,4},{4,0},{8,12},{12,8},{1,5},{5,1},{9,13},{13,9},{2,6},{6,2},{1... | collective-permute-start | bytes 1179656 | tf_op jit(solution)/shard_map/ppermute | solution.py:228
  425.7 32.6 %copy-start.12 = (bf16[4,4,32,256]{3,2,1,0:T(8,128)(2,1)S(1)}, bf16[4,4,32,256]{3,2,1,0:T(8,128)(2,1)}, u32[]{:S(2)}) copy-start(bf16[4,4,32,256]{3,2,1,0:T(8,128)(2,1)} %gather_fusion.1) | copy-start | bytes 786436
  426.9 33.7 %copy-start.10 = (bf16[4,4,32,256]{3,2,1,0:T(8,128)(2,1)S(1)}, bf16[4,4,32,256]{3,2,1,0:T(8,128)(2,1)}, u32[]{:S(2)}) copy-start(bf16[4,4,32,256]{3,2,1,0:T(8,128)(2,1)} %gather_fusion.4) | copy-start | bytes 786436
  427.0 5.3 %collective-permute-start.24 = (bf16[2,32,2048]{2,1,0:T(8,128)(2,1)S(1)}, bf16[2,32,2048]{2,1,0:T(8,128)(2,1)S(1)}, u32[]{:S(2)}, u32[]{:S(2)}) collective-permute-start(bf16[2,32,2048]{2,1,0:T(8,128)(2,1)S(1)} %get-tuple-element.40), channel_id=1, source_target_pairs={{0,1},{1,0},{2,3},{3,2},{4,5},{5,4},{6,7},{7,6},{8,9},{9,8},{10,11... | collective-permute-start | bytes 786440 | tf_op jit(solution)/shard_map/ppermute | solution.py:228
  427.0 9.2 %collective-permute-start.25 = (bf16[2,32,2048]{2,1,0:T(8,128)(2,1)S(1)}, bf16[2,32,2048]{2,1,0:T(8,128)(2,1)S(1)}, u32[]{:S(2)}, u32[]{:S(2)}) collective-permute-start(bf16[2,32,2048]{2,1,0:T(8,128)(2,1)S(1)} %get-tuple-element.42), channel_id=1, source_target_pairs={{0,2},{1,3},{2,0},{3,1},{4,6},{5,7},{6,4},{7,5},{8,10},{9,11},{10,... | collective-permute-start | bytes 786440 | tf_op jit(solution)/shard_map/ppermute | solution.py:228
  428.6 12.3 %collective-permute-start.26 = (bf16[2,32,2048]{2,1,0:T(8,128)(2,1)S(1)}, bf16[2,32,2048]{2,1,0:T(8,128)(2,1)S(1)}, u32[]{:S(2)}, u32[]{:S(2)}) collective-permute-start(bf16[2,32,2048]{2,1,0:T(8,128)(2,1)S(1)} %get-tuple-element.41), channel_id=1, source_target_pairs={{0,3},{1,2},{2,1},{3,0},{4,7},{5,6},{6,5},{7,4},{8,11},{9,10},{10,... | collective-permute-start | bytes 786440 | tf_op jit(solution)/shard_map/ppermute | solution.py:228
  428.9 0.8 copy-start.7
  429.7 28.6 %collective-permute-start.22 = (bf16[384,1024]{1,0:T(8,128)(2,1)S(1)}, bf16[384,1024]{1,0:T(8,128)(2,1)S(1)}, u32[]{:S(2)}, u32[]{:S(2)}) collective-permute-start(bf16[384,1024]{1,0:T(8,128)(2,1)S(1)} %pad_maximum_fusion.2), channel_id=1, source_target_pairs={{0,2},{1,3},{2,0},{3,1},{4,6},{5,7},{6,4},{7,5},{8,10},{9,11},{10,... | collective-permute-start | bytes 2359304 | tf_op jit(solution)/shard_map/ppermute | solution.py:228
  431.2 30.7 %copy-start.5 = (bf16[4,4,32,256]{3,2,0,1:T(8,128)(2,1)S(1)}, bf16[4,4,32,256]{3,2,0,1:T(8,128)(2,1)}, u32[]{:S(2)}) copy-start(bf16[4,4,32,256]{3,2,0,1:T(8,128)(2,1)} %get-tuple-element.52) | copy-start | bytes 786436
  442.0 16.4 %collective-permute-start.27 = (bf16[64,1024]{1,0:T(8,128)(2,1)S(1)}, bf16[64,1024]{1,0:T(8,128)(2,1)S(1)}, u32[]{:S(2)}, u32[]{:S(2)}) collective-permute-start(bf16[64,1024]{1,0:T(8,128)(2,1)S(1)} %get-tuple-element.49), channel_id=1, source_target_pairs={{0,4},{4,0},{8,12},{12,8},{1,5},{5,1},{9,13},{13,9},{2,6},{6,2},{1... | collective-permute-start | bytes 393224 | tf_op jit(solution)/shard_map/ppermute | solution.py:228
  458.3 20.7 %collective-permute-start.23 = (bf16[768,1024]{1,0:T(8,128)(2,1)S(1)}, bf16[768,1024]{1,0:T(8,128)(2,1)}, u32[]{:S(2)}, u32[]{:S(2)}) collective-permute-start(bf16[768,1024]{1,0:T(8,128)(2,1)S(1)} %constant_dynamic-update-slice_fusion.10.refs_0_), channel_id=1, source_target_pairs={{0,1},{1,0},{2,3},{3,2},{4,5},{5,4},{6,7},{7,6},{8,9},{9,8},{10,11... | collective-permute-start | bytes 4718600 | tf_op jit(solution)/shard_map/ppermute | solution.py:228
  459.1 9.0 %collective-permute-start.28 = (bf16[128,1024]{1,0:T(8,128)(2,1)}, bf16[128,1024]{1,0:T(8,128)(2,1)}, u32[]{:S(2)}, u32[]{:S(2)}) collective-permute-start(bf16[128,1024]{1,0:T(8,128)(2,1)} %pad_maximum_fusion.5), channel_id=1, source_target_pairs={{0,2},{1,3},{2,0},{3,1},{4,6},{5,7},{6,4},{7,5},{8,10},{9,11},{10,... | collective-permute-start | bytes 786440 | tf_op jit(solution)/shard_map/ppermute | solution.py:228
  469.1 9.8 %collective-permute-start.29 = (bf16[256,1024]{1,0:T(8,128)(2,1)S(1)}, bf16[256,1024]{1,0:T(8,128)(2,1)}, u32[]{:S(2)}, u32[]{:S(2)}) collective-permute-start(bf16[256,1024]{1,0:T(8,128)(2,1)S(1)} %pad_maximum_fusion.3.refs_2_), channel_id=1, source_target_pairs={{0,1},{1,0},{2,3},{3,2},{4,5},{5,4},{6,7},{7,6},{8,9},{9,8},{10,11... | collective-permute-start | bytes 1572872 | tf_op jit(solution)/shard_map/ppermute | solution.py:228
  469.3 9.7 %copy-start.1 = (f32[1024,256]{1,0:T(8,128)S(1)}, f32[1024,256]{1,0:T(8,128)}, u32[]{:S(2)}) copy-start(f32[1024,256]{1,0:T(8,128)} %refs_5_.1) | copy-start | bytes 3145732
  476.6 2.4 copy-start
  484.7 2.0 collective-permute-start.30
  485.2 3.6 collective-permute-start.31
  486.7 3.0 collective-permute-start.32
  489.7 4.4 collective-permute-start.33
  489.7 5.4 %collective-permute-start.34 = (f32[4,4]{1,0:T(4,128)S(1)}, f32[4,4]{1,0:T(4,128)S(1)}, u32[]{:S(2)}, u32[]{:S(2)}) collective-permute-start(f32[4,4]{1,0:T(4,128)S(1)} %add_add_fusion.1), channel_id=1, source_target_pairs={{0,8},{4,12},{8,0},{12,4},{1,9},{5,13},{9,1},{13,5},{2,10},{6,14},... | collective-permute-start | bytes 200 | tf_op jit(solution)/shard_map/ppermute | solution.py:173
  493.5 5.4 %collective-permute-start.35 = (f32[4,4]{1,0:T(4,128)S(1)}, f32[4,4]{1,0:T(4,128)S(1)}, u32[]{:S(2)}, u32[]{:S(2)}) collective-permute-start(f32[4,4]{1,0:T(4,128)S(1)} %add_add_fusion.1), channel_id=1, source_target_pairs={{0,12},{4,8},{8,4},{12,0},{1,13},{5,9},{9,5},{13,1},{2,14},{6,10},... | collective-permute-start | bytes 200 | tf_op jit(solution)/shard_map/ppermute | solution.py:173
Sparse Core Ops, SparseCore 0:
  67.9 42.1 all-gather.2

commit v10 on v9

--- a/solution.py
+++ b/solution.py
@@ -214,14 +214,29 @@
         piece = flat[a * slab : b * slab]
         partner.append(lax.ppermute(after(piece, *tie), "row", ends))
 
-    own_end = project(flags, [(flat, 0, cands * tok)], [], [near_basis, after(far_basis, partner[0])])
-    bases = [grad_basis, near_basis, far_basis]
     sub, full = tok // parts, cands * tok
-    products = [
-        jnp.concatenate([own_own, own_end], axis=1),
-        project(flags, [(partner[0], 0, 2 * slab), (partner[1], 0, 2 * slab)], [(other[0], 0, full // 2)], bases),
-        project(flags, [(partner[2], 0, full // 2)], [(other[1], 0, full // 2)], bases),
+
+    def by_part(block):
+        split = block.reshape(cands, parts, sub, -1)
+        return jnp.stack(
+            [lax.dynamic_index_in_dim(split, col ^ d, 1, keepdims=False) for d in (0, 2, 1, 3)]
+        )
+
+    act = [
+        by_part(lax.dynamic_index_in_dim(every_act, i, 0, keepdims=False))
+        for i in (row, row ^ 1, planes - 1 - row, planes - 1 - (row ^ 1))
     ]
+    act_rot = [jnp.stack(act[i : i + 2], axis=1) for i in (0, 2)]
+    act_rot = [jnp.moveaxis(x, 2, 0).reshape(cands, 2 * tok, -1) for x in act_rot]
+    act_rot = jnp.concatenate(act_rot, axis=1)
+
+    own_end = project(flags, [(flat, 0, full)], [], [near_basis, after(far_basis, partner[0], act_rot)])
+    outer = project(
+        flags,
+        [(partner[0], 0, 2 * slab), (partner[1], 0, 2 * slab)],
+        [(other[0], 0, full // 2)],
+        [grad_basis, near_basis, after(far_basis, own_end)],
+    )
 
     def swap(value, axis, d):
         size = planes if axis == "row" else parts
@@ -235,44 +250,39 @@
             total = total + swap(sent, "col", d).astype(F32)
         return total.astype(BF16).reshape(-1, 2 * dirs)
 
-    def gather(total, *earlier):
-        got = swap(total[:, dirs:], "row", 1)
-        mine = jnp.concatenate([after(total[:, :dirs], *earlier), got], axis=0)
+    def to_neighbour(total):
+        return jnp.concatenate([total[:, :dirs], swap(total[:, dirs:], "row", 1)], axis=0)
+
+    def gather(mine):
         pair = jnp.concatenate([mine, swap(mine, "col", 2)], axis=0)
         return [pair, swap(pair, "col", 1)]
 
-    sums = [scatter_sum(x) for x in products]
-    early, last = jnp.concatenate(sums[:2], axis=0), sums[2]
-    arrays = gather(early, partner[2]) + gather(last)
+    own = scatter_sum(jnp.concatenate([own_own, own_end], axis=1))
+    early = to_neighbour(jnp.concatenate([own, scatter_sum(outer)], axis=0))
+    product = project(
+        flags,
+        [(partner[2], 0, full // 2)],
+        [(other[1], 0, full // 2)],
+        [grad_basis, near_basis, after(far_basis, early)],
+    )
+    last = to_neighbour(scatter_sum(product))
+    arrays = gather(early) + gather(last)
     segments = [[] for _ in range(cands)]
     for kind in (0, 1):
         for c in range(cands):
             for j in (0, 1):
                 for side in (0, 1):
                     for plane in (0, 1):
-                        base = (side * 2 + plane) * early.shape[0]
+                        base = (side * 2 + plane) * early.shape[0] // 2
                         if kind == 0:
                             segments[c].append((j, base + c * sub, sub))
                         elif c < cands // 2:
                             segments[c].append((j, base + (cands + c) * sub, sub))
                         else:
-                            base = (side * 2 + plane) * last.shape[0]
+                            base = (side * 2 + plane) * last.shape[0] // 2
                             segments[c].append((2 + j, base + (c - cands // 2) * sub, sub))
     layout = tuple(tuple(s) for s in segments)
 
-    def by_part(block):
-        split = block.reshape(cands, parts, sub, -1)
-        split = jnp.where((col & 1) == 1, split[:, jnp.array([1, 0, 3, 2])], split)
-        split = jnp.where((col & 2) == 2, split[:, jnp.array([2, 3, 0, 1])], split)
-        return jnp.moveaxis(split[:, jnp.array([0, 2, 1, 3])], 1, 0)
-
-    act = [
-        by_part(lax.dynamic_index_in_dim(every_act, i, 0, keepdims=False))
-        for i in (row, row ^ 1, planes - 1 - row, planes - 1 - (row ^ 1))
-    ]
-    act_rot = [jnp.stack(act[i : i + 2], axis=1) for i in (0, 2)]
-    act_rot = [jnp.moveaxis(x, 2, 0).reshape(cands, 2 * tok, -1) for x in act_rot]
-    act_rot = jnp.concatenate(act_rot, axis=1)
     rotated, scores = rotate_and_score(arrays, layout, act_rot, eigenvalues, query_rotated)
     scores = exchange_sum(exchange_sum(scores, "col", parts), "row", planes)
     return rotated, scores

time: 507 us -> 491 us (0.968)
  local copies, waits for them, and re-layouts: 68.6 us -> 47.3 us
  waiting for transfers between devices: 260 us -> 276 us
  other arithmetic: 14.1 us -> 4.88 us
    ppermute x15, waiting for transfers between devices: 55.2 us -> 96 us  [swap(): return lax.ppermute(value, axis, [(i, i ^ d) for i in range(size)])]
    ppermute x3, waiting for transfers between devices: 42.1 us -> 8.51 us  [chain_body(): partner.append(lax.ppermute(after(piece, *tie), 'row', ends))]
    gather x12 -> x0, local copies, waits for them, and re-layouts: 13.3 us -> none  [the longest x4 4.59 us: by_part(): return jnp.moveaxis(split[:, jnp.array([0, 2, 1, 3])], 1, 0)]
    ppermute x5, waiting for transfers between devices: 21.9 us -> 32.9 us  [chain_body(): far.append(lax.ppermute(near[i], 'groups', [(0, 1), (1, 0)]))]
    unnamed x54 -> x26, local copies, waits for them, and re-layouts: 25.8 us -> 22.4 us
  transfers between devices with their start and end apart: 37 -> 37, of which waited for: 17 -> 22; matrix products, arithmetic and copies ran while one was open for 16% -> 11% of each run, Pallas kernels for 14% -> 14%
where the time goes in v10:
time: 491 us; the launch traced here: 490 us
  waiting for transfers between devices  276 us (56%)
  Pallas kernels  73.2 us (15%)
  starting transfers between devices  67 us (14%)
  local copies, waits for them, and re-layouts  47.3 us (10%)
  between operations  14.4 us (3%)
  matrix products  7.61 us (2%)
    ppermute x5, waiting for transfers between devices, chain_body(): near.append(lax.ppermute(piece, 'row', beside))  133 us
    ppermute x15, waiting for transfers between devices, swap(): return lax.ppermute(value, axis, [(i, i ^ d) for i in range(size)])  96 us
    pallas_call x4, Pallas kernels, project(): pl.pallas_call(functools.partial(project_kernel, len(ends), len(tokens),...  68.8 us
    ppermute x5, waiting for transfers between devices, chain_body(): far.append(lax.ppermute(near[i], 'groups', [(0, 1), (1, 0)]))  32.9 us
    ppermute x5, starting transfers between devices, chain_body(): near.append(lax.ppermute(piece, 'row', beside))  26.4 us
    unnamed x26, local copies, waits for them, and re-layouts  22.4 us
    ppermute x3, starting transfers between devices, chain_body(): partner.append(lax.ppermute(after(piece, *tie), 'row', ends))  13 us
  transfers between devices with their start and end apart: 37, of which 22 were waited for; matrix products, arithmetic and copies ran while one was open for 11% of the time, Pallas kernels for 14%

profile of v10, /device:TPU:0, one launch (start us, length us, event | category | flops | bytes accessed | tf_op | source)
XLA Modules:
  0.0 490.0 jit_solution(10706750379554535310)
XLA Ops:
  7.2 6.0 %fusion.18 = (bf16[2,128,8192]{2,1,0:T(8,128)(2,1)}, bf16[2,128,8192]{2,1,0:T(8,128)(2,1)}) fusion(bf16[4,128,8192]{2,1,0:T(8,128)(2,1)} %param.9), kind=kLoop, calls=%fused_computation.85 | loop fusion | bytes 16777216 | tf_op jit(solution)/shard_map/slice | solution.py:201
  13.2 2.6 collective-permute-start.3
  15.9 2.6 constant_dynamic-slice_fusion.4
  18.5 3.9 collective-permute-start
  22.4 5.4 %constant_dynamic-slice_fusion.7 = (bf16[2048,512]{1,0:T(8,128)(2,1)}, bf16[2048,512]{1,0:T(8,128)(2,1)S(1)}, bf16[2048,512]{1,0:T(8,128)(2,1)}) fusion(bf16[8192,1024]{1,0:T(8,128)(2,1)} %refs_3_.1, s32[]{:T(128)S(6)} %select_n.63), kind=kLoop, calls=%fused_computation.83 | loop fusion | bytes 12582916 | tf_op jit(solution)/shard_map/dynamic_slice | solution.py:196
  28.1 7.6 %fusion.5 = bf16[4,128,256]{2,1,0:T(8,128)(2,1)} fusion(bf16[4,128,8192]{2,1,0:T(8,128)(2,1)} %param.8, bf16[8192,256]{1,0:T(8,128)(2,1)} %param.10, f32[4,128]{1,0:T(4,128)S(1)} %compare_convert_fusion), kind=kOutput, calls=%fused_computation.7 | convolution fusion | flops 2147745792 | bytes 12847104 | tf_op jit(solution)/shard_map/ctd,dk->ctk/dot_general | solution.py:25
  35.7 11.0 %collective-permute-done = bf16[1024,512]{1,0:T(8,128)(2,1)} collective-permute-done((bf16[1024,512]{1,0:T(8,128)(2,1)}, bf16[1024,512]{1,0:T(8,128)(2,1)}, u32[]{:S(2)}, u32[]{:S(2)}) %collective-permute-start) | collective-permute-done | bytes 1048608 | tf_op jit(solution)/shard_map/ppermute | solution.py:203
  46.7 2.7 collective-permute-start.11
  50.0 15.9 %shard_map.95 = bf16[512,1024]{1,0:T(8,128)(2,1)} custom-call(s32[2]{0:T(128)} %pad_add_fusion.refs_0_, bf16[512,8192]{1,0:T(8,128)(2,1)} %bitcast.107, bf16[8192,1024]{1,0:T(8,128)(2,1)} %refs_3_.1), custom_call_target="tpu_custom_call" | custom-call | flops 536870912 | bytes 1572864 | tf_op jit(solution)/shard_map/pallas_call | solution.py:148
  65.9 1.7 collective-permute-start.2
  67.7 1.6 collective-permute-start.6
  69.2 39.3 %collective-permute-done.1 = bf16[2048,512]{1,0:T(8,128)(2,1)} collective-permute-done((bf16[2048,512]{1,0:T(8,128)(2,1)}, bf16[2048,512]{1,0:T(8,128)(2,1)}, u32[]{:S(2)}, u32[]{:S(2)}) %collective-permute-start.1) | collective-permute-done | bytes 2097184 | tf_op jit(solution)/shard_map/ppermute | solution.py:203
  108.5 1.5 collective-permute-start.7
  110.1 18.7 %collective-permute-start.4 = (bf16[2048,512]{1,0:T(8,128)(2,1)S(1)}, bf16[2048,512]{1,0:T(8,128)(2,1)}, u32[]{:S(2)}, u32[]{:S(2)}) collective-permute-start(bf16[2048,512]{1,0:T(8,128)(2,1)S(1)} %get-tuple-element.15), channel_id=1, source_target_pairs={{0,4},{4,0},{8,12},{12,8},{1,5},{5,1},{9,13},{13,9},{2,6},{6,2},{1... | collective-permute-start | bytes 6291464 | tf_op jit(solution)/shard_map/ppermute | solution.py:203
  128.8 24.7 %collective-permute-done.2 = bf16[2048,512]{1,0:T(8,128)(2,1)} collective-permute-done((bf16[2048,512]{1,0:T(8,128)(2,1)}, bf16[2048,512]{1,0:T(8,128)(2,1)}, u32[]{:S(2)}, u32[]{:S(2)}) %collective-permute-start.2) | collective-permute-done | bytes 2097184 | tf_op jit(solution)/shard_map/ppermute | solution.py:203
  153.5 2.1 collective-permute-start.5
  155.5 1.5 collective-permute-start.8
  157.1 4.7 slice_bitcast_fusion
  161.8 57.9 %collective-permute-done.5 = bf16[1024,512]{1,0:T(8,128)(2,1)S(1)} collective-permute-done((bf16[1024,512]{1,0:T(8,128)(2,1)S(1)}, bf16[1024,512]{1,0:T(8,128)(2,1)S(1)}, u32[]{:S(2)}, u32[]{:S(2)}) %collective-permute-start.5) | collective-permute-done | bytes 1048608 | tf_op jit(solution)/shard_map/ppermute | solution.py:203
  220.6 5.2 %collective-permute-start.12 = (bf16[128,8192]{1,0:T(8,128)(2,1)}, bf16[128,8192]{1,0:T(8,128)(2,1)}, u32[]{:S(2)}, u32[]{:S(2)}) collective-permute-start(bf16[128,8192]{1,0:T(8,128)(2,1)} %get-tuple-element.18), channel_id=1, source_target_pairs={{0,12},{12,0},{1,13},{13,1},{2,14},{14,2},{3,15},{15,3},{16,28},{2... | collective-permute-start | bytes 6291464 | tf_op jit(solution)/shard_map/ppermute | solution.py:215
  225.9 2.2 constant_dynamic-update-slice_fusion.4
  228.1 1.3 constant_dynamic-slice_fusion.3
  229.4 1.6 collective-permute-start.10
  232.0 23.5 %collective-permute-done.10 = bf16[1024,512]{1,0:T(8,128)(2,1)S(1)} collective-permute-done((bf16[1024,512]{1,0:T(8,128)(2,1)S(1)}, bf16[1024,512]{1,0:T(8,128)(2,1)S(1)}, u32[]{:S(2)}, u32[]{:S(2)}) %collective-permute-start.10) | collective-permute-done | bytes 1048608 | tf_op jit(solution)/shard_map/ppermute | solution.py:204
  255.6 2.5 collective-permute-start.16
  258.1 2.3 constant_dynamic-update-slice_fusion.9
  260.4 3.2 constant_dynamic-update-slice_fusion.3
  263.6 3.1 constant_dynamic-update-slice_fusion.2
  266.7 6.6 %collective-permute-done.12.refs_1_ = bf16[128,8192]{1,0:T(8,128)(2,1)} collective-permute-done((bf16[128,8192]{1,0:T(8,128)(2,1)}, bf16[128,8192]{1,0:T(8,128)(2,1)}, u32[]{:S(2)}, u32[]{:S(2)}) %collective-permute-start.12) | collective-permute-done | bytes 2097184 | tf_op jit(solution)/shard_map/ppermute | solution.py:215
  273.3 5.3 %collective-permute-start.23 = (bf16[256,8192]{1,0:T(8,128)(2,1)S(1)}, bf16[256,8192]{1,0:T(8,128)(2,1)}, u32[]{:S(2)}, u32[]{:S(2)}) collective-permute-start(bf16[256,8192]{1,0:T(8,128)(2,1)S(1)} %bitcast.116), channel_id=1, source_target_pairs={{0,12},{12,0},{1,13},{13,1},{2,14},{14,2},{3,15},{15,3},{16,28},{2... | collective-permute-start | bytes 12582920 | tf_op jit(solution)/shard_map/ppermute | solution.py:215
  278.6 3.0 constant_dynamic-update-slice_fusion.8
  281.6 3.1 constant_dynamic-update-slice_fusion.7
  284.7 3.0 constant_dynamic-update-slice_fusion.1
  288.8 9.4 %collective-permute-done.9 = bf16[2048,512]{1,0:T(8,128)(2,1)S(1)} collective-permute-done((bf16[2048,512]{1,0:T(8,128)(2,1)}, bf16[2048,512]{1,0:T(8,128)(2,1)S(1)}, u32[]{:S(2)}, u32[]{:S(2)}) %collective-permute-start.9) | collective-permute-done | bytes 2097184 | tf_op jit(solution)/shard_map/ppermute | solution.py:204
  298.2 1.5 constant_dynamic-update-slice_fusion.6
  299.6 1.1 constant_dynamic-update-slice_fusion.5.refs_3_.refs_6_.refs_5_
  300.7 15.6 %shard_map.96 = bf16[512,1024]{1,0:T(8,128)(2,1)} custom-call(s32[2]{0:T(128)} %pad_add_fusion.refs_0_, bf16[512,8192]{1,0:T(8,128)(2,1)} %bitcast.108, bf16[8192,512]{1,0:T(8,128)(2,1)} %constant_dynamic-update-slice_fusion.refs_2_.refs_5_.refs_4_, bf16[8192,512]{1,0:T(8,128)(2,1)} %constant_dynamic-update-slice_fusion.5.refs_3_.refs_6_.refs_5_), custom_call_target="tpu_custom_call" | custom-call | flops 536870912 | bytes 1572864 | tf_op jit(solution)/shard_map/pallas_call | solution.py:148
  316.4 1.9 collective-permute-done.16.refs_2_
  318.2 18.7 %shard_map.97 = bf16[256,2048]{1,0:T(8,128)(2,1)} custom-call(s32[2]{0:T(128)} %pad_add_fusion.refs_0_, bf16[128,8192]{1,0:T(8,128)(2,1)} %collective-permute-done.12.refs_1_, bf16[128,8192]{1,0:T(8,128)(2,1)} %collective-permute-done.16.refs_2_, bf16[256,8192]{1,0:T(8,128)(2,1)} %collective-permute-done.3.refs_3_, bf16[8192,1024]{1,0:T(8,128)(2,1)} %refs_3_.1, ...), custom_call_target="tpu_custom_call" | custom-call | flops 536870912 | bytes 2359296 | tf_op jit(solution)/shard_map/pallas_call | solution.py:148
  337.0 1.2 dynamic-slice_bitcast_fusion.8
  338.2 1.6 collective-permute-start.18
  340.4 1.2 collective-permute-start.15
  341.6 5.2 %collective-permute-done.19 = bf16[2,32,2048]{2,1,0:T(8,128)(2,1)S(1)} collective-permute-done((bf16[2,32,2048]{2,1,0:T(8,128)(2,1)S(1)}, bf16[2,32,2048]{2,1,0:T(8,128)(2,1)S(1)}, u32[]{:S(2)}, u32[]{:S(2)}) %collective-permute-start.19) | collective-permute-done | bytes 262176 | tf_op jit(solution)/shard_map/ppermute | solution.py:243
  346.8 1.5 collective-permute-start.14
  348.3 4.2 collective-permute-done.18
  352.6 1.1 fusion.16
  353.7 9.9 %collective-permute-done.15 = bf16[4,32,2048]{2,1,0:T(8,128)(2,1)S(1)} collective-permute-done((bf16[4,32,2048]{2,1,0:T(8,128)(2,1)S(1)}, bf16[4,32,2048]{2,1,0:T(8,128)(2,1)S(1)}, u32[]{:S(2)}, u32[]{:S(2)}) %collective-permute-start.15) | collective-permute-done | bytes 524320 | tf_op jit(solution)/shard_map/ppermute | solution.py:243
  363.6 11.3 %collective-permute-done.14 = bf16[4,32,2048]{2,1,0:T(8,128)(2,1)S(1)} collective-permute-done((bf16[4,32,2048]{2,1,0:T(8,128)(2,1)S(1)}, bf16[4,32,2048]{2,1,0:T(8,128)(2,1)S(1)}, u32[]{:S(2)}, u32[]{:S(2)}) %collective-permute-start.14) | collective-permute-done | bytes 524320 | tf_op jit(solution)/shard_map/ppermute | solution.py:243
  375.4 39.0 %collective-permute-done.20 = bf16[192,1024]{1,0:T(8,128)(2,1)S(1)} collective-permute-done((bf16[192,1024]{1,0:T(8,128)(2,1)S(1)}, bf16[192,1024]{1,0:T(8,128)(2,1)S(1)}, u32[]{:S(2)}, u32[]{:S(2)}) %collective-permute-start.20) | collective-permute-done | bytes 393248 | tf_op jit(solution)/shard_map/ppermute | solution.py:243
  414.4 1.5 collective-permute-start.21
  416.0 18.5 %shard_map.98 = bf16[256,2048]{1,0:T(8,128)(2,1)} custom-call(s32[2]{0:T(128)} %pad_add_fusion.refs_0_, bf16[256,8192]{1,0:T(8,128)(2,1)} %collective-permute-done.23.refs_1_, bf16[256,8192]{1,0:T(8,128)(2,1)} %collective-permute-done.11.refs_2_, bf16[8192,1024]{1,0:T(8,128)(2,1)} %refs_3_.1, ...), custom_call_target="tpu_custom_call" | custom-call | flops 536870912 | bytes 2359296 | tf_op jit(solution)/shard_map/pallas_call | solution.py:148
  434.5 1.3 dynamic-slice_bitcast_fusion.5
  435.9 1.5 collective-permute-start.25
  438.1 6.4 %collective-permute-done.26 = bf16[2,32,2048]{2,1,0:T(8,128)(2,1)S(1)} collective-permute-done((bf16[2,32,2048]{2,1,0:T(8,128)(2,1)S(1)}, bf16[2,32,2048]{2,1,0:T(8,128)(2,1)S(1)}, u32[]{:S(2)}, u32[]{:S(2)}) %collective-permute-start.26) | collective-permute-done | bytes 262176 | tf_op jit(solution)/shard_map/ppermute | solution.py:243
  444.5 5.6 %collective-permute-done.25 = bf16[2,32,2048]{2,1,0:T(8,128)(2,1)S(1)} collective-permute-done((bf16[2,32,2048]{2,1,0:T(8,128)(2,1)S(1)}, bf16[2,32,2048]{2,1,0:T(8,128)(2,1)S(1)}, u32[]{:S(2)}, u32[]{:S(2)}) %collective-permute-start.25) | collective-permute-done | bytes 262176 | tf_op jit(solution)/shard_map/ppermute | solution.py:243
  451.3 5.5 %collective-permute-done.27 = bf16[64,1024]{1,0:T(8,128)(2,1)S(1)} collective-permute-done((bf16[64,1024]{1,0:T(8,128)(2,1)S(1)}, bf16[64,1024]{1,0:T(8,128)(2,1)S(1)}, u32[]{:S(2)}, u32[]{:S(2)}) %collective-permute-start.27) | collective-permute-done | bytes 131104 | tf_op jit(solution)/shard_map/ppermute | solution.py:243
  457.4 7.0 %collective-permute-done.28 = bf16[128,1024]{1,0:T(8,128)(2,1)S(1)} collective-permute-done((bf16[128,1024]{1,0:T(8,128)(2,1)S(1)}, bf16[128,1024]{1,0:T(8,128)(2,1)S(1)}, u32[]{:S(2)}, u32[]{:S(2)}) %collective-permute-start.28) | collective-permute-done | bytes 262176 | tf_op jit(solution)/shard_map/ppermute | solution.py:243
  464.5 1.9 collective-permute-done.29.refs_3_
  466.4 4.4 shard_map.99
  471.2 1.5 collective-permute-start.31
  472.8 1.1 collective-permute-done.32
  474.8 3.3 collective-permute-start.35
  478.1 1.2 collective-permute-start.33
  480.3 2.3 collective-permute-done.34
  (80 shorter events, 10.9 us)
Async XLA Ops:
  7.2 102.9 %all-gather.3.cloned.1.call-start = ((), (), s32[]{:S(2)}) async-start(), calls=%async_computation | async-start | bytes 1310720 | tf_op jit(solution)/shard_map/all_gather | solution.py:191
  13.2 96.8 %collective-permute-start.3 = (bf16[256,8192]{1,0:T(8,128)(2,1)}, bf16[256,8192]{1,0:T(8,128)(2,1)}, u32[]{:S(2)}, u32[]{:S(2)}) collective-permute-start(bf16[256,8192]{1,0:T(8,128)(2,1)} %bitcast.4), channel_id=1, source_target_pairs={{4,8},{8,4},{5,9},{9,5},{6,10},{10,6},{7,11},{11,7},{20,24},{24,20... | collective-permute-start | bytes 12582920 | tf_op jit(solution)/shard_map/ppermute | solution.py:202
  18.5 9.3 %copy-start.7 = (s32[2048]{0:T(1024)S(1)}, s32[2048]{0:T(1024)}, u32[]{:S(2)}) copy-start(s32[2048]{0:T(1024)} %param.15) | copy-start | bytes 24580
  18.5 9.3 %copy-start.8 = (s32[4]{0:T(128)S(1)}, s32[4]{0:T(128)}, u32[]{:S(2)}) copy-start(s32[4]{0:T(128)} %param.14) | copy-start | bytes 52
  18.5 28.2 %collective-permute-start = (bf16[1024,512]{1,0:T(8,128)(2,1)}, bf16[1024,512]{1,0:T(8,128)(2,1)}, u32[]{:S(2)}, u32[]{:S(2)}) collective-permute-start(bf16[1024,512]{1,0:T(8,128)(2,1)} %get-tuple-element.26), channel_id=1, source_target_pairs={{0,4},{4,0},{8,12},{12,8},{1,5},{5,1},{9,13},{13,9},{2,6},{6,2},{1... | collective-permute-start | bytes 3145736 | tf_op jit(solution)/shard_map/ppermute | solution.py:203
  27.8 80.8 %collective-permute-start.1 = (bf16[2048,512]{1,0:T(8,128)(2,1)}, bf16[2048,512]{1,0:T(8,128)(2,1)}, u32[]{:S(2)}, u32[]{:S(2)}) collective-permute-start(bf16[2048,512]{1,0:T(8,128)(2,1)} %get-tuple-element.30), channel_id=1, source_target_pairs={{0,4},{4,0},{8,12},{12,8},{1,5},{5,1},{9,13},{13,9},{2,6},{6,2},{1... | collective-permute-start | bytes 6291464 | tf_op jit(solution)/shard_map/ppermute | solution.py:203
  46.7 172.9 %collective-permute-start.11 = (bf16[256,8192]{1,0:T(8,128)(2,1)}, bf16[256,8192]{1,0:T(8,128)(2,1)}, u32[]{:S(2)}, u32[]{:S(2)}) collective-permute-start(bf16[256,8192]{1,0:T(8,128)(2,1)} %bitcast.115), channel_id=1, source_target_pairs={{4,8},{8,4},{5,9},{9,5},{6,10},{10,6},{7,11},{11,7},{20,24},{24,20... | collective-permute-start | bytes 12582920 | tf_op jit(solution)/shard_map/ppermute | solution.py:202
  65.9 87.5 %collective-permute-start.2 = (bf16[2048,512]{1,0:T(8,128)(2,1)}, bf16[2048,512]{1,0:T(8,128)(2,1)}, u32[]{:S(2)}, u32[]{:S(2)}) collective-permute-start(bf16[2048,512]{1,0:T(8,128)(2,1)} %get-tuple-element.14), channel_id=1, source_target_pairs={{0,4},{4,0},{8,12},{12,8},{1,5},{5,1},{9,13},{13,9},{2,6},{6,2},{1... | collective-permute-start | bytes 6291464 | tf_op jit(solution)/shard_map/ppermute | solution.py:203
  67.7 87.9 %collective-permute-start.6 = (bf16[1024,512]{1,0:T(8,128)(2,1)}, bf16[1024,512]{1,0:T(8,128)(2,1)}, u32[]{:S(2)}, u32[]{:S(2)}) collective-permute-start(bf16[1024,512]{1,0:T(8,128)(2,1)} %collective-permute-done), channel_id=1, source_target_pairs={{0,16},{16,0},{1,17},{17,1},{2,18},{18,2},{3,19},{19,3},{4,20},{20... | collective-permute-start | bytes 3145736 | tf_op jit(solution)/shard_map/ppermute | solution.py:204
  108.5 111.1 %collective-permute-start.7 = (bf16[2048,512]{1,0:T(8,128)(2,1)}, bf16[2048,512]{1,0:T(8,128)(2,1)}, u32[]{:S(2)}, u32[]{:S(2)}) collective-permute-start(bf16[2048,512]{1,0:T(8,128)(2,1)} %collective-permute-done.1), channel_id=1, source_target_pairs={{0,16},{16,0},{1,17},{17,1},{2,18},{18,2},{3,19},{19,3},{4,20},{20... | collective-permute-start | bytes 6291464 | tf_op jit(solution)/shard_map/ppermute | solution.py:204
  110.1 109.6 %collective-permute-start.4 = (bf16[2048,512]{1,0:T(8,128)(2,1)S(1)}, bf16[2048,512]{1,0:T(8,128)(2,1)}, u32[]{:S(2)}, u32[]{:S(2)}) collective-permute-start(bf16[2048,512]{1,0:T(8,128)(2,1)S(1)} %get-tuple-element.15), channel_id=1, source_target_pairs={{0,4},{4,0},{8,12},{12,8},{1,5},{5,1},{9,13},{13,9},{2,6},{6,2},{1... | collective-permute-start | bytes 6291464 | tf_op jit(solution)/shard_map/ppermute | solution.py:203
  153.5 66.2 %collective-permute-start.5 = (bf16[1024,512]{1,0:T(8,128)(2,1)S(1)}, bf16[1024,512]{1,0:T(8,128)(2,1)S(1)}, u32[]{:S(2)}, u32[]{:S(2)}) collective-permute-start(bf16[1024,512]{1,0:T(8,128)(2,1)S(1)} %get-tuple-element.16), channel_id=1, source_target_pairs={{0,4},{4,0},{8,12},{12,8},{1,5},{5,1},{9,13},{13,9},{2,6},{6,2},{1... | collective-permute-start | bytes 3145736 | tf_op jit(solution)/shard_map/ppermute | solution.py:203
  155.5 76.5 %collective-permute-start.8 = (bf16[2048,512]{1,0:T(8,128)(2,1)}, bf16[2048,512]{1,0:T(8,128)(2,1)}, u32[]{:S(2)}, u32[]{:S(2)}) collective-permute-start(bf16[2048,512]{1,0:T(8,128)(2,1)} %collective-permute-done.2), channel_id=1, source_target_pairs={{0,16},{16,0},{1,17},{17,1},{2,18},{18,2},{3,19},{19,3},{4,20},{20... | collective-permute-start | bytes 6291464 | tf_op jit(solution)/shard_map/ppermute | solution.py:204
  219.6 1.0 copy-start.5
  220.6 8.8 %copy-start.6 = (bf16[1024,512]{1,0:T(8,128)(2,1)S(1)}, bf16[1024,512]{1,0:T(8,128)(2,1)}, u32[]{:S(2)}) copy-start(bf16[1024,512]{1,0:T(8,128)(2,1)} %copy-done.5) | copy-start | bytes 3145732
  220.6 52.7 %collective-permute-start.12 = (bf16[128,8192]{1,0:T(8,128)(2,1)}, bf16[128,8192]{1,0:T(8,128)(2,1)}, u32[]{:S(2)}, u32[]{:S(2)}) collective-permute-start(bf16[128,8192]{1,0:T(8,128)(2,1)} %get-tuple-element.18), channel_id=1, source_target_pairs={{0,12},{12,0},{1,13},{13,1},{2,14},{14,2},{3,15},{15,3},{16,28},{2... | collective-permute-start | bytes 6291464 | tf_op jit(solution)/shard_map/ppermute | solution.py:215
  229.4 26.2 %collective-permute-start.10 = (bf16[1024,512]{1,0:T(8,128)(2,1)S(1)}, bf16[1024,512]{1,0:T(8,128)(2,1)S(1)}, u32[]{:S(2)}, u32[]{:S(2)}) collective-permute-start(bf16[1024,512]{1,0:T(8,128)(2,1)S(1)} %copy-done.6), channel_id=1, source_target_pairs={{0,16},{16,0},{1,17},{17,1},{2,18},{18,2},{3,19},{19,3},{4,20},{20... | collective-permute-start | bytes 3145736 | tf_op jit(solution)/shard_map/ppermute | solution.py:204
  231.2 66.9 %collective-permute-start.9 = (bf16[2048,512]{1,0:T(8,128)(2,1)}, bf16[2048,512]{1,0:T(8,128)(2,1)S(1)}, u32[]{:S(2)}, u32[]{:S(2)}) collective-permute-start(bf16[2048,512]{1,0:T(8,128)(2,1)} %collective-permute-done.4), channel_id=1, source_target_pairs={{0,16},{16,0},{1,17},{17,1},{2,18},{18,2},{3,19},{19,3},{4,20},{20... | collective-permute-start | bytes 6291464 | tf_op jit(solution)/shard_map/ppermute | solution.py:204
  255.6 62.7 %collective-permute-start.16 = (bf16[128,8192]{1,0:T(8,128)(2,1)}, bf16[128,8192]{1,0:T(8,128)(2,1)}, u32[]{:S(2)}, u32[]{:S(2)}) collective-permute-start(bf16[128,8192]{1,0:T(8,128)(2,1)} %get-tuple-element.20), channel_id=1, source_target_pairs={{0,12},{12,0},{1,13},{13,1},{2,14},{14,2},{3,15},{15,3},{16,28},{2... | collective-permute-start | bytes 6291464 | tf_op jit(solution)/shard_map/ppermute | solution.py:215
  260.4 12.9 %copy-start.4 = (bf16[2,128,8192]{2,1,0:T(8,128)(2,1)S(1)}, bf16[2,128,8192]{2,1,0:T(8,128)(2,1)}, u32[]{:S(2)}) copy-start(bf16[2,128,8192]{2,1,0:T(8,128)(2,1)} %get-tuple-element.33) | copy-start | bytes 12582916
  273.3 142.7 %collective-permute-start.23 = (bf16[256,8192]{1,0:T(8,128)(2,1)S(1)}, bf16[256,8192]{1,0:T(8,128)(2,1)}, u32[]{:S(2)}, u32[]{:S(2)}) collective-permute-start(bf16[256,8192]{1,0:T(8,128)(2,1)S(1)} %bitcast.116), channel_id=1, source_target_pairs={{0,12},{12,0},{1,13},{13,1},{2,14},{14,2},{3,15},{15,3},{16,28},{2... | collective-permute-start | bytes 12582920 | tf_op jit(solution)/shard_map/ppermute | solution.py:215
  316.3 23.7 %copy-start.2 = (bf16[512,1024]{1,0:T(8,128)(2,1)S(1)}, bf16[512,1024]{1,0:T(8,128)(2,1)}, u32[]{:S(2)}) copy-start(bf16[512,1024]{1,0:T(8,128)(2,1)} %shard_map.95) | copy-start | bytes 3145732
  316.4 23.7 %copy-start.3 = (bf16[512,1024]{1,0:T(8,128)(2,1)S(1)}, bf16[512,1024]{1,0:T(8,128)(2,1)}, u32[]{:S(2)}) copy-start(bf16[512,1024]{1,0:T(8,128)(2,1)} %shard_map.96) | copy-start | bytes 3145732
  338.2 8.6 %collective-permute-start.19 = (bf16[2,32,2048]{2,1,0:T(8,128)(2,1)S(1)}, bf16[2,32,2048]{2,1,0:T(8,128)(2,1)S(1)}, u32[]{:S(2)}, u32[]{:S(2)}) collective-permute-start(bf16[2,32,2048]{2,1,0:T(8,128)(2,1)S(1)} %get-tuple-element.42), channel_id=1, source_target_pairs={{0,3},{1,2},{2,1},{3,0},{4,7},{5,6},{6,5},{7,4},{8,11},{9,10},{10,... | collective-permute-start | bytes 786440 | tf_op jit(solution)/shard_map/ppermute | solution.py:243
  338.2 14.3 %collective-permute-start.18 = (bf16[2,32,2048]{2,1,0:T(8,128)(2,1)S(1)}, bf16[2,32,2048]{2,1,0:T(8,128)(2,1)S(1)}, u32[]{:S(2)}, u32[]{:S(2)}) collective-permute-start(bf16[2,32,2048]{2,1,0:T(8,128)(2,1)S(1)} %get-tuple-element.43), channel_id=1, source_target_pairs={{0,2},{1,3},{2,0},{3,1},{4,6},{5,7},{6,4},{7,5},{8,10},{9,11},{10,... | collective-permute-start | bytes 786440 | tf_op jit(solution)/shard_map/ppermute | solution.py:243
  339.8 12.8 %collective-permute-start.17 = (bf16[2,32,2048]{2,1,0:T(8,128)(2,1)S(1)}, bf16[2,32,2048]{2,1,0:T(8,128)(2,1)S(1)}, u32[]{:S(2)}, u32[]{:S(2)}) collective-permute-start(bf16[2,32,2048]{2,1,0:T(8,128)(2,1)S(1)} %get-tuple-element.41), channel_id=1, source_target_pairs={{0,1},{1,0},{2,3},{3,2},{4,5},{5,4},{6,7},{7,6},{8,9},{9,8},{10,11... | collective-permute-start | bytes 786440 | tf_op jit(solution)/shard_map/ppermute | solution.py:243
  340.4 23.2 %collective-permute-start.15 = (bf16[4,32,2048]{2,1,0:T(8,128)(2,1)S(1)}, bf16[4,32,2048]{2,1,0:T(8,128)(2,1)S(1)}, u32[]{:S(2)}, u32[]{:S(2)}) collective-permute-start(bf16[4,32,2048]{2,1,0:T(8,128)(2,1)S(1)} %get-tuple-element.36), channel_id=1, source_target_pairs={{0,3},{1,2},{2,1},{3,0},{4,7},{5,6},{6,5},{7,4},{8,11},{9,10},{10,... | collective-permute-start | bytes 1572872 | tf_op jit(solution)/shard_map/ppermute | solution.py:243
  346.8 28.1 %collective-permute-start.14 = (bf16[4,32,2048]{2,1,0:T(8,128)(2,1)S(1)}, bf16[4,32,2048]{2,1,0:T(8,128)(2,1)S(1)}, u32[]{:S(2)}, u32[]{:S(2)}) collective-permute-start(bf16[4,32,2048]{2,1,0:T(8,128)(2,1)S(1)} %get-tuple-element.37), channel_id=1, source_target_pairs={{0,2},{1,3},{2,0},{3,1},{4,6},{5,7},{6,4},{7,5},{8,10},{9,11},{10,... | collective-permute-start | bytes 1572872 | tf_op jit(solution)/shard_map/ppermute | solution.py:243
  352.5 22.4 %collective-permute-start.13 = (bf16[4,32,2048]{2,1,0:T(8,128)(2,1)S(1)}, bf16[4,32,2048]{2,1,0:T(8,128)(2,1)S(1)}, u32[]{:S(2)}, u32[]{:S(2)}) collective-permute-start(bf16[4,32,2048]{2,1,0:T(8,128)(2,1)S(1)} %get-tuple-element.35), channel_id=1, source_target_pairs={{0,1},{1,0},{2,3},{3,2},{4,5},{5,4},{6,7},{7,6},{8,9},{9,8},{10,11... | collective-permute-start | bytes 1572872 | tf_op jit(solution)/shard_map/ppermute | solution.py:243
  375.3 39.0 %collective-permute-start.20 = (bf16[192,1024]{1,0:T(8,128)(2,1)S(1)}, bf16[192,1024]{1,0:T(8,128)(2,1)S(1)}, u32[]{:S(2)}, u32[]{:S(2)}) collective-permute-start(bf16[192,1024]{1,0:T(8,128)(2,1)S(1)} %get-tuple-element.49), channel_id=1, source_target_pairs={{0,4},{4,0},{8,12},{12,8},{1,5},{5,1},{9,13},{13,9},{2,6},{6,2},{1... | collective-permute-start | bytes 1179656 | tf_op jit(solution)/shard_map/ppermute | solution.py:243
  414.4 23.3 %collective-permute-start.21 = (bf16[384,1024]{1,0:T(8,128)(2,1)S(1)}, bf16[384,1024]{1,0:T(8,128)(2,1)S(1)}, u32[]{:S(2)}, u32[]{:S(2)}) collective-permute-start(bf16[384,1024]{1,0:T(8,128)(2,1)S(1)} %pad_maximum_fusion.3), channel_id=1, source_target_pairs={{0,2},{1,3},{2,0},{3,1},{4,6},{5,7},{6,4},{7,5},{8,10},{9,11},{10,... | collective-permute-start | bytes 2359304 | tf_op jit(solution)/shard_map/ppermute | solution.py:243
  434.5 31.9 %copy-start = (bf16[4,1024,256]{2,1,0:T(8,128)(2,1)S(1)}, bf16[4,1024,256]{2,1,0:T(8,128)(2,1)}, u32[]{:S(2)}) copy-start(bf16[4,1024,256]{2,1,0:T(8,128)(2,1)} %refs_6_.1) | copy-start | bytes 6291460
  434.5 31.9 %copy-start.1 = (f32[1024,256]{1,0:T(8,128)S(1)}, f32[1024,256]{1,0:T(8,128)}, u32[]{:S(2)}) copy-start(f32[1024,256]{1,0:T(8,128)} %refs_5_.1) | copy-start | bytes 3145732
  435.8 8.7 %collective-permute-start.26 = (bf16[2,32,2048]{2,1,0:T(8,128)(2,1)S(1)}, bf16[2,32,2048]{2,1,0:T(8,128)(2,1)S(1)}, u32[]{:S(2)}, u32[]{:S(2)}) collective-permute-start(bf16[2,32,2048]{2,1,0:T(8,128)(2,1)S(1)} %get-tuple-element.39), channel_id=1, source_target_pairs={{0,3},{1,2},{2,1},{3,0},{4,7},{5,6},{6,5},{7,4},{8,11},{9,10},{10,... | collective-permute-start | bytes 786440 | tf_op jit(solution)/shard_map/ppermute | solution.py:243
  435.9 14.2 %collective-permute-start.25 = (bf16[2,32,2048]{2,1,0:T(8,128)(2,1)S(1)}, bf16[2,32,2048]{2,1,0:T(8,128)(2,1)S(1)}, u32[]{:S(2)}, u32[]{:S(2)}) collective-permute-start(bf16[2,32,2048]{2,1,0:T(8,128)(2,1)S(1)} %get-tuple-element.40), channel_id=1, source_target_pairs={{0,2},{1,3},{2,0},{3,1},{4,6},{5,7},{6,4},{7,5},{8,10},{9,11},{10,... | collective-permute-start | bytes 786440 | tf_op jit(solution)/shard_map/ppermute | solution.py:243
  437.4 12.8 %collective-permute-start.24 = (bf16[2,32,2048]{2,1,0:T(8,128)(2,1)S(1)}, bf16[2,32,2048]{2,1,0:T(8,128)(2,1)S(1)}, u32[]{:S(2)}, u32[]{:S(2)}) collective-permute-start(bf16[2,32,2048]{2,1,0:T(8,128)(2,1)S(1)} %get-tuple-element.38), channel_id=1, source_target_pairs={{0,1},{1,0},{2,3},{3,2},{4,5},{5,4},{6,7},{7,6},{8,9},{9,8},{10,11... | collective-permute-start | bytes 786440 | tf_op jit(solution)/shard_map/ppermute | solution.py:243
  437.9 26.6 %collective-permute-start.22 = (bf16[768,1024]{1,0:T(8,128)(2,1)S(1)}, bf16[768,1024]{1,0:T(8,128)(2,1)S(1)}, u32[]{:S(2)}, u32[]{:S(2)}) collective-permute-start(bf16[768,1024]{1,0:T(8,128)(2,1)S(1)} %pad_maximum_fusion.1.refs_0_), channel_id=1, source_target_pairs={{0,1},{1,0},{2,3},{3,2},{4,5},{5,4},{6,7},{7,6},{8,9},{9,8},{10,11... | collective-permute-start | bytes 4718600 | tf_op jit(solution)/shard_map/ppermute | solution.py:243
  451.3 5.6 %collective-permute-start.27 = (bf16[64,1024]{1,0:T(8,128)(2,1)S(1)}, bf16[64,1024]{1,0:T(8,128)(2,1)S(1)}, u32[]{:S(2)}, u32[]{:S(2)}) collective-permute-start(bf16[64,1024]{1,0:T(8,128)(2,1)S(1)} %get-tuple-element.51), channel_id=1, source_target_pairs={{0,4},{4,0},{8,12},{12,8},{1,5},{5,1},{9,13},{13,9},{2,6},{6,2},{1... | collective-permute-start | bytes 393224 | tf_op jit(solution)/shard_map/ppermute | solution.py:243
  456.8 7.5 %collective-permute-start.28 = (bf16[128,1024]{1,0:T(8,128)(2,1)S(1)}, bf16[128,1024]{1,0:T(8,128)(2,1)S(1)}, u32[]{:S(2)}, u32[]{:S(2)}) collective-permute-start(bf16[128,1024]{1,0:T(8,128)(2,1)S(1)} %pad_maximum_fusion.8), channel_id=1, source_target_pairs={{0,2},{1,3},{2,0},{3,1},{4,6},{5,7},{6,4},{7,5},{8,10},{9,11},{10,... | collective-permute-start | bytes 786440 | tf_op jit(solution)/shard_map/ppermute | solution.py:243
  464.4 2.0 collective-permute-start.29
  471.0 3.0 collective-permute-start.32
  471.2 3.6 collective-permute-start.31
  472.8 2.1 collective-permute-start.30
  474.8 5.4 %collective-permute-start.35 = (f32[4,4]{1,0:T(4,128)S(1)}, f32[4,4]{1,0:T(4,128)S(1)}, u32[]{:S(2)}, u32[]{:S(2)}) collective-permute-start(f32[4,4]{1,0:T(4,128)S(1)} %add_add_fusion.1), channel_id=1, source_target_pairs={{0,12},{4,8},{8,4},{12,0},{1,13},{5,9},{9,5},{13,1},{2,14},{6,10},... | collective-permute-start | bytes 200 | tf_op jit(solution)/shard_map/ppermute | solution.py:173
  478.1 4.5 collective-permute-start.34
  478.1 4.5 collective-permute-start.33
Sparse Core Ops, SparseCore 0:
  67.8 42.1 all-gather.2

commit v11 on v10

--- a/solution.py
+++ b/solution.py
@@ -188,14 +188,13 @@
     units, deep, slab = 8, feats // 8, cands * tok // 8
     lengths = candidate_lengths(example_ids, token_counts)
     local_act = local_activations(acts, act_basis, lengths)
-    every_act = lax.all_gather(local_act, "row", axis=0)
     near, far, other = [], [], []
-    spans = [(0, 1), (1, 3), (3, 5), (5, 7), (7, units)]
+    spans = [(0, 2), (2, 4), (4, 6), (6, 7), (7, units)]
     own_own = project(flags, [(flat, 0, cands * tok)], [], [grad_basis])
     for i, (a, b) in enumerate(spans):
         piece = lax.dynamic_slice(grad_basis, (a * deep, group * half), ((b - a) * deep, half))
         if i >= 2:
-            early = {2: [own_own, local_act], 3: [other[0], every_act], 4: [every_act]}[i]
+            early = {2: [own_own, local_act], 3: [other[0]], 4: []}[i]
             piece = after(piece, near[i - 2], *early)
         if i in (0, 2):
             part = flat[: 4 * slab] if i == 0 else after(flat[4 * slab :], near[0])
@@ -205,9 +204,9 @@
     near_basis = jnp.concatenate(near, axis=0)
     far_basis = jnp.concatenate(far, axis=0)
 
-    ranges = [(0, 2), (2, 4), (4, units)]
+    ranges = [(0, 2), (2, 4), (4, 6), (6, units)]
     phase = [near[3], near[4], other[1]]
-    ties = [[*phase, far[0], far[1]], [*phase, far[2], far[4]], []]
+    ties = [[*phase, far[0], far[1]], [*phase, far[2], far[4]], [], []]
     partner = []
     for k, (a, b) in enumerate(ranges):
         tie = ties[k] + ([partner[k - 2]] if k >= 2 else [])
@@ -222,6 +221,7 @@
             [lax.dynamic_index_in_dim(split, col ^ d, 1, keepdims=False) for d in (0, 2, 1, 3)]
         )
 
+    every_act = lax.all_gather(after(local_act, partner[2]), "row", axis=0)
     act = [
         by_part(lax.dynamic_index_in_dim(every_act, i, 0, keepdims=False))
         for i in (row, row ^ 1, planes - 1 - row, planes - 1 - (row ^ 1))
@@ -230,7 +230,7 @@
     act_rot = [jnp.moveaxis(x, 2, 0).reshape(cands, 2 * tok, -1) for x in act_rot]
     act_rot = jnp.concatenate(act_rot, axis=1)
 
-    own_end = project(flags, [(flat, 0, full)], [], [near_basis, after(far_basis, partner[0], act_rot)])
+    own_end = project(flags, [(flat, 0, full)], [], [near_basis, after(far_basis, partner[0])])
     outer = project(
         flags,
         [(partner[0], 0, 2 * slab), (partner[1], 0, 2 * slab)],
@@ -250,22 +250,25 @@
             total = total + swap(sent, "col", d).astype(F32)
         return total.astype(BF16).reshape(-1, 2 * dirs)
 
-    def to_neighbour(total):
-        return jnp.concatenate([total[:, :dirs], swap(total[:, dirs:], "row", 1)], axis=0)
-
     def gather(mine):
         pair = jnp.concatenate([mine, swap(mine, "col", 2)], axis=0)
         return [pair, swap(pair, "col", 1)]
 
-    own = scatter_sum(jnp.concatenate([own_own, own_end], axis=1))
-    early = to_neighbour(jnp.concatenate([own, scatter_sum(outer)], axis=0))
-    product = project(
-        flags,
-        [(partner[2], 0, full // 2)],
-        [(other[1], 0, full // 2)],
-        [grad_basis, near_basis, after(far_basis, early)],
-    )
-    last = to_neighbour(scatter_sum(product))
+    sums = [scatter_sum(jnp.concatenate([own_own, own_end], axis=1)), scatter_sum(outer)]
+    for k in (2, 3):
+        product = project(
+            flags,
+            [(partner[k], 0, tok)],
+            [(other[1], (k - 2) * tok, tok)],
+            [grad_basis, near_basis, after(far_basis, sums[-1])],
+        )
+        if k == 2:
+            sums.append(scatter_sum(product))
+            early = jnp.concatenate(sums, axis=0)
+            got = swap(early[:, dirs:], "row", 1)
+    early = jnp.concatenate([early[:, :dirs], after(got, product)], axis=0)
+    last = scatter_sum(after(product, early))
+    last = jnp.concatenate([last[:, :dirs], swap(last[:, dirs:], "row", 1)], axis=0)
     arrays = gather(early) + gather(last)
     segments = [[] for _ in range(cands)]
     for kind in (0, 1):
@@ -276,11 +279,11 @@
                         base = (side * 2 + plane) * early.shape[0] // 2
                         if kind == 0:
                             segments[c].append((j, base + c * sub, sub))
-                        elif c < cands // 2:
+                        elif c < cands - 1:
                             segments[c].append((j, base + (cands + c) * sub, sub))
                         else:
                             base = (side * 2 + plane) * last.shape[0] // 2
-                            segments[c].append((2 + j, base + (c - cands // 2) * sub, sub))
+                            segments[c].append((2 + j, base, sub))
     layout = tuple(tuple(s) for s in segments)
 
     rotated, scores = rotate_and_score(arrays, layout, act_rot, eigenvalues, query_rotated)

time: 491 us -> 493 us (level)
  Pallas kernels: 73.2 us -> 86.4 us
  starting transfers between devices: 67 us -> 56.6 us
  waiting for transfers between devices: 276 us -> 271 us
    ppermute x15 -> x18, waiting for transfers between devices: 96 us -> 44.9 us  [swap(): return lax.ppermute(value, axis, [(i, i ^ d) for i in range(size)])]
    ppermute x5, waiting for transfers between devices: 32.9 us -> 80.6 us  [chain_body(): far.append(lax.ppermute(near[i], 'groups', [(0, 1), (1, 0)]))]
    ppermute x5, starting transfers between devices: 26.4 us -> 8.37 us  [chain_body(): near.append(lax.ppermute(piece, 'row', beside))]
    ppermute x5, waiting for transfers between devices: 133 us -> 119 us  [chain_body(): near.append(lax.ppermute(piece, 'row', beside))]
    pallas_call x4 -> x5, Pallas kernels: 68.8 us -> 80.9 us  [project(): pl.pallas_call(functools.partial(project_kernel, len(ends), len(tokens),...]
    ppermute x3 -> x4, waiting for transfers between devices: 8.51 us -> 20.4 us  [chain_body(): partner.append(lax.ppermute(after(piece, *tie), 'row', ends))]
    ppermute x3 -> x4, starting transfers between devices: 13 us -> 18.1 us  [chain_body(): partner.append(lax.ppermute(after(piece, *tie), 'row', ends))]
    ppermute x15 -> x18, starting transfers between devices: 9.17 us -> 11.1 us  [swap(): return lax.ppermute(value, axis, [(i, i ^ d) for i in range(size)])]
  transfers between devices with their start and end apart: 37 -> 41, of which waited for: 22 -> 22; matrix products, arithmetic and copies ran while one was open for 11% -> 10% of each run, Pallas kernels for 14% -> 16%
where the time goes in v11:
time: 493 us; the launch traced here: 492 us
  waiting for transfers between devices  271 us (55%)
  Pallas kernels  86.4 us (18%)
  starting transfers between devices  56.6 us (11%)
  local copies, waits for them, and re-layouts  48.7 us (10%)
  between operations  14.4 us (3%)
  other arithmetic  8.31 us (2%)
  matrix products  6.46 us (1%)
    ppermute x5, waiting for transfers between devices, chain_body(): near.append(lax.ppermute(piece, 'row', beside))  119 us
    pallas_call x5, Pallas kernels, project(): pl.pallas_call(functools.partial(project_kernel, len(ends), len(tokens),...  80.9 us
    ppermute x5, waiting for transfers between devices, chain_body(): far.append(lax.ppermute(near[i], 'groups', [(0, 1), (1, 0)]))  80.6 us
    ppermute x18, waiting for transfers between devices, swap(): return lax.ppermute(value, axis, [(i, i ^ d) for i in range(size)])  44.9 us
    unnamed x44, local copies, waits for them, and re-layouts  23.3 us
    ppermute x4, waiting for transfers between devices, chain_body(): partner.append(lax.ppermute(after(piece, *tie), 'row', ends))  20.4 us
    ppermute x4, starting transfers between devices, chain_body(): partner.append(lax.ppermute(after(piece, *tie), 'row', ends))  18.1 us
    ppermute x18, starting transfers between devices, swap(): return lax.ppermute(value, axis, [(i, i ^ d) for i in range(size)])  11.1 us
  transfers between devices with their start and end apart: 41, of which 22 were waited for; matrix products, arithmetic and copies ran while one was open for 10% of the time, Pallas kernels for 16%

profile of v11, /device:TPU:0, one launch (start us, length us, event | category | flops | bytes accessed | tf_op | source)
XLA Modules:
  0.0 491.8 jit_solution(17220255554611341388)
XLA Ops:
  7.2 5.6 %constant_dynamic-slice_fusion.4 = (bf16[2048,512]{1,0:T(8,128)(2,1)}, bf16[2048,512]{1,0:T(8,128)(2,1)}, bf16[2048,512]{1,0:T(8,128)(2,1)S(1)}) fusion(bf16[8192,1024]{1,0:T(8,128)(2,1)} %refs_3_.3, s32[]{:T(128)S(6)} %select_n.68), kind=kLoop, calls=%fused_computation.83 | loop fusion | bytes 12582916 | tf_op jit(solution)/shard_map/dynamic_slice | solution.py:195
  12.8 3.0 collective-permute-start
  15.8 3.8 fusion.22
  19.6 2.7 collective-permute-start.3
  22.9 16.1 %shard_map.95 = bf16[512,1024]{1,0:T(8,128)(2,1)} custom-call(s32[2]{0:T(128)} %pad_add_fusion.refs_0_, bf16[512,8192]{1,0:T(8,128)(2,1)} %bitcast.122, bf16[8192,1024]{1,0:T(8,128)(2,1)} %refs_3_.3), custom_call_target="tpu_custom_call" | custom-call | flops 536870912 | bytes 1572864 | tf_op jit(solution)/shard_map/pallas_call | solution.py:148
  39.3 6.5 %fusion.5 = bf16[4,128,256]{2,1,0:T(8,128)(2,1)} fusion(bf16[4,128,8192]{2,1,0:T(8,128)(2,1)} %param.8, bf16[8192,256]{1,0:T(8,128)(2,1)S(1)} %copy-done.17, f32[4,128]{1,0:T(4,128)S(1)} %compare_convert_fusion), kind=kOutput, calls=%fused_computation.9 | convolution fusion | flops 2147745792 | bytes 12847104 | tf_op jit(solution)/shard_map/ctd,dk->ctk/dot_general | solution.py:25
  45.7 16.0 %collective-permute-done = bf16[2048,512]{1,0:T(8,128)(2,1)} collective-permute-done((bf16[2048,512]{1,0:T(8,128)(2,1)}, bf16[2048,512]{1,0:T(8,128)(2,1)}, u32[]{:S(2)}, u32[]{:S(2)}) %collective-permute-start) | collective-permute-done | bytes 2097184 | tf_op jit(solution)/shard_map/ppermute | solution.py:202
  61.8 1.7 collective-permute-start.2
  63.8 2.6 collective-permute-start.11
  66.4 1.7 collective-permute-start.6
  68.1 1.7 constant_dynamic-slice_fusion.5
  69.8 40.8 %collective-permute-done.2 = bf16[2048,512]{1,0:T(8,128)(2,1)} collective-permute-done((bf16[2048,512]{1,0:T(8,128)(2,1)}, bf16[2048,512]{1,0:T(8,128)(2,1)}, u32[]{:S(2)}, u32[]{:S(2)}) %collective-permute-start.2) | collective-permute-done | bytes 2097184 | tf_op jit(solution)/shard_map/ppermute | solution.py:202
  110.7 1.7 collective-permute-start.5
  112.4 43.1 %collective-permute-done.1 = bf16[2048,512]{1,0:T(8,128)(2,1)S(1)} collective-permute-done((bf16[2048,512]{1,0:T(8,128)(2,1)S(1)}, bf16[2048,512]{1,0:T(8,128)(2,1)S(1)}, u32[]{:S(2)}, u32[]{:S(2)}) %collective-permute-start.1) | collective-permute-done | bytes 2097184 | tf_op jit(solution)/shard_map/ppermute | solution.py:202
  155.5 1.7 collective-permute-start.7
  157.2 1.6 collective-permute-start.4
  159.3 18.7 %collective-permute-done.5 = bf16[1024,512]{1,0:T(8,128)(2,1)S(1)} collective-permute-done((bf16[1024,512]{1,0:T(8,128)(2,1)S(1)}, bf16[1024,512]{1,0:T(8,128)(2,1)S(1)}, u32[]{:S(2)}, u32[]{:S(2)}) %collective-permute-start.5) | collective-permute-done | bytes 1048608 | tf_op jit(solution)/shard_map/ppermute | solution.py:202
  178.0 1.7 collective-permute-start.10
  179.6 6.0 %slice_bitcast_fusion = (bf16[128,8192]{1,0:T(8,128)(2,1)}, bf16[128,8192]{1,0:T(8,128)(2,1)}, bf16[128,8192]{1,0:T(8,128)(2,1)}, bf16[128,8192]{1,0:T(8,128)(2,1)}) fusion(bf16[4,128,8192]{2,1,0:T(8,128)(2,1)} %param.9), kind=kLoop, calls=%fused_computation.3 | loop fusion | bytes 16777216 | tf_op jit(solution)/shard_map/slice | solution.py:213
  185.6 18.4 %collective-permute-done.7 = bf16[2048,512]{1,0:T(8,128)(2,1)S(1)} collective-permute-done((bf16[2048,512]{1,0:T(8,128)(2,1)S(1)}, bf16[2048,512]{1,0:T(8,128)(2,1)S(1)}, u32[]{:S(2)}, u32[]{:S(2)}) %collective-permute-start.7) | collective-permute-done | bytes 2097184 | tf_op jit(solution)/shard_map/ppermute | solution.py:203
  204.1 1.3 copy-done.9
  205.7 5.7 %collective-permute-start.12 = (bf16[128,8192]{1,0:T(8,128)(2,1)}, bf16[128,8192]{1,0:T(8,128)(2,1)S(1)}, u32[]{:S(2)}, u32[]{:S(2)}) collective-permute-start(bf16[128,8192]{1,0:T(8,128)(2,1)} %get-tuple-element.23), channel_id=1, source_target_pairs={{0,12},{12,0},{1,13},{13,1},{2,14},{14,2},{3,15},{15,3},{16,28},{2... | collective-permute-start | bytes 6291464 | tf_op jit(solution)/shard_map/ppermute | solution.py:214
  211.4 37.7 %collective-permute-done.8 = bf16[2048,512]{1,0:T(8,128)(2,1)} collective-permute-done((bf16[2048,512]{1,0:T(8,128)(2,1)}, bf16[2048,512]{1,0:T(8,128)(2,1)}, u32[]{:S(2)}, u32[]{:S(2)}) %collective-permute-start.8) | collective-permute-done | bytes 2097184 | tf_op jit(solution)/shard_map/ppermute | solution.py:203
  249.1 18.0 %collective-permute-done.10 = bf16[1024,512]{1,0:T(8,128)(2,1)} collective-permute-done((bf16[1024,512]{1,0:T(8,128)(2,1)S(1)}, bf16[1024,512]{1,0:T(8,128)(2,1)}, u32[]{:S(2)}, u32[]{:S(2)}) %collective-permute-start.10) | collective-permute-done | bytes 1048608 | tf_op jit(solution)/shard_map/ppermute | solution.py:203
  267.2 5.0 %collective-permute-start.16 = (bf16[128,8192]{1,0:T(8,128)(2,1)}, bf16[128,8192]{1,0:T(8,128)(2,1)S(1)}, u32[]{:S(2)}, u32[]{:S(2)}) collective-permute-start(bf16[128,8192]{1,0:T(8,128)(2,1)} %get-tuple-element.25), channel_id=1, source_target_pairs={{0,12},{12,0},{1,13},{13,1},{2,14},{14,2},{3,15},{15,3},{16,28},{2... | collective-permute-start | bytes 6291464 | tf_op jit(solution)/shard_map/ppermute | solution.py:214
  272.2 3.0 constant_dynamic-update-slice_fusion.4
  275.2 1.5 constant_dynamic-update-slice_fusion.3
  276.8 3.2 constant_dynamic-update-slice_fusion.9
  280.0 1.5 collective-permute-start.9
  281.5 3.0 constant_dynamic-update-slice_fusion.2
  284.6 1.5 constant_dynamic-update-slice_fusion.8
  286.0 2.1 collective-permute-start.20
  290.3 3.1 constant_dynamic-update-slice_fusion.7
  293.4 6.5 %collective-permute-done.9 = bf16[1024,512]{1,0:T(8,128)(2,1)S(1)} collective-permute-done((bf16[1024,512]{1,0:T(8,128)(2,1)S(1)}, bf16[1024,512]{1,0:T(8,128)(2,1)S(1)}, u32[]{:S(2)}, u32[]{:S(2)}) %collective-permute-start.9) | collective-permute-done | bytes 1048608 | tf_op jit(solution)/shard_map/ppermute | solution.py:203
  300.9 2.3 constant_dynamic-update-slice_fusion.5.refs_3_.refs_6_.refs_5_
  303.2 15.6 %shard_map.96 = bf16[512,1024]{1,0:T(8,128)(2,1)} custom-call(s32[2]{0:T(128)} %pad_add_fusion.refs_0_, bf16[512,8192]{1,0:T(8,128)(2,1)} %bitcast.123, bf16[8192,512]{1,0:T(8,128)(2,1)} %constant_dynamic-update-slice_fusion.refs_2_.refs_5_.refs_4_, bf16[8192,512]{1,0:T(8,128)(2,1)} %constant_dynamic-update-slice_fusion.5.refs_3_.refs_6_.refs_5_), custom_call_target="tpu_custom_call" | custom-call | flops 536870912 | bytes 1572864 | tf_op jit(solution)/shard_map/pallas_call | solution.py:148
  319.6 1.3 copy-done.6
  320.9 18.7 %shard_map.97 = bf16[256,2048]{1,0:T(8,128)(2,1)} custom-call(s32[2]{0:T(128)} %pad_add_fusion.refs_0_, bf16[128,8192]{1,0:T(8,128)(2,1)} %copy-done.5, bf16[128,8192]{1,0:T(8,128)(2,1)} %copy-done.6, bf16[256,8192]{1,0:T(8,128)(2,1)} %collective-permute-done.3.refs_3_, bf16[8192,1024]{1,0:T(8,128)(2,1)} %refs_3_.3, ...), custom_call_target="tpu_custom_call" | custom-call | flops 536870912 | bytes 2359296 | tf_op jit(solution)/shard_map/pallas_call | solution.py:148
  339.7 1.2 dynamic-slice_bitcast_fusion.5
  340.9 1.1 collective-permute-start.18
  343.9 5.6 %collective-permute-done.19 = bf16[2,32,2048]{2,1,0:T(8,128)(2,1)S(1)} collective-permute-done((bf16[2,32,2048]{2,1,0:T(8,128)(2,1)S(1)}, bf16[2,32,2048]{2,1,0:T(8,128)(2,1)S(1)}, u32[]{:S(2)}, u32[]{:S(2)}) %collective-permute-start.19) | collective-permute-done | bytes 262176 | tf_op jit(solution)/shard_map/ppermute | solution.py:243
  350.5 3.9 collective-permute-done.18
  355.3 5.3 %collective-permute-start.25 = (bf16[128,8192]{1,0:T(8,128)(2,1)S(1)}, bf16[128,8192]{1,0:T(8,128)(2,1)S(1)}, u32[]{:S(2)}, u32[]{:S(2)}) collective-permute-start(bf16[128,8192]{1,0:T(8,128)(2,1)S(1)} %copy-done.11), channel_id=1, source_target_pairs={{0,12},{12,0},{1,13},{13,1},{2,14},{14,2},{3,15},{15,3},{16,28},{2... | collective-permute-start | bytes 6291464 | tf_op jit(solution)/shard_map/ppermute | solution.py:214
  360.6 1.1 fusion.13
  361.7 15.2 %shard_map.98 = bf16[128,2048]{1,0:T(8,128)(2,1)} custom-call(s32[2]{0:T(128)} %pad_add_fusion.refs_0_, bf16[128,8192]{1,0:T(8,128)(2,1)} %collective-permute-done.20.refs_1_, bf16[256,8192]{1,0:T(8,128)(2,1)} %collective-permute-done.11.refs_2_, bf16[8192,1024]{1,0:T(8,128)(2,1)} %refs_3_.3, ...), custom_call_target="tpu_custom_call" | custom-call | flops 268435456 | bytes 2228224 | tf_op jit(solution)/shard_map/pallas_call | solution.py:148
  379.9 1.7 fusion.10
  381.6 1.9 collective-permute-done.23
  383.6 3.1 collective-permute-done.22
  387.8 19.6 %collective-permute-done.25.refs_1_ = bf16[128,8192]{1,0:T(8,128)(2,1)S(1)} collective-permute-done((bf16[128,8192]{1,0:T(8,128)(2,1)S(1)}, bf16[128,8192]{1,0:T(8,128)(2,1)S(1)}, u32[]{:S(2)}, u32[]{:S(2)}) %collective-permute-start.25) | collective-permute-done | bytes 2097184 | tf_op jit(solution)/shard_map/ppermute | solution.py:214
  407.5 1.3 copy-done.12
  408.8 15.2 %shard_map.99 = bf16[128,2048]{1,0:T(8,128)(2,1)} custom-call(s32[2]{0:T(128)} %pad_add_fusion.refs_0_, bf16[128,8192]{1,0:T(8,128)(2,1)} %copy-done.12, bf16[256,8192]{1,0:T(8,128)(2,1)} %collective-permute-done.11.refs_2_, bf16[8192,1024]{1,0:T(8,128)(2,1)} %refs_3_.3, bf16[8192,512]{1,0:T(8,128)(2,1)} %constant_dynamic-update-slice_fusion.refs_2_.refs_5_.refs_4_, ...), custom_call_target="tpu_custom_call" | custom-call | flops 268435456 | bytes 2228224 | tf_op jit(solution)/shard_map/pallas_call | solution.py:148
  428.2 19.5 %collective-permute-done.30 = bf16[1,32,2048]{2,1,0:T(8,128)(2,1)S(1)} collective-permute-done((bf16[1,32,2048]{2,1,0:T(8,128)(2,1)S(1)}, bf16[1,32,2048]{2,1,0:T(8,128)(2,1)S(1)}, u32[]{:S(2)}, u32[]{:S(2)}) %collective-permute-start.30) | collective-permute-done | bytes 131104 | tf_op jit(solution)/shard_map/ppermute | solution.py:243
  447.7 2.6 collective-permute-done.29
  451.2 1.3 pad_maximum_fusion.1.refs_0_
  452.7 4.5 collective-permute-done.31
  457.2 1.4 collective-permute-start.32
  458.6 3.8 collective-permute-done.32
  462.5 1.3 constant_dynamic-slice_fusion.3
  464.4 1.1 copy-done
  465.8 5.5 %shard_map.100 = (f32[4,1024,256]{2,1,0:T(8,128)}, f32[4,16,256]{2,1,0:T(8,128)S(1)}) custom-call(bf16[896,1024]{1,0:T(8,128)(2,1)S(1)} %pad_maximum_fusion.1.refs_0_, bf16[896,1024]{1,0:T(8,128)(2,1)} %collective-permute-done.27.refs_1_, bf16[128,1024]{1,0:T(8,128)(2,1)S(1)} %pad_maximum_fusion.7.refs_2_, ...), custom_call_target="tpu_custom_call" | custom-call | tf_op jit(solution)/shard_map/pallas_call | solution.py:53
  471.4 1.4 collective-permute-start.36
  474.5 1.9 collective-permute-done.35
  476.4 3.5 collective-permute-start.39
  481.8 2.5 collective-permute-done.38
  (110 shorter events, 24.6 us)
Async XLA Ops:
  7.2 455.4 %all-gather.3.cloned.1.call-start = ((), (), s32[]{:S(2)}) async-start(), calls=%async_computation | async-start | bytes 1310720 | tf_op jit(solution)/shard_map/all_gather | solution.py:224
  7.2 8.6 %copy-start.2 = (bf16[4,128,8192]{2,1,0:T(8,128)(2,1)S(1)}, bf16[4,128,8192]{2,1,0:T(8,128)(2,1)}, u32[]{:S(2)}) copy-start(bf16[4,128,8192]{2,1,0:T(8,128)(2,1)} %param.9) | copy-start | bytes 25165828
  12.8 49.0 %collective-permute-start = (bf16[2048,512]{1,0:T(8,128)(2,1)}, bf16[2048,512]{1,0:T(8,128)(2,1)}, u32[]{:S(2)}, u32[]{:S(2)}) collective-permute-start(bf16[2048,512]{1,0:T(8,128)(2,1)} %get-tuple-element.36), channel_id=1, source_target_pairs={{0,4},{4,0},{8,12},{12,8},{1,5},{5,1},{9,13},{13,9},{2,6},{6,2},{1... | collective-permute-start | bytes 6291464 | tf_op jit(solution)/shard_map/ppermute | solution.py:202
  19.6 137.6 %collective-permute-start.3 = (bf16[256,8192]{1,0:T(8,128)(2,1)}, bf16[256,8192]{1,0:T(8,128)(2,1)}, u32[]{:S(2)}, u32[]{:S(2)}) collective-permute-start(bf16[256,8192]{1,0:T(8,128)(2,1)} %bitcast.4), channel_id=1, source_target_pairs={{4,8},{8,4},{5,9},{9,5},{6,10},{10,6},{7,11},{11,7},{20,24},{24,20... | collective-permute-start | bytes 12582920 | tf_op jit(solution)/shard_map/ppermute | solution.py:201
  22.9 16.1 %copy-start.15 = (s32[2048]{0:T(1024)S(1)}, s32[2048]{0:T(1024)}, u32[]{:S(2)}) copy-start(s32[2048]{0:T(1024)} %param.15) | copy-start | bytes 24580
  22.9 16.1 %copy-start.16 = (s32[4]{0:T(128)S(1)}, s32[4]{0:T(128)}, u32[]{:S(2)}) copy-start(s32[4]{0:T(128)} %param.14) | copy-start | bytes 52
  22.9 16.4 %copy-start.17 = (bf16[8192,256]{1,0:T(8,128)(2,1)S(1)}, bf16[8192,256]{1,0:T(8,128)(2,1)}, u32[]{:S(2)}) copy-start(bf16[8192,256]{1,0:T(8,128)(2,1)} %param.10) | copy-start | bytes 12582916
  61.8 48.9 %collective-permute-start.2 = (bf16[2048,512]{1,0:T(8,128)(2,1)}, bf16[2048,512]{1,0:T(8,128)(2,1)}, u32[]{:S(2)}, u32[]{:S(2)}) collective-permute-start(bf16[2048,512]{1,0:T(8,128)(2,1)} %get-tuple-element.19), channel_id=1, source_target_pairs={{0,4},{4,0},{8,12},{12,8},{1,5},{5,1},{9,13},{13,9},{2,6},{6,2},{1... | collective-permute-start | bytes 6291464 | tf_op jit(solution)/shard_map/ppermute | solution.py:202
  63.5 92.0 %collective-permute-start.1 = (bf16[2048,512]{1,0:T(8,128)(2,1)S(1)}, bf16[2048,512]{1,0:T(8,128)(2,1)S(1)}, u32[]{:S(2)}, u32[]{:S(2)}) collective-permute-start(bf16[2048,512]{1,0:T(8,128)(2,1)S(1)} %get-tuple-element.38), channel_id=1, source_target_pairs={{0,4},{4,0},{8,12},{12,8},{1,5},{5,1},{9,13},{13,9},{2,6},{6,2},{1... | collective-permute-start | bytes 6291464 | tf_op jit(solution)/shard_map/ppermute | solution.py:202
  63.8 140.3 %collective-permute-start.11 = (bf16[256,8192]{1,0:T(8,128)(2,1)}, bf16[256,8192]{1,0:T(8,128)(2,1)}, u32[]{:S(2)}, u32[]{:S(2)}) collective-permute-start(bf16[256,8192]{1,0:T(8,128)(2,1)} %bitcast.128), channel_id=1, source_target_pairs={{4,8},{8,4},{5,9},{9,5},{6,10},{10,6},{7,11},{11,7},{20,24},{24,20... | collective-permute-start | bytes 12582920 | tf_op jit(solution)/shard_map/ppermute | solution.py:201
  66.4 92.3 %collective-permute-start.6 = (bf16[2048,512]{1,0:T(8,128)(2,1)}, bf16[2048,512]{1,0:T(8,128)(2,1)}, u32[]{:S(2)}, u32[]{:S(2)}) collective-permute-start(bf16[2048,512]{1,0:T(8,128)(2,1)} %collective-permute-done), channel_id=1, source_target_pairs={{0,16},{16,0},{1,17},{17,1},{2,18},{18,2},{3,19},{19,3},{4,20},{20... | collective-permute-start | bytes 6291464 | tf_op jit(solution)/shard_map/ppermute | solution.py:203
  110.7 67.3 %collective-permute-start.5 = (bf16[1024,512]{1,0:T(8,128)(2,1)S(1)}, bf16[1024,512]{1,0:T(8,128)(2,1)S(1)}, u32[]{:S(2)}, u32[]{:S(2)}) collective-permute-start(bf16[1024,512]{1,0:T(8,128)(2,1)S(1)} %get-tuple-element.21), channel_id=1, source_target_pairs={{0,4},{4,0},{8,12},{12,8},{1,5},{5,1},{9,13},{13,9},{2,6},{6,2},{1... | collective-permute-start | bytes 3145736 | tf_op jit(solution)/shard_map/ppermute | solution.py:202
  155.5 30.2 %copy-start.7 = (bf16[2048,512]{1,0:T(8,128)(2,1)}, bf16[2048,512]{1,0:T(8,128)(2,1)S(1)}, u32[]{:S(2)}) copy-start(bf16[2048,512]{1,0:T(8,128)(2,1)S(1)} %collective-permute-done.1) | copy-start | bytes 6291460
  155.5 48.6 %collective-permute-start.7 = (bf16[2048,512]{1,0:T(8,128)(2,1)S(1)}, bf16[2048,512]{1,0:T(8,128)(2,1)S(1)}, u32[]{:S(2)}, u32[]{:S(2)}) collective-permute-start(bf16[2048,512]{1,0:T(8,128)(2,1)S(1)} %collective-permute-done.1), channel_id=1, source_target_pairs={{0,16},{16,0},{1,17},{17,1},{2,18},{18,2},{3,19},{19,3},{4,20},{20... | collective-permute-start | bytes 6291464 | tf_op jit(solution)/shard_map/ppermute | solution.py:203
  157.2 46.9 %collective-permute-start.4 = (bf16[1024,512]{1,0:T(8,128)(2,1)S(1)}, bf16[1024,512]{1,0:T(8,128)(2,1)S(1)}, u32[]{:S(2)}, u32[]{:S(2)}) collective-permute-start(bf16[1024,512]{1,0:T(8,128)(2,1)S(1)} %get-tuple-element.20), channel_id=1, source_target_pairs={{0,4},{4,0},{8,12},{12,8},{1,5},{5,1},{9,13},{13,9},{2,6},{6,2},{1... | collective-permute-start | bytes 3145736 | tf_op jit(solution)/shard_map/ppermute | solution.py:202
  158.8 90.3 %collective-permute-start.8 = (bf16[2048,512]{1,0:T(8,128)(2,1)}, bf16[2048,512]{1,0:T(8,128)(2,1)}, u32[]{:S(2)}, u32[]{:S(2)}) collective-permute-start(bf16[2048,512]{1,0:T(8,128)(2,1)} %collective-permute-done.2), channel_id=1, source_target_pairs={{0,16},{16,0},{1,17},{17,1},{2,18},{18,2},{3,19},{19,3},{4,20},{20... | collective-permute-start | bytes 6291464 | tf_op jit(solution)/shard_map/ppermute | solution.py:203
  178.0 89.2 %collective-permute-start.10 = (bf16[1024,512]{1,0:T(8,128)(2,1)S(1)}, bf16[1024,512]{1,0:T(8,128)(2,1)}, u32[]{:S(2)}, u32[]{:S(2)}) collective-permute-start(bf16[1024,512]{1,0:T(8,128)(2,1)S(1)} %collective-permute-done.5), channel_id=1, source_target_pairs={{0,16},{16,0},{1,17},{17,1},{2,18},{18,2},{3,19},{19,3},{4,20},{20... | collective-permute-start | bytes 3145736 | tf_op jit(solution)/shard_map/ppermute | solution.py:203
  204.1 1.3 copy-start.9
  204.1 1.7 copy-start.13
  205.7 80.3 %collective-permute-start.12 = (bf16[128,8192]{1,0:T(8,128)(2,1)}, bf16[128,8192]{1,0:T(8,128)(2,1)S(1)}, u32[]{:S(2)}, u32[]{:S(2)}) collective-permute-start(bf16[128,8192]{1,0:T(8,128)(2,1)} %get-tuple-element.23), channel_id=1, source_target_pairs={{0,12},{12,0},{1,13},{13,1},{2,14},{14,2},{3,15},{15,3},{16,28},{2... | collective-permute-start | bytes 6291464 | tf_op jit(solution)/shard_map/ppermute | solution.py:214
  211.4 63.8 %copy-start.8 = (bf16[2048,512]{1,0:T(8,128)(2,1)S(1)}, bf16[2048,512]{1,0:T(8,128)(2,1)}, u32[]{:S(2)}) copy-start(bf16[2048,512]{1,0:T(8,128)(2,1)} %copy-done.7) | copy-start | bytes 6291460
  267.2 52.5 %collective-permute-start.16 = (bf16[128,8192]{1,0:T(8,128)(2,1)}, bf16[128,8192]{1,0:T(8,128)(2,1)S(1)}, u32[]{:S(2)}, u32[]{:S(2)}) collective-permute-start(bf16[128,8192]{1,0:T(8,128)(2,1)} %get-tuple-element.25), channel_id=1, source_target_pairs={{0,12},{12,0},{1,13},{13,1},{2,14},{14,2},{3,15},{15,3},{16,28},{2... | collective-permute-start | bytes 6291464 | tf_op jit(solution)/shard_map/ppermute | solution.py:214
  275.2 4.8 copy-start.14
  276.8 7.8 %copy-start.10 = (bf16[2048,512]{1,0:T(8,128)(2,1)S(1)}, bf16[2048,512]{1,0:T(8,128)(2,1)}, u32[]{:S(2)}) copy-start(bf16[2048,512]{1,0:T(8,128)(2,1)} %copy-done.9) | copy-start | bytes 6291460
  280.0 19.8 %collective-permute-start.9 = (bf16[1024,512]{1,0:T(8,128)(2,1)S(1)}, bf16[1024,512]{1,0:T(8,128)(2,1)S(1)}, u32[]{:S(2)}, u32[]{:S(2)}) collective-permute-start(bf16[1024,512]{1,0:T(8,128)(2,1)S(1)} %copy-done.14), channel_id=1, source_target_pairs={{0,16},{16,0},{1,17},{17,1},{2,18},{18,2},{3,19},{19,3},{4,20},{20... | collective-permute-start | bytes 3145736 | tf_op jit(solution)/shard_map/ppermute | solution.py:203
  286.0 7.3 %copy-start.5 = (bf16[128,8192]{1,0:T(8,128)(2,1)}, bf16[128,8192]{1,0:T(8,128)(2,1)S(1)}, u32[]{:S(2)}) copy-start(bf16[128,8192]{1,0:T(8,128)(2,1)S(1)} %collective-permute-done.12.refs_1_) | copy-start | bytes 6291460
  286.0 75.6 %collective-permute-start.20 = (bf16[128,8192]{1,0:T(8,128)(2,1)}, bf16[128,8192]{1,0:T(8,128)(2,1)}, u32[]{:S(2)}, u32[]{:S(2)}) collective-permute-start(bf16[128,8192]{1,0:T(8,128)(2,1)} %get-tuple-element.27), channel_id=1, source_target_pairs={{0,12},{12,0},{1,13},{13,1},{2,14},{14,2},{3,15},{15,3},{16,28},{2... | collective-permute-start | bytes 6291464 | tf_op jit(solution)/shard_map/ppermute | solution.py:214
  318.8 23.9 %copy-start.3 = (bf16[512,1024]{1,0:T(8,128)(2,1)S(1)}, bf16[512,1024]{1,0:T(8,128)(2,1)}, u32[]{:S(2)}) copy-start(bf16[512,1024]{1,0:T(8,128)(2,1)} %shard_map.95) | copy-start | bytes 3145732
  318.8 23.9 %copy-start.4 = (bf16[512,1024]{1,0:T(8,128)(2,1)S(1)}, bf16[512,1024]{1,0:T(8,128)(2,1)}, u32[]{:S(2)}) copy-start(bf16[512,1024]{1,0:T(8,128)(2,1)} %shard_map.96) | copy-start | bytes 3145732
  319.6 1.3 copy-start.6
  340.9 8.6 %collective-permute-start.19 = (bf16[2,32,2048]{2,1,0:T(8,128)(2,1)S(1)}, bf16[2,32,2048]{2,1,0:T(8,128)(2,1)S(1)}, u32[]{:S(2)}, u32[]{:S(2)}) collective-permute-start(bf16[2,32,2048]{2,1,0:T(8,128)(2,1)S(1)} %get-tuple-element.55), channel_id=1, source_target_pairs={{0,3},{1,2},{2,1},{3,0},{4,7},{5,6},{6,5},{7,4},{8,11},{9,10},{10,... | collective-permute-start | bytes 786440 | tf_op jit(solution)/shard_map/ppermute | solution.py:243
  340.9 13.5 %collective-permute-start.18 = (bf16[2,32,2048]{2,1,0:T(8,128)(2,1)S(1)}, bf16[2,32,2048]{2,1,0:T(8,128)(2,1)S(1)}, u32[]{:S(2)}, u32[]{:S(2)}) collective-permute-start(bf16[2,32,2048]{2,1,0:T(8,128)(2,1)S(1)} %get-tuple-element.56), channel_id=1, source_target_pairs={{0,2},{1,3},{2,0},{3,1},{4,6},{5,7},{6,4},{7,5},{8,10},{9,11},{10,... | collective-permute-start | bytes 786440 | tf_op jit(solution)/shard_map/ppermute | solution.py:243
  342.0 13.3 %copy-start.11 = (bf16[128,8192]{1,0:T(8,128)(2,1)S(1)}, bf16[128,8192]{1,0:T(8,128)(2,1)}, u32[]{:S(2)}) copy-start(bf16[128,8192]{1,0:T(8,128)(2,1)} %get-tuple-element.29) | copy-start | bytes 6291460
  342.0 13.3 %collective-permute-start.17 = (bf16[2,32,2048]{2,1,0:T(8,128)(2,1)S(1)}, bf16[2,32,2048]{2,1,0:T(8,128)(2,1)S(1)}, u32[]{:S(2)}, u32[]{:S(2)}) collective-permute-start(bf16[2,32,2048]{2,1,0:T(8,128)(2,1)S(1)} %get-tuple-element.54), channel_id=1, source_target_pairs={{0,1},{1,0},{2,3},{3,2},{4,5},{5,4},{6,7},{7,6},{8,9},{9,8},{10,11... | collective-permute-start | bytes 786440 | tf_op jit(solution)/shard_map/ppermute | solution.py:243
  343.2 35.7 %collective-permute-start.15 = (bf16[4,32,2048]{2,1,0:T(8,128)(2,1)S(1)}, bf16[4,32,2048]{2,1,0:T(8,128)(2,1)}, u32[]{:S(2)}, u32[]{:S(2)}) collective-permute-start(bf16[4,32,2048]{2,1,0:T(8,128)(2,1)S(1)} %get-tuple-element.48), channel_id=1, source_target_pairs={{0,3},{1,2},{2,1},{3,0},{4,7},{5,6},{6,5},{7,4},{8,11},{9,10},{10,... | collective-permute-start | bytes 1572872 | tf_op jit(solution)/shard_map/ppermute | solution.py:243
  349.4 30.3 %collective-permute-start.14 = (bf16[4,32,2048]{2,1,0:T(8,128)(2,1)S(1)}, bf16[4,32,2048]{2,1,0:T(8,128)(2,1)}, u32[]{:S(2)}, u32[]{:S(2)}) collective-permute-start(bf16[4,32,2048]{2,1,0:T(8,128)(2,1)S(1)} %get-tuple-element.49), channel_id=1, source_target_pairs={{0,2},{1,3},{2,0},{3,1},{4,6},{5,7},{6,4},{7,5},{8,10},{9,11},{10,... | collective-permute-start | bytes 1572872 | tf_op jit(solution)/shard_map/ppermute | solution.py:243
  354.4 25.5 %collective-permute-start.13 = (bf16[4,32,2048]{2,1,0:T(8,128)(2,1)S(1)}, bf16[4,32,2048]{2,1,0:T(8,128)(2,1)}, u32[]{:S(2)}, u32[]{:S(2)}) collective-permute-start(bf16[4,32,2048]{2,1,0:T(8,128)(2,1)S(1)} %get-tuple-element.47), channel_id=1, source_target_pairs={{0,1},{1,0},{2,3},{3,2},{4,5},{5,4},{6,7},{7,6},{8,9},{9,8},{10,11... | collective-permute-start | bytes 1572872 | tf_op jit(solution)/shard_map/ppermute | solution.py:243
  355.3 52.2 %collective-permute-start.25 = (bf16[128,8192]{1,0:T(8,128)(2,1)S(1)}, bf16[128,8192]{1,0:T(8,128)(2,1)S(1)}, u32[]{:S(2)}, u32[]{:S(2)}) collective-permute-start(bf16[128,8192]{1,0:T(8,128)(2,1)S(1)} %copy-done.11), channel_id=1, source_target_pairs={{0,12},{12,0},{1,13},{13,1},{2,14},{14,2},{3,15},{15,3},{16,28},{2... | collective-permute-start | bytes 6291464 | tf_op jit(solution)/shard_map/ppermute | solution.py:214
  378.0 5.6 %collective-permute-start.23 = (bf16[1,32,2048]{2,1,0:T(8,128)(2,1)S(1)}, bf16[1,32,2048]{2,1,0:T(8,128)(2,1)S(1)}, u32[]{:S(2)}, u32[]{:S(2)}) collective-permute-start(bf16[1,32,2048]{2,1,0:T(8,128)(2,1)S(1)} %get-tuple-element.63), channel_id=1, source_target_pairs={{0,3},{1,2},{2,1},{3,0},{4,7},{5,6},{6,5},{7,4},{8,11},{9,10},{10,... | collective-permute-start | bytes 393224 | tf_op jit(solution)/shard_map/ppermute | solution.py:243
  378.9 7.8 %collective-permute-start.22 = (bf16[1,32,2048]{2,1,0:T(8,128)(2,1)S(1)}, bf16[1,32,2048]{2,1,0:T(8,128)(2,1)S(1)}, u32[]{:S(2)}, u32[]{:S(2)}) collective-permute-start(bf16[1,32,2048]{2,1,0:T(8,128)(2,1)S(1)} %get-tuple-element.64), channel_id=1, source_target_pairs={{0,2},{1,3},{2,0},{3,1},{4,6},{5,7},{6,4},{7,5},{8,10},{9,11},{10,... | collective-permute-start | bytes 393224 | tf_op jit(solution)/shard_map/ppermute | solution.py:243
  379.7 6.9 %collective-permute-start.21 = (bf16[1,32,2048]{2,1,0:T(8,128)(2,1)S(1)}, bf16[1,32,2048]{2,1,0:T(8,128)(2,1)S(1)}, u32[]{:S(2)}, u32[]{:S(2)}) collective-permute-start(bf16[1,32,2048]{2,1,0:T(8,128)(2,1)S(1)} %get-tuple-element.62), channel_id=1, source_target_pairs={{0,1},{1,0},{2,3},{3,2},{4,5},{5,4},{6,7},{7,6},{8,9},{9,8},{10,11... | collective-permute-start | bytes 393224 | tf_op jit(solution)/shard_map/ppermute | solution.py:243
  387.8 36.2 %collective-permute-start.24 = (bf16[224,1024]{1,0:T(8,128)(2,1)S(1)}, bf16[224,1024]{1,0:T(8,128)(2,1)S(1)}, u32[]{:S(2)}, u32[]{:S(2)}) collective-permute-start(bf16[224,1024]{1,0:T(8,128)(2,1)S(1)} %get-tuple-element.58), channel_id=1, source_target_pairs={{0,4},{4,0},{8,12},{12,8},{1,5},{5,1},{9,13},{13,9},{2,6},{6,2},{1... | collective-permute-start | bytes 1376264 | tf_op jit(solution)/shard_map/ppermute | solution.py:243
  407.5 1.3 copy-start.12
  424.1 27.2 %collective-permute-start.26 = (bf16[448,1024]{1,0:T(8,128)(2,1)S(1)}, bf16[448,1024]{1,0:T(8,128)(2,1)}, u32[]{:S(2)}, u32[]{:S(2)}) collective-permute-start(bf16[448,1024]{1,0:T(8,128)(2,1)S(1)} %pad_maximum_fusion.4), channel_id=1, source_target_pairs={{0,2},{1,3},{2,0},{3,1},{4,6},{5,7},{6,4},{7,5},{8,10},{9,11},{10,... | collective-permute-start | bytes 2752520 | tf_op jit(solution)/shard_map/ppermute | solution.py:243
  426.3 21.4 %collective-permute-start.30 = (bf16[1,32,2048]{2,1,0:T(8,128)(2,1)S(1)}, bf16[1,32,2048]{2,1,0:T(8,128)(2,1)S(1)}, u32[]{:S(2)}, u32[]{:S(2)}) collective-permute-start(bf16[1,32,2048]{2,1,0:T(8,128)(2,1)S(1)} %get-tuple-element.60), channel_id=1, source_target_pairs={{0,3},{1,2},{2,1},{3,0},{4,7},{5,6},{6,5},{7,4},{8,11},{9,10},{10,... | collective-permute-start | bytes 393224 | tf_op jit(solution)/shard_map/ppermute | solution.py:243
  426.3 23.9 %collective-permute-start.29 = (bf16[1,32,2048]{2,1,0:T(8,128)(2,1)S(1)}, bf16[1,32,2048]{2,1,0:T(8,128)(2,1)S(1)}, u32[]{:S(2)}, u32[]{:S(2)}) collective-permute-start(bf16[1,32,2048]{2,1,0:T(8,128)(2,1)S(1)} %get-tuple-element.61), channel_id=1, source_target_pairs={{0,2},{1,3},{2,0},{3,1},{4,6},{5,7},{6,4},{7,5},{8,10},{9,11},{10,... | collective-permute-start | bytes 393224 | tf_op jit(solution)/shard_map/ppermute | solution.py:243
  427.4 22.8 %collective-permute-start.28 = (bf16[1,32,2048]{2,1,0:T(8,128)(2,1)S(1)}, bf16[1,32,2048]{2,1,0:T(8,128)(2,1)S(1)}, u32[]{:S(2)}, u32[]{:S(2)}) collective-permute-start(bf16[1,32,2048]{2,1,0:T(8,128)(2,1)S(1)} %get-tuple-element.59), channel_id=1, source_target_pairs={{0,1},{1,0},{2,3},{3,2},{4,5},{5,4},{6,7},{7,6},{8,9},{9,8},{10,11... | collective-permute-start | bytes 393224 | tf_op jit(solution)/shard_map/ppermute | solution.py:243
  452.6 11.8 %collective-permute-start.27 = (bf16[896,1024]{1,0:T(8,128)(2,1)S(1)}, bf16[896,1024]{1,0:T(8,128)(2,1)}, u32[]{:S(2)}, u32[]{:S(2)}) collective-permute-start(bf16[896,1024]{1,0:T(8,128)(2,1)S(1)} %pad_maximum_fusion.1.refs_0_), channel_id=1, source_target_pairs={{0,1},{1,0},{2,3},{3,2},{4,5},{5,4},{6,7},{7,6},{8,9},{9,8},{10,11... | collective-permute-start | bytes 5505032 | tf_op jit(solution)/shard_map/ppermute | solution.py:243
  452.7 4.6 collective-permute-start.31
  457.2 5.2 %collective-permute-start.32 = (bf16[64,1024]{1,0:T(8,128)(2,1)S(1)}, bf16[64,1024]{1,0:T(8,128)(2,1)S(1)}, u32[]{:S(2)}, u32[]{:S(2)}) collective-permute-start(bf16[64,1024]{1,0:T(8,128)(2,1)S(1)} %pad_maximum_fusion.8), channel_id=1, source_target_pairs={{0,2},{1,3},{2,0},{3,1},{4,6},{5,7},{6,4},{7,5},{8,10},{9,11},{10,... | collective-permute-start | bytes 393224 | tf_op jit(solution)/shard_map/ppermute | solution.py:243
  462.4 1.9 collective-permute-start.33
  463.9 1.6 copy-start
  463.9 1.8 copy-start.1
  471.4 3.0 collective-permute-start.36
  472.8 3.6 collective-permute-start.35
  473.5 2.9 collective-permute-start.34
  476.4 5.4 %collective-permute-start.39 = (f32[4,4]{1,0:T(4,128)S(1)}, f32[4,4]{1,0:T(4,128)S(1)}, u32[]{:S(2)}, u32[]{:S(2)}) collective-permute-start(f32[4,4]{1,0:T(4,128)S(1)} %add_add_fusion.1), channel_id=1, source_target_pairs={{0,12},{4,8},{8,4},{12,0},{1,13},{5,9},{9,5},{13,1},{2,14},{6,10},... | collective-permute-start | bytes 200 | tf_op jit(solution)/shard_map/ppermute | solution.py:173
  479.8 4.5 collective-permute-start.38
  479.8 4.5 collective-permute-start.37
Sparse Core Ops, SparseCore 0:
  425.3 28.3 all-gather.2

commit v12 on v11

--- a/solution.py
+++ b/solution.py
@@ -194,7 +194,7 @@
     for i, (a, b) in enumerate(spans):
         piece = lax.dynamic_slice(grad_basis, (a * deep, group * half), ((b - a) * deep, half))
         if i >= 2:
-            early = {2: [own_own, local_act], 3: [other[0]], 4: []}[i]
+            early = {2: [own_own, local_act], 3: [other[0], far[0]], 4: [far[1]]}[i]
             piece = after(piece, near[i - 2], *early)
         if i in (0, 2):
             part = flat[: 4 * slab] if i == 0 else after(flat[4 * slab :], near[0])
@@ -206,7 +206,7 @@
 
     ranges = [(0, 2), (2, 4), (4, 6), (6, units)]
     phase = [near[3], near[4], other[1]]
-    ties = [[*phase, far[0], far[1]], [*phase, far[2], far[4]], [], []]
+    ties = [[*phase, far[0]], [*phase, far[2]], [far[3], far[4]], []]
     partner = []
     for k, (a, b) in enumerate(ranges):
         tie = ties[k] + ([partner[k - 2]] if k >= 2 else [])
@@ -215,20 +215,7 @@
 
     sub, full = tok // parts, cands * tok
 
-    def by_part(block):
-        split = block.reshape(cands, parts, sub, -1)
-        return jnp.stack(
-            [lax.dynamic_index_in_dim(split, col ^ d, 1, keepdims=False) for d in (0, 2, 1, 3)]
-        )
-
     every_act = lax.all_gather(after(local_act, partner[2]), "row", axis=0)
-    act = [
-        by_part(lax.dynamic_index_in_dim(every_act, i, 0, keepdims=False))
-        for i in (row, row ^ 1, planes - 1 - row, planes - 1 - (row ^ 1))
-    ]
-    act_rot = [jnp.stack(act[i : i + 2], axis=1) for i in (0, 2)]
-    act_rot = [jnp.moveaxis(x, 2, 0).reshape(cands, 2 * tok, -1) for x in act_rot]
-    act_rot = jnp.concatenate(act_rot, axis=1)
 
     own_end = project(flags, [(flat, 0, full)], [], [near_basis, after(far_basis, partner[0])])
     outer = project(
@@ -250,8 +237,8 @@
             total = total + swap(sent, "col", d).astype(F32)
         return total.astype(BF16).reshape(-1, 2 * dirs)
 
-    def gather(mine):
-        pair = jnp.concatenate([mine, swap(mine, "col", 2)], axis=0)
+    def gather(mine, *earlier):
+        pair = jnp.concatenate([mine, after(swap(mine, "col", 2), *earlier)], axis=0)
         return [pair, swap(pair, "col", 1)]
 
     sums = [scatter_sum(jnp.concatenate([own_own, own_end], axis=1)), scatter_sum(outer)]
@@ -266,24 +253,42 @@
             sums.append(scatter_sum(product))
             early = jnp.concatenate(sums, axis=0)
             got = swap(early[:, dirs:], "row", 1)
-    early = jnp.concatenate([early[:, :dirs], after(got, product)], axis=0)
-    last = scatter_sum(after(product, early))
+    early_own = gather(early[:, :dirs])
+    last = scatter_sum(after(product, got, *early_own))
+    got = after(got, last)
+    last = after(last, every_act)
     last = jnp.concatenate([last[:, :dirs], swap(last[:, dirs:], "row", 1)], axis=0)
-    arrays = gather(early) + gather(last)
+    early_got = gather(got, last)
+    arrays = early_own + early_got + gather(last)
+    every_act = after(every_act, last)
+
+    def by_part(block):
+        split = block.reshape(cands, parts, sub, -1)
+        return jnp.stack(
+            [lax.dynamic_index_in_dim(split, col ^ d, 1, keepdims=False) for d in (0, 2, 1, 3)]
+        )
+
+    act = [
+        by_part(lax.dynamic_index_in_dim(every_act, i, 0, keepdims=False))
+        for i in (row, row ^ 1, planes - 1 - row, planes - 1 - (row ^ 1))
+    ]
+    act_rot = [jnp.stack(act[i : i + 2], axis=1) for i in (0, 2)]
+    act_rot = [jnp.moveaxis(x, 2, 0).reshape(cands, 2 * tok, -1) for x in act_rot]
+    act_rot = jnp.concatenate(act_rot, axis=1)
+
     segments = [[] for _ in range(cands)]
     for kind in (0, 1):
         for c in range(cands):
             for j in (0, 1):
                 for side in (0, 1):
                     for plane in (0, 1):
-                        base = (side * 2 + plane) * early.shape[0] // 2
+                        base = side * early.shape[0]
                         if kind == 0:
-                            segments[c].append((j, base + c * sub, sub))
+                            segments[c].append((2 * plane + j, base + c * sub, sub))
                         elif c < cands - 1:
-                            segments[c].append((j, base + (cands + c) * sub, sub))
+                            segments[c].append((2 * plane + j, base + (cands + c) * sub, sub))
                         else:
-                            base = (side * 2 + plane) * last.shape[0] // 2
-                            segments[c].append((2 + j, base, sub))
+                            segments[c].append((4 + j, (side * 2 + plane) * sub, sub))
     layout = tuple(tuple(s) for s in segments)
 
     rotated, scores = rotate_and_score(arrays, layout, act_rot, eigenvalues, query_rotated)

time: 493 us -> 506 us (1.026)
  waiting for transfers between devices: 271 us -> 287 us
    ppermute x5, waiting for transfers between devices: 80.6 us -> 131 us  [chain_body(): far.append(lax.ppermute(near[i], 'groups', [(0, 1), (1, 0)]))]
    ppermute x5, waiting for transfers between devices: 119 us -> 89.7 us  [chain_body(): near.append(lax.ppermute(piece, 'row', beside))]
    ppermute x4, waiting for transfers between devices: 20.4 us -> 8.23 us  [chain_body(): partner.append(lax.ppermute(after(piece, *tie), 'row', ends))]
    ppermute x18 -> x20, waiting for transfers between devices: 44.9 us -> 51.2 us  [swap(): return lax.ppermute(value, axis, [(i, i ^ d) for i in range(size)])]
    ppermute x18 -> x20, starting transfers between devices: 11.1 us -> 14.7 us  [swap(): return lax.ppermute(value, axis, [(i, i ^ d) for i in range(size)])]
    unnamed x44 -> x35, local copies, waits for them, and re-layouts: 23.3 us -> 22.7 us
  transfers between devices with their start and end apart: 41 -> 43, of which waited for: 22 -> 24; matrix products, arithmetic and copies ran while one was open for 10% -> 10% of each run, Pallas kernels for 16% -> 16%
where the time goes in v12:
time: 506 us; the launch traced here: 505 us
  waiting for transfers between devices  287 us (57%)
  Pallas kernels  85.3 us (17%)
  starting transfers between devices  59 us (12%)
  local copies, waits for them, and re-layouts  46.9 us (9%)
  between operations  14.5 us (3%)
  matrix products  7.61 us (2%)
  other arithmetic  5.68 us (1%)
    ppermute x5, waiting for transfers between devices, chain_body(): far.append(lax.ppermute(near[i], 'groups', [(0, 1), (1, 0)]))  131 us
    ppermute x5, waiting for transfers between devices, chain_body(): near.append(lax.ppermute(piece, 'row', beside))  89.7 us
    pallas_call x5, Pallas kernels, project(): pl.pallas_call(functools.partial(project_kernel, len(ends), len(tokens),...  80.8 us
    ppermute x20, waiting for transfers between devices, swap(): return lax.ppermute(value, axis, [(i, i ^ d) for i in range(size)])  51.2 us
    unnamed x35, local copies, waits for them, and re-layouts  22.7 us
    ppermute x4, starting transfers between devices, chain_body(): partner.append(lax.ppermute(after(piece, *tie), 'row', ends))  16.7 us
    ppermute x20, starting transfers between devices, swap(): return lax.ppermute(value, axis, [(i, i ^ d) for i in range(size)])  14.7 us
  transfers between devices with their start and end apart: 43, of which 24 were waited for; matrix products, arithmetic and copies ran while one was open for 10% of the time, Pallas kernels for 16%

profile of v12, /device:TPU:0, one launch (start us, length us, event | category | flops | bytes accessed | tf_op | source)
XLA Modules:
  0.0 505.5 jit_solution(14757872503783221646)
XLA Ops:
  7.2 5.6 %constant_dynamic-slice_fusion.7 = (bf16[2048,512]{1,0:T(8,128)(2,1)S(1)}, bf16[2048,512]{1,0:T(8,128)(2,1)}, bf16[2048,512]{1,0:T(8,128)(2,1)}) fusion(bf16[8192,1024]{1,0:T(8,128)(2,1)} %refs_3_.3, s32[]{:T(128)S(6)} %select_n.68), kind=kLoop, calls=%fused_computation.92 | loop fusion | bytes 12582916 | tf_op jit(solution)/shard_map/dynamic_slice | solution.py:195
  12.8 3.0 collective-permute-start.1
  15.9 3.8 fusion.22
  19.7 2.7 collective-permute-start.3
  23.3 7.6 %fusion.5 = bf16[4,128,256]{2,1,0:T(8,128)(2,1)} fusion(bf16[4,128,8192]{2,1,0:T(8,128)(2,1)} %param.8, bf16[8192,256]{1,0:T(8,128)(2,1)} %param.10, f32[4,128]{1,0:T(4,128)S(1)} %compare_convert_fusion), kind=kOutput, calls=%fused_computation.8 | convolution fusion | flops 2147745792 | bytes 12847104 | tf_op jit(solution)/shard_map/ctd,dk->ctk/dot_general | solution.py:25
  30.9 75.8 %collective-permute-done = bf16[2048,512]{1,0:T(8,128)(2,1)} collective-permute-done((bf16[2048,512]{1,0:T(8,128)(2,1)}, bf16[2048,512]{1,0:T(8,128)(2,1)}, u32[]{:S(2)}, u32[]{:S(2)}) %collective-permute-start) | collective-permute-done | bytes 2097184 | tf_op jit(solution)/shard_map/ppermute | solution.py:202
  106.7 2.6 collective-permute-start.11
  109.4 15.9 %shard_map.95 = bf16[512,1024]{1,0:T(8,128)(2,1)} custom-call(s32[2]{0:T(128)} %pad_add_fusion.refs_0_, bf16[512,8192]{1,0:T(8,128)(2,1)} %bitcast.122, bf16[8192,1024]{1,0:T(8,128)(2,1)} %refs_3_.3), custom_call_target="tpu_custom_call" | custom-call | flops 536870912 | bytes 1572864 | tf_op jit(solution)/shard_map/pallas_call | solution.py:148
  125.3 1.7 collective-permute-start.6
  127.0 2.4 collective-permute-start.2
  129.9 1.7 constant_dynamic-slice_fusion.5
  131.6 42.5 %collective-permute-done.6 = bf16[2048,512]{1,0:T(8,128)(2,1)S(1)} collective-permute-done((bf16[2048,512]{1,0:T(8,128)(2,1)}, bf16[2048,512]{1,0:T(8,128)(2,1)S(1)}, u32[]{:S(2)}, u32[]{:S(2)}) %collective-permute-start.6) | collective-permute-done | bytes 2097184 | tf_op jit(solution)/shard_map/ppermute | solution.py:203
  174.1 1.4 copy-done.7
  175.4 2.6 collective-permute-start.7
  178.0 39.3 %collective-permute-done.4 = bf16[2048,512]{1,0:T(8,128)(2,1)} collective-permute-done((bf16[2048,512]{1,0:T(8,128)(2,1)}, bf16[2048,512]{1,0:T(8,128)(2,1)}, u32[]{:S(2)}, u32[]{:S(2)}) %collective-permute-start.4) | collective-permute-done | bytes 2097184 | tf_op jit(solution)/shard_map/ppermute | solution.py:203
  217.4 2.0 collective-permute-start.5
  219.4 1.5 collective-permute-start.8
  220.9 6.0 %slice_bitcast_fusion = (bf16[128,8192]{1,0:T(8,128)(2,1)}, bf16[128,8192]{1,0:T(8,128)(2,1)}, bf16[128,8192]{1,0:T(8,128)(2,1)}, bf16[128,8192]{1,0:T(8,128)(2,1)}) fusion(bf16[4,128,8192]{2,1,0:T(8,128)(2,1)} %param.9), kind=kLoop, calls=%fused_computation.3 | loop fusion | bytes 16777216 | tf_op jit(solution)/shard_map/slice | solution.py:213
  226.9 13.9 %collective-permute-done.5 = bf16[1024,512]{1,0:T(8,128)(2,1)S(1)} collective-permute-done((bf16[1024,512]{1,0:T(8,128)(2,1)S(1)}, bf16[1024,512]{1,0:T(8,128)(2,1)S(1)}, u32[]{:S(2)}, u32[]{:S(2)}) %collective-permute-start.5) | collective-permute-done | bytes 1048608 | tf_op jit(solution)/shard_map/ppermute | solution.py:202
  241.8 5.0 collective-permute-start.12
  246.8 17.9 %collective-permute-done.8 = bf16[2048,512]{1,0:T(8,128)(2,1)} collective-permute-done((bf16[2048,512]{1,0:T(8,128)(2,1)}, bf16[2048,512]{1,0:T(8,128)(2,1)}, u32[]{:S(2)}, u32[]{:S(2)}) %collective-permute-start.8) | collective-permute-done | bytes 2097184 | tf_op jit(solution)/shard_map/ppermute | solution.py:203
  264.7 3.9 collective-permute-start.16
  268.6 3.1 constant_dynamic-update-slice_fusion.4
  271.7 1.5 collective-permute-start.10
  273.7 3.1 constant_dynamic-update-slice_fusion.3
  276.8 3.0 constant_dynamic-update-slice_fusion.9
  279.9 1.6 constant_dynamic-update-slice_fusion.8
  281.4 3.1 constant_dynamic-update-slice_fusion.2
  284.5 13.3 %collective-permute-done.10 = bf16[1024,512]{1,0:T(8,128)(2,1)S(1)} collective-permute-done((bf16[1024,512]{1,0:T(8,128)(2,1)S(1)}, bf16[1024,512]{1,0:T(8,128)(2,1)S(1)}, u32[]{:S(2)}, u32[]{:S(2)}) %collective-permute-start.10) | collective-permute-done | bytes 1048608 | tf_op jit(solution)/shard_map/ppermute | solution.py:203
  297.8 18.3 %collective-permute-done.9 = bf16[1024,512]{1,0:T(8,128)(2,1)S(1)} collective-permute-done((bf16[1024,512]{1,0:T(8,128)(2,1)S(1)}, bf16[1024,512]{1,0:T(8,128)(2,1)S(1)}, u32[]{:S(2)}, u32[]{:S(2)}) %collective-permute-start.9) | collective-permute-done | bytes 1048608 | tf_op jit(solution)/shard_map/ppermute | solution.py:203
  316.1 3.1 collective-permute-start.20
  321.4 3.0 constant_dynamic-update-slice_fusion.7
  326.5 15.7 %shard_map.96 = bf16[512,1024]{1,0:T(8,128)(2,1)} custom-call(s32[2]{0:T(128)} %pad_add_fusion.refs_0_, bf16[512,8192]{1,0:T(8,128)(2,1)} %bitcast.123, bf16[8192,512]{1,0:T(8,128)(2,1)} %constant_dynamic-update-slice_fusion.refs_2_.refs_5_.refs_4_, bf16[8192,512]{1,0:T(8,128)(2,1)} %constant_dynamic-update-slice_fusion.5.refs_3_.refs_6_.refs_5_), custom_call_target="tpu_custom_call" | custom-call | flops 536870912 | bytes 1572864 | tf_op jit(solution)/shard_map/pallas_call | solution.py:148
  342.2 1.3 copy-done.6
  343.5 18.8 %shard_map.97 = bf16[256,2048]{1,0:T(8,128)(2,1)} custom-call(s32[2]{0:T(128)} %pad_add_fusion.refs_0_, bf16[128,8192]{1,0:T(8,128)(2,1)} %copy-done.5, bf16[128,8192]{1,0:T(8,128)(2,1)} %copy-done.6, bf16[256,8192]{1,0:T(8,128)(2,1)} %collective-permute-done.3.refs_3_, bf16[8192,1024]{1,0:T(8,128)(2,1)} %refs_3_.3, ...), custom_call_target="tpu_custom_call" | custom-call | flops 536870912 | bytes 2359296 | tf_op jit(solution)/shard_map/pallas_call | solution.py:148
  363.6 1.6 collective-permute-start.19
  366.2 1.6 collective-permute-start.15
  367.8 4.0 collective-permute-done.19
  371.8 1.3 collective-permute-start.14
  373.2 5.3 %collective-permute-done.18 = bf16[2,32,2048]{2,1,0:T(8,128)(2,1)S(1)} collective-permute-done((bf16[2,32,2048]{2,1,0:T(8,128)(2,1)S(1)}, bf16[2,32,2048]{2,1,0:T(8,128)(2,1)S(1)}, u32[]{:S(2)}, u32[]{:S(2)}) %collective-permute-start.18) | collective-permute-done | bytes 262176 | tf_op jit(solution)/shard_map/ppermute | solution.py:230
  378.4 4.7 collective-permute-start.27
  384.2 15.2 %shard_map.98 = bf16[128,2048]{1,0:T(8,128)(2,1)} custom-call(s32[2]{0:T(128)} %pad_add_fusion.refs_0_, bf16[128,8192]{1,0:T(8,128)(2,1)} %collective-permute-done.20.refs_1_, bf16[256,8192]{1,0:T(8,128)(2,1)} %collective-permute-done.11.refs_2_, bf16[8192,1024]{1,0:T(8,128)(2,1)} %refs_3_.3, ...), custom_call_target="tpu_custom_call" | custom-call | flops 268435456 | bytes 2228224 | tf_op jit(solution)/shard_map/pallas_call | solution.py:148
  400.6 1.6 collective-permute-start.23
  403.1 2.9 collective-permute-done.23
  406.0 3.2 collective-permute-done.22
  410.4 1.6 collective-permute-start.24
  411.9 10.6 %collective-permute-done.24 = bf16[224,1024]{1,0:T(8,128)(2,1)S(1)} collective-permute-done((bf16[224,1024]{1,0:T(8,128)(2,1)S(1)}, bf16[224,1024]{1,0:T(8,128)(2,1)S(1)}, u32[]{:S(2)}, u32[]{:S(2)}) %collective-permute-start.24) | collective-permute-done | bytes 458784 | tf_op jit(solution)/shard_map/ppermute | solution.py:230
  422.8 8.2 %collective-permute-done.27.refs_1_ = bf16[128,8192]{1,0:T(8,128)(2,1)} collective-permute-done((bf16[128,8192]{1,0:T(8,128)(2,1)}, bf16[128,8192]{1,0:T(8,128)(2,1)}, u32[]{:S(2)}, u32[]{:S(2)}) %collective-permute-start.27) | collective-permute-done | bytes 2097184 | tf_op jit(solution)/shard_map/ppermute | solution.py:214
  431.0 15.2 %shard_map.99 = bf16[128,2048]{1,0:T(8,128)(2,1)} custom-call(s32[2]{0:T(128)} %pad_add_fusion.refs_0_, bf16[128,8192]{1,0:T(8,128)(2,1)} %collective-permute-done.27.refs_1_, bf16[256,8192]{1,0:T(8,128)(2,1)} %collective-permute-done.11.refs_2_, bf16[8192,1024]{1,0:T(8,128)(2,1)} %refs_3_.3, ...), custom_call_target="tpu_custom_call" | custom-call | flops 268435456 | bytes 2228224 | tf_op jit(solution)/shard_map/pallas_call | solution.py:148
  446.2 7.3 %collective-permute-done.26 = bf16[224,1024]{1,0:T(8,128)(2,1)S(1)} collective-permute-done((bf16[224,1024]{1,0:T(8,128)(2,1)S(1)}, bf16[224,1024]{1,0:T(8,128)(2,1)S(1)}, u32[]{:S(2)}, u32[]{:S(2)}) %collective-permute-start.26) | collective-permute-done | bytes 458784 | tf_op jit(solution)/shard_map/ppermute | solution.py:230
  454.7 1.6 collective-permute-start.30
  456.8 3.3 collective-permute-done.30
  460.1 3.2 collective-permute-done.29
  464.4 1.6 collective-permute-start.31
  466.0 2.7 collective-permute-done.32
  468.7 1.6 collective-permute-start.34
  470.2 1.3 constant_dynamic-slice_fusion.3
  471.7 6.2 %collective-permute-done.31 = bf16[224,1024]{1,0:T(8,128)(2,1)S(1)} collective-permute-done((bf16[224,1024]{1,0:T(8,128)(2,1)S(1)}, bf16[224,1024]{1,0:T(8,128)(2,1)S(1)}, u32[]{:S(2)}, u32[]{:S(2)}) %collective-permute-start.31) | collective-permute-done | bytes 458784 | tf_op jit(solution)/shard_map/ppermute | solution.py:230
  479.5 1.4 collective-permute-done.35.refs_5_
  480.9 4.4 shard_map.100
  485.5 1.2 collective-permute-start.38
  488.5 1.8 collective-permute-done.37
  490.4 3.2 collective-permute-start.41
  495.8 2.2 collective-permute-done.40
  (105 shorter events, 23.4 us)
Async XLA Ops:
  7.2 457.1 %all-gather.3.cloned.1.call-start = ((), (), s32[]{:S(2)}) async-start(), calls=%async_computation | async-start | bytes 1310720 | tf_op jit(solution)/shard_map/all_gather | solution.py:218
  7.2 8.7 %copy-start.2 = (bf16[4,128,8192]{2,1,0:T(8,128)(2,1)S(1)}, bf16[4,128,8192]{2,1,0:T(8,128)(2,1)}, u32[]{:S(2)}) copy-start(bf16[4,128,8192]{2,1,0:T(8,128)(2,1)} %param.9) | copy-start | bytes 25165828
  12.8 112.5 %collective-permute-start.1 = (bf16[2048,512]{1,0:T(8,128)(2,1)}, bf16[2048,512]{1,0:T(8,128)(2,1)}, u32[]{:S(2)}, u32[]{:S(2)}) collective-permute-start(bf16[2048,512]{1,0:T(8,128)(2,1)} %get-tuple-element.43), channel_id=1, source_target_pairs={{0,4},{4,0},{8,12},{12,8},{1,5},{5,1},{9,13},{13,9},{2,6},{6,2},{1... | collective-permute-start | bytes 6291464 | tf_op jit(solution)/shard_map/ppermute | solution.py:202
  15.8 7.2 %copy-start.11 = (s32[2048]{0:T(1024)S(1)}, s32[2048]{0:T(1024)}, u32[]{:S(2)}) copy-start(s32[2048]{0:T(1024)} %param.15) | copy-start | bytes 24580
  15.8 7.2 %copy-start.12 = (s32[4]{0:T(128)S(1)}, s32[4]{0:T(128)}, u32[]{:S(2)}) copy-start(s32[4]{0:T(128)} %param.14) | copy-start | bytes 52
  15.8 90.9 %collective-permute-start = (bf16[2048,512]{1,0:T(8,128)(2,1)}, bf16[2048,512]{1,0:T(8,128)(2,1)}, u32[]{:S(2)}, u32[]{:S(2)}) collective-permute-start(bf16[2048,512]{1,0:T(8,128)(2,1)} %get-tuple-element.44), channel_id=1, source_target_pairs={{0,4},{4,0},{8,12},{12,8},{1,5},{5,1},{9,13},{13,9},{2,6},{6,2},{1... | collective-permute-start | bytes 6291464 | tf_op jit(solution)/shard_map/ppermute | solution.py:202
  19.7 197.7 %collective-permute-start.3 = (bf16[256,8192]{1,0:T(8,128)(2,1)}, bf16[256,8192]{1,0:T(8,128)(2,1)}, u32[]{:S(2)}, u32[]{:S(2)}) collective-permute-start(bf16[256,8192]{1,0:T(8,128)(2,1)} %bitcast.4), channel_id=1, source_target_pairs={{4,8},{8,4},{5,9},{9,5},{6,10},{10,6},{7,11},{11,7},{20,24},{24,20... | collective-permute-start | bytes 12582920 | tf_op jit(solution)/shard_map/ppermute | solution.py:201
  106.7 134.1 %collective-permute-start.11 = (bf16[256,8192]{1,0:T(8,128)(2,1)}, bf16[256,8192]{1,0:T(8,128)(2,1)}, u32[]{:S(2)}, u32[]{:S(2)}) collective-permute-start(bf16[256,8192]{1,0:T(8,128)(2,1)} %bitcast.128), channel_id=1, source_target_pairs={{4,8},{8,4},{5,9},{9,5},{6,10},{10,6},{7,11},{11,7},{20,24},{24,20... | collective-permute-start | bytes 12582920 | tf_op jit(solution)/shard_map/ppermute | solution.py:201
  125.3 48.8 %collective-permute-start.6 = (bf16[2048,512]{1,0:T(8,128)(2,1)}, bf16[2048,512]{1,0:T(8,128)(2,1)S(1)}, u32[]{:S(2)}, u32[]{:S(2)}) collective-permute-start(bf16[2048,512]{1,0:T(8,128)(2,1)} %collective-permute-done.1), channel_id=1, source_target_pairs={{0,16},{16,0},{1,17},{17,1},{2,18},{18,2},{3,19},{19,3},{4,20},{20... | collective-permute-start | bytes 6291464 | tf_op jit(solution)/shard_map/ppermute | solution.py:203
  127.0 47.1 %collective-permute-start.2 = (bf16[2048,512]{1,0:T(8,128)(2,1)S(1)}, bf16[2048,512]{1,0:T(8,128)(2,1)}, u32[]{:S(2)}, u32[]{:S(2)}) collective-permute-start(bf16[2048,512]{1,0:T(8,128)(2,1)S(1)} %get-tuple-element.22), channel_id=1, source_target_pairs={{0,4},{4,0},{8,12},{12,8},{1,5},{5,1},{9,13},{13,9},{2,6},{6,2},{1... | collective-permute-start | bytes 6291464 | tf_op jit(solution)/shard_map/ppermute | solution.py:202
  129.4 88.0 %collective-permute-start.4 = (bf16[2048,512]{1,0:T(8,128)(2,1)}, bf16[2048,512]{1,0:T(8,128)(2,1)}, u32[]{:S(2)}, u32[]{:S(2)}) collective-permute-start(bf16[2048,512]{1,0:T(8,128)(2,1)} %collective-permute-done), channel_id=1, source_target_pairs={{0,16},{16,0},{1,17},{17,1},{2,18},{18,2},{3,19},{19,3},{4,20},{20... | collective-permute-start | bytes 6291464 | tf_op jit(solution)/shard_map/ppermute | solution.py:203
  174.1 1.4 copy-start.7
  175.4 51.5 %collective-permute-start.7 = (bf16[1024,512]{1,0:T(8,128)(2,1)S(1)}, bf16[1024,512]{1,0:T(8,128)(2,1)S(1)}, u32[]{:S(2)}, u32[]{:S(2)}) collective-permute-start(bf16[1024,512]{1,0:T(8,128)(2,1)S(1)} %get-tuple-element.24), channel_id=1, source_target_pairs={{0,4},{4,0},{8,12},{12,8},{1,5},{5,1},{9,13},{13,9},{2,6},{6,2},{1... | collective-permute-start | bytes 3145736 | tf_op jit(solution)/shard_map/ppermute | solution.py:202
  217.4 23.4 %collective-permute-start.5 = (bf16[1024,512]{1,0:T(8,128)(2,1)S(1)}, bf16[1024,512]{1,0:T(8,128)(2,1)S(1)}, u32[]{:S(2)}, u32[]{:S(2)}) collective-permute-start(bf16[1024,512]{1,0:T(8,128)(2,1)S(1)} %get-tuple-element.23), channel_id=1, source_target_pairs={{0,4},{4,0},{8,12},{12,8},{1,5},{5,1},{9,13},{13,9},{2,6},{6,2},{1... | collective-permute-start | bytes 3145736 | tf_op jit(solution)/shard_map/ppermute | solution.py:202
  219.4 45.3 %collective-permute-start.8 = (bf16[2048,512]{1,0:T(8,128)(2,1)}, bf16[2048,512]{1,0:T(8,128)(2,1)}, u32[]{:S(2)}, u32[]{:S(2)}) collective-permute-start(bf16[2048,512]{1,0:T(8,128)(2,1)} %collective-permute-done.2), channel_id=1, source_target_pairs={{0,16},{16,0},{1,17},{17,1},{2,18},{18,2},{3,19},{19,3},{4,20},{20... | collective-permute-start | bytes 6291464 | tf_op jit(solution)/shard_map/ppermute | solution.py:203
  240.8 1.0 copy-start.9
  241.8 74.3 %collective-permute-start.12 = (bf16[128,8192]{1,0:T(8,128)(2,1)}, bf16[128,8192]{1,0:T(8,128)(2,1)S(1)}, u32[]{:S(2)}, u32[]{:S(2)}) collective-permute-start(bf16[128,8192]{1,0:T(8,128)(2,1)} %get-tuple-element.26), channel_id=1, source_target_pairs={{0,12},{12,0},{1,13},{13,1},{2,14},{14,2},{3,15},{15,3},{16,28},{2... | collective-permute-start | bytes 6291464 | tf_op jit(solution)/shard_map/ppermute | solution.py:214
  246.8 26.4 %copy-start.10 = (bf16[1024,512]{1,0:T(8,128)(2,1)S(1)}, bf16[1024,512]{1,0:T(8,128)(2,1)}, u32[]{:S(2)}) copy-start(bf16[1024,512]{1,0:T(8,128)(2,1)} %copy-done.9) | copy-start | bytes 3145732
  264.7 77.5 %collective-permute-start.16 = (bf16[128,8192]{1,0:T(8,128)(2,1)}, bf16[128,8192]{1,0:T(8,128)(2,1)S(1)}, u32[]{:S(2)}, u32[]{:S(2)}) collective-permute-start(bf16[128,8192]{1,0:T(8,128)(2,1)} %get-tuple-element.28), channel_id=1, source_target_pairs={{0,12},{12,0},{1,13},{13,1},{2,14},{14,2},{3,15},{15,3},{16,28},{2... | collective-permute-start | bytes 6291464 | tf_op jit(solution)/shard_map/ppermute | solution.py:214
  271.7 8.2 %copy-start.8 = (bf16[2048,512]{1,0:T(8,128)(2,1)S(1)}, bf16[2048,512]{1,0:T(8,128)(2,1)}, u32[]{:S(2)}) copy-start(bf16[2048,512]{1,0:T(8,128)(2,1)} %copy-done.7) | copy-start | bytes 6291460
  271.7 26.1 %collective-permute-start.10 = (bf16[1024,512]{1,0:T(8,128)(2,1)S(1)}, bf16[1024,512]{1,0:T(8,128)(2,1)S(1)}, u32[]{:S(2)}, u32[]{:S(2)}) collective-permute-start(bf16[1024,512]{1,0:T(8,128)(2,1)S(1)} %collective-permute-done.7), channel_id=1, source_target_pairs={{0,16},{16,0},{1,17},{17,1},{2,18},{18,2},{3,19},{19,3},{4,20},{20... | collective-permute-start | bytes 3145736 | tf_op jit(solution)/shard_map/ppermute | solution.py:203
  273.2 42.9 %collective-permute-start.9 = (bf16[1024,512]{1,0:T(8,128)(2,1)S(1)}, bf16[1024,512]{1,0:T(8,128)(2,1)S(1)}, u32[]{:S(2)}, u32[]{:S(2)}) collective-permute-start(bf16[1024,512]{1,0:T(8,128)(2,1)S(1)} %copy-done.10), channel_id=1, source_target_pairs={{0,16},{16,0},{1,17},{17,1},{2,18},{18,2},{3,19},{19,3},{4,20},{20... | collective-permute-start | bytes 3145736 | tf_op jit(solution)/shard_map/ppermute | solution.py:203
  316.1 8.4 %copy-start.5 = (bf16[128,8192]{1,0:T(8,128)(2,1)}, bf16[128,8192]{1,0:T(8,128)(2,1)S(1)}, u32[]{:S(2)}) copy-start(bf16[128,8192]{1,0:T(8,128)(2,1)S(1)} %collective-permute-done.12.refs_1_) | copy-start | bytes 6291460
  316.1 68.1 %collective-permute-start.20 = (bf16[128,8192]{1,0:T(8,128)(2,1)}, bf16[128,8192]{1,0:T(8,128)(2,1)}, u32[]{:S(2)}, u32[]{:S(2)}) collective-permute-start(bf16[128,8192]{1,0:T(8,128)(2,1)} %get-tuple-element.30), channel_id=1, source_target_pairs={{0,12},{12,0},{1,13},{13,1},{2,14},{14,2},{3,15},{15,3},{16,28},{2... | collective-permute-start | bytes 6291464 | tf_op jit(solution)/shard_map/ppermute | solution.py:214
  342.2 23.5 %copy-start.3 = (bf16[512,1024]{1,0:T(8,128)(2,1)S(1)}, bf16[512,1024]{1,0:T(8,128)(2,1)}, u32[]{:S(2)}) copy-start(bf16[512,1024]{1,0:T(8,128)(2,1)} %shard_map.95) | copy-start | bytes 3145732
  342.2 23.5 %copy-start.4 = (bf16[512,1024]{1,0:T(8,128)(2,1)S(1)}, bf16[512,1024]{1,0:T(8,128)(2,1)}, u32[]{:S(2)}) copy-start(bf16[512,1024]{1,0:T(8,128)(2,1)} %shard_map.96) | copy-start | bytes 3145732
  342.2 1.3 copy-start.6
  363.5 2.7 collective-permute-start.17
  363.6 8.2 %collective-permute-start.19 = (bf16[2,32,2048]{2,1,0:T(8,128)(2,1)S(1)}, bf16[2,32,2048]{2,1,0:T(8,128)(2,1)S(1)}, u32[]{:S(2)}, u32[]{:S(2)}) collective-permute-start(bf16[2,32,2048]{2,1,0:T(8,128)(2,1)S(1)} %get-tuple-element.61), channel_id=1, source_target_pairs={{0,3},{1,2},{2,1},{3,0},{4,7},{5,6},{6,5},{7,4},{8,11},{9,10},{10,... | collective-permute-start | bytes 786440 | tf_op jit(solution)/shard_map/ppermute | solution.py:230
  365.2 13.2 %collective-permute-start.18 = (bf16[2,32,2048]{2,1,0:T(8,128)(2,1)S(1)}, bf16[2,32,2048]{2,1,0:T(8,128)(2,1)S(1)}, u32[]{:S(2)}, u32[]{:S(2)}) collective-permute-start(bf16[2,32,2048]{2,1,0:T(8,128)(2,1)S(1)} %get-tuple-element.62), channel_id=1, source_target_pairs={{0,2},{1,3},{2,0},{3,1},{4,6},{5,7},{6,4},{7,5},{8,10},{9,11},{10,... | collective-permute-start | bytes 786440 | tf_op jit(solution)/shard_map/ppermute | solution.py:230
  366.1 34.5 %collective-permute-start.13 = (bf16[4,32,2048]{2,1,0:T(8,128)(2,1)S(1)}, bf16[4,32,2048]{2,1,0:T(8,128)(2,1)S(1)}, u32[]{:S(2)}, u32[]{:S(2)}) collective-permute-start(bf16[4,32,2048]{2,1,0:T(8,128)(2,1)S(1)} %get-tuple-element.53), channel_id=1, source_target_pairs={{0,1},{1,0},{2,3},{3,2},{4,5},{5,4},{6,7},{7,6},{8,9},{9,8},{10,11... | collective-permute-start | bytes 1572872 | tf_op jit(solution)/shard_map/ppermute | solution.py:230
  366.2 36.0 %collective-permute-start.15 = (bf16[4,32,2048]{2,1,0:T(8,128)(2,1)S(1)}, bf16[4,32,2048]{2,1,0:T(8,128)(2,1)S(1)}, u32[]{:S(2)}, u32[]{:S(2)}) collective-permute-start(bf16[4,32,2048]{2,1,0:T(8,128)(2,1)S(1)} %get-tuple-element.54), channel_id=1, source_target_pairs={{0,3},{1,2},{2,1},{3,0},{4,7},{5,6},{6,5},{7,4},{8,11},{9,10},{10,... | collective-permute-start | bytes 1572872 | tf_op jit(solution)/shard_map/ppermute | solution.py:230
  371.8 30.9 %collective-permute-start.14 = (bf16[4,32,2048]{2,1,0:T(8,128)(2,1)S(1)}, bf16[4,32,2048]{2,1,0:T(8,128)(2,1)S(1)}, u32[]{:S(2)}, u32[]{:S(2)}) collective-permute-start(bf16[4,32,2048]{2,1,0:T(8,128)(2,1)S(1)} %get-tuple-element.55), channel_id=1, source_target_pairs={{0,2},{1,3},{2,0},{3,1},{4,6},{5,7},{6,4},{7,5},{8,10},{9,11},{10,... | collective-permute-start | bytes 1572872 | tf_op jit(solution)/shard_map/ppermute | solution.py:230
  378.4 52.6 %collective-permute-start.27 = (bf16[128,8192]{1,0:T(8,128)(2,1)}, bf16[128,8192]{1,0:T(8,128)(2,1)}, u32[]{:S(2)}, u32[]{:S(2)}) collective-permute-start(bf16[128,8192]{1,0:T(8,128)(2,1)} %get-tuple-element.32), channel_id=1, source_target_pairs={{0,12},{12,0},{1,13},{13,1},{2,14},{14,2},{3,15},{15,3},{16,28},{2... | collective-permute-start | bytes 6291464 | tf_op jit(solution)/shard_map/ppermute | solution.py:214
  400.5 2.6 collective-permute-start.21
  400.6 5.4 %collective-permute-start.23 = (bf16[1,32,2048]{2,1,0:T(8,128)(2,1)S(1)}, bf16[1,32,2048]{2,1,0:T(8,128)(2,1)S(1)}, u32[]{:S(2)}, u32[]{:S(2)}) collective-permute-start(bf16[1,32,2048]{2,1,0:T(8,128)(2,1)S(1)} %get-tuple-element.69), channel_id=1, source_target_pairs={{0,3},{1,2},{2,1},{3,0},{4,7},{5,6},{6,5},{7,4},{8,11},{9,10},{10,... | collective-permute-start | bytes 393224 | tf_op jit(solution)/shard_map/ppermute | solution.py:230
  402.2 7.1 %collective-permute-start.22 = (bf16[1,32,2048]{2,1,0:T(8,128)(2,1)S(1)}, bf16[1,32,2048]{2,1,0:T(8,128)(2,1)S(1)}, u32[]{:S(2)}, u32[]{:S(2)}) collective-permute-start(bf16[1,32,2048]{2,1,0:T(8,128)(2,1)S(1)} %get-tuple-element.70), channel_id=1, source_target_pairs={{0,2},{1,3},{2,0},{3,1},{4,6},{5,7},{6,4},{7,5},{8,10},{9,11},{10,... | collective-permute-start | bytes 393224 | tf_op jit(solution)/shard_map/ppermute | solution.py:230
  410.4 12.1 %collective-permute-start.24 = (bf16[224,1024]{1,0:T(8,128)(2,1)S(1)}, bf16[224,1024]{1,0:T(8,128)(2,1)S(1)}, u32[]{:S(2)}, u32[]{:S(2)}) collective-permute-start(bf16[224,1024]{1,0:T(8,128)(2,1)S(1)} %get-tuple-element.64), channel_id=1, source_target_pairs={{0,2},{1,3},{2,0},{3,1},{4,6},{5,7},{6,4},{7,5},{8,10},{9,11},{10,... | collective-permute-start | bytes 1376264 | tf_op jit(solution)/shard_map/ppermute | solution.py:230
  422.6 30.9 %collective-permute-start.25 = (bf16[448,1024]{1,0:T(8,128)(2,1)S(1)}, bf16[448,1024]{1,0:T(8,128)(2,1)S(1)}, u32[]{:S(2)}, u32[]{:S(2)}) collective-permute-start(bf16[448,1024]{1,0:T(8,128)(2,1)S(1)} %pad_maximum_fusion.3.refs_0_), channel_id=1, source_target_pairs={{0,1},{1,0},{2,3},{3,2},{4,5},{5,4},{6,7},{7,6},{8,9},{9,8},{10,11... | collective-permute-start | bytes 2752520 | tf_op jit(solution)/shard_map/ppermute | solution.py:230
  422.7 30.8 %collective-permute-start.26 = (bf16[224,1024]{1,0:T(8,128)(2,1)S(1)}, bf16[224,1024]{1,0:T(8,128)(2,1)S(1)}, u32[]{:S(2)}, u32[]{:S(2)}) collective-permute-start(bf16[224,1024]{1,0:T(8,128)(2,1)S(1)} %get-tuple-element.63), channel_id=1, source_target_pairs={{0,4},{4,0},{8,12},{12,8},{1,5},{5,1},{9,13},{13,9},{2,6},{6,2},{1... | collective-permute-start | bytes 1376264 | tf_op jit(solution)/shard_map/ppermute | solution.py:230
  454.6 2.2 collective-permute-start.28
  454.7 5.4 %collective-permute-start.30 = (bf16[1,32,2048]{2,1,0:T(8,128)(2,1)S(1)}, bf16[1,32,2048]{2,1,0:T(8,128)(2,1)S(1)}, u32[]{:S(2)}, u32[]{:S(2)}) collective-permute-start(bf16[1,32,2048]{2,1,0:T(8,128)(2,1)S(1)} %get-tuple-element.66), channel_id=1, source_target_pairs={{0,3},{1,2},{2,1},{3,0},{4,7},{5,6},{6,5},{7,4},{8,11},{9,10},{10,... | collective-permute-start | bytes 393224 | tf_op jit(solution)/shard_map/ppermute | solution.py:230
  456.2 7.1 %collective-permute-start.29 = (bf16[1,32,2048]{2,1,0:T(8,128)(2,1)S(1)}, bf16[1,32,2048]{2,1,0:T(8,128)(2,1)S(1)}, u32[]{:S(2)}, u32[]{:S(2)}) collective-permute-start(bf16[1,32,2048]{2,1,0:T(8,128)(2,1)S(1)} %get-tuple-element.67), channel_id=1, source_target_pairs={{0,2},{1,3},{2,0},{3,1},{4,6},{5,7},{6,4},{7,5},{8,10},{9,11},{10,... | collective-permute-start | bytes 393224 | tf_op jit(solution)/shard_map/ppermute | solution.py:230
  464.3 4.3 collective-permute-start.32
  464.4 13.4 %collective-permute-start.31 = (bf16[224,1024]{1,0:T(8,128)(2,1)S(1)}, bf16[224,1024]{1,0:T(8,128)(2,1)S(1)}, u32[]{:S(2)}, u32[]{:S(2)}) collective-permute-start(bf16[224,1024]{1,0:T(8,128)(2,1)S(1)} %collective-permute-done.26), channel_id=1, source_target_pairs={{0,2},{1,3},{2,0},{3,1},{4,6},{5,7},{6,4},{7,5},{8,10},{9,11},{10,... | collective-permute-start | bytes 1376264 | tf_op jit(solution)/shard_map/ppermute | solution.py:230
  468.7 10.6 %collective-permute-start.34 = (bf16[64,1024]{1,0:T(8,128)(2,1)S(1)}, bf16[64,1024]{1,0:T(8,128)(2,1)S(1)}, u32[]{:S(2)}, u32[]{:S(2)}) collective-permute-start(bf16[64,1024]{1,0:T(8,128)(2,1)S(1)} %pad_maximum_fusion.7), channel_id=1, source_target_pairs={{0,2},{1,3},{2,0},{3,1},{4,6},{5,7},{6,4},{7,5},{8,10},{9,11},{10,... | collective-permute-start | bytes 393224 | tf_op jit(solution)/shard_map/ppermute | solution.py:230
  471.6 9.3 %copy-start = (bf16[4,1024,256]{2,1,0:T(8,128)(2,1)S(1)}, bf16[4,1024,256]{2,1,0:T(8,128)(2,1)}, u32[]{:S(2)}) copy-start(bf16[4,1024,256]{2,1,0:T(8,128)(2,1)} %refs_8_.1) | copy-start | bytes 6291460
  471.6 9.3 %copy-start.1 = (f32[1024,256]{1,0:T(8,128)S(1)}, f32[1024,256]{1,0:T(8,128)}, u32[]{:S(2)}) copy-start(f32[1024,256]{1,0:T(8,128)} %refs_7_.1) | copy-start | bytes 3145732
  477.9 3.0 collective-permute-start.33
  479.3 1.6 collective-permute-start.35
  485.5 3.0 collective-permute-start.38
  486.8 3.6 collective-permute-start.37
  487.3 3.1 collective-permute-start.36
  490.4 5.4 %collective-permute-start.41 = (f32[4,4]{1,0:T(4,128)S(1)}, f32[4,4]{1,0:T(4,128)S(1)}, u32[]{:S(2)}, u32[]{:S(2)}) collective-permute-start(f32[4,4]{1,0:T(4,128)S(1)} %add_add_fusion.1), channel_id=1, source_target_pairs={{0,12},{4,8},{8,4},{12,0},{1,13},{5,9},{9,5},{13,1},{2,14},{6,10},... | collective-permute-start | bytes 200 | tf_op jit(solution)/shard_map/ppermute | solution.py:173
  493.5 4.5 collective-permute-start.40
  493.8 4.2 collective-permute-start.39
Sparse Core Ops, SparseCore 0:
  422.8 33.1 all-gather.2

commit v13 on v12

--- a/solution.py
+++ b/solution.py
@@ -189,12 +189,12 @@
     lengths = candidate_lengths(example_ids, token_counts)
     local_act = local_activations(acts, act_basis, lengths)
     near, far, other = [], [], []
-    spans = [(0, 2), (2, 4), (4, 6), (6, 7), (7, units)]
+    spans = [(0, 1), (1, 3), (3, 5), (5, 7), (7, units)]
     own_own = project(flags, [(flat, 0, cands * tok)], [], [grad_basis])
     for i, (a, b) in enumerate(spans):
         piece = lax.dynamic_slice(grad_basis, (a * deep, group * half), ((b - a) * deep, half))
         if i >= 2:
-            early = {2: [own_own, local_act], 3: [other[0], far[0]], 4: [far[1]]}[i]
+            early = {2: [own_own, local_act], 3: [other[0]], 4: []}[i]
             piece = after(piece, near[i - 2], *early)
         if i in (0, 2):
             part = flat[: 4 * slab] if i == 0 else after(flat[4 * slab :], near[0])
@@ -206,7 +206,7 @@
 
     ranges = [(0, 2), (2, 4), (4, 6), (6, units)]
     phase = [near[3], near[4], other[1]]
-    ties = [[*phase, far[0]], [*phase, far[2]], [far[3], far[4]], []]
+    ties = [[*phase, far[0], far[1]], [*phase, far[2]], [far[4]], []]
     partner = []
     for k, (a, b) in enumerate(ranges):
         tie = ties[k] + ([partner[k - 2]] if k >= 2 else [])

time: 506 us -> 471 us (0.931)
  waiting for transfers between devices: 287 us -> 233 us
  starting transfers between devices: 59 us -> 73.1 us
    ppermute x5, waiting for transfers between devices: 131 us -> 49.1 us  [chain_body(): far.append(lax.ppermute(near[i], 'groups', [(0, 1), (1, 0)]))]
    ppermute x5, waiting for transfers between devices: 89.7 us -> 115 us  [chain_body(): near.append(lax.ppermute(piece, 'row', beside))]
    ppermute x5, starting transfers between devices: 10.1 us -> 26.4 us  [chain_body(): near.append(lax.ppermute(piece, 'row', beside))]
    unnamed x35 -> x37, local copies, waits for them, and re-layouts: 22.7 us -> 24.3 us
  transfers between devices with their start and end apart: 43 -> 43, of which waited for: 24 -> 22; matrix products, arithmetic and copies ran while one was open for 10% -> 12% of each run, Pallas kernels for 16% -> 17%
where the time goes in v13:
time: 471 us
  waiting for transfers between devices  233 us (49%)
  Pallas kernels  85.4 us (18%)
  starting transfers between devices  73.1 us (16%)
  local copies, waits for them, and re-layouts  51.7 us (11%)
  between operations  14.4 us (3%)
  matrix products  7.6 us (2%)
  other arithmetic  5.62 us (1%)
    ppermute x5, waiting for transfers between devices, chain_body(): near.append(lax.ppermute(piece, 'row', beside))  115 us
    pallas_call x5, Pallas kernels, project(): pl.pallas_call(functools.partial(project_kernel, len(ends), len(tokens),...  81 us
    ppermute x20, waiting for transfers between devices, swap(): return lax.ppermute(value, axis, [(i, i ^ d) for i in range(size)])  55.8 us
    ppermute x5, waiting for transfers between devices, chain_body(): far.append(lax.ppermute(near[i], 'groups', [(0, 1), (1, 0)]))  49.1 us
    ppermute x5, starting transfers between devices, chain_body(): near.append(lax.ppermute(piece, 'row', beside))  26.4 us
    unnamed x37, local copies, waits for them, and re-layouts  24.3 us
    ppermute x4, starting transfers between devices, chain_body(): partner.append(lax.ppermute(after(piece, *tie), 'row', ends))  15.4 us
    ppermute x20, starting transfers between devices, swap(): return lax.ppermute(value, axis, [(i, i ^ d) for i in range(size)])  12.5 us
  transfers between devices with their start and end apart: 43, of which 22 were waited for; matrix products, arithmetic and copies ran while one was open for 12% of the time, Pallas kernels for 17%

profile of v13, /device:TPU:0, one launch (start us, length us, event | category | flops | bytes accessed | tf_op | source)
XLA Modules:
  0.0 470.6 jit_solution(11659480761784456380)
XLA Ops:
  7.2 6.0 %fusion.22 = (bf16[2,128,8192]{2,1,0:T(8,128)(2,1)}, bf16[2,128,8192]{2,1,0:T(8,128)(2,1)}) fusion(bf16[4,128,8192]{2,1,0:T(8,128)(2,1)} %param.9), kind=kLoop, calls=%fused_computation.94 | loop fusion | bytes 16777216 | tf_op jit(solution)/shard_map/slice | solution.py:200
  13.2 2.7 collective-permute-start.3
  15.9 2.7 constant_dynamic-slice_fusion.4
  18.6 3.8 collective-permute-start
  22.4 5.5 %constant_dynamic-slice_fusion.8 = (bf16[2048,512]{1,0:T(8,128)(2,1)}, bf16[2048,512]{1,0:T(8,128)(2,1)S(1)}, bf16[2048,512]{1,0:T(8,128)(2,1)}) fusion(bf16[8192,1024]{1,0:T(8,128)(2,1)} %refs_3_.3, s32[]{:T(128)S(6)} %select_n.68), kind=kLoop, calls=%fused_computation.93 | loop fusion | bytes 12582916 | tf_op jit(solution)/shard_map/dynamic_slice | solution.py:195
  28.8 7.6 %fusion.5 = bf16[4,128,256]{2,1,0:T(8,128)(2,1)} fusion(bf16[4,128,8192]{2,1,0:T(8,128)(2,1)} %param.8, bf16[8192,256]{1,0:T(8,128)(2,1)} %param.10, f32[4,128]{1,0:T(4,128)S(1)} %compare_convert_fusion), kind=kOutput, calls=%fused_computation.8 | convolution fusion | flops 2147745792 | bytes 12847104 | tf_op jit(solution)/shard_map/ctd,dk->ctk/dot_general | solution.py:25
  36.4 10.4 %collective-permute-done = bf16[1024,512]{1,0:T(8,128)(2,1)} collective-permute-done((bf16[1024,512]{1,0:T(8,128)(2,1)}, bf16[1024,512]{1,0:T(8,128)(2,1)}, u32[]{:S(2)}, u32[]{:S(2)}) %collective-permute-start) | collective-permute-done | bytes 1048608 | tf_op jit(solution)/shard_map/ppermute | solution.py:202
  46.8 2.6 collective-permute-start.11
  49.4 16.1 %shard_map.95 = bf16[512,1024]{1,0:T(8,128)(2,1)} custom-call(s32[2]{0:T(128)} %pad_add_fusion.refs_0_, bf16[512,8192]{1,0:T(8,128)(2,1)} %bitcast.122, bf16[8192,1024]{1,0:T(8,128)(2,1)} %refs_3_.3), custom_call_target="tpu_custom_call" | custom-call | flops 536870912 | bytes 1572864 | tf_op jit(solution)/shard_map/pallas_call | solution.py:148
  65.5 1.7 collective-permute-start.2
  67.2 1.5 collective-permute-start.6
  68.7 23.0 %collective-permute-done.1 = bf16[2048,512]{1,0:T(8,128)(2,1)} collective-permute-done((bf16[2048,512]{1,0:T(8,128)(2,1)}, bf16[2048,512]{1,0:T(8,128)(2,1)}, u32[]{:S(2)}, u32[]{:S(2)}) %collective-permute-start.1) | collective-permute-done | bytes 2097184 | tf_op jit(solution)/shard_map/ppermute | solution.py:202
  91.7 1.5 collective-permute-start.7
  93.2 18.7 %collective-permute-start.4 = (bf16[2048,512]{1,0:T(8,128)(2,1)S(1)}, bf16[2048,512]{1,0:T(8,128)(2,1)}, u32[]{:S(2)}, u32[]{:S(2)}) collective-permute-start(bf16[2048,512]{1,0:T(8,128)(2,1)S(1)} %get-tuple-element.23), channel_id=1, source_target_pairs={{0,4},{4,0},{8,12},{12,8},{1,5},{5,1},{9,13},{13,9},{2,6},{6,2},{1... | collective-permute-start | bytes 6291464 | tf_op jit(solution)/shard_map/ppermute | solution.py:202
  111.9 24.7 %collective-permute-done.2 = bf16[2048,512]{1,0:T(8,128)(2,1)} collective-permute-done((bf16[2048,512]{1,0:T(8,128)(2,1)S(1)}, bf16[2048,512]{1,0:T(8,128)(2,1)}, u32[]{:S(2)}, u32[]{:S(2)}) %collective-permute-start.2) | collective-permute-done | bytes 2097184 | tf_op jit(solution)/shard_map/ppermute | solution.py:202
  136.6 2.1 collective-permute-start.5
  138.7 1.5 collective-permute-start.8
  140.2 6.0 %slice_bitcast_fusion = (bf16[128,8192]{1,0:T(8,128)(2,1)}, bf16[128,8192]{1,0:T(8,128)(2,1)}, bf16[128,8192]{1,0:T(8,128)(2,1)}, bf16[128,8192]{1,0:T(8,128)(2,1)}) fusion(bf16[4,128,8192]{2,1,0:T(8,128)(2,1)} %param.9), kind=kLoop, calls=%fused_computation.3 | loop fusion | bytes 16777216 | tf_op jit(solution)/shard_map/slice | solution.py:213
  146.3 56.5 %collective-permute-done.5 = bf16[1024,512]{1,0:T(8,128)(2,1)S(1)} collective-permute-done((bf16[1024,512]{1,0:T(8,128)(2,1)S(1)}, bf16[1024,512]{1,0:T(8,128)(2,1)S(1)}, u32[]{:S(2)}, u32[]{:S(2)}) %collective-permute-start.5) | collective-permute-done | bytes 1048608 | tf_op jit(solution)/shard_map/ppermute | solution.py:202
  202.8 1.4 copy-done.7
  204.4 5.1 %collective-permute-start.12 = (bf16[128,8192]{1,0:T(8,128)(2,1)}, bf16[128,8192]{1,0:T(8,128)(2,1)S(1)}, u32[]{:S(2)}, u32[]{:S(2)}) collective-permute-start(bf16[128,8192]{1,0:T(8,128)(2,1)} %get-tuple-element.26), channel_id=1, source_target_pairs={{0,12},{12,0},{1,13},{13,1},{2,14},{14,2},{3,15},{15,3},{16,28},{2... | collective-permute-start | bytes 6291464 | tf_op jit(solution)/shard_map/ppermute | solution.py:214
  209.6 1.6 collective-permute-start.9
  211.1 2.2 constant_dynamic-update-slice_fusion.4
  213.4 2.5 collective-permute-start.16
  215.9 2.3 constant_dynamic-update-slice_fusion.9
  218.7 3.2 constant_dynamic-update-slice_fusion.3
  221.9 3.1 constant_dynamic-update-slice_fusion.2
  224.9 1.4 constant_dynamic-update-slice_fusion.8
  226.4 3.0 constant_dynamic-update-slice_fusion.7
  229.4 49.1 %collective-permute-done.10 = bf16[1024,512]{1,0:T(8,128)(2,1)S(1)} collective-permute-done((bf16[1024,512]{1,0:T(8,128)(2,1)S(1)}, bf16[1024,512]{1,0:T(8,128)(2,1)S(1)}, u32[]{:S(2)}, u32[]{:S(2)}) %collective-permute-start.10) | collective-permute-done | bytes 1048608 | tf_op jit(solution)/shard_map/ppermute | solution.py:203
  278.5 2.5 collective-permute-start.20
  281.0 3.0 constant_dynamic-update-slice_fusion.1
  285.1 3.1 constant_dynamic-update-slice_fusion.6
  289.3 15.6 %shard_map.96 = bf16[512,1024]{1,0:T(8,128)(2,1)} custom-call(s32[2]{0:T(128)} %pad_add_fusion.refs_0_, bf16[512,8192]{1,0:T(8,128)(2,1)} %bitcast.123, bf16[8192,512]{1,0:T(8,128)(2,1)} %constant_dynamic-update-slice_fusion.refs_2_.refs_5_.refs_4_, bf16[8192,512]{1,0:T(8,128)(2,1)} %constant_dynamic-update-slice_fusion.5.refs_3_.refs_6_.refs_5_), custom_call_target="tpu_custom_call" | custom-call | flops 536870912 | bytes 1572864 | tf_op jit(solution)/shard_map/pallas_call | solution.py:148
  305.0 1.3 copy-done.6
  306.3 18.8 %shard_map.97 = bf16[256,2048]{1,0:T(8,128)(2,1)} custom-call(s32[2]{0:T(128)} %pad_add_fusion.refs_0_, bf16[128,8192]{1,0:T(8,128)(2,1)} %copy-done.4, bf16[128,8192]{1,0:T(8,128)(2,1)} %copy-done.6, bf16[256,8192]{1,0:T(8,128)(2,1)} %collective-permute-done.3.refs_3_, bf16[8192,1024]{1,0:T(8,128)(2,1)} %refs_3_.3, ...), custom_call_target="tpu_custom_call" | custom-call | flops 536870912 | bytes 2359296 | tf_op jit(solution)/shard_map/pallas_call | solution.py:148
  325.1 1.2 dynamic-slice_bitcast_fusion.5
  326.3 1.6 collective-permute-start.18
  328.5 1.2 collective-permute-start.15
  329.7 5.2 %collective-permute-done.19 = bf16[2,32,2048]{2,1,0:T(8,128)(2,1)S(1)} collective-permute-done((bf16[2,32,2048]{2,1,0:T(8,128)(2,1)S(1)}, bf16[2,32,2048]{2,1,0:T(8,128)(2,1)S(1)}, u32[]{:S(2)}, u32[]{:S(2)}) %collective-permute-start.19) | collective-permute-done | bytes 262176 | tf_op jit(solution)/shard_map/ppermute | solution.py:230
  334.9 1.5 collective-permute-start.14
  336.4 4.2 collective-permute-done.18
  340.7 5.3 %collective-permute-start.27 = (bf16[128,8192]{1,0:T(8,128)(2,1)}, bf16[128,8192]{1,0:T(8,128)(2,1)}, u32[]{:S(2)}, u32[]{:S(2)}) collective-permute-start(bf16[128,8192]{1,0:T(8,128)(2,1)} %get-tuple-element.32), channel_id=1, source_target_pairs={{0,12},{12,0},{1,13},{13,1},{2,14},{14,2},{3,15},{15,3},{16,28},{2... | collective-permute-start | bytes 6291464 | tf_op jit(solution)/shard_map/ppermute | solution.py:214
  347.1 15.2 %shard_map.98 = bf16[128,2048]{1,0:T(8,128)(2,1)} custom-call(s32[2]{0:T(128)} %pad_add_fusion.refs_0_, bf16[128,8192]{1,0:T(8,128)(2,1)} %collective-permute-done.20.refs_1_, bf16[256,8192]{1,0:T(8,128)(2,1)} %collective-permute-done.11.refs_2_, bf16[8192,1024]{1,0:T(8,128)(2,1)} %refs_3_.3, ...), custom_call_target="tpu_custom_call" | custom-call | flops 268435456 | bytes 2228224 | tf_op jit(solution)/shard_map/pallas_call | solution.py:148
  365.7 3.3 collective-permute-done.23
  369.0 3.1 collective-permute-done.22
  373.2 1.4 collective-permute-start.24
  374.6 11.1 %collective-permute-done.24 = bf16[224,1024]{1,0:T(8,128)(2,1)S(1)} collective-permute-done((bf16[224,1024]{1,0:T(8,128)(2,1)S(1)}, bf16[224,1024]{1,0:T(8,128)(2,1)S(1)}, u32[]{:S(2)}, u32[]{:S(2)}) %collective-permute-start.24) | collective-permute-done | bytes 458784 | tf_op jit(solution)/shard_map/ppermute | solution.py:230
  385.9 7.2 %collective-permute-done.27.refs_1_ = bf16[128,8192]{1,0:T(8,128)(2,1)} collective-permute-done((bf16[128,8192]{1,0:T(8,128)(2,1)}, bf16[128,8192]{1,0:T(8,128)(2,1)}, u32[]{:S(2)}, u32[]{:S(2)}) %collective-permute-start.27) | collective-permute-done | bytes 2097184 | tf_op jit(solution)/shard_map/ppermute | solution.py:214
  393.2 15.3 %shard_map.99 = bf16[128,2048]{1,0:T(8,128)(2,1)} custom-call(s32[2]{0:T(128)} %pad_add_fusion.refs_0_, bf16[128,8192]{1,0:T(8,128)(2,1)} %collective-permute-done.27.refs_1_, bf16[256,8192]{1,0:T(8,128)(2,1)} %collective-permute-done.11.refs_2_, bf16[8192,1024]{1,0:T(8,128)(2,1)} %refs_3_.3, ...), custom_call_target="tpu_custom_call" | custom-call | flops 268435456 | bytes 2228224 | tf_op jit(solution)/shard_map/pallas_call | solution.py:148
  408.4 9.8 %collective-permute-done.26 = bf16[224,1024]{1,0:T(8,128)(2,1)S(1)} collective-permute-done((bf16[224,1024]{1,0:T(8,128)(2,1)S(1)}, bf16[224,1024]{1,0:T(8,128)(2,1)S(1)}, u32[]{:S(2)}, u32[]{:S(2)}) %collective-permute-start.26) | collective-permute-done | bytes 458784 | tf_op jit(solution)/shard_map/ppermute | solution.py:230
  419.4 1.7 collective-permute-start.29
  421.2 3.7 collective-permute-done.30
  424.9 3.1 collective-permute-done.29
  429.5 4.2 collective-permute-done.32
  433.7 1.8 collective-permute-start.34
  435.5 1.3 constant_dynamic-slice_fusion.3
  436.9 5.6 %collective-permute-done.31 = bf16[224,1024]{1,0:T(8,128)(2,1)S(1)} collective-permute-done((bf16[224,1024]{1,0:T(8,128)(2,1)S(1)}, bf16[224,1024]{1,0:T(8,128)(2,1)S(1)}, u32[]{:S(2)}, u32[]{:S(2)}) %collective-permute-start.31) | collective-permute-done | bytes 458784 | tf_op jit(solution)/shard_map/ppermute | solution.py:230
  442.8 1.3 collective-permute-done.34
  444.3 1.4 collective-permute-done.35.refs_5_
  445.7 4.4 shard_map.100
  450.7 1.4 collective-permute-start.37
  454.3 4.3 collective-permute-start.41
  460.3 2.9 collective-permute-done.40
  (107 shorter events, 18.8 us)
Async XLA Ops:
  7.2 422.2 %all-gather.3.cloned.1.call-start = ((), (), s32[]{:S(2)}) async-start(), calls=%async_computation | async-start | bytes 1310720 | tf_op jit(solution)/shard_map/all_gather | solution.py:218
  13.2 80.0 %collective-permute-start.3 = (bf16[256,8192]{1,0:T(8,128)(2,1)}, bf16[256,8192]{1,0:T(8,128)(2,1)}, u32[]{:S(2)}, u32[]{:S(2)}) collective-permute-start(bf16[256,8192]{1,0:T(8,128)(2,1)} %bitcast.4), channel_id=1, source_target_pairs={{4,8},{8,4},{5,9},{9,5},{6,10},{10,6},{7,11},{11,7},{20,24},{24,20... | collective-permute-start | bytes 12582920 | tf_op jit(solution)/shard_map/ppermute | solution.py:201
  18.6 10.0 %copy-start.12 = (s32[2048]{0:T(1024)S(1)}, s32[2048]{0:T(1024)}, u32[]{:S(2)}) copy-start(s32[2048]{0:T(1024)} %param.15) | copy-start | bytes 24580
  18.6 10.0 %copy-start.13 = (s32[4]{0:T(128)S(1)}, s32[4]{0:T(128)}, u32[]{:S(2)}) copy-start(s32[4]{0:T(128)} %param.14) | copy-start | bytes 52
  18.6 28.2 %collective-permute-start = (bf16[1024,512]{1,0:T(8,128)(2,1)}, bf16[1024,512]{1,0:T(8,128)(2,1)}, u32[]{:S(2)}, u32[]{:S(2)}) collective-permute-start(bf16[1024,512]{1,0:T(8,128)(2,1)} %get-tuple-element.45), channel_id=1, source_target_pairs={{0,4},{4,0},{8,12},{12,8},{1,5},{5,1},{9,13},{13,9},{2,6},{6,2},{1... | collective-permute-start | bytes 3145736 | tf_op jit(solution)/shard_map/ppermute | solution.py:202
  27.9 63.8 %collective-permute-start.1 = (bf16[2048,512]{1,0:T(8,128)(2,1)}, bf16[2048,512]{1,0:T(8,128)(2,1)}, u32[]{:S(2)}, u32[]{:S(2)}) collective-permute-start(bf16[2048,512]{1,0:T(8,128)(2,1)} %get-tuple-element.42), channel_id=1, source_target_pairs={{0,4},{4,0},{8,12},{12,8},{1,5},{5,1},{9,13},{13,9},{2,6},{6,2},{1... | collective-permute-start | bytes 6291464 | tf_op jit(solution)/shard_map/ppermute | solution.py:202
  46.8 156.1 %collective-permute-start.11 = (bf16[256,8192]{1,0:T(8,128)(2,1)}, bf16[256,8192]{1,0:T(8,128)(2,1)}, u32[]{:S(2)}, u32[]{:S(2)}) collective-permute-start(bf16[256,8192]{1,0:T(8,128)(2,1)} %bitcast.128), channel_id=1, source_target_pairs={{4,8},{8,4},{5,9},{9,5},{6,10},{10,6},{7,11},{11,7},{20,24},{24,20... | collective-permute-start | bytes 12582920 | tf_op jit(solution)/shard_map/ppermute | solution.py:201
  49.4 16.1 %copy-start.5 = (bf16[2048,512]{1,0:T(8,128)(2,1)S(1)}, bf16[2048,512]{1,0:T(8,128)(2,1)}, u32[]{:S(2)}) copy-start(bf16[2048,512]{1,0:T(8,128)(2,1)} %get-tuple-element.22) | copy-start | bytes 6291460
  65.5 71.2 %collective-permute-start.2 = (bf16[2048,512]{1,0:T(8,128)(2,1)S(1)}, bf16[2048,512]{1,0:T(8,128)(2,1)}, u32[]{:S(2)}, u32[]{:S(2)}) collective-permute-start(bf16[2048,512]{1,0:T(8,128)(2,1)S(1)} %copy-done.5), channel_id=1, source_target_pairs={{0,4},{4,0},{8,12},{12,8},{1,5},{5,1},{9,13},{13,9},{2,6},{6,2},{1... | collective-permute-start | bytes 6291464 | tf_op jit(solution)/shard_map/ppermute | solution.py:202
  67.2 71.5 %collective-permute-start.6 = (bf16[1024,512]{1,0:T(8,128)(2,1)}, bf16[1024,512]{1,0:T(8,128)(2,1)S(1)}, u32[]{:S(2)}, u32[]{:S(2)}) collective-permute-start(bf16[1024,512]{1,0:T(8,128)(2,1)} %collective-permute-done), channel_id=1, source_target_pairs={{0,16},{16,0},{1,17},{17,1},{2,18},{18,2},{3,19},{19,3},{4,20},{20... | collective-permute-start | bytes 3145736 | tf_op jit(solution)/shard_map/ppermute | solution.py:203
  91.7 111.1 %collective-permute-start.7 = (bf16[2048,512]{1,0:T(8,128)(2,1)}, bf16[2048,512]{1,0:T(8,128)(2,1)S(1)}, u32[]{:S(2)}, u32[]{:S(2)}) collective-permute-start(bf16[2048,512]{1,0:T(8,128)(2,1)} %collective-permute-done.1), channel_id=1, source_target_pairs={{0,16},{16,0},{1,17},{17,1},{2,18},{18,2},{3,19},{19,3},{4,20},{20... | collective-permute-start | bytes 6291464 | tf_op jit(solution)/shard_map/ppermute | solution.py:203
  93.2 109.6 %collective-permute-start.4 = (bf16[2048,512]{1,0:T(8,128)(2,1)S(1)}, bf16[2048,512]{1,0:T(8,128)(2,1)}, u32[]{:S(2)}, u32[]{:S(2)}) collective-permute-start(bf16[2048,512]{1,0:T(8,128)(2,1)S(1)} %get-tuple-element.23), channel_id=1, source_target_pairs={{0,4},{4,0},{8,12},{12,8},{1,5},{5,1},{9,13},{13,9},{2,6},{6,2},{1... | collective-permute-start | bytes 6291464 | tf_op jit(solution)/shard_map/ppermute | solution.py:202
  136.6 66.2 %collective-permute-start.5 = (bf16[1024,512]{1,0:T(8,128)(2,1)S(1)}, bf16[1024,512]{1,0:T(8,128)(2,1)S(1)}, u32[]{:S(2)}, u32[]{:S(2)}) collective-permute-start(bf16[1024,512]{1,0:T(8,128)(2,1)S(1)} %get-tuple-element.24), channel_id=1, source_target_pairs={{0,4},{4,0},{8,12},{12,8},{1,5},{5,1},{9,13},{13,9},{2,6},{6,2},{1... | collective-permute-start | bytes 3145736 | tf_op jit(solution)/shard_map/ppermute | solution.py:202
  138.7 7.6 %copy-start.11 = (bf16[1024,512]{1,0:T(8,128)(2,1)}, bf16[1024,512]{1,0:T(8,128)(2,1)S(1)}, u32[]{:S(2)}) copy-start(bf16[1024,512]{1,0:T(8,128)(2,1)S(1)} %collective-permute-done.6) | copy-start | bytes 3145732
  138.7 74.7 %collective-permute-start.8 = (bf16[2048,512]{1,0:T(8,128)(2,1)}, bf16[2048,512]{1,0:T(8,128)(2,1)}, u32[]{:S(2)}, u32[]{:S(2)}) collective-permute-start(bf16[2048,512]{1,0:T(8,128)(2,1)} %collective-permute-done.2), channel_id=1, source_target_pairs={{0,16},{16,0},{1,17},{17,1},{2,18},{18,2},{3,19},{19,3},{4,20},{20... | collective-permute-start | bytes 6291464 | tf_op jit(solution)/shard_map/ppermute | solution.py:203
  202.8 1.6 copy-start.9
  202.8 1.4 copy-start.7
  204.4 74.1 %collective-permute-start.12 = (bf16[128,8192]{1,0:T(8,128)(2,1)}, bf16[128,8192]{1,0:T(8,128)(2,1)S(1)}, u32[]{:S(2)}, u32[]{:S(2)}) collective-permute-start(bf16[128,8192]{1,0:T(8,128)(2,1)} %get-tuple-element.26), channel_id=1, source_target_pairs={{0,12},{12,0},{1,13},{13,1},{2,14},{14,2},{3,15},{15,3},{16,28},{2... | collective-permute-start | bytes 6291464 | tf_op jit(solution)/shard_map/ppermute | solution.py:214
  209.5 8.7 %copy-start.10 = (bf16[1024,512]{1,0:T(8,128)(2,1)S(1)}, bf16[1024,512]{1,0:T(8,128)(2,1)}, u32[]{:S(2)}) copy-start(bf16[1024,512]{1,0:T(8,128)(2,1)} %copy-done.9) | copy-start | bytes 3145732
  209.6 75.6 %collective-permute-start.9 = (bf16[2048,512]{1,0:T(8,128)(2,1)}, bf16[2048,512]{1,0:T(8,128)(2,1)}, u32[]{:S(2)}, u32[]{:S(2)}) collective-permute-start(bf16[2048,512]{1,0:T(8,128)(2,1)} %collective-permute-done.4), channel_id=1, source_target_pairs={{0,16},{16,0},{1,17},{17,1},{2,18},{18,2},{3,19},{19,3},{4,20},{20... | collective-permute-start | bytes 6291464 | tf_op jit(solution)/shard_map/ppermute | solution.py:203
  213.4 91.6 %collective-permute-start.16 = (bf16[128,8192]{1,0:T(8,128)(2,1)}, bf16[128,8192]{1,0:T(8,128)(2,1)S(1)}, u32[]{:S(2)}, u32[]{:S(2)}) collective-permute-start(bf16[128,8192]{1,0:T(8,128)(2,1)} %get-tuple-element.28), channel_id=1, source_target_pairs={{0,12},{12,0},{1,13},{13,1},{2,14},{14,2},{3,15},{15,3},{16,28},{2... | collective-permute-start | bytes 6291464 | tf_op jit(solution)/shard_map/ppermute | solution.py:214
  218.2 6.7 %copy-start.8 = (bf16[2048,512]{1,0:T(8,128)(2,1)S(1)}, bf16[2048,512]{1,0:T(8,128)(2,1)}, u32[]{:S(2)}) copy-start(bf16[2048,512]{1,0:T(8,128)(2,1)} %copy-done.7) | copy-start | bytes 6291460
  218.2 60.3 %collective-permute-start.10 = (bf16[1024,512]{1,0:T(8,128)(2,1)S(1)}, bf16[1024,512]{1,0:T(8,128)(2,1)S(1)}, u32[]{:S(2)}, u32[]{:S(2)}) collective-permute-start(bf16[1024,512]{1,0:T(8,128)(2,1)S(1)} %copy-done.10), channel_id=1, source_target_pairs={{0,16},{16,0},{1,17},{17,1},{2,18},{18,2},{3,19},{19,3},{4,20},{20... | collective-permute-start | bytes 3145736 | tf_op jit(solution)/shard_map/ppermute | solution.py:203
  278.5 9.7 %copy-start.4 = (bf16[128,8192]{1,0:T(8,128)(2,1)}, bf16[128,8192]{1,0:T(8,128)(2,1)S(1)}, u32[]{:S(2)}) copy-start(bf16[128,8192]{1,0:T(8,128)(2,1)S(1)} %collective-permute-done.12.refs_1_) | copy-start | bytes 6291460
  278.5 68.6 %collective-permute-start.20 = (bf16[128,8192]{1,0:T(8,128)(2,1)}, bf16[128,8192]{1,0:T(8,128)(2,1)}, u32[]{:S(2)}, u32[]{:S(2)}) collective-permute-start(bf16[128,8192]{1,0:T(8,128)(2,1)} %get-tuple-element.30), channel_id=1, source_target_pairs={{0,12},{12,0},{1,13},{13,1},{2,14},{14,2},{3,15},{15,3},{16,28},{2... | collective-permute-start | bytes 6291464 | tf_op jit(solution)/shard_map/ppermute | solution.py:214
  305.0 23.2 %copy-start.2 = (bf16[512,1024]{1,0:T(8,128)(2,1)S(1)}, bf16[512,1024]{1,0:T(8,128)(2,1)}, u32[]{:S(2)}) copy-start(bf16[512,1024]{1,0:T(8,128)(2,1)} %shard_map.95) | copy-start | bytes 3145732
  305.0 23.2 %copy-start.3 = (bf16[512,1024]{1,0:T(8,128)(2,1)S(1)}, bf16[512,1024]{1,0:T(8,128)(2,1)}, u32[]{:S(2)}) copy-start(bf16[512,1024]{1,0:T(8,128)(2,1)} %shard_map.96) | copy-start | bytes 3145732
  305.0 1.3 copy-start.6
  326.2 8.6 %collective-permute-start.19 = (bf16[2,32,2048]{2,1,0:T(8,128)(2,1)S(1)}, bf16[2,32,2048]{2,1,0:T(8,128)(2,1)S(1)}, u32[]{:S(2)}, u32[]{:S(2)}) collective-permute-start(bf16[2,32,2048]{2,1,0:T(8,128)(2,1)S(1)} %get-tuple-element.61), channel_id=1, source_target_pairs={{0,3},{1,2},{2,1},{3,0},{4,7},{5,6},{6,5},{7,4},{8,11},{9,10},{10,... | collective-permute-start | bytes 786440 | tf_op jit(solution)/shard_map/ppermute | solution.py:230
  326.3 14.3 %collective-permute-start.18 = (bf16[2,32,2048]{2,1,0:T(8,128)(2,1)S(1)}, bf16[2,32,2048]{2,1,0:T(8,128)(2,1)S(1)}, u32[]{:S(2)}, u32[]{:S(2)}) collective-permute-start(bf16[2,32,2048]{2,1,0:T(8,128)(2,1)S(1)} %get-tuple-element.62), channel_id=1, source_target_pairs={{0,2},{1,3},{2,0},{3,1},{4,6},{5,7},{6,4},{7,5},{8,10},{9,11},{10,... | collective-permute-start | bytes 786440 | tf_op jit(solution)/shard_map/ppermute | solution.py:230
  327.9 12.8 %collective-permute-start.17 = (bf16[2,32,2048]{2,1,0:T(8,128)(2,1)S(1)}, bf16[2,32,2048]{2,1,0:T(8,128)(2,1)S(1)}, u32[]{:S(2)}, u32[]{:S(2)}) collective-permute-start(bf16[2,32,2048]{2,1,0:T(8,128)(2,1)S(1)} %get-tuple-element.60), channel_id=1, source_target_pairs={{0,1},{1,0},{2,3},{3,2},{4,5},{5,4},{6,7},{7,6},{8,9},{9,8},{10,11... | collective-permute-start | bytes 786440 | tf_op jit(solution)/shard_map/ppermute | solution.py:230
  328.5 35.8 %collective-permute-start.15 = (bf16[4,32,2048]{2,1,0:T(8,128)(2,1)S(1)}, bf16[4,32,2048]{2,1,0:T(8,128)(2,1)S(1)}, u32[]{:S(2)}, u32[]{:S(2)}) collective-permute-start(bf16[4,32,2048]{2,1,0:T(8,128)(2,1)S(1)} %get-tuple-element.54), channel_id=1, source_target_pairs={{0,3},{1,2},{2,1},{3,0},{4,7},{5,6},{6,5},{7,4},{8,11},{9,10},{10,... | collective-permute-start | bytes 1572872 | tf_op jit(solution)/shard_map/ppermute | solution.py:230
  334.9 30.4 %collective-permute-start.14 = (bf16[4,32,2048]{2,1,0:T(8,128)(2,1)S(1)}, bf16[4,32,2048]{2,1,0:T(8,128)(2,1)S(1)}, u32[]{:S(2)}, u32[]{:S(2)}) collective-permute-start(bf16[4,32,2048]{2,1,0:T(8,128)(2,1)S(1)} %get-tuple-element.55), channel_id=1, source_target_pairs={{0,2},{1,3},{2,0},{3,1},{4,6},{5,7},{6,4},{7,5},{8,10},{9,11},{10,... | collective-permute-start | bytes 1572872 | tf_op jit(solution)/shard_map/ppermute | solution.py:230
  340.6 24.8 %collective-permute-start.13 = (bf16[4,32,2048]{2,1,0:T(8,128)(2,1)S(1)}, bf16[4,32,2048]{2,1,0:T(8,128)(2,1)S(1)}, u32[]{:S(2)}, u32[]{:S(2)}) collective-permute-start(bf16[4,32,2048]{2,1,0:T(8,128)(2,1)S(1)} %get-tuple-element.53), channel_id=1, source_target_pairs={{0,1},{1,0},{2,3},{3,2},{4,5},{5,4},{6,7},{7,6},{8,9},{9,8},{10,11... | collective-permute-start | bytes 1572872 | tf_op jit(solution)/shard_map/ppermute | solution.py:230
  340.7 52.5 %collective-permute-start.27 = (bf16[128,8192]{1,0:T(8,128)(2,1)}, bf16[128,8192]{1,0:T(8,128)(2,1)}, u32[]{:S(2)}, u32[]{:S(2)}) collective-permute-start(bf16[128,8192]{1,0:T(8,128)(2,1)} %get-tuple-element.32), channel_id=1, source_target_pairs={{0,12},{12,0},{1,13},{13,1},{2,14},{14,2},{3,15},{15,3},{16,28},{2... | collective-permute-start | bytes 6291464 | tf_op jit(solution)/shard_map/ppermute | solution.py:214
  363.4 5.6 %collective-permute-start.23 = (bf16[1,32,2048]{2,1,0:T(8,128)(2,1)S(1)}, bf16[1,32,2048]{2,1,0:T(8,128)(2,1)S(1)}, u32[]{:S(2)}, u32[]{:S(2)}) collective-permute-start(bf16[1,32,2048]{2,1,0:T(8,128)(2,1)S(1)} %get-tuple-element.69), channel_id=1, source_target_pairs={{0,3},{1,2},{2,1},{3,0},{4,7},{5,6},{6,5},{7,4},{8,11},{9,10},{10,... | collective-permute-start | bytes 393224 | tf_op jit(solution)/shard_map/ppermute | solution.py:230
  364.3 7.8 %collective-permute-start.22 = (bf16[1,32,2048]{2,1,0:T(8,128)(2,1)S(1)}, bf16[1,32,2048]{2,1,0:T(8,128)(2,1)S(1)}, u32[]{:S(2)}, u32[]{:S(2)}) collective-permute-start(bf16[1,32,2048]{2,1,0:T(8,128)(2,1)S(1)} %get-tuple-element.70), channel_id=1, source_target_pairs={{0,2},{1,3},{2,0},{3,1},{4,6},{5,7},{6,4},{7,5},{8,10},{9,11},{10,... | collective-permute-start | bytes 393224 | tf_op jit(solution)/shard_map/ppermute | solution.py:230
  365.2 6.9 %collective-permute-start.21 = (bf16[1,32,2048]{2,1,0:T(8,128)(2,1)S(1)}, bf16[1,32,2048]{2,1,0:T(8,128)(2,1)S(1)}, u32[]{:S(2)}, u32[]{:S(2)}) collective-permute-start(bf16[1,32,2048]{2,1,0:T(8,128)(2,1)S(1)} %get-tuple-element.68), channel_id=1, source_target_pairs={{0,1},{1,0},{2,3},{3,2},{4,5},{5,4},{6,7},{7,6},{8,9},{9,8},{10,11... | collective-permute-start | bytes 393224 | tf_op jit(solution)/shard_map/ppermute | solution.py:230
  373.2 12.4 %collective-permute-start.24 = (bf16[224,1024]{1,0:T(8,128)(2,1)S(1)}, bf16[224,1024]{1,0:T(8,128)(2,1)S(1)}, u32[]{:S(2)}, u32[]{:S(2)}) collective-permute-start(bf16[224,1024]{1,0:T(8,128)(2,1)S(1)} %get-tuple-element.64), channel_id=1, source_target_pairs={{0,2},{1,3},{2,0},{3,1},{4,6},{5,7},{6,4},{7,5},{8,10},{9,11},{10,... | collective-permute-start | bytes 1376264 | tf_op jit(solution)/shard_map/ppermute | solution.py:230
  385.7 32.5 %collective-permute-start.25 = (bf16[448,1024]{1,0:T(8,128)(2,1)S(1)}, bf16[448,1024]{1,0:T(8,128)(2,1)S(1)}, u32[]{:S(2)}, u32[]{:S(2)}) collective-permute-start(bf16[448,1024]{1,0:T(8,128)(2,1)S(1)} %pad_maximum_fusion.3.refs_0_), channel_id=1, source_target_pairs={{0,1},{1,0},{2,3},{3,2},{4,5},{5,4},{6,7},{7,6},{8,9},{9,8},{10,11... | collective-permute-start | bytes 2752520 | tf_op jit(solution)/shard_map/ppermute | solution.py:230
  385.8 32.4 %collective-permute-start.26 = (bf16[224,1024]{1,0:T(8,128)(2,1)S(1)}, bf16[224,1024]{1,0:T(8,128)(2,1)S(1)}, u32[]{:S(2)}, u32[]{:S(2)}) collective-permute-start(bf16[224,1024]{1,0:T(8,128)(2,1)S(1)} %get-tuple-element.63), channel_id=1, source_target_pairs={{0,4},{4,0},{8,12},{12,8},{1,5},{5,1},{9,13},{13,9},{2,6},{6,2},{1... | collective-permute-start | bytes 1376264 | tf_op jit(solution)/shard_map/ppermute | solution.py:230
  419.3 5.6 %collective-permute-start.30 = (bf16[1,32,2048]{2,1,0:T(8,128)(2,1)S(1)}, bf16[1,32,2048]{2,1,0:T(8,128)(2,1)S(1)}, u32[]{:S(2)}, u32[]{:S(2)}) collective-permute-start(bf16[1,32,2048]{2,1,0:T(8,128)(2,1)S(1)} %get-tuple-element.66), channel_id=1, source_target_pairs={{0,3},{1,2},{2,1},{3,0},{4,7},{5,6},{6,5},{7,4},{8,11},{9,10},{10,... | collective-permute-start | bytes 393224 | tf_op jit(solution)/shard_map/ppermute | solution.py:230
  419.4 8.6 %collective-permute-start.29 = (bf16[1,32,2048]{2,1,0:T(8,128)(2,1)S(1)}, bf16[1,32,2048]{2,1,0:T(8,128)(2,1)S(1)}, u32[]{:S(2)}, u32[]{:S(2)}) collective-permute-start(bf16[1,32,2048]{2,1,0:T(8,128)(2,1)S(1)} %get-tuple-element.67), channel_id=1, source_target_pairs={{0,2},{1,3},{2,0},{3,1},{4,6},{5,7},{6,4},{7,5},{8,10},{9,11},{10,... | collective-permute-start | bytes 393224 | tf_op jit(solution)/shard_map/ppermute | solution.py:230
  421.1 6.9 %collective-permute-start.28 = (bf16[1,32,2048]{2,1,0:T(8,128)(2,1)S(1)}, bf16[1,32,2048]{2,1,0:T(8,128)(2,1)S(1)}, u32[]{:S(2)}, u32[]{:S(2)}) collective-permute-start(bf16[1,32,2048]{2,1,0:T(8,128)(2,1)S(1)} %get-tuple-element.65), channel_id=1, source_target_pairs={{0,1},{1,0},{2,3},{3,2},{4,5},{5,4},{6,7},{7,6},{8,9},{9,8},{10,11... | collective-permute-start | bytes 393224 | tf_op jit(solution)/shard_map/ppermute | solution.py:230
  428.9 13.5 %collective-permute-start.31 = (bf16[224,1024]{1,0:T(8,128)(2,1)S(1)}, bf16[224,1024]{1,0:T(8,128)(2,1)S(1)}, u32[]{:S(2)}, u32[]{:S(2)}) collective-permute-start(bf16[224,1024]{1,0:T(8,128)(2,1)S(1)} %collective-permute-done.26), channel_id=1, source_target_pairs={{0,2},{1,3},{2,0},{3,1},{4,6},{5,7},{6,4},{7,5},{8,10},{9,11},{10,... | collective-permute-start | bytes 1376264 | tf_op jit(solution)/shard_map/ppermute | solution.py:230
  429.4 4.3 collective-permute-start.32
  433.7 10.4 %collective-permute-start.34 = (bf16[64,1024]{1,0:T(8,128)(2,1)S(1)}, bf16[64,1024]{1,0:T(8,128)(2,1)S(1)}, u32[]{:S(2)}, u32[]{:S(2)}) collective-permute-start(bf16[64,1024]{1,0:T(8,128)(2,1)S(1)} %pad_maximum_fusion.7), channel_id=1, source_target_pairs={{0,2},{1,3},{2,0},{3,1},{4,6},{5,7},{6,4},{7,5},{8,10},{9,11},{10,... | collective-permute-start | bytes 393224 | tf_op jit(solution)/shard_map/ppermute | solution.py:230
  436.8 8.9 %copy-start = (bf16[4,1024,256]{2,1,0:T(8,128)(2,1)S(1)}, bf16[4,1024,256]{2,1,0:T(8,128)(2,1)}, u32[]{:S(2)}) copy-start(bf16[4,1024,256]{2,1,0:T(8,128)(2,1)} %refs_8_.1) | copy-start | bytes 6291460
  436.9 8.9 %copy-start.1 = (f32[1024,256]{1,0:T(8,128)S(1)}, f32[1024,256]{1,0:T(8,128)}, u32[]{:S(2)}) copy-start(f32[1024,256]{1,0:T(8,128)} %refs_7_.1) | copy-start | bytes 3145732
  442.5 3.3 collective-permute-start.33
  444.1 1.6 collective-permute-start.35
  450.4 3.0 collective-permute-start.38
  450.7 3.6 collective-permute-start.37
  452.2 2.2 collective-permute-start.36
  454.3 5.9 %collective-permute-start.41 = (f32[4,4]{1,0:T(4,128)S(1)}, f32[4,4]{1,0:T(4,128)S(1)}, u32[]{:S(2)}, u32[]{:S(2)}) collective-permute-start(f32[4,4]{1,0:T(4,128)S(1)} %add_add_fusion.1), channel_id=1, source_target_pairs={{0,12},{4,8},{8,4},{12,0},{1,13},{5,9},{9,5},{13,1},{2,14},{6,10},... | collective-permute-start | bytes 200 | tf_op jit(solution)/shard_map/ppermute | solution.py:173
  458.7 4.5 collective-permute-start.40
  458.7 4.5 collective-permute-start.39
Sparse Core Ops, SparseCore 0:
  386.0 33.6 all-gather.2

commit v14 on v13

--- a/solution.py
+++ b/solution.py
@@ -135,7 +135,7 @@
                 out[:, e:f] = acc[:, c:d].astype(BF16)
 
 
-def project(flags, ends, middles, bases):
+def project(flags, ends, middles, bases, weight=8):
     tokens = ends + middles
     feats = bases[0].shape[0]
     widths = tuple(x.shape[1] for x in bases)
@@ -156,8 +156,8 @@
         scratch_shapes=[pltpu.VMEM((rows, total), F32)],
         compiler_params=pltpu.CompilerParams(vmem_limit_bytes=56 * 2**20),
         cost_estimate=pl.CostEstimate(
-            flops=rows * feats * total // 8,
-            bytes_accessed=feats * (total + rows) // 8,
+            flops=rows * feats * total // weight,
+            bytes_accessed=feats * (total + rows) // weight,
             transcendentals=0,
         ),
     )(flags, *[array for array, _, _ in tokens], *bases)
@@ -197,7 +197,7 @@
             early = {2: [own_own, local_act], 3: [other[0]], 4: []}[i]
             piece = after(piece, near[i - 2], *early)
         if i in (0, 2):
-            part = flat[: 4 * slab] if i == 0 else after(flat[4 * slab :], near[0])
+            part = flat[: 4 * slab] if i == 0 else after(flat, near[0])[4 * slab :]
             other.append(lax.ppermute(part, "row", middle))
         near.append(lax.ppermute(piece, "row", beside))
         far.append(lax.ppermute(near[i], "groups", [(0, 1), (1, 0)]))
@@ -242,19 +242,23 @@
         return [pair, swap(pair, "col", 1)]
 
     sums = [scatter_sum(jnp.concatenate([own_own, own_end], axis=1)), scatter_sum(outer)]
+    waits = sums[-1:]
     for k in (2, 3):
         product = project(
             flags,
             [(partner[k], 0, tok)],
             [(other[1], (k - 2) * tok, tok)],
-            [grad_basis, near_basis, after(far_basis, sums[-1])],
+            [grad_basis, near_basis, after(far_basis, *waits)],
+            weight=8 if k == 2 else 8192,
         )
         if k == 2:
             sums.append(scatter_sum(product))
             early = jnp.concatenate(sums, axis=0)
             got = swap(early[:, dirs:], "row", 1)
-    early_own = gather(early[:, :dirs])
-    last = scatter_sum(after(product, got, *early_own))
+            waits = [swap(early[:, :dirs], "col", 2)]
+    pair = jnp.concatenate([early[:, :dirs], *waits], axis=0)
+    early_own = [pair, swap(pair, "col", 1)]
+    last = scatter_sum(after(product, got))
     got = after(got, last)
     last = after(last, every_act)
     last = jnp.concatenate([last[:, :dirs], swap(last[:, dirs:], "row", 1)], axis=0)

time: 471 us -> 471 us (level)
    ppermute x20, waiting for transfers between devices: 55.8 us -> 43.5 us  [swap(): return lax.ppermute(value, axis, [(i, i ^ d) for i in range(size)])]
    ppermute x4, waiting for transfers between devices: 7.25 us -> 17.5 us  [chain_body(): partner.append(lax.ppermute(after(piece, *tie), 'row', ends))]
    unnamed x37 -> x35, local copies, waits for them, and re-layouts: 24.3 us -> 25.5 us
  transfers between devices with their start and end apart: 43 -> 43, of which waited for: 22 -> 20; matrix products, arithmetic and copies ran while one was open for 12% -> 13% of each run, Pallas kernels for 17% -> 17%
where the time goes in v14:
time: 471 us; the launch traced here: 470 us
  waiting for transfers between devices  229 us (49%)
  Pallas kernels  85.2 us (18%)
  starting transfers between devices  74.7 us (16%)
  local copies, waits for them, and re-layouts  54.2 us (12%)
  between operations  14.4 us (3%)
  matrix products  7.61 us (2%)
  other arithmetic  5.75 us (1%)
    ppermute x5, waiting for transfers between devices, chain_body(): near.append(lax.ppermute(piece, 'row', beside))  112 us
    pallas_call x5, Pallas kernels, project(): pl.pallas_call(functools.partial(project_kernel, len(ends), len(tokens),...  80.7 us
    ppermute x5, waiting for transfers between devices, chain_body(): far.append(lax.ppermute(near[i], 'groups', [(0, 1), (1, 0)]))  49.1 us
    ppermute x20, waiting for transfers between devices, swap(): return lax.ppermute(value, axis, [(i, i ^ d) for i in range(size)])  43.5 us
    ppermute x5, starting transfers between devices, chain_body(): near.append(lax.ppermute(piece, 'row', beside))  26.4 us
    unnamed x35, local copies, waits for them, and re-layouts  25.5 us
    ppermute x4, waiting for transfers between devices, chain_body(): partner.append(lax.ppermute(after(piece, *tie), 'row', ends))  17.5 us
    ppermute x4, starting transfers between devices, chain_body(): partner.append(lax.ppermute(after(piece, *tie), 'row', ends))  15.4 us
  transfers between devices with their start and end apart: 43, of which 20 were waited for; matrix products, arithmetic and copies ran while one was open for 13% of the time, Pallas kernels for 17%

profile of v14, /device:TPU:0, one launch (start us, length us, event | category | flops | bytes accessed | tf_op | source)
XLA Modules:
  0.0 470.4 jit_solution(5993628842463071302)
XLA Ops:
  7.2 4.6 slice.46
  11.8 2.7 collective-permute-start.3
  14.5 2.6 constant_dynamic-slice_fusion.4
  17.2 3.9 collective-permute-start
  21.0 5.5 %constant_dynamic-slice_fusion.8 = (bf16[2048,512]{1,0:T(8,128)(2,1)}, bf16[2048,512]{1,0:T(8,128)(2,1)S(1)}, bf16[2048,512]{1,0:T(8,128)(2,1)}) fusion(bf16[8192,1024]{1,0:T(8,128)(2,1)} %refs_3_.3, s32[]{:T(128)S(6)} %select_n.68), kind=kLoop, calls=%fused_computation.93 | loop fusion | bytes 12582916 | tf_op jit(solution)/shard_map/dynamic_slice | solution.py:195
  27.4 7.6 %fusion.5 = bf16[4,128,256]{2,1,0:T(8,128)(2,1)} fusion(bf16[4,128,8192]{2,1,0:T(8,128)(2,1)} %param.8, bf16[8192,256]{1,0:T(8,128)(2,1)} %param.10, f32[4,128]{1,0:T(4,128)S(1)} %compare_convert_fusion), kind=kOutput, calls=%fused_computation.8 | convolution fusion | flops 2147745792 | bytes 12847104 | tf_op jit(solution)/shard_map/ctd,dk->ctk/dot_general | solution.py:25
  35.0 10.3 %collective-permute-done = bf16[1024,512]{1,0:T(8,128)(2,1)} collective-permute-done((bf16[1024,512]{1,0:T(8,128)(2,1)}, bf16[1024,512]{1,0:T(8,128)(2,1)}, u32[]{:S(2)}, u32[]{:S(2)}) %collective-permute-start) | collective-permute-done | bytes 1048608 | tf_op jit(solution)/shard_map/ppermute | solution.py:202
  45.3 2.6 slice.50
  48.0 2.7 collective-permute-start.11
  50.6 15.9 %shard_map.95 = bf16[512,1024]{1,0:T(8,128)(2,1)} custom-call(s32[2]{0:T(128)} %pad_add_fusion.refs_0_, bf16[512,8192]{1,0:T(8,128)(2,1)} %bitcast.122, bf16[8192,1024]{1,0:T(8,128)(2,1)} %refs_3_.3), custom_call_target="tpu_custom_call" | custom-call | flops 536870912 | bytes 1572864 | tf_op jit(solution)/shard_map/pallas_call | solution.py:148
  66.5 1.7 collective-permute-start.2
  68.2 1.5 collective-permute-start.6
  69.8 20.5 %collective-permute-done.1 = bf16[2048,512]{1,0:T(8,128)(2,1)} collective-permute-done((bf16[2048,512]{1,0:T(8,128)(2,1)}, bf16[2048,512]{1,0:T(8,128)(2,1)}, u32[]{:S(2)}, u32[]{:S(2)}) %collective-permute-start.1) | collective-permute-done | bytes 2097184 | tf_op jit(solution)/shard_map/ppermute | solution.py:202
  90.3 1.5 collective-permute-start.7
  91.8 18.7 %collective-permute-start.4 = (bf16[2048,512]{1,0:T(8,128)(2,1)S(1)}, bf16[2048,512]{1,0:T(8,128)(2,1)}, u32[]{:S(2)}, u32[]{:S(2)}) collective-permute-start(bf16[2048,512]{1,0:T(8,128)(2,1)S(1)} %get-tuple-element.23), channel_id=1, source_target_pairs={{0,4},{4,0},{8,12},{12,8},{1,5},{5,1},{9,13},{13,9},{2,6},{6,2},{1... | collective-permute-start | bytes 6291464 | tf_op jit(solution)/shard_map/ppermute | solution.py:202
  110.5 24.7 %collective-permute-done.2 = bf16[2048,512]{1,0:T(8,128)(2,1)} collective-permute-done((bf16[2048,512]{1,0:T(8,128)(2,1)}, bf16[2048,512]{1,0:T(8,128)(2,1)}, u32[]{:S(2)}, u32[]{:S(2)}) %collective-permute-start.2) | collective-permute-done | bytes 2097184 | tf_op jit(solution)/shard_map/ppermute | solution.py:202
  135.2 2.1 collective-permute-start.5
  137.3 1.5 collective-permute-start.8
  138.8 5.9 %slice_bitcast_fusion = (bf16[128,8192]{1,0:T(8,128)(2,1)}, bf16[128,8192]{1,0:T(8,128)(2,1)}, bf16[128,8192]{1,0:T(8,128)(2,1)}, bf16[128,8192]{1,0:T(8,128)(2,1)}) fusion(bf16[4,128,8192]{2,1,0:T(8,128)(2,1)} %param.9), kind=kLoop, calls=%fused_computation.3 | loop fusion | bytes 16777216 | tf_op jit(solution)/shard_map/slice | solution.py:213
  144.8 56.6 %collective-permute-done.5 = bf16[1024,512]{1,0:T(8,128)(2,1)S(1)} collective-permute-done((bf16[1024,512]{1,0:T(8,128)(2,1)S(1)}, bf16[1024,512]{1,0:T(8,128)(2,1)S(1)}, u32[]{:S(2)}, u32[]{:S(2)}) %collective-permute-start.5) | collective-permute-done | bytes 1048608 | tf_op jit(solution)/shard_map/ppermute | solution.py:202
  201.4 1.3 copy-done.6
  203.1 5.1 %collective-permute-start.12 = (bf16[128,8192]{1,0:T(8,128)(2,1)}, bf16[128,8192]{1,0:T(8,128)(2,1)S(1)}, u32[]{:S(2)}, u32[]{:S(2)}) collective-permute-start(bf16[128,8192]{1,0:T(8,128)(2,1)} %get-tuple-element.26), channel_id=1, source_target_pairs={{0,12},{12,0},{1,13},{13,1},{2,14},{14,2},{3,15},{15,3},{16,28},{2... | collective-permute-start | bytes 6291464 | tf_op jit(solution)/shard_map/ppermute | solution.py:214
  208.2 1.6 collective-permute-start.9
  209.8 2.3 constant_dynamic-update-slice_fusion.4
  212.1 2.5 collective-permute-start.16
  214.6 2.3 constant_dynamic-update-slice_fusion.9
  217.4 3.2 constant_dynamic-update-slice_fusion.3
  220.6 3.1 constant_dynamic-update-slice_fusion.2
  223.6 1.4 constant_dynamic-update-slice_fusion.8
  225.1 3.0 constant_dynamic-update-slice_fusion.7
  228.1 49.1 %collective-permute-done.10 = bf16[1024,512]{1,0:T(8,128)(2,1)S(1)} collective-permute-done((bf16[1024,512]{1,0:T(8,128)(2,1)S(1)}, bf16[1024,512]{1,0:T(8,128)(2,1)S(1)}, u32[]{:S(2)}, u32[]{:S(2)}) %collective-permute-start.10) | collective-permute-done | bytes 1048608 | tf_op jit(solution)/shard_map/ppermute | solution.py:203
  277.2 2.5 collective-permute-start.20
  279.7 3.0 constant_dynamic-update-slice_fusion.1
  283.8 3.1 constant_dynamic-update-slice_fusion.6
  288.0 15.6 %shard_map.96 = bf16[512,1024]{1,0:T(8,128)(2,1)} custom-call(s32[2]{0:T(128)} %pad_add_fusion.refs_0_, bf16[512,8192]{1,0:T(8,128)(2,1)} %bitcast.123, bf16[8192,512]{1,0:T(8,128)(2,1)} %constant_dynamic-update-slice_fusion.refs_2_.refs_5_.refs_4_, bf16[8192,512]{1,0:T(8,128)(2,1)} %constant_dynamic-update-slice_fusion.5.refs_3_.refs_6_.refs_5_), custom_call_target="tpu_custom_call" | custom-call | flops 536870912 | bytes 1572864 | tf_op jit(solution)/shard_map/pallas_call | solution.py:148
  303.6 1.4 copy-done.5
  305.0 18.7 %shard_map.97 = bf16[256,2048]{1,0:T(8,128)(2,1)} custom-call(s32[2]{0:T(128)} %pad_add_fusion.refs_0_, bf16[128,8192]{1,0:T(8,128)(2,1)} %copy-done.4, bf16[128,8192]{1,0:T(8,128)(2,1)} %copy-done.5, bf16[256,8192]{1,0:T(8,128)(2,1)} %collective-permute-done.3.refs_3_, bf16[8192,1024]{1,0:T(8,128)(2,1)} %refs_3_.3, ...), custom_call_target="tpu_custom_call" | custom-call | flops 536870912 | bytes 2359296 | tf_op jit(solution)/shard_map/pallas_call | solution.py:148
  323.8 1.3 dynamic-slice_bitcast_fusion.5
  325.2 1.6 collective-permute-start.19
  327.8 1.6 collective-permute-start.15
  329.4 4.1 collective-permute-done.19
  333.4 1.3 collective-permute-start.14
  334.8 5.3 %collective-permute-done.18 = bf16[2,32,2048]{2,1,0:T(8,128)(2,1)S(1)} collective-permute-done((bf16[2,32,2048]{2,1,0:T(8,128)(2,1)S(1)}, bf16[2,32,2048]{2,1,0:T(8,128)(2,1)S(1)}, u32[]{:S(2)}, u32[]{:S(2)}) %collective-permute-start.18) | collective-permute-done | bytes 262176 | tf_op jit(solution)/shard_map/ppermute | solution.py:230
  340.0 5.3 %collective-permute-start.27 = (bf16[128,8192]{1,0:T(8,128)(2,1)S(1)}, bf16[128,8192]{1,0:T(8,128)(2,1)}, u32[]{:S(2)}, u32[]{:S(2)}) collective-permute-start(bf16[128,8192]{1,0:T(8,128)(2,1)S(1)} %copy-done.8), channel_id=1, source_target_pairs={{0,12},{12,0},{1,13},{13,1},{2,14},{14,2},{3,15},{15,3},{16,28},{2... | collective-permute-start | bytes 6291464 | tf_op jit(solution)/shard_map/ppermute | solution.py:214
  346.4 15.2 %shard_map.98 = bf16[128,2048]{1,0:T(8,128)(2,1)} custom-call(s32[2]{0:T(128)} %pad_add_fusion.refs_0_, bf16[128,8192]{1,0:T(8,128)(2,1)} %collective-permute-done.20.refs_1_, bf16[256,8192]{1,0:T(8,128)(2,1)} %collective-permute-done.11.refs_2_, bf16[8192,1024]{1,0:T(8,128)(2,1)} %refs_3_.3, ...), custom_call_target="tpu_custom_call" | custom-call | flops 268435456 | bytes 2228224 | tf_op jit(solution)/shard_map/pallas_call | solution.py:148
  362.8 1.6 collective-permute-start.23
  365.4 2.9 collective-permute-done.23
  368.3 3.3 collective-permute-done.22
  372.8 1.6 collective-permute-start.24
  374.4 10.4 %collective-permute-done.24 = bf16[224,1024]{1,0:T(8,128)(2,1)S(1)} collective-permute-done((bf16[224,1024]{1,0:T(8,128)(2,1)S(1)}, bf16[224,1024]{1,0:T(8,128)(2,1)S(1)}, u32[]{:S(2)}, u32[]{:S(2)}) %collective-permute-start.24) | collective-permute-done | bytes 458784 | tf_op jit(solution)/shard_map/ppermute | solution.py:230
  384.9 17.5 %collective-permute-done.27.refs_1_ = bf16[128,8192]{1,0:T(8,128)(2,1)} collective-permute-done((bf16[128,8192]{1,0:T(8,128)(2,1)S(1)}, bf16[128,8192]{1,0:T(8,128)(2,1)}, u32[]{:S(2)}, u32[]{:S(2)}) %collective-permute-start.27) | collective-permute-done | bytes 2097184 | tf_op jit(solution)/shard_map/ppermute | solution.py:214
  402.4 15.2 %shard_map.99 = bf16[128,2048]{1,0:T(8,128)(2,1)} custom-call(s32[2]{0:T(128)} %pad_add_fusion.refs_0_, bf16[128,8192]{1,0:T(8,128)(2,1)} %collective-permute-done.27.refs_1_, bf16[256,8192]{1,0:T(8,128)(2,1)} %collective-permute-done.11.refs_2_, bf16[8192,1024]{1,0:T(8,128)(2,1)} %refs_3_.3, ...), custom_call_target="tpu_custom_call" | custom-call | flops 262144 | bytes 2176 | tf_op jit(solution)/shard_map/pallas_call | solution.py:148
  418.7 1.6 collective-permute-start.30
  421.0 3.1 collective-permute-done.30
  424.2 3.2 collective-permute-done.29
  428.4 1.6 collective-permute-start.31
  431.4 2.9 collective-permute-done.32
  434.9 7.1 %collective-permute-done.31 = bf16[224,1024]{1,0:T(8,128)(2,1)S(1)} collective-permute-done((bf16[224,1024]{1,0:T(8,128)(2,1)}, bf16[224,1024]{1,0:T(8,128)(2,1)S(1)}, u32[]{:S(2)}, u32[]{:S(2)}) %collective-permute-start.31) | collective-permute-done | bytes 458784 | tf_op jit(solution)/shard_map/ppermute | solution.py:230
  442.2 1.3 constant_dynamic-slice_fusion.3
  445.6 4.4 shard_map.100
  450.2 1.5 collective-permute-start.38
  453.3 2.0 collective-permute-done.37
  455.3 3.2 collective-permute-start.41
  460.8 2.2 collective-permute-done.40
  (106 shorter events, 20.9 us)
Async XLA Ops:
  7.2 422.8 %all-gather.3.cloned.1.call-start = ((), (), s32[]{:S(2)}) async-start(), calls=%async_computation | async-start | bytes 1310720 | tf_op jit(solution)/shard_map/all_gather | solution.py:218
  11.8 80.0 %collective-permute-start.3 = (bf16[256,8192]{1,0:T(8,128)(2,1)}, bf16[256,8192]{1,0:T(8,128)(2,1)}, u32[]{:S(2)}, u32[]{:S(2)}) collective-permute-start(bf16[256,8192]{1,0:T(8,128)(2,1)} %bitcast.4), channel_id=1, source_target_pairs={{4,8},{8,4},{5,9},{9,5},{6,10},{10,6},{7,11},{11,7},{20,24},{24,20... | collective-permute-start | bytes 12582920 | tf_op jit(solution)/shard_map/ppermute | solution.py:201
  17.1 10.0 %copy-start.11 = (s32[2048]{0:T(1024)S(1)}, s32[2048]{0:T(1024)}, u32[]{:S(2)}) copy-start(s32[2048]{0:T(1024)} %param.15) | copy-start | bytes 24580
  17.1 10.0 %copy-start.12 = (s32[4]{0:T(128)S(1)}, s32[4]{0:T(128)}, u32[]{:S(2)}) copy-start(s32[4]{0:T(128)} %param.14) | copy-start | bytes 52
  17.2 28.2 %collective-permute-start = (bf16[1024,512]{1,0:T(8,128)(2,1)}, bf16[1024,512]{1,0:T(8,128)(2,1)}, u32[]{:S(2)}, u32[]{:S(2)}) collective-permute-start(bf16[1024,512]{1,0:T(8,128)(2,1)} %get-tuple-element.45), channel_id=1, source_target_pairs={{0,4},{4,0},{8,12},{12,8},{1,5},{5,1},{9,13},{13,9},{2,6},{6,2},{1... | collective-permute-start | bytes 3145736 | tf_op jit(solution)/shard_map/ppermute | solution.py:202
  26.5 63.8 %collective-permute-start.1 = (bf16[2048,512]{1,0:T(8,128)(2,1)}, bf16[2048,512]{1,0:T(8,128)(2,1)}, u32[]{:S(2)}, u32[]{:S(2)}) collective-permute-start(bf16[2048,512]{1,0:T(8,128)(2,1)} %get-tuple-element.42), channel_id=1, source_target_pairs={{0,4},{4,0},{8,12},{12,8},{1,5},{5,1},{9,13},{13,9},{2,6},{6,2},{1... | collective-permute-start | bytes 6291464 | tf_op jit(solution)/shard_map/ppermute | solution.py:202
  48.0 153.4 %collective-permute-start.11 = (bf16[256,8192]{1,0:T(8,128)(2,1)S(1)}, bf16[256,8192]{1,0:T(8,128)(2,1)}, u32[]{:S(2)}, u32[]{:S(2)}) collective-permute-start(bf16[256,8192]{1,0:T(8,128)(2,1)S(1)} %slice.50), channel_id=1, source_target_pairs={{4,8},{8,4},{5,9},{9,5},{6,10},{10,6},{7,11},{11,7},{20,24},{24,20... | collective-permute-start | bytes 12582920 | tf_op jit(solution)/shard_map/ppermute | solution.py:201
  66.5 68.7 %collective-permute-start.2 = (bf16[2048,512]{1,0:T(8,128)(2,1)}, bf16[2048,512]{1,0:T(8,128)(2,1)}, u32[]{:S(2)}, u32[]{:S(2)}) collective-permute-start(bf16[2048,512]{1,0:T(8,128)(2,1)} %get-tuple-element.22), channel_id=1, source_target_pairs={{0,4},{4,0},{8,12},{12,8},{1,5},{5,1},{9,13},{13,9},{2,6},{6,2},{1... | collective-permute-start | bytes 6291464 | tf_op jit(solution)/shard_map/ppermute | solution.py:202
  68.2 69.1 %collective-permute-start.6 = (bf16[1024,512]{1,0:T(8,128)(2,1)}, bf16[1024,512]{1,0:T(8,128)(2,1)}, u32[]{:S(2)}, u32[]{:S(2)}) collective-permute-start(bf16[1024,512]{1,0:T(8,128)(2,1)} %collective-permute-done), channel_id=1, source_target_pairs={{0,16},{16,0},{1,17},{17,1},{2,18},{18,2},{3,19},{19,3},{4,20},{20... | collective-permute-start | bytes 3145736 | tf_op jit(solution)/shard_map/ppermute | solution.py:203
  90.3 111.1 %collective-permute-start.7 = (bf16[2048,512]{1,0:T(8,128)(2,1)}, bf16[2048,512]{1,0:T(8,128)(2,1)S(1)}, u32[]{:S(2)}, u32[]{:S(2)}) collective-permute-start(bf16[2048,512]{1,0:T(8,128)(2,1)} %collective-permute-done.1), channel_id=1, source_target_pairs={{0,16},{16,0},{1,17},{17,1},{2,18},{18,2},{3,19},{19,3},{4,20},{20... | collective-permute-start | bytes 6291464 | tf_op jit(solution)/shard_map/ppermute | solution.py:203
  91.8 109.6 %collective-permute-start.4 = (bf16[2048,512]{1,0:T(8,128)(2,1)S(1)}, bf16[2048,512]{1,0:T(8,128)(2,1)}, u32[]{:S(2)}, u32[]{:S(2)}) collective-permute-start(bf16[2048,512]{1,0:T(8,128)(2,1)S(1)} %get-tuple-element.23), channel_id=1, source_target_pairs={{0,4},{4,0},{8,12},{12,8},{1,5},{5,1},{9,13},{13,9},{2,6},{6,2},{1... | collective-permute-start | bytes 6291464 | tf_op jit(solution)/shard_map/ppermute | solution.py:202
  135.2 66.2 %collective-permute-start.5 = (bf16[1024,512]{1,0:T(8,128)(2,1)S(1)}, bf16[1024,512]{1,0:T(8,128)(2,1)S(1)}, u32[]{:S(2)}, u32[]{:S(2)}) collective-permute-start(bf16[1024,512]{1,0:T(8,128)(2,1)S(1)} %get-tuple-element.24), channel_id=1, source_target_pairs={{0,4},{4,0},{8,12},{12,8},{1,5},{5,1},{9,13},{13,9},{2,6},{6,2},{1... | collective-permute-start | bytes 3145736 | tf_op jit(solution)/shard_map/ppermute | solution.py:202
  137.3 74.8 %collective-permute-start.8 = (bf16[2048,512]{1,0:T(8,128)(2,1)}, bf16[2048,512]{1,0:T(8,128)(2,1)}, u32[]{:S(2)}, u32[]{:S(2)}) collective-permute-start(bf16[2048,512]{1,0:T(8,128)(2,1)} %collective-permute-done.2), channel_id=1, source_target_pairs={{0,16},{16,0},{1,17},{17,1},{2,18},{18,2},{3,19},{19,3},{4,20},{20... | collective-permute-start | bytes 6291464 | tf_op jit(solution)/shard_map/ppermute | solution.py:203
  201.4 1.7 copy-start.9
  201.4 1.4 copy-start.6
  203.1 74.1 %collective-permute-start.12 = (bf16[128,8192]{1,0:T(8,128)(2,1)}, bf16[128,8192]{1,0:T(8,128)(2,1)S(1)}, u32[]{:S(2)}, u32[]{:S(2)}) collective-permute-start(bf16[128,8192]{1,0:T(8,128)(2,1)} %get-tuple-element.26), channel_id=1, source_target_pairs={{0,12},{12,0},{1,13},{13,1},{2,14},{14,2},{3,15},{15,3},{16,28},{2... | collective-permute-start | bytes 6291464 | tf_op jit(solution)/shard_map/ppermute | solution.py:214
  208.2 8.7 %copy-start.10 = (bf16[1024,512]{1,0:T(8,128)(2,1)S(1)}, bf16[1024,512]{1,0:T(8,128)(2,1)}, u32[]{:S(2)}) copy-start(bf16[1024,512]{1,0:T(8,128)(2,1)} %copy-done.9) | copy-start | bytes 3145732
  208.2 75.6 %collective-permute-start.9 = (bf16[2048,512]{1,0:T(8,128)(2,1)}, bf16[2048,512]{1,0:T(8,128)(2,1)}, u32[]{:S(2)}, u32[]{:S(2)}) collective-permute-start(bf16[2048,512]{1,0:T(8,128)(2,1)} %collective-permute-done.4), channel_id=1, source_target_pairs={{0,16},{16,0},{1,17},{17,1},{2,18},{18,2},{3,19},{19,3},{4,20},{20... | collective-permute-start | bytes 6291464 | tf_op jit(solution)/shard_map/ppermute | solution.py:203
  212.1 91.5 %collective-permute-start.16 = (bf16[128,8192]{1,0:T(8,128)(2,1)}, bf16[128,8192]{1,0:T(8,128)(2,1)S(1)}, u32[]{:S(2)}, u32[]{:S(2)}) collective-permute-start(bf16[128,8192]{1,0:T(8,128)(2,1)} %get-tuple-element.28), channel_id=1, source_target_pairs={{0,12},{12,0},{1,13},{13,1},{2,14},{14,2},{3,15},{15,3},{16,28},{2... | collective-permute-start | bytes 6291464 | tf_op jit(solution)/shard_map/ppermute | solution.py:214
  216.9 6.7 %copy-start.7 = (bf16[2048,512]{1,0:T(8,128)(2,1)S(1)}, bf16[2048,512]{1,0:T(8,128)(2,1)}, u32[]{:S(2)}) copy-start(bf16[2048,512]{1,0:T(8,128)(2,1)} %copy-done.6) | copy-start | bytes 6291460
  216.9 60.3 %collective-permute-start.10 = (bf16[1024,512]{1,0:T(8,128)(2,1)S(1)}, bf16[1024,512]{1,0:T(8,128)(2,1)S(1)}, u32[]{:S(2)}, u32[]{:S(2)}) collective-permute-start(bf16[1024,512]{1,0:T(8,128)(2,1)S(1)} %copy-done.10), channel_id=1, source_target_pairs={{0,16},{16,0},{1,17},{17,1},{2,18},{18,2},{3,19},{19,3},{4,20},{20... | collective-permute-start | bytes 3145736 | tf_op jit(solution)/shard_map/ppermute | solution.py:203
  277.2 9.7 %copy-start.4 = (bf16[128,8192]{1,0:T(8,128)(2,1)}, bf16[128,8192]{1,0:T(8,128)(2,1)S(1)}, u32[]{:S(2)}) copy-start(bf16[128,8192]{1,0:T(8,128)(2,1)S(1)} %collective-permute-done.12.refs_1_) | copy-start | bytes 6291460
  277.2 69.3 %collective-permute-start.20 = (bf16[128,8192]{1,0:T(8,128)(2,1)}, bf16[128,8192]{1,0:T(8,128)(2,1)}, u32[]{:S(2)}, u32[]{:S(2)}) collective-permute-start(bf16[128,8192]{1,0:T(8,128)(2,1)} %get-tuple-element.30), channel_id=1, source_target_pairs={{0,12},{12,0},{1,13},{13,1},{2,14},{14,2},{3,15},{15,3},{16,28},{2... | collective-permute-start | bytes 6291464 | tf_op jit(solution)/shard_map/ppermute | solution.py:214
  303.6 23.7 %copy-start.2 = (bf16[512,1024]{1,0:T(8,128)(2,1)S(1)}, bf16[512,1024]{1,0:T(8,128)(2,1)}, u32[]{:S(2)}) copy-start(bf16[512,1024]{1,0:T(8,128)(2,1)} %shard_map.95) | copy-start | bytes 3145732
  303.6 23.7 %copy-start.3 = (bf16[512,1024]{1,0:T(8,128)(2,1)S(1)}, bf16[512,1024]{1,0:T(8,128)(2,1)}, u32[]{:S(2)}) copy-start(bf16[512,1024]{1,0:T(8,128)(2,1)} %shard_map.96) | copy-start | bytes 3145732
  303.6 1.4 copy-start.5
  323.8 16.3 %copy-start.8 = (bf16[128,8192]{1,0:T(8,128)(2,1)S(1)}, bf16[128,8192]{1,0:T(8,128)(2,1)}, u32[]{:S(2)}) copy-start(bf16[128,8192]{1,0:T(8,128)(2,1)} %get-tuple-element.32) | copy-start | bytes 6291460
  325.1 2.7 collective-permute-start.17
  325.2 8.2 %collective-permute-start.19 = (bf16[2,32,2048]{2,1,0:T(8,128)(2,1)S(1)}, bf16[2,32,2048]{2,1,0:T(8,128)(2,1)S(1)}, u32[]{:S(2)}, u32[]{:S(2)}) collective-permute-start(bf16[2,32,2048]{2,1,0:T(8,128)(2,1)S(1)} %get-tuple-element.59), channel_id=1, source_target_pairs={{0,3},{1,2},{2,1},{3,0},{4,7},{5,6},{6,5},{7,4},{8,11},{9,10},{10,... | collective-permute-start | bytes 786440 | tf_op jit(solution)/shard_map/ppermute | solution.py:230
  326.8 13.2 %collective-permute-start.18 = (bf16[2,32,2048]{2,1,0:T(8,128)(2,1)S(1)}, bf16[2,32,2048]{2,1,0:T(8,128)(2,1)S(1)}, u32[]{:S(2)}, u32[]{:S(2)}) collective-permute-start(bf16[2,32,2048]{2,1,0:T(8,128)(2,1)S(1)} %get-tuple-element.60), channel_id=1, source_target_pairs={{0,2},{1,3},{2,0},{3,1},{4,6},{5,7},{6,4},{7,5},{8,10},{9,11},{10,... | collective-permute-start | bytes 786440 | tf_op jit(solution)/shard_map/ppermute | solution.py:230
  327.7 35.1 %collective-permute-start.13 = (bf16[4,32,2048]{2,1,0:T(8,128)(2,1)S(1)}, bf16[4,32,2048]{2,1,0:T(8,128)(2,1)S(1)}, u32[]{:S(2)}, u32[]{:S(2)}) collective-permute-start(bf16[4,32,2048]{2,1,0:T(8,128)(2,1)S(1)} %get-tuple-element.51), channel_id=1, source_target_pairs={{0,1},{1,0},{2,3},{3,2},{4,5},{5,4},{6,7},{7,6},{8,9},{9,8},{10,11... | collective-permute-start | bytes 1572872 | tf_op jit(solution)/shard_map/ppermute | solution.py:230
  327.8 36.7 %collective-permute-start.15 = (bf16[4,32,2048]{2,1,0:T(8,128)(2,1)S(1)}, bf16[4,32,2048]{2,1,0:T(8,128)(2,1)S(1)}, u32[]{:S(2)}, u32[]{:S(2)}) collective-permute-start(bf16[4,32,2048]{2,1,0:T(8,128)(2,1)S(1)} %get-tuple-element.52), channel_id=1, source_target_pairs={{0,3},{1,2},{2,1},{3,0},{4,7},{5,6},{6,5},{7,4},{8,11},{9,10},{10,... | collective-permute-start | bytes 1572872 | tf_op jit(solution)/shard_map/ppermute | solution.py:230
  333.4 31.5 %collective-permute-start.14 = (bf16[4,32,2048]{2,1,0:T(8,128)(2,1)S(1)}, bf16[4,32,2048]{2,1,0:T(8,128)(2,1)S(1)}, u32[]{:S(2)}, u32[]{:S(2)}) collective-permute-start(bf16[4,32,2048]{2,1,0:T(8,128)(2,1)S(1)} %get-tuple-element.53), channel_id=1, source_target_pairs={{0,2},{1,3},{2,0},{3,1},{4,6},{5,7},{6,4},{7,5},{8,10},{9,11},{10,... | collective-permute-start | bytes 1572872 | tf_op jit(solution)/shard_map/ppermute | solution.py:230
  340.0 62.3 %collective-permute-start.27 = (bf16[128,8192]{1,0:T(8,128)(2,1)S(1)}, bf16[128,8192]{1,0:T(8,128)(2,1)}, u32[]{:S(2)}, u32[]{:S(2)}) collective-permute-start(bf16[128,8192]{1,0:T(8,128)(2,1)S(1)} %copy-done.8), channel_id=1, source_target_pairs={{0,12},{12,0},{1,13},{13,1},{2,14},{14,2},{3,15},{15,3},{16,28},{2... | collective-permute-start | bytes 6291464 | tf_op jit(solution)/shard_map/ppermute | solution.py:214
  362.7 2.6 collective-permute-start.21
  362.8 5.4 %collective-permute-start.23 = (bf16[1,32,2048]{2,1,0:T(8,128)(2,1)S(1)}, bf16[1,32,2048]{2,1,0:T(8,128)(2,1)S(1)}, u32[]{:S(2)}, u32[]{:S(2)}) collective-permute-start(bf16[1,32,2048]{2,1,0:T(8,128)(2,1)S(1)} %get-tuple-element.67), channel_id=1, source_target_pairs={{0,3},{1,2},{2,1},{3,0},{4,7},{5,6},{6,5},{7,4},{8,11},{9,10},{10,... | collective-permute-start | bytes 393224 | tf_op jit(solution)/shard_map/ppermute | solution.py:230
  364.4 7.2 %collective-permute-start.22 = (bf16[1,32,2048]{2,1,0:T(8,128)(2,1)S(1)}, bf16[1,32,2048]{2,1,0:T(8,128)(2,1)}, u32[]{:S(2)}, u32[]{:S(2)}) collective-permute-start(bf16[1,32,2048]{2,1,0:T(8,128)(2,1)S(1)} %get-tuple-element.68), channel_id=1, source_target_pairs={{0,2},{1,3},{2,0},{3,1},{4,6},{5,7},{6,4},{7,5},{8,10},{9,11},{10,... | collective-permute-start | bytes 393224 | tf_op jit(solution)/shard_map/ppermute | solution.py:230
  372.8 12.0 %collective-permute-start.24 = (bf16[224,1024]{1,0:T(8,128)(2,1)S(1)}, bf16[224,1024]{1,0:T(8,128)(2,1)S(1)}, u32[]{:S(2)}, u32[]{:S(2)}) collective-permute-start(bf16[224,1024]{1,0:T(8,128)(2,1)S(1)} %get-tuple-element.62), channel_id=1, source_target_pairs={{0,2},{1,3},{2,0},{3,1},{4,6},{5,7},{6,4},{7,5},{8,10},{9,11},{10,... | collective-permute-start | bytes 1376264 | tf_op jit(solution)/shard_map/ppermute | solution.py:230
  374.4 43.2 %collective-permute-start.26 = (bf16[224,1024]{1,0:T(8,128)(2,1)S(1)}, bf16[224,1024]{1,0:T(8,128)(2,1)}, u32[]{:S(2)}, u32[]{:S(2)}) collective-permute-start(bf16[224,1024]{1,0:T(8,128)(2,1)S(1)} %get-tuple-element.61), channel_id=1, source_target_pairs={{0,4},{4,0},{8,12},{12,8},{1,5},{5,1},{9,13},{13,9},{2,6},{6,2},{1... | collective-permute-start | bytes 1376264 | tf_op jit(solution)/shard_map/ppermute | solution.py:230
  418.7 2.4 collective-permute-start.28
  418.7 5.4 %collective-permute-start.30 = (bf16[1,32,2048]{2,1,0:T(8,128)(2,1)S(1)}, bf16[1,32,2048]{2,1,0:T(8,128)(2,1)S(1)}, u32[]{:S(2)}, u32[]{:S(2)}) collective-permute-start(bf16[1,32,2048]{2,1,0:T(8,128)(2,1)S(1)} %get-tuple-element.64), channel_id=1, source_target_pairs={{0,3},{1,2},{2,1},{3,0},{4,7},{5,6},{6,5},{7,4},{8,11},{9,10},{10,... | collective-permute-start | bytes 393224 | tf_op jit(solution)/shard_map/ppermute | solution.py:230
  420.4 7.1 %collective-permute-start.29 = (bf16[1,32,2048]{2,1,0:T(8,128)(2,1)S(1)}, bf16[1,32,2048]{2,1,0:T(8,128)(2,1)S(1)}, u32[]{:S(2)}, u32[]{:S(2)}) collective-permute-start(bf16[1,32,2048]{2,1,0:T(8,128)(2,1)S(1)} %get-tuple-element.65), channel_id=1, source_target_pairs={{0,2},{1,3},{2,0},{3,1},{4,6},{5,7},{6,4},{7,5},{8,10},{9,11},{10,... | collective-permute-start | bytes 393224 | tf_op jit(solution)/shard_map/ppermute | solution.py:230
  421.0 23.6 %collective-permute-start.25 = (bf16[448,1024]{1,0:T(8,128)(2,1)S(1)}, bf16[448,1024]{1,0:T(8,128)(2,1)S(1)}, u32[]{:S(2)}, u32[]{:S(2)}) collective-permute-start(bf16[448,1024]{1,0:T(8,128)(2,1)S(1)} %pad_maximum_fusion.3.refs_0_), channel_id=1, source_target_pairs={{0,1},{1,0},{2,3},{3,2},{4,5},{5,4},{6,7},{7,6},{8,9},{9,8},{10,11... | collective-permute-start | bytes 2752520 | tf_op jit(solution)/shard_map/ppermute | solution.py:230
  428.4 13.6 %collective-permute-start.31 = (bf16[224,1024]{1,0:T(8,128)(2,1)}, bf16[224,1024]{1,0:T(8,128)(2,1)S(1)}, u32[]{:S(2)}, u32[]{:S(2)}) collective-permute-start(bf16[224,1024]{1,0:T(8,128)(2,1)} %collective-permute-done.26), channel_id=1, source_target_pairs={{0,2},{1,3},{2,0},{3,1},{4,6},{5,7},{6,4},{7,5},{8,10},{9,11},{10,... | collective-permute-start | bytes 1376264 | tf_op jit(solution)/shard_map/ppermute | solution.py:230
  430.0 4.3 collective-permute-start.32
  434.3 9.5 %collective-permute-start.34 = (bf16[64,1024]{1,0:T(8,128)(2,1)S(1)}, bf16[64,1024]{1,0:T(8,128)(2,1)S(1)}, u32[]{:S(2)}, u32[]{:S(2)}) collective-permute-start(bf16[64,1024]{1,0:T(8,128)(2,1)S(1)} %pad_maximum_fusion.7), channel_id=1, source_target_pairs={{0,2},{1,3},{2,0},{3,1},{4,6},{5,7},{6,4},{7,5},{8,10},{9,11},{10,... | collective-permute-start | bytes 393224 | tf_op jit(solution)/shard_map/ppermute | solution.py:230
  442.1 3.5 collective-permute-start.33
  443.5 2.1 copy-start
  443.5 2.1 copy-start.1
  443.9 1.7 collective-permute-start.35
  450.2 3.0 collective-permute-start.38
  451.7 3.6 collective-permute-start.37
  452.2 3.1 collective-permute-start.36
  455.3 5.5 %collective-permute-start.41 = (f32[4,4]{1,0:T(4,128)S(1)}, f32[4,4]{1,0:T(4,128)S(1)}, u32[]{:S(2)}, u32[]{:S(2)}) collective-permute-start(f32[4,4]{1,0:T(4,128)S(1)} %add_add_fusion.1), channel_id=1, source_target_pairs={{0,12},{4,8},{8,4},{12,0},{1,13},{5,9},{9,5},{13,1},{2,14},{6,10},... | collective-permute-start | bytes 200 | tf_op jit(solution)/shard_map/ppermute | solution.py:173
  458.5 4.5 collective-permute-start.40
  458.5 4.5 collective-permute-start.39
Sparse Core Ops, SparseCore 0:
  365.5 50.5 all-gather.2

commit v15 on v14

--- a/solution.py
+++ b/solution.py
@@ -215,8 +215,6 @@
 
     sub, full = tok // parts, cands * tok
 
-    every_act = lax.all_gather(after(local_act, partner[2]), "row", axis=0)
-
     own_end = project(flags, [(flat, 0, full)], [], [near_basis, after(far_basis, partner[0])])
     outer = project(
         flags,
@@ -254,13 +252,13 @@
         if k == 2:
             sums.append(scatter_sum(product))
             early = jnp.concatenate(sums, axis=0)
-            got = swap(early[:, dirs:], "row", 1)
+            got = swap(after(early[:, dirs:], partner[3]), "row", 1)
             waits = [swap(early[:, :dirs], "col", 2)]
     pair = jnp.concatenate([early[:, :dirs], *waits], axis=0)
     early_own = [pair, swap(pair, "col", 1)]
     last = scatter_sum(after(product, got))
+    every_act = lax.all_gather(after(local_act, got), "row", axis=0)
     got = after(got, last)
-    last = after(last, every_act)
     last = jnp.concatenate([last[:, :dirs], swap(last[:, dirs:], "row", 1)], axis=0)
     early_got = gather(got, last)
     arrays = early_own + early_got + gather(last)

time: 471 us -> 475 us (level)
    unnamed x35 -> x37, local copies, waits for them, and re-layouts: 25.5 us -> 26.9 us
  transfers between devices with their start and end apart: 43 -> 43, of which waited for: 20 -> 20; matrix products, arithmetic and copies ran while one was open for 13% -> 13% of each run, Pallas kernels for 17% -> 14%
where the time goes in v15:
time: 475 us; the launch traced here: 474 us
  waiting for transfers between devices  227 us (48%)
  Pallas kernels  86.1 us (18%)
  starting transfers between devices  75.8 us (16%)
  local copies, waits for them, and re-layouts  55.5 us (12%)
  between operations  14.5 us (3%)
  matrix products  7.6 us (2%)
  other arithmetic  7.02 us (1%)
    ppermute x5, waiting for transfers between devices, chain_body(): near.append(lax.ppermute(piece, 'row', beside))  112 us
    pallas_call x5, Pallas kernels, project(): pl.pallas_call(functools.partial(project_kernel, len(ends), len(tokens),...  80.7 us
    ppermute x5, waiting for transfers between devices, chain_body(): far.append(lax.ppermute(near[i], 'groups', [(0, 1), (1, 0)]))  49.1 us
    ppermute x20, waiting for transfers between devices, swap(): return lax.ppermute(value, axis, [(i, i ^ d) for i in range(size)])  41.8 us
    unnamed x37, local copies, waits for them, and re-layouts  26.9 us
    ppermute x5, starting transfers between devices, chain_body(): near.append(lax.ppermute(piece, 'row', beside))  26.4 us
    ppermute x4, waiting for transfers between devices, chain_body(): partner.append(lax.ppermute(after(piece, *tie), 'row', ends))  16.2 us
    ppermute x20, starting transfers between devices, swap(): return lax.ppermute(value, axis, [(i, i ^ d) for i in range(size)])  15.7 us
  transfers between devices with their start and end apart: 43, of which 20 were waited for; matrix products, arithmetic and copies ran while one was open for 13% of the time, Pallas kernels for 14%

profile of v15, /device:TPU:0, one launch (start us, length us, event | category | flops | bytes accessed | tf_op | source)
XLA Modules:
  0.0 473.9 jit_solution(3050606185362576392)
XLA Ops:
  7.2 4.6 slice.46
  11.8 2.7 collective-permute-start.3
  14.5 2.6 constant_dynamic-slice_fusion.4
  17.2 3.8 collective-permute-start
  21.0 5.5 %constant_dynamic-slice_fusion.8 = (bf16[2048,512]{1,0:T(8,128)(2,1)}, bf16[2048,512]{1,0:T(8,128)(2,1)S(1)}, bf16[2048,512]{1,0:T(8,128)(2,1)}) fusion(bf16[8192,1024]{1,0:T(8,128)(2,1)} %refs_3_.3, s32[]{:T(128)S(6)} %select_n.68), kind=kLoop, calls=%fused_computation.93 | loop fusion | bytes 12582916 | tf_op jit(solution)/shard_map/dynamic_slice | solution.py:195
  27.4 7.6 %fusion.5 = bf16[4,128,256]{2,1,0:T(8,128)(2,1)} fusion(bf16[4,128,8192]{2,1,0:T(8,128)(2,1)} %param.8, bf16[8192,256]{1,0:T(8,128)(2,1)} %param.10, f32[4,128]{1,0:T(4,128)S(1)} %compare_convert_fusion), kind=kOutput, calls=%fused_computation.8 | convolution fusion | flops 2147745792 | bytes 12847104 | tf_op jit(solution)/shard_map/ctd,dk->ctk/dot_general | solution.py:25
  35.0 10.3 %collective-permute-done = bf16[1024,512]{1,0:T(8,128)(2,1)} collective-permute-done((bf16[1024,512]{1,0:T(8,128)(2,1)}, bf16[1024,512]{1,0:T(8,128)(2,1)}, u32[]{:S(2)}, u32[]{:S(2)}) %collective-permute-start) | collective-permute-done | bytes 1048608 | tf_op jit(solution)/shard_map/ppermute | solution.py:202
  45.3 2.6 slice.50
  48.0 2.7 collective-permute-start.11
  50.6 15.9 %shard_map.95 = bf16[512,1024]{1,0:T(8,128)(2,1)} custom-call(s32[2]{0:T(128)} %pad_add_fusion.refs_0_, bf16[512,8192]{1,0:T(8,128)(2,1)} %bitcast.122, bf16[8192,1024]{1,0:T(8,128)(2,1)} %refs_3_.3), custom_call_target="tpu_custom_call" | custom-call | flops 536870912 | bytes 1572864 | tf_op jit(solution)/shard_map/pallas_call | solution.py:148
  66.5 1.7 collective-permute-start.2
  68.2 1.5 collective-permute-start.6
  69.7 20.5 %collective-permute-done.1 = bf16[2048,512]{1,0:T(8,128)(2,1)} collective-permute-done((bf16[2048,512]{1,0:T(8,128)(2,1)}, bf16[2048,512]{1,0:T(8,128)(2,1)}, u32[]{:S(2)}, u32[]{:S(2)}) %collective-permute-start.1) | collective-permute-done | bytes 2097184 | tf_op jit(solution)/shard_map/ppermute | solution.py:202
  90.3 1.5 collective-permute-start.7
  91.8 18.7 %collective-permute-start.4 = (bf16[2048,512]{1,0:T(8,128)(2,1)S(1)}, bf16[2048,512]{1,0:T(8,128)(2,1)}, u32[]{:S(2)}, u32[]{:S(2)}) collective-permute-start(bf16[2048,512]{1,0:T(8,128)(2,1)S(1)} %get-tuple-element.23), channel_id=1, source_target_pairs={{0,4},{4,0},{8,12},{12,8},{1,5},{5,1},{9,13},{13,9},{2,6},{6,2},{1... | collective-permute-start | bytes 6291464 | tf_op jit(solution)/shard_map/ppermute | solution.py:202
  110.5 24.7 %collective-permute-done.2 = bf16[2048,512]{1,0:T(8,128)(2,1)} collective-permute-done((bf16[2048,512]{1,0:T(8,128)(2,1)}, bf16[2048,512]{1,0:T(8,128)(2,1)}, u32[]{:S(2)}, u32[]{:S(2)}) %collective-permute-start.2) | collective-permute-done | bytes 2097184 | tf_op jit(solution)/shard_map/ppermute | solution.py:202
  135.2 2.1 collective-permute-start.5
  137.3 1.5 collective-permute-start.8
  138.8 5.9 %slice_bitcast_fusion = (bf16[128,8192]{1,0:T(8,128)(2,1)}, bf16[128,8192]{1,0:T(8,128)(2,1)}, bf16[128,8192]{1,0:T(8,128)(2,1)}, bf16[128,8192]{1,0:T(8,128)(2,1)}) fusion(bf16[4,128,8192]{2,1,0:T(8,128)(2,1)} %param.9), kind=kLoop, calls=%fused_computation.3 | loop fusion | bytes 16777216 | tf_op jit(solution)/shard_map/slice | solution.py:213
  144.8 56.6 %collective-permute-done.5 = bf16[1024,512]{1,0:T(8,128)(2,1)S(1)} collective-permute-done((bf16[1024,512]{1,0:T(8,128)(2,1)S(1)}, bf16[1024,512]{1,0:T(8,128)(2,1)S(1)}, u32[]{:S(2)}, u32[]{:S(2)}) %collective-permute-start.5) | collective-permute-done | bytes 1048608 | tf_op jit(solution)/shard_map/ppermute | solution.py:202
  201.4 1.3 copy-done.6
  203.1 5.1 %collective-permute-start.12 = (bf16[128,8192]{1,0:T(8,128)(2,1)}, bf16[128,8192]{1,0:T(8,128)(2,1)S(1)}, u32[]{:S(2)}, u32[]{:S(2)}) collective-permute-start(bf16[128,8192]{1,0:T(8,128)(2,1)} %get-tuple-element.26), channel_id=1, source_target_pairs={{0,12},{12,0},{1,13},{13,1},{2,14},{14,2},{3,15},{15,3},{16,28},{2... | collective-permute-start | bytes 6291464 | tf_op jit(solution)/shard_map/ppermute | solution.py:214
  208.2 1.6 collective-permute-start.9
  209.8 2.3 constant_dynamic-update-slice_fusion.4
  212.1 2.5 collective-permute-start.16
  214.6 2.3 constant_dynamic-update-slice_fusion.9
  217.4 3.1 constant_dynamic-update-slice_fusion.3
  220.5 3.1 constant_dynamic-update-slice_fusion.2
  223.6 1.4 constant_dynamic-update-slice_fusion.8
  225.0 3.0 constant_dynamic-update-slice_fusion.7
  228.1 49.1 %collective-permute-done.10 = bf16[1024,512]{1,0:T(8,128)(2,1)S(1)} collective-permute-done((bf16[1024,512]{1,0:T(8,128)(2,1)S(1)}, bf16[1024,512]{1,0:T(8,128)(2,1)S(1)}, u32[]{:S(2)}, u32[]{:S(2)}) %collective-permute-start.10) | collective-permute-done | bytes 1048608 | tf_op jit(solution)/shard_map/ppermute | solution.py:203
  277.2 2.5 collective-permute-start.20
  279.7 3.0 constant_dynamic-update-slice_fusion.1
  283.8 3.1 constant_dynamic-update-slice_fusion.6
  288.0 15.6 %shard_map.96 = bf16[512,1024]{1,0:T(8,128)(2,1)} custom-call(s32[2]{0:T(128)} %pad_add_fusion.refs_0_, bf16[512,8192]{1,0:T(8,128)(2,1)} %bitcast.123, bf16[8192,512]{1,0:T(8,128)(2,1)} %constant_dynamic-update-slice_fusion.refs_2_.refs_5_.refs_4_, bf16[8192,512]{1,0:T(8,128)(2,1)} %constant_dynamic-update-slice_fusion.5.refs_3_.refs_6_.refs_5_), custom_call_target="tpu_custom_call" | custom-call | flops 536870912 | bytes 1572864 | tf_op jit(solution)/shard_map/pallas_call | solution.py:148
  303.7 1.4 copy-done.5
  305.1 18.7 %shard_map.97 = bf16[256,2048]{1,0:T(8,128)(2,1)} custom-call(s32[2]{0:T(128)} %pad_add_fusion.refs_0_, bf16[128,8192]{1,0:T(8,128)(2,1)} %copy-done.4, bf16[128,8192]{1,0:T(8,128)(2,1)} %copy-done.5, bf16[256,8192]{1,0:T(8,128)(2,1)} %collective-permute-done.3.refs_3_, bf16[8192,1024]{1,0:T(8,128)(2,1)} %refs_3_.3, ...), custom_call_target="tpu_custom_call" | custom-call | flops 536870912 | bytes 2359296 | tf_op jit(solution)/shard_map/pallas_call | solution.py:148
  325.2 1.6 collective-permute-start.19
  327.8 1.6 collective-permute-start.15
  329.4 4.0 collective-permute-done.19
  333.5 1.3 collective-permute-start.14
  334.8 5.3 %collective-permute-done.18 = bf16[2,32,2048]{2,1,0:T(8,128)(2,1)S(1)} collective-permute-done((bf16[2,32,2048]{2,1,0:T(8,128)(2,1)S(1)}, bf16[2,32,2048]{2,1,0:T(8,128)(2,1)S(1)}, u32[]{:S(2)}, u32[]{:S(2)}) %collective-permute-start.18) | collective-permute-done | bytes 262176 | tf_op jit(solution)/shard_map/ppermute | solution.py:228
  340.1 5.3 %collective-permute-start.26 = (bf16[128,8192]{1,0:T(8,128)(2,1)S(1)}, bf16[128,8192]{1,0:T(8,128)(2,1)S(1)}, u32[]{:S(2)}, u32[]{:S(2)}) collective-permute-start(bf16[128,8192]{1,0:T(8,128)(2,1)S(1)} %copy-done.8), channel_id=1, source_target_pairs={{0,12},{12,0},{1,13},{13,1},{2,14},{14,2},{3,15},{15,3},{16,28},{2... | collective-permute-start | bytes 6291464 | tf_op jit(solution)/shard_map/ppermute | solution.py:214
  346.5 15.2 %shard_map.98 = bf16[128,2048]{1,0:T(8,128)(2,1)} custom-call(s32[2]{0:T(128)} %pad_add_fusion.refs_0_, bf16[128,8192]{1,0:T(8,128)(2,1)} %collective-permute-done.20.refs_1_, bf16[256,8192]{1,0:T(8,128)(2,1)} %collective-permute-done.11.refs_2_, bf16[8192,1024]{1,0:T(8,128)(2,1)} %refs_3_.3, ...), custom_call_target="tpu_custom_call" | custom-call | flops 268435456 | bytes 2228224 | tf_op jit(solution)/shard_map/pallas_call | solution.py:148
  362.9 1.6 collective-permute-start.23
  365.0 1.7 fusion.10
  366.7 1.6 collective-permute-done.23
  368.3 3.2 collective-permute-done.22
  372.7 1.6 collective-permute-start.24
  374.2 16.1 %collective-permute-done.26.refs_1_ = bf16[128,8192]{1,0:T(8,128)(2,1)S(1)} collective-permute-done((bf16[128,8192]{1,0:T(8,128)(2,1)S(1)}, bf16[128,8192]{1,0:T(8,128)(2,1)S(1)}, u32[]{:S(2)}, u32[]{:S(2)}) %collective-permute-start.26) | collective-permute-done | bytes 2097184 | tf_op jit(solution)/shard_map/ppermute | solution.py:214
  390.4 10.7 %collective-permute-done.27 = bf16[224,1024]{1,0:T(8,128)(2,1)} collective-permute-done((bf16[224,1024]{1,0:T(8,128)(2,1)S(1)}, bf16[224,1024]{1,0:T(8,128)(2,1)}, u32[]{:S(2)}, u32[]{:S(2)}) %collective-permute-start.27) | collective-permute-done | bytes 458784 | tf_op jit(solution)/shard_map/ppermute | solution.py:228
  401.1 15.3 %shard_map.99 = bf16[128,2048]{1,0:T(8,128)(2,1)} custom-call(s32[2]{0:T(128)} %pad_add_fusion.refs_0_, bf16[128,8192]{1,0:T(8,128)(2,1)} %copy-done.9, bf16[256,8192]{1,0:T(8,128)(2,1)} %collective-permute-done.11.refs_2_, bf16[8192,1024]{1,0:T(8,128)(2,1)} %refs_3_.3, bf16[8192,512]{1,0:T(8,128)(2,1)} %constant_dynamic-update-slice_fusion.refs_2_.refs_5_.refs_4_, ...), custom_call_target="tpu_custom_call" | custom-call | flops 262144 | bytes 2176 | tf_op jit(solution)/shard_map/pallas_call | solution.py:148
  417.5 1.6 collective-permute-start.30
  419.6 3.3 collective-permute-done.30
  422.9 3.2 collective-permute-done.29
  427.9 1.5 collective-permute-start.31
  429.4 6.4 %collective-permute-done.32 = bf16[32,1024]{1,0:T(8,128)(2,1)S(1)} collective-permute-done((bf16[32,1024]{1,0:T(8,128)(2,1)S(1)}, bf16[32,1024]{1,0:T(8,128)(2,1)S(1)}, u32[]{:S(2)}, u32[]{:S(2)}) %collective-permute-start.32) | collective-permute-done | bytes 65568 | tf_op jit(solution)/shard_map/ppermute | solution.py:228
  435.8 1.5 collective-permute-start.34
  438.6 4.0 collective-permute-done.34
  443.3 2.9 all-gather.3.cloned.1.call-done
  449.4 5.4 %shard_map.100 = (f32[4,1024,256]{2,1,0:T(8,128)}, f32[4,16,256]{2,1,0:T(8,128)S(1)}) custom-call(bf16[448,1024]{1,0:T(8,128)(2,1)S(1)} %pad_maximum_fusion.3.refs_0_, bf16[448,1024]{1,0:T(8,128)(2,1)S(1)} %collective-permute-done.25.refs_1_, bf16[448,1024]{1,0:T(8,128)(2,1)S(1)} %constant_dynamic-update-slice_fusion.10.refs_2_, ...), custom_call_target="tpu_custom_call" | custom-call | tf_op jit(solution)/shard_map/pallas_call | solution.py:53
  458.0 1.4 collective-permute-done.37
  459.4 2.5 collective-permute-start.41
  464.9 1.6 collective-permute-done.40
  (108 shorter events, 25.3 us)
Async XLA Ops:
  7.2 439.1 %all-gather.3.cloned.1.call-start = ((), (), s32[]{:S(2)}) async-start(), calls=%async_computation | async-start | bytes 1310720 | tf_op jit(solution)/shard_map/all_gather | solution.py:260
  11.8 80.0 %collective-permute-start.3 = (bf16[256,8192]{1,0:T(8,128)(2,1)}, bf16[256,8192]{1,0:T(8,128)(2,1)}, u32[]{:S(2)}, u32[]{:S(2)}) collective-permute-start(bf16[256,8192]{1,0:T(8,128)(2,1)} %bitcast.4), channel_id=1, source_target_pairs={{4,8},{8,4},{5,9},{9,5},{6,10},{10,6},{7,11},{11,7},{20,24},{24,20... | collective-permute-start | bytes 12582920 | tf_op jit(solution)/shard_map/ppermute | solution.py:201
  17.2 10.0 %copy-start.12 = (s32[2048]{0:T(1024)S(1)}, s32[2048]{0:T(1024)}, u32[]{:S(2)}) copy-start(s32[2048]{0:T(1024)} %param.15) | copy-start | bytes 24580
  17.2 10.0 %copy-start.13 = (s32[4]{0:T(128)S(1)}, s32[4]{0:T(128)}, u32[]{:S(2)}) copy-start(s32[4]{0:T(128)} %param.14) | copy-start | bytes 52
  17.2 28.2 %collective-permute-start = (bf16[1024,512]{1,0:T(8,128)(2,1)}, bf16[1024,512]{1,0:T(8,128)(2,1)}, u32[]{:S(2)}, u32[]{:S(2)}) collective-permute-start(bf16[1024,512]{1,0:T(8,128)(2,1)} %get-tuple-element.45), channel_id=1, source_target_pairs={{0,4},{4,0},{8,12},{12,8},{1,5},{5,1},{9,13},{13,9},{2,6},{6,2},{1... | collective-permute-start | bytes 3145736 | tf_op jit(solution)/shard_map/ppermute | solution.py:202
  26.5 63.8 %collective-permute-start.1 = (bf16[2048,512]{1,0:T(8,128)(2,1)}, bf16[2048,512]{1,0:T(8,128)(2,1)}, u32[]{:S(2)}, u32[]{:S(2)}) collective-permute-start(bf16[2048,512]{1,0:T(8,128)(2,1)} %get-tuple-element.42), channel_id=1, source_target_pairs={{0,4},{4,0},{8,12},{12,8},{1,5},{5,1},{9,13},{13,9},{2,6},{6,2},{1... | collective-permute-start | bytes 6291464 | tf_op jit(solution)/shard_map/ppermute | solution.py:202
  48.0 153.4 %collective-permute-start.11 = (bf16[256,8192]{1,0:T(8,128)(2,1)S(1)}, bf16[256,8192]{1,0:T(8,128)(2,1)}, u32[]{:S(2)}, u32[]{:S(2)}) collective-permute-start(bf16[256,8192]{1,0:T(8,128)(2,1)S(1)} %slice.50), channel_id=1, source_target_pairs={{4,8},{8,4},{5,9},{9,5},{6,10},{10,6},{7,11},{11,7},{20,24},{24,20... | collective-permute-start | bytes 12582920 | tf_op jit(solution)/shard_map/ppermute | solution.py:201
  66.5 68.7 %collective-permute-start.2 = (bf16[2048,512]{1,0:T(8,128)(2,1)}, bf16[2048,512]{1,0:T(8,128)(2,1)}, u32[]{:S(2)}, u32[]{:S(2)}) collective-permute-start(bf16[2048,512]{1,0:T(8,128)(2,1)} %get-tuple-element.22), channel_id=1, source_target_pairs={{0,4},{4,0},{8,12},{12,8},{1,5},{5,1},{9,13},{13,9},{2,6},{6,2},{1... | collective-permute-start | bytes 6291464 | tf_op jit(solution)/shard_map/ppermute | solution.py:202
  68.2 69.1 %collective-permute-start.6 = (bf16[1024,512]{1,0:T(8,128)(2,1)}, bf16[1024,512]{1,0:T(8,128)(2,1)}, u32[]{:S(2)}, u32[]{:S(2)}) collective-permute-start(bf16[1024,512]{1,0:T(8,128)(2,1)} %collective-permute-done), channel_id=1, source_target_pairs={{0,16},{16,0},{1,17},{17,1},{2,18},{18,2},{3,19},{19,3},{4,20},{20... | collective-permute-start | bytes 3145736 | tf_op jit(solution)/shard_map/ppermute | solution.py:203
  90.3 111.1 %collective-permute-start.7 = (bf16[2048,512]{1,0:T(8,128)(2,1)}, bf16[2048,512]{1,0:T(8,128)(2,1)S(1)}, u32[]{:S(2)}, u32[]{:S(2)}) collective-permute-start(bf16[2048,512]{1,0:T(8,128)(2,1)} %collective-permute-done.1), channel_id=1, source_target_pairs={{0,16},{16,0},{1,17},{17,1},{2,18},{18,2},{3,19},{19,3},{4,20},{20... | collective-permute-start | bytes 6291464 | tf_op jit(solution)/shard_map/ppermute | solution.py:203
  91.8 109.6 %collective-permute-start.4 = (bf16[2048,512]{1,0:T(8,128)(2,1)S(1)}, bf16[2048,512]{1,0:T(8,128)(2,1)}, u32[]{:S(2)}, u32[]{:S(2)}) collective-permute-start(bf16[2048,512]{1,0:T(8,128)(2,1)S(1)} %get-tuple-element.23), channel_id=1, source_target_pairs={{0,4},{4,0},{8,12},{12,8},{1,5},{5,1},{9,13},{13,9},{2,6},{6,2},{1... | collective-permute-start | bytes 6291464 | tf_op jit(solution)/shard_map/ppermute | solution.py:202
  135.2 66.2 %collective-permute-start.5 = (bf16[1024,512]{1,0:T(8,128)(2,1)S(1)}, bf16[1024,512]{1,0:T(8,128)(2,1)S(1)}, u32[]{:S(2)}, u32[]{:S(2)}) collective-permute-start(bf16[1024,512]{1,0:T(8,128)(2,1)S(1)} %get-tuple-element.24), channel_id=1, source_target_pairs={{0,4},{4,0},{8,12},{12,8},{1,5},{5,1},{9,13},{13,9},{2,6},{6,2},{1... | collective-permute-start | bytes 3145736 | tf_op jit(solution)/shard_map/ppermute | solution.py:202
  137.3 74.8 %collective-permute-start.8 = (bf16[2048,512]{1,0:T(8,128)(2,1)}, bf16[2048,512]{1,0:T(8,128)(2,1)}, u32[]{:S(2)}, u32[]{:S(2)}) collective-permute-start(bf16[2048,512]{1,0:T(8,128)(2,1)} %collective-permute-done.2), channel_id=1, source_target_pairs={{0,16},{16,0},{1,17},{17,1},{2,18},{18,2},{3,19},{19,3},{4,20},{20... | collective-permute-start | bytes 6291464 | tf_op jit(solution)/shard_map/ppermute | solution.py:203
  201.4 1.7 copy-start.10
  201.4 1.3 copy-start.6
  203.1 74.1 %collective-permute-start.12 = (bf16[128,8192]{1,0:T(8,128)(2,1)}, bf16[128,8192]{1,0:T(8,128)(2,1)S(1)}, u32[]{:S(2)}, u32[]{:S(2)}) collective-permute-start(bf16[128,8192]{1,0:T(8,128)(2,1)} %get-tuple-element.26), channel_id=1, source_target_pairs={{0,12},{12,0},{1,13},{13,1},{2,14},{14,2},{3,15},{15,3},{16,28},{2... | collective-permute-start | bytes 6291464 | tf_op jit(solution)/shard_map/ppermute | solution.py:214
  208.2 8.7 %copy-start.11 = (bf16[1024,512]{1,0:T(8,128)(2,1)S(1)}, bf16[1024,512]{1,0:T(8,128)(2,1)}, u32[]{:S(2)}) copy-start(bf16[1024,512]{1,0:T(8,128)(2,1)} %copy-done.10) | copy-start | bytes 3145732
  208.2 75.6 %collective-permute-start.9 = (bf16[2048,512]{1,0:T(8,128)(2,1)}, bf16[2048,512]{1,0:T(8,128)(2,1)}, u32[]{:S(2)}, u32[]{:S(2)}) collective-permute-start(bf16[2048,512]{1,0:T(8,128)(2,1)} %collective-permute-done.4), channel_id=1, source_target_pairs={{0,16},{16,0},{1,17},{17,1},{2,18},{18,2},{3,19},{19,3},{4,20},{20... | collective-permute-start | bytes 6291464 | tf_op jit(solution)/shard_map/ppermute | solution.py:203
  212.1 91.6 %collective-permute-start.16 = (bf16[128,8192]{1,0:T(8,128)(2,1)}, bf16[128,8192]{1,0:T(8,128)(2,1)S(1)}, u32[]{:S(2)}, u32[]{:S(2)}) collective-permute-start(bf16[128,8192]{1,0:T(8,128)(2,1)} %get-tuple-element.28), channel_id=1, source_target_pairs={{0,12},{12,0},{1,13},{13,1},{2,14},{14,2},{3,15},{15,3},{16,28},{2... | collective-permute-start | bytes 6291464 | tf_op jit(solution)/shard_map/ppermute | solution.py:214
  216.9 6.7 %copy-start.7 = (bf16[2048,512]{1,0:T(8,128)(2,1)S(1)}, bf16[2048,512]{1,0:T(8,128)(2,1)}, u32[]{:S(2)}) copy-start(bf16[2048,512]{1,0:T(8,128)(2,1)} %copy-done.6) | copy-start | bytes 6291460
  216.9 60.3 %collective-permute-start.10 = (bf16[1024,512]{1,0:T(8,128)(2,1)S(1)}, bf16[1024,512]{1,0:T(8,128)(2,1)S(1)}, u32[]{:S(2)}, u32[]{:S(2)}) collective-permute-start(bf16[1024,512]{1,0:T(8,128)(2,1)S(1)} %copy-done.11), channel_id=1, source_target_pairs={{0,16},{16,0},{1,17},{17,1},{2,18},{18,2},{3,19},{19,3},{4,20},{20... | collective-permute-start | bytes 3145736 | tf_op jit(solution)/shard_map/ppermute | solution.py:203
  277.2 9.7 %copy-start.4 = (bf16[128,8192]{1,0:T(8,128)(2,1)}, bf16[128,8192]{1,0:T(8,128)(2,1)S(1)}, u32[]{:S(2)}) copy-start(bf16[128,8192]{1,0:T(8,128)(2,1)S(1)} %collective-permute-done.12.refs_1_) | copy-start | bytes 6291460
  277.2 69.3 %collective-permute-start.20 = (bf16[128,8192]{1,0:T(8,128)(2,1)}, bf16[128,8192]{1,0:T(8,128)(2,1)}, u32[]{:S(2)}, u32[]{:S(2)}) collective-permute-start(bf16[128,8192]{1,0:T(8,128)(2,1)} %get-tuple-element.30), channel_id=1, source_target_pairs={{0,12},{12,0},{1,13},{13,1},{2,14},{14,2},{3,15},{15,3},{16,28},{2... | collective-permute-start | bytes 6291464 | tf_op jit(solution)/shard_map/ppermute | solution.py:214
  303.6 23.7 %copy-start.2 = (bf16[512,1024]{1,0:T(8,128)(2,1)S(1)}, bf16[512,1024]{1,0:T(8,128)(2,1)}, u32[]{:S(2)}) copy-start(bf16[512,1024]{1,0:T(8,128)(2,1)} %shard_map.95) | copy-start | bytes 3145732
  303.6 23.7 %copy-start.3 = (bf16[512,1024]{1,0:T(8,128)(2,1)S(1)}, bf16[512,1024]{1,0:T(8,128)(2,1)}, u32[]{:S(2)}) copy-start(bf16[512,1024]{1,0:T(8,128)(2,1)} %shard_map.96) | copy-start | bytes 3145732
  303.6 1.4 copy-start.5
  323.8 16.3 %copy-start.8 = (bf16[128,8192]{1,0:T(8,128)(2,1)S(1)}, bf16[128,8192]{1,0:T(8,128)(2,1)}, u32[]{:S(2)}) copy-start(bf16[128,8192]{1,0:T(8,128)(2,1)} %get-tuple-element.32) | copy-start | bytes 6291460
  325.1 2.7 collective-permute-start.17
  325.2 8.2 %collective-permute-start.19 = (bf16[2,32,2048]{2,1,0:T(8,128)(2,1)S(1)}, bf16[2,32,2048]{2,1,0:T(8,128)(2,1)S(1)}, u32[]{:S(2)}, u32[]{:S(2)}) collective-permute-start(bf16[2,32,2048]{2,1,0:T(8,128)(2,1)S(1)} %get-tuple-element.59), channel_id=1, source_target_pairs={{0,3},{1,2},{2,1},{3,0},{4,7},{5,6},{6,5},{7,4},{8,11},{9,10},{10,... | collective-permute-start | bytes 786440 | tf_op jit(solution)/shard_map/ppermute | solution.py:228
  326.8 13.2 %collective-permute-start.18 = (bf16[2,32,2048]{2,1,0:T(8,128)(2,1)S(1)}, bf16[2,32,2048]{2,1,0:T(8,128)(2,1)S(1)}, u32[]{:S(2)}, u32[]{:S(2)}) collective-permute-start(bf16[2,32,2048]{2,1,0:T(8,128)(2,1)S(1)} %get-tuple-element.60), channel_id=1, source_target_pairs={{0,2},{1,3},{2,0},{3,1},{4,6},{5,7},{6,4},{7,5},{8,10},{9,11},{10,... | collective-permute-start | bytes 786440 | tf_op jit(solution)/shard_map/ppermute | solution.py:228
  327.7 35.1 %collective-permute-start.13 = (bf16[4,32,2048]{2,1,0:T(8,128)(2,1)S(1)}, bf16[4,32,2048]{2,1,0:T(8,128)(2,1)}, u32[]{:S(2)}, u32[]{:S(2)}) collective-permute-start(bf16[4,32,2048]{2,1,0:T(8,128)(2,1)S(1)} %get-tuple-element.51), channel_id=1, source_target_pairs={{0,1},{1,0},{2,3},{3,2},{4,5},{5,4},{6,7},{7,6},{8,9},{9,8},{10,11... | collective-permute-start | bytes 1572872 | tf_op jit(solution)/shard_map/ppermute | solution.py:228
  327.8 36.7 %collective-permute-start.15 = (bf16[4,32,2048]{2,1,0:T(8,128)(2,1)S(1)}, bf16[4,32,2048]{2,1,0:T(8,128)(2,1)}, u32[]{:S(2)}, u32[]{:S(2)}) collective-permute-start(bf16[4,32,2048]{2,1,0:T(8,128)(2,1)S(1)} %get-tuple-element.52), channel_id=1, source_target_pairs={{0,3},{1,2},{2,1},{3,0},{4,7},{5,6},{6,5},{7,4},{8,11},{9,10},{10,... | collective-permute-start | bytes 1572872 | tf_op jit(solution)/shard_map/ppermute | solution.py:228
  333.5 31.6 %collective-permute-start.14 = (bf16[4,32,2048]{2,1,0:T(8,128)(2,1)S(1)}, bf16[4,32,2048]{2,1,0:T(8,128)(2,1)}, u32[]{:S(2)}, u32[]{:S(2)}) collective-permute-start(bf16[4,32,2048]{2,1,0:T(8,128)(2,1)S(1)} %get-tuple-element.53), channel_id=1, source_target_pairs={{0,2},{1,3},{2,0},{3,1},{4,6},{5,7},{6,4},{7,5},{8,10},{9,11},{10,... | collective-permute-start | bytes 1572872 | tf_op jit(solution)/shard_map/ppermute | solution.py:228
  340.1 50.3 %collective-permute-start.26 = (bf16[128,8192]{1,0:T(8,128)(2,1)S(1)}, bf16[128,8192]{1,0:T(8,128)(2,1)S(1)}, u32[]{:S(2)}, u32[]{:S(2)}) collective-permute-start(bf16[128,8192]{1,0:T(8,128)(2,1)S(1)} %copy-done.8), channel_id=1, source_target_pairs={{0,12},{12,0},{1,13},{13,1},{2,14},{14,2},{3,15},{15,3},{16,28},{2... | collective-permute-start | bytes 6291464 | tf_op jit(solution)/shard_map/ppermute | solution.py:214
  362.8 3.9 collective-permute-start.21
  362.9 5.4 %collective-permute-start.23 = (bf16[1,32,2048]{2,1,0:T(8,128)(2,1)S(1)}, bf16[1,32,2048]{2,1,0:T(8,128)(2,1)S(1)}, u32[]{:S(2)}, u32[]{:S(2)}) collective-permute-start(bf16[1,32,2048]{2,1,0:T(8,128)(2,1)S(1)} %get-tuple-element.67), channel_id=1, source_target_pairs={{0,3},{1,2},{2,1},{3,0},{4,7},{5,6},{6,5},{7,4},{8,11},{9,10},{10,... | collective-permute-start | bytes 393224 | tf_op jit(solution)/shard_map/ppermute | solution.py:228
  364.5 7.1 %collective-permute-start.22 = (bf16[1,32,2048]{2,1,0:T(8,128)(2,1)S(1)}, bf16[1,32,2048]{2,1,0:T(8,128)(2,1)S(1)}, u32[]{:S(2)}, u32[]{:S(2)}) collective-permute-start(bf16[1,32,2048]{2,1,0:T(8,128)(2,1)S(1)} %get-tuple-element.68), channel_id=1, source_target_pairs={{0,2},{1,3},{2,0},{3,1},{4,6},{5,7},{6,4},{7,5},{8,10},{9,11},{10,... | collective-permute-start | bytes 393224 | tf_op jit(solution)/shard_map/ppermute | solution.py:228
  372.7 17.7 %collective-permute-start.24 = (bf16[224,1024]{1,0:T(8,128)(2,1)S(1)}, bf16[224,1024]{1,0:T(8,128)(2,1)S(1)}, u32[]{:S(2)}, u32[]{:S(2)}) collective-permute-start(bf16[224,1024]{1,0:T(8,128)(2,1)S(1)} %get-tuple-element.62), channel_id=1, source_target_pairs={{0,2},{1,3},{2,0},{3,1},{4,6},{5,7},{6,4},{7,5},{8,10},{9,11},{10,... | collective-permute-start | bytes 1376264 | tf_op jit(solution)/shard_map/ppermute | solution.py:228
  390.4 10.7 %copy-start.9 = (bf16[128,8192]{1,0:T(8,128)(2,1)}, bf16[128,8192]{1,0:T(8,128)(2,1)S(1)}, u32[]{:S(2)}) copy-start(bf16[128,8192]{1,0:T(8,128)(2,1)S(1)} %collective-permute-done.26.refs_1_) | copy-start | bytes 6291460
  390.4 10.7 %collective-permute-start.27 = (bf16[224,1024]{1,0:T(8,128)(2,1)S(1)}, bf16[224,1024]{1,0:T(8,128)(2,1)}, u32[]{:S(2)}, u32[]{:S(2)}) collective-permute-start(bf16[224,1024]{1,0:T(8,128)(2,1)S(1)} %get-tuple-element.33), channel_id=1, source_target_pairs={{0,4},{4,0},{8,12},{12,8},{1,5},{5,1},{9,13},{13,9},{2,6},{6,2},{1... | collective-permute-start | bytes 1376264 | tf_op jit(solution)/shard_map/ppermute | solution.py:228
  417.4 2.2 collective-permute-start.28
  417.5 5.4 %collective-permute-start.30 = (bf16[1,32,2048]{2,1,0:T(8,128)(2,1)S(1)}, bf16[1,32,2048]{2,1,0:T(8,128)(2,1)S(1)}, u32[]{:S(2)}, u32[]{:S(2)}) collective-permute-start(bf16[1,32,2048]{2,1,0:T(8,128)(2,1)S(1)} %get-tuple-element.64), channel_id=1, source_target_pairs={{0,3},{1,2},{2,1},{3,0},{4,7},{5,6},{6,5},{7,4},{8,11},{9,10},{10,... | collective-permute-start | bytes 393224 | tf_op jit(solution)/shard_map/ppermute | solution.py:228
  419.1 7.1 %collective-permute-start.29 = (bf16[1,32,2048]{2,1,0:T(8,128)(2,1)S(1)}, bf16[1,32,2048]{2,1,0:T(8,128)(2,1)S(1)}, u32[]{:S(2)}, u32[]{:S(2)}) collective-permute-start(bf16[1,32,2048]{2,1,0:T(8,128)(2,1)S(1)} %get-tuple-element.65), channel_id=1, source_target_pairs={{0,2},{1,3},{2,0},{3,1},{4,6},{5,7},{6,4},{7,5},{8,10},{9,11},{10,... | collective-permute-start | bytes 393224 | tf_op jit(solution)/shard_map/ppermute | solution.py:228
  427.2 8.6 %collective-permute-start.32 = (bf16[32,1024]{1,0:T(8,128)(2,1)S(1)}, bf16[32,1024]{1,0:T(8,128)(2,1)S(1)}, u32[]{:S(2)}, u32[]{:S(2)}) collective-permute-start(bf16[32,1024]{1,0:T(8,128)(2,1)S(1)} %get-tuple-element.86), channel_id=1, source_target_pairs={{0,4},{4,0},{8,12},{12,8},{1,5},{5,1},{9,13},{13,9},{2,6},{6,2},{1... | collective-permute-start | bytes 196616 | tf_op jit(solution)/shard_map/ppermute | solution.py:228
  427.9 14.8 %collective-permute-start.31 = (bf16[224,1024]{1,0:T(8,128)(2,1)}, bf16[224,1024]{1,0:T(8,128)(2,1)S(1)}, u32[]{:S(2)}, u32[]{:S(2)}) collective-permute-start(bf16[224,1024]{1,0:T(8,128)(2,1)} %collective-permute-done.27), channel_id=1, source_target_pairs={{0,2},{1,3},{2,0},{3,1},{4,6},{5,7},{6,4},{7,5},{8,10},{9,11},{10,... | collective-permute-start | bytes 1376264 | tf_op jit(solution)/shard_map/ppermute | solution.py:228
  435.8 6.8 %collective-permute-start.34 = (bf16[64,1024]{1,0:T(8,128)(2,1)S(1)}, bf16[64,1024]{1,0:T(8,128)(2,1)S(1)}, u32[]{:S(2)}, u32[]{:S(2)}) collective-permute-start(bf16[64,1024]{1,0:T(8,128)(2,1)S(1)} %pad_maximum_fusion.7), channel_id=1, source_target_pairs={{0,2},{1,3},{2,0},{3,1},{4,6},{5,7},{6,4},{7,5},{8,10},{9,11},{10,... | collective-permute-start | bytes 393224 | tf_op jit(solution)/shard_map/ppermute | solution.py:228
  437.4 10.6 %collective-permute-start.25 = (bf16[448,1024]{1,0:T(8,128)(2,1)S(1)}, bf16[448,1024]{1,0:T(8,128)(2,1)S(1)}, u32[]{:S(2)}, u32[]{:S(2)}) collective-permute-start(bf16[448,1024]{1,0:T(8,128)(2,1)S(1)} %pad_maximum_fusion.3.refs_0_), channel_id=1, source_target_pairs={{0,1},{1,0},{2,3},{3,2},{4,5},{5,4},{6,7},{7,6},{8,9},{9,8},{10,11... | collective-permute-start | bytes 2752520 | tf_op jit(solution)/shard_map/ppermute | solution.py:228
  442.6 5.4 %collective-permute-start.35 = (bf16[128,1024]{1,0:T(8,128)(2,1)S(1)}, bf16[128,1024]{1,0:T(8,128)(2,1)S(1)}, u32[]{:S(2)}, u32[]{:S(2)}) collective-permute-start(bf16[128,1024]{1,0:T(8,128)(2,1)S(1)} %pad_maximum_fusion.6.refs_4_), channel_id=1, source_target_pairs={{0,1},{1,0},{2,3},{3,2},{4,5},{5,4},{6,7},{7,6},{8,9},{9,8},{10,11... | collective-permute-start | bytes 786440 | tf_op jit(solution)/shard_map/ppermute | solution.py:228
  442.8 5.3 %collective-permute-start.33 = (bf16[448,1024]{1,0:T(8,128)(2,1)S(1)}, bf16[448,1024]{1,0:T(8,128)(2,1)}, u32[]{:S(2)}, u32[]{:S(2)}) collective-permute-start(bf16[448,1024]{1,0:T(8,128)(2,1)S(1)} %constant_dynamic-update-slice_fusion.10.refs_2_), channel_id=1, source_target_pairs={{0,1},{1,0},{2,3},{3,2},{4,5},{5,4},{6,7},{7,6},{8,9},{9,8},{10,11... | collective-permute-start | bytes 2752520 | tf_op jit(solution)/shard_map/ppermute | solution.py:228
  447.5 1.6 copy-start
  447.5 1.8 copy-start.1
  455.0 3.0 collective-permute-start.38
  455.8 3.6 collective-permute-start.37
  456.5 2.9 collective-permute-start.36
  459.4 5.4 %collective-permute-start.41 = (f32[4,4]{1,0:T(4,128)S(1)}, f32[4,4]{1,0:T(4,128)S(1)}, u32[]{:S(2)}, u32[]{:S(2)}) collective-permute-start(f32[4,4]{1,0:T(4,128)S(1)} %add_add_fusion.1), channel_id=1, source_target_pairs={{0,12},{4,8},{8,4},{12,0},{1,13},{5,9},{9,5},{13,1},{2,14},{6,10},... | collective-permute-start | bytes 200 | tf_op jit(solution)/shard_map/ppermute | solution.py:173
  462.0 4.5 collective-permute-start.40
  462.7 3.7 collective-permute-start.39
Sparse Core Ops, SparseCore 0:
  416.5 29.7 all-gather.2

commit v16 on v13

--- a/solution.py
+++ b/solution.py
@@ -215,8 +215,6 @@
 
     sub, full = tok // parts, cands * tok
 
-    every_act = lax.all_gather(after(local_act, partner[2]), "row", axis=0)
-
     own_end = project(flags, [(flat, 0, full)], [], [near_basis, after(far_basis, partner[0])])
     outer = project(
         flags,
@@ -253,10 +251,10 @@
             sums.append(scatter_sum(product))
             early = jnp.concatenate(sums, axis=0)
             got = swap(early[:, dirs:], "row", 1)
+    every_act = lax.all_gather(after(local_act, got), "row", axis=0)
     early_own = gather(early[:, :dirs])
     last = scatter_sum(after(product, got, *early_own))
     got = after(got, last)
-    last = after(last, every_act)
     last = jnp.concatenate([last[:, :dirs], swap(last[:, dirs:], "row", 1)], axis=0)
     early_got = gather(got, last)
     arrays = early_own + early_got + gather(last)

time: 471 us -> 468 us (level)
  waiting for transfers between devices: 233 us -> 224 us
    ppermute x20, waiting for transfers between devices: 55.8 us -> 45.6 us  [swap(): return lax.ppermute(value, axis, [(i, i ^ d) for i in range(size)])]
    unnamed x37 -> x39, local copies, waits for them, and re-layouts: 24.3 us -> 28 us
  transfers between devices with their start and end apart: 43 -> 43, of which waited for: 22 -> 20; matrix products, arithmetic and copies ran while one was open for 12% -> 12% of each run, Pallas kernels for 17% -> 17%
where the time goes in v16:
time: 468 us; the launch traced here: 467 us
  waiting for transfers between devices  224 us (48%)
  Pallas kernels  86.4 us (18%)
  starting transfers between devices  73.1 us (16%)
  local copies, waits for them, and re-layouts  56.4 us (12%)
  between operations  14.4 us (3%)
  matrix products  7.61 us (2%)
  other arithmetic  5.69 us (1%)
    ppermute x5, waiting for transfers between devices, chain_body(): near.append(lax.ppermute(piece, 'row', beside))  114 us
    pallas_call x5, Pallas kernels, project(): pl.pallas_call(functools.partial(project_kernel, len(ends), len(tokens),...  81 us
    ppermute x5, waiting for transfers between devices, chain_body(): far.append(lax.ppermute(near[i], 'groups', [(0, 1), (1, 0)]))  49.1 us
    ppermute x20, waiting for transfers between devices, swap(): return lax.ppermute(value, axis, [(i, i ^ d) for i in range(size)])  45.6 us
    unnamed x39, local copies, waits for them, and re-layouts  28 us
    ppermute x5, starting transfers between devices, chain_body(): near.append(lax.ppermute(piece, 'row', beside))  26.4 us
    ppermute x4, starting transfers between devices, chain_body(): partner.append(lax.ppermute(after(piece, *tie), 'row', ends))  15.4 us
    ppermute x20, starting transfers between devices, swap(): return lax.ppermute(value, axis, [(i, i ^ d) for i in range(size)])  13 us
  transfers between devices with their start and end apart: 43, of which 20 were waited for; matrix products, arithmetic and copies ran while one was open for 12% of the time, Pallas kernels for 17%

profile of v16, /device:TPU:0, one launch (start us, length us, event | category | flops | bytes accessed | tf_op | source)
XLA Modules:
  0.0 467.2 jit_solution(13283087121261082826)
XLA Ops:
  7.2 6.0 %fusion.22 = (bf16[2,128,8192]{2,1,0:T(8,128)(2,1)}, bf16[2,128,8192]{2,1,0:T(8,128)(2,1)}) fusion(bf16[4,128,8192]{2,1,0:T(8,128)(2,1)} %param.9), kind=kLoop, calls=%fused_computation.94 | loop fusion | bytes 16777216 | tf_op jit(solution)/shard_map/slice | solution.py:200
  13.2 2.7 collective-permute-start.3
  15.9 2.7 constant_dynamic-slice_fusion.4
  18.6 3.9 collective-permute-start
  22.4 5.5 %constant_dynamic-slice_fusion.8 = (bf16[2048,512]{1,0:T(8,128)(2,1)}, bf16[2048,512]{1,0:T(8,128)(2,1)S(1)}, bf16[2048,512]{1,0:T(8,128)(2,1)}) fusion(bf16[8192,1024]{1,0:T(8,128)(2,1)} %refs_3_.3, s32[]{:T(128)S(6)} %select_n.68), kind=kLoop, calls=%fused_computation.93 | loop fusion | bytes 12582916 | tf_op jit(solution)/shard_map/dynamic_slice | solution.py:195
  28.9 7.6 %fusion.5 = bf16[4,128,256]{2,1,0:T(8,128)(2,1)} fusion(bf16[4,128,8192]{2,1,0:T(8,128)(2,1)} %param.8, bf16[8192,256]{1,0:T(8,128)(2,1)} %param.10, f32[4,128]{1,0:T(4,128)S(1)} %compare_convert_fusion), kind=kOutput, calls=%fused_computation.8 | convolution fusion | flops 2147745792 | bytes 12847104 | tf_op jit(solution)/shard_map/ctd,dk->ctk/dot_general | solution.py:25
  36.5 10.3 %collective-permute-done = bf16[1024,512]{1,0:T(8,128)(2,1)} collective-permute-done((bf16[1024,512]{1,0:T(8,128)(2,1)}, bf16[1024,512]{1,0:T(8,128)(2,1)}, u32[]{:S(2)}, u32[]{:S(2)}) %collective-permute-start) | collective-permute-done | bytes 1048608 | tf_op jit(solution)/shard_map/ppermute | solution.py:202
  46.7 2.6 collective-permute-start.11
  49.4 16.1 %shard_map.95 = bf16[512,1024]{1,0:T(8,128)(2,1)} custom-call(s32[2]{0:T(128)} %pad_add_fusion.refs_0_, bf16[512,8192]{1,0:T(8,128)(2,1)} %bitcast.122, bf16[8192,1024]{1,0:T(8,128)(2,1)} %refs_3_.3), custom_call_target="tpu_custom_call" | custom-call | flops 536870912 | bytes 1572864 | tf_op jit(solution)/shard_map/pallas_call | solution.py:148
  65.5 1.7 collective-permute-start.2
  67.2 1.5 collective-permute-start.6
  68.7 23.0 %collective-permute-done.1 = bf16[2048,512]{1,0:T(8,128)(2,1)} collective-permute-done((bf16[2048,512]{1,0:T(8,128)(2,1)}, bf16[2048,512]{1,0:T(8,128)(2,1)}, u32[]{:S(2)}, u32[]{:S(2)}) %collective-permute-start.1) | collective-permute-done | bytes 2097184 | tf_op jit(solution)/shard_map/ppermute | solution.py:202
  91.7 1.5 collective-permute-start.7
  93.2 18.7 %collective-permute-start.4 = (bf16[2048,512]{1,0:T(8,128)(2,1)S(1)}, bf16[2048,512]{1,0:T(8,128)(2,1)}, u32[]{:S(2)}, u32[]{:S(2)}) collective-permute-start(bf16[2048,512]{1,0:T(8,128)(2,1)S(1)} %get-tuple-element.22), channel_id=1, source_target_pairs={{0,4},{4,0},{8,12},{12,8},{1,5},{5,1},{9,13},{13,9},{2,6},{6,2},{1... | collective-permute-start | bytes 6291464 | tf_op jit(solution)/shard_map/ppermute | solution.py:202
  111.9 24.7 %collective-permute-done.2 = bf16[2048,512]{1,0:T(8,128)(2,1)} collective-permute-done((bf16[2048,512]{1,0:T(8,128)(2,1)S(1)}, bf16[2048,512]{1,0:T(8,128)(2,1)}, u32[]{:S(2)}, u32[]{:S(2)}) %collective-permute-start.2) | collective-permute-done | bytes 2097184 | tf_op jit(solution)/shard_map/ppermute | solution.py:202
  136.6 2.1 collective-permute-start.5
  138.7 1.5 collective-permute-start.8
  140.2 6.1 %slice_bitcast_fusion = (bf16[128,8192]{1,0:T(8,128)(2,1)}, bf16[128,8192]{1,0:T(8,128)(2,1)}, bf16[128,8192]{1,0:T(8,128)(2,1)}, bf16[128,8192]{1,0:T(8,128)(2,1)}) fusion(bf16[4,128,8192]{2,1,0:T(8,128)(2,1)} %param.9), kind=kLoop, calls=%fused_computation.3 | loop fusion | bytes 16777216 | tf_op jit(solution)/shard_map/slice | solution.py:213
  146.3 56.5 %collective-permute-done.5 = bf16[1024,512]{1,0:T(8,128)(2,1)S(1)} collective-permute-done((bf16[1024,512]{1,0:T(8,128)(2,1)S(1)}, bf16[1024,512]{1,0:T(8,128)(2,1)S(1)}, u32[]{:S(2)}, u32[]{:S(2)}) %collective-permute-start.5) | collective-permute-done | bytes 1048608 | tf_op jit(solution)/shard_map/ppermute | solution.py:202
  202.8 1.3 copy-done.7
  204.4 5.1 %collective-permute-start.12 = (bf16[128,8192]{1,0:T(8,128)(2,1)}, bf16[128,8192]{1,0:T(8,128)(2,1)S(1)}, u32[]{:S(2)}, u32[]{:S(2)}) collective-permute-start(bf16[128,8192]{1,0:T(8,128)(2,1)} %get-tuple-element.25), channel_id=1, source_target_pairs={{0,12},{12,0},{1,13},{13,1},{2,14},{14,2},{3,15},{15,3},{16,28},{2... | collective-permute-start | bytes 6291464 | tf_op jit(solution)/shard_map/ppermute | solution.py:214
  209.5 1.6 collective-permute-start.9
  211.1 2.2 constant_dynamic-update-slice_fusion.4
  213.4 2.5 collective-permute-start.16
  215.9 2.3 constant_dynamic-update-slice_fusion.9
  218.7 3.2 constant_dynamic-update-slice_fusion.3
  221.8 3.1 constant_dynamic-update-slice_fusion.2
  224.9 1.4 constant_dynamic-update-slice_fusion.8
  226.4 3.0 constant_dynamic-update-slice_fusion.7
  229.4 49.1 %collective-permute-done.10 = bf16[1024,512]{1,0:T(8,128)(2,1)S(1)} collective-permute-done((bf16[1024,512]{1,0:T(8,128)(2,1)S(1)}, bf16[1024,512]{1,0:T(8,128)(2,1)S(1)}, u32[]{:S(2)}, u32[]{:S(2)}) %collective-permute-start.10) | collective-permute-done | bytes 1048608 | tf_op jit(solution)/shard_map/ppermute | solution.py:203
  278.5 2.5 collective-permute-start.20
  281.0 3.0 constant_dynamic-update-slice_fusion.1
  285.1 3.1 constant_dynamic-update-slice_fusion.6
  289.3 15.6 %shard_map.96 = bf16[512,1024]{1,0:T(8,128)(2,1)} custom-call(s32[2]{0:T(128)} %pad_add_fusion.refs_0_, bf16[512,8192]{1,0:T(8,128)(2,1)} %bitcast.123, bf16[8192,512]{1,0:T(8,128)(2,1)} %constant_dynamic-update-slice_fusion.refs_2_.refs_5_.refs_4_, bf16[8192,512]{1,0:T(8,128)(2,1)} %constant_dynamic-update-slice_fusion.5.refs_3_.refs_6_.refs_5_), custom_call_target="tpu_custom_call" | custom-call | flops 536870912 | bytes 1572864 | tf_op jit(solution)/shard_map/pallas_call | solution.py:148
  304.9 1.3 copy-done.6
  306.2 18.8 %shard_map.97 = bf16[256,2048]{1,0:T(8,128)(2,1)} custom-call(s32[2]{0:T(128)} %pad_add_fusion.refs_0_, bf16[128,8192]{1,0:T(8,128)(2,1)} %copy-done.4, bf16[128,8192]{1,0:T(8,128)(2,1)} %copy-done.6, bf16[256,8192]{1,0:T(8,128)(2,1)} %collective-permute-done.3.refs_3_, bf16[8192,1024]{1,0:T(8,128)(2,1)} %refs_3_.3, ...), custom_call_target="tpu_custom_call" | custom-call | flops 536870912 | bytes 2359296 | tf_op jit(solution)/shard_map/pallas_call | solution.py:148
  325.0 1.2 dynamic-slice_bitcast_fusion.5
  326.3 1.6 collective-permute-start.18
  328.5 1.2 collective-permute-start.15
  329.7 5.1 %collective-permute-done.19 = bf16[2,32,2048]{2,1,0:T(8,128)(2,1)S(1)} collective-permute-done((bf16[2,32,2048]{2,1,0:T(8,128)(2,1)S(1)}, bf16[2,32,2048]{2,1,0:T(8,128)(2,1)S(1)}, u32[]{:S(2)}, u32[]{:S(2)}) %collective-permute-start.19) | collective-permute-done | bytes 262176 | tf_op jit(solution)/shard_map/ppermute | solution.py:228
  334.8 1.5 collective-permute-start.14
  336.3 4.2 collective-permute-done.18
  340.7 5.3 %collective-permute-start.27 = (bf16[128,8192]{1,0:T(8,128)(2,1)}, bf16[128,8192]{1,0:T(8,128)(2,1)S(1)}, u32[]{:S(2)}, u32[]{:S(2)}) collective-permute-start(bf16[128,8192]{1,0:T(8,128)(2,1)} %get-tuple-element.31), channel_id=1, source_target_pairs={{0,12},{12,0},{1,13},{13,1},{2,14},{14,2},{3,15},{15,3},{16,28},{2... | collective-permute-start | bytes 6291464 | tf_op jit(solution)/shard_map/ppermute | solution.py:214
  347.1 15.2 %shard_map.98 = bf16[128,2048]{1,0:T(8,128)(2,1)} custom-call(s32[2]{0:T(128)} %pad_add_fusion.refs_0_, bf16[128,8192]{1,0:T(8,128)(2,1)} %collective-permute-done.20.refs_1_, bf16[256,8192]{1,0:T(8,128)(2,1)} %collective-permute-done.11.refs_2_, bf16[8192,1024]{1,0:T(8,128)(2,1)} %refs_3_.3, ...), custom_call_target="tpu_custom_call" | custom-call | flops 268435456 | bytes 2228224 | tf_op jit(solution)/shard_map/pallas_call | solution.py:148
  365.7 3.3 collective-permute-done.23
  369.0 3.1 collective-permute-done.22
  373.2 1.4 collective-permute-start.24
  374.6 11.0 %collective-permute-done.24 = bf16[224,1024]{1,0:T(8,128)(2,1)S(1)} collective-permute-done((bf16[224,1024]{1,0:T(8,128)(2,1)S(1)}, bf16[224,1024]{1,0:T(8,128)(2,1)S(1)}, u32[]{:S(2)}, u32[]{:S(2)}) %collective-permute-start.24) | collective-permute-done | bytes 458784 | tf_op jit(solution)/shard_map/ppermute | solution.py:228
  385.7 7.3 %collective-permute-done.27.refs_1_ = bf16[128,8192]{1,0:T(8,128)(2,1)S(1)} collective-permute-done((bf16[128,8192]{1,0:T(8,128)(2,1)}, bf16[128,8192]{1,0:T(8,128)(2,1)S(1)}, u32[]{:S(2)}, u32[]{:S(2)}) %collective-permute-start.27) | collective-permute-done | bytes 2097184 | tf_op jit(solution)/shard_map/ppermute | solution.py:214
  393.0 1.3 copy-done.9
  394.3 15.2 %shard_map.99 = bf16[128,2048]{1,0:T(8,128)(2,1)} custom-call(s32[2]{0:T(128)} %pad_add_fusion.refs_0_, bf16[128,8192]{1,0:T(8,128)(2,1)} %copy-done.9, bf16[256,8192]{1,0:T(8,128)(2,1)} %collective-permute-done.11.refs_2_, bf16[8192,1024]{1,0:T(8,128)(2,1)} %refs_3_.3, bf16[8192,512]{1,0:T(8,128)(2,1)} %constant_dynamic-update-slice_fusion.refs_2_.refs_5_.refs_4_, ...), custom_call_target="tpu_custom_call" | custom-call | flops 268435456 | bytes 2228224 | tf_op jit(solution)/shard_map/pallas_call | solution.py:148
  410.8 1.6 collective-permute-start.29
  412.6 3.8 collective-permute-done.30
  416.4 2.9 collective-permute-done.29
  420.5 8.8 %collective-permute-done.32 = bf16[32,1024]{1,0:T(8,128)(2,1)S(1)} collective-permute-done((bf16[32,1024]{1,0:T(8,128)(2,1)S(1)}, bf16[32,1024]{1,0:T(8,128)(2,1)S(1)}, u32[]{:S(2)}, u32[]{:S(2)}) %collective-permute-start.32) | collective-permute-done | bytes 65568 | tf_op jit(solution)/shard_map/ppermute | solution.py:228
  429.3 2.1 collective-permute-start.34
  432.5 3.4 collective-permute-done.34
  437.6 2.0 all-gather.3.cloned.1.call-done
  439.5 1.3 constant_dynamic-slice_fusion.3
  442.7 5.4 %shard_map.100 = (f32[4,1024,256]{2,1,0:T(8,128)}, f32[4,16,256]{2,1,0:T(8,128)S(1)}) custom-call(bf16[448,1024]{1,0:T(8,128)(2,1)S(1)} %pad_maximum_fusion.3.refs_0_, bf16[448,1024]{1,0:T(8,128)(2,1)S(1)} %collective-permute-done.25.refs_1_, bf16[448,1024]{1,0:T(8,128)(2,1)S(1)} %constant_dynamic-update-slice_fusion.10.refs_2_, ...), custom_call_target="tpu_custom_call" | custom-call | tf_op jit(solution)/shard_map/pallas_call | solution.py:53
  451.3 1.4 collective-permute-done.37
  452.7 2.5 collective-permute-start.41
  456.0 1.2 collective-permute-start.39
  458.2 1.6 collective-permute-done.40
  (109 shorter events, 23.1 us)
Async XLA Ops:
  7.2 432.4 %all-gather.3.cloned.1.call-start = ((), (), s32[]{:S(2)}) async-start(), calls=%async_computation | async-start | bytes 1310720 | tf_op jit(solution)/shard_map/all_gather | solution.py:254
  13.2 80.0 %collective-permute-start.3 = (bf16[256,8192]{1,0:T(8,128)(2,1)}, bf16[256,8192]{1,0:T(8,128)(2,1)}, u32[]{:S(2)}, u32[]{:S(2)}) collective-permute-start(bf16[256,8192]{1,0:T(8,128)(2,1)} %bitcast.4), channel_id=1, source_target_pairs={{4,8},{8,4},{5,9},{9,5},{6,10},{10,6},{7,11},{11,7},{20,24},{24,20... | collective-permute-start | bytes 12582920 | tf_op jit(solution)/shard_map/ppermute | solution.py:201
  18.6 10.0 %copy-start.13 = (s32[2048]{0:T(1024)S(1)}, s32[2048]{0:T(1024)}, u32[]{:S(2)}) copy-start(s32[2048]{0:T(1024)} %param.15) | copy-start | bytes 24580
  18.6 10.0 %copy-start.14 = (s32[4]{0:T(128)S(1)}, s32[4]{0:T(128)}, u32[]{:S(2)}) copy-start(s32[4]{0:T(128)} %param.14) | copy-start | bytes 52
  18.6 28.2 %collective-permute-start = (bf16[1024,512]{1,0:T(8,128)(2,1)}, bf16[1024,512]{1,0:T(8,128)(2,1)}, u32[]{:S(2)}, u32[]{:S(2)}) collective-permute-start(bf16[1024,512]{1,0:T(8,128)(2,1)} %get-tuple-element.43), channel_id=1, source_target_pairs={{0,4},{4,0},{8,12},{12,8},{1,5},{5,1},{9,13},{13,9},{2,6},{6,2},{1... | collective-permute-start | bytes 3145736 | tf_op jit(solution)/shard_map/ppermute | solution.py:202
  27.9 63.8 %collective-permute-start.1 = (bf16[2048,512]{1,0:T(8,128)(2,1)}, bf16[2048,512]{1,0:T(8,128)(2,1)}, u32[]{:S(2)}, u32[]{:S(2)}) collective-permute-start(bf16[2048,512]{1,0:T(8,128)(2,1)} %get-tuple-element.40), channel_id=1, source_target_pairs={{0,4},{4,0},{8,12},{12,8},{1,5},{5,1},{9,13},{13,9},{2,6},{6,2},{1... | collective-permute-start | bytes 6291464 | tf_op jit(solution)/shard_map/ppermute | solution.py:202
  46.7 156.1 %collective-permute-start.11 = (bf16[256,8192]{1,0:T(8,128)(2,1)}, bf16[256,8192]{1,0:T(8,128)(2,1)}, u32[]{:S(2)}, u32[]{:S(2)}) collective-permute-start(bf16[256,8192]{1,0:T(8,128)(2,1)} %bitcast.128), channel_id=1, source_target_pairs={{4,8},{8,4},{5,9},{9,5},{6,10},{10,6},{7,11},{11,7},{20,24},{24,20... | collective-permute-start | bytes 12582920 | tf_op jit(solution)/shard_map/ppermute | solution.py:201
  49.4 16.1 %copy-start.5 = (bf16[2048,512]{1,0:T(8,128)(2,1)S(1)}, bf16[2048,512]{1,0:T(8,128)(2,1)}, u32[]{:S(2)}) copy-start(bf16[2048,512]{1,0:T(8,128)(2,1)} %get-tuple-element.21) | copy-start | bytes 6291460
  65.5 71.2 %collective-permute-start.2 = (bf16[2048,512]{1,0:T(8,128)(2,1)S(1)}, bf16[2048,512]{1,0:T(8,128)(2,1)}, u32[]{:S(2)}, u32[]{:S(2)}) collective-permute-start(bf16[2048,512]{1,0:T(8,128)(2,1)S(1)} %copy-done.5), channel_id=1, source_target_pairs={{0,4},{4,0},{8,12},{12,8},{1,5},{5,1},{9,13},{13,9},{2,6},{6,2},{1... | collective-permute-start | bytes 6291464 | tf_op jit(solution)/shard_map/ppermute | solution.py:202
  67.2 71.5 %collective-permute-start.6 = (bf16[1024,512]{1,0:T(8,128)(2,1)}, bf16[1024,512]{1,0:T(8,128)(2,1)S(1)}, u32[]{:S(2)}, u32[]{:S(2)}) collective-permute-start(bf16[1024,512]{1,0:T(8,128)(2,1)} %collective-permute-done), channel_id=1, source_target_pairs={{0,16},{16,0},{1,17},{17,1},{2,18},{18,2},{3,19},{19,3},{4,20},{20... | collective-permute-start | bytes 3145736 | tf_op jit(solution)/shard_map/ppermute | solution.py:203
  91.7 111.1 %collective-permute-start.7 = (bf16[2048,512]{1,0:T(8,128)(2,1)}, bf16[2048,512]{1,0:T(8,128)(2,1)S(1)}, u32[]{:S(2)}, u32[]{:S(2)}) collective-permute-start(bf16[2048,512]{1,0:T(8,128)(2,1)} %collective-permute-done.1), channel_id=1, source_target_pairs={{0,16},{16,0},{1,17},{17,1},{2,18},{18,2},{3,19},{19,3},{4,20},{20... | collective-permute-start | bytes 6291464 | tf_op jit(solution)/shard_map/ppermute | solution.py:203
  93.2 109.6 %collective-permute-start.4 = (bf16[2048,512]{1,0:T(8,128)(2,1)S(1)}, bf16[2048,512]{1,0:T(8,128)(2,1)}, u32[]{:S(2)}, u32[]{:S(2)}) collective-permute-start(bf16[2048,512]{1,0:T(8,128)(2,1)S(1)} %get-tuple-element.22), channel_id=1, source_target_pairs={{0,4},{4,0},{8,12},{12,8},{1,5},{5,1},{9,13},{13,9},{2,6},{6,2},{1... | collective-permute-start | bytes 6291464 | tf_op jit(solution)/shard_map/ppermute | solution.py:202
  136.6 66.2 %collective-permute-start.5 = (bf16[1024,512]{1,0:T(8,128)(2,1)S(1)}, bf16[1024,512]{1,0:T(8,128)(2,1)S(1)}, u32[]{:S(2)}, u32[]{:S(2)}) collective-permute-start(bf16[1024,512]{1,0:T(8,128)(2,1)S(1)} %get-tuple-element.23), channel_id=1, source_target_pairs={{0,4},{4,0},{8,12},{12,8},{1,5},{5,1},{9,13},{13,9},{2,6},{6,2},{1... | collective-permute-start | bytes 3145736 | tf_op jit(solution)/shard_map/ppermute | solution.py:202
  138.7 7.6 %copy-start.12 = (bf16[1024,512]{1,0:T(8,128)(2,1)}, bf16[1024,512]{1,0:T(8,128)(2,1)S(1)}, u32[]{:S(2)}) copy-start(bf16[1024,512]{1,0:T(8,128)(2,1)S(1)} %collective-permute-done.6) | copy-start | bytes 3145732
  138.7 74.7 %collective-permute-start.8 = (bf16[2048,512]{1,0:T(8,128)(2,1)}, bf16[2048,512]{1,0:T(8,128)(2,1)}, u32[]{:S(2)}, u32[]{:S(2)}) collective-permute-start(bf16[2048,512]{1,0:T(8,128)(2,1)} %collective-permute-done.2), channel_id=1, source_target_pairs={{0,16},{16,0},{1,17},{17,1},{2,18},{18,2},{3,19},{19,3},{4,20},{20... | collective-permute-start | bytes 6291464 | tf_op jit(solution)/shard_map/ppermute | solution.py:203
  202.8 1.6 copy-start.10
  202.8 1.4 copy-start.7
  204.4 74.1 %collective-permute-start.12 = (bf16[128,8192]{1,0:T(8,128)(2,1)}, bf16[128,8192]{1,0:T(8,128)(2,1)S(1)}, u32[]{:S(2)}, u32[]{:S(2)}) collective-permute-start(bf16[128,8192]{1,0:T(8,128)(2,1)} %get-tuple-element.25), channel_id=1, source_target_pairs={{0,12},{12,0},{1,13},{13,1},{2,14},{14,2},{3,15},{15,3},{16,28},{2... | collective-permute-start | bytes 6291464 | tf_op jit(solution)/shard_map/ppermute | solution.py:214
  209.5 8.7 %copy-start.11 = (bf16[1024,512]{1,0:T(8,128)(2,1)S(1)}, bf16[1024,512]{1,0:T(8,128)(2,1)}, u32[]{:S(2)}) copy-start(bf16[1024,512]{1,0:T(8,128)(2,1)} %copy-done.10) | copy-start | bytes 3145732
  209.5 75.6 %collective-permute-start.9 = (bf16[2048,512]{1,0:T(8,128)(2,1)}, bf16[2048,512]{1,0:T(8,128)(2,1)}, u32[]{:S(2)}, u32[]{:S(2)}) collective-permute-start(bf16[2048,512]{1,0:T(8,128)(2,1)} %collective-permute-done.4), channel_id=1, source_target_pairs={{0,16},{16,0},{1,17},{17,1},{2,18},{18,2},{3,19},{19,3},{4,20},{20... | collective-permute-start | bytes 6291464 | tf_op jit(solution)/shard_map/ppermute | solution.py:203
  213.4 91.6 %collective-permute-start.16 = (bf16[128,8192]{1,0:T(8,128)(2,1)}, bf16[128,8192]{1,0:T(8,128)(2,1)S(1)}, u32[]{:S(2)}, u32[]{:S(2)}) collective-permute-start(bf16[128,8192]{1,0:T(8,128)(2,1)} %get-tuple-element.27), channel_id=1, source_target_pairs={{0,12},{12,0},{1,13},{13,1},{2,14},{14,2},{3,15},{15,3},{16,28},{2... | collective-permute-start | bytes 6291464 | tf_op jit(solution)/shard_map/ppermute | solution.py:214
  218.2 6.7 %copy-start.8 = (bf16[2048,512]{1,0:T(8,128)(2,1)S(1)}, bf16[2048,512]{1,0:T(8,128)(2,1)}, u32[]{:S(2)}) copy-start(bf16[2048,512]{1,0:T(8,128)(2,1)} %copy-done.7) | copy-start | bytes 6291460
  218.2 60.3 %collective-permute-start.10 = (bf16[1024,512]{1,0:T(8,128)(2,1)S(1)}, bf16[1024,512]{1,0:T(8,128)(2,1)S(1)}, u32[]{:S(2)}, u32[]{:S(2)}) collective-permute-start(bf16[1024,512]{1,0:T(8,128)(2,1)S(1)} %copy-done.11), channel_id=1, source_target_pairs={{0,16},{16,0},{1,17},{17,1},{2,18},{18,2},{3,19},{19,3},{4,20},{20... | collective-permute-start | bytes 3145736 | tf_op jit(solution)/shard_map/ppermute | solution.py:203
  278.5 9.7 %copy-start.4 = (bf16[128,8192]{1,0:T(8,128)(2,1)}, bf16[128,8192]{1,0:T(8,128)(2,1)S(1)}, u32[]{:S(2)}) copy-start(bf16[128,8192]{1,0:T(8,128)(2,1)S(1)} %collective-permute-done.12.refs_1_) | copy-start | bytes 6291460
  278.5 68.6 %collective-permute-start.20 = (bf16[128,8192]{1,0:T(8,128)(2,1)}, bf16[128,8192]{1,0:T(8,128)(2,1)}, u32[]{:S(2)}, u32[]{:S(2)}) collective-permute-start(bf16[128,8192]{1,0:T(8,128)(2,1)} %get-tuple-element.29), channel_id=1, source_target_pairs={{0,12},{12,0},{1,13},{13,1},{2,14},{14,2},{3,15},{15,3},{16,28},{2... | collective-permute-start | bytes 6291464 | tf_op jit(solution)/shard_map/ppermute | solution.py:214
  304.9 23.2 %copy-start.2 = (bf16[512,1024]{1,0:T(8,128)(2,1)S(1)}, bf16[512,1024]{1,0:T(8,128)(2,1)}, u32[]{:S(2)}) copy-start(bf16[512,1024]{1,0:T(8,128)(2,1)} %shard_map.95) | copy-start | bytes 3145732
  304.9 23.2 %copy-start.3 = (bf16[512,1024]{1,0:T(8,128)(2,1)S(1)}, bf16[512,1024]{1,0:T(8,128)(2,1)}, u32[]{:S(2)}) copy-start(bf16[512,1024]{1,0:T(8,128)(2,1)} %shard_map.96) | copy-start | bytes 3145732
  304.9 1.3 copy-start.6
  326.2 8.6 %collective-permute-start.19 = (bf16[2,32,2048]{2,1,0:T(8,128)(2,1)S(1)}, bf16[2,32,2048]{2,1,0:T(8,128)(2,1)S(1)}, u32[]{:S(2)}, u32[]{:S(2)}) collective-permute-start(bf16[2,32,2048]{2,1,0:T(8,128)(2,1)S(1)} %get-tuple-element.59), channel_id=1, source_target_pairs={{0,3},{1,2},{2,1},{3,0},{4,7},{5,6},{6,5},{7,4},{8,11},{9,10},{10,... | collective-permute-start | bytes 786440 | tf_op jit(solution)/shard_map/ppermute | solution.py:228
  326.3 14.3 %collective-permute-start.18 = (bf16[2,32,2048]{2,1,0:T(8,128)(2,1)S(1)}, bf16[2,32,2048]{2,1,0:T(8,128)(2,1)S(1)}, u32[]{:S(2)}, u32[]{:S(2)}) collective-permute-start(bf16[2,32,2048]{2,1,0:T(8,128)(2,1)S(1)} %get-tuple-element.60), channel_id=1, source_target_pairs={{0,2},{1,3},{2,0},{3,1},{4,6},{5,7},{6,4},{7,5},{8,10},{9,11},{10,... | collective-permute-start | bytes 786440 | tf_op jit(solution)/shard_map/ppermute | solution.py:228
  327.8 12.8 %collective-permute-start.17 = (bf16[2,32,2048]{2,1,0:T(8,128)(2,1)S(1)}, bf16[2,32,2048]{2,1,0:T(8,128)(2,1)S(1)}, u32[]{:S(2)}, u32[]{:S(2)}) collective-permute-start(bf16[2,32,2048]{2,1,0:T(8,128)(2,1)S(1)} %get-tuple-element.58), channel_id=1, source_target_pairs={{0,1},{1,0},{2,3},{3,2},{4,5},{5,4},{6,7},{7,6},{8,9},{9,8},{10,11... | collective-permute-start | bytes 786440 | tf_op jit(solution)/shard_map/ppermute | solution.py:228
  328.5 35.8 %collective-permute-start.15 = (bf16[4,32,2048]{2,1,0:T(8,128)(2,1)S(1)}, bf16[4,32,2048]{2,1,0:T(8,128)(2,1)S(1)}, u32[]{:S(2)}, u32[]{:S(2)}) collective-permute-start(bf16[4,32,2048]{2,1,0:T(8,128)(2,1)S(1)} %get-tuple-element.52), channel_id=1, source_target_pairs={{0,3},{1,2},{2,1},{3,0},{4,7},{5,6},{6,5},{7,4},{8,11},{9,10},{10,... | collective-permute-start | bytes 1572872 | tf_op jit(solution)/shard_map/ppermute | solution.py:228
  334.8 30.4 %collective-permute-start.14 = (bf16[4,32,2048]{2,1,0:T(8,128)(2,1)S(1)}, bf16[4,32,2048]{2,1,0:T(8,128)(2,1)S(1)}, u32[]{:S(2)}, u32[]{:S(2)}) collective-permute-start(bf16[4,32,2048]{2,1,0:T(8,128)(2,1)S(1)} %get-tuple-element.53), channel_id=1, source_target_pairs={{0,2},{1,3},{2,0},{3,1},{4,6},{5,7},{6,4},{7,5},{8,10},{9,11},{10,... | collective-permute-start | bytes 1572872 | tf_op jit(solution)/shard_map/ppermute | solution.py:228
  340.5 24.8 %collective-permute-start.13 = (bf16[4,32,2048]{2,1,0:T(8,128)(2,1)S(1)}, bf16[4,32,2048]{2,1,0:T(8,128)(2,1)S(1)}, u32[]{:S(2)}, u32[]{:S(2)}) collective-permute-start(bf16[4,32,2048]{2,1,0:T(8,128)(2,1)S(1)} %get-tuple-element.51), channel_id=1, source_target_pairs={{0,1},{1,0},{2,3},{3,2},{4,5},{5,4},{6,7},{7,6},{8,9},{9,8},{10,11... | collective-permute-start | bytes 1572872 | tf_op jit(solution)/shard_map/ppermute | solution.py:228
  340.7 52.4 %collective-permute-start.27 = (bf16[128,8192]{1,0:T(8,128)(2,1)}, bf16[128,8192]{1,0:T(8,128)(2,1)S(1)}, u32[]{:S(2)}, u32[]{:S(2)}) collective-permute-start(bf16[128,8192]{1,0:T(8,128)(2,1)} %get-tuple-element.31), channel_id=1, source_target_pairs={{0,12},{12,0},{1,13},{13,1},{2,14},{14,2},{3,15},{15,3},{16,28},{2... | collective-permute-start | bytes 6291464 | tf_op jit(solution)/shard_map/ppermute | solution.py:214
  363.4 5.6 %collective-permute-start.23 = (bf16[1,32,2048]{2,1,0:T(8,128)(2,1)S(1)}, bf16[1,32,2048]{2,1,0:T(8,128)(2,1)S(1)}, u32[]{:S(2)}, u32[]{:S(2)}) collective-permute-start(bf16[1,32,2048]{2,1,0:T(8,128)(2,1)S(1)} %get-tuple-element.67), channel_id=1, source_target_pairs={{0,3},{1,2},{2,1},{3,0},{4,7},{5,6},{6,5},{7,4},{8,11},{9,10},{10,... | collective-permute-start | bytes 393224 | tf_op jit(solution)/shard_map/ppermute | solution.py:228
  364.3 7.8 %collective-permute-start.22 = (bf16[1,32,2048]{2,1,0:T(8,128)(2,1)S(1)}, bf16[1,32,2048]{2,1,0:T(8,128)(2,1)S(1)}, u32[]{:S(2)}, u32[]{:S(2)}) collective-permute-start(bf16[1,32,2048]{2,1,0:T(8,128)(2,1)S(1)} %get-tuple-element.68), channel_id=1, source_target_pairs={{0,2},{1,3},{2,0},{3,1},{4,6},{5,7},{6,4},{7,5},{8,10},{9,11},{10,... | collective-permute-start | bytes 393224 | tf_op jit(solution)/shard_map/ppermute | solution.py:228
  365.2 6.9 %collective-permute-start.21 = (bf16[1,32,2048]{2,1,0:T(8,128)(2,1)S(1)}, bf16[1,32,2048]{2,1,0:T(8,128)(2,1)S(1)}, u32[]{:S(2)}, u32[]{:S(2)}) collective-permute-start(bf16[1,32,2048]{2,1,0:T(8,128)(2,1)S(1)} %get-tuple-element.66), channel_id=1, source_target_pairs={{0,1},{1,0},{2,3},{3,2},{4,5},{5,4},{6,7},{7,6},{8,9},{9,8},{10,11... | collective-permute-start | bytes 393224 | tf_op jit(solution)/shard_map/ppermute | solution.py:228
  373.2 12.3 %collective-permute-start.24 = (bf16[224,1024]{1,0:T(8,128)(2,1)S(1)}, bf16[224,1024]{1,0:T(8,128)(2,1)S(1)}, u32[]{:S(2)}, u32[]{:S(2)}) collective-permute-start(bf16[224,1024]{1,0:T(8,128)(2,1)S(1)} %get-tuple-element.62), channel_id=1, source_target_pairs={{0,2},{1,3},{2,0},{3,1},{4,6},{5,7},{6,4},{7,5},{8,10},{9,11},{10,... | collective-permute-start | bytes 1376264 | tf_op jit(solution)/shard_map/ppermute | solution.py:228
  385.6 24.0 %collective-permute-start.25 = (bf16[448,1024]{1,0:T(8,128)(2,1)S(1)}, bf16[448,1024]{1,0:T(8,128)(2,1)S(1)}, u32[]{:S(2)}, u32[]{:S(2)}) collective-permute-start(bf16[448,1024]{1,0:T(8,128)(2,1)S(1)} %pad_maximum_fusion.3.refs_0_), channel_id=1, source_target_pairs={{0,1},{1,0},{2,3},{3,2},{4,5},{5,4},{6,7},{7,6},{8,9},{9,8},{10,11... | collective-permute-start | bytes 2752520 | tf_op jit(solution)/shard_map/ppermute | solution.py:228
  385.7 23.9 %collective-permute-start.26 = (bf16[224,1024]{1,0:T(8,128)(2,1)S(1)}, bf16[224,1024]{1,0:T(8,128)(2,1)}, u32[]{:S(2)}, u32[]{:S(2)}) collective-permute-start(bf16[224,1024]{1,0:T(8,128)(2,1)S(1)} %get-tuple-element.61), channel_id=1, source_target_pairs={{0,4},{4,0},{8,12},{12,8},{1,5},{5,1},{9,13},{13,9},{2,6},{6,2},{1... | collective-permute-start | bytes 1376264 | tf_op jit(solution)/shard_map/ppermute | solution.py:228
  393.0 1.3 copy-start.9
  410.7 5.7 %collective-permute-start.30 = (bf16[1,32,2048]{2,1,0:T(8,128)(2,1)S(1)}, bf16[1,32,2048]{2,1,0:T(8,128)(2,1)S(1)}, u32[]{:S(2)}, u32[]{:S(2)}) collective-permute-start(bf16[1,32,2048]{2,1,0:T(8,128)(2,1)S(1)} %get-tuple-element.64), channel_id=1, source_target_pairs={{0,3},{1,2},{2,1},{3,0},{4,7},{5,6},{6,5},{7,4},{8,11},{9,10},{10,... | collective-permute-start | bytes 393224 | tf_op jit(solution)/shard_map/ppermute | solution.py:228
  410.8 8.6 %collective-permute-start.29 = (bf16[1,32,2048]{2,1,0:T(8,128)(2,1)S(1)}, bf16[1,32,2048]{2,1,0:T(8,128)(2,1)S(1)}, u32[]{:S(2)}, u32[]{:S(2)}) collective-permute-start(bf16[1,32,2048]{2,1,0:T(8,128)(2,1)S(1)} %get-tuple-element.65), channel_id=1, source_target_pairs={{0,2},{1,3},{2,0},{3,1},{4,6},{5,7},{6,4},{7,5},{8,10},{9,11},{10,... | collective-permute-start | bytes 393224 | tf_op jit(solution)/shard_map/ppermute | solution.py:228
  412.4 7.0 %collective-permute-start.28 = (bf16[1,32,2048]{2,1,0:T(8,128)(2,1)S(1)}, bf16[1,32,2048]{2,1,0:T(8,128)(2,1)S(1)}, u32[]{:S(2)}, u32[]{:S(2)}) collective-permute-start(bf16[1,32,2048]{2,1,0:T(8,128)(2,1)S(1)} %get-tuple-element.63), channel_id=1, source_target_pairs={{0,1},{1,0},{2,3},{3,2},{4,5},{5,4},{6,7},{7,6},{8,9},{9,8},{10,11... | collective-permute-start | bytes 393224 | tf_op jit(solution)/shard_map/ppermute | solution.py:228
  420.3 15.6 %collective-permute-start.31 = (bf16[224,1024]{1,0:T(8,128)(2,1)}, bf16[224,1024]{1,0:T(8,128)(2,1)}, u32[]{:S(2)}, u32[]{:S(2)}) collective-permute-start(bf16[224,1024]{1,0:T(8,128)(2,1)} %collective-permute-done.26), channel_id=1, source_target_pairs={{0,2},{1,3},{2,0},{3,1},{4,6},{5,7},{6,4},{7,5},{8,10},{9,11},{10,... | collective-permute-start | bytes 1376264 | tf_op jit(solution)/shard_map/ppermute | solution.py:228
  420.4 8.9 %collective-permute-start.32 = (bf16[32,1024]{1,0:T(8,128)(2,1)S(1)}, bf16[32,1024]{1,0:T(8,128)(2,1)S(1)}, u32[]{:S(2)}, u32[]{:S(2)}) collective-permute-start(bf16[32,1024]{1,0:T(8,128)(2,1)S(1)} %get-tuple-element.86), channel_id=1, source_target_pairs={{0,4},{4,0},{8,12},{12,8},{1,5},{5,1},{9,13},{13,9},{2,6},{6,2},{1... | collective-permute-start | bytes 196616 | tf_op jit(solution)/shard_map/ppermute | solution.py:228
  429.3 6.5 %collective-permute-start.34 = (bf16[64,1024]{1,0:T(8,128)(2,1)S(1)}, bf16[64,1024]{1,0:T(8,128)(2,1)S(1)}, u32[]{:S(2)}, u32[]{:S(2)}) collective-permute-start(bf16[64,1024]{1,0:T(8,128)(2,1)S(1)} %pad_maximum_fusion.7), channel_id=1, source_target_pairs={{0,2},{1,3},{2,0},{3,1},{4,6},{5,7},{6,4},{7,5},{8,10},{9,11},{10,... | collective-permute-start | bytes 393224 | tf_op jit(solution)/shard_map/ppermute | solution.py:228
  435.9 5.5 %collective-permute-start.35 = (bf16[128,1024]{1,0:T(8,128)(2,1)S(1)}, bf16[128,1024]{1,0:T(8,128)(2,1)S(1)}, u32[]{:S(2)}, u32[]{:S(2)}) collective-permute-start(bf16[128,1024]{1,0:T(8,128)(2,1)S(1)} %pad_maximum_fusion.6.refs_4_), channel_id=1, source_target_pairs={{0,1},{1,0},{2,3},{3,2},{4,5},{5,4},{6,7},{7,6},{8,9},{9,8},{10,11... | collective-permute-start | bytes 786440 | tf_op jit(solution)/shard_map/ppermute | solution.py:228
  437.0 4.3 collective-permute-start.33
  440.8 1.6 copy-start
  440.8 1.8 copy-start.1
  448.3 3.0 collective-permute-start.38
  449.1 3.6 collective-permute-start.37
  449.8 2.9 collective-permute-start.36
  452.7 5.4 %collective-permute-start.41 = (f32[4,4]{1,0:T(4,128)S(1)}, f32[4,4]{1,0:T(4,128)S(1)}, u32[]{:S(2)}, u32[]{:S(2)}) collective-permute-start(f32[4,4]{1,0:T(4,128)S(1)} %add_add_fusion.1), channel_id=1, source_target_pairs={{0,12},{4,8},{8,4},{12,0},{1,13},{5,9},{9,5},{13,1},{2,14},{6,10},... | collective-permute-start | bytes 200 | tf_op jit(solution)/shard_map/ppermute | solution.py:173
  455.3 4.5 collective-permute-start.40
  456.0 3.7 collective-permute-start.39
Sparse Core Ops, SparseCore 0:
  409.7 29.7 all-gather.2
